TPU v7x, 32 devices: a whole 2x2x4 slice. The times are simulated.
32 devices in a mesh: grp: 2 (over x), leaf: 16 (over z, y, core).
Axes of the slice: x: 2, y: 2, z: 4, core: 2. Of those that a mesh axis runs over, the one named last changes fastest.
Arguments:
- probes: bfloat16 [65, 32768], P(None, ('grp', 'leaf')), parts along dimension 1, may hold values from -6 to 6
- basis: bfloat16 [256, 64, 128], P(('grp', 'leaf')), parts along dimension 0, may hold values from -0.5 to 0.5
- transfer: bfloat16 [256, 64, 64], P(('grp', 'leaf')), parts along dimension 0, may hold values from -0.75 to 0.75
- local_blocks: bfloat16 [256, 8, 128, 128], P(('grp', 'leaf')), parts along dimension 0, may hold values from -0.1875 to 0.1875
- remote_blocks: bfloat16 [256, 4, 128, 128], P(('grp', 'leaf')), parts along dimension 0, may hold values from -0.25 to 0.25
- near_dest: int32 [256, 4], P(('grp', 'leaf')), parts along dimension 0, may hold values from 0 to 15, as said below
- near_leaf: int32 [256, 4], P(('grp', 'leaf')), parts along dimension 0, may hold values from 0 to 7, as said below
- couplings: bfloat16 [32, 12, 64, 64], P(('grp', 'leaf')), parts along dimension 0, may hold values from -0.078125 to 0.078125
- far_list: int32 [32, 12], P(('grp', 'leaf')), parts along dimension 0, may hold values from 0 to 15, as said below
Outputs:
- mean_and_probes: float32 [65, 32768], P(None, ('grp', 'leaf')), parts along dimension 1
There are 2 independent parts, one for each index of `grp`. A program takes and returns all parts, laid end to end along the dimension named above; each array names one. Nothing has to cross between parts.
Inputs may be any that keep to these rules, and one draw needn't show every extreme that they name: `near_dest`: among the rows of one device, exactly 8 distinct devices appear, each exactly 4 times; some device appears in the rows of every device. Within the rows of one device no pair of near_dest and near_leaf repeats. `far_list`: each row names 12 distinct boxes, never its own box.
All inputs are finite; a program needn't handle non-finite values.
Results may differ from a plain program's by a relative error of at most 0.0031.
Values may be sent and summed in bfloat16 or wider, within the bound.
No kernel may reach another device: no remote copies, remote signals or barrier semaphores. Data moves between devices by JAX's collectives and lax.ppermute only.
A program may use at most 128 MiB of HBM per device.

v0:
```python
import jax
import jax.numpy as jnp
from jax import lax
from jax.sharding import PartitionSpec as P


def per_device(
    probes, basis, transfer, local_blocks, remote_blocks, near_dest, near_leaf, couplings, far_list
):
    columns = probes.shape[0]
    leaves = basis.shape[0]
    leaf_size = basis.shape[2]
    devices = lax.axis_size("leaf")
    values = probes.reshape(columns, leaves, leaf_size)
    products = jnp.einsum(
        "jbpq,rjq->jbrp", remote_blocks, values, preferred_element_type=jnp.float32
    ).astype(jnp.bfloat16)
    blocks_here = products.shape[0] * products.shape[1]
    products = products.reshape(blocks_here, columns, leaf_size)
    targets = near_dest.reshape(blocks_here)
    target_leaf = near_leaf.reshape(blocks_here)
    places = targets * leaves + target_leaf
    outgoing = (
        jnp.zeros((devices * leaves, columns, leaf_size), jnp.bfloat16).at[places].set(products)
    )
    incoming = lax.all_to_all(
        outgoing.reshape(devices, leaves, columns, leaf_size),
        "leaf",
        split_axis=0,
        concat_axis=0,
        tiled=True,
    )
    remote_part = jnp.sum(incoming, axis=0, dtype=jnp.float32)
    local_part = jnp.einsum(
        "icpq,rcq->irp", local_blocks, values, preferred_element_type=jnp.float32
    )
    leaf_coef = jnp.einsum(
        "jkp,rjp->jrk", basis, values, preferred_element_type=jnp.float32
    ).astype(jnp.bfloat16)
    box_coef = jnp.einsum(
        "jkl,jrl->rk", transfer, leaf_coef, preferred_element_type=jnp.float32
    ).astype(jnp.bfloat16)
    partners = far_list[0]
    every_box = lax.all_gather(box_coef[None], "leaf", axis=0, tiled=True)
    chosen = every_box[partners]
    far_box = jnp.einsum(
        "fkl,frl->rk", couplings[0], chosen, preferred_element_type=jnp.float32
    ).astype(jnp.bfloat16)
    down_coef = jnp.einsum(
        "jkl,rk->jrl", transfer, far_box, preferred_element_type=jnp.float32
    ).astype(jnp.bfloat16)
    far_part = jnp.einsum("jlp,jrl->jrp", basis, down_coef, preferred_element_type=jnp.float32)
    combined = local_part + remote_part + far_part
    return jnp.transpose(combined, (1, 0, 2)).reshape(columns, leaves * leaf_size)


def solution(mesh):
    placed = (
        P(None, ("grp", "leaf")),
        P(("grp", "leaf"), None, None),
        P(("grp", "leaf"), None, None),
        P(("grp", "leaf"), None, None, None),
        P(("grp", "leaf"), None, None, None),
        P(("grp", "leaf"), None),
        P(("grp", "leaf"), None),
        P(("grp", "leaf"), None, None, None),
        P(("grp", "leaf"), None),
    )
    return jax.shard_map(
        per_device, mesh=mesh, in_specs=placed, out_specs=P(None, ("grp", "leaf")), check_vma=False
    )
```

profile of v0, /device:TPU:9, one launch (start us, length us, event | category | flops | bytes accessed | tf_op | source)
XLA Modules:
  0.0 84.4 jit_solution(10576049090726735798)
XLA Ops:
  0.0 0.0 copy-start
  0.0 1.1 %copy.54 = bf16[9,8,8,128]{3,2,1,0:T(8,128)(2,1)S(1)} copy(bf16[9,8,8,128]{3,1,2,0:T(8,128)(2,1)} %bitcast.70) | data formatting | bytes 294912
  1.1 0.7 multiply_add_fusion
  1.8 0.1 copy.40
  1.9 0.1 add.45
  2.0 2.0 %convolution_convert_fusion = bf16[8,65,4,128]{3,1,2,0:T(8,128)(2,1)S(1)} fusion(bf16[8,4,128,128]{3,2,1,0:T(8,128)(2,1)} %param.13, bf16[65,8,128,1]{2,1,0,3:T(8,128)(2,1)S(1)} %get-tuple-element.6), kind=kOutput, calls=%fused_computation.3 | convolution fusion | flops 68423680 | bytes 1714176 | tf_op jit(solution)/shard_map/jbpq,rjq->jbrp/dot_general | solution.py:15
  4.0 1.7 %broadcast_in_dim.8 = bf16[128,65,128]{2,1,0:T(8,128)(2,1)} broadcast(bf16[]{:T(256)} %constant.6.clone.1), dimensions={} | broadcast | bytes 2129922 | tf_op jit(solution)/shard_map/broadcast_in_dim | solution.py:24
  5.7 4.4 %scatter_fusion = bf16[128,65,128]{2,1,0:T(8,128)(2,1)} fusion(bf16[128,65,128]{2,1,0:T(8,128)(2,1)} %broadcast_in_dim.8, s32[32]{0:T(128)S(1)} %fusion.17, bf16[32,65,128]{2,1,0:T(8,128)(2,1)S(1)} %bitcast.65), kind=kCustom, calls=%fused_computation.1 | custom fusion | bytes 1597568 | tf_op jit(solution)/shard_map/scatter | solution.py:24
  10.1 3.3 %copy.43 = bf16[16,8,65,128]{3,1,2,0:T(8,128)(2,1)} copy(bf16[16,8,65,128]{3,2,1,0:T(8,128)(2,1)} %bitcast.64) | data formatting | bytes 4259840 | tf_op jit(solution)/shard_map/reshape | solution.py:27
  13.4 6.8 %all-to-all-start = ((bf16[16,8,65,128]{3,1,2,0:T(8,128)(2,1)}), bf16[16,8,65,128]{3,1,2,0:T(8,128)(2,1)}, u32[]{:S(2)}, u32[]{:S(2)}) async-start(bf16[16,8,65,128]{3,1,2,0:T(8,128)(2,1)} %copy.43), calls=%async_computation | async-start | bytes 4259840 | tf_op jit(solution)/shard_map/all_to_all | solution.py:26
  20.1 0.0 copy-done.3
  20.1 0.1 copy.46
  20.3 0.0 copy-done.2
  20.3 0.4 fusion.7
  20.6 58.9 %all-gather.1 = bf16[16,65,64]{1,2,0:T(8,128)(2,1)S(1)} all-gather(bf16[1,65,64]{1,2,0:T(8,128)(2,1)S(1)} %fusion.7), channel_id=2, replica_groups=mesh['grp'=2,'leaf'=16] {'leaf'}, dimensions={0}, use_global_device_ids=true | all-gather | bytes 141440 | tf_op jit(solution)/shard_map/all_gather | solution.py:44
  79.5 0.0 copy-done.4
  79.5 0.6 gather_fusion
  80.2 0.4 fusion.6
  80.6 0.0 all-to-all-done
  80.6 1.9 %convert_reduce_fusion = f32[8,65,128]{2,0,1:T(8,128)S(1)} fusion(bf16[16,8,65,128]{3,1,2,0:T(8,128)(2,1)} %all-to-all-done), kind=kLoop, calls=%fused_computation.2 | loop fusion | flops 2063360 | bytes 2396160 | tf_op jit(solution)/shard_map/reduce_sum | solution.py:33
  82.5 0.8 fusion.1
  83.3 0.3 fusion
  83.6 0.1 copy.47
  83.7 0.8 copy.55
  (11 shorter events, 0.1 us)
Async XLA Ops:
  0.0 82.5 %copy-start = (bf16[8,8,128,128]{3,2,1,0:T(8,128)(2,1)S(1)}, bf16[8,8,128,128]{3,2,1,0:T(8,128)(2,1)}, u32[]{:S(2)}) copy-start(bf16[8,8,128,128]{3,2,1,0:T(8,128)(2,1)} %param.12) | copy-start | bytes 6291460
  13.4 6.8 %copy-start.3 = (bf16[8,64,64]{2,1,0:T(8,128)(2,1)S(1)}, bf16[8,64,64]{2,1,0:T(8,128)(2,1)}, u32[]{:S(2)}) copy-start(bf16[8,64,64]{2,1,0:T(8,128)(2,1)} %param.11) | copy-start | bytes 196612
  13.4 6.9 %copy-start.2 = (bf16[8,64,128]{2,1,0:T(8,128)(2,1)S(1)}, bf16[8,64,128]{2,1,0:T(8,128)(2,1)}, u32[]{:S(2)}) copy-start(bf16[8,64,128]{2,1,0:T(8,128)(2,1)} %param.10) | copy-start | bytes 393220
  13.4 66.2 %copy-start.4 = (s32[1,12]{1,0:T(1,128)S(1)}, s32[1,12]{1,0:T(1,128)}, u32[]{:S(2)}) copy-start(s32[1,12]{1,0:T(1,128)} %param.17) | copy-start | bytes 148
  13.4 66.8 %copy-start.1 = (bf16[1,12,64,64]{3,2,1,0:T(8,128)(2,1)S(1)}, bf16[1,12,64,64]{3,2,1,0:T(8,128)(2,1)}, u32[]{:S(2)}) copy-start(bf16[1,12,64,64]{3,2,1,0:T(8,128)(2,1)} %param.16) | copy-start | bytes 294916
  13.4 67.2 %all-to-all-start = ((bf16[16,8,65,128]{3,1,2,0:T(8,128)(2,1)}), bf16[16,8,65,128]{3,1,2,0:T(8,128)(2,1)}, u32[]{:S(2)}, u32[]{:S(2)}) async-start(bf16[16,8,65,128]{3,1,2,0:T(8,128)(2,1)} %copy.43), calls=%async_computation | async-start | bytes 4259840 | tf_op jit(solution)/shard_map/all_to_all | solution.py:26
where the time goes:
time: 84.9 us; the launch traced here: 84.4 us
  blocking collectives  58.9 us (69%)
  local copies, waits for them, and re-layouts  12.2 us (14%)
  starting transfers between devices  6.77 us (8%)
  matrix products  3.8 us (4%)
  other arithmetic  2.64 us (3%)
    all_gather x1, blocking collectives, per_device(): every_box = lax.all_gather(box_coef[None], 'leaf', axis=0, tiled=True)  58.9 us
    all_to_all x1, starting transfers between devices, per_device(): lax.all_to_all(outgoing.reshape(devices, leaves, columns, leaf_size), 'le...  6.77 us
    scatter x1, local copies, waits for them, and re-layouts, per_device(): jnp.zeros((devices * leaves, columns, leaf_size), jnp.bfloat16).at[places]  4.39 us
    reshape x1, local copies, waits for them, and re-layouts, per_device(): outgoing.reshape(devices, leaves, columns, leaf_size)  3.26 us
    unnamed x14, local copies, waits for them, and re-layouts  2.02 us
    dot_general x1, matrix products, per_device(): jnp.einsum('jbpq,rjq->jbrp', remote_blocks, values, preferred_element_typ...  1.99 us
    reduce_sum x1, other arithmetic, per_device(): remote_part = jnp.sum(incoming, axis=0, dtype=jnp.float32)  1.91 us
    broadcast_in_dim x1, local copies, waits for them, and re-layouts, per_device(): jnp.zeros((devices * leaves, columns, leaf_size), jnp.bfloat16).at[places]  1.73 us
  transfers between devices with their start and end apart: 1, of which 0 were waited for; matrix products, arithmetic and copies ran while one was open for 2% of the time, Pallas kernels for 0%

commit v1 on v0

v1 whole, which is shorter than its diff:
```python
import functools

import jax
import jax.numpy as jnp
from jax import lax
from jax.experimental import pallas as pl
from jax.experimental.pallas import tpu as pltpu
from jax.sharding import PartitionSpec as P

CAP = 4
TILE = 16
HALF = 64
VMEM_BYTES = 48 * 2**20

F32 = jnp.float32
BF16 = jnp.bfloat16

VMEM = pl.BlockSpec(memory_space=pltpu.VMEM)
SMEM = pl.BlockSpec(memory_space=pltpu.SMEM)


def dot_t(lhs, rhs):
    return lax.dot_general(lhs, rhs, (((1,), (1,)), ((), ())), preferred_element_type=F32)


def dot(lhs, rhs):
    return lax.dot_general(lhs, rhs, (((1,), (0,)), ((), ())), preferred_element_type=F32)


def products_kernel(main, dest_ref, probes_ref, blocks_ref, send_ref, tails, count):
    devices = send_ref.shape[0]
    leaves, per_leaf, size = blocks_ref.shape[:3]

    @pl.loop(0, devices)
    def _(i):
        count[i] = 0
        tails[i] = jnp.zeros_like(tails[i])

    for j in range(leaves):
        x = probes_ref[:, j * size : (j + 1) * size]
        for first in range(0, per_leaf, 4):
            many = min(4, per_leaf - first)
            rhs = blocks_ref[j, first : first + many].reshape(many * size, size)
            product = dot_t(x, rhs)
            for b in range(many):
                target = dest_ref[j, first + b]
                slot = count[target]
                count[target] = slot + 1
                block = product[:, b * size : (b + 1) * size]
                send_ref[target, pl.ds(pl.multiple_of(slot * main, TILE), main), :] = block[:main].astype(BF16)
                tails[target, pl.ds(slot, 1), :] = block[main:]

    @pl.loop(0, devices)
    def _(i):
        send_ref[i, CAP * main :, :] = tails[i].astype(BF16)


def near_kernel(
    devices, dest_ref, leaf_ref, probes_ref, basis_ref, transfer_ref, local_ref, pay_ref, base_ref, count
):
    leaves, rank, size = basis_ref.shape
    columns = probes_ref.shape[0]
    per_leaf = dest_ref.shape[1]
    box = jnp.zeros((columns, rank), F32)
    for j in range(leaves):
        coef = dot_t(probes_ref[:, j * size : (j + 1) * size], basis_ref[j]).astype(BF16)
        box += dot_t(coef, transfer_ref[j])
    pay_ref[:, :HALF] = box.astype(BF16)

    @pl.loop(0, devices)
    def _(i):
        count[i] = 0

    where = HALF * lax.broadcasted_iota(jnp.int32, (columns, HALF), 0) + lax.broadcasted_iota(
        jnp.int32, (columns, HALF), 1
    )
    rows = -(-devices * CAP // HALF)
    rows = min(columns, -(-rows // 8) * 8)
    where = where[:rows]
    table = jnp.full((rows, HALF), leaves, jnp.int32)
    for j in range(leaves):
        for b in range(per_leaf):
            target = dest_ref[j, b]
            slot = count[target]
            count[target] = slot + 1
            table = jnp.where(where == target * CAP + slot, leaf_ref[j, b], table)
    pay_ref[:rows, HALF:] = table.astype(F32).astype(BF16)
    pay_ref[rows:, HALF:] = jnp.zeros((columns - rows, HALF), BF16)

    for i in range(leaves):
        total = dot_t(probes_ref[:, :size], local_ref[i, 0])
        for c in range(1, leaves):
            total += dot_t(probes_ref[:, c * size : (c + 1) * size], local_ref[i, c])
        base_ref[:, i * size : (i + 1) * size] = total


def far_kernel(partner_ref, pay_ref, couplings_ref, transfer_ref, basis_ref, base_ref, out_ref):
    leaves, rank, size = basis_ref.shape
    columns = base_ref.shape[0]
    far = jnp.zeros((columns, rank), F32)
    for f in range(couplings_ref.shape[1]):
        far += dot_t(pay_ref[partner_ref[0, f]][:, :HALF], couplings_ref[0, f])
    far = far.astype(BF16)
    for j in range(leaves):
        down = dot(far, transfer_ref[j]).astype(BF16)
        cols = slice(j * size, (j + 1) * size)
        out_ref[:, cols] = base_ref[:, cols] + dot(down, basis_ref[j])


def gather_kernel(main, leaf_ref, base_ref, incoming_ref, out_ref, total):
    columns, points = base_ref.shape
    size = incoming_ref.shape[2]
    total[:, :points] = base_ref[...]
    total[:, points:] = jnp.zeros((columns, size), F32)

    @pl.loop(0, incoming_ref.shape[0])
    def _(source):
        tail = incoming_ref[source, CAP * main :, :].astype(F32)
        for slot in range(CAP):
            cols = pl.ds(pl.multiple_of(leaf_ref[source * CAP + slot] * size, size), size)
            total[:main, cols] += incoming_ref[source, slot * main : (slot + 1) * main, :].astype(F32)
            total[main:, cols] += tail[slot : slot + 1]

    out_ref[...] = total[:, :points]


def call(kernel, out_shape, in_specs, scratch, flops, nbytes):
    return pl.pallas_call(
        kernel,
        out_shape=out_shape,
        in_specs=in_specs,
        out_specs=jax.tree.map(lambda _: VMEM, out_shape),
        scratch_shapes=scratch,
        compiler_params=pltpu.CompilerParams(vmem_limit_bytes=VMEM_BYTES),
        cost_estimate=pl.CostEstimate(flops=flops, bytes_accessed=nbytes, transcendentals=0),
    )


def per_device(
    probes, basis, transfer, local_blocks, remote_blocks, near_dest, near_leaf, couplings, far_list
):
    columns, points = probes.shape
    leaves, rank, size = basis.shape
    devices = lax.axis_size("leaf")
    main = columns // TILE * TILE
    depth = CAP * main + TILE
    blocks = remote_blocks.shape[0] * remote_blocks.shape[1]
    unit = 2 * columns * size * size

    send = call(
        functools.partial(products_kernel, main),
        jax.ShapeDtypeStruct((devices, depth, size), BF16),
        [SMEM, VMEM, VMEM],
        [pltpu.VMEM((devices, TILE, size), F32), pltpu.SMEM((devices,), jnp.int32)],
        blocks * unit,
        remote_blocks.size * 2 + devices * depth * size * 2,
    )(near_dest, probes, remote_blocks)
    incoming = lax.all_to_all(send, "leaf", split_axis=0, concat_axis=0, tiled=True)

    pay, base = call(
        functools.partial(near_kernel, devices),
        (
            jax.ShapeDtypeStruct((columns, 2 * HALF), BF16),
            jax.ShapeDtypeStruct((columns, points), F32),
        ),
        [SMEM, SMEM, VMEM, VMEM, VMEM, VMEM],
        [pltpu.SMEM((devices,), jnp.int32)],
        leaves * leaves * unit,
        local_blocks.size * 2,
    )(near_dest, near_leaf, probes, basis, transfer, local_blocks)
    every = lax.all_gather(pay[None], "leaf", axis=0, tiled=True)
    first = lax.axis_index("leaf") * CAP
    mine = lax.dynamic_slice(every, (0, first // HALF, HALF + first % HALF), (devices, 1, CAP))
    slots = mine.reshape(devices * CAP).astype(jnp.int32)

    base = call(
        far_kernel,
        jax.ShapeDtypeStruct((columns, points), F32),
        [SMEM, VMEM, VMEM, VMEM, VMEM, VMEM],
        [],
        4 * leaves * unit,
        couplings.size * 2 + every.size * 2,
    )(far_list, every, couplings, transfer, basis, base)

    return call(
        functools.partial(gather_kernel, main),
        jax.ShapeDtypeStruct((columns, points), F32),
        [SMEM, VMEM, VMEM],
        [pltpu.VMEM((columns, points + size), F32)],
        devices * CAP * columns * size,
        devices * depth * size * 2,
    )(slots, base, incoming)


def solution(mesh):
    placed = (
        P(None, ("grp", "leaf")),
        P(("grp", "leaf"), None, None),
        P(("grp", "leaf"), None, None),
        P(("grp", "leaf"), None, None, None),
        P(("grp", "leaf"), None, None, None),
        P(("grp", "leaf"), None),
        P(("grp", "leaf"), None),
        P(("grp", "leaf"), None, None, None),
        P(("grp", "leaf"), None),
    )
    return jax.shard_map(
        per_device, mesh=mesh, in_specs=placed, out_specs=P(None, ("grp", "leaf")), check_vma=False
    )
```

time: 84.9 us -> 56.8 us (0.67)
  the two profiles are of different devices: /device:TPU:9 before, /device:TPU:11 now
where the time goes in v1:
time: 56.8 us; the launch traced here: 56.4 us
  blocking collectives  33.2 us (58%)
  Pallas kernels  8.74 us (15%)
  local copies, waits for them, and re-layouts  7.48 us (13%)
  starting transfers between devices  6.74 us (12%)
    all_gather x1, blocking collectives, per_device(): every = lax.all_gather(pay[None], 'leaf', axis=0, tiled=True)  33.2 us
    unnamed x26, local copies, waits for them, and re-layouts  7.39 us
    all_to_all x1, starting transfers between devices, per_device(): lax.all_to_all(send, 'leaf', split_axis=0, concat_axis=0, tiled=True)  6.74 us
    pallas_call x1, Pallas kernels, per_device(): call(functools.partial(near_kernel, devices), (jax.ShapeDtypeStruct((colu...  2.71 us
    pallas_call x1, Pallas kernels, per_device(): call(functools.partial(products_kernel, main), jax.ShapeDtypeStruct((devi...  2.27 us
    pallas_call x1, Pallas kernels, per_device(): call(far_kernel, jax.ShapeDtypeStruct((columns, points), F32), [SMEM, VME...  2 us
    pallas_call x1, Pallas kernels, per_device(): call(functools.partial(gather_kernel, main), jax.ShapeDtypeStruct((column...  1.76 us
  transfers between devices with their start and end apart: 1, of which 0 were waited for; matrix products, arithmetic and copies ran while one was open for 0% of the time, Pallas kernels for 8%

profile of v1, /device:TPU:11, one launch (start us, length us, event | category | flops | bytes accessed | tf_op | source)
XLA Modules:
  0.0 56.4 jit_solution(8517260172856132867)
XLA Ops:
  0.0 0.8 %copy.16.dest_ref = s32[8,4]{1,0:T(8,128)S(1)} copy(s32[8,4]{0,1:T(4,128)} %param.14) | data formatting | bytes 256 | tf_op args[5]
  0.8 1.2 %copy-done.1 = bf16[8,4,128,128]{3,2,1,0:T(8,128)(2,1)S(1)} copy-done((bf16[8,4,128,128]{3,2,1,0:T(8,128)(2,1)S(1)}, bf16[8,4,128,128]{3,2,1,0:T(8,128)(2,1)}, u32[]{:S(2)}) %copy-start.1) | copy-done | bytes 1048600
  2.0 0.9 %copy-done.2 = bf16[65,1024]{1,0:T(8,128)(2,1)S(1)} copy-done((bf16[65,1024]{1,0:T(8,128)(2,1)S(1)}, bf16[65,1024]{1,0:T(8,128)(2,1)}, u32[]{:S(2)}) %copy-start.2) | copy-done | bytes 133144
  2.9 2.3 %shard_map.93 = bf16[16,272,128]{2,1,0:T(8,128)(2,1)} custom-call(s32[8,4]{1,0:T(8,128)S(1)} %copy.16.dest_ref, bf16[65,1024]{1,0:T(8,128)(2,1)S(1)} %copy-done.2, bf16[8,4,128,128]{3,2,1,0:T(8,128)(2,1)S(1)} %copy-done.1), custom_call_target="tpu_custom_call" | custom-call | flops 68157440 | bytes 2162688 | tf_op jit(solution)/shard_map/pallas_call | solution.py:150
  5.2 6.7 %all-to-all-start = ((bf16[16,272,128]{2,1,0:T(8,128)(2,1)}), bf16[16,272,128]{2,1,0:T(8,128)(2,1)S(1)}, u32[]{:S(2)}, u32[]{:S(2)}) async-start(bf16[16,272,128]{2,1,0:T(8,128)(2,1)} %shard_map.93), calls=%async_computation | async-start | bytes 2228224 | tf_op jit(solution)/shard_map/all_to_all | solution.py:158
  11.9 0.0 copy-done.11
  11.9 0.1 copy.17.leaf_ref
  12.0 0.0 copy-done.4
  12.0 0.0 copy-done
  12.0 0.0 copy-done.3
  12.0 0.9 %copy-done.5 = bf16[8,64,64]{2,1,0:T(8,128)(2,1)S(1)} copy-done((bf16[8,64,64]{2,1,0:T(8,128)(2,1)S(1)}, bf16[8,64,64]{2,1,0:T(8,128)(2,1)}, u32[]{:S(2)}) %copy-start.5) | copy-done | bytes 65560
  12.9 2.7 %shard_map.91 = (bf16[65,128]{1,0:T(8,128)(2,1)S(1)}, f32[65,1024]{1,0:T(8,128)S(1)}) custom-call(s32[8,4]{1,0:T(8,128)S(1)} %copy.16.dest_ref, s32[8,4]{1,0:T(8,128)S(1)} %copy.17.leaf_ref, bf16[65,1024]{1,0:T(8,128)(2,1)S(1)} %copy-done.3, bf16[8,64,128]{2,1,0:T(8,128)(2,1)S(1)} %copy-done.4, bf16[8,64,64]{2,1,0:T(8,128)(2,1)S(1)} %copy-done.5, ...), custom_call_target="tpu_custom_call" | custom-call | flops 136314880 | bytes 2097152 | tf_op jit(solution)/shard_map/pallas_call | solution.py:160
  15.6 0.0 copy-start.7
  15.6 0.7 %copy-done.7 = f32[65,1024]{1,0:T(8,128)} copy-done((f32[65,1024]{1,0:T(8,128)}, f32[65,1024]{1,0:T(8,128)S(1)}, u32[]{:S(2)}) %copy-start.7) | copy-done | bytes 266264
  16.4 33.2 %all-gather.1.pay_ref = bf16[16,65,128]{2,1,0:T(8,128)(2,1)S(1)} all-gather(bf16[1,65,128]{2,1,0:T(8,128)(2,1)S(1)} %bitcast.1), channel_id=2, replica_groups=mesh['grp'=2,'leaf'=16] {'leaf'}, dimensions={0}, use_global_device_ids=true | all-gather | bytes 282880 | tf_op jit(solution)/shard_map/all_gather | solution.py:171
  49.6 0.1 fusion
  49.7 0.1 reshape.3.leaf_ref
  49.8 0.0 copy-start.6
  49.8 0.9 %copy-done.6 = bf16[8,64,64]{2,1,0:T(8,128)(2,1)S(1)} copy-done((bf16[8,64,64]{2,1,0:T(8,128)(2,1)S(1)}, bf16[8,64,64]{2,1,0:T(8,128)(2,1)}, u32[]{:S(2)}) %copy-start.6) | copy-done | bytes 65560
  50.7 1.0 %copy-done.8 = f32[65,1024]{1,0:T(8,128)S(1)} copy-done((f32[65,1024]{1,0:T(8,128)S(1)}, f32[65,1024]{1,0:T(8,128)}, u32[]{:S(2)}) %copy-start.8) | copy-done | bytes 266264
  51.7 0.9 %copy-done.9 = bf16[1,12,64,64]{3,2,1,0:T(8,128)(2,1)S(1)} copy-done((bf16[1,12,64,64]{3,2,1,0:T(8,128)(2,1)S(1)}, bf16[1,12,64,64]{3,2,1,0:T(8,128)(2,1)}, u32[]{:S(2)}) %copy-start.9) | copy-done | bytes 98328
  52.6 2.0 %shard_map.92.base_ref = f32[65,1024]{1,0:T(8,128)S(1)} custom-call(s32[1,12]{1,0:T(1,128)S(1)} %copy-done.10, bf16[16,65,128]{2,1,0:T(8,128)(2,1)S(1)} %all-gather.1.pay_ref, bf16[1,12,64,64]{3,2,1,0:T(8,128)(2,1)S(1)} %copy-done.9, bf16[8,64,64]{2,1,0:T(8,128)(2,1)S(1)} %copy-done.6, bf16[8,64,128]{2,1,0:T(8,128)(2,1)S(1)} %copy-done.4, ...), custom_call_target="tpu_custom_call" | custom-call | flops 68157440 | bytes 364544 | tf_op jit(solution)/shard_map/pallas_call | solution.py:176
  54.6 0.0 all-to-all-done.incoming_ref
  54.6 1.8 %shard_map.94 = f32[65,1024]{1,0:T(8,128)} custom-call(s32[64]{0:T(128)S(1)} %reshape.3.leaf_ref, f32[65,1024]{1,0:T(8,128)S(1)} %shard_map.92.base_ref, bf16[16,272,128]{2,1,0:T(8,128)(2,1)S(1)} %all-to-all-done.incoming_ref), custom_call_target="tpu_custom_call" | custom-call | flops 532480 | bytes 1114112 | tf_op jit(solution)/shard_map/pallas_call | solution.py:185
  (11 shorter events, 0.0 us)
Async XLA Ops:
  0.8 1.2 %copy-start.1 = (bf16[8,4,128,128]{3,2,1,0:T(8,128)(2,1)S(1)}, bf16[8,4,128,128]{3,2,1,0:T(8,128)(2,1)}, u32[]{:S(2)}) copy-start(bf16[8,4,128,128]{3,2,1,0:T(8,128)(2,1)} %blocks_ref.1) | copy-start | bytes 3145732
  2.0 0.9 %copy-start.2 = (bf16[65,1024]{1,0:T(8,128)(2,1)S(1)}, bf16[65,1024]{1,0:T(8,128)(2,1)}, u32[]{:S(2)}) copy-start(bf16[65,1024]{1,0:T(8,128)(2,1)} %probes_ref.3) | copy-start | bytes 399364
  2.9 9.1 %copy-start.4 = (bf16[8,64,128]{2,1,0:T(8,128)(2,1)S(1)}, bf16[8,64,128]{2,1,0:T(8,128)(2,1)}, u32[]{:S(2)}) copy-start(bf16[8,64,128]{2,1,0:T(8,128)(2,1)} %basis_ref.3) | copy-start | bytes 393220
  5.2 6.8 %copy-start.11 = (s32[8,4]{0,1:T(4,128)S(1)}, s32[8,4]{0,1:T(4,128)}, u32[]{:S(2)}) copy-start(s32[8,4]{0,1:T(4,128)} %param.15) | copy-start | bytes 388
  5.2 6.8 %copy-start = (bf16[8,8,128,128]{3,2,1,0:T(8,128)(2,1)S(1)}, bf16[8,8,128,128]{3,2,1,0:T(8,128)(2,1)}, u32[]{:S(2)}) copy-start(bf16[8,8,128,128]{3,2,1,0:T(8,128)(2,1)} %local_ref.1) | copy-start | bytes 6291460
  5.2 6.8 %copy-start.3 = (bf16[65,1024]{1,0:T(8,128)(2,1)S(1)}, bf16[65,1024]{1,0:T(8,128)(2,1)}, u32[]{:S(2)}) copy-start(bf16[65,1024]{1,0:T(8,128)(2,1)} %probes_ref.3) | copy-start | bytes 399364
  5.2 49.4 %all-to-all-start = ((bf16[16,272,128]{2,1,0:T(8,128)(2,1)}), bf16[16,272,128]{2,1,0:T(8,128)(2,1)S(1)}, u32[]{:S(2)}, u32[]{:S(2)}) async-start(bf16[16,272,128]{2,1,0:T(8,128)(2,1)} %shard_map.93), calls=%async_computation | async-start | bytes 2228224 | tf_op jit(solution)/shard_map/all_to_all | solution.py:158
  12.0 0.9 %copy-start.5 = (bf16[8,64,64]{2,1,0:T(8,128)(2,1)S(1)}, bf16[8,64,64]{2,1,0:T(8,128)(2,1)}, u32[]{:S(2)}) copy-start(bf16[8,64,64]{2,1,0:T(8,128)(2,1)} %transfer_ref.3) | copy-start | bytes 196612
  12.9 36.9 %copy-start.10 = (s32[1,12]{1,0:T(1,128)S(1)}, s32[1,12]{1,0:T(1,128)}, u32[]{:S(2)}) copy-start(s32[1,12]{1,0:T(1,128)} %partner_ref.1) | copy-start | bytes 148
  15.6 0.7 %copy-start.7 = (f32[65,1024]{1,0:T(8,128)}, f32[65,1024]{1,0:T(8,128)S(1)}, u32[]{:S(2)}) copy-start(f32[65,1024]{1,0:T(8,128)S(1)} %get-tuple-element.8.base_ref) | copy-start | bytes 798724
  49.8 0.9 %copy-start.6 = (bf16[8,64,64]{2,1,0:T(8,128)(2,1)S(1)}, bf16[8,64,64]{2,1,0:T(8,128)(2,1)}, u32[]{:S(2)}) copy-start(bf16[8,64,64]{2,1,0:T(8,128)(2,1)} %transfer_ref.3) | copy-start | bytes 196612
  50.7 1.0 %copy-start.8 = (f32[65,1024]{1,0:T(8,128)S(1)}, f32[65,1024]{1,0:T(8,128)}, u32[]{:S(2)}) copy-start(f32[65,1024]{1,0:T(8,128)} %copy-done.7) | copy-start | bytes 798724
  51.7 0.9 %copy-start.9 = (bf16[1,12,64,64]{3,2,1,0:T(8,128)(2,1)S(1)}, bf16[1,12,64,64]{3,2,1,0:T(8,128)(2,1)}, u32[]{:S(2)}) copy-start(bf16[1,12,64,64]{3,2,1,0:T(8,128)(2,1)} %couplings_ref.1) | copy-start | bytes 294916

commit v2 on v1

v2 whole, which is shorter than its diff:
```python
import functools

import jax
import jax.numpy as jnp
from jax import lax
from jax.experimental import pallas as pl
from jax.experimental.pallas import tpu as pltpu
from jax.sharding import PartitionSpec as P

CAP = 4
TILE = 16

F32 = jnp.float32
BF16 = jnp.bfloat16

VMEM = pl.BlockSpec(memory_space=pltpu.VMEM)
SMEM = pl.BlockSpec(memory_space=pltpu.SMEM)
ANY = pl.BlockSpec(memory_space=pl.ANY)


def dot_t(lhs, rhs):
    return lax.dot_general(lhs, rhs, (((1,), (1,)), ((), ())), preferred_element_type=F32)


def dot(lhs, rhs):
    return lax.dot_general(lhs, rhs, (((1,), (0,)), ((), ())), preferred_element_type=F32)


def products_kernel(
    main,
    dest_ref,
    leaf_ref,
    probes_hbm,
    basis_hbm,
    transfer_hbm,
    blocks_hbm,
    send_ref,
    probes_ref,
    basis_ref,
    transfer_ref,
    blocks_ref,
    tails,
    count,
    sems,
):
    devices = send_ref.shape[0]
    leaves, per_leaf, size = blocks_ref.shape[:3]
    columns, rank = probes_ref.shape[0], basis_ref.shape[1]
    copies = [
        pltpu.make_async_copy(probes_hbm, probes_ref, sems.at[0]),
        pltpu.make_async_copy(basis_hbm, basis_ref, sems.at[1]),
        pltpu.make_async_copy(transfer_hbm, transfer_ref, sems.at[2]),
    ] + [pltpu.make_async_copy(blocks_hbm.at[j], blocks_ref.at[j], sems.at[3 + j]) for j in range(leaves)]
    for copy in copies:
        copy.start()

    @pl.loop(0, devices)
    def _(i):
        count[i] = 0
        tails[i] = jnp.full(tails.shape[1:], leaves, F32)

    for copy in copies[:3]:
        copy.wait()
    box = jnp.zeros((columns, rank), F32)
    for j in range(leaves):
        coef = dot_t(probes_ref[:, j * size : (j + 1) * size], basis_ref[j]).astype(BF16)
        box += dot_t(coef, transfer_ref[j])
    half = main // 2
    packed = jnp.concatenate([box[:half], box[half:main]], axis=1).astype(BF16)
    last = jnp.concatenate([box[main:], jnp.zeros_like(box[main:])], axis=1)

    for j in range(leaves):
        copies[3 + j].wait()
        x = probes_ref[:, j * size : (j + 1) * size]
        for first in range(0, per_leaf, 4):
            many = min(4, per_leaf - first)
            rhs = blocks_ref[j, first : first + many].reshape(many * size, size)
            product = dot_t(x, rhs)
            for b in range(many):
                target = dest_ref[first + b, j]
                slot = count[target]
                count[target] = slot + 1
                block = product[:, b * size : (b + 1) * size]
                send_ref[target, pl.ds(pl.multiple_of(slot * main, TILE), main), :] = block[:main].astype(BF16)
                tails[target, pl.ds(slot, 1), :] = block[main:]
                tails[target, pl.ds(CAP + slot, 1), :] = jnp.full((1, size), leaf_ref[first + b, j], F32)

    @pl.loop(0, devices)
    def _(i):
        tails[i, 2 * CAP : 2 * CAP + 1, :] = last
        send_ref[i, CAP * main : CAP * main + TILE, :] = tails[i].astype(BF16)
        send_ref[i, CAP * main + TILE :, :] = packed


def local_kernel(probes_ref, local_ref, base_ref):
    leaves, size = local_ref.shape[0], local_ref.shape[2]
    for i in range(leaves):
        total = dot_t(probes_ref[:, :size], local_ref[i, 0])
        for c in range(1, leaves):
            total += dot_t(probes_ref[:, c * size : (c + 1) * size], local_ref[i, c])
        base_ref[:, i * size : (i + 1) * size] = total


def gather_kernel(
    main,
    leaf_ref,
    partner_ref,
    base_ref,
    incoming_ref,
    couplings_ref,
    transfer_ref,
    basis_ref,
    out_ref,
    total,
):
    columns, points = base_ref.shape
    leaves, rank, size = basis_ref.shape
    far = jnp.zeros((columns, rank), F32)
    for f in range(couplings_ref.shape[1]):
        source = partner_ref[0, f]
        packed = incoming_ref[source, CAP * main + TILE :, :]
        last = incoming_ref[source, CAP * main : CAP * main + TILE, :].astype(F32)[2 * CAP : 2 * CAP + 1, :rank]
        box = jnp.concatenate(
            [packed[:, :rank].astype(F32), packed[:, rank:].astype(F32), last], axis=0
        ).astype(BF16)
        far += dot_t(box, couplings_ref[0, f])
    far = far.astype(BF16)
    for j in range(leaves):
        down = dot(far, transfer_ref[j]).astype(BF16)
        cols = slice(j * size, (j + 1) * size)
        total[:, cols] = base_ref[:, cols] + dot(down, basis_ref[j])
    total[:, points:] = jnp.zeros((columns, size), F32)

    @pl.loop(0, incoming_ref.shape[0])
    def _(source):
        tail = incoming_ref[source, CAP * main : CAP * main + TILE, :].astype(F32)
        for slot in range(CAP):
            cols = pl.ds(pl.multiple_of(leaf_ref[source * CAP + slot] * size, size), size)
            total[:main, cols] += incoming_ref[source, slot * main : (slot + 1) * main, :].astype(F32)
            total[main:, cols] += tail[slot : slot + 1]

    out_ref[...] = total[:, :points]


def call(kernel, out_shape, in_specs, scratch, flops, nbytes, vmem):
    return pl.pallas_call(
        kernel,
        out_shape=out_shape,
        in_specs=in_specs,
        out_specs=VMEM,
        scratch_shapes=scratch,
        compiler_params=pltpu.CompilerParams(vmem_limit_bytes=vmem + 4 * 2**20),
        cost_estimate=pl.CostEstimate(flops=flops, bytes_accessed=nbytes, transcendentals=0),
    )


def per_device(
    probes, basis, transfer, local_blocks, remote_blocks, near_dest, near_leaf, couplings, far_list
):
    columns, points = probes.shape
    leaves, rank, size = basis.shape
    devices = lax.axis_size("leaf")
    main = columns // TILE * TILE
    depth = CAP * main + TILE + main // 2
    blocks = remote_blocks.shape[0] * remote_blocks.shape[1]
    unit = 2 * columns * size * size
    send_bytes = devices * depth * size * 2

    send = call(
        functools.partial(products_kernel, main),
        jax.ShapeDtypeStruct((devices, depth, size), BF16),
        [SMEM, SMEM, ANY, ANY, ANY, ANY],
        [
            pltpu.VMEM(probes.shape, BF16),
            pltpu.VMEM(basis.shape, BF16),
            pltpu.VMEM(transfer.shape, BF16),
            pltpu.VMEM(remote_blocks.shape, BF16),
            pltpu.VMEM((devices, TILE, size), F32),
            pltpu.SMEM((devices,), jnp.int32),
            pltpu.SemaphoreType.DMA((3 + leaves,)),
        ],
        blocks * unit,
        remote_blocks.size * 2 + send_bytes,
        remote_blocks.size * 2 + 2 * send_bytes,
    )(near_dest.T, near_leaf.T, probes, basis, transfer, remote_blocks)
    incoming = lax.all_to_all(send, "leaf", split_axis=0, concat_axis=0, tiled=True)

    base = call(
        local_kernel,
        jax.ShapeDtypeStruct((columns, points), F32),
        [VMEM, VMEM],
        [],
        leaves * leaves * unit,
        local_blocks.size * 2,
        2 * local_blocks.size,
    )(probes, local_blocks)

    slots = incoming[:, CAP * main + CAP : CAP * main + 2 * CAP, 0].astype(jnp.int32)
    return call(
        functools.partial(gather_kernel, main),
        jax.ShapeDtypeStruct((columns, points), F32),
        [SMEM, SMEM, VMEM, VMEM, VMEM, VMEM, VMEM],
        [pltpu.VMEM((columns, points + size), F32)],
        devices * CAP * columns * size,
        send_bytes,
        send_bytes + 4 * 2**20,
    )(slots.reshape(devices * CAP), far_list, base, incoming, couplings, transfer, basis)


def solution(mesh):
    placed = (
        P(None, ("grp", "leaf")),
        P(("grp", "leaf"), None, None),
        P(("grp", "leaf"), None, None),
        P(("grp", "leaf"), None, None, None),
        P(("grp", "leaf"), None, None, None),
        P(("grp", "leaf"), None),
        P(("grp", "leaf"), None),
        P(("grp", "leaf"), None, None, None),
        P(("grp", "leaf"), None),
    )
    return jax.shard_map(
        per_device, mesh=mesh, in_specs=placed, out_specs=P(None, ("grp", "leaf")), check_vma=False
    )
```

time: 56.8 us -> 54.9 us (0.967)
  the two profiles are of different devices: /device:TPU:11 before, /device:TPU:15 now
where the time goes in v2:
time: 54.9 us; the launch traced here: 54.4 us
  waiting for transfers between devices  26.9 us (49%)
  Pallas kernels  10.6 us (19%)
  local copies, waits for them, and re-layouts  9.82 us (18%)
  starting transfers between devices  6.71 us (12%)
    all_to_all x1, waiting for transfers between devices, per_device(): lax.all_to_all(send, 'leaf', split_axis=0, concat_axis=0, tiled=True)  26.9 us
    unnamed x28, local copies, waits for them, and re-layouts  9.73 us
    all_to_all x1, starting transfers between devices, per_device(): lax.all_to_all(send, 'leaf', split_axis=0, concat_axis=0, tiled=True)  6.71 us
    pallas_call x1, Pallas kernels, per_device(): call(functools.partial(products_kernel, main), jax.ShapeDtypeStruct((devi...  5.83 us
    pallas_call x1, Pallas kernels, per_device(): call(functools.partial(gather_kernel, main), jax.ShapeDtypeStruct((column...  3.25 us
    pallas_call x1, Pallas kernels, per_device(): call(local_kernel, jax.ShapeDtypeStruct((columns, points), F32), [VMEM, V...  1.52 us
  transfers between devices with their start and end apart: 1, of which 1 were waited for; matrix products, arithmetic and copies ran while one was open for 0% of the time, Pallas kernels for 3%

profile of v2, /device:TPU:15, one launch (start us, length us, event | category | flops | bytes accessed | tf_op | source)
XLA Modules:
  0.0 54.4 jit_solution(12058913037105420063)
XLA Ops:
  0.0 1.2 %copy-done.3 = bf16[8,4,128,128]{3,2,1,0:T(8,128)(2,1)S(1)} copy-done((bf16[8,4,128,128]{3,2,1,0:T(8,128)(2,1)S(1)}, bf16[8,4,128,128]{3,2,1,0:T(8,128)(2,1)}, u32[]{:S(2)}) %copy-start.3) | copy-done | bytes 1048600
  1.2 0.9 %copy-done.4 = bf16[65,1024]{1,0:T(8,128)(2,1)S(1)} copy-done((bf16[65,1024]{1,0:T(8,128)(2,1)S(1)}, bf16[65,1024]{1,0:T(8,128)(2,1)}, u32[]{:S(2)}) %copy-start.4) | copy-done | bytes 133144
  2.1 0.9 %copy-done.6 = bf16[8,64,128]{2,1,0:T(8,128)(2,1)S(1)} copy-done((bf16[8,64,128]{2,1,0:T(8,128)(2,1)S(1)}, bf16[8,64,128]{2,1,0:T(8,128)(2,1)}, u32[]{:S(2)}) %copy-start.6) | copy-done | bytes 131096
  3.0 0.9 %copy-done.8 = bf16[8,64,64]{2,1,0:T(8,128)(2,1)S(1)} copy-done((bf16[8,64,64]{2,1,0:T(8,128)(2,1)S(1)}, bf16[8,64,64]{2,1,0:T(8,128)(2,1)}, u32[]{:S(2)}) %copy-start.8) | copy-done | bytes 65560
  3.9 0.7 %copy-done.11 = s32[8,4]{0,1:T(4,128)S(1)} copy-done((s32[8,4]{0,1:T(4,128)S(1)}, s32[8,4]{0,1:T(4,128)}, u32[]{:S(2)}) %copy-start.11) | copy-done | bytes 152
  4.6 0.7 %copy-done.12 = s32[8,4]{0,1:T(4,128)S(1)} copy-done((s32[8,4]{0,1:T(4,128)S(1)}, s32[8,4]{0,1:T(4,128)}, u32[]{:S(2)}) %copy-start.12) | copy-done | bytes 152
  5.3 5.8 %shard_map.91 = bf16[16,304,128]{2,1,0:T(8,128)(2,1)} custom-call(s32[4,8]{1,0:T(4,128)S(1)} %bitcast.2, s32[4,8]{1,0:T(4,128)S(1)} %bitcast.3, bf16[65,1024]{1,0:T(8,128)(2,1)S(1)} %copy-done.4, bf16[8,64,128]{2,1,0:T(8,128)(2,1)S(1)} %copy-done.6, bf16[8,64,64]{2,1,0:T(8,128)(2,1)S(1)} %copy-done.8, bf16[8,4,128,128]{3,2,1,0:T(8,128)(2,1)S(1)} %copy-done.3), custom_call_target="tpu_custom_call" | custom-call | flops 68157440 | bytes 2293760 | tf_op jit(solution)/shard_map/pallas_call | solution.py:169
  11.1 0.0 copy-start
  11.2 0.0 copy-start.5
  11.2 6.7 %all-to-all-start = ((bf16[16,304,128]{2,1,0:T(8,128)(2,1)}), bf16[16,304,128]{2,1,0:T(8,128)(2,1)S(1)}, u32[]{:S(2)}, u32[]{:S(2)}) async-start(bf16[16,304,128]{2,1,0:T(8,128)(2,1)} %shard_map.91), calls=%async_computation | async-start | bytes 2490368 | tf_op jit(solution)/shard_map/all_to_all | solution.py:186
  17.9 0.0 copy-done
  17.9 0.0 copy-start.13
  17.9 1.5 %shard_map.92.base_ref = f32[65,1024]{1,0:T(8,128)S(1)} custom-call(bf16[65,1024]{1,0:T(8,128)(2,1)S(1)} %copy-done.5, bf16[8,8,128,128]{3,2,1,0:T(8,128)(2,1)S(1)} %copy-done), custom_call_target="tpu_custom_call" | custom-call | flops 136314880 | bytes 2097152 | tf_op jit(solution)/shard_map/pallas_call | solution.py:188
  19.4 0.0 copy-start.1
  19.4 0.7 %copy-done.1 = f32[65,1024]{1,0:T(8,128)} copy-done((f32[65,1024]{1,0:T(8,128)}, f32[65,1024]{1,0:T(8,128)S(1)}, u32[]{:S(2)}) %copy-start.1) | copy-done | bytes 266264
  20.1 26.9 %all-to-all-done.incoming_ref = bf16[16,304,128]{2,1,0:T(8,128)(2,1)S(1)} async-done(((bf16[16,304,128]{2,1,0:T(8,128)(2,1)}), bf16[16,304,128]{2,1,0:T(8,128)(2,1)S(1)}, u32[]{:S(2)}, u32[]{:S(2)}) %all-to-all-start) | async-done | bytes 1245216 | tf_op jit(solution)/shard_map/all_to_all | solution.py:186
  47.0 0.3 convert_reduce_fusion
  47.4 0.1 reshape.4.leaf_ref
  47.5 0.0 copy-start.2
  47.5 1.0 %copy-done.2 = f32[65,1024]{1,0:T(8,128)S(1)} copy-done((f32[65,1024]{1,0:T(8,128)S(1)}, f32[65,1024]{1,0:T(8,128)}, u32[]{:S(2)}) %copy-start.2) | copy-done | bytes 266264
  48.5 0.9 %copy-done.7 = bf16[8,64,128]{2,1,0:T(8,128)(2,1)S(1)} copy-done((bf16[8,64,128]{2,1,0:T(8,128)(2,1)S(1)}, bf16[8,64,128]{2,1,0:T(8,128)(2,1)}, u32[]{:S(2)}) %copy-start.7) | copy-done | bytes 131096
  49.4 0.9 %copy-done.9 = bf16[8,64,64]{2,1,0:T(8,128)(2,1)S(1)} copy-done((bf16[8,64,64]{2,1,0:T(8,128)(2,1)S(1)}, bf16[8,64,64]{2,1,0:T(8,128)(2,1)}, u32[]{:S(2)}) %copy-start.9) | copy-done | bytes 65560
  50.3 0.9 %copy-done.10 = bf16[1,12,64,64]{3,2,1,0:T(8,128)(2,1)S(1)} copy-done((bf16[1,12,64,64]{3,2,1,0:T(8,128)(2,1)S(1)}, bf16[1,12,64,64]{3,2,1,0:T(8,128)(2,1)}, u32[]{:S(2)}) %copy-start.10) | copy-done | bytes 98328
  51.2 3.3 %shard_map.93 = f32[65,1024]{1,0:T(8,128)} custom-call(s32[64]{0:T(128)S(1)} %reshape.4.leaf_ref, s32[1,12]{1,0:T(1,128)S(1)} %copy-done.13, f32[65,1024]{1,0:T(8,128)S(1)} %copy-done.2, bf16[16,304,128]{2,1,0:T(8,128)(2,1)S(1)} %all-to-all-done.incoming_ref, bf16[1,12,64,64]{3,2,1,0:T(8,128)(2,1)S(1)} %copy-done.10, bf16[8,64,64]{2,1,0:T(8,128)(2,1)S(1)} %copy-done.9, ...), custom_call_target="tpu_custom_call" | custom-call | flops 532480 | bytes 1245184 | tf_op jit(solution)/shard_map/pallas_call | solution.py:199
  (11 shorter events, 0.0 us)
Async XLA Ops:
  0.0 1.2 %copy-start.3 = (bf16[8,4,128,128]{3,2,1,0:T(8,128)(2,1)S(1)}, bf16[8,4,128,128]{3,2,1,0:T(8,128)(2,1)}, u32[]{:S(2)}) copy-start(bf16[8,4,128,128]{3,2,1,0:T(8,128)(2,1)} %blocks_hbm.1) | copy-start | bytes 3145732
  1.2 0.9 %copy-start.4 = (bf16[65,1024]{1,0:T(8,128)(2,1)S(1)}, bf16[65,1024]{1,0:T(8,128)(2,1)}, u32[]{:S(2)}) copy-start(bf16[65,1024]{1,0:T(8,128)(2,1)} %probes_ref.1) | copy-start | bytes 399364
  2.1 0.9 %copy-start.6 = (bf16[8,64,128]{2,1,0:T(8,128)(2,1)S(1)}, bf16[8,64,128]{2,1,0:T(8,128)(2,1)}, u32[]{:S(2)}) copy-start(bf16[8,64,128]{2,1,0:T(8,128)(2,1)} %basis_ref.1) | copy-start | bytes 393220
  3.0 0.9 %copy-start.8 = (bf16[8,64,64]{2,1,0:T(8,128)(2,1)S(1)}, bf16[8,64,64]{2,1,0:T(8,128)(2,1)}, u32[]{:S(2)}) copy-start(bf16[8,64,64]{2,1,0:T(8,128)(2,1)} %transfer_ref.1) | copy-start | bytes 196612
  3.9 0.7 %copy-start.11 = (s32[8,4]{0,1:T(4,128)S(1)}, s32[8,4]{0,1:T(4,128)}, u32[]{:S(2)}) copy-start(s32[8,4]{0,1:T(4,128)} %param.14) | copy-start | bytes 388
  4.6 0.7 %copy-start.12 = (s32[8,4]{0,1:T(4,128)S(1)}, s32[8,4]{0,1:T(4,128)}, u32[]{:S(2)}) copy-start(s32[8,4]{0,1:T(4,128)} %param.15) | copy-start | bytes 388
  11.1 6.7 %copy-start = (bf16[8,8,128,128]{3,2,1,0:T(8,128)(2,1)S(1)}, bf16[8,8,128,128]{3,2,1,0:T(8,128)(2,1)}, u32[]{:S(2)}) copy-start(bf16[8,8,128,128]{3,2,1,0:T(8,128)(2,1)} %local_ref.1) | copy-start | bytes 6291460
  11.2 6.7 %copy-start.5 = (bf16[65,1024]{1,0:T(8,128)(2,1)S(1)}, bf16[65,1024]{1,0:T(8,128)(2,1)}, u32[]{:S(2)}) copy-start(bf16[65,1024]{1,0:T(8,128)(2,1)} %probes_ref.1) | copy-start | bytes 399364
  11.2 35.9 %all-to-all-start = ((bf16[16,304,128]{2,1,0:T(8,128)(2,1)}), bf16[16,304,128]{2,1,0:T(8,128)(2,1)S(1)}, u32[]{:S(2)}, u32[]{:S(2)}) async-start(bf16[16,304,128]{2,1,0:T(8,128)(2,1)} %shard_map.91), calls=%async_computation | async-start | bytes 2490368 | tf_op jit(solution)/shard_map/all_to_all | solution.py:186
  17.9 29.6 %copy-start.13 = (s32[1,12]{1,0:T(1,128)S(1)}, s32[1,12]{1,0:T(1,128)}, u32[]{:S(2)}) copy-start(s32[1,12]{1,0:T(1,128)} %partner_ref.1) | copy-start | bytes 148
  19.4 0.7 %copy-start.1 = (f32[65,1024]{1,0:T(8,128)}, f32[65,1024]{1,0:T(8,128)S(1)}, u32[]{:S(2)}) copy-start(f32[65,1024]{1,0:T(8,128)S(1)} %shard_map.92.base_ref) | copy-start | bytes 798724
  47.5 1.0 %copy-start.2 = (f32[65,1024]{1,0:T(8,128)S(1)}, f32[65,1024]{1,0:T(8,128)}, u32[]{:S(2)}) copy-start(f32[65,1024]{1,0:T(8,128)} %copy-done.1) | copy-start | bytes 798724
  48.5 0.9 %copy-start.7 = (bf16[8,64,128]{2,1,0:T(8,128)(2,1)S(1)}, bf16[8,64,128]{2,1,0:T(8,128)(2,1)}, u32[]{:S(2)}) copy-start(bf16[8,64,128]{2,1,0:T(8,128)(2,1)} %basis_ref.1) | copy-start | bytes 393220
  49.4 0.9 %copy-start.9 = (bf16[8,64,64]{2,1,0:T(8,128)(2,1)S(1)}, bf16[8,64,64]{2,1,0:T(8,128)(2,1)}, u32[]{:S(2)}) copy-start(bf16[8,64,64]{2,1,0:T(8,128)(2,1)} %transfer_ref.1) | copy-start | bytes 196612
  50.3 0.9 %copy-start.10 = (bf16[1,12,64,64]{3,2,1,0:T(8,128)(2,1)S(1)}, bf16[1,12,64,64]{3,2,1,0:T(8,128)(2,1)}, u32[]{:S(2)}) copy-start(bf16[1,12,64,64]{3,2,1,0:T(8,128)(2,1)} %couplings_ref.1) | copy-start | bytes 294916

commit v3 on v1

v3 whole, which is shorter than its diff:
```python
import functools

import jax
import jax.numpy as jnp
from jax import lax
from jax.experimental import pallas as pl
from jax.experimental.pallas import tpu as pltpu
from jax.sharding import PartitionSpec as P

TILE = 16

F32 = jnp.float32
BF16 = jnp.bfloat16

VMEM = pl.BlockSpec(memory_space=pltpu.VMEM)
SMEM = pl.BlockSpec(memory_space=pltpu.SMEM)
HBM = pl.BlockSpec(memory_space=pl.ANY)


def dot_t(lhs, rhs):
    return lax.dot_general(lhs, rhs, (((1,), (1,)), ((), ())), preferred_element_type=F32)


def dot(lhs, rhs):
    return lax.dot_general(lhs, rhs, (((1,), (0,)), ((), ())), preferred_element_type=F32)


def fetch(pairs, sems):
    copies = [pltpu.make_async_copy(src, dst, sems.at[i]) for i, (src, dst) in enumerate(pairs)]
    for copy in copies:
        copy.start()
    return copies


def box_kernel(probes_hbm, basis_hbm, transfer_hbm, box_ref, probes_ref, basis_ref, transfer_ref, sems):
    copies = fetch(
        [(probes_hbm, probes_ref), (basis_hbm, basis_ref), (transfer_hbm, transfer_ref)], sems
    )
    for copy in copies:
        copy.wait()
    leaves, rank, size = basis_ref.shape
    box = jnp.zeros(box_ref.shape, F32)
    for j in range(leaves):
        coef = dot_t(probes_ref[:, j * size : (j + 1) * size], basis_ref[j]).astype(BF16)
        box += dot_t(coef, transfer_ref[j])
    box_ref[...] = box.astype(BF16)


def products_kernel(
    main, dest_ref, leaf_ref, probes_hbm, blocks_hbm, send_ref, probes_ref, blocks_ref, tails, sems
):
    devices = send_ref.shape[0]
    leaves, per_leaf, size = blocks_ref.shape[:3]
    copies = fetch(
        [(probes_hbm, probes_ref)] + [(blocks_hbm.at[j], blocks_ref.at[j]) for j in range(leaves)], sems
    )

    @pl.loop(0, devices)
    def _(i):
        send_ref[i] = jnp.zeros(send_ref.shape[1:], BF16)
        tails[i] = jnp.zeros(tails.shape[1:], F32)

    copies[0].wait()
    for j in range(leaves):
        copies[1 + j].wait()
        x = probes_ref[:, j * size : (j + 1) * size]
        for first in range(0, per_leaf, 4):
            many = min(4, per_leaf - first)
            rhs = blocks_ref[j, first : first + many].reshape(many * size, size)
            product = dot_t(x, rhs)
            for b in range(many):
                target = dest_ref[first + b, j]
                row = leaf_ref[first + b, j]
                block = product[:, b * size : (b + 1) * size]
                send_ref[target, pl.ds(pl.multiple_of(row * main, TILE), main), :] = block[:main].astype(BF16)
                tails[target, pl.ds(row, 1), :] = block[main:]

    @pl.loop(0, devices)
    def _(i):
        send_ref[i, leaves * main :, :] = tails[i].astype(BF16)


def local_kernel(probes_hbm, local_hbm, base_ref, probes_ref, local_ref, sems):
    leaves, size = local_ref.shape[0], local_ref.shape[2]
    copies = fetch(
        [(probes_hbm, probes_ref)] + [(local_hbm.at[i], local_ref.at[i]) for i in range(leaves)], sems
    )
    copies[0].wait()
    for i in range(leaves):
        copies[1 + i].wait()
        total = dot_t(probes_ref[:, :size], local_ref[i, 0])
        for c in range(1, leaves):
            total += dot_t(probes_ref[:, c * size : (c + 1) * size], local_ref[i, c])
        base_ref[:, i * size : (i + 1) * size] = total


def far_kernel(
    partner_ref,
    base_ref,
    boxes_ref,
    couplings_hbm,
    transfer_hbm,
    basis_hbm,
    out_ref,
    couplings_ref,
    transfer_ref,
    basis_ref,
    sems,
):
    copies = fetch(
        [(couplings_hbm, couplings_ref), (transfer_hbm, transfer_ref), (basis_hbm, basis_ref)], sems
    )
    for copy in copies:
        copy.wait()
    leaves, rank, size = basis_ref.shape
    columns = base_ref.shape[0]
    far = jnp.zeros((columns, rank), F32)
    for f in range(couplings_ref.shape[1]):
        far += dot_t(boxes_ref[partner_ref[0, f]], couplings_ref[0, f])
    far = far.astype(BF16)
    for j in range(leaves):
        down = dot(far, transfer_ref[j]).astype(BF16)
        cols = slice(j * size, (j + 1) * size)
        out_ref[:, cols] = base_ref[:, cols] + dot(down, basis_ref[j])


def add_kernel(main, base_ref, near_ref, out_ref):
    columns, points = base_ref.shape
    size = near_ref.shape[1]
    leaves = points // size
    tail = near_ref[leaves * main :, :].astype(F32)
    for j in range(leaves):
        cols = slice(j * size, (j + 1) * size)
        out_ref[:main, cols] = base_ref[:main, cols] + near_ref[j * main : (j + 1) * main, :].astype(F32)
        out_ref[main:, cols] = base_ref[main:, cols] + tail[j : j + 1]


def call(kernel, out_shape, in_specs, scratch, flops, nbytes):
    return pl.pallas_call(
        kernel,
        out_shape=out_shape,
        in_specs=in_specs,
        out_specs=VMEM,
        scratch_shapes=scratch,
        cost_estimate=pl.CostEstimate(flops=flops, bytes_accessed=nbytes, transcendentals=0),
    )


def per_device(
    probes, basis, transfer, local_blocks, remote_blocks, near_dest, near_leaf, couplings, far_list
):
    columns, points = probes.shape
    leaves, rank, size = basis.shape
    devices = lax.axis_size("leaf")
    main = columns // TILE * TILE
    depth = leaves * main + TILE
    blocks = remote_blocks.shape[0] * remote_blocks.shape[1]
    unit = 2 * columns * size * size
    send_bytes = devices * depth * size * 2
    scratch = lambda *arrays: [pltpu.VMEM(a.shape, a.dtype) for a in arrays]

    box = call(
        box_kernel,
        jax.ShapeDtypeStruct((columns, rank), BF16),
        [HBM, HBM, HBM],
        scratch(probes, basis, transfer) + [pltpu.SemaphoreType.DMA((3,))],
        2 * leaves * unit,
        basis.size * 2 + transfer.size * 2,
    )(probes, basis, transfer)
    boxes = lax.all_gather(box[None], "leaf", axis=0, tiled=True)

    send = call(
        functools.partial(products_kernel, main),
        jax.ShapeDtypeStruct((devices, depth, size), BF16),
        [SMEM, SMEM, HBM, HBM],
        scratch(probes, remote_blocks)
        + [pltpu.VMEM((devices, TILE, size), F32), pltpu.SemaphoreType.DMA((1 + leaves,))],
        blocks * unit,
        remote_blocks.size * 2 + send_bytes,
    )(near_dest.T, near_leaf.T, probes, remote_blocks)
    near = lax.psum_scatter(send, "leaf", scatter_dimension=0, tiled=True)[0]

    base = call(
        local_kernel,
        jax.ShapeDtypeStruct((columns, points), F32),
        [HBM, HBM],
        scratch(probes, local_blocks) + [pltpu.SemaphoreType.DMA((1 + leaves,))],
        leaves * leaves * unit,
        local_blocks.size * 2,
    )(probes, local_blocks)
    base = call(
        far_kernel,
        jax.ShapeDtypeStruct((columns, points), F32),
        [SMEM, VMEM, VMEM, HBM, HBM, HBM],
        scratch(couplings, transfer, basis) + [pltpu.SemaphoreType.DMA((3,))],
        4 * leaves * unit,
        couplings.size * 2 + boxes.size * 2,
    )(far_list, base, boxes, couplings, transfer, basis)

    return call(
        functools.partial(add_kernel, main),
        jax.ShapeDtypeStruct((columns, points), F32),
        [VMEM, VMEM],
        [],
        columns * points,
        depth * size * 2,
    )(base, near)


def solution(mesh):
    placed = (
        P(None, ("grp", "leaf")),
        P(("grp", "leaf"), None, None),
        P(("grp", "leaf"), None, None),
        P(("grp", "leaf"), None, None, None),
        P(("grp", "leaf"), None, None, None),
        P(("grp", "leaf"), None),
        P(("grp", "leaf"), None),
        P(("grp", "leaf"), None, None, None),
        P(("grp", "leaf"), None),
    )
    return jax.shard_map(
        per_device, mesh=mesh, in_specs=placed, out_specs=P(None, ("grp", "leaf")), check_vma=False
    )
```

time: 56.8 us -> 84.7 us (1.49)
  the two profiles are of different devices: /device:TPU:11 before, /device:TPU:0 now
where the time goes in v3:
time: 84.7 us; the launch traced here: 84.4 us
  waiting for transfers between devices  27.5 us (32%)
  blocking collectives  23.8 us (28%)
  Pallas kernels  17.9 us (21%)
  between operations  13.4 us (16%)
  local copies, waits for them, and re-layouts  1.73 us (2%)
    reduce_scatter x1, waiting for transfers between devices, per_device(): near = lax.psum_scatter(send, 'leaf', scatter_dimension=0, tiled=True)[0]  27.5 us
    all_gather x1, blocking collectives, per_device(): boxes = lax.all_gather(box[None], 'leaf', axis=0, tiled=True)  23.8 us
    pallas_call x1, Pallas kernels, per_device(): call(local_kernel, jax.ShapeDtypeStruct((columns, points), F32), [HBM, HB...  5.05 us
    pallas_call x1, Pallas kernels, per_device(): call(functools.partial(products_kernel, main), jax.ShapeDtypeStruct((devi...  4.65 us
    pallas_call x1, Pallas kernels, per_device(): call(far_kernel, jax.ShapeDtypeStruct((columns, points), F32), [SMEM, VME...  4.34 us
    pallas_call x1, Pallas kernels, per_device(): call(box_kernel, jax.ShapeDtypeStruct((columns, rank), BF16), [HBM, HBM,...  2.11 us
    pallas_call x1, Pallas kernels, per_device(): call(functools.partial(add_kernel, main), jax.ShapeDtypeStruct((columns,...  1.74 us
  transfers between devices with their start and end apart: 1, of which 1 were waited for; matrix products, arithmetic and copies ran while one was open for 2% of the time, Pallas kernels for 14%

profile of v3, /device:TPU:0, one launch (start us, length us, event | category | flops | bytes accessed | tf_op | source)
XLA Modules:
  0.0 84.4 jit_solution(8674462187882137207)
XLA Ops:
  6.5 0.0 reduce-scatter.2.cloned.1.call-start
  6.5 4.6 %shard_map.94 = bf16[16,528,128]{2,1,0:T(8,128)(2,1)} custom-call(s32[4,8]{1,0:T(4,128)} %bitcast.6, s32[4,8]{1,0:T(4,128)} %bitcast.7, bf16[65,1024]{1,0:T(8,128)(2,1)} %probes_hbm.5, bf16[8,4,128,128]{3,2,1,0:T(8,128)(2,1)} %blocks_hbm.1), custom_call_target="tpu_custom_call" | custom-call | flops 68157440 | bytes 3211264 | tf_op jit(solution)/shard_map/pallas_call | solution.py:172
  11.2 0.0 reduce-scatter.2.cloned.1.call-update
  11.2 2.1 %shard_map.92 = bf16[65,64]{1,0:T(8,128)(2,1)} custom-call(bf16[65,1024]{1,0:T(8,128)(2,1)} %probes_hbm.5, bf16[8,64,128]{2,1,0:T(8,128)(2,1)} %basis_hbm.3, bf16[8,64,64]{2,1,0:T(8,128)(2,1)} %transfer_hbm.3), custom_call_target="tpu_custom_call" | custom-call | flops 34078720 | bytes 196608 | tf_op jit(solution)/shard_map/pallas_call | solution.py:162
  13.3 0.8 copy.10
  14.2 23.8 %all-gather.1 = bf16[16,65,64]{1,2,0:T(8,128)(2,1)S(1)} all-gather(bf16[1,65,64]{1,2,0:T(8,128)(2,1)S(1)} %copy.10), channel_id=2, replica_groups=mesh['grp'=2,'leaf'=16] {'leaf'}, dimensions={0}, use_global_device_ids=true | all-gather | bytes 141440 | tf_op jit(solution)/shard_map/all_gather | solution.py:170
  38.0 0.9 %copy.11.boxes_ref = bf16[16,65,64]{2,1,0:T(8,128)(2,1)} copy(bf16[16,65,64]{1,2,0:T(8,128)(2,1)S(1)} %all-gather.1) | data formatting | bytes 266240 | tf_op jit(solution)/shard_map/all_gather | solution.py:170
  38.9 5.1 %shard_map.91.base_ref = f32[65,1024]{1,0:T(8,128)} custom-call(bf16[65,1024]{1,0:T(8,128)(2,1)} %probes_hbm.5, bf16[8,8,128,128]{3,2,1,0:T(8,128)(2,1)} %local_hbm.1), custom_call_target="tpu_custom_call" | custom-call | flops 136314880 | bytes 2097152 | tf_op jit(solution)/shard_map/pallas_call | solution.py:183
  43.9 4.3 %shard_map.93.base_ref = f32[65,1024]{1,0:T(8,128)} custom-call(s32[1,12]{1,0:T(1,128)} %partner_ref.1, f32[65,1024]{1,0:T(8,128)} %shard_map.91.base_ref, bf16[16,65,64]{2,1,0:T(8,128)(2,1)} %copy.11.boxes_ref, bf16[1,12,64,64]{3,2,1,0:T(8,128)(2,1)} %couplings_hbm.1, bf16[8,64,64]{2,1,0:T(8,128)(2,1)} %transfer_hbm.3, bf16[8,64,128]{2,1,0:T(8,128)(2,1)} %basis_hbm.3), custom_call_target="tpu_custom_call" | custom-call | flops 68157440 | bytes 231424 | tf_op jit(solution)/shard_map/pallas_call | solution.py:191
  48.3 27.5 %reduce-scatter.2.cloned.1.call-done = bf16[1,528,128]{2,1,0:T(8,128)(2,1)} async-done(((bf16[16,528,128]{2,1,0:T(8,128)(2,1)}), bf16[1,528,128]{2,1,0:T(8,128)(2,1)}) %reduce-scatter.2.cloned.1.call-update) | async-done | bytes 135184 | tf_op jit(solution)/shard_map/reduce_scatter | solution.py:181
  75.8 1.7 %shard_map.95 = f32[65,1024]{1,0:T(8,128)} custom-call(f32[65,1024]{1,0:T(8,128)} %shard_map.93.base_ref, bf16[528,128]{1,0:T(8,128)(2,1)} %bitcast.4), custom_call_target="tpu_custom_call" | custom-call | flops 66560 | bytes 135168 | tf_op jit(solution)/shard_map/pallas_call | solution.py:200
Async XLA Ops:
  6.5 69.3 %reduce-scatter.2.cloned.1.call-start = ((), (), s32[]{:S(2)}) async-start(), calls=%async_computation.1 | async-start | bytes 2297856 | tf_op jit(solution)/shard_map/reduce_scatter | solution.py:181
Sparse Core Ops, SparseCore 0:
  11.3 64.4 reduce-scatter.1

commit v4 on v2

v4 whole, which is shorter than its diff:
```python
import functools

import jax
import jax.numpy as jnp
from jax import lax
from jax.experimental import pallas as pl
from jax.experimental.pallas import tpu as pltpu
from jax.sharding import PartitionSpec as P

CAP = 4
TILE = 16
LANES = 128
DIRECT = 16

F32 = jnp.float32
BF16 = jnp.bfloat16
I32 = jnp.int32

ANY = pl.BlockSpec(memory_space=pl.ANY)
VMEM = pl.BlockSpec(memory_space=pltpu.VMEM)


def dot_t(lhs, rhs):
    return lax.dot_general(lhs, rhs, (((1,), (1,)), ((), ())), preferred_element_type=F32)


def dot(lhs, rhs):
    return lax.dot_general(lhs, rhs, (((1,), (0,)), ((), ())), preferred_element_type=F32)


class Copies:
    def __init__(self, sems):
        self.sems, self.used = sems, 0

    def start(self, src, dst):
        copy = pltpu.make_async_copy(src, dst, self.sems.at[self.used])
        self.used += 1
        copy.start()
        return copy


def relative(devices):
    return devices <= DIRECT


def place(device, devices):
    return jnp.bitwise_xor(device, lax.axis_index("leaf")) if relative(devices) else device


def products_kernel(main, devices, *refs):
    dest_hbm, leaf_hbm, probes_hbm, basis_hbm, transfer_hbm, blocks_hbm = refs[:6]
    outs = refs[6:-10]
    dest_ref, leaf_ref, probes_ref, basis_ref, transfer_ref, blocks_ref, send_ref, tails, count, sems = refs[-10:]
    leaves, per_leaf, size = blocks_ref.shape[:3]
    columns, rank = probes_ref.shape[0], basis_ref.shape[1]
    copies = Copies(sems)
    early = [
        copies.start(probes_hbm, probes_ref),
        copies.start(basis_hbm, basis_ref),
        copies.start(transfer_hbm, transfer_ref),
        copies.start(dest_hbm, dest_ref),
        copies.start(leaf_hbm, leaf_ref),
    ]
    arrivals = [copies.start(blocks_hbm.at[j], blocks_ref.at[j]) for j in range(leaves)]

    @pl.loop(0, devices)
    def _(i):
        count[i] = 0
        tails[i] = jnp.full(tails.shape[1:], leaves, F32)

    for copy in early:
        copy.wait()
    box = jnp.zeros((columns, rank), F32)
    for j in range(leaves):
        coef = dot_t(probes_ref[:, j * size : (j + 1) * size], basis_ref[j]).astype(BF16)
        box += dot_t(coef, transfer_ref[j])
    half = main // 2
    packed = jnp.concatenate([box[:half], box[half:main]], axis=1).astype(BF16)
    last = jnp.concatenate([box[main:], jnp.zeros_like(box[main:])], axis=1)

    lane = lax.broadcasted_iota(I32, (1, size), 1)
    for j in range(leaves):
        arrivals[j].wait()
        x = probes_ref[:, j * size : (j + 1) * size]
        for first in range(0, per_leaf, 4):
            many = min(4, per_leaf - first)
            rhs = blocks_ref[j, first : first + many].reshape(many * size, size)
            product = dot_t(x, rhs)
            for b in range(many):
                target = place(dest_ref[first + b, j], devices)
                slot = count[target]
                count[target] = slot + 1
                block = product[:, b * size : (b + 1) * size]
                send_ref[target, pl.ds(pl.multiple_of(slot * main, TILE), main), :] = block[:main].astype(BF16)
                tails[target, pl.ds(slot, 1), :] = block[main:]
                number = leaf_ref[first + b, j].astype(F32)
                tails[target, CAP : CAP + 1, :] = jnp.where(lane == slot, number, tails[target, CAP : CAP + 1, :])

    @pl.loop(0, devices)
    def _(i):
        tails[i, CAP + 1 : CAP + 2, :] = last
        send_ref[i, CAP * main : CAP * main + TILE, :] = tails[i].astype(BF16)
        send_ref[i, CAP * main + TILE :, :] = packed

    leaving = []
    for m in order(devices):
        out = outs[m] if relative(devices) else outs[0].at[m]
        leaving.append(copies.start(send_ref.at[m], out))
    for copy in leaving:
        copy.wait()


def order(devices):
    return sorted(range(devices), reverse=True)


def local_kernel(probes_hbm, local_hbm, base_ref, probes_ref, local_ref, sems):
    leaves, size = local_ref.shape[0], local_ref.shape[2]
    copies = Copies(sems)
    early = copies.start(probes_hbm, probes_ref)
    arrivals = [copies.start(local_hbm.at[i], local_ref.at[i]) for i in range(leaves)]
    early.wait()
    for i in range(leaves):
        arrivals[i].wait()
        total = dot_t(probes_ref[:, :size], local_ref[i, 0])
        for c in range(1, leaves):
            total += dot_t(probes_ref[:, c * size : (c + 1) * size], local_ref[i, c])
        base_ref[:, i * size : (i + 1) * size] = total


def gather_kernel(main, devices, *refs):
    partner_hbm, base_hbm, couplings_hbm, transfer_hbm, basis_hbm = refs[:5]
    parts = refs[5:-11]
    out_ref, partner_ref, couplings_ref, transfer_ref, basis_ref, incoming_ref, meta, leaf_ref, total, sems, late = (
        refs[-11:]
    )
    columns = out_ref.shape[0]
    leaves, rank, size = basis_ref.shape
    points = leaves * size
    edge = CAP * main
    copies = Copies(sems)
    part = lambda m: parts[m] if relative(devices) else parts[0].at[m]
    small = [
        copies.start(part(m).at[pl.ds(edge, incoming_ref.shape[1] - edge)], incoming_ref.at[m, pl.ds(edge, incoming_ref.shape[1] - edge)])
        for m in range(devices)
    ]
    weights = [
        copies.start(partner_hbm, partner_ref),
        copies.start(couplings_hbm, couplings_ref),
        copies.start(transfer_hbm, transfer_ref),
        copies.start(basis_hbm, basis_ref),
        copies.start(base_hbm, total.at[:, pl.ds(0, points)]),
    ]
    large = [copies.start(part(m).at[pl.ds(0, edge)], incoming_ref.at[m, pl.ds(0, edge)]) for m in range(devices)]

    for m in range(devices):
        small[m].wait()
        meta[m : m + 1, :] = incoming_ref[m, edge : edge + TILE, :].astype(F32)[CAP : CAP + 1].astype(I32)
    numbers = pltpu.make_async_copy(meta, leaf_ref, late)
    numbers.start()

    for copy in weights:
        copy.wait()
    total[:, points:] = jnp.zeros((columns, size), F32)
    far = jnp.zeros((columns, rank), F32)
    for f in range(couplings_ref.shape[1]):
        source = place(partner_ref[0, f], devices)
        packed = incoming_ref[source, edge + TILE :, :]
        last = incoming_ref[source, edge : edge + TILE, :].astype(F32)[CAP + 1 : CAP + 2, :rank]
        box = jnp.concatenate(
            [packed[:, :rank].astype(F32), packed[:, rank:].astype(F32), last], axis=0
        ).astype(BF16)
        far += dot_t(box, couplings_ref[0, f])
    far = far.astype(BF16)
    for j in range(leaves):
        down = dot(far, transfer_ref[j]).astype(BF16)
        total[:, j * size : (j + 1) * size] += dot(down, basis_ref[j])

    numbers.wait()
    for copy in large:
        copy.wait()

    @pl.loop(0, devices)
    def _(m):
        tail = incoming_ref[m, edge : edge + TILE, :].astype(F32)
        for slot in range(CAP):
            cols = pl.ds(pl.multiple_of(leaf_ref[m, slot] * size, size), size)
            total[:main, cols] += incoming_ref[m, slot * main : (slot + 1) * main, :].astype(F32)
            total[main:, cols] += tail[slot : slot + 1]

    out_ref[...] = total[:, :points]


def call(kernel, out_shape, out_specs, operands, scratch, flops, nbytes):
    return pl.pallas_call(
        kernel,
        out_shape=out_shape,
        in_specs=[ANY] * len(operands),
        out_specs=out_specs,
        scratch_shapes=scratch,
        cost_estimate=pl.CostEstimate(flops=flops, bytes_accessed=nbytes, transcendentals=0),
    )(*operands)


def per_device(
    probes, basis, transfer, local_blocks, remote_blocks, near_dest, near_leaf, couplings, far_list
):
    columns, points = probes.shape
    leaves, rank, size = basis.shape
    devices = lax.axis_size("leaf")
    main = columns // TILE * TILE
    depth = CAP * main + TILE + main // 2
    blocks = remote_blocks.shape[0] * remote_blocks.shape[1]
    unit = 2 * columns * size * size
    send_bytes = devices * depth * size * 2
    like = lambda *arrays: [pltpu.VMEM(a.shape, a.dtype) for a in arrays]
    numbers = lambda *arrays: [pltpu.SMEM(a.shape, a.dtype) for a in arrays]
    sems = lambda count: [pltpu.SemaphoreType.DMA((count,))]

    if relative(devices):
        outgoing = [jax.ShapeDtypeStruct((depth, size), BF16)] * devices
    else:
        outgoing = [jax.ShapeDtypeStruct((devices, depth, size), BF16)]
    dest, leaf = near_dest.T, near_leaf.T
    send = call(
        functools.partial(products_kernel, main, devices),
        outgoing,
        [ANY] * len(outgoing),
        (dest, leaf, probes, basis, transfer, remote_blocks),
        numbers(dest, leaf)
        + like(probes, basis, transfer, remote_blocks)
        + [
            pltpu.VMEM((devices, depth, size), BF16),
            pltpu.VMEM((devices, TILE, size), F32),
            pltpu.SMEM((devices,), I32),
        ]
        + sems(5 + leaves + devices),
        blocks * unit,
        remote_blocks.size * 2 + send_bytes,
    )
    if relative(devices):
        incoming = list(send)
        for m in order(devices)[:-1]:
            incoming[m] = lax.ppermute(send[m], "leaf", [(i, i ^ m) for i in range(devices)])
    else:
        incoming = [lax.all_to_all(send[0], "leaf", split_axis=0, concat_axis=0, tiled=True)]

    base = call(
        local_kernel,
        jax.ShapeDtypeStruct((columns, points), F32),
        VMEM,
        (probes, local_blocks),
        like(probes, local_blocks) + sems(1 + leaves),
        leaves * leaves * unit,
        local_blocks.size * 2,
    )

    return call(
        functools.partial(gather_kernel, main, devices),
        jax.ShapeDtypeStruct((columns, points), F32),
        VMEM,
        (far_list, base, couplings, transfer, basis, *incoming),
        numbers(far_list)
        + like(couplings, transfer, basis)
        + [
            pltpu.VMEM((devices, depth, size), BF16),
            pltpu.VMEM((devices, LANES), I32),
            pltpu.SMEM((devices, LANES), I32),
            pltpu.VMEM((columns, points + size), F32),
        ]
        + sems(5 + 2 * devices)
        + [pltpu.SemaphoreType.DMA(())],
        devices * CAP * columns * size,
        send_bytes,
    )


def solution(mesh):
    placed = (
        P(None, ("grp", "leaf")),
        P(("grp", "leaf"), None, None),
        P(("grp", "leaf"), None, None),
        P(("grp", "leaf"), None, None, None),
        P(("grp", "leaf"), None, None, None),
        P(("grp", "leaf"), None),
        P(("grp", "leaf"), None),
        P(("grp", "leaf"), None, None, None),
        P(("grp", "leaf"), None),
    )
    return jax.shard_map(
        per_device, mesh=mesh, in_specs=placed, out_specs=P(None, ("grp", "leaf")), check_vma=False
    )
```

time: 54.9 us -> 48.1 us (0.88)
  the two profiles are of different devices: /device:TPU:15 before, /device:TPU:17 now
where the time goes in v4:
time: 48.1 us; the launch traced here: 47.9 us
  starting transfers between devices  24.8 us (52%)
  Pallas kernels  14 us (29%)
  waiting for transfers between devices  8.4 us (17%)
  local copies, waits for them, and re-layouts  0.58 us (1%)
    ppermute x15, starting transfers between devices, per_device(): lax.ppermute(send[m], 'leaf', [(i, i ^ m) for i in range(devices)])  24.8 us
    pallas_call x3, Pallas kernels, call(): pl.pallas_call(kernel, out_shape=out_shape, in_specs=[ANY] * len(operands...  14 us
    ppermute x15, waiting for transfers between devices, per_device(): lax.ppermute(send[m], 'leaf', [(i, i ^ m) for i in range(devices)])  8.4 us
  transfers between devices with their start and end apart: 15, of which 5 were waited for; matrix products, arithmetic and copies ran while one was open for 0% of the time, Pallas kernels for 11%

profile of v4, /device:TPU:17, one launch (start us, length us, event | category | flops | bytes accessed | tf_op | source)
XLA Modules:
  0.0 47.9 jit_solution(17078310357033902597)
XLA Ops:
  0.0 4.5 %shard_map.92 = (bf16[304,128]{1,0:T(8,128)(2,1)}, bf16[304,128]{1,0:T(8,128)(2,1)}, bf16[304,128]{1,0:T(8,128)(2,1)}, bf16[304,128]{1,0:T(8,128)(2,1)}, bf16[30...) custom-call(s32[4,8]{1,0:T(4,128)} %bitcast.2, ...), custom_call_target="tpu_custom_call" | custom-call | flops 68157440 | bytes 2293760 | tf_op jit(solution)/shard_map/pallas_call | solution.py:195
  4.5 0.7 %collective-permute-start = (bf16[304,128]{1,0:T(8,128)(2,1)}, bf16[304,128]{1,0:T(8,128)(2,1)S(1)}, u32[]{:S(2)}, u32[]{:S(2)}) collective-permute-start(bf16[304,128]{1,0:T(8,128)(2,1)} %get-tuple-element.22), channel_id=1, source_target_pairs={{0,1},{1,0},{2,3},{3,2},{4,5},{5,4},{6,7},{7,6},{8,9},{9,8},{10,11... | collective-permute-start | bytes 233480 | tf_op jit(solution)/shard_map/ppermute | solution.py:244
  5.2 1.3 %collective-permute-start.1 = (bf16[304,128]{1,0:T(8,128)(2,1)}, bf16[304,128]{1,0:T(8,128)(2,1)S(1)}, u32[]{:S(2)}, u32[]{:S(2)}) collective-permute-start(bf16[304,128]{1,0:T(8,128)(2,1)} %get-tuple-element.23), channel_id=1, source_target_pairs={{0,2},{1,3},{2,0},{3,1},{4,6},{5,7},{6,4},{7,5},{8,10},{9,11},{10,... | collective-permute-start | bytes 233480 | tf_op jit(solution)/shard_map/ppermute | solution.py:244
  6.5 0.5 collective-permute-start.2
  7.0 1.3 %collective-permute-start.3 = (bf16[304,128]{1,0:T(8,128)(2,1)}, bf16[304,128]{1,0:T(8,128)(2,1)S(1)}, u32[]{:S(2)}, u32[]{:S(2)}) collective-permute-start(bf16[304,128]{1,0:T(8,128)(2,1)} %get-tuple-element.25), channel_id=1, source_target_pairs={{0,4},{1,5},{2,6},{3,7},{4,0},{5,1},{6,2},{7,3},{8,12},{9,13},{10,... | collective-permute-start | bytes 233480 | tf_op jit(solution)/shard_map/ppermute | solution.py:244
  8.2 0.5 %collective-permute-start.4 = (bf16[304,128]{1,0:T(8,128)(2,1)}, bf16[304,128]{1,0:T(8,128)(2,1)S(1)}, u32[]{:S(2)}, u32[]{:S(2)}) collective-permute-start(bf16[304,128]{1,0:T(8,128)(2,1)} %get-tuple-element.26), channel_id=1, source_target_pairs={{0,5},{1,4},{2,7},{3,6},{4,1},{5,0},{6,3},{7,2},{8,13},{9,12},{10,... | collective-permute-start | bytes 233480 | tf_op jit(solution)/shard_map/ppermute | solution.py:244
  8.8 2.3 %collective-permute-start.5 = (bf16[304,128]{1,0:T(8,128)(2,1)}, bf16[304,128]{1,0:T(8,128)(2,1)S(1)}, u32[]{:S(2)}, u32[]{:S(2)}) collective-permute-start(bf16[304,128]{1,0:T(8,128)(2,1)} %get-tuple-element.27), channel_id=1, source_target_pairs={{0,6},{1,7},{2,4},{3,5},{4,2},{5,3},{6,0},{7,1},{8,14},{9,15},{10,... | collective-permute-start | bytes 233480 | tf_op jit(solution)/shard_map/ppermute | solution.py:244
  11.0 0.0 collective-permute-done.1.refs_7_
  11.0 1.8 %collective-permute-start.6 = (bf16[304,128]{1,0:T(8,128)(2,1)}, bf16[304,128]{1,0:T(8,128)(2,1)S(1)}, u32[]{:S(2)}, u32[]{:S(2)}) collective-permute-start(bf16[304,128]{1,0:T(8,128)(2,1)} %get-tuple-element.28), channel_id=1, source_target_pairs={{0,7},{1,6},{2,5},{3,4},{4,3},{5,2},{6,1},{7,0},{8,15},{9,14},{10,... | collective-permute-start | bytes 233480 | tf_op jit(solution)/shard_map/ppermute | solution.py:244
  12.8 0.1 collective-permute-start.7
  12.9 1.7 %collective-permute-start.8 = (bf16[304,128]{1,0:T(8,128)(2,1)}, bf16[304,128]{1,0:T(8,128)(2,1)S(1)}, u32[]{:S(2)}, u32[]{:S(2)}) collective-permute-start(bf16[304,128]{1,0:T(8,128)(2,1)} %get-tuple-element.30), channel_id=1, source_target_pairs={{0,9},{1,8},{2,11},{3,10},{4,13},{5,12},{6,15},{7,14},{8,1},{9,0},... | collective-permute-start | bytes 233480 | tf_op jit(solution)/shard_map/ppermute | solution.py:244
  14.6 0.6 %collective-permute-start.9 = (bf16[304,128]{1,0:T(8,128)(2,1)}, bf16[304,128]{1,0:T(8,128)(2,1)S(1)}, u32[]{:S(2)}, u32[]{:S(2)}) collective-permute-start(bf16[304,128]{1,0:T(8,128)(2,1)} %get-tuple-element.31), channel_id=1, source_target_pairs={{0,10},{1,11},{2,8},{3,9},{4,14},{5,15},{6,12},{7,13},{8,2},{9,3},... | collective-permute-start | bytes 233480 | tf_op jit(solution)/shard_map/ppermute | solution.py:244
  15.2 0.4 collective-permute-done.5.refs_11_
  15.6 3.4 %collective-permute-start.10 = (bf16[304,128]{1,0:T(8,128)(2,1)}, bf16[304,128]{1,0:T(8,128)(2,1)S(1)}, u32[]{:S(2)}, u32[]{:S(2)}) collective-permute-start(bf16[304,128]{1,0:T(8,128)(2,1)} %get-tuple-element.32), channel_id=1, source_target_pairs={{0,11},{1,10},{2,9},{3,8},{4,15},{5,14},{6,13},{7,12},{8,3},{9,2},... | collective-permute-start | bytes 233480 | tf_op jit(solution)/shard_map/ppermute | solution.py:244
  19.1 6.6 %collective-permute-start.12 = (bf16[304,128]{1,0:T(8,128)(2,1)}, bf16[304,128]{1,0:T(8,128)(2,1)S(1)}, u32[]{:S(2)}, u32[]{:S(2)}) collective-permute-start(bf16[304,128]{1,0:T(8,128)(2,1)} %get-tuple-element.34), channel_id=1, source_target_pairs={{0,13},{1,12},{2,15},{3,14},{4,9},{5,8},{6,11},{7,10},{8,5},{9,4},... | collective-permute-start | bytes 233480 | tf_op jit(solution)/shard_map/ppermute | solution.py:244
  25.7 1.4 %collective-permute-start.13 = (bf16[304,128]{1,0:T(8,128)(2,1)}, bf16[304,128]{1,0:T(8,128)(2,1)S(1)}, u32[]{:S(2)}, u32[]{:S(2)}) collective-permute-start(bf16[304,128]{1,0:T(8,128)(2,1)} %get-tuple-element.35), channel_id=1, source_target_pairs={{0,14},{1,15},{2,12},{3,13},{4,10},{5,11},{6,8},{7,9},{8,6},{9,7},... | collective-permute-start | bytes 233480 | tf_op jit(solution)/shard_map/ppermute | solution.py:244
  27.1 2.7 %collective-permute-start.14 = (bf16[304,128]{1,0:T(8,128)(2,1)}, bf16[304,128]{1,0:T(8,128)(2,1)S(1)}, u32[]{:S(2)}, u32[]{:S(2)}) collective-permute-start(bf16[304,128]{1,0:T(8,128)(2,1)} %get-tuple-element.36), channel_id=1, source_target_pairs={{0,15},{1,14},{2,13},{3,12},{4,11},{5,10},{6,9},{7,8},{8,7},{9,6},... | collective-permute-start | bytes 233480 | tf_op jit(solution)/shard_map/ppermute | solution.py:244
  29.8 5.1 %shard_map.91.refs_1_ = f32[65,1024]{1,0:T(8,128)} custom-call(bf16[65,1024]{1,0:T(8,128)(2,1)} %refs_2_.2, bf16[8,8,128,128]{3,2,1,0:T(8,128)(2,1)} %local_hbm.1), custom_call_target="tpu_custom_call" | custom-call | flops 136314880 | bytes 2097152 | tf_op jit(solution)/shard_map/pallas_call | solution.py:195
  34.8 0.5 collective-permute-done.11.refs_17_
  35.3 3.7 %collective-permute-done.12.refs_18_ = bf16[304,128]{1,0:T(8,128)(2,1)S(1)} collective-permute-done((bf16[304,128]{1,0:T(8,128)(2,1)}, bf16[304,128]{1,0:T(8,128)(2,1)S(1)}, u32[]{:S(2)}, u32[]{:S(2)}) %collective-permute-start.12) | collective-permute-done | bytes 77856 | tf_op jit(solution)/shard_map/ppermute | solution.py:244
  39.1 2.0 %collective-permute-done.13.refs_19_ = bf16[304,128]{1,0:T(8,128)(2,1)S(1)} collective-permute-done((bf16[304,128]{1,0:T(8,128)(2,1)}, bf16[304,128]{1,0:T(8,128)(2,1)S(1)}, u32[]{:S(2)}, u32[]{:S(2)}) %collective-permute-start.13) | collective-permute-done | bytes 77856 | tf_op jit(solution)/shard_map/ppermute | solution.py:244
  41.0 1.7 %collective-permute-done.14.refs_20_ = bf16[304,128]{1,0:T(8,128)(2,1)S(1)} collective-permute-done((bf16[304,128]{1,0:T(8,128)(2,1)}, bf16[304,128]{1,0:T(8,128)(2,1)S(1)}, u32[]{:S(2)}, u32[]{:S(2)}) %collective-permute-start.14) | collective-permute-done | bytes 77856 | tf_op jit(solution)/shard_map/ppermute | solution.py:244
  42.9 0.5 %copy-done.14 = bf16[304,128]{1,0:T(8,128)(2,1)} copy-done((bf16[304,128]{1,0:T(8,128)(2,1)}, bf16[304,128]{1,0:T(8,128)(2,1)S(1)}, u32[]{:S(2)}) %copy-start.14) | copy-done | bytes 77848
  43.4 4.4 %shard_map.93 = f32[65,1024]{1,0:T(8,128)} custom-call(s32[1,12]{1,0:T(1,128)} %refs_0_.1, f32[65,1024]{1,0:T(8,128)} %shard_map.91.refs_1_, bf16[1,12,64,64]{3,2,1,0:T(8,128)(2,1)} %refs_2_.3, bf16[8,64,64]{2,1,0:T(8,128)(2,1)} %refs_3_.3, bf16[8,64,128]{2,1,0:T(8,128)(2,1)} %refs_4_.3, bf16[304,128]{1,0:T(8,128)(2,1)} %get-tuple-element.21.refs_5_, ...), custom_call_target="tpu_custom_call" | custom-call | flops 532480 | bytes 1245184 | tf_op jit(solution)/shard_map/pallas_call | solution.py:195
  (39 shorter events, 0.1 us)
Async XLA Ops:
  4.5 4.3 %collective-permute-start = (bf16[304,128]{1,0:T(8,128)(2,1)}, bf16[304,128]{1,0:T(8,128)(2,1)S(1)}, u32[]{:S(2)}, u32[]{:S(2)}) collective-permute-start(bf16[304,128]{1,0:T(8,128)(2,1)} %get-tuple-element.22), channel_id=1, source_target_pairs={{0,1},{1,0},{2,3},{3,2},{4,5},{5,4},{6,7},{7,6},{8,9},{9,8},{10,11... | collective-permute-start | bytes 233480 | tf_op jit(solution)/shard_map/ppermute | solution.py:244
  5.2 5.8 %collective-permute-start.1 = (bf16[304,128]{1,0:T(8,128)(2,1)}, bf16[304,128]{1,0:T(8,128)(2,1)S(1)}, u32[]{:S(2)}, u32[]{:S(2)}) collective-permute-start(bf16[304,128]{1,0:T(8,128)(2,1)} %get-tuple-element.23), channel_id=1, source_target_pairs={{0,2},{1,3},{2,0},{3,1},{4,6},{5,7},{6,4},{7,5},{8,10},{9,11},{10,... | collective-permute-start | bytes 233480 | tf_op jit(solution)/shard_map/ppermute | solution.py:244
  6.5 6.3 %collective-permute-start.2 = (bf16[304,128]{1,0:T(8,128)(2,1)}, bf16[304,128]{1,0:T(8,128)(2,1)S(1)}, u32[]{:S(2)}, u32[]{:S(2)}) collective-permute-start(bf16[304,128]{1,0:T(8,128)(2,1)} %get-tuple-element.24), channel_id=1, source_target_pairs={{0,3},{1,2},{2,1},{3,0},{4,7},{5,6},{6,5},{7,4},{8,11},{9,10},{10,... | collective-permute-start | bytes 233480 | tf_op jit(solution)/shard_map/ppermute | solution.py:244
  7.0 5.9 %collective-permute-start.3 = (bf16[304,128]{1,0:T(8,128)(2,1)}, bf16[304,128]{1,0:T(8,128)(2,1)S(1)}, u32[]{:S(2)}, u32[]{:S(2)}) collective-permute-start(bf16[304,128]{1,0:T(8,128)(2,1)} %get-tuple-element.25), channel_id=1, source_target_pairs={{0,4},{1,5},{2,6},{3,7},{4,0},{5,1},{6,2},{7,3},{8,12},{9,13},{10,... | collective-permute-start | bytes 233480 | tf_op jit(solution)/shard_map/ppermute | solution.py:244
  8.2 6.3 %collective-permute-start.4 = (bf16[304,128]{1,0:T(8,128)(2,1)}, bf16[304,128]{1,0:T(8,128)(2,1)S(1)}, u32[]{:S(2)}, u32[]{:S(2)}) collective-permute-start(bf16[304,128]{1,0:T(8,128)(2,1)} %get-tuple-element.26), channel_id=1, source_target_pairs={{0,5},{1,4},{2,7},{3,6},{4,1},{5,0},{6,3},{7,2},{8,13},{9,12},{10,... | collective-permute-start | bytes 233480 | tf_op jit(solution)/shard_map/ppermute | solution.py:244
  8.8 34.0 %copy-start = (bf16[304,128]{1,0:T(8,128)(2,1)}, bf16[304,128]{1,0:T(8,128)(2,1)S(1)}, u32[]{:S(2)}) copy-start(bf16[304,128]{1,0:T(8,128)(2,1)S(1)} %collective-permute-done.refs_6_) | copy-start | bytes 233476
  8.8 6.9 %collective-permute-start.5 = (bf16[304,128]{1,0:T(8,128)(2,1)}, bf16[304,128]{1,0:T(8,128)(2,1)S(1)}, u32[]{:S(2)}, u32[]{:S(2)}) collective-permute-start(bf16[304,128]{1,0:T(8,128)(2,1)} %get-tuple-element.27), channel_id=1, source_target_pairs={{0,6},{1,7},{2,4},{3,5},{4,2},{5,3},{6,0},{7,1},{8,14},{9,15},{10,... | collective-permute-start | bytes 233480 | tf_op jit(solution)/shard_map/ppermute | solution.py:244
  11.0 31.8 %copy-start.1 = (bf16[304,128]{1,0:T(8,128)(2,1)}, bf16[304,128]{1,0:T(8,128)(2,1)S(1)}, u32[]{:S(2)}) copy-start(bf16[304,128]{1,0:T(8,128)(2,1)S(1)} %collective-permute-done.1.refs_7_) | copy-start | bytes 233476
  11.0 8.0 %collective-permute-start.6 = (bf16[304,128]{1,0:T(8,128)(2,1)}, bf16[304,128]{1,0:T(8,128)(2,1)S(1)}, u32[]{:S(2)}, u32[]{:S(2)}) collective-permute-start(bf16[304,128]{1,0:T(8,128)(2,1)} %get-tuple-element.28), channel_id=1, source_target_pairs={{0,7},{1,6},{2,5},{3,4},{4,3},{5,2},{6,1},{7,0},{8,15},{9,14},{10,... | collective-permute-start | bytes 233480 | tf_op jit(solution)/shard_map/ppermute | solution.py:244
  12.8 30.0 %copy-start.2 = (bf16[304,128]{1,0:T(8,128)(2,1)}, bf16[304,128]{1,0:T(8,128)(2,1)S(1)}, u32[]{:S(2)}) copy-start(bf16[304,128]{1,0:T(8,128)(2,1)S(1)} %collective-permute-done.2.refs_8_) | copy-start | bytes 233476
  12.8 6.2 %collective-permute-start.7 = (bf16[304,128]{1,0:T(8,128)(2,1)}, bf16[304,128]{1,0:T(8,128)(2,1)S(1)}, u32[]{:S(2)}, u32[]{:S(2)}) collective-permute-start(bf16[304,128]{1,0:T(8,128)(2,1)} %get-tuple-element.29), channel_id=1, source_target_pairs={{0,8},{1,9},{2,10},{3,11},{4,12},{5,13},{6,14},{7,15},{8,0},{9,1},... | collective-permute-start | bytes 233480 | tf_op jit(solution)/shard_map/ppermute | solution.py:244
  12.9 29.9 %copy-start.3 = (bf16[304,128]{1,0:T(8,128)(2,1)}, bf16[304,128]{1,0:T(8,128)(2,1)S(1)}, u32[]{:S(2)}) copy-start(bf16[304,128]{1,0:T(8,128)(2,1)S(1)} %collective-permute-done.3.refs_9_) | copy-start | bytes 233476
  12.9 12.8 %collective-permute-start.8 = (bf16[304,128]{1,0:T(8,128)(2,1)}, bf16[304,128]{1,0:T(8,128)(2,1)S(1)}, u32[]{:S(2)}, u32[]{:S(2)}) collective-permute-start(bf16[304,128]{1,0:T(8,128)(2,1)} %get-tuple-element.30), channel_id=1, source_target_pairs={{0,9},{1,8},{2,11},{3,10},{4,13},{5,12},{6,15},{7,14},{8,1},{9,0},... | collective-permute-start | bytes 233480 | tf_op jit(solution)/shard_map/ppermute | solution.py:244
  14.6 28.2 %copy-start.4 = (bf16[304,128]{1,0:T(8,128)(2,1)}, bf16[304,128]{1,0:T(8,128)(2,1)S(1)}, u32[]{:S(2)}) copy-start(bf16[304,128]{1,0:T(8,128)(2,1)S(1)} %collective-permute-done.4.refs_10_) | copy-start | bytes 233476
  14.6 12.5 %collective-permute-start.9 = (bf16[304,128]{1,0:T(8,128)(2,1)}, bf16[304,128]{1,0:T(8,128)(2,1)S(1)}, u32[]{:S(2)}, u32[]{:S(2)}) collective-permute-start(bf16[304,128]{1,0:T(8,128)(2,1)} %get-tuple-element.31), channel_id=1, source_target_pairs={{0,10},{1,11},{2,8},{3,9},{4,14},{5,15},{6,12},{7,13},{8,2},{9,3},... | collective-permute-start | bytes 233480 | tf_op jit(solution)/shard_map/ppermute | solution.py:244
  15.6 27.2 %copy-start.5 = (bf16[304,128]{1,0:T(8,128)(2,1)}, bf16[304,128]{1,0:T(8,128)(2,1)S(1)}, u32[]{:S(2)}) copy-start(bf16[304,128]{1,0:T(8,128)(2,1)S(1)} %collective-permute-done.5.refs_11_) | copy-start | bytes 233476
  15.6 19.2 %collective-permute-start.10 = (bf16[304,128]{1,0:T(8,128)(2,1)}, bf16[304,128]{1,0:T(8,128)(2,1)S(1)}, u32[]{:S(2)}, u32[]{:S(2)}) collective-permute-start(bf16[304,128]{1,0:T(8,128)(2,1)} %get-tuple-element.32), channel_id=1, source_target_pairs={{0,11},{1,10},{2,9},{3,8},{4,15},{5,14},{6,13},{7,12},{8,3},{9,2},... | collective-permute-start | bytes 233480 | tf_op jit(solution)/shard_map/ppermute | solution.py:244
  19.0 23.8 %copy-start.6 = (bf16[304,128]{1,0:T(8,128)(2,1)}, bf16[304,128]{1,0:T(8,128)(2,1)S(1)}, u32[]{:S(2)}) copy-start(bf16[304,128]{1,0:T(8,128)(2,1)S(1)} %collective-permute-done.6.refs_12_) | copy-start | bytes 233476
  19.0 16.3 %collective-permute-start.11 = (bf16[304,128]{1,0:T(8,128)(2,1)}, bf16[304,128]{1,0:T(8,128)(2,1)S(1)}, u32[]{:S(2)}, u32[]{:S(2)}) collective-permute-start(bf16[304,128]{1,0:T(8,128)(2,1)} %get-tuple-element.33), channel_id=1, source_target_pairs={{0,12},{1,13},{2,14},{3,15},{4,8},{5,9},{6,10},{7,11},{8,4},{9,5},... | collective-permute-start | bytes 233480 | tf_op jit(solution)/shard_map/ppermute | solution.py:244
  19.1 23.8 %copy-start.7 = (bf16[304,128]{1,0:T(8,128)(2,1)}, bf16[304,128]{1,0:T(8,128)(2,1)S(1)}, u32[]{:S(2)}) copy-start(bf16[304,128]{1,0:T(8,128)(2,1)S(1)} %collective-permute-done.7.refs_13_) | copy-start | bytes 233476
  19.1 20.0 %collective-permute-start.12 = (bf16[304,128]{1,0:T(8,128)(2,1)}, bf16[304,128]{1,0:T(8,128)(2,1)S(1)}, u32[]{:S(2)}, u32[]{:S(2)}) collective-permute-start(bf16[304,128]{1,0:T(8,128)(2,1)} %get-tuple-element.34), channel_id=1, source_target_pairs={{0,13},{1,12},{2,15},{3,14},{4,9},{5,8},{6,11},{7,10},{8,5},{9,4},... | collective-permute-start | bytes 233480 | tf_op jit(solution)/shard_map/ppermute | solution.py:244
  25.7 17.2 %copy-start.8 = (bf16[304,128]{1,0:T(8,128)(2,1)}, bf16[304,128]{1,0:T(8,128)(2,1)S(1)}, u32[]{:S(2)}) copy-start(bf16[304,128]{1,0:T(8,128)(2,1)S(1)} %collective-permute-done.8.refs_14_) | copy-start | bytes 233476
  25.7 15.4 %collective-permute-start.13 = (bf16[304,128]{1,0:T(8,128)(2,1)}, bf16[304,128]{1,0:T(8,128)(2,1)S(1)}, u32[]{:S(2)}, u32[]{:S(2)}) collective-permute-start(bf16[304,128]{1,0:T(8,128)(2,1)} %get-tuple-element.35), channel_id=1, source_target_pairs={{0,14},{1,15},{2,12},{3,13},{4,10},{5,11},{6,8},{7,9},{8,6},{9,7},... | collective-permute-start | bytes 233480 | tf_op jit(solution)/shard_map/ppermute | solution.py:244
  27.1 15.7 %collective-permute-start.14 = (bf16[304,128]{1,0:T(8,128)(2,1)}, bf16[304,128]{1,0:T(8,128)(2,1)S(1)}, u32[]{:S(2)}, u32[]{:S(2)}) collective-permute-start(bf16[304,128]{1,0:T(8,128)(2,1)} %get-tuple-element.36), channel_id=1, source_target_pairs={{0,15},{1,14},{2,13},{3,12},{4,11},{5,10},{6,9},{7,8},{8,7},{9,6},... | collective-permute-start | bytes 233480 | tf_op jit(solution)/shard_map/ppermute | solution.py:244
  (6 other events, 37.8 us)

commit v5 on v4

--- a/solution.py
+++ b/solution.py
@@ -11,6 +11,7 @@
 TILE = 16
 LANES = 128
 DIRECT = 16
+AHEAD = 5
 
 F32 = jnp.float32
 BF16 = jnp.bfloat16
@@ -61,7 +62,11 @@
         copies.start(dest_hbm, dest_ref),
         copies.start(leaf_hbm, leaf_ref),
     ]
-    arrivals = [copies.start(blocks_hbm.at[j], blocks_ref.at[j]) for j in range(leaves)]
+    chunk = leaves // 2
+    arrivals = [
+        copies.start(blocks_hbm.at[pl.ds(j, chunk)], blocks_ref.at[pl.ds(j, chunk)])
+        for j in range(0, leaves, chunk)
+    ]
 
     @pl.loop(0, devices)
     def _(i):
@@ -80,7 +85,8 @@
 
     lane = lax.broadcasted_iota(I32, (1, size), 1)
     for j in range(leaves):
-        arrivals[j].wait()
+        if j % chunk == 0:
+            arrivals[j // chunk].wait()
         x = probes_ref[:, j * size : (j + 1) * size]
         for first in range(0, per_leaf, 4):
             many = min(4, per_leaf - first)
@@ -111,84 +117,116 @@
 
 
 def order(devices):
-    return sorted(range(devices), reverse=True)
-
-
-def local_kernel(probes_hbm, local_hbm, base_ref, probes_ref, local_ref, sems):
+    half = devices // 2
+    far, near = list(range(half, devices)), list(range(1, half)) + [0]
+    return [m for pair in zip(far, near) for m in pair]
+
+
+def local_part(probes_ref, local_ref, out_ref):
     leaves, size = local_ref.shape[0], local_ref.shape[2]
-    copies = Copies(sems)
-    early = copies.start(probes_hbm, probes_ref)
-    arrivals = [copies.start(local_hbm.at[i], local_ref.at[i]) for i in range(leaves)]
-    early.wait()
     for i in range(leaves):
-        arrivals[i].wait()
         total = dot_t(probes_ref[:, :size], local_ref[i, 0])
         for c in range(1, leaves):
             total += dot_t(probes_ref[:, c * size : (c + 1) * size], local_ref[i, c])
-        base_ref[:, i * size : (i + 1) * size] = total
-
-
-def gather_kernel(main, devices, *refs):
+        out_ref[:, i * size : (i + 1) * size] = total
+
+
+def local_kernel(probes_hbm, local_hbm, base_ref, probes_ref, local_ref, sems):
+    copies = Copies(sems)
+    for copy in [copies.start(probes_hbm, probes_ref), copies.start(local_hbm, local_ref)]:
+        copy.wait()
+    local_part(probes_ref, local_ref, base_ref)
+
+
+def add_slots(main, members, parts, incoming_ref, meta, leaf_ref, total, copies, late, between):
+    size = incoming_ref.shape[2]
+    points = total.shape[1] - size
+    edge = CAP * main
+    tiles = [
+        copies.start(parts(m).at[pl.ds(edge, TILE)], incoming_ref.at[i, pl.ds(edge, TILE)])
+        for i, m in enumerate(members)
+    ]
+    large = [
+        copies.start(parts(m).at[pl.ds(0, edge)], incoming_ref.at[i, pl.ds(0, edge)])
+        for i, m in enumerate(members)
+    ]
+    total[:, points:] = jnp.zeros((total.shape[0], size), F32)
+    for i, copy in enumerate(tiles):
+        copy.wait()
+        meta[i : i + 1, :] = incoming_ref[i, edge : edge + TILE, :].astype(F32)[CAP : CAP + 1].astype(I32)
+    numbers = pltpu.make_async_copy(meta, leaf_ref, late)
+    numbers.start()
+    between()
+    numbers.wait()
+    for copy in large:
+        copy.wait()
+
+    @pl.loop(0, len(members))
+    def _(i):
+        tail = incoming_ref[i, edge : edge + TILE, :].astype(F32)
+        for slot in range(CAP):
+            cols = pl.ds(pl.multiple_of(leaf_ref[i, slot] * size, size), size)
+            total[:main, cols] += incoming_ref[i, slot * main : (slot + 1) * main, :].astype(F32)
+            total[main:, cols] += tail[slot : slot + 1]
+
+
+def early_kernel(main, devices, members, probes_hbm, local_hbm, *refs):
+    parts = refs[:-9]
+    out_ref, probes_ref, local_ref, incoming_ref, meta, leaf_ref, total, sems, late = refs[-9:]
+    part = lambda m: parts[members.index(m)]
+    copies = Copies(sems)
+    arrivals = [copies.start(probes_hbm, probes_ref), copies.start(local_hbm, local_ref)]
+
+    def between():
+        for copy in arrivals:
+            copy.wait()
+        local_part(probes_ref, local_ref, total)
+
+    add_slots(main, members, part, incoming_ref, meta, leaf_ref, total, copies, late, between)
+    out_ref[...] = total[:, : out_ref.shape[1]]
+
+
+def last_kernel(main, devices, members, *refs):
     partner_hbm, base_hbm, couplings_hbm, transfer_hbm, basis_hbm = refs[:5]
-    parts = refs[5:-11]
-    out_ref, partner_ref, couplings_ref, transfer_ref, basis_ref, incoming_ref, meta, leaf_ref, total, sems, late = (
-        refs[-11:]
-    )
+    parts = refs[5:-12]
+    (
+        out_ref, partner_ref, couplings_ref, transfer_ref, basis_ref,
+        boxes_ref, incoming_ref, meta, leaf_ref, total, sems, late,
+    ) = refs[-12:]
     columns = out_ref.shape[0]
     leaves, rank, size = basis_ref.shape
-    points = leaves * size
     edge = CAP * main
     copies = Copies(sems)
     part = lambda m: parts[m] if relative(devices) else parts[0].at[m]
-    small = [
-        copies.start(part(m).at[pl.ds(edge, incoming_ref.shape[1] - edge)], incoming_ref.at[m, pl.ds(edge, incoming_ref.shape[1] - edge)])
-        for m in range(devices)
-    ]
-    weights = [
+    arrivals = [
+        copies.start(part(m).at[pl.ds(edge, boxes_ref.shape[1])], boxes_ref.at[m]) for m in range(devices)
+    ] + [
         copies.start(partner_hbm, partner_ref),
         copies.start(couplings_hbm, couplings_ref),
         copies.start(transfer_hbm, transfer_ref),
         copies.start(basis_hbm, basis_ref),
-        copies.start(base_hbm, total.at[:, pl.ds(0, points)]),
-    ]
-    large = [copies.start(part(m).at[pl.ds(0, edge)], incoming_ref.at[m, pl.ds(0, edge)]) for m in range(devices)]
-
-    for m in range(devices):
-        small[m].wait()
-        meta[m : m + 1, :] = incoming_ref[m, edge : edge + TILE, :].astype(F32)[CAP : CAP + 1].astype(I32)
-    numbers = pltpu.make_async_copy(meta, leaf_ref, late)
-    numbers.start()
-
-    for copy in weights:
-        copy.wait()
-    total[:, points:] = jnp.zeros((columns, size), F32)
-    far = jnp.zeros((columns, rank), F32)
-    for f in range(couplings_ref.shape[1]):
-        source = place(partner_ref[0, f], devices)
-        packed = incoming_ref[source, edge + TILE :, :]
-        last = incoming_ref[source, edge : edge + TILE, :].astype(F32)[CAP + 1 : CAP + 2, :rank]
-        box = jnp.concatenate(
-            [packed[:, :rank].astype(F32), packed[:, rank:].astype(F32), last], axis=0
-        ).astype(BF16)
-        far += dot_t(box, couplings_ref[0, f])
-    far = far.astype(BF16)
-    for j in range(leaves):
-        down = dot(far, transfer_ref[j]).astype(BF16)
-        total[:, j * size : (j + 1) * size] += dot(down, basis_ref[j])
-
-    numbers.wait()
-    for copy in large:
-        copy.wait()
-
-    @pl.loop(0, devices)
-    def _(m):
-        tail = incoming_ref[m, edge : edge + TILE, :].astype(F32)
-        for slot in range(CAP):
-            cols = pl.ds(pl.multiple_of(leaf_ref[m, slot] * size, size), size)
-            total[:main, cols] += incoming_ref[m, slot * main : (slot + 1) * main, :].astype(F32)
-            total[main:, cols] += tail[slot : slot + 1]
-
-    out_ref[...] = total[:, :points]
+        copies.start(base_hbm, total.at[:, pl.ds(0, leaves * size)]),
+    ]
+
+    def far_part():
+        for copy in arrivals:
+            copy.wait()
+        far = jnp.zeros((columns, rank), F32)
+        for f in range(couplings_ref.shape[1]):
+            source = place(partner_ref[0, f], devices)
+            packed = boxes_ref[source, TILE:, :]
+            last = boxes_ref[source, :TILE, :].astype(F32)[CAP + 1 : CAP + 2, :rank]
+            box = jnp.concatenate(
+                [packed[:, :rank].astype(F32), packed[:, rank:].astype(F32), last], axis=0
+            ).astype(BF16)
+            far += dot_t(box, couplings_ref[0, f])
+        far = far.astype(BF16)
+        for j in range(leaves):
+            down = dot(far, transfer_ref[j]).astype(BF16)
+            total[:, j * size : (j + 1) * size] += dot(down, basis_ref[j])
+
+    add_slots(main, members, part, incoming_ref, meta, leaf_ref, total, copies, late, far_part)
+    out_ref[...] = total[:, : out_ref.shape[1]]
 
 
 def call(kernel, out_shape, out_specs, operands, scratch, flops, nbytes):
@@ -234,43 +272,62 @@
             pltpu.VMEM((devices, TILE, size), F32),
             pltpu.SMEM((devices,), I32),
         ]
-        + sems(5 + leaves + devices),
+        + sems(7 + devices),
         blocks * unit,
         remote_blocks.size * 2 + send_bytes,
     )
+    gathering = lambda members: [
+        pltpu.VMEM((len(members), depth, size), BF16),
+        pltpu.VMEM((len(members), LANES), I32),
+        pltpu.SMEM((len(members), LANES), I32),
+        pltpu.VMEM((columns, points + size), F32),
+    ]
+
+    late = list(range(devices))
     if relative(devices):
-        incoming = list(send)
-        for m in order(devices)[:-1]:
+        ways = order(devices)[:-1]
+        send = list(send)
+        incoming = [send[0]] + [None] * (devices - 1)
+        for m in ways:
             incoming[m] = lax.ppermute(send[m], "leaf", [(i, i ^ m) for i in range(devices)])
+        late = ways[-AHEAD:]
+        early = [0] + ways[:-AHEAD]
+        base = call(
+            functools.partial(early_kernel, main, devices, early),
+            jax.ShapeDtypeStruct((columns, points), F32),
+            VMEM,
+            (probes, local_blocks, *[incoming[m] for m in early]),
+            like(probes, local_blocks)
+            + gathering(early)
+            + sems(2 + 2 * len(early))
+            + [pltpu.SemaphoreType.DMA(())],
+            leaves * leaves * unit,
+            local_blocks.size * 2 + len(early) * depth * size * 2,
+        )
     else:
         incoming = [lax.all_to_all(send[0], "leaf", split_axis=0, concat_axis=0, tiled=True)]
-
-    base = call(
-        local_kernel,
-        jax.ShapeDtypeStruct((columns, points), F32),
-        VMEM,
-        (probes, local_blocks),
-        like(probes, local_blocks) + sems(1 + leaves),
-        leaves * leaves * unit,
-        local_blocks.size * 2,
-    )
+        base = call(
+            local_kernel,
+            jax.ShapeDtypeStruct((columns, points), F32),
+            VMEM,
+            (probes, local_blocks),
+            like(probes, local_blocks) + sems(2),
+            leaves * leaves * unit,
+            local_blocks.size * 2,
+        )
 
     return call(
-        functools.partial(gather_kernel, main, devices),
+        functools.partial(last_kernel, main, devices, late),
         jax.ShapeDtypeStruct((columns, points), F32),
         VMEM,
         (far_list, base, couplings, transfer, basis, *incoming),
         numbers(far_list)
         + like(couplings, transfer, basis)
-        + [
-            pltpu.VMEM((devices, depth, size), BF16),
-            pltpu.VMEM((devices, LANES), I32),
-            pltpu.SMEM((devices, LANES), I32),
-            pltpu.VMEM((columns, points + size), F32),
-        ]
-        + sems(5 + 2 * devices)
+        + [pltpu.VMEM((devices, depth - CAP * main, size), BF16)]
+        + gathering(late)
+        + sems(5 + devices + 2 * len(late))
         + [pltpu.SemaphoreType.DMA(())],
-        devices * CAP * columns * size,
+        len(late) * CAP * columns * size,
         send_bytes,
     )
 

time: 48.1 us -> 44.1 us (0.917)
  the two profiles are of different devices: /device:TPU:17 before, /device:TPU:0 now
where the time goes in v5:
time: 44.1 us; the launch traced here: 43.9 us
  starting transfers between devices  29 us (66%)
  Pallas kernels  12 us (27%)
  waiting for transfers between devices  1.64 us (4%)
  local copies, waits for them, and re-layouts  1.11 us (3%)
    ppermute x15, starting transfers between devices, per_device(): lax.ppermute(send[m], 'leaf', [(i, i ^ m) for i in range(devices)])  29 us
    pallas_call x3, Pallas kernels, call(): pl.pallas_call(kernel, out_shape=out_shape, in_specs=[ANY] * len(operands...  12 us
    ppermute x15, waiting for transfers between devices, per_device(): lax.ppermute(send[m], 'leaf', [(i, i ^ m) for i in range(devices)])  1.64 us
    unnamed x30, local copies, waits for them, and re-layouts  1.11 us
  transfers between devices with their start and end apart: 15, of which 2 were waited for; matrix products, arithmetic and copies ran while one was open for 0% of the time, Pallas kernels for 10%

profile of v5, /device:TPU:0, one launch (start us, length us, event | category | flops | bytes accessed | tf_op | source)
XLA Modules:
  0.0 43.9 jit_solution(12497781014589610332)
XLA Ops:
  0.0 3.5 %shard_map.91 = (bf16[304,128]{1,0:T(8,128)(2,1)}, bf16[304,128]{1,0:T(8,128)(2,1)}, bf16[304,128]{1,0:T(8,128)(2,1)}, bf16[304,128]{1,0:T(8,128)(2,1)}, bf16[30...) custom-call(s32[4,8]{1,0:T(4,128)} %bitcast.2, ...), custom_call_target="tpu_custom_call" | custom-call | flops 68157440 | bytes 2293760 | tf_op jit(solution)/shard_map/pallas_call | solution.py:233
  3.6 4.1 %collective-permute-start = (bf16[304,128]{1,0:T(8,128)(2,1)}, bf16[304,128]{1,0:T(8,128)(2,1)S(1)}, u32[]{:S(2)}, u32[]{:S(2)}) collective-permute-start(bf16[304,128]{1,0:T(8,128)(2,1)} %get-tuple-element.22), channel_id=1, source_target_pairs={{0,8},{1,9},{2,10},{3,11},{4,12},{5,13},{6,14},{7,15},{8,0},{9,1},... | collective-permute-start | bytes 233480 | tf_op jit(solution)/shard_map/ppermute | solution.py:292
  7.7 0.2 collective-permute-start.2
  7.9 1.8 %collective-permute-start.3 = (bf16[304,128]{1,0:T(8,128)(2,1)}, bf16[304,128]{1,0:T(8,128)(2,1)S(1)}, u32[]{:S(2)}, u32[]{:S(2)}) collective-permute-start(bf16[304,128]{1,0:T(8,128)(2,1)} %get-tuple-element.25), channel_id=1, source_target_pairs={{0,2},{1,3},{2,0},{3,1},{4,6},{5,7},{6,4},{7,5},{8,10},{9,11},{10,... | collective-permute-start | bytes 233480 | tf_op jit(solution)/shard_map/ppermute | solution.py:292
  9.6 2.5 %collective-permute-start.4 = (bf16[304,128]{1,0:T(8,128)(2,1)}, bf16[304,128]{1,0:T(8,128)(2,1)S(1)}, u32[]{:S(2)}, u32[]{:S(2)}) collective-permute-start(bf16[304,128]{1,0:T(8,128)(2,1)} %get-tuple-element.26), channel_id=1, source_target_pairs={{0,10},{1,11},{2,8},{3,9},{4,14},{5,15},{6,12},{7,13},{8,2},{9,3},... | collective-permute-start | bytes 233480 | tf_op jit(solution)/shard_map/ppermute | solution.py:292
  12.2 0.6 %collective-permute-start.5 = (bf16[304,128]{1,0:T(8,128)(2,1)}, bf16[304,128]{1,0:T(8,128)(2,1)S(1)}, u32[]{:S(2)}, u32[]{:S(2)}) collective-permute-start(bf16[304,128]{1,0:T(8,128)(2,1)} %get-tuple-element.27), channel_id=1, source_target_pairs={{0,3},{1,2},{2,1},{3,0},{4,7},{5,6},{6,5},{7,4},{8,11},{9,10},{10,... | collective-permute-start | bytes 233480 | tf_op jit(solution)/shard_map/ppermute | solution.py:292
  12.7 2.3 %collective-permute-start.6 = (bf16[304,128]{1,0:T(8,128)(2,1)}, bf16[304,128]{1,0:T(8,128)(2,1)S(1)}, u32[]{:S(2)}, u32[]{:S(2)}) collective-permute-start(bf16[304,128]{1,0:T(8,128)(2,1)} %get-tuple-element.28), channel_id=1, source_target_pairs={{0,11},{1,10},{2,9},{3,8},{4,15},{5,14},{6,13},{7,12},{8,3},{9,2},... | collective-permute-start | bytes 233480 | tf_op jit(solution)/shard_map/ppermute | solution.py:292
  15.0 1.4 %collective-permute-done.2.refs_3_.refs_14_ = bf16[304,128]{1,0:T(8,128)(2,1)S(1)} collective-permute-done((bf16[304,128]{1,0:T(8,128)(2,1)}, bf16[304,128]{1,0:T(8,128)(2,1)S(1)}, u32[]{:S(2)}, u32[]{:S(2)}) %collective-permute-start.2) | collective-permute-done | bytes 77856 | tf_op jit(solution)/shard_map/ppermute | solution.py:292
  16.4 4.2 %collective-permute-start.7 = (bf16[304,128]{1,0:T(8,128)(2,1)}, bf16[304,128]{1,0:T(8,128)(2,1)S(1)}, u32[]{:S(2)}, u32[]{:S(2)}) collective-permute-start(bf16[304,128]{1,0:T(8,128)(2,1)} %get-tuple-element.29), channel_id=1, source_target_pairs={{0,4},{1,5},{2,6},{3,7},{4,0},{5,1},{6,2},{7,3},{8,12},{9,13},{10,... | collective-permute-start | bytes 233480 | tf_op jit(solution)/shard_map/ppermute | solution.py:292
  20.7 1.4 %collective-permute-start.8 = (bf16[304,128]{1,0:T(8,128)(2,1)}, bf16[304,128]{1,0:T(8,128)(2,1)S(1)}, u32[]{:S(2)}, u32[]{:S(2)}) collective-permute-start(bf16[304,128]{1,0:T(8,128)(2,1)} %get-tuple-element.30), channel_id=1, source_target_pairs={{0,12},{1,13},{2,14},{3,15},{4,8},{5,9},{6,10},{7,11},{8,4},{9,5},... | collective-permute-start | bytes 233480 | tf_op jit(solution)/shard_map/ppermute | solution.py:292
  22.1 0.2 collective-permute-start.9
  22.3 2.5 %collective-permute-start.10 = (bf16[304,128]{1,0:T(8,128)(2,1)}, bf16[304,128]{1,0:T(8,128)(2,1)S(1)}, u32[]{:S(2)}, u32[]{:S(2)}) collective-permute-start(bf16[304,128]{1,0:T(8,128)(2,1)} %get-tuple-element.32), channel_id=1, source_target_pairs={{0,6},{1,7},{2,4},{3,5},{4,2},{5,3},{6,0},{7,1},{8,14},{9,15},{10,... | collective-permute-start | bytes 233480 | tf_op jit(solution)/shard_map/ppermute | solution.py:292
  24.7 0.7 %collective-permute-start.11 = (bf16[304,128]{1,0:T(8,128)(2,1)}, bf16[304,128]{1,0:T(8,128)(2,1)S(1)}, u32[]{:S(2)}, u32[]{:S(2)}) collective-permute-start(bf16[304,128]{1,0:T(8,128)(2,1)} %get-tuple-element.33), channel_id=1, source_target_pairs={{0,7},{1,6},{2,5},{3,4},{4,3},{5,2},{6,1},{7,0},{8,15},{9,14},{10,... | collective-permute-start | bytes 233480 | tf_op jit(solution)/shard_map/ppermute | solution.py:292
  25.5 3.9 %collective-permute-start.12 = (bf16[304,128]{1,0:T(8,128)(2,1)}, bf16[304,128]{1,0:T(8,128)(2,1)S(1)}, u32[]{:S(2)}, u32[]{:S(2)}) collective-permute-start(bf16[304,128]{1,0:T(8,128)(2,1)} %get-tuple-element.34), channel_id=1, source_target_pairs={{0,13},{1,12},{2,15},{3,14},{4,9},{5,8},{6,11},{7,10},{8,5},{9,4},... | collective-permute-start | bytes 233480 | tf_op jit(solution)/shard_map/ppermute | solution.py:292
  29.4 2.0 %collective-permute-start.13 = (bf16[304,128]{1,0:T(8,128)(2,1)}, bf16[304,128]{1,0:T(8,128)(2,1)S(1)}, u32[]{:S(2)}, u32[]{:S(2)}) collective-permute-start(bf16[304,128]{1,0:T(8,128)(2,1)} %get-tuple-element.35), channel_id=1, source_target_pairs={{0,14},{1,15},{2,12},{3,13},{4,10},{5,11},{6,8},{7,9},{8,6},{9,7},... | collective-permute-start | bytes 233480 | tf_op jit(solution)/shard_map/ppermute | solution.py:292
  31.4 2.7 %collective-permute-start.14 = (bf16[304,128]{1,0:T(8,128)(2,1)}, bf16[304,128]{1,0:T(8,128)(2,1)S(1)}, u32[]{:S(2)}, u32[]{:S(2)}) collective-permute-start(bf16[304,128]{1,0:T(8,128)(2,1)} %get-tuple-element.36), channel_id=1, source_target_pairs={{0,15},{1,14},{2,13},{3,12},{4,11},{5,10},{6,9},{7,8},{8,7},{9,6},... | collective-permute-start | bytes 233480 | tf_op jit(solution)/shard_map/ppermute | solution.py:292
  34.1 4.4 %shard_map.92.refs_1_ = f32[65,1024]{1,0:T(8,128)} custom-call(bf16[65,1024]{1,0:T(8,128)(2,1)} %probes_hbm.1, bf16[8,8,128,128]{3,2,1,0:T(8,128)(2,1)} %local_hbm.1, bf16[304,128]{1,0:T(8,128)(2,1)} %get-tuple-element.21.refs_0_.refs_5_, bf16[304,128]{1,0:T(8,128)(2,1)} %copy-done, bf16[304,128]{1,0:T(8,128)(2,1)} %copy-done.1, bf16[304,128]{1,0:T(8,128)(2,1)} %copy-done.2, ...), custom_call_target="tpu_custom_call" | custom-call | flops 136314880 | bytes 2953216 | tf_op jit(solution)/shard_map/pallas_call | solution.py:233
  38.6 0.2 collective-permute-done.14.refs_20_
  38.8 0.4 copy-done.10
  39.1 0.0 copy-done.11
  39.2 0.0 copy-done.12
  39.2 0.0 copy-done.13
  39.2 0.6 %copy-done.14 = bf16[304,128]{1,0:T(8,128)(2,1)} copy-done((bf16[304,128]{1,0:T(8,128)(2,1)}, bf16[304,128]{1,0:T(8,128)(2,1)S(1)}, u32[]{:S(2)}) %copy-start.14) | copy-done | bytes 77848
  39.9 4.0 %shard_map.93 = f32[65,1024]{1,0:T(8,128)} custom-call(s32[1,12]{1,0:T(1,128)} %refs_0_.1, f32[65,1024]{1,0:T(8,128)} %shard_map.92.refs_1_, bf16[1,12,64,64]{3,2,1,0:T(8,128)(2,1)} %refs_2_.3, bf16[8,64,64]{2,1,0:T(8,128)(2,1)} %refs_3_.3, bf16[8,64,128]{2,1,0:T(8,128)(2,1)} %refs_4_.3, bf16[304,128]{1,0:T(8,128)(2,1)} %get-tuple-element.21.refs_0_.refs_5_, ...), custom_call_target="tpu_custom_call" | custom-call | flops 166400 | bytes 1245184 | tf_op jit(solution)/shard_map/pallas_call | solution.py:233
  (39 shorter events, 0.1 us)
Async XLA Ops:
  3.6 8.6 %collective-permute-start = (bf16[304,128]{1,0:T(8,128)(2,1)}, bf16[304,128]{1,0:T(8,128)(2,1)S(1)}, u32[]{:S(2)}, u32[]{:S(2)}) collective-permute-start(bf16[304,128]{1,0:T(8,128)(2,1)} %get-tuple-element.22), channel_id=1, source_target_pairs={{0,8},{1,9},{2,10},{3,11},{4,12},{5,13},{6,14},{7,15},{8,0},{9,1},... | collective-permute-start | bytes 233480 | tf_op jit(solution)/shard_map/ppermute | solution.py:292
  7.7 5.1 %collective-permute-start.1 = (bf16[304,128]{1,0:T(8,128)(2,1)}, bf16[304,128]{1,0:T(8,128)(2,1)S(1)}, u32[]{:S(2)}, u32[]{:S(2)}) collective-permute-start(bf16[304,128]{1,0:T(8,128)(2,1)} %get-tuple-element.23), channel_id=1, source_target_pairs={{0,1},{1,0},{2,3},{3,2},{4,5},{5,4},{6,7},{7,6},{8,9},{9,8},{10,11... | collective-permute-start | bytes 233480 | tf_op jit(solution)/shard_map/ppermute | solution.py:292
  7.7 8.8 %collective-permute-start.2 = (bf16[304,128]{1,0:T(8,128)(2,1)}, bf16[304,128]{1,0:T(8,128)(2,1)S(1)}, u32[]{:S(2)}, u32[]{:S(2)}) collective-permute-start(bf16[304,128]{1,0:T(8,128)(2,1)} %get-tuple-element.24), channel_id=1, source_target_pairs={{0,9},{1,8},{2,11},{3,10},{4,13},{5,12},{6,15},{7,14},{8,1},{9,0},... | collective-permute-start | bytes 233480 | tf_op jit(solution)/shard_map/ppermute | solution.py:292
  7.9 12.8 %collective-permute-start.3 = (bf16[304,128]{1,0:T(8,128)(2,1)}, bf16[304,128]{1,0:T(8,128)(2,1)S(1)}, u32[]{:S(2)}, u32[]{:S(2)}) collective-permute-start(bf16[304,128]{1,0:T(8,128)(2,1)} %get-tuple-element.25), channel_id=1, source_target_pairs={{0,2},{1,3},{2,0},{3,1},{4,6},{5,7},{6,4},{7,5},{8,10},{9,11},{10,... | collective-permute-start | bytes 233480 | tf_op jit(solution)/shard_map/ppermute | solution.py:292
  9.6 12.4 %collective-permute-start.4 = (bf16[304,128]{1,0:T(8,128)(2,1)}, bf16[304,128]{1,0:T(8,128)(2,1)S(1)}, u32[]{:S(2)}, u32[]{:S(2)}) collective-permute-start(bf16[304,128]{1,0:T(8,128)(2,1)} %get-tuple-element.26), channel_id=1, source_target_pairs={{0,10},{1,11},{2,8},{3,9},{4,14},{5,15},{6,12},{7,13},{8,2},{9,3},... | collective-permute-start | bytes 233480 | tf_op jit(solution)/shard_map/ppermute | solution.py:292
  12.2 21.8 %copy-start = (bf16[304,128]{1,0:T(8,128)(2,1)}, bf16[304,128]{1,0:T(8,128)(2,1)S(1)}, u32[]{:S(2)}) copy-start(bf16[304,128]{1,0:T(8,128)(2,1)S(1)} %collective-permute-done.refs_1_.refs_13_) | copy-start | bytes 233476
  12.2 10.1 %collective-permute-start.5 = (bf16[304,128]{1,0:T(8,128)(2,1)}, bf16[304,128]{1,0:T(8,128)(2,1)S(1)}, u32[]{:S(2)}, u32[]{:S(2)}) collective-permute-start(bf16[304,128]{1,0:T(8,128)(2,1)} %get-tuple-element.27), channel_id=1, source_target_pairs={{0,3},{1,2},{2,1},{3,0},{4,7},{5,6},{6,5},{7,4},{8,11},{9,10},{10,... | collective-permute-start | bytes 233480 | tf_op jit(solution)/shard_map/ppermute | solution.py:292
  12.7 21.3 %copy-start.1 = (bf16[304,128]{1,0:T(8,128)(2,1)}, bf16[304,128]{1,0:T(8,128)(2,1)S(1)}, u32[]{:S(2)}) copy-start(bf16[304,128]{1,0:T(8,128)(2,1)S(1)} %collective-permute-done.1.refs_2_.refs_6_) | copy-start | bytes 233476
  12.7 12.0 %collective-permute-start.6 = (bf16[304,128]{1,0:T(8,128)(2,1)}, bf16[304,128]{1,0:T(8,128)(2,1)S(1)}, u32[]{:S(2)}, u32[]{:S(2)}) collective-permute-start(bf16[304,128]{1,0:T(8,128)(2,1)} %get-tuple-element.28), channel_id=1, source_target_pairs={{0,11},{1,10},{2,9},{3,8},{4,15},{5,14},{6,13},{7,12},{8,3},{9,2},... | collective-permute-start | bytes 233480 | tf_op jit(solution)/shard_map/ppermute | solution.py:292
  16.4 17.6 %copy-start.2 = (bf16[304,128]{1,0:T(8,128)(2,1)}, bf16[304,128]{1,0:T(8,128)(2,1)S(1)}, u32[]{:S(2)}) copy-start(bf16[304,128]{1,0:T(8,128)(2,1)S(1)} %collective-permute-done.2.refs_3_.refs_14_) | copy-start | bytes 233476
  16.4 9.1 %collective-permute-start.7 = (bf16[304,128]{1,0:T(8,128)(2,1)}, bf16[304,128]{1,0:T(8,128)(2,1)S(1)}, u32[]{:S(2)}, u32[]{:S(2)}) collective-permute-start(bf16[304,128]{1,0:T(8,128)(2,1)} %get-tuple-element.29), channel_id=1, source_target_pairs={{0,4},{1,5},{2,6},{3,7},{4,0},{5,1},{6,2},{7,3},{8,12},{9,13},{10,... | collective-permute-start | bytes 233480 | tf_op jit(solution)/shard_map/ppermute | solution.py:292
  20.7 13.4 %copy-start.3 = (bf16[304,128]{1,0:T(8,128)(2,1)}, bf16[304,128]{1,0:T(8,128)(2,1)S(1)}, u32[]{:S(2)}) copy-start(bf16[304,128]{1,0:T(8,128)(2,1)S(1)} %collective-permute-done.3.refs_4_.refs_7_) | copy-start | bytes 233476
  20.7 8.7 %collective-permute-start.8 = (bf16[304,128]{1,0:T(8,128)(2,1)}, bf16[304,128]{1,0:T(8,128)(2,1)S(1)}, u32[]{:S(2)}, u32[]{:S(2)}) collective-permute-start(bf16[304,128]{1,0:T(8,128)(2,1)} %get-tuple-element.30), channel_id=1, source_target_pairs={{0,12},{1,13},{2,14},{3,15},{4,8},{5,9},{6,10},{7,11},{8,4},{9,5},... | collective-permute-start | bytes 233480 | tf_op jit(solution)/shard_map/ppermute | solution.py:292
  22.1 12.0 %copy-start.4 = (bf16[304,128]{1,0:T(8,128)(2,1)}, bf16[304,128]{1,0:T(8,128)(2,1)S(1)}, u32[]{:S(2)}) copy-start(bf16[304,128]{1,0:T(8,128)(2,1)S(1)} %collective-permute-done.4.refs_5_.refs_15_) | copy-start | bytes 233476
  22.1 9.3 %collective-permute-start.9 = (bf16[304,128]{1,0:T(8,128)(2,1)}, bf16[304,128]{1,0:T(8,128)(2,1)S(1)}, u32[]{:S(2)}, u32[]{:S(2)}) collective-permute-start(bf16[304,128]{1,0:T(8,128)(2,1)} %get-tuple-element.31), channel_id=1, source_target_pairs={{0,5},{1,4},{2,7},{3,6},{4,1},{5,0},{6,3},{7,2},{8,13},{9,12},{10,... | collective-permute-start | bytes 233480 | tf_op jit(solution)/shard_map/ppermute | solution.py:292
  22.3 11.8 %copy-start.5 = (bf16[304,128]{1,0:T(8,128)(2,1)}, bf16[304,128]{1,0:T(8,128)(2,1)S(1)}, u32[]{:S(2)}) copy-start(bf16[304,128]{1,0:T(8,128)(2,1)S(1)} %collective-permute-done.5.refs_6_.refs_8_) | copy-start | bytes 233476
  22.3 16.2 %collective-permute-start.10 = (bf16[304,128]{1,0:T(8,128)(2,1)}, bf16[304,128]{1,0:T(8,128)(2,1)S(1)}, u32[]{:S(2)}, u32[]{:S(2)}) collective-permute-start(bf16[304,128]{1,0:T(8,128)(2,1)} %get-tuple-element.32), channel_id=1, source_target_pairs={{0,6},{1,7},{2,4},{3,5},{4,2},{5,3},{6,0},{7,1},{8,14},{9,15},{10,... | collective-permute-start | bytes 233480 | tf_op jit(solution)/shard_map/ppermute | solution.py:292
  24.7 9.3 %copy-start.6 = (bf16[304,128]{1,0:T(8,128)(2,1)}, bf16[304,128]{1,0:T(8,128)(2,1)S(1)}, u32[]{:S(2)}) copy-start(bf16[304,128]{1,0:T(8,128)(2,1)S(1)} %collective-permute-done.6.refs_7_.refs_16_) | copy-start | bytes 233476
  24.7 13.8 %collective-permute-start.11 = (bf16[304,128]{1,0:T(8,128)(2,1)}, bf16[304,128]{1,0:T(8,128)(2,1)S(1)}, u32[]{:S(2)}, u32[]{:S(2)}) collective-permute-start(bf16[304,128]{1,0:T(8,128)(2,1)} %get-tuple-element.33), channel_id=1, source_target_pairs={{0,7},{1,6},{2,5},{3,4},{4,3},{5,2},{6,1},{7,0},{8,15},{9,14},{10,... | collective-permute-start | bytes 233480 | tf_op jit(solution)/shard_map/ppermute | solution.py:292
  25.5 8.6 %copy-start.7 = (bf16[304,128]{1,0:T(8,128)(2,1)}, bf16[304,128]{1,0:T(8,128)(2,1)S(1)}, u32[]{:S(2)}) copy-start(bf16[304,128]{1,0:T(8,128)(2,1)S(1)} %collective-permute-done.7.refs_8_.refs_9_) | copy-start | bytes 233476
  25.5 13.1 %collective-permute-start.12 = (bf16[304,128]{1,0:T(8,128)(2,1)}, bf16[304,128]{1,0:T(8,128)(2,1)S(1)}, u32[]{:S(2)}, u32[]{:S(2)}) collective-permute-start(bf16[304,128]{1,0:T(8,128)(2,1)} %get-tuple-element.34), channel_id=1, source_target_pairs={{0,13},{1,12},{2,15},{3,14},{4,9},{5,8},{6,11},{7,10},{8,5},{9,4},... | collective-permute-start | bytes 233480 | tf_op jit(solution)/shard_map/ppermute | solution.py:292
  29.4 4.7 %copy-start.8 = (bf16[304,128]{1,0:T(8,128)(2,1)}, bf16[304,128]{1,0:T(8,128)(2,1)S(1)}, u32[]{:S(2)}) copy-start(bf16[304,128]{1,0:T(8,128)(2,1)S(1)} %collective-permute-done.8.refs_9_.refs_17_) | copy-start | bytes 233476
  29.4 9.2 %collective-permute-start.13 = (bf16[304,128]{1,0:T(8,128)(2,1)}, bf16[304,128]{1,0:T(8,128)(2,1)S(1)}, u32[]{:S(2)}, u32[]{:S(2)}) collective-permute-start(bf16[304,128]{1,0:T(8,128)(2,1)} %get-tuple-element.35), channel_id=1, source_target_pairs={{0,14},{1,15},{2,12},{3,13},{4,10},{5,11},{6,8},{7,9},{8,6},{9,7},... | collective-permute-start | bytes 233480 | tf_op jit(solution)/shard_map/ppermute | solution.py:292
  31.4 7.4 %collective-permute-start.14 = (bf16[304,128]{1,0:T(8,128)(2,1)}, bf16[304,128]{1,0:T(8,128)(2,1)S(1)}, u32[]{:S(2)}, u32[]{:S(2)}) collective-permute-start(bf16[304,128]{1,0:T(8,128)(2,1)} %get-tuple-element.36), channel_id=1, source_target_pairs={{0,15},{1,14},{2,13},{3,12},{4,11},{5,10},{6,9},{7,8},{8,7},{9,6},... | collective-permute-start | bytes 233480 | tf_op jit(solution)/shard_map/ppermute | solution.py:292
  (6 other events, 5.9 us)

commit v6 on v4

v6 whole, which is shorter than its diff:
```python
import functools

import jax
import jax.numpy as jnp
from jax import lax
from jax.experimental import pallas as pl
from jax.experimental.pallas import tpu as pltpu
from jax.sharding import PartitionSpec as P

CAP = 4
TILE = 16
LANES = 128
F32 = jnp.float32
BF16 = jnp.bfloat16
I32 = jnp.int32

ANY = pl.BlockSpec(memory_space=pl.ANY)
VMEM = pl.BlockSpec(memory_space=pltpu.VMEM)


def dot_t(lhs, rhs):
    return lax.dot_general(lhs, rhs, (((1,), (1,)), ((), ())), preferred_element_type=F32)


def dot(lhs, rhs):
    return lax.dot_general(lhs, rhs, (((1,), (0,)), ((), ())), preferred_element_type=F32)


class Copies:
    def __init__(self, sems):
        self.sems, self.used = sems, 0

    def start(self, src, dst):
        copy = pltpu.make_async_copy(src, dst, self.sems.at[self.used])
        self.used += 1
        copy.start()
        return copy


def grid_of(devices):
    low = 1 << (devices.bit_length() // 2)
    return devices // low, low


def up(rows):
    return -(-rows // TILE) * TILE


class Route:
    def __init__(self, first, last, fan, extra, main, columns, leaves, sources):
        self.first, self.rows, self.fan, self.extra, self.main = first, last - first, fan, extra, main
        self.leaves, self.half = leaves, main // 2
        slots = fan * CAP
        self.tails = slots * self.rows
        self.meta = self.tails + (up(slots) if extra else 0)
        self.box = self.meta + TILE
        self.depth = self.box + (self.half if extra else 0)
        self.dense_tails = leaves * self.rows
        self.dense_box = self.dense_tails + (up(leaves + sources) if extra else 0)
        self.dense_depth = self.dense_box + (sources * self.half if extra else 0)


def routes_of(devices, main, columns, leaves):
    high, low = grid_of(devices)
    split = main // 4 * 3
    return (
        Route(0, split, high, False, main, columns, leaves, low),
        Route(split, main, low, True, main, columns, leaves, high),
    )


def products_kernel(routes, devices, *refs):
    dest_hbm, leaf_hbm, probes_hbm, basis_hbm, transfer_hbm, blocks_hbm = refs[:6]
    (
        outs_low, outs_high, dest_ref, leaf_ref, probes_ref, basis_ref, transfer_ref, blocks_ref,
        send_low, send_high, tails, meta_low, meta_high, count, sems,
    ) = refs[6:]
    by_low, by_high = routes
    high, low = grid_of(devices)
    main = by_high.main
    leaves, per_leaf, size = blocks_ref.shape[:3]
    columns, rank = probes_ref.shape[0], basis_ref.shape[1]
    copies = Copies(sems)
    early = [
        copies.start(probes_hbm, probes_ref),
        copies.start(basis_hbm, basis_ref),
        copies.start(transfer_hbm, transfer_ref),
        copies.start(dest_hbm, dest_ref),
        copies.start(leaf_hbm, leaf_ref),
    ]
    chunk = leaves // 2
    arrivals = [
        copies.start(blocks_hbm.at[pl.ds(j, chunk)], blocks_ref.at[pl.ds(j, chunk)])
        for j in range(0, leaves, chunk)
    ]

    @pl.loop(0, devices)
    def _(i):
        count[i] = 0

    tails[...] = jnp.zeros(tails.shape, F32)
    meta_low[...] = jnp.full(meta_low.shape, leaves, F32)
    meta_high[...] = jnp.full(meta_high.shape, leaves, F32)
    for copy in early:
        copy.wait()
    box = jnp.zeros((columns, rank), F32)
    for j in range(leaves):
        coef = dot_t(probes_ref[:, j * size : (j + 1) * size], basis_ref[j]).astype(BF16)
        box += dot_t(coef, transfer_ref[j])
    half = by_high.half
    packed = jnp.concatenate([box[:half], box[half:main]], axis=1).astype(BF16)
    last = jnp.concatenate([box[main:], jnp.zeros_like(box[main:])], axis=1)

    lane = lax.broadcasted_iota(I32, (1, size), 1)
    for j in range(leaves):
        if j % chunk == 0:
            arrivals[j // chunk].wait()
        x = probes_ref[:, j * size : (j + 1) * size]
        for first in range(0, per_leaf, 4):
            many = min(4, per_leaf - first)
            rhs = blocks_ref[j, first : first + many].reshape(many * size, size)
            product = dot_t(x, rhs)
            for b in range(many):
                target = dest_ref[first + b, j]
                slot = count[target]
                count[target] = slot + 1
                to_high, to_low = target // low, target % low
                block = product[:, b * size : (b + 1) * size]
                piece = block[:main].astype(BF16)
                number = leaf_ref[first + b, j].astype(F32)

                at = to_high * CAP + slot
                rows = pl.ds(pl.multiple_of(at * by_low.rows, TILE), by_low.rows)
                send_low[to_low, rows, :] = piece[: by_low.rows]
                meta_low[to_low, 0:1, :] = jnp.where(lane == at, number, meta_low[to_low, 0:1, :])

                at = to_low * CAP + slot
                rows = pl.ds(pl.multiple_of(at * by_high.rows, TILE), by_high.rows)
                send_high[to_high, rows, :] = piece[by_low.rows :]
                tails[to_high, pl.ds(at, 1), :] = block[main:]
                meta_high[to_high, 0:1, :] = jnp.where(lane == at, number, meta_high[to_high, 0:1, :])

    for i in range(low):
        send_low[i, by_low.meta : by_low.box, :] = meta_low[i].astype(BF16)
    for i in range(high):
        meta_high[i, 1:2, :] = last
        send_high[i, by_high.tails : by_high.meta, :] = tails[i].astype(BF16)
        send_high[i, by_high.meta : by_high.box, :] = meta_high[i].astype(BF16)
        send_high[i, by_high.box :, :] = packed
    for copy in [copies.start(send_low, outs_low), copies.start(send_high, outs_high)]:
        copy.wait()


def sum_kernel(routes, devices, *refs):
    came_low, came_high, outs_high, outs_low = refs[:4]
    in_low, in_high, meta, leaf_ref, total_low, total_high, total_tails, send_high, send_low, sems, late = refs[4:]
    by_low, by_high = routes
    high, low = grid_of(devices)
    leaves = by_low.leaves
    copies = Copies(sems)
    arrivals = [
        [
            copies.start(came.at[i, pl.ds(route.meta, TILE)], ref.at[i, pl.ds(route.meta, TILE)])
            for i in range(ways)
        ]
        for came, ref, route, ways in ((came_low, in_low, by_low, low), (came_high, in_high, by_high, high))
    ]
    large = [
        copies.start(came_low.at[:, pl.ds(0, by_low.meta)], in_low.at[:, pl.ds(0, by_low.meta)]),
        copies.start(came_high.at[:, pl.ds(0, by_high.meta)], in_high.at[:, pl.ds(0, by_high.meta)]),
        copies.start(
            came_high.at[:, pl.ds(by_high.box, by_high.half)], in_high.at[:, pl.ds(by_high.box, by_high.half)]
        ),
    ]
    at = 0
    for ref, route, group in ((in_low, by_low, arrivals[0]), (in_high, by_high, arrivals[1])):
        for i, copy in enumerate(group):
            copy.wait()
            tile = ref[i, route.meta : route.box, :].astype(F32)
            meta[at : at + 1, :] = tile[:1].astype(I32)
            at += 1
    numbers = pltpu.make_async_copy(meta, leaf_ref, late)
    numbers.start()
    total_low[...] = jnp.zeros(total_low.shape, F32)
    total_high[...] = jnp.zeros(total_high.shape, F32)
    total_tails[...] = jnp.zeros(total_tails.shape, F32)
    numbers.wait()
    for copy in large:
        copy.wait()

    @pl.loop(0, low)
    def _(i):
        for k in range(high):
            for slot in range(CAP):
                at = k * CAP + slot
                leaf = leaf_ref[i, at]
                rows = pl.ds(pl.multiple_of(leaf * by_low.rows, TILE), by_low.rows)
                total_low[k, rows, :] += in_low[i, at * by_low.rows : (at + 1) * by_low.rows, :].astype(F32)

    @pl.loop(0, high)
    def _(i):
        tail = in_high[i, by_high.tails : by_high.meta, :].astype(F32)
        for k in range(low):
            for slot in range(CAP):
                at = k * CAP + slot
                leaf = leaf_ref[low + i, at]
                rows = pl.ds(pl.multiple_of(leaf * by_high.rows, TILE), by_high.rows)
                total_high[k, rows, :] += in_high[i, at * by_high.rows : (at + 1) * by_high.rows, :].astype(F32)
                total_tails[k, pl.ds(leaf, 1), :] += tail[at : at + 1]

    for k in range(high):
        send_high[k] = total_low[k, : by_low.dense_tails, :].astype(BF16)
    lasts = [in_high[i, by_high.meta : by_high.box, :].astype(F32)[1:2] for i in range(high)]
    for k in range(low):
        send_low[k, : by_high.dense_tails, :] = total_high[k, : by_high.dense_tails, :].astype(BF16)
        for i in range(high):
            total_tails[k, leaves + i : leaves + i + 1, :] = lasts[i]
            start = by_high.dense_box + i * by_high.half
            send_low[k, start : start + by_high.half, :] = in_high[i, by_high.box :, :]
        send_low[k, by_high.dense_tails : by_high.dense_box, :] = total_tails[k].astype(BF16)
    for copy in [copies.start(send_high, outs_high), copies.start(send_low, outs_low)]:
        copy.wait()


def local_part(probes_ref, local_ref, out_ref):
    leaves, size = local_ref.shape[0], local_ref.shape[2]
    for i in range(leaves):
        total = dot_t(probes_ref[:, :size], local_ref[i, 0])
        for c in range(1, leaves):
            total += dot_t(probes_ref[:, c * size : (c + 1) * size], local_ref[i, c])
        out_ref[:, i * size : (i + 1) * size] = total


def local_kernel(probes_hbm, local_hbm, base_ref, probes_ref, local_ref, sems):
    copies = Copies(sems)
    for copy in [copies.start(probes_hbm, probes_ref), copies.start(local_hbm, local_ref)]:
        copy.wait()
    local_part(probes_ref, local_ref, base_ref)


def last_kernel(routes, devices, *refs):
    (
        partner_hbm, base_hbm, couplings_hbm, transfer_hbm, basis_hbm, came_high, came_low,
        out_ref, partner_ref, base_ref, couplings_ref, transfer_ref, basis_ref, in_high, in_low, sems,
    ) = refs
    by_low, by_high = routes
    high, low = grid_of(devices)
    columns = out_ref.shape[0]
    leaves, rank, size = basis_ref.shape
    split, main = by_low.rows, by_low.main
    copies = Copies(sems)
    early = [
        copies.start(came_low, in_low),
        copies.start(partner_hbm, partner_ref),
        copies.start(couplings_hbm, couplings_ref),
        copies.start(transfer_hbm, transfer_ref),
        copies.start(basis_hbm, basis_ref),
    ]
    later = [copies.start(came_high, in_high), copies.start(base_hbm, base_ref)]
    for copy in early:
        copy.wait()
    far = jnp.zeros((columns, rank), F32)
    for f in range(couplings_ref.shape[1]):
        source = partner_ref[0, f]
        to_high, to_low = source // low, source % low
        start = pl.multiple_of(by_high.dense_box + to_high * by_high.half, TILE)
        packed = in_low[to_low, pl.ds(start, by_high.half), :]
        tile = in_low[to_low, by_high.dense_tails : by_high.dense_box, :].astype(F32)
        row = lax.broadcasted_iota(I32, tile.shape, 0)
        last = jnp.sum(jnp.where(row == leaves + to_high, tile, 0.0), axis=0, keepdims=True)[:, :rank]
        box = jnp.concatenate(
            [packed[:, :rank].astype(F32), packed[:, rank:].astype(F32), last], axis=0
        ).astype(BF16)
        far += dot_t(box, couplings_ref[0, f])
    far = far.astype(BF16)
    down = [dot(far, transfer_ref[j]).astype(BF16) for j in range(leaves)]
    far_part = [dot(down[j], basis_ref[j]) for j in range(leaves)]
    for copy in later:
        copy.wait()
    tails = sum(in_low[k, by_high.dense_tails : by_high.dense_box, :].astype(F32) for k in range(low))
    for j in range(leaves):
        cols = slice(j * size, (j + 1) * size)
        upper = sum(in_high[k, j * by_low.rows : (j + 1) * by_low.rows, :].astype(F32) for k in range(high))
        lower = sum(in_low[k, j * by_high.rows : (j + 1) * by_high.rows, :].astype(F32) for k in range(low))
        out_ref[:split, cols] = base_ref[:split, cols] + far_part[j][:split] + upper
        out_ref[split:main, cols] = base_ref[split:main, cols] + far_part[j][split:main] + lower
        out_ref[main:, cols] = base_ref[main:, cols] + far_part[j][main:] + tails[j : j + 1]


def call(kernel, out_shape, out_specs, operands, scratch, flops, nbytes):
    return pl.pallas_call(
        kernel,
        out_shape=out_shape,
        in_specs=[ANY] * len(operands),
        out_specs=out_specs,
        scratch_shapes=scratch,
        cost_estimate=pl.CostEstimate(flops=flops, bytes_accessed=nbytes, transcendentals=0),
    )(*operands)


def per_device(
    probes, basis, transfer, local_blocks, remote_blocks, near_dest, near_leaf, couplings, far_list
):
    columns, points = probes.shape
    leaves, rank, size = basis.shape
    devices = lax.axis_size("leaf")
    main = columns // TILE * TILE
    routes = by_low, by_high = routes_of(devices, main, columns, leaves)
    high, low = grid_of(devices)
    blocks = remote_blocks.shape[0] * remote_blocks.shape[1]
    unit = 2 * columns * size * size
    like = lambda *arrays: [pltpu.VMEM(a.shape, a.dtype) for a in arrays]
    numbers = lambda *arrays: [pltpu.SMEM(a.shape, a.dtype) for a in arrays]
    sems = lambda count: [pltpu.SemaphoreType.DMA((count,))]
    same_high = [[h * low + l for l in range(low)] for h in range(high)]
    same_low = [[h * low + l for h in range(high)] for l in range(low)]
    exchange = lambda x, groups: lax.all_to_all(
        x, "leaf", split_axis=0, concat_axis=0, tiled=True, axis_index_groups=groups
    )

    to_low = jax.ShapeDtypeStruct((low, by_low.depth, size), BF16)
    to_high = jax.ShapeDtypeStruct((high, by_high.depth, size), BF16)
    dest, leaf = near_dest.T, near_leaf.T
    send_low, send_high = call(
        functools.partial(products_kernel, routes, devices),
        [to_low, to_high],
        [ANY, ANY],
        (dest, leaf, probes, basis, transfer, remote_blocks),
        numbers(dest, leaf)
        + like(probes, basis, transfer, remote_blocks, to_low, to_high)
        + [
            pltpu.VMEM((high, by_high.meta - by_high.tails, size), F32),
            pltpu.VMEM((low, TILE, size), F32),
            pltpu.VMEM((high, TILE, size), F32),
            pltpu.SMEM((devices,), I32),
        ]
        + sems(9),
        blocks * unit,
        remote_blocks.size * 2 + to_low.size * 2 + to_high.size * 2,
    )
    came_low = exchange(send_low, same_high)
    came_high = exchange(send_high, same_low)

    base = call(
        local_kernel,
        jax.ShapeDtypeStruct((columns, points), F32),
        VMEM,
        (probes, local_blocks),
        like(probes, local_blocks) + sems(2),
        leaves * leaves * unit,
        local_blocks.size * 2,
    )

    dense_high = jax.ShapeDtypeStruct((high, by_low.dense_depth, size), BF16)
    dense_low = jax.ShapeDtypeStruct((low, by_high.dense_depth, size), BF16)
    send_high, send_low = call(
        functools.partial(sum_kernel, routes, devices),
        [dense_high, dense_low],
        [ANY, ANY],
        (came_low, came_high),
        like(came_low, came_high)
        + [
            pltpu.VMEM((low + high, size), I32),
            pltpu.SMEM((low + high, size), I32),
            pltpu.VMEM((high, (leaves + 1) * by_low.rows, size), F32),
            pltpu.VMEM((low, (leaves + 1) * by_high.rows, size), F32),
            pltpu.VMEM((low, by_high.dense_box - by_high.dense_tails, size), F32),
        ]
        + like(dense_high, dense_low)
        + sems(5 + low + high)
        + [pltpu.SemaphoreType.DMA(())],
        devices * CAP * columns * size,
        4 * (to_low.size + to_high.size),
    )
    came_high = exchange(send_high, same_low)
    came_low = exchange(send_low, same_high)

    return call(
        functools.partial(last_kernel, routes, devices),
        jax.ShapeDtypeStruct((columns, points), F32),
        VMEM,
        (far_list, base, couplings, transfer, basis, came_high, came_low),
        numbers(far_list) + like(base, couplings, transfer, basis, came_high, came_low) + sems(7),
        devices * columns * size,
        2 * (dense_high.size + dense_low.size),
    )


def solution(mesh):
    placed = (
        P(None, ("grp", "leaf")),
        P(("grp", "leaf"), None, None),
        P(("grp", "leaf"), None, None),
        P(("grp", "leaf"), None, None, None),
        P(("grp", "leaf"), None, None, None),
        P(("grp", "leaf"), None),
        P(("grp", "leaf"), None),
        P(("grp", "leaf"), None, None, None),
        P(("grp", "leaf"), None),
    )
    return jax.shard_map(
        per_device, mesh=mesh, in_specs=placed, out_specs=P(None, ("grp", "leaf")), check_vma=False
    )
```

time: 48.1 us -> 69.3 us (1.44)
  the two profiles are of different devices: /device:TPU:17 before, /device:TPU:0 now
where the time goes in v6:
time: 69.3 us; the launch traced here: 68.8 us
  blocking collectives  43.2 us (62%)
  Pallas kernels  13.2 us (19%)
  waiting for transfers between devices  8.18 us (12%)
  starting transfers between devices  3.46 us (5%)
  local copies, waits for them, and re-layouts  0.75 us (1%)
    all_to_all x3, blocking collectives, per_device(): lax.all_to_all(x, 'leaf', split_axis=0, concat_axis=0, tiled=True, axis_i...  43.2 us
    pallas_call x4, Pallas kernels, call(): pl.pallas_call(kernel, out_shape=out_shape, in_specs=[ANY] * len(operands...  13.2 us
    all_to_all x1, waiting for transfers between devices, per_device(): lax.all_to_all(x, 'leaf', split_axis=0, concat_axis=0, tiled=True, axis_i...  8.18 us
    all_to_all x1, starting transfers between devices, per_device(): lax.all_to_all(x, 'leaf', split_axis=0, concat_axis=0, tiled=True, axis_i...  3.46 us
  transfers between devices with their start and end apart: 1, of which 1 were waited for; matrix products, arithmetic and copies ran while one was open for 0% of the time, Pallas kernels for 6%

profile of v6, /device:TPU:0, one launch (start us, length us, event | category | flops | bytes accessed | tf_op | source)
XLA Modules:
  0.0 68.8 jit_solution(3670499962595737725)
XLA Ops:
  0.0 3.3 %shard_map.92 = (bf16[4,784,128]{2,1,0:T(8,128)(2,1)}, bf16[4,320,128]{2,1,0:T(8,128)(2,1)}) custom-call(s32[4,8]{1,0:T(4,128)} %bitcast.2, s32[4,8]{1,0:T(4,128)} %bitcast.3, bf16[65,1024]{1,0:T(8,128)(2,1)} %refs_2_.2, bf16[8,64,128]{2,1,0:T(8,128)(2,1)} %refs_4_.3, bf16[8,64,64]{2,1,0:T(8,128)(2,1)} %refs_3_.3, bf16[8,4,128,128]{3,2,1,0:T(8,128)(2,1)} %refs_5_.1), custom_call_target="tpu_custom_call" | custom-call | flops 68157440 | bytes 2179072 | tf_op jit(solution)/shard_map/pallas_call | solution.py:291
  3.4 16.7 %all_to_all.20.refs_1_ = bf16[4,320,128]{2,1,0:T(8,128)(2,1)} all-to-all(bf16[4,320,128]{2,1,0:T(8,128)(2,1)} %get-tuple-element.10), channel_id=1, replica_groups={{0,4,8,12},{1,5,9,13},{2,6,10,14},{3,7,11,15},{16,20,24,28},{17,21,25,2..., dimensions={0} | all-to-all | bytes 655360 | tf_op jit(solution)/shard_map/all_to_all | solution.py:317
  20.1 16.1 %all_to_all.21.refs_0_ = bf16[4,784,128]{2,1,0:T(8,128)(2,1)} all-to-all(bf16[4,784,128]{2,1,0:T(8,128)(2,1)} %get-tuple-element.9), channel_id=1, replica_groups={{0,1,2,3},{4,5,6,7},{8,9,10,11},{12,13,14,15},{16,17,18,19},{20,21,22,2..., dimensions={0} | all-to-all | bytes 1605632 | tf_op jit(solution)/shard_map/all_to_all | solution.py:317
  36.2 3.1 %shard_map.93 = (bf16[4,384,128]{2,1,0:T(8,128)(2,1)}, bf16[4,272,128]{2,1,0:T(8,128)(2,1)}) custom-call(bf16[4,784,128]{2,1,0:T(8,128)(2,1)} %all_to_all.21.refs_0_, bf16[4,320,128]{2,1,0:T(8,128)(2,1)} %all_to_all.20.refs_1_), custom_call_target="tpu_custom_call" | custom-call | flops 532480 | bytes 2260992 | tf_op jit(solution)/shard_map/pallas_call | solution.py:291
  39.2 10.4 %all_to_all.22.refs_6_ = bf16[4,272,128]{2,1,0:T(8,128)(2,1)} all-to-all(bf16[4,272,128]{2,1,0:T(8,128)(2,1)} %get-tuple-element.12), channel_id=1, replica_groups={{0,1,2,3},{4,5,6,7},{8,9,10,11},{12,13,14,15},{16,17,18,19},{20,21,22,2..., dimensions={0} | all-to-all | bytes 557056 | tf_op jit(solution)/shard_map/all_to_all | solution.py:317
  49.6 3.5 %all-to-all-start.2 = ((bf16[4,384,128]{2,1,0:T(8,128)(2,1)}), bf16[4,384,128]{2,1,0:T(8,128)(2,1)S(1)}, u32[]{:S(2)}, u32[]{:S(2)}) async-start(bf16[4,384,128]{2,1,0:T(8,128)(2,1)} %get-tuple-element.11), calls=%async_computation.2 | async-start | bytes 786432 | tf_op jit(solution)/shard_map/all_to_all | solution.py:317
  53.1 3.9 %shard_map.91.refs_1_ = f32[65,1024]{1,0:T(8,128)} custom-call(bf16[65,1024]{1,0:T(8,128)(2,1)} %refs_2_.2, bf16[8,8,128,128]{3,2,1,0:T(8,128)(2,1)} %local_hbm.1), custom_call_target="tpu_custom_call" | custom-call | flops 136314880 | bytes 2097152 | tf_op jit(solution)/shard_map/pallas_call | solution.py:291
  57.0 8.2 %all-to-all-done.2.refs_5_ = bf16[4,384,128]{2,1,0:T(8,128)(2,1)S(1)} async-done(((bf16[4,384,128]{2,1,0:T(8,128)(2,1)}), bf16[4,384,128]{2,1,0:T(8,128)(2,1)S(1)}, u32[]{:S(2)}, u32[]{:S(2)}) %all-to-all-start.2) | async-done | bytes 393248 | tf_op jit(solution)/shard_map/all_to_all | solution.py:317
  65.2 0.0 copy-start
  65.2 0.7 %copy-done = bf16[4,384,128]{2,1,0:T(8,128)(2,1)} copy-done((bf16[4,384,128]{2,1,0:T(8,128)(2,1)}, bf16[4,384,128]{2,1,0:T(8,128)(2,1)S(1)}, u32[]{:S(2)}) %copy-start) | copy-done | bytes 393240
  65.9 2.9 %shard_map.94 = f32[65,1024]{1,0:T(8,128)} custom-call(s32[1,12]{1,0:T(1,128)} %refs_0_.1, f32[65,1024]{1,0:T(8,128)} %shard_map.91.refs_1_, bf16[1,12,64,64]{3,2,1,0:T(8,128)(2,1)} %refs_2_.3, bf16[8,64,64]{2,1,0:T(8,128)(2,1)} %refs_3_.3, bf16[8,64,128]{2,1,0:T(8,128)(2,1)} %refs_4_.3, bf16[4,384,128]{2,1,0:T(8,128)(2,1)} %copy-done, ...), custom_call_target="tpu_custom_call" | custom-call | flops 133120 | bytes 671744 | tf_op jit(solution)/shard_map/pallas_call | solution.py:291
Async XLA Ops:
  49.6 15.6 %all-to-all-start.2 = ((bf16[4,384,128]{2,1,0:T(8,128)(2,1)}), bf16[4,384,128]{2,1,0:T(8,128)(2,1)S(1)}, u32[]{:S(2)}, u32[]{:S(2)}) async-start(bf16[4,384,128]{2,1,0:T(8,128)(2,1)} %get-tuple-element.11), calls=%async_computation.2 | async-start | bytes 786432 | tf_op jit(solution)/shard_map/all_to_all | solution.py:317
  65.2 0.7 %copy-start = (bf16[4,384,128]{2,1,0:T(8,128)(2,1)}, bf16[4,384,128]{2,1,0:T(8,128)(2,1)S(1)}, u32[]{:S(2)}) copy-start(bf16[4,384,128]{2,1,0:T(8,128)(2,1)S(1)} %all-to-all-done.2.refs_5_) | copy-start | bytes 1179652

commit v7 on v6

--- a/solution.py
+++ b/solution.py
@@ -62,7 +62,7 @@
 
 def routes_of(devices, main, columns, leaves):
     high, low = grid_of(devices)
-    split = main // 4 * 3
+    split = up(main // 2)
     return (
         Route(0, split, high, False, main, columns, leaves, low),
         Route(split, main, low, True, main, columns, leaves, high),
@@ -71,12 +71,14 @@
 
 def products_kernel(routes, devices, *refs):
     dest_hbm, leaf_hbm, probes_hbm, basis_hbm, transfer_hbm, blocks_hbm = refs[:6]
+    outs = refs[6:-13]
     (
-        outs_low, outs_high, dest_ref, leaf_ref, probes_ref, basis_ref, transfer_ref, blocks_ref,
+        dest_ref, leaf_ref, probes_ref, basis_ref, transfer_ref, blocks_ref,
         send_low, send_high, tails, meta_low, meta_high, count, sems,
-    ) = refs[6:]
+    ) = refs[-13:]
     by_low, by_high = routes
     high, low = grid_of(devices)
+    me = lax.axis_index("leaf")
     main = by_high.main
     leaves, per_leaf, size = blocks_ref.shape[:3]
     columns, rank = probes_ref.shape[0], basis_ref.shape[1]
@@ -121,7 +123,7 @@
             rhs = blocks_ref[j, first : first + many].reshape(many * size, size)
             product = dot_t(x, rhs)
             for b in range(many):
-                target = dest_ref[first + b, j]
+                target = jnp.bitwise_xor(dest_ref[first + b, j], me)
                 slot = count[target]
                 count[target] = slot + 1
                 to_high, to_low = target // low, target % low
@@ -147,78 +149,67 @@
         send_high[i, by_high.tails : by_high.meta, :] = tails[i].astype(BF16)
         send_high[i, by_high.meta : by_high.box, :] = meta_high[i].astype(BF16)
         send_high[i, by_high.box :, :] = packed
-    for copy in [copies.start(send_low, outs_low), copies.start(send_high, outs_high)]:
-        copy.wait()
-
-
-def sum_kernel(routes, devices, *refs):
-    came_low, came_high, outs_high, outs_low = refs[:4]
-    in_low, in_high, meta, leaf_ref, total_low, total_high, total_tails, send_high, send_low, sems, late = refs[4:]
-    by_low, by_high = routes
-    high, low = grid_of(devices)
-    leaves = by_low.leaves
+    leaving = [copies.start(send_low.at[i], outs[i]) for i in range(low)]
+    leaving += [copies.start(send_high.at[i], outs[low + i]) for i in range(high)]
+    for copy in leaving:
+        copy.wait()
+
+
+def sum_kernel(route, ways, *refs):
+    came, outs = refs[:ways], refs[ways : ways + route.fan]
+    in_ref, meta, leaf_ref, total, tails, send_ref, sems, late = refs[ways + route.fan :]
+    leaves, half = route.leaves, route.half
     copies = Copies(sems)
-    arrivals = [
-        [
-            copies.start(came.at[i, pl.ds(route.meta, TILE)], ref.at[i, pl.ds(route.meta, TILE)])
+    small = [
+        copies.start(came[i].at[pl.ds(route.meta, TILE)], in_ref.at[i, pl.ds(route.meta, TILE)])
+        for i in range(ways)
+    ]
+    large = [
+        copies.start(came[i].at[pl.ds(0, route.meta)], in_ref.at[i, pl.ds(0, route.meta)]) for i in range(ways)
+    ]
+    if route.extra:
+        large += [
+            copies.start(came[i].at[pl.ds(route.box, half)], in_ref.at[i, pl.ds(route.box, half)])
             for i in range(ways)
         ]
-        for came, ref, route, ways in ((came_low, in_low, by_low, low), (came_high, in_high, by_high, high))
-    ]
-    large = [
-        copies.start(came_low.at[:, pl.ds(0, by_low.meta)], in_low.at[:, pl.ds(0, by_low.meta)]),
-        copies.start(came_high.at[:, pl.ds(0, by_high.meta)], in_high.at[:, pl.ds(0, by_high.meta)]),
-        copies.start(
-            came_high.at[:, pl.ds(by_high.box, by_high.half)], in_high.at[:, pl.ds(by_high.box, by_high.half)]
-        ),
-    ]
-    at = 0
-    for ref, route, group in ((in_low, by_low, arrivals[0]), (in_high, by_high, arrivals[1])):
-        for i, copy in enumerate(group):
-            copy.wait()
-            tile = ref[i, route.meta : route.box, :].astype(F32)
-            meta[at : at + 1, :] = tile[:1].astype(I32)
-            at += 1
+    lasts = []
+    for i in range(ways):
+        small[i].wait()
+        tile = in_ref[i, route.meta : route.box, :].astype(F32)
+        meta[i : i + 1, :] = tile[:1].astype(I32)
+        lasts.append(tile[1:2])
     numbers = pltpu.make_async_copy(meta, leaf_ref, late)
     numbers.start()
-    total_low[...] = jnp.zeros(total_low.shape, F32)
-    total_high[...] = jnp.zeros(total_high.shape, F32)
-    total_tails[...] = jnp.zeros(total_tails.shape, F32)
+    total[...] = jnp.zeros(total.shape, F32)
+    tails[...] = jnp.zeros(tails.shape, F32)
     numbers.wait()
     for copy in large:
         copy.wait()
 
-    @pl.loop(0, low)
+    @pl.loop(0, ways)
     def _(i):
-        for k in range(high):
+        if route.extra:
+            tail = in_ref[i, route.tails : route.meta, :].astype(F32)
+        for k in range(route.fan):
             for slot in range(CAP):
                 at = k * CAP + slot
                 leaf = leaf_ref[i, at]
-                rows = pl.ds(pl.multiple_of(leaf * by_low.rows, TILE), by_low.rows)
-                total_low[k, rows, :] += in_low[i, at * by_low.rows : (at + 1) * by_low.rows, :].astype(F32)
-
-    @pl.loop(0, high)
-    def _(i):
-        tail = in_high[i, by_high.tails : by_high.meta, :].astype(F32)
-        for k in range(low):
-            for slot in range(CAP):
-                at = k * CAP + slot
-                leaf = leaf_ref[low + i, at]
-                rows = pl.ds(pl.multiple_of(leaf * by_high.rows, TILE), by_high.rows)
-                total_high[k, rows, :] += in_high[i, at * by_high.rows : (at + 1) * by_high.rows, :].astype(F32)
-                total_tails[k, pl.ds(leaf, 1), :] += tail[at : at + 1]
-
-    for k in range(high):
-        send_high[k] = total_low[k, : by_low.dense_tails, :].astype(BF16)
-    lasts = [in_high[i, by_high.meta : by_high.box, :].astype(F32)[1:2] for i in range(high)]
-    for k in range(low):
-        send_low[k, : by_high.dense_tails, :] = total_high[k, : by_high.dense_tails, :].astype(BF16)
-        for i in range(high):
-            total_tails[k, leaves + i : leaves + i + 1, :] = lasts[i]
-            start = by_high.dense_box + i * by_high.half
-            send_low[k, start : start + by_high.half, :] = in_high[i, by_high.box :, :]
-        send_low[k, by_high.dense_tails : by_high.dense_box, :] = total_tails[k].astype(BF16)
-    for copy in [copies.start(send_high, outs_high), copies.start(send_low, outs_low)]:
+                rows = pl.ds(pl.multiple_of(leaf * route.rows, TILE), route.rows)
+                total[k, rows, :] += in_ref[i, at * route.rows : (at + 1) * route.rows, :].astype(F32)
+                if route.extra:
+                    tails[k, pl.ds(leaf, 1), :] += tail[at : at + 1]
+
+    leaving = []
+    for k in range(route.fan):
+        send_ref[k, : route.dense_tails, :] = total[k, : route.dense_tails, :].astype(BF16)
+        if route.extra:
+            for i in range(ways):
+                tails[k, leaves + i : leaves + i + 1, :] = lasts[i]
+                start = route.dense_box + i * half
+                send_ref[k, start : start + half, :] = in_ref[i, route.box :, :]
+            send_ref[k, route.dense_tails : route.dense_box, :] = tails[k].astype(BF16)
+        leaving.append(copies.start(send_ref.at[k], outs[k]))
+    for copy in leaving:
         copy.wait()
 
 
@@ -239,29 +230,32 @@
 
 
 def last_kernel(routes, devices, *refs):
-    (
-        partner_hbm, base_hbm, couplings_hbm, transfer_hbm, basis_hbm, came_high, came_low,
-        out_ref, partner_ref, base_ref, couplings_ref, transfer_ref, basis_ref, in_high, in_low, sems,
-    ) = refs
+    partner_hbm, base_hbm, couplings_hbm, transfer_hbm, basis_hbm = refs[:5]
     by_low, by_high = routes
     high, low = grid_of(devices)
+    came_high, came_low = refs[5 : 5 + high], refs[5 + high : 5 + high + low]
+    (
+        out_ref, partner_ref, base_ref, couplings_ref, transfer_ref, basis_ref, in_high, in_low, sems,
+    ) = refs[5 + high + low :]
+    me = lax.axis_index("leaf")
     columns = out_ref.shape[0]
     leaves, rank, size = basis_ref.shape
     split, main = by_low.rows, by_low.main
     copies = Copies(sems)
-    early = [
-        copies.start(came_low, in_low),
+    early = [copies.start(came_low[k], in_low.at[k]) for k in range(low)]
+    early += [
         copies.start(partner_hbm, partner_ref),
         copies.start(couplings_hbm, couplings_ref),
         copies.start(transfer_hbm, transfer_ref),
         copies.start(basis_hbm, basis_ref),
     ]
-    later = [copies.start(came_high, in_high), copies.start(base_hbm, base_ref)]
+    later = [copies.start(came_high[k], in_high.at[k]) for k in range(high)]
+    later += [copies.start(base_hbm, base_ref)]
     for copy in early:
         copy.wait()
     far = jnp.zeros((columns, rank), F32)
     for f in range(couplings_ref.shape[1]):
-        source = partner_ref[0, f]
+        source = jnp.bitwise_xor(partner_ref[0, f], me)
         to_high, to_low = source // low, source % low
         start = pl.multiple_of(by_high.dense_box + to_high * by_high.half, TILE)
         packed = in_low[to_low, pl.ds(start, by_high.half), :]
@@ -312,77 +306,89 @@
     like = lambda *arrays: [pltpu.VMEM(a.shape, a.dtype) for a in arrays]
     numbers = lambda *arrays: [pltpu.SMEM(a.shape, a.dtype) for a in arrays]
     sems = lambda count: [pltpu.SemaphoreType.DMA((count,))]
-    same_high = [[h * low + l for l in range(low)] for h in range(high)]
-    same_low = [[h * low + l for h in range(high)] for l in range(low)]
-    exchange = lambda x, groups: lax.all_to_all(
-        x, "leaf", split_axis=0, concat_axis=0, tiled=True, axis_index_groups=groups
-    )
-
-    to_low = jax.ShapeDtypeStruct((low, by_low.depth, size), BF16)
-    to_high = jax.ShapeDtypeStruct((high, by_high.depth, size), BF16)
+    relative = lambda x, way: lax.ppermute(x, "leaf", [(i, i ^ way) for i in range(devices)])
+    message = lambda route: jax.ShapeDtypeStruct((route.depth, size), BF16)
+    dense = lambda route: jax.ShapeDtypeStruct((route.dense_depth, size), BF16)
+
+    def stacked(count, like_this):
+        return pltpu.VMEM((count, *like_this.shape), like_this.dtype)
+
+    def summed(route, ways, came):
+        return call(
+            functools.partial(sum_kernel, route, ways),
+            [dense(route)] * route.fan,
+            [ANY] * route.fan,
+            came,
+            [
+                stacked(ways, message(route)),
+                pltpu.VMEM((ways, size), I32),
+                pltpu.SMEM((ways, size), I32),
+                pltpu.VMEM((route.fan, (leaves + 1) * route.rows, size), F32),
+                pltpu.VMEM((route.fan, max(TILE, route.dense_box - route.dense_tails), size), F32),
+                stacked(route.fan, dense(route)),
+            ]
+            + sems(3 * ways + route.fan)
+            + [pltpu.SemaphoreType.DMA(())],
+            devices * CAP * route.rows * size,
+            2 * ways * message(route).size,
+        )
+
     dest, leaf = near_dest.T, near_leaf.T
-    send_low, send_high = call(
+    sent = call(
         functools.partial(products_kernel, routes, devices),
-        [to_low, to_high],
-        [ANY, ANY],
+        [message(by_low)] * low + [message(by_high)] * high,
+        [ANY] * (low + high),
         (dest, leaf, probes, basis, transfer, remote_blocks),
         numbers(dest, leaf)
-        + like(probes, basis, transfer, remote_blocks, to_low, to_high)
+        + like(probes, basis, transfer, remote_blocks)
         + [
+            stacked(low, message(by_low)),
+            stacked(high, message(by_high)),
             pltpu.VMEM((high, by_high.meta - by_high.tails, size), F32),
             pltpu.VMEM((low, TILE, size), F32),
             pltpu.VMEM((high, TILE, size), F32),
             pltpu.SMEM((devices,), I32),
         ]
-        + sems(9),
+        + sems(7 + low + high),
         blocks * unit,
-        remote_blocks.size * 2 + to_low.size * 2 + to_high.size * 2,
-    )
-    came_low = exchange(send_low, same_high)
-    came_high = exchange(send_high, same_low)
+        remote_blocks.size * 2 + 2 * low * message(by_low).size + 2 * high * message(by_high).size,
+    )
+    came_low, came_high = list(sent[:low]), list(sent[low:])
+    came_low[1] = relative(came_low[1], 1)
+    for k in range(high - 1, 1, -1):
+        came_high[k] = relative(came_high[k], k * low)
+    for k in range(low - 1, 1, -1):
+        came_low[k] = relative(came_low[k], k)
+    came_high[1] = relative(came_high[1], low)
+
+    to_high = list(summed(by_low, low, came_low))
+    for k in range(high - 1, 0, -1):
+        to_high[k] = relative(to_high[k], k * low)
+    to_low = list(summed(by_high, high, came_high))
+    probes_then, to_low[0] = lax.optimization_barrier((probes, to_low[0]))
+    for k in range(low - 1, 0, -1):
+        to_low[k] = relative(to_low[k], k)
 
     base = call(
         local_kernel,
         jax.ShapeDtypeStruct((columns, points), F32),
         VMEM,
-        (probes, local_blocks),
+        (probes_then, local_blocks),
         like(probes, local_blocks) + sems(2),
         leaves * leaves * unit,
         local_blocks.size * 2,
     )
-
-    dense_high = jax.ShapeDtypeStruct((high, by_low.dense_depth, size), BF16)
-    dense_low = jax.ShapeDtypeStruct((low, by_high.dense_depth, size), BF16)
-    send_high, send_low = call(
-        functools.partial(sum_kernel, routes, devices),
-        [dense_high, dense_low],
-        [ANY, ANY],
-        (came_low, came_high),
-        like(came_low, came_high)
-        + [
-            pltpu.VMEM((low + high, size), I32),
-            pltpu.SMEM((low + high, size), I32),
-            pltpu.VMEM((high, (leaves + 1) * by_low.rows, size), F32),
-            pltpu.VMEM((low, (leaves + 1) * by_high.rows, size), F32),
-            pltpu.VMEM((low, by_high.dense_box - by_high.dense_tails, size), F32),
-        ]
-        + like(dense_high, dense_low)
-        + sems(5 + low + high)
-        + [pltpu.SemaphoreType.DMA(())],
-        devices * CAP * columns * size,
-        4 * (to_low.size + to_high.size),
-    )
-    came_high = exchange(send_high, same_low)
-    came_low = exchange(send_low, same_high)
-
     return call(
         functools.partial(last_kernel, routes, devices),
         jax.ShapeDtypeStruct((columns, points), F32),
         VMEM,
-        (far_list, base, couplings, transfer, basis, came_high, came_low),
-        numbers(far_list) + like(base, couplings, transfer, basis, came_high, came_low) + sems(7),
+        (far_list, base, couplings, transfer, basis, *to_high, *to_low),
+        numbers(far_list)
+        + like(base, couplings, transfer, basis)
+        + [stacked(high, dense(by_low)), stacked(low, dense(by_high))]
+        + sems(5 + low + high),
         devices * columns * size,
-        2 * (dense_high.size + dense_low.size),
+        2 * (high * dense(by_low).size + low * dense(by_high).size),
     )
 
 

time: 69.3 us -> 42 us (0.61)
  blocking collectives: 43.2 us -> 0 us
  starting transfers between devices: 3.46 us -> 16.4 us
  Pallas kernels: 13.2 us -> 15.4 us
  local copies, waits for them, and re-layouts: 0.75 us -> 2.12 us
    all_to_all x3 -> x0, blocking collectives: 43.2 us -> none  [per_device(): lax.all_to_all(x, 'leaf', split_axis=0, concat_axis=0, tiled=True, axis_i...]
    ppermute x0 -> x12, starting transfers between devices: none -> 16.4 us  [per_device(): lax.ppermute(x, 'leaf', [(i, i ^ way) for i in range(devices)])]
    all_to_all x1 -> x0, waiting for transfers between devices: 8.18 us -> none  [per_device(): lax.all_to_all(x, 'leaf', split_axis=0, concat_axis=0, tiled=True, axis_i...]
    ppermute x0 -> x12, waiting for transfers between devices: none -> 7.77 us  [per_device(): lax.ppermute(x, 'leaf', [(i, i ^ way) for i in range(devices)])]
    all_to_all x1 -> x0, starting transfers between devices: 3.46 us -> none  [per_device(): lax.all_to_all(x, 'leaf', split_axis=0, concat_axis=0, tiled=True, axis_i...]
    pallas_call x4 -> x5, Pallas kernels: 13.2 us -> 15.4 us  [call(): pl.pallas_call(kernel, out_shape=out_shape, in_specs=[ANY] * len(operands...]
    unnamed x2 -> x24, local copies, waits for them, and re-layouts: 0.75 us -> 2.12 us
  transfers between devices with their start and end apart: 1 -> 12, of which waited for: 1 -> 4; matrix products, arithmetic and copies ran while one was open for 0% -> 0% of each run, Pallas kernels for 6% -> 22%
where the time goes in v7:
time: 42 us; the launch traced here: 41.8 us
  starting transfers between devices  16.4 us (39%)
  Pallas kernels  15.4 us (37%)
  waiting for transfers between devices  7.77 us (18%)
  local copies, waits for them, and re-layouts  2.12 us (5%)
    ppermute x12, starting transfers between devices, per_device(): lax.ppermute(x, 'leaf', [(i, i ^ way) for i in range(devices)])  16.4 us
    pallas_call x5, Pallas kernels, call(): pl.pallas_call(kernel, out_shape=out_shape, in_specs=[ANY] * len(operands...  15.4 us
    ppermute x12, waiting for transfers between devices, per_device(): lax.ppermute(x, 'leaf', [(i, i ^ way) for i in range(devices)])  7.77 us
    unnamed x24, local copies, waits for them, and re-layouts  2.12 us
  transfers between devices with their start and end apart: 12, of which 4 were waited for; matrix products, arithmetic and copies ran while one was open for 0% of the time, Pallas kernels for 22%

profile of v7, /device:TPU:0, one launch (start us, length us, event | category | flops | bytes accessed | tf_op | source)
XLA Modules:
  0.0 41.8 jit_solution(12325762566160822854)
XLA Ops:
  0.0 3.4 %shard_map.91 = (bf16[528,128]{1,0:T(8,128)(2,1)}, bf16[528,128]{1,0:T(8,128)(2,1)}, bf16[528,128]{1,0:T(8,128)(2,1)}, bf16[528,128]{1,0:T(8,128)(2,1)}, bf16[57...) custom-call(s32[4,8]{1,0:T(4,128)} %bitcast.2, ...), custom_call_target="tpu_custom_call" | custom-call | flops 68157440 | bytes 2179072 | tf_op jit(solution)/shard_map/pallas_call | solution.py:285
  3.4 0.5 %collective-permute-start.3 = (bf16[528,128]{1,0:T(8,128)(2,1)}, bf16[528,128]{1,0:T(8,128)(2,1)S(1)}, u32[]{:S(2)}, u32[]{:S(2)}) collective-permute-start(bf16[528,128]{1,0:T(8,128)(2,1)} %get-tuple-element.30), channel_id=1, source_target_pairs={{0,1},{1,0},{2,3},{3,2},{4,5},{5,4},{6,7},{7,6},{8,9},{9,8},{10,11... | collective-permute-start | bytes 405512 | tf_op jit(solution)/shard_map/ppermute | solution.py:309
  3.9 2.6 %collective-permute-start.4 = (bf16[528,128]{1,0:T(8,128)(2,1)}, bf16[528,128]{1,0:T(8,128)(2,1)S(1)}, u32[]{:S(2)}, u32[]{:S(2)}) collective-permute-start(bf16[528,128]{1,0:T(8,128)(2,1)} %get-tuple-element.31), channel_id=1, source_target_pairs={{0,2},{1,3},{2,0},{3,1},{4,6},{5,7},{6,4},{7,5},{8,10},{9,11},{10,... | collective-permute-start | bytes 405512 | tf_op jit(solution)/shard_map/ppermute | solution.py:309
  6.5 0.1 collective-permute-start.5
  6.6 1.8 %collective-permute-start = (bf16[576,128]{1,0:T(8,128)(2,1)}, bf16[576,128]{1,0:T(8,128)(2,1)S(1)}, u32[]{:S(2)}, u32[]{:S(2)}) collective-permute-start(bf16[576,128]{1,0:T(8,128)(2,1)} %get-tuple-element.24), channel_id=1, source_target_pairs={{0,4},{1,5},{2,6},{3,7},{4,0},{5,1},{6,2},{7,3},{8,12},{9,13},{10,... | collective-permute-start | bytes 442376 | tf_op jit(solution)/shard_map/ppermute | solution.py:309
  8.4 2.6 %collective-permute-start.1 = (bf16[576,128]{1,0:T(8,128)(2,1)}, bf16[576,128]{1,0:T(8,128)(2,1)S(1)}, u32[]{:S(2)}, u32[]{:S(2)}) collective-permute-start(bf16[576,128]{1,0:T(8,128)(2,1)} %get-tuple-element.25), channel_id=1, source_target_pairs={{0,8},{1,9},{2,10},{3,11},{4,12},{5,13},{6,14},{7,15},{8,0},{9,1},... | collective-permute-start | bytes 442376 | tf_op jit(solution)/shard_map/ppermute | solution.py:309
  11.0 0.2 collective-permute-done.4.refs_2_
  11.1 2.4 %collective-permute-done.5.refs_3_ = bf16[528,128]{1,0:T(8,128)(2,1)S(1)} collective-permute-done((bf16[528,128]{1,0:T(8,128)(2,1)}, bf16[528,128]{1,0:T(8,128)(2,1)S(1)}, u32[]{:S(2)}, u32[]{:S(2)}) %collective-permute-start.5) | collective-permute-done | bytes 135200 | tf_op jit(solution)/shard_map/ppermute | solution.py:309
  13.5 0.7 %copy-done.5 = bf16[528,128]{1,0:T(8,128)(2,1)} copy-done((bf16[528,128]{1,0:T(8,128)(2,1)}, bf16[528,128]{1,0:T(8,128)(2,1)S(1)}, u32[]{:S(2)}) %copy-start.5) | copy-done | bytes 135192
  14.2 2.5 %shard_map.94 = (bf16[256,128]{1,0:T(8,128)(2,1)}, bf16[256,128]{1,0:T(8,128)(2,1)}, bf16[256,128]{1,0:T(8,128)(2,1)}, bf16[256,128]{1,0:T(8,128)(2,1)}) custom-call(bf16[528,128]{1,0:T(8,128)(2,1)} %get-tuple-element.29.refs_0_, bf16[528,128]{1,0:T(8,128)(2,1)} %copy-done.3, bf16[528,128]{1,0:T(8,128)(2,1)} %copy-done.4, bf16[528,128]{1,0:T(8,128)(2,1)} %copy-done.5), custom_call_target="tpu_custom_call" | custom-call | flops 262144 | bytes 540672 | tf_op jit(solution)/shard_map/pallas_call | solution.py:285
  16.7 1.7 %collective-permute-start.6 = (bf16[256,128]{1,0:T(8,128)(2,1)}, bf16[256,128]{1,0:T(8,128)(2,1)S(1)}, u32[]{:S(2)}, u32[]{:S(2)}) collective-permute-start(bf16[256,128]{1,0:T(8,128)(2,1)} %get-tuple-element.34), channel_id=1, source_target_pairs={{0,4},{1,5},{2,6},{3,7},{4,0},{5,1},{6,2},{7,3},{8,12},{9,13},{10,... | collective-permute-start | bytes 196616 | tf_op jit(solution)/shard_map/ppermute | solution.py:309
  18.3 4.2 %collective-permute-done.1.refs_2_ = bf16[576,128]{1,0:T(8,128)(2,1)S(1)} collective-permute-done((bf16[576,128]{1,0:T(8,128)(2,1)}, bf16[576,128]{1,0:T(8,128)(2,1)S(1)}, u32[]{:S(2)}, u32[]{:S(2)}) %collective-permute-start.1) | collective-permute-done | bytes 147488 | tf_op jit(solution)/shard_map/ppermute | solution.py:309
  22.6 0.7 %copy-done.1 = bf16[576,128]{1,0:T(8,128)(2,1)} copy-done((bf16[576,128]{1,0:T(8,128)(2,1)}, bf16[576,128]{1,0:T(8,128)(2,1)S(1)}, u32[]{:S(2)}) %copy-start.1) | copy-done | bytes 147480
  23.3 2.6 %shard_map.92 = (bf16[400,128]{1,0:T(8,128)(2,1)}, bf16[400,128]{1,0:T(8,128)(2,1)}, bf16[400,128]{1,0:T(8,128)(2,1)}, bf16[400,128]{1,0:T(8,128)(2,1)}) custom-call(bf16[576,128]{1,0:T(8,128)(2,1)} %get-tuple-element.23.refs_0_, bf16[576,128]{1,0:T(8,128)(2,1)} %copy-done, bf16[576,128]{1,0:T(8,128)(2,1)} %copy-done.1, bf16[576,128]{1,0:T(8,128)(2,1)} %copy-done.2), custom_call_target="tpu_custom_call" | custom-call | flops 262144 | bytes 589824 | tf_op jit(solution)/shard_map/pallas_call | solution.py:285
  25.9 0.1 collective-permute-start.9
  26.0 1.6 %collective-permute-start.10 = (bf16[400,128]{1,0:T(8,128)(2,1)}, bf16[400,128]{1,0:T(8,128)(2,1)S(1)}, u32[]{:S(2)}, u32[]{:S(2)}) collective-permute-start(bf16[400,128]{1,0:T(8,128)(2,1)} %get-tuple-element.39), channel_id=1, source_target_pairs={{0,2},{1,3},{2,0},{3,1},{4,6},{5,7},{6,4},{7,5},{8,10},{9,11},{10,... | collective-permute-start | bytes 307208 | tf_op jit(solution)/shard_map/ppermute | solution.py:309
  27.6 0.3 collective-permute-start.11
  27.8 3.8 %collective-permute-start.7 = (bf16[256,128]{1,0:T(8,128)(2,1)}, bf16[256,128]{1,0:T(8,128)(2,1)S(1)}, u32[]{:S(2)}, u32[]{:S(2)}) collective-permute-start(bf16[256,128]{1,0:T(8,128)(2,1)} %get-tuple-element.35), channel_id=1, source_target_pairs={{0,8},{1,9},{2,10},{3,11},{4,12},{5,13},{6,14},{7,15},{8,0},{9,1},... | collective-permute-start | bytes 196616 | tf_op jit(solution)/shard_map/ppermute | solution.py:309
  31.7 1.4 %collective-permute-start.8 = (bf16[256,128]{1,0:T(8,128)(2,1)}, bf16[256,128]{1,0:T(8,128)(2,1)S(1)}, u32[]{:S(2)}, u32[]{:S(2)}) collective-permute-start(bf16[256,128]{1,0:T(8,128)(2,1)} %get-tuple-element.36), channel_id=1, source_target_pairs={{0,12},{1,13},{2,14},{3,15},{4,8},{5,9},{6,10},{7,11},{8,4},{9,5},... | collective-permute-start | bytes 196616 | tf_op jit(solution)/shard_map/ppermute | solution.py:309
  33.0 3.9 %shard_map.93.refs_1_ = f32[65,1024]{1,0:T(8,128)} custom-call(bf16[65,1024]{1,0:T(8,128)(2,1)} %probes_hbm, bf16[8,8,128,128]{3,2,1,0:T(8,128)(2,1)} %local_hbm.1), custom_call_target="tpu_custom_call" | custom-call | flops 136314880 | bytes 2097152 | tf_op jit(solution)/shard_map/pallas_call | solution.py:285
  37.0 1.0 %collective-permute-done.8.refs_8_ = bf16[256,128]{1,0:T(8,128)(2,1)S(1)} collective-permute-done((bf16[256,128]{1,0:T(8,128)(2,1)}, bf16[256,128]{1,0:T(8,128)(2,1)S(1)}, u32[]{:S(2)}, u32[]{:S(2)}) %collective-permute-start.8) | collective-permute-done | bytes 65568 | tf_op jit(solution)/shard_map/ppermute | solution.py:309
  38.0 0.6 %copy-done.11 = bf16[256,128]{1,0:T(8,128)(2,1)} copy-done((bf16[256,128]{1,0:T(8,128)(2,1)}, bf16[256,128]{1,0:T(8,128)(2,1)S(1)}, u32[]{:S(2)}) %copy-start.11) | copy-done | bytes 65560
  38.7 0.1 copy-done.8
  38.8 3.0 %shard_map.95 = f32[65,1024]{1,0:T(8,128)} custom-call(s32[1,12]{1,0:T(1,128)} %refs_0_.1, f32[65,1024]{1,0:T(8,128)} %shard_map.93.refs_1_, bf16[1,12,64,64]{3,2,1,0:T(8,128)(2,1)} %refs_2_.3, bf16[8,64,64]{2,1,0:T(8,128)(2,1)} %refs_3_.3, bf16[8,64,128]{2,1,0:T(8,128)(2,1)} %refs_4_.3, bf16[256,128]{1,0:T(8,128)(2,1)} %get-tuple-element.33.refs_5_, ...), custom_call_target="tpu_custom_call" | custom-call | flops 133120 | bytes 671744 | tf_op jit(solution)/shard_map/pallas_call | solution.py:285
  (29 shorter events, 0.2 us)
Async XLA Ops:
  3.4 7.6 %collective-permute-start.3 = (bf16[528,128]{1,0:T(8,128)(2,1)}, bf16[528,128]{1,0:T(8,128)(2,1)S(1)}, u32[]{:S(2)}, u32[]{:S(2)}) collective-permute-start(bf16[528,128]{1,0:T(8,128)(2,1)} %get-tuple-element.30), channel_id=1, source_target_pairs={{0,1},{1,0},{2,3},{3,2},{4,5},{5,4},{6,7},{7,6},{8,9},{9,8},{10,11... | collective-permute-start | bytes 405512 | tf_op jit(solution)/shard_map/ppermute | solution.py:309
  3.9 7.2 %collective-permute-start.4 = (bf16[528,128]{1,0:T(8,128)(2,1)}, bf16[528,128]{1,0:T(8,128)(2,1)S(1)}, u32[]{:S(2)}, u32[]{:S(2)}) collective-permute-start(bf16[528,128]{1,0:T(8,128)(2,1)} %get-tuple-element.31), channel_id=1, source_target_pairs={{0,2},{1,3},{2,0},{3,1},{4,6},{5,7},{6,4},{7,5},{8,10},{9,11},{10,... | collective-permute-start | bytes 405512 | tf_op jit(solution)/shard_map/ppermute | solution.py:309
  6.5 7.0 %collective-permute-start.5 = (bf16[528,128]{1,0:T(8,128)(2,1)}, bf16[528,128]{1,0:T(8,128)(2,1)S(1)}, u32[]{:S(2)}, u32[]{:S(2)}) collective-permute-start(bf16[528,128]{1,0:T(8,128)(2,1)} %get-tuple-element.32), channel_id=1, source_target_pairs={{0,3},{1,2},{2,1},{3,0},{4,7},{5,6},{6,5},{7,4},{8,11},{9,10},{10,... | collective-permute-start | bytes 405512 | tf_op jit(solution)/shard_map/ppermute | solution.py:309
  6.6 11.8 %collective-permute-start = (bf16[576,128]{1,0:T(8,128)(2,1)}, bf16[576,128]{1,0:T(8,128)(2,1)S(1)}, u32[]{:S(2)}, u32[]{:S(2)}) collective-permute-start(bf16[576,128]{1,0:T(8,128)(2,1)} %get-tuple-element.24), channel_id=1, source_target_pairs={{0,4},{1,5},{2,6},{3,7},{4,0},{5,1},{6,2},{7,3},{8,12},{9,13},{10,... | collective-permute-start | bytes 442376 | tf_op jit(solution)/shard_map/ppermute | solution.py:309
  8.4 14.2 %collective-permute-start.1 = (bf16[576,128]{1,0:T(8,128)(2,1)}, bf16[576,128]{1,0:T(8,128)(2,1)S(1)}, u32[]{:S(2)}, u32[]{:S(2)}) collective-permute-start(bf16[576,128]{1,0:T(8,128)(2,1)} %get-tuple-element.25), channel_id=1, source_target_pairs={{0,8},{1,9},{2,10},{3,11},{4,12},{5,13},{6,14},{7,15},{8,0},{9,1},... | collective-permute-start | bytes 442376 | tf_op jit(solution)/shard_map/ppermute | solution.py:309
  10.9 2.6 %copy-start.3 = (bf16[528,128]{1,0:T(8,128)(2,1)}, bf16[528,128]{1,0:T(8,128)(2,1)S(1)}, u32[]{:S(2)}) copy-start(bf16[528,128]{1,0:T(8,128)(2,1)S(1)} %collective-permute-done.3.refs_1_) | copy-start | bytes 405508
  10.9 11.6 %collective-permute-start.2 = (bf16[576,128]{1,0:T(8,128)(2,1)}, bf16[576,128]{1,0:T(8,128)(2,1)S(1)}, u32[]{:S(2)}, u32[]{:S(2)}) collective-permute-start(bf16[576,128]{1,0:T(8,128)(2,1)} %get-tuple-element.26), channel_id=1, source_target_pairs={{0,12},{1,13},{2,14},{3,15},{4,8},{5,9},{6,10},{7,11},{8,4},{9,5},... | collective-permute-start | bytes 442376 | tf_op jit(solution)/shard_map/ppermute | solution.py:309
  11.1 2.4 %copy-start.4 = (bf16[528,128]{1,0:T(8,128)(2,1)}, bf16[528,128]{1,0:T(8,128)(2,1)S(1)}, u32[]{:S(2)}) copy-start(bf16[528,128]{1,0:T(8,128)(2,1)S(1)} %collective-permute-done.4.refs_2_) | copy-start | bytes 405508
  13.5 0.7 %copy-start.5 = (bf16[528,128]{1,0:T(8,128)(2,1)}, bf16[528,128]{1,0:T(8,128)(2,1)S(1)}, u32[]{:S(2)}) copy-start(bf16[528,128]{1,0:T(8,128)(2,1)S(1)} %collective-permute-done.5.refs_3_) | copy-start | bytes 405508
  16.7 15.0 %collective-permute-start.6 = (bf16[256,128]{1,0:T(8,128)(2,1)}, bf16[256,128]{1,0:T(8,128)(2,1)S(1)}, u32[]{:S(2)}, u32[]{:S(2)}) collective-permute-start(bf16[256,128]{1,0:T(8,128)(2,1)} %get-tuple-element.34), channel_id=1, source_target_pairs={{0,4},{1,5},{2,6},{3,7},{4,0},{5,1},{6,2},{7,3},{8,12},{9,13},{10,... | collective-permute-start | bytes 196616 | tf_op jit(solution)/shard_map/ppermute | solution.py:309
  18.3 4.2 %copy-start = (bf16[576,128]{1,0:T(8,128)(2,1)}, bf16[576,128]{1,0:T(8,128)(2,1)S(1)}, u32[]{:S(2)}) copy-start(bf16[576,128]{1,0:T(8,128)(2,1)S(1)} %collective-permute-done.refs_1_) | copy-start | bytes 442372
  22.5 0.7 %copy-start.1 = (bf16[576,128]{1,0:T(8,128)(2,1)}, bf16[576,128]{1,0:T(8,128)(2,1)S(1)}, u32[]{:S(2)}) copy-start(bf16[576,128]{1,0:T(8,128)(2,1)S(1)} %collective-permute-done.1.refs_2_) | copy-start | bytes 442372
  22.5 0.7 %copy-start.2 = (bf16[576,128]{1,0:T(8,128)(2,1)}, bf16[576,128]{1,0:T(8,128)(2,1)S(1)}, u32[]{:S(2)}) copy-start(bf16[576,128]{1,0:T(8,128)(2,1)S(1)} %collective-permute-done.2.refs_3_) | copy-start | bytes 442372
  25.9 12.1 %collective-permute-start.9 = (bf16[400,128]{1,0:T(8,128)(2,1)}, bf16[400,128]{1,0:T(8,128)(2,1)S(1)}, u32[]{:S(2)}, u32[]{:S(2)}) collective-permute-start(bf16[400,128]{1,0:T(8,128)(2,1)} %get-tuple-element.38), channel_id=1, source_target_pairs={{0,1},{1,0},{2,3},{3,2},{4,5},{5,4},{6,7},{7,6},{8,9},{9,8},{10,11... | collective-permute-start | bytes 307208 | tf_op jit(solution)/shard_map/ppermute | solution.py:309
  26.0 12.0 %collective-permute-start.10 = (bf16[400,128]{1,0:T(8,128)(2,1)}, bf16[400,128]{1,0:T(8,128)(2,1)S(1)}, u32[]{:S(2)}, u32[]{:S(2)}) collective-permute-start(bf16[400,128]{1,0:T(8,128)(2,1)} %get-tuple-element.39), channel_id=1, source_target_pairs={{0,2},{1,3},{2,0},{3,1},{4,6},{5,7},{6,4},{7,5},{8,10},{9,11},{10,... | collective-permute-start | bytes 307208 | tf_op jit(solution)/shard_map/ppermute | solution.py:309
  27.6 10.4 %collective-permute-start.11 = (bf16[400,128]{1,0:T(8,128)(2,1)}, bf16[400,128]{1,0:T(8,128)(2,1)S(1)}, u32[]{:S(2)}, u32[]{:S(2)}) collective-permute-start(bf16[400,128]{1,0:T(8,128)(2,1)} %get-tuple-element.40), channel_id=1, source_target_pairs={{0,3},{1,2},{2,1},{3,0},{4,7},{5,6},{6,5},{7,4},{8,11},{9,10},{10,... | collective-permute-start | bytes 307208 | tf_op jit(solution)/shard_map/ppermute | solution.py:309
  27.8 9.2 %collective-permute-start.7 = (bf16[256,128]{1,0:T(8,128)(2,1)}, bf16[256,128]{1,0:T(8,128)(2,1)S(1)}, u32[]{:S(2)}, u32[]{:S(2)}) collective-permute-start(bf16[256,128]{1,0:T(8,128)(2,1)} %get-tuple-element.35), channel_id=1, source_target_pairs={{0,8},{1,9},{2,10},{3,11},{4,12},{5,13},{6,14},{7,15},{8,0},{9,1},... | collective-permute-start | bytes 196616 | tf_op jit(solution)/shard_map/ppermute | solution.py:309
  31.7 6.4 %copy-start.9 = (bf16[256,128]{1,0:T(8,128)(2,1)}, bf16[256,128]{1,0:T(8,128)(2,1)S(1)}, u32[]{:S(2)}) copy-start(bf16[256,128]{1,0:T(8,128)(2,1)S(1)} %collective-permute-done.6.refs_6_) | copy-start | bytes 196612
  31.7 6.3 %collective-permute-start.8 = (bf16[256,128]{1,0:T(8,128)(2,1)}, bf16[256,128]{1,0:T(8,128)(2,1)S(1)}, u32[]{:S(2)}, u32[]{:S(2)}) collective-permute-start(bf16[256,128]{1,0:T(8,128)(2,1)} %get-tuple-element.36), channel_id=1, source_target_pairs={{0,12},{1,13},{2,14},{3,15},{4,8},{5,9},{6,10},{7,11},{8,4},{9,5},... | collective-permute-start | bytes 196616 | tf_op jit(solution)/shard_map/ppermute | solution.py:309
  37.0 1.1 %copy-start.10 = (bf16[256,128]{1,0:T(8,128)(2,1)}, bf16[256,128]{1,0:T(8,128)(2,1)S(1)}, u32[]{:S(2)}) copy-start(bf16[256,128]{1,0:T(8,128)(2,1)S(1)} %collective-permute-done.7.refs_7_) | copy-start | bytes 196612
  38.0 0.6 %copy-start.11 = (bf16[256,128]{1,0:T(8,128)(2,1)}, bf16[256,128]{1,0:T(8,128)(2,1)S(1)}, u32[]{:S(2)}) copy-start(bf16[256,128]{1,0:T(8,128)(2,1)S(1)} %collective-permute-done.8.refs_8_) | copy-start | bytes 196612
  38.0 0.7 %copy-start.6 = (bf16[400,128]{1,0:T(8,128)(2,1)}, bf16[400,128]{1,0:T(8,128)(2,1)S(1)}, u32[]{:S(2)}) copy-start(bf16[400,128]{1,0:T(8,128)(2,1)S(1)} %collective-permute-done.9.refs_10_) | copy-start | bytes 307204
  38.0 0.7 %copy-start.7 = (bf16[400,128]{1,0:T(8,128)(2,1)}, bf16[400,128]{1,0:T(8,128)(2,1)S(1)}, u32[]{:S(2)}) copy-start(bf16[400,128]{1,0:T(8,128)(2,1)S(1)} %collective-permute-done.10.refs_11_) | copy-start | bytes 307204
  38.0 0.8 %copy-start.8 = (bf16[400,128]{1,0:T(8,128)(2,1)}, bf16[400,128]{1,0:T(8,128)(2,1)S(1)}, u32[]{:S(2)}) copy-start(bf16[400,128]{1,0:T(8,128)(2,1)S(1)} %collective-permute-done.11.refs_12_) | copy-start | bytes 307204

commit v8 on v7

--- a/solution.py
+++ b/solution.py
@@ -16,6 +16,7 @@
 
 ANY = pl.BlockSpec(memory_space=pl.ANY)
 VMEM = pl.BlockSpec(memory_space=pltpu.VMEM)
+SMEM = pl.BlockSpec(memory_space=pltpu.SMEM)
 
 
 def dot_t(lhs, rhs):
@@ -62,7 +63,7 @@
 
 def routes_of(devices, main, columns, leaves):
     high, low = grid_of(devices)
-    split = up(main // 2)
+    split = up(main * 3 // 4)
     return (
         Route(0, split, high, False, main, columns, leaves, low),
         Route(split, main, low, True, main, columns, leaves, high),
@@ -157,25 +158,11 @@
 
 def sum_kernel(route, ways, *refs):
     came, outs = refs[:ways], refs[ways : ways + route.fan]
-    in_ref, meta, leaf_ref, total, tails, send_ref, sems, late = refs[ways + route.fan :]
+    meta, leaf_ref, total, tails, late = refs[ways + route.fan :]
     leaves, half = route.leaves, route.half
-    copies = Copies(sems)
-    small = [
-        copies.start(came[i].at[pl.ds(route.meta, TILE)], in_ref.at[i, pl.ds(route.meta, TILE)])
-        for i in range(ways)
-    ]
-    large = [
-        copies.start(came[i].at[pl.ds(0, route.meta)], in_ref.at[i, pl.ds(0, route.meta)]) for i in range(ways)
-    ]
-    if route.extra:
-        large += [
-            copies.start(came[i].at[pl.ds(route.box, half)], in_ref.at[i, pl.ds(route.box, half)])
-            for i in range(ways)
-        ]
     lasts = []
     for i in range(ways):
-        small[i].wait()
-        tile = in_ref[i, route.meta : route.box, :].astype(F32)
+        tile = came[i][route.meta : route.box, :].astype(F32)
         meta[i : i + 1, :] = tile[:1].astype(I32)
         lasts.append(tile[1:2])
     numbers = pltpu.make_async_copy(meta, leaf_ref, late)
@@ -183,37 +170,29 @@
     total[...] = jnp.zeros(total.shape, F32)
     tails[...] = jnp.zeros(tails.shape, F32)
     numbers.wait()
-    for copy in large:
-        copy.wait()
-
-    @pl.loop(0, ways)
-    def _(i):
+    for i in range(ways):
         if route.extra:
-            tail = in_ref[i, route.tails : route.meta, :].astype(F32)
+            tail = came[i][route.tails : route.meta, :].astype(F32)
         for k in range(route.fan):
             for slot in range(CAP):
                 at = k * CAP + slot
                 leaf = leaf_ref[i, at]
                 rows = pl.ds(pl.multiple_of(leaf * route.rows, TILE), route.rows)
-                total[k, rows, :] += in_ref[i, at * route.rows : (at + 1) * route.rows, :].astype(F32)
+                total[k, rows, :] += came[i][at * route.rows : (at + 1) * route.rows, :].astype(F32)
                 if route.extra:
                     tails[k, pl.ds(leaf, 1), :] += tail[at : at + 1]
 
-    leaving = []
     for k in range(route.fan):
-        send_ref[k, : route.dense_tails, :] = total[k, : route.dense_tails, :].astype(BF16)
+        outs[k][: route.dense_tails, :] = total[k, : route.dense_tails, :].astype(BF16)
         if route.extra:
             for i in range(ways):
                 tails[k, leaves + i : leaves + i + 1, :] = lasts[i]
                 start = route.dense_box + i * half
-                send_ref[k, start : start + half, :] = in_ref[i, route.box :, :]
-            send_ref[k, route.dense_tails : route.dense_box, :] = tails[k].astype(BF16)
-        leaving.append(copies.start(send_ref.at[k], outs[k]))
-    for copy in leaving:
-        copy.wait()
-
-
-def local_part(probes_ref, local_ref, out_ref):
+                outs[k][start : start + half, :] = came[i][route.box :, :]
+            outs[k][route.dense_tails : route.dense_box, :] = tails[k].astype(BF16)
+
+
+def local_kernel(probes_ref, local_ref, out_ref):
     leaves, size = local_ref.shape[0], local_ref.shape[2]
     for i in range(leaves):
         total = dot_t(probes_ref[:, :size], local_ref[i, 0])
@@ -222,72 +201,59 @@
         out_ref[:, i * size : (i + 1) * size] = total
 
 
-def local_kernel(probes_hbm, local_hbm, base_ref, probes_ref, local_ref, sems):
-    copies = Copies(sems)
-    for copy in [copies.start(probes_hbm, probes_ref), copies.start(local_hbm, local_ref)]:
-        copy.wait()
-    local_part(probes_ref, local_ref, base_ref)
-
-
-def last_kernel(routes, devices, *refs):
-    partner_hbm, base_hbm, couplings_hbm, transfer_hbm, basis_hbm = refs[:5]
-    by_low, by_high = routes
-    high, low = grid_of(devices)
-    came_high, came_low = refs[5 : 5 + high], refs[5 + high : 5 + high + low]
-    (
-        out_ref, partner_ref, base_ref, couplings_ref, transfer_ref, basis_ref, in_high, in_low, sems,
-    ) = refs[5 + high + low :]
-    me = lax.axis_index("leaf")
+def far_kernel(by_high, low, partner_ref, base_ref, couplings_ref, transfer_ref, basis_ref, *refs):
+    came, out_ref, boxes = refs[:low], refs[low], refs[low + 1]
     columns = out_ref.shape[0]
     leaves, rank, size = basis_ref.shape
-    split, main = by_low.rows, by_low.main
-    copies = Copies(sems)
-    early = [copies.start(came_low[k], in_low.at[k]) for k in range(low)]
-    early += [
-        copies.start(partner_hbm, partner_ref),
-        copies.start(couplings_hbm, couplings_ref),
-        copies.start(transfer_hbm, transfer_ref),
-        copies.start(basis_hbm, basis_ref),
-    ]
-    later = [copies.start(came_high[k], in_high.at[k]) for k in range(high)]
-    later += [copies.start(base_hbm, base_ref)]
-    for copy in early:
-        copy.wait()
+    high = boxes.shape[0] // low
+    me = lax.axis_index("leaf")
+    for k in range(low):
+        tile = came[k][by_high.dense_tails : by_high.dense_box, :].astype(F32)
+        for i in range(high):
+            start = by_high.dense_box + i * by_high.half
+            packed = came[k][start : start + by_high.half, :]
+            last = tile[leaves + i : leaves + i + 1, :rank]
+            boxes[i * low + k] = jnp.concatenate(
+                [packed[:, :rank].astype(F32), packed[:, rank:].astype(F32), last], axis=0
+            ).astype(BF16)
     far = jnp.zeros((columns, rank), F32)
     for f in range(couplings_ref.shape[1]):
         source = jnp.bitwise_xor(partner_ref[0, f], me)
-        to_high, to_low = source // low, source % low
-        start = pl.multiple_of(by_high.dense_box + to_high * by_high.half, TILE)
-        packed = in_low[to_low, pl.ds(start, by_high.half), :]
-        tile = in_low[to_low, by_high.dense_tails : by_high.dense_box, :].astype(F32)
-        row = lax.broadcasted_iota(I32, tile.shape, 0)
-        last = jnp.sum(jnp.where(row == leaves + to_high, tile, 0.0), axis=0, keepdims=True)[:, :rank]
-        box = jnp.concatenate(
-            [packed[:, :rank].astype(F32), packed[:, rank:].astype(F32), last], axis=0
-        ).astype(BF16)
-        far += dot_t(box, couplings_ref[0, f])
+        far += dot_t(boxes[source], couplings_ref[0, f])
     far = far.astype(BF16)
     down = [dot(far, transfer_ref[j]).astype(BF16) for j in range(leaves)]
-    far_part = [dot(down[j], basis_ref[j]) for j in range(leaves)]
-    for copy in later:
-        copy.wait()
-    tails = sum(in_low[k, by_high.dense_tails : by_high.dense_box, :].astype(F32) for k in range(low))
     for j in range(leaves):
         cols = slice(j * size, (j + 1) * size)
-        upper = sum(in_high[k, j * by_low.rows : (j + 1) * by_low.rows, :].astype(F32) for k in range(high))
-        lower = sum(in_low[k, j * by_high.rows : (j + 1) * by_high.rows, :].astype(F32) for k in range(low))
-        out_ref[:split, cols] = base_ref[:split, cols] + far_part[j][:split] + upper
-        out_ref[split:main, cols] = base_ref[split:main, cols] + far_part[j][split:main] + lower
-        out_ref[main:, cols] = base_ref[main:, cols] + far_part[j][main:] + tails[j : j + 1]
-
-
-def call(kernel, out_shape, out_specs, operands, scratch, flops, nbytes):
+        out_ref[:, cols] = base_ref[:, cols] + dot(down[j], basis_ref[j])
+
+
+def last_kernel(routes, devices, base_ref, *refs):
+    by_low, by_high = routes
+    high, low = grid_of(devices)
+    came_high, came_low, out_ref = refs[:high], refs[high : high + low], refs[high + low]
+    leaves, split, main = by_low.leaves, by_low.rows, by_low.main
+    size = base_ref.shape[1] // leaves
+    tails = sum(came_low[k][by_high.dense_tails : by_high.dense_box, :].astype(F32) for k in range(low))
+    for j in range(leaves):
+        cols = slice(j * size, (j + 1) * size)
+        upper = sum(came_high[k][j * by_low.rows : (j + 1) * by_low.rows, :].astype(F32) for k in range(high))
+        lower = sum(came_low[k][j * by_high.rows : (j + 1) * by_high.rows, :].astype(F32) for k in range(low))
+        out_ref[:split, cols] = base_ref[:split, cols] + upper
+        out_ref[split:main, cols] = base_ref[split:main, cols] + lower
+        out_ref[main:, cols] = base_ref[main:, cols] + tails[j : j + 1]
+
+
+def call(kernel, out_shape, specs, operands, scratch, flops, room=None):
+    outs = jax.tree.leaves(out_shape)
+    nbytes = sum(a.size * a.dtype.itemsize for a in (*operands, *outs))
+    limit = None if room is None else nbytes + room + 2**21
     return pl.pallas_call(
         kernel,
         out_shape=out_shape,
-        in_specs=[ANY] * len(operands),
-        out_specs=out_specs,
+        in_specs=specs[0],
+        out_specs=specs[1],
         scratch_shapes=scratch,
+        compiler_params=pltpu.CompilerParams(vmem_limit_bytes=limit),
         cost_estimate=pl.CostEstimate(flops=flops, bytes_accessed=nbytes, transcendentals=0),
     )(*operands)
 
@@ -314,30 +280,25 @@
         return pltpu.VMEM((count, *like_this.shape), like_this.dtype)
 
     def summed(route, ways, came):
+        total = jax.ShapeDtypeStruct((route.fan, (leaves + 1) * route.rows, size), F32)
+        tails = jax.ShapeDtypeStruct((route.fan, max(TILE, route.dense_box - route.dense_tails), size), F32)
         return call(
             functools.partial(sum_kernel, route, ways),
             [dense(route)] * route.fan,
-            [ANY] * route.fan,
+            ([VMEM] * ways, [VMEM] * route.fan),
             came,
-            [
-                stacked(ways, message(route)),
-                pltpu.VMEM((ways, size), I32),
-                pltpu.SMEM((ways, size), I32),
-                pltpu.VMEM((route.fan, (leaves + 1) * route.rows, size), F32),
-                pltpu.VMEM((route.fan, max(TILE, route.dense_box - route.dense_tails), size), F32),
-                stacked(route.fan, dense(route)),
-            ]
-            + sems(3 * ways + route.fan)
+            [pltpu.VMEM((ways, size), I32), pltpu.SMEM((ways, size), I32)]
+            + like(total, tails)
             + [pltpu.SemaphoreType.DMA(())],
             devices * CAP * route.rows * size,
-            2 * ways * message(route).size,
+            4 * (total.size + tails.size),
         )
 
     dest, leaf = near_dest.T, near_leaf.T
     sent = call(
         functools.partial(products_kernel, routes, devices),
         [message(by_low)] * low + [message(by_high)] * high,
-        [ANY] * (low + high),
+        ([ANY] * 6, [ANY] * (low + high)),
         (dest, leaf, probes, basis, transfer, remote_blocks),
         numbers(dest, leaf)
         + like(probes, basis, transfer, remote_blocks)
@@ -351,7 +312,6 @@
         ]
         + sems(7 + low + high),
         blocks * unit,
-        remote_blocks.size * 2 + 2 * low * message(by_low).size + 2 * high * message(by_high).size,
     )
     came_low, came_high = list(sent[:low]), list(sent[low:])
     came_low[1] = relative(came_low[1], 1)
@@ -361,34 +321,38 @@
         came_low[k] = relative(came_low[k], k)
     came_high[1] = relative(came_high[1], low)
 
+    probes_then, came_low[0] = lax.optimization_barrier((probes, came_low[0]))
+    base_shape = jax.ShapeDtypeStruct((columns, points), F32)
+    base = call(
+        local_kernel, base_shape, ([VMEM] * 2, VMEM), (probes_then, local_blocks), [], leaves * leaves * unit, 0
+    )
+
     to_high = list(summed(by_low, low, came_low))
     for k in range(high - 1, 0, -1):
         to_high[k] = relative(to_high[k], k * low)
+    came_high[0], to_high[0] = lax.optimization_barrier((came_high[0], to_high[0]))
     to_low = list(summed(by_high, high, came_high))
-    probes_then, to_low[0] = lax.optimization_barrier((probes, to_low[0]))
     for k in range(low - 1, 0, -1):
         to_low[k] = relative(to_low[k], k)
 
+    boxes = jax.ShapeDtypeStruct((devices, columns, rank), BF16)
     base = call(
-        local_kernel,
-        jax.ShapeDtypeStruct((columns, points), F32),
-        VMEM,
-        (probes_then, local_blocks),
-        like(probes, local_blocks) + sems(2),
-        leaves * leaves * unit,
-        local_blocks.size * 2,
+        functools.partial(far_kernel, by_high, low),
+        base_shape,
+        ([SMEM] + [VMEM] * (4 + low), VMEM),
+        (far_list, base, couplings, transfer, basis, *to_low),
+        like(boxes),
+        4 * leaves * unit,
+        4 * boxes.size,
     )
     return call(
         functools.partial(last_kernel, routes, devices),
-        jax.ShapeDtypeStruct((columns, points), F32),
-        VMEM,
-        (far_list, base, couplings, transfer, basis, *to_high, *to_low),
-        numbers(far_list)
-        + like(base, couplings, transfer, basis)
-        + [stacked(high, dense(by_low)), stacked(low, dense(by_high))]
-        + sems(5 + low + high),
+        base_shape,
+        ([VMEM] * (1 + high + low), VMEM),
+        (base, *to_high, *to_low),
+        [],
         devices * columns * size,
-        2 * (high * dense(by_low).size + low * dense(by_high).size),
+        0,
     )
 
 

time: 42 us -> 34 us (0.81)
  Pallas kernels: 15.4 us -> 9.22 us
  starting transfers between devices: 16.4 us -> 14.2 us
  waiting for transfers between devices: 7.77 us -> 8.51 us
    pallas_call x5 -> x6, Pallas kernels: 15.4 us -> 9.22 us  [call(): pl.pallas_call(kernel, out_shape=out_shape, in_specs=specs[0], out_specs=...]
    ppermute x12, starting transfers between devices: 16.4 us -> 14.2 us  [per_device(): lax.ppermute(x, 'leaf', [(i, i ^ way) for i in range(devices)])]
    ppermute x12, waiting for transfers between devices: 7.77 us -> 8.51 us  [per_device(): lax.ppermute(x, 'leaf', [(i, i ^ way) for i in range(devices)])]
    unnamed x24 -> x16, local copies, waits for them, and re-layouts: 2.12 us -> 1.84 us
  transfers between devices with their start and end apart: 12 -> 12, of which waited for: 4 -> 5; matrix products, arithmetic and copies ran while one was open for 0% -> 0% of each run, Pallas kernels for 22% -> 12%
where the time goes in v8:
time: 34 us; the launch traced here: 33.9 us
  starting transfers between devices  14.2 us (42%)
  Pallas kernels  9.22 us (27%)
  waiting for transfers between devices  8.51 us (25%)
  local copies, waits for them, and re-layouts  1.84 us (5%)
    ppermute x12, starting transfers between devices, per_device(): lax.ppermute(x, 'leaf', [(i, i ^ way) for i in range(devices)])  14.2 us
    pallas_call x6, Pallas kernels, call(): pl.pallas_call(kernel, out_shape=out_shape, in_specs=specs[0], out_specs=...  9.22 us
    ppermute x12, waiting for transfers between devices, per_device(): lax.ppermute(x, 'leaf', [(i, i ^ way) for i in range(devices)])  8.51 us
    unnamed x16, local copies, waits for them, and re-layouts  1.84 us
  transfers between devices with their start and end apart: 12, of which 5 were waited for; matrix products, arithmetic and copies ran while one was open for 0% of the time, Pallas kernels for 12%

profile of v8, /device:TPU:0, one launch (start us, length us, event | category | flops | bytes accessed | tf_op | source)
XLA Modules:
  0.0 33.9 jit_solution(12977660616596645488)
XLA Ops:
  0.0 3.5 %shard_map.91 = (bf16[784,128]{1,0:T(8,128)(2,1)}, bf16[784,128]{1,0:T(8,128)(2,1)}, bf16[784,128]{1,0:T(8,128)(2,1)}, bf16[784,128]{1,0:T(8,128)(2,1)}, bf16[32...) custom-call(s32[4,8]{1,0:T(4,128)} %bitcast.2, ...), custom_call_target="tpu_custom_call" | custom-call | flops 68157440 | bytes 2509056 | tf_op jit(solution)/shard_map/pallas_call | solution.py:250
  3.5 0.0 copy-start.3
  3.6 0.5 %collective-permute-start = (bf16[784,128]{1,0:T(8,128)(2,1)}, bf16[784,128]{1,0:T(8,128)(2,1)S(1)}, u32[]{:S(2)}, u32[]{:S(2)}) collective-permute-start(bf16[784,128]{1,0:T(8,128)(2,1)} %get-tuple-element.29), channel_id=1, source_target_pairs={{0,1},{1,0},{2,3},{3,2},{4,5},{5,4},{6,7},{7,6},{8,9},{9,8},{10,11... | collective-permute-start | bytes 602120 | tf_op jit(solution)/shard_map/ppermute | solution.py:275
  4.1 2.6 %collective-permute-start.1 = (bf16[784,128]{1,0:T(8,128)(2,1)}, bf16[784,128]{1,0:T(8,128)(2,1)S(1)}, u32[]{:S(2)}, u32[]{:S(2)}) collective-permute-start(bf16[784,128]{1,0:T(8,128)(2,1)} %get-tuple-element.30), channel_id=1, source_target_pairs={{0,2},{1,3},{2,0},{3,1},{4,6},{5,7},{6,4},{7,5},{8,10},{9,11},{10,... | collective-permute-start | bytes 602120 | tf_op jit(solution)/shard_map/ppermute | solution.py:275
  6.7 0.1 collective-permute-start.2
  6.7 1.8 %collective-permute-start.3 = (bf16[320,128]{1,0:T(8,128)(2,1)}, bf16[320,128]{1,0:T(8,128)(2,1)S(1)}, u32[]{:S(2)}, u32[]{:S(2)}) collective-permute-start(bf16[320,128]{1,0:T(8,128)(2,1)} %get-tuple-element.34), channel_id=1, source_target_pairs={{0,4},{1,5},{2,6},{3,7},{4,0},{5,1},{6,2},{7,3},{8,12},{9,13},{10,... | collective-permute-start | bytes 245768 | tf_op jit(solution)/shard_map/ppermute | solution.py:275
  8.5 2.6 %collective-permute-start.4 = (bf16[320,128]{1,0:T(8,128)(2,1)}, bf16[320,128]{1,0:T(8,128)(2,1)S(1)}, u32[]{:S(2)}, u32[]{:S(2)}) collective-permute-start(bf16[320,128]{1,0:T(8,128)(2,1)} %get-tuple-element.35), channel_id=1, source_target_pairs={{0,8},{1,9},{2,10},{3,11},{4,12},{5,13},{6,14},{7,15},{8,0},{9,1},... | collective-permute-start | bytes 245768 | tf_op jit(solution)/shard_map/ppermute | solution.py:275
  11.1 0.0 collective-permute-start.5
  11.1 1.6 %collective-permute-done.1.refs_2_ = bf16[784,128]{1,0:T(8,128)(2,1)S(1)} collective-permute-done((bf16[784,128]{1,0:T(8,128)(2,1)}, bf16[784,128]{1,0:T(8,128)(2,1)S(1)}, u32[]{:S(2)}, u32[]{:S(2)}) %collective-permute-start.1) | collective-permute-done | bytes 200736 | tf_op jit(solution)/shard_map/ppermute | solution.py:275
  12.7 3.8 %collective-permute-done.2.refs_3_ = bf16[784,128]{1,0:T(8,128)(2,1)S(1)} collective-permute-done((bf16[784,128]{1,0:T(8,128)(2,1)}, bf16[784,128]{1,0:T(8,128)(2,1)S(1)}, u32[]{:S(2)}, u32[]{:S(2)}) %collective-permute-start.2) | collective-permute-done | bytes 200736 | tf_op jit(solution)/shard_map/ppermute | solution.py:275
  16.5 0.9 %copy-done.4 = bf16[784,128]{1,0:T(8,128)(2,1)S(1)} copy-done((bf16[784,128]{1,0:T(8,128)(2,1)S(1)}, bf16[784,128]{1,0:T(8,128)(2,1)}, u32[]{:S(2)}) %copy-start.4) | copy-done | bytes 200728
  17.4 1.1 %shard_map.93 = (bf16[384,128]{1,0:T(8,128)(2,1)S(1)}, bf16[384,128]{1,0:T(8,128)(2,1)S(1)}, bf16[384,128]{1,0:T(8,128)(2,1)S(1)}, bf16[384,128]{1,0:T(8,128)(2,1)S(1)}) custom-call(bf16[784,128]{1,0:T(8,128)(2,1)S(1)} %copy-done.4, bf16[784,128]{1,0:T(8,128)(2,1)S(1)} %collective-permute-done.refs_1_, bf16[784,128]{1,0:T(8,128)(2,1)S(1)} %collective-permute-done.1.refs_2_, ...), custom_call_target="tpu_custom_call" | custom-call | flops 393216 | bytes 1196032 | tf_op jit(solution)/shard_map/pallas_call | solution.py:250
  18.5 0.9 %copy-done.6 = bf16[320,128]{1,0:T(8,128)(2,1)S(1)} copy-done((bf16[320,128]{1,0:T(8,128)(2,1)S(1)}, bf16[320,128]{1,0:T(8,128)(2,1)}, u32[]{:S(2)}) %copy-start.6) | copy-done | bytes 81944
  19.4 0.9 %shard_map.94 = (bf16[272,128]{1,0:T(8,128)(2,1)S(1)}, bf16[272,128]{1,0:T(8,128)(2,1)S(1)}, bf16[272,128]{1,0:T(8,128)(2,1)S(1)}, bf16[272,128]{1,0:T(8,128)(2,1)S(1)}) custom-call(bf16[320,128]{1,0:T(8,128)(2,1)S(1)} %copy-done.6, bf16[320,128]{1,0:T(8,128)(2,1)S(1)} %collective-permute-done.3.refs_1_, ...), custom_call_target="tpu_custom_call" | custom-call | flops 131072 | bytes 606208 | tf_op jit(solution)/shard_map/pallas_call | solution.py:250
  20.3 0.4 %collective-permute-start.6 = (bf16[272,128]{1,0:T(8,128)(2,1)S(1)}, bf16[272,128]{1,0:T(8,128)(2,1)S(1)}, u32[]{:S(2)}, u32[]{:S(2)}) collective-permute-start(bf16[272,128]{1,0:T(8,128)(2,1)S(1)} %get-tuple-element.38), channel_id=1, source_target_pairs={{0,1},{1,0},{2,3},{3,2},{4,5},{5,4},{6,7},{7,6},{8,9},{9,8},{10,11... | collective-permute-start | bytes 208904 | tf_op jit(solution)/shard_map/ppermute | solution.py:275
  20.8 1.6 %collective-permute-start.9 = (bf16[384,128]{1,0:T(8,128)(2,1)S(1)}, bf16[384,128]{1,0:T(8,128)(2,1)S(1)}, u32[]{:S(2)}, u32[]{:S(2)}) collective-permute-start(bf16[384,128]{1,0:T(8,128)(2,1)S(1)} %get-tuple-element.42), channel_id=1, source_target_pairs={{0,4},{1,5},{2,6},{3,7},{4,0},{5,1},{6,2},{7,3},{8,12},{9,13},{10,... | collective-permute-start | bytes 294920 | tf_op jit(solution)/shard_map/ppermute | solution.py:275
  22.3 2.9 %collective-permute-start.10 = (bf16[384,128]{1,0:T(8,128)(2,1)S(1)}, bf16[384,128]{1,0:T(8,128)(2,1)S(1)}, u32[]{:S(2)}, u32[]{:S(2)}) collective-permute-start(bf16[384,128]{1,0:T(8,128)(2,1)S(1)} %get-tuple-element.43), channel_id=1, source_target_pairs={{0,8},{1,9},{2,10},{3,11},{4,12},{5,13},{6,14},{7,15},{8,0},{9,1},... | collective-permute-start | bytes 294920 | tf_op jit(solution)/shard_map/ppermute | solution.py:275
  25.2 1.7 %collective-permute-start.7 = (bf16[272,128]{1,0:T(8,128)(2,1)S(1)}, bf16[272,128]{1,0:T(8,128)(2,1)S(1)}, u32[]{:S(2)}, u32[]{:S(2)}) collective-permute-start(bf16[272,128]{1,0:T(8,128)(2,1)S(1)} %get-tuple-element.39), channel_id=1, source_target_pairs={{0,2},{1,3},{2,0},{3,1},{4,6},{5,7},{6,4},{7,5},{8,10},{9,11},{10,... | collective-permute-start | bytes 208904 | tf_op jit(solution)/shard_map/ppermute | solution.py:275
  27.0 1.5 %shard_map.92.base_ref = f32[65,1024]{1,0:T(8,128)S(1)} custom-call(bf16[65,1024]{1,0:T(8,128)(2,1)S(1)} %copy-done.1, bf16[8,8,128,128]{3,2,1,0:T(8,128)(2,1)S(1)} %copy-done), custom_call_target="tpu_custom_call" | custom-call | flops 136314880 | bytes 2496512 | tf_op jit(solution)/shard_map/pallas_call | solution.py:250
  28.5 1.0 %collective-permute-done.7.refs_2_.refs_6_ = bf16[272,128]{1,0:T(8,128)(2,1)S(1)} collective-permute-done((bf16[272,128]{1,0:T(8,128)(2,1)S(1)}, bf16[272,128]{1,0:T(8,128)(2,1)S(1)}, u32[]{:S(2)}, u32[]{:S(2)}) %collective-permute-start.7) | collective-permute-done | bytes 69664 | tf_op jit(solution)/shard_map/ppermute | solution.py:275
  29.5 1.5 %collective-permute-done.8.refs_3_.refs_7_ = bf16[272,128]{1,0:T(8,128)(2,1)S(1)} collective-permute-done((bf16[272,128]{1,0:T(8,128)(2,1)S(1)}, bf16[272,128]{1,0:T(8,128)(2,1)S(1)}, u32[]{:S(2)}, u32[]{:S(2)}) %collective-permute-start.8) | collective-permute-done | bytes 69664 | tf_op jit(solution)/shard_map/ppermute | solution.py:275
  31.0 1.4 %shard_map.95.base_ref = f32[65,1024]{1,0:T(8,128)S(1)} custom-call(s32[1,12]{1,0:T(1,128)S(1)} %copy-done.7, f32[65,1024]{1,0:T(8,128)S(1)} %shard_map.92.base_ref, bf16[1,12,64,64]{3,2,1,0:T(8,128)(2,1)S(1)} %copy-done.5, bf16[8,64,64]{2,1,0:T(8,128)(2,1)S(1)} %copy-done.2, bf16[8,64,128]{2,1,0:T(8,128)(2,1)S(1)} %copy-done.3, ...), custom_call_target="tpu_custom_call" | custom-call | flops 68157440 | bytes 1105968 | tf_op jit(solution)/shard_map/pallas_call | solution.py:250
  32.4 0.6 %collective-permute-done.10.refs_2_ = bf16[384,128]{1,0:T(8,128)(2,1)S(1)} collective-permute-done((bf16[384,128]{1,0:T(8,128)(2,1)S(1)}, bf16[384,128]{1,0:T(8,128)(2,1)S(1)}, u32[]{:S(2)}, u32[]{:S(2)}) %collective-permute-start.10) | collective-permute-done | bytes 98336 | tf_op jit(solution)/shard_map/ppermute | solution.py:275
  33.1 0.8 %shard_map.96 = f32[65,1024]{1,0:T(8,128)} custom-call(f32[65,1024]{1,0:T(8,128)S(1)} %shard_map.95.base_ref, bf16[384,128]{1,0:T(8,128)(2,1)S(1)} %get-tuple-element.41.refs_0_, bf16[384,128]{1,0:T(8,128)(2,1)S(1)} %collective-permute-done.9.refs_1_, bf16[384,128]{1,0:T(8,128)(2,1)S(1)} %collective-permute-done.10.refs_2_, ...), custom_call_target="tpu_custom_call" | custom-call | flops 133120 | bytes 1204224 | tf_op jit(solution)/shard_map/pallas_call | solution.py:250
  (22 shorter events, 0.1 us)
Async XLA Ops:
  0.0 27.0 %copy-start.1 = (bf16[65,1024]{1,0:T(8,128)(2,1)S(1)}, bf16[65,1024]{1,0:T(8,128)(2,1)}, u32[]{:S(2)}) copy-start(bf16[65,1024]{1,0:T(8,128)(2,1)} %probes_ref) | copy-start | bytes 399364
  0.0 27.0 %copy-start = (bf16[8,8,128,128]{3,2,1,0:T(8,128)(2,1)S(1)}, bf16[8,8,128,128]{3,2,1,0:T(8,128)(2,1)}, u32[]{:S(2)}) copy-start(bf16[8,8,128,128]{3,2,1,0:T(8,128)(2,1)} %local_ref.1) | copy-start | bytes 6291460
  3.5 27.5 %copy-start.2 = (bf16[8,64,64]{2,1,0:T(8,128)(2,1)S(1)}, bf16[8,64,64]{2,1,0:T(8,128)(2,1)}, u32[]{:S(2)}) copy-start(bf16[8,64,64]{2,1,0:T(8,128)(2,1)} %transfer_ref.1) | copy-start | bytes 196612
  3.5 27.5 %copy-start.3 = (bf16[8,64,128]{2,1,0:T(8,128)(2,1)S(1)}, bf16[8,64,128]{2,1,0:T(8,128)(2,1)}, u32[]{:S(2)}) copy-start(bf16[8,64,128]{2,1,0:T(8,128)(2,1)} %basis_ref.1) | copy-start | bytes 393220
  3.6 7.6 %collective-permute-start = (bf16[784,128]{1,0:T(8,128)(2,1)}, bf16[784,128]{1,0:T(8,128)(2,1)S(1)}, u32[]{:S(2)}, u32[]{:S(2)}) collective-permute-start(bf16[784,128]{1,0:T(8,128)(2,1)} %get-tuple-element.29), channel_id=1, source_target_pairs={{0,1},{1,0},{2,3},{3,2},{4,5},{5,4},{6,7},{7,6},{8,9},{9,8},{10,11... | collective-permute-start | bytes 602120 | tf_op jit(solution)/shard_map/ppermute | solution.py:275
  4.1 8.6 %collective-permute-start.1 = (bf16[784,128]{1,0:T(8,128)(2,1)}, bf16[784,128]{1,0:T(8,128)(2,1)S(1)}, u32[]{:S(2)}, u32[]{:S(2)}) collective-permute-start(bf16[784,128]{1,0:T(8,128)(2,1)} %get-tuple-element.30), channel_id=1, source_target_pairs={{0,2},{1,3},{2,0},{3,1},{4,6},{5,7},{6,4},{7,5},{8,10},{9,11},{10,... | collective-permute-start | bytes 602120 | tf_op jit(solution)/shard_map/ppermute | solution.py:275
  6.7 9.8 %collective-permute-start.2 = (bf16[784,128]{1,0:T(8,128)(2,1)}, bf16[784,128]{1,0:T(8,128)(2,1)S(1)}, u32[]{:S(2)}, u32[]{:S(2)}) collective-permute-start(bf16[784,128]{1,0:T(8,128)(2,1)} %get-tuple-element.31), channel_id=1, source_target_pairs={{0,3},{1,2},{2,1},{3,0},{4,7},{5,6},{6,5},{7,4},{8,11},{9,10},{10,... | collective-permute-start | bytes 602120 | tf_op jit(solution)/shard_map/ppermute | solution.py:275
  6.7 11.8 %collective-permute-start.3 = (bf16[320,128]{1,0:T(8,128)(2,1)}, bf16[320,128]{1,0:T(8,128)(2,1)S(1)}, u32[]{:S(2)}, u32[]{:S(2)}) collective-permute-start(bf16[320,128]{1,0:T(8,128)(2,1)} %get-tuple-element.34), channel_id=1, source_target_pairs={{0,4},{1,5},{2,6},{3,7},{4,0},{5,1},{6,2},{7,3},{8,12},{9,13},{10,... | collective-permute-start | bytes 245768 | tf_op jit(solution)/shard_map/ppermute | solution.py:275
  8.5 10.0 %collective-permute-start.4 = (bf16[320,128]{1,0:T(8,128)(2,1)}, bf16[320,128]{1,0:T(8,128)(2,1)S(1)}, u32[]{:S(2)}, u32[]{:S(2)}) collective-permute-start(bf16[320,128]{1,0:T(8,128)(2,1)} %get-tuple-element.35), channel_id=1, source_target_pairs={{0,8},{1,9},{2,10},{3,11},{4,12},{5,13},{6,14},{7,15},{8,0},{9,1},... | collective-permute-start | bytes 245768 | tf_op jit(solution)/shard_map/ppermute | solution.py:275
  11.1 7.4 %collective-permute-start.5 = (bf16[320,128]{1,0:T(8,128)(2,1)}, bf16[320,128]{1,0:T(8,128)(2,1)S(1)}, u32[]{:S(2)}, u32[]{:S(2)}) collective-permute-start(bf16[320,128]{1,0:T(8,128)(2,1)} %get-tuple-element.36), channel_id=1, source_target_pairs={{0,12},{1,13},{2,14},{3,15},{4,8},{5,9},{6,10},{7,11},{8,4},{9,5},... | collective-permute-start | bytes 245768 | tf_op jit(solution)/shard_map/ppermute | solution.py:275
  16.5 0.9 %copy-start.4 = (bf16[784,128]{1,0:T(8,128)(2,1)S(1)}, bf16[784,128]{1,0:T(8,128)(2,1)}, u32[]{:S(2)}) copy-start(bf16[784,128]{1,0:T(8,128)(2,1)} %get-tuple-element.28.refs_0_) | copy-start | bytes 602116
  17.4 13.6 %copy-start.5 = (bf16[1,12,64,64]{3,2,1,0:T(8,128)(2,1)S(1)}, bf16[1,12,64,64]{3,2,1,0:T(8,128)(2,1)}, u32[]{:S(2)}) copy-start(bf16[1,12,64,64]{3,2,1,0:T(8,128)(2,1)} %couplings_ref.1) | copy-start | bytes 294916
  18.5 0.9 %copy-start.6 = (bf16[320,128]{1,0:T(8,128)(2,1)S(1)}, bf16[320,128]{1,0:T(8,128)(2,1)}, u32[]{:S(2)}) copy-start(bf16[320,128]{1,0:T(8,128)(2,1)} %get-tuple-element.33.refs_0_) | copy-start | bytes 245764
  19.4 11.6 %copy-start.7 = (s32[1,12]{1,0:T(1,128)S(1)}, s32[1,12]{1,0:T(1,128)}, u32[]{:S(2)}) copy-start(s32[1,12]{1,0:T(1,128)} %partner_ref.1) | copy-start | bytes 148
  20.3 6.6 %collective-permute-start.6 = (bf16[272,128]{1,0:T(8,128)(2,1)S(1)}, bf16[272,128]{1,0:T(8,128)(2,1)S(1)}, u32[]{:S(2)}, u32[]{:S(2)}) collective-permute-start(bf16[272,128]{1,0:T(8,128)(2,1)S(1)} %get-tuple-element.38), channel_id=1, source_target_pairs={{0,1},{1,0},{2,3},{3,2},{4,5},{5,4},{6,7},{7,6},{8,9},{9,8},{10,11... | collective-permute-start | bytes 208904 | tf_op jit(solution)/shard_map/ppermute | solution.py:275
  20.8 11.7 %collective-permute-start.9 = (bf16[384,128]{1,0:T(8,128)(2,1)S(1)}, bf16[384,128]{1,0:T(8,128)(2,1)S(1)}, u32[]{:S(2)}, u32[]{:S(2)}) collective-permute-start(bf16[384,128]{1,0:T(8,128)(2,1)S(1)} %get-tuple-element.42), channel_id=1, source_target_pairs={{0,4},{1,5},{2,6},{3,7},{4,0},{5,1},{6,2},{7,3},{8,12},{9,13},{10,... | collective-permute-start | bytes 294920 | tf_op jit(solution)/shard_map/ppermute | solution.py:275
  22.3 10.7 %collective-permute-start.10 = (bf16[384,128]{1,0:T(8,128)(2,1)S(1)}, bf16[384,128]{1,0:T(8,128)(2,1)S(1)}, u32[]{:S(2)}, u32[]{:S(2)}) collective-permute-start(bf16[384,128]{1,0:T(8,128)(2,1)S(1)} %get-tuple-element.43), channel_id=1, source_target_pairs={{0,8},{1,9},{2,10},{3,11},{4,12},{5,13},{6,14},{7,15},{8,0},{9,1},... | collective-permute-start | bytes 294920 | tf_op jit(solution)/shard_map/ppermute | solution.py:275
  25.2 7.9 %collective-permute-start.11 = (bf16[384,128]{1,0:T(8,128)(2,1)S(1)}, bf16[384,128]{1,0:T(8,128)(2,1)S(1)}, u32[]{:S(2)}, u32[]{:S(2)}) collective-permute-start(bf16[384,128]{1,0:T(8,128)(2,1)S(1)} %get-tuple-element.44), channel_id=1, source_target_pairs={{0,12},{1,13},{2,14},{3,15},{4,8},{5,9},{6,10},{7,11},{8,4},{9,5},... | collective-permute-start | bytes 294920 | tf_op jit(solution)/shard_map/ppermute | solution.py:275
  25.2 4.3 %collective-permute-start.7 = (bf16[272,128]{1,0:T(8,128)(2,1)S(1)}, bf16[272,128]{1,0:T(8,128)(2,1)S(1)}, u32[]{:S(2)}, u32[]{:S(2)}) collective-permute-start(bf16[272,128]{1,0:T(8,128)(2,1)S(1)} %get-tuple-element.39), channel_id=1, source_target_pairs={{0,2},{1,3},{2,0},{3,1},{4,6},{5,7},{6,4},{7,5},{8,10},{9,11},{10,... | collective-permute-start | bytes 208904 | tf_op jit(solution)/shard_map/ppermute | solution.py:275
  26.9 4.0 %collective-permute-start.8 = (bf16[272,128]{1,0:T(8,128)(2,1)S(1)}, bf16[272,128]{1,0:T(8,128)(2,1)S(1)}, u32[]{:S(2)}, u32[]{:S(2)}) collective-permute-start(bf16[272,128]{1,0:T(8,128)(2,1)S(1)} %get-tuple-element.40), channel_id=1, source_target_pairs={{0,3},{1,2},{2,1},{3,0},{4,7},{5,6},{6,5},{7,4},{8,11},{9,10},{10,... | collective-permute-start | bytes 208904 | tf_op jit(solution)/shard_map/ppermute | solution.py:275

commit v9 on v8

--- a/solution.py
+++ b/solution.py
@@ -192,7 +192,9 @@
             outs[k][route.dense_tails : route.dense_box, :] = tails[k].astype(BF16)
 
 
-def local_kernel(probes_ref, local_ref, out_ref):
+def local_kernel(probes_ref, local_ref, own_low, own_high, out_ref, kept_low, kept_high):
+    kept_low[...] = own_low[...]
+    kept_high[...] = own_high[...]
     leaves, size = local_ref.shape[0], local_ref.shape[2]
     for i in range(leaves):
         total = dot_t(probes_ref[:, :size], local_ref[i, 0])
@@ -321,10 +323,15 @@
         came_low[k] = relative(came_low[k], k)
     came_high[1] = relative(came_high[1], low)
 
-    probes_then, came_low[0] = lax.optimization_barrier((probes, came_low[0]))
     base_shape = jax.ShapeDtypeStruct((columns, points), F32)
-    base = call(
-        local_kernel, base_shape, ([VMEM] * 2, VMEM), (probes_then, local_blocks), [], leaves * leaves * unit, 0
+    base, came_low[0], came_high[0] = call(
+        local_kernel,
+        (base_shape, message(by_low), message(by_high)),
+        ([VMEM] * 4, (VMEM,) * 3),
+        (probes, local_blocks, came_low[0], came_high[0]),
+        [],
+        leaves * leaves * unit,
+        0,
     )
 
     to_high = list(summed(by_low, low, came_low))
@@ -332,7 +339,7 @@
         to_high[k] = relative(to_high[k], k * low)
     came_high[0], to_high[0] = lax.optimization_barrier((came_high[0], to_high[0]))
     to_low = list(summed(by_high, high, came_high))
-    for k in range(low - 1, 0, -1):
+    for k in range(1, low):
         to_low[k] = relative(to_low[k], k)
 
     boxes = jax.ShapeDtypeStruct((devices, columns, rank), BF16)

time: 34 us -> 32.7 us (0.962)
  waiting for transfers between devices: 8.51 us -> 5.09 us
  local copies, waits for them, and re-layouts: 1.84 us -> 4.33 us
  starting transfers between devices: 14.2 us -> 13.7 us
    ppermute x12, waiting for transfers between devices: 8.51 us -> 5.09 us  [per_device(): lax.ppermute(x, 'leaf', [(i, i ^ way) for i in range(devices)])]
    unnamed x16, local copies, waits for them, and re-layouts: 1.84 us -> 4.33 us
    ppermute x12, starting transfers between devices: 14.2 us -> 13.7 us  [per_device(): lax.ppermute(x, 'leaf', [(i, i ^ way) for i in range(devices)])]
  transfers between devices with their start and end apart: 12 -> 12, of which waited for: 5 -> 4; matrix products, arithmetic and copies ran while one was open for 0% -> 0% of each run, Pallas kernels for 12% -> 12%
where the time goes in v9:
time: 32.7 us; the launch traced here: 32.4 us
  starting transfers between devices  13.7 us (42%)
  Pallas kernels  9.2 us (28%)
  waiting for transfers between devices  5.09 us (16%)
  local copies, waits for them, and re-layouts  4.33 us (13%)
    ppermute x12, starting transfers between devices, per_device(): lax.ppermute(x, 'leaf', [(i, i ^ way) for i in range(devices)])  13.7 us
    pallas_call x6, Pallas kernels, call(): pl.pallas_call(kernel, out_shape=out_shape, in_specs=specs[0], out_specs=...  9.2 us
    ppermute x12, waiting for transfers between devices, per_device(): lax.ppermute(x, 'leaf', [(i, i ^ way) for i in range(devices)])  5.09 us
    unnamed x16, local copies, waits for them, and re-layouts  4.33 us
  transfers between devices with their start and end apart: 12, of which 4 were waited for; matrix products, arithmetic and copies ran while one was open for 0% of the time, Pallas kernels for 12%

profile of v9, /device:TPU:0, one launch (start us, length us, event | category | flops | bytes accessed | tf_op | source)
XLA Modules:
  0.0 32.4 jit_solution(13748020714806466626)
XLA Ops:
  0.0 3.4 %shard_map.91 = (bf16[784,128]{1,0:T(8,128)(2,1)}, bf16[784,128]{1,0:T(8,128)(2,1)}, bf16[784,128]{1,0:T(8,128)(2,1)}, bf16[784,128]{1,0:T(8,128)(2,1)}, bf16[32...) custom-call(s32[4,8]{1,0:T(4,128)} %bitcast.2, ...), custom_call_target="tpu_custom_call" | custom-call | flops 68157440 | bytes 2509056 | tf_op jit(solution)/shard_map/pallas_call | solution.py:252
  3.5 0.5 %collective-permute-start = (bf16[784,128]{1,0:T(8,128)(2,1)}, bf16[784,128]{1,0:T(8,128)(2,1)S(1)}, u32[]{:S(2)}, u32[]{:S(2)}) collective-permute-start(bf16[784,128]{1,0:T(8,128)(2,1)} %get-tuple-element.31), channel_id=1, source_target_pairs={{0,1},{1,0},{2,3},{3,2},{4,5},{5,4},{6,7},{7,6},{8,9},{9,8},{10,11... | collective-permute-start | bytes 602120 | tf_op jit(solution)/shard_map/ppermute | solution.py:277
  4.0 2.6 %collective-permute-start.1 = (bf16[784,128]{1,0:T(8,128)(2,1)}, bf16[784,128]{1,0:T(8,128)(2,1)S(1)}, u32[]{:S(2)}, u32[]{:S(2)}) collective-permute-start(bf16[784,128]{1,0:T(8,128)(2,1)} %get-tuple-element.32), channel_id=1, source_target_pairs={{0,2},{1,3},{2,0},{3,1},{4,6},{5,7},{6,4},{7,5},{8,10},{9,11},{10,... | collective-permute-start | bytes 602120 | tf_op jit(solution)/shard_map/ppermute | solution.py:277
  6.6 0.1 collective-permute-start.2
  6.6 1.8 %collective-permute-start.3 = (bf16[320,128]{1,0:T(8,128)(2,1)}, bf16[320,128]{1,0:T(8,128)(2,1)S(1)}, u32[]{:S(2)}, u32[]{:S(2)}) collective-permute-start(bf16[320,128]{1,0:T(8,128)(2,1)} %get-tuple-element.36), channel_id=1, source_target_pairs={{0,4},{1,5},{2,6},{3,7},{4,0},{5,1},{6,2},{7,3},{8,12},{9,13},{10,... | collective-permute-start | bytes 245768 | tf_op jit(solution)/shard_map/ppermute | solution.py:277
  8.4 2.6 %collective-permute-start.4 = (bf16[320,128]{1,0:T(8,128)(2,1)}, bf16[320,128]{1,0:T(8,128)(2,1)S(1)}, u32[]{:S(2)}, u32[]{:S(2)}) collective-permute-start(bf16[320,128]{1,0:T(8,128)(2,1)} %get-tuple-element.37), channel_id=1, source_target_pairs={{0,8},{1,9},{2,10},{3,11},{4,12},{5,13},{6,14},{7,15},{8,0},{9,1},... | collective-permute-start | bytes 245768 | tf_op jit(solution)/shard_map/ppermute | solution.py:277
  11.0 1.6 %copy-done = bf16[8,8,128,128]{3,2,1,0:T(8,128)(2,1)S(1)} copy-done((bf16[8,8,128,128]{3,2,1,0:T(8,128)(2,1)S(1)}, bf16[8,8,128,128]{3,2,1,0:T(8,128)(2,1)}, u32[]{:S(2)}) %copy-start) | copy-done | bytes 2097176
  12.6 0.9 %copy-done.1 = bf16[65,1024]{1,0:T(8,128)(2,1)S(1)} copy-done((bf16[65,1024]{1,0:T(8,128)(2,1)S(1)}, bf16[65,1024]{1,0:T(8,128)(2,1)}, u32[]{:S(2)}) %copy-start.1) | copy-done | bytes 133144
  13.5 0.9 %copy-done.4 = bf16[784,128]{1,0:T(8,128)(2,1)S(1)} copy-done((bf16[784,128]{1,0:T(8,128)(2,1)S(1)}, bf16[784,128]{1,0:T(8,128)(2,1)}, u32[]{:S(2)}) %copy-start.4) | copy-done | bytes 200728
  14.5 0.9 %copy-done.6 = bf16[320,128]{1,0:T(8,128)(2,1)S(1)} copy-done((bf16[320,128]{1,0:T(8,128)(2,1)S(1)}, bf16[320,128]{1,0:T(8,128)(2,1)}, u32[]{:S(2)}) %copy-start.6) | copy-done | bytes 81944
  15.4 1.6 %shard_map.92 = (f32[65,1024]{1,0:T(8,128)S(1)}, bf16[784,128]{1,0:T(8,128)(2,1)S(1)}, bf16[320,128]{1,0:T(8,128)(2,1)S(1)}) custom-call(bf16[65,1024]{1,0:T(8,128)(2,1)S(1)} %copy-done.1, bf16[8,8,128,128]{3,2,1,0:T(8,128)(2,1)S(1)} %copy-done, bf16[784,128]{1,0:T(8,128)(2,1)S(1)} %copy-done.4, bf16[320,128]{1,0:T(8,128)(2,1)S(1)} %copy-done.6), custom_call_target="tpu_custom_call" | custom-call | flops 136314880 | bytes 3061760 | tf_op jit(solution)/shard_map/pallas_call | solution.py:252
  16.9 1.0 %shard_map.93 = (bf16[384,128]{1,0:T(8,128)(2,1)S(1)}, bf16[384,128]{1,0:T(8,128)(2,1)S(1)}, bf16[384,128]{1,0:T(8,128)(2,1)S(1)}, bf16[384,128]{1,0:T(8,128)(2,1)S(1)}) custom-call(bf16[784,128]{1,0:T(8,128)(2,1)S(1)} %get-tuple-element.30.refs_0_, bf16[784,128]{1,0:T(8,128)(2,1)S(1)} %collective-permute-done.refs_1_, ...), custom_call_target="tpu_custom_call" | custom-call | flops 393216 | bytes 1196032 | tf_op jit(solution)/shard_map/pallas_call | solution.py:252
  18.0 0.1 collective-permute-done.4.refs_2_
  18.1 1.0 %shard_map.94 = (bf16[272,128]{1,0:T(8,128)(2,1)S(1)}, bf16[272,128]{1,0:T(8,128)(2,1)S(1)}, bf16[272,128]{1,0:T(8,128)(2,1)S(1)}, bf16[272,128]{1,0:T(8,128)(2,1)S(1)}) custom-call(bf16[320,128]{1,0:T(8,128)(2,1)S(1)} %get-tuple-element.35.refs_0_, bf16[320,128]{1,0:T(8,128)(2,1)S(1)} %collective-permute-done.3.refs_1_, ...), custom_call_target="tpu_custom_call" | custom-call | flops 131072 | bytes 606208 | tf_op jit(solution)/shard_map/pallas_call | solution.py:252
  19.1 0.1 collective-permute-start.6
  19.2 1.7 %collective-permute-start.9 = (bf16[384,128]{1,0:T(8,128)(2,1)S(1)}, bf16[384,128]{1,0:T(8,128)(2,1)S(1)}, u32[]{:S(2)}, u32[]{:S(2)}) collective-permute-start(bf16[384,128]{1,0:T(8,128)(2,1)S(1)} %get-tuple-element.44), channel_id=1, source_target_pairs={{0,4},{1,5},{2,6},{3,7},{4,0},{5,1},{6,2},{7,3},{8,12},{9,13},{10,... | collective-permute-start | bytes 294920 | tf_op jit(solution)/shard_map/ppermute | solution.py:277
  20.9 2.6 %collective-permute-start.10 = (bf16[384,128]{1,0:T(8,128)(2,1)S(1)}, bf16[384,128]{1,0:T(8,128)(2,1)S(1)}, u32[]{:S(2)}, u32[]{:S(2)}) collective-permute-start(bf16[384,128]{1,0:T(8,128)(2,1)S(1)} %get-tuple-element.45), channel_id=1, source_target_pairs={{0,8},{1,9},{2,10},{3,11},{4,12},{5,13},{6,14},{7,15},{8,0},{9,1},... | collective-permute-start | bytes 294920 | tf_op jit(solution)/shard_map/ppermute | solution.py:277
  23.5 0.2 collective-permute-start.11
  23.6 1.6 %collective-permute-start.7 = (bf16[272,128]{1,0:T(8,128)(2,1)S(1)}, bf16[272,128]{1,0:T(8,128)(2,1)S(1)}, u32[]{:S(2)}, u32[]{:S(2)}) collective-permute-start(bf16[272,128]{1,0:T(8,128)(2,1)S(1)} %get-tuple-element.41), channel_id=1, source_target_pairs={{0,2},{1,3},{2,0},{3,1},{4,6},{5,7},{6,4},{7,5},{8,10},{9,11},{10,... | collective-permute-start | bytes 208904 | tf_op jit(solution)/shard_map/ppermute | solution.py:277
  25.2 2.7 %collective-permute-done.7.refs_2_.refs_6_ = bf16[272,128]{1,0:T(8,128)(2,1)S(1)} collective-permute-done((bf16[272,128]{1,0:T(8,128)(2,1)S(1)}, bf16[272,128]{1,0:T(8,128)(2,1)S(1)}, u32[]{:S(2)}, u32[]{:S(2)}) %collective-permute-start.7) | collective-permute-done | bytes 69664 | tf_op jit(solution)/shard_map/ppermute | solution.py:277
  27.9 1.5 %collective-permute-done.8.refs_3_.refs_7_ = bf16[272,128]{1,0:T(8,128)(2,1)S(1)} collective-permute-done((bf16[272,128]{1,0:T(8,128)(2,1)S(1)}, bf16[272,128]{1,0:T(8,128)(2,1)S(1)}, u32[]{:S(2)}, u32[]{:S(2)}) %collective-permute-start.8) | collective-permute-done | bytes 69664 | tf_op jit(solution)/shard_map/ppermute | solution.py:277
  29.4 1.4 %shard_map.95.base_ref = f32[65,1024]{1,0:T(8,128)S(1)} custom-call(s32[1,12]{1,0:T(1,128)S(1)} %copy-done.7, f32[65,1024]{1,0:T(8,128)S(1)} %get-tuple-element.28.base_ref, bf16[1,12,64,64]{3,2,1,0:T(8,128)(2,1)S(1)} %copy-done.5, bf16[8,64,64]{2,1,0:T(8,128)(2,1)S(1)} %copy-done.3, bf16[8,64,128]{2,1,0:T(8,128)(2,1)S(1)} %copy-done.2, ...), custom_call_target="tpu_custom_call" | custom-call | flops 68157440 | bytes 1105968 | tf_op jit(solution)/shard_map/pallas_call | solution.py:252
  30.9 0.8 %collective-permute-done.10.refs_2_ = bf16[384,128]{1,0:T(8,128)(2,1)S(1)} collective-permute-done((bf16[384,128]{1,0:T(8,128)(2,1)S(1)}, bf16[384,128]{1,0:T(8,128)(2,1)S(1)}, u32[]{:S(2)}, u32[]{:S(2)}) %collective-permute-start.10) | collective-permute-done | bytes 98336 | tf_op jit(solution)/shard_map/ppermute | solution.py:277
  31.6 0.8 %shard_map.96 = f32[65,1024]{1,0:T(8,128)} custom-call(f32[65,1024]{1,0:T(8,128)S(1)} %shard_map.95.base_ref, bf16[384,128]{1,0:T(8,128)(2,1)S(1)} %get-tuple-element.43.refs_0_, bf16[384,128]{1,0:T(8,128)(2,1)S(1)} %collective-permute-done.9.refs_1_, bf16[384,128]{1,0:T(8,128)(2,1)S(1)} %collective-permute-done.10.refs_2_, ...), custom_call_target="tpu_custom_call" | custom-call | flops 133120 | bytes 1204224 | tf_op jit(solution)/shard_map/pallas_call | solution.py:252
  (22 shorter events, 0.1 us)
Async XLA Ops:
  0.0 29.4 %copy-start.2 = (bf16[8,64,128]{2,1,0:T(8,128)(2,1)S(1)}, bf16[8,64,128]{2,1,0:T(8,128)(2,1)}, u32[]{:S(2)}) copy-start(bf16[8,64,128]{2,1,0:T(8,128)(2,1)} %basis_ref.1) | copy-start | bytes 393220
  0.0 29.4 %copy-start.3 = (bf16[8,64,64]{2,1,0:T(8,128)(2,1)S(1)}, bf16[8,64,64]{2,1,0:T(8,128)(2,1)}, u32[]{:S(2)}) copy-start(bf16[8,64,64]{2,1,0:T(8,128)(2,1)} %transfer_ref.1) | copy-start | bytes 196612
  0.0 29.4 %copy-start.5 = (bf16[1,12,64,64]{3,2,1,0:T(8,128)(2,1)S(1)}, bf16[1,12,64,64]{3,2,1,0:T(8,128)(2,1)}, u32[]{:S(2)}) copy-start(bf16[1,12,64,64]{3,2,1,0:T(8,128)(2,1)} %couplings_ref.1) | copy-start | bytes 294916
  3.4 26.0 %copy-start.7 = (s32[1,12]{1,0:T(1,128)S(1)}, s32[1,12]{1,0:T(1,128)}, u32[]{:S(2)}) copy-start(s32[1,12]{1,0:T(1,128)} %partner_ref.1) | copy-start | bytes 148
  3.5 7.6 %collective-permute-start = (bf16[784,128]{1,0:T(8,128)(2,1)}, bf16[784,128]{1,0:T(8,128)(2,1)S(1)}, u32[]{:S(2)}, u32[]{:S(2)}) collective-permute-start(bf16[784,128]{1,0:T(8,128)(2,1)} %get-tuple-element.31), channel_id=1, source_target_pairs={{0,1},{1,0},{2,3},{3,2},{4,5},{5,4},{6,7},{7,6},{8,9},{9,8},{10,11... | collective-permute-start | bytes 602120 | tf_op jit(solution)/shard_map/ppermute | solution.py:277
  4.0 12.9 %collective-permute-start.1 = (bf16[784,128]{1,0:T(8,128)(2,1)}, bf16[784,128]{1,0:T(8,128)(2,1)S(1)}, u32[]{:S(2)}, u32[]{:S(2)}) collective-permute-start(bf16[784,128]{1,0:T(8,128)(2,1)} %get-tuple-element.32), channel_id=1, source_target_pairs={{0,2},{1,3},{2,0},{3,1},{4,6},{5,7},{6,4},{7,5},{8,10},{9,11},{10,... | collective-permute-start | bytes 602120 | tf_op jit(solution)/shard_map/ppermute | solution.py:277
  6.6 10.3 %collective-permute-start.2 = (bf16[784,128]{1,0:T(8,128)(2,1)}, bf16[784,128]{1,0:T(8,128)(2,1)S(1)}, u32[]{:S(2)}, u32[]{:S(2)}) collective-permute-start(bf16[784,128]{1,0:T(8,128)(2,1)} %get-tuple-element.33), channel_id=1, source_target_pairs={{0,3},{1,2},{2,1},{3,0},{4,7},{5,6},{6,5},{7,4},{8,11},{9,10},{10,... | collective-permute-start | bytes 602120 | tf_op jit(solution)/shard_map/ppermute | solution.py:277
  6.6 11.3 %collective-permute-start.3 = (bf16[320,128]{1,0:T(8,128)(2,1)}, bf16[320,128]{1,0:T(8,128)(2,1)S(1)}, u32[]{:S(2)}, u32[]{:S(2)}) collective-permute-start(bf16[320,128]{1,0:T(8,128)(2,1)} %get-tuple-element.36), channel_id=1, source_target_pairs={{0,4},{1,5},{2,6},{3,7},{4,0},{5,1},{6,2},{7,3},{8,12},{9,13},{10,... | collective-permute-start | bytes 245768 | tf_op jit(solution)/shard_map/ppermute | solution.py:277
  8.4 9.7 %collective-permute-start.4 = (bf16[320,128]{1,0:T(8,128)(2,1)}, bf16[320,128]{1,0:T(8,128)(2,1)S(1)}, u32[]{:S(2)}, u32[]{:S(2)}) collective-permute-start(bf16[320,128]{1,0:T(8,128)(2,1)} %get-tuple-element.37), channel_id=1, source_target_pairs={{0,8},{1,9},{2,10},{3,11},{4,12},{5,13},{6,14},{7,15},{8,0},{9,1},... | collective-permute-start | bytes 245768 | tf_op jit(solution)/shard_map/ppermute | solution.py:277
  11.0 7.1 %collective-permute-start.5 = (bf16[320,128]{1,0:T(8,128)(2,1)}, bf16[320,128]{1,0:T(8,128)(2,1)S(1)}, u32[]{:S(2)}, u32[]{:S(2)}) collective-permute-start(bf16[320,128]{1,0:T(8,128)(2,1)} %get-tuple-element.38), channel_id=1, source_target_pairs={{0,12},{1,13},{2,14},{3,15},{4,8},{5,9},{6,10},{7,11},{8,4},{9,5},... | collective-permute-start | bytes 245768 | tf_op jit(solution)/shard_map/ppermute | solution.py:277
  11.0 1.6 %copy-start = (bf16[8,8,128,128]{3,2,1,0:T(8,128)(2,1)S(1)}, bf16[8,8,128,128]{3,2,1,0:T(8,128)(2,1)}, u32[]{:S(2)}) copy-start(bf16[8,8,128,128]{3,2,1,0:T(8,128)(2,1)} %local_ref.1) | copy-start | bytes 6291460
  12.6 0.9 %copy-start.1 = (bf16[65,1024]{1,0:T(8,128)(2,1)S(1)}, bf16[65,1024]{1,0:T(8,128)(2,1)}, u32[]{:S(2)}) copy-start(bf16[65,1024]{1,0:T(8,128)(2,1)} %probes_ref.1) | copy-start | bytes 399364
  13.5 0.9 %copy-start.4 = (bf16[784,128]{1,0:T(8,128)(2,1)S(1)}, bf16[784,128]{1,0:T(8,128)(2,1)}, u32[]{:S(2)}) copy-start(bf16[784,128]{1,0:T(8,128)(2,1)} %get-tuple-element.26.own_low) | copy-start | bytes 602116
  14.5 0.9 %copy-start.6 = (bf16[320,128]{1,0:T(8,128)(2,1)S(1)}, bf16[320,128]{1,0:T(8,128)(2,1)}, u32[]{:S(2)}) copy-start(bf16[320,128]{1,0:T(8,128)(2,1)} %get-tuple-element.27.own_high) | copy-start | bytes 245764
  19.1 6.1 %collective-permute-start.6 = (bf16[272,128]{1,0:T(8,128)(2,1)S(1)}, bf16[272,128]{1,0:T(8,128)(2,1)S(1)}, u32[]{:S(2)}, u32[]{:S(2)}) collective-permute-start(bf16[272,128]{1,0:T(8,128)(2,1)S(1)} %get-tuple-element.40), channel_id=1, source_target_pairs={{0,1},{1,0},{2,3},{3,2},{4,5},{5,4},{6,7},{7,6},{8,9},{9,8},{10,11... | collective-permute-start | bytes 208904 | tf_op jit(solution)/shard_map/ppermute | solution.py:277
  19.2 11.7 %collective-permute-start.9 = (bf16[384,128]{1,0:T(8,128)(2,1)S(1)}, bf16[384,128]{1,0:T(8,128)(2,1)S(1)}, u32[]{:S(2)}, u32[]{:S(2)}) collective-permute-start(bf16[384,128]{1,0:T(8,128)(2,1)S(1)} %get-tuple-element.44), channel_id=1, source_target_pairs={{0,4},{1,5},{2,6},{3,7},{4,0},{5,1},{6,2},{7,3},{8,12},{9,13},{10,... | collective-permute-start | bytes 294920 | tf_op jit(solution)/shard_map/ppermute | solution.py:277
  20.9 10.8 %collective-permute-start.10 = (bf16[384,128]{1,0:T(8,128)(2,1)S(1)}, bf16[384,128]{1,0:T(8,128)(2,1)S(1)}, u32[]{:S(2)}, u32[]{:S(2)}) collective-permute-start(bf16[384,128]{1,0:T(8,128)(2,1)S(1)} %get-tuple-element.45), channel_id=1, source_target_pairs={{0,8},{1,9},{2,10},{3,11},{4,12},{5,13},{6,14},{7,15},{8,0},{9,1},... | collective-permute-start | bytes 294920 | tf_op jit(solution)/shard_map/ppermute | solution.py:277
  23.5 8.2 %collective-permute-start.11 = (bf16[384,128]{1,0:T(8,128)(2,1)S(1)}, bf16[384,128]{1,0:T(8,128)(2,1)S(1)}, u32[]{:S(2)}, u32[]{:S(2)}) collective-permute-start(bf16[384,128]{1,0:T(8,128)(2,1)S(1)} %get-tuple-element.46), channel_id=1, source_target_pairs={{0,12},{1,13},{2,14},{3,15},{4,8},{5,9},{6,10},{7,11},{8,4},{9,5},... | collective-permute-start | bytes 294920 | tf_op jit(solution)/shard_map/ppermute | solution.py:277
  23.6 4.3 %collective-permute-start.7 = (bf16[272,128]{1,0:T(8,128)(2,1)S(1)}, bf16[272,128]{1,0:T(8,128)(2,1)S(1)}, u32[]{:S(2)}, u32[]{:S(2)}) collective-permute-start(bf16[272,128]{1,0:T(8,128)(2,1)S(1)} %get-tuple-element.41), channel_id=1, source_target_pairs={{0,2},{1,3},{2,0},{3,1},{4,6},{5,7},{6,4},{7,5},{8,10},{9,11},{10,... | collective-permute-start | bytes 208904 | tf_op jit(solution)/shard_map/ppermute | solution.py:277
  25.2 4.2 %collective-permute-start.8 = (bf16[272,128]{1,0:T(8,128)(2,1)S(1)}, bf16[272,128]{1,0:T(8,128)(2,1)S(1)}, u32[]{:S(2)}, u32[]{:S(2)}) collective-permute-start(bf16[272,128]{1,0:T(8,128)(2,1)S(1)} %get-tuple-element.42), channel_id=1, source_target_pairs={{0,3},{1,2},{2,1},{3,0},{4,7},{5,6},{6,5},{7,4},{8,11},{9,10},{10,... | collective-permute-start | bytes 208904 | tf_op jit(solution)/shard_map/ppermute | solution.py:277

commit v10 on v8

--- a/solution.py
+++ b/solution.py
@@ -156,27 +156,15 @@
         copy.wait()
 
 
-def sum_kernel(route, ways, *refs):
-    came, outs = refs[:ways], refs[ways : ways + route.fan]
-    meta, leaf_ref, total, tails, late = refs[ways + route.fan :]
-    leaves, half = route.leaves, route.half
-    lasts = []
-    for i in range(ways):
-        tile = came[i][route.meta : route.box, :].astype(F32)
-        meta[i : i + 1, :] = tile[:1].astype(I32)
-        lasts.append(tile[1:2])
-    numbers = pltpu.make_async_copy(meta, leaf_ref, late)
-    numbers.start()
-    total[...] = jnp.zeros(total.shape, F32)
-    tails[...] = jnp.zeros(tails.shape, F32)
-    numbers.wait()
+def sum_route(route, came, outs, base, leaf_ref, total, tails):
+    leaves, half, ways = route.leaves, route.half, len(came)
     for i in range(ways):
         if route.extra:
             tail = came[i][route.tails : route.meta, :].astype(F32)
         for k in range(route.fan):
             for slot in range(CAP):
                 at = k * CAP + slot
-                leaf = leaf_ref[i, at]
+                leaf = leaf_ref[base + i, at]
                 rows = pl.ds(pl.multiple_of(leaf * route.rows, TILE), route.rows)
                 total[k, rows, :] += came[i][at * route.rows : (at + 1) * route.rows, :].astype(F32)
                 if route.extra:
@@ -186,10 +174,33 @@
         outs[k][: route.dense_tails, :] = total[k, : route.dense_tails, :].astype(BF16)
         if route.extra:
             for i in range(ways):
-                tails[k, leaves + i : leaves + i + 1, :] = lasts[i]
+                last = came[i][route.meta : route.box, :].astype(F32)[1:2]
+                tails[k, leaves + i : leaves + i + 1, :] = last
                 start = route.dense_box + i * half
                 outs[k][start : start + half, :] = came[i][route.box :, :]
             outs[k][route.dense_tails : route.dense_box, :] = tails[k].astype(BF16)
+
+
+def sum_kernel(routes, devices, *refs):
+    by_low, by_high = routes
+    high, low = grid_of(devices)
+    ways = low + high
+    came, outs, scratch = refs[:ways], refs[ways : 2 * ways], refs[2 * ways :]
+    meta, leaf_ref, total_low, total_high, tails, late = scratch
+    for i, route in enumerate([by_low] * low + [by_high] * high):
+        meta[i : i + 1, :] = came[i][route.meta : route.box, :].astype(F32)[:1].astype(I32)
+    numbers = pltpu.make_async_copy(meta, leaf_ref, late)
+    numbers.start()
+    for ref in (total_low, total_high, tails):
+        ref[...] = jnp.zeros(ref.shape, F32)
+    numbers.wait()
+    sum_route(by_low, came[:low], outs[:high], 0, leaf_ref, total_low, None)
+    sum_route(by_high, came[low:], outs[high:], low, leaf_ref, total_high, tails)
+
+
+def keep_kernel(own_low, own_high, kept_low, kept_high):
+    kept_low[...] = own_low[...]
+    kept_high[...] = own_high[...]
 
 
 def local_kernel(probes_ref, local_ref, out_ref):
@@ -279,21 +290,6 @@
     def stacked(count, like_this):
         return pltpu.VMEM((count, *like_this.shape), like_this.dtype)
 
-    def summed(route, ways, came):
-        total = jax.ShapeDtypeStruct((route.fan, (leaves + 1) * route.rows, size), F32)
-        tails = jax.ShapeDtypeStruct((route.fan, max(TILE, route.dense_box - route.dense_tails), size), F32)
-        return call(
-            functools.partial(sum_kernel, route, ways),
-            [dense(route)] * route.fan,
-            ([VMEM] * ways, [VMEM] * route.fan),
-            came,
-            [pltpu.VMEM((ways, size), I32), pltpu.SMEM((ways, size), I32)]
-            + like(total, tails)
-            + [pltpu.SemaphoreType.DMA(())],
-            devices * CAP * route.rows * size,
-            4 * (total.size + tails.size),
-        )
-
     dest, leaf = near_dest.T, near_leaf.T
     sent = call(
         functools.partial(products_kernel, routes, devices),
@@ -315,26 +311,46 @@
     )
     came_low, came_high = list(sent[:low]), list(sent[low:])
     came_low[1] = relative(came_low[1], 1)
-    for k in range(high - 1, 1, -1):
-        came_high[k] = relative(came_high[k], k * low)
-    for k in range(low - 1, 1, -1):
-        came_low[k] = relative(came_low[k], k)
-    came_high[1] = relative(came_high[1], low)
-
-    probes_then, came_low[0] = lax.optimization_barrier((probes, came_low[0]))
+    for k in range(max(low, high) - 1, 0, -1):
+        if 1 < k < low:
+            came_low[k] = relative(came_low[k], k)
+        if k < high:
+            came_high[k] = relative(came_high[k], k * low)
+    came_low[0], came_high[0] = call(
+        keep_kernel,
+        (message(by_low), message(by_high)),
+        ([VMEM] * 2, (VMEM,) * 2),
+        (came_low[0], came_high[0]),
+        [],
+        0,
+        0,
+    )
+
+    total = lambda route: jax.ShapeDtypeStruct((route.fan, (leaves + 1) * route.rows, size), F32)
+    tails = jax.ShapeDtypeStruct((low, by_high.dense_box - by_high.dense_tails, size), F32)
+    sums = call(
+        functools.partial(sum_kernel, routes, devices),
+        [dense(by_low)] * high + [dense(by_high)] * low,
+        ([VMEM] * (low + high), [VMEM] * (low + high)),
+        (*came_low, *came_high),
+        [pltpu.VMEM((low + high, size), I32), pltpu.SMEM((low + high, size), I32)]
+        + like(total(by_low), total(by_high), tails)
+        + [pltpu.SemaphoreType.DMA(())],
+        devices * CAP * columns * size,
+        4 * (total(by_low).size + total(by_high).size + tails.size),
+    )
+    to_high, to_low = list(sums[:high]), list(sums[high:])
+    probes_then, to_low[0] = lax.optimization_barrier((probes, to_low[0]))
+    for k in range(max(low, high) - 1, 0, -1):
+        if k < high:
+            to_high[k] = relative(to_high[k], k * low)
+        if k < low:
+            to_low[k] = relative(to_low[k], k)
+
     base_shape = jax.ShapeDtypeStruct((columns, points), F32)
     base = call(
         local_kernel, base_shape, ([VMEM] * 2, VMEM), (probes_then, local_blocks), [], leaves * leaves * unit, 0
     )
-
-    to_high = list(summed(by_low, low, came_low))
-    for k in range(high - 1, 0, -1):
-        to_high[k] = relative(to_high[k], k * low)
-    came_high[0], to_high[0] = lax.optimization_barrier((came_high[0], to_high[0]))
-    to_low = list(summed(by_high, high, came_high))
-    for k in range(low - 1, 0, -1):
-        to_low[k] = relative(to_low[k], k)
-
     boxes = jax.ShapeDtypeStruct((devices, columns, rank), BF16)
     base = call(
         functools.partial(far_kernel, by_high, low),

time: 34 us -> 33.6 us (0.988)
  starting transfers between devices: 14.2 us -> 18.4 us
  waiting for transfers between devices: 8.51 us -> 4.64 us
  Pallas kernels: 9.22 us -> 8.48 us
    ppermute x12, starting transfers between devices: 14.2 us -> 18.4 us  [per_device(): lax.ppermute(x, 'leaf', [(i, i ^ way) for i in range(devices)])]
    ppermute x12, waiting for transfers between devices: 8.51 us -> 4.64 us  [per_device(): lax.ppermute(x, 'leaf', [(i, i ^ way) for i in range(devices)])]
    pallas_call x6, Pallas kernels: 9.22 us -> 8.48 us  [call(): pl.pallas_call(kernel, out_shape=out_shape, in_specs=specs[0], out_specs=...]
  transfers between devices with their start and end apart: 12 -> 12, of which waited for: 5 -> 5; matrix products, arithmetic and copies ran while one was open for 0% -> 0% of each run, Pallas kernels for 12% -> 9%
where the time goes in v10:
time: 33.6 us; the launch traced here: 33.5 us
  starting transfers between devices  18.4 us (55%)
  Pallas kernels  8.48 us (25%)
  waiting for transfers between devices  4.64 us (14%)
  local copies, waits for them, and re-layouts  1.84 us (5%)
    ppermute x12, starting transfers between devices, per_device(): lax.ppermute(x, 'leaf', [(i, i ^ way) for i in range(devices)])  18.4 us
    pallas_call x6, Pallas kernels, call(): pl.pallas_call(kernel, out_shape=out_shape, in_specs=specs[0], out_specs=...  8.48 us
    ppermute x12, waiting for transfers between devices, per_device(): lax.ppermute(x, 'leaf', [(i, i ^ way) for i in range(devices)])  4.64 us
    unnamed x16, local copies, waits for them, and re-layouts  1.84 us
  transfers between devices with their start and end apart: 12, of which 5 were waited for; matrix products, arithmetic and copies ran while one was open for 0% of the time, Pallas kernels for 9%

profile of v10, /device:TPU:0, one launch (start us, length us, event | category | flops | bytes accessed | tf_op | source)
XLA Modules:
  0.0 33.5 jit_solution(3361496705295412724)
XLA Ops:
  0.0 3.5 %shard_map.91 = (bf16[784,128]{1,0:T(8,128)(2,1)}, bf16[784,128]{1,0:T(8,128)(2,1)}, bf16[784,128]{1,0:T(8,128)(2,1)}, bf16[784,128]{1,0:T(8,128)(2,1)}, bf16[32...) custom-call(s32[4,8]{1,0:T(4,128)} %bitcast.2, ...), custom_call_target="tpu_custom_call" | custom-call | flops 68157440 | bytes 2509056 | tf_op jit(solution)/shard_map/pallas_call | solution.py:261
  3.5 0.0 copy-start.2
  3.6 0.5 %collective-permute-start = (bf16[784,128]{1,0:T(8,128)(2,1)}, bf16[784,128]{1,0:T(8,128)(2,1)S(1)}, u32[]{:S(2)}, u32[]{:S(2)}) collective-permute-start(bf16[784,128]{1,0:T(8,128)(2,1)} %get-tuple-element.28), channel_id=1, source_target_pairs={{0,1},{1,0},{2,3},{3,2},{4,5},{5,4},{6,7},{7,6},{8,9},{9,8},{10,11... | collective-permute-start | bytes 602120 | tf_op jit(solution)/shard_map/ppermute | solution.py:286
  4.1 2.6 %collective-permute-start.1 = (bf16[784,128]{1,0:T(8,128)(2,1)}, bf16[784,128]{1,0:T(8,128)(2,1)S(1)}, u32[]{:S(2)}, u32[]{:S(2)}) collective-permute-start(bf16[784,128]{1,0:T(8,128)(2,1)} %get-tuple-element.29), channel_id=1, source_target_pairs={{0,2},{1,3},{2,0},{3,1},{4,6},{5,7},{6,4},{7,5},{8,10},{9,11},{10,... | collective-permute-start | bytes 602120 | tf_op jit(solution)/shard_map/ppermute | solution.py:286
  6.7 0.1 collective-permute-start.2
  6.7 1.8 %collective-permute-start.3 = (bf16[320,128]{1,0:T(8,128)(2,1)}, bf16[320,128]{1,0:T(8,128)(2,1)S(1)}, u32[]{:S(2)}, u32[]{:S(2)}) collective-permute-start(bf16[320,128]{1,0:T(8,128)(2,1)} %get-tuple-element.32), channel_id=1, source_target_pairs={{0,4},{1,5},{2,6},{3,7},{4,0},{5,1},{6,2},{7,3},{8,12},{9,13},{10,... | collective-permute-start | bytes 245768 | tf_op jit(solution)/shard_map/ppermute | solution.py:286
  8.5 2.6 %collective-permute-start.4 = (bf16[320,128]{1,0:T(8,128)(2,1)}, bf16[320,128]{1,0:T(8,128)(2,1)S(1)}, u32[]{:S(2)}, u32[]{:S(2)}) collective-permute-start(bf16[320,128]{1,0:T(8,128)(2,1)} %get-tuple-element.33), channel_id=1, source_target_pairs={{0,8},{1,9},{2,10},{3,11},{4,12},{5,13},{6,14},{7,15},{8,0},{9,1},... | collective-permute-start | bytes 245768 | tf_op jit(solution)/shard_map/ppermute | solution.py:286
  11.1 0.6 %collective-permute-done.3.refs_5_ = bf16[320,128]{1,0:T(8,128)(2,1)S(1)} collective-permute-done((bf16[320,128]{1,0:T(8,128)(2,1)}, bf16[320,128]{1,0:T(8,128)(2,1)S(1)}, u32[]{:S(2)}, u32[]{:S(2)}) %collective-permute-start.3) | collective-permute-done | bytes 81952 | tf_op jit(solution)/shard_map/ppermute | solution.py:286
  11.7 4.8 %collective-permute-start.5 = (bf16[320,128]{1,0:T(8,128)(2,1)}, bf16[320,128]{1,0:T(8,128)(2,1)S(1)}, u32[]{:S(2)}, u32[]{:S(2)}) collective-permute-start(bf16[320,128]{1,0:T(8,128)(2,1)} %get-tuple-element.34), channel_id=1, source_target_pairs={{0,12},{1,13},{2,14},{3,15},{4,8},{5,9},{6,10},{7,11},{8,4},{9,5},... | collective-permute-start | bytes 245768 | tf_op jit(solution)/shard_map/ppermute | solution.py:286
  16.5 0.9 %copy-done.4 = bf16[784,128]{1,0:T(8,128)(2,1)S(1)} copy-done((bf16[784,128]{1,0:T(8,128)(2,1)S(1)}, bf16[784,128]{1,0:T(8,128)(2,1)}, u32[]{:S(2)}) %copy-start.4) | copy-done | bytes 200728
  17.5 0.9 %copy-done.6 = bf16[320,128]{1,0:T(8,128)(2,1)S(1)} copy-done((bf16[320,128]{1,0:T(8,128)(2,1)S(1)}, bf16[320,128]{1,0:T(8,128)(2,1)}, u32[]{:S(2)}) %copy-start.6) | copy-done | bytes 81944
  18.4 0.8 %collective-permute-done.5.refs_7_ = bf16[320,128]{1,0:T(8,128)(2,1)S(1)} collective-permute-done((bf16[320,128]{1,0:T(8,128)(2,1)}, bf16[320,128]{1,0:T(8,128)(2,1)S(1)}, u32[]{:S(2)}, u32[]{:S(2)}) %collective-permute-start.5) | collective-permute-done | bytes 81952 | tf_op jit(solution)/shard_map/ppermute | solution.py:286
  19.2 1.2 %shard_map.93 = (bf16[384,128]{1,0:T(8,128)(2,1)S(1)}, bf16[384,128]{1,0:T(8,128)(2,1)S(1)}, bf16[384,128]{1,0:T(8,128)(2,1)S(1)}, bf16[384,128]{1,0:T(8,128)(2,...) custom-call(bf16[784,128]{1,0:T(8,128)(2,1)S(1)} %get-tuple-element., ...), custom_call_target="tpu_custom_call" | custom-call | flops 532480 | bytes 1802240 | tf_op jit(solution)/shard_map/pallas_call | solution.py:261
  20.4 0.1 collective-permute-start.6
  20.5 0.8 %collective-permute-start.9 = (bf16[384,128]{1,0:T(8,128)(2,1)S(1)}, bf16[384,128]{1,0:T(8,128)(2,1)S(1)}, u32[]{:S(2)}, u32[]{:S(2)}) collective-permute-start(bf16[384,128]{1,0:T(8,128)(2,1)S(1)} %get-tuple-element.42), channel_id=1, source_target_pairs={{0,4},{1,5},{2,6},{3,7},{4,0},{5,1},{6,2},{7,3},{8,12},{9,13},{10,... | collective-permute-start | bytes 294920 | tf_op jit(solution)/shard_map/ppermute | solution.py:286
  21.3 3.5 %collective-permute-start.10 = (bf16[384,128]{1,0:T(8,128)(2,1)S(1)}, bf16[384,128]{1,0:T(8,128)(2,1)S(1)}, u32[]{:S(2)}, u32[]{:S(2)}) collective-permute-start(bf16[384,128]{1,0:T(8,128)(2,1)S(1)} %get-tuple-element.43), channel_id=1, source_target_pairs={{0,8},{1,9},{2,10},{3,11},{4,12},{5,13},{6,14},{7,15},{8,0},{9,1},... | collective-permute-start | bytes 294920 | tf_op jit(solution)/shard_map/ppermute | solution.py:286
  24.9 0.1 collective-permute-start.11
  25.0 1.5 %collective-permute-start.7 = (bf16[272,128]{1,0:T(8,128)(2,1)S(1)}, bf16[272,128]{1,0:T(8,128)(2,1)S(1)}, u32[]{:S(2)}, u32[]{:S(2)}) collective-permute-start(bf16[272,128]{1,0:T(8,128)(2,1)S(1)} %get-tuple-element.39), channel_id=1, source_target_pairs={{0,2},{1,3},{2,0},{3,1},{4,6},{5,7},{6,4},{7,5},{8,10},{9,11},{10,... | collective-permute-start | bytes 208904 | tf_op jit(solution)/shard_map/ppermute | solution.py:286
  26.5 1.5 %shard_map.94.base_ref = f32[65,1024]{1,0:T(8,128)S(1)} custom-call(bf16[65,1024]{1,0:T(8,128)(2,1)S(1)} %copy-done.1, bf16[8,8,128,128]{3,2,1,0:T(8,128)(2,1)S(1)} %copy-done), custom_call_target="tpu_custom_call" | custom-call | flops 136314880 | bytes 2496512 | tf_op jit(solution)/shard_map/pallas_call | solution.py:261
  28.0 1.3 %collective-permute-done.7.refs_2_.refs_6_ = bf16[272,128]{1,0:T(8,128)(2,1)S(1)} collective-permute-done((bf16[272,128]{1,0:T(8,128)(2,1)S(1)}, bf16[272,128]{1,0:T(8,128)(2,1)S(1)}, u32[]{:S(2)}, u32[]{:S(2)}) %collective-permute-start.7) | collective-permute-done | bytes 69664 | tf_op jit(solution)/shard_map/ppermute | solution.py:286
  29.3 1.5 %collective-permute-done.8.refs_3_.refs_7_ = bf16[272,128]{1,0:T(8,128)(2,1)S(1)} collective-permute-done((bf16[272,128]{1,0:T(8,128)(2,1)S(1)}, bf16[272,128]{1,0:T(8,128)(2,1)S(1)}, u32[]{:S(2)}, u32[]{:S(2)}) %collective-permute-start.8) | collective-permute-done | bytes 69664 | tf_op jit(solution)/shard_map/ppermute | solution.py:286
  30.8 1.4 %shard_map.95.base_ref = f32[65,1024]{1,0:T(8,128)S(1)} custom-call(s32[1,12]{1,0:T(1,128)S(1)} %copy-done.7, f32[65,1024]{1,0:T(8,128)S(1)} %shard_map.94.base_ref, bf16[1,12,64,64]{3,2,1,0:T(8,128)(2,1)S(1)} %copy-done.5, bf16[8,64,64]{2,1,0:T(8,128)(2,1)S(1)} %copy-done.2, bf16[8,64,128]{2,1,0:T(8,128)(2,1)S(1)} %copy-done.3, ...), custom_call_target="tpu_custom_call" | custom-call | flops 68157440 | bytes 1105968 | tf_op jit(solution)/shard_map/pallas_call | solution.py:261
  32.2 0.4 %collective-permute-done.10.refs_2_ = bf16[384,128]{1,0:T(8,128)(2,1)S(1)} collective-permute-done((bf16[384,128]{1,0:T(8,128)(2,1)S(1)}, bf16[384,128]{1,0:T(8,128)(2,1)S(1)}, u32[]{:S(2)}, u32[]{:S(2)}) %collective-permute-start.10) | collective-permute-done | bytes 98336 | tf_op jit(solution)/shard_map/ppermute | solution.py:286
  32.7 0.8 %shard_map.96 = f32[65,1024]{1,0:T(8,128)} custom-call(f32[65,1024]{1,0:T(8,128)S(1)} %shard_map.95.base_ref, bf16[384,128]{1,0:T(8,128)(2,1)S(1)} %get-tuple-element.41.refs_0_, bf16[384,128]{1,0:T(8,128)(2,1)S(1)} %collective-permute-done.9.refs_1_, bf16[384,128]{1,0:T(8,128)(2,1)S(1)} %collective-permute-done.10.refs_2_, ...), custom_call_target="tpu_custom_call" | custom-call | flops 133120 | bytes 1204224 | tf_op jit(solution)/shard_map/pallas_call | solution.py:261
  (22 shorter events, 0.1 us)
Async XLA Ops:
  0.0 26.4 %copy-start.1 = (bf16[65,1024]{1,0:T(8,128)(2,1)S(1)}, bf16[65,1024]{1,0:T(8,128)(2,1)}, u32[]{:S(2)}) copy-start(bf16[65,1024]{1,0:T(8,128)(2,1)} %probes_ref) | copy-start | bytes 399364
  0.0 26.4 %copy-start = (bf16[8,8,128,128]{3,2,1,0:T(8,128)(2,1)S(1)}, bf16[8,8,128,128]{3,2,1,0:T(8,128)(2,1)}, u32[]{:S(2)}) copy-start(bf16[8,8,128,128]{3,2,1,0:T(8,128)(2,1)} %local_ref.1) | copy-start | bytes 6291460
  3.5 27.2 %copy-start.2 = (bf16[8,64,64]{2,1,0:T(8,128)(2,1)S(1)}, bf16[8,64,64]{2,1,0:T(8,128)(2,1)}, u32[]{:S(2)}) copy-start(bf16[8,64,64]{2,1,0:T(8,128)(2,1)} %transfer_ref.1) | copy-start | bytes 196612
  3.6 27.2 %copy-start.3 = (bf16[8,64,128]{2,1,0:T(8,128)(2,1)S(1)}, bf16[8,64,128]{2,1,0:T(8,128)(2,1)}, u32[]{:S(2)}) copy-start(bf16[8,64,128]{2,1,0:T(8,128)(2,1)} %basis_ref.1) | copy-start | bytes 393220
  3.6 15.6 %collective-permute-start = (bf16[784,128]{1,0:T(8,128)(2,1)}, bf16[784,128]{1,0:T(8,128)(2,1)S(1)}, u32[]{:S(2)}, u32[]{:S(2)}) collective-permute-start(bf16[784,128]{1,0:T(8,128)(2,1)} %get-tuple-element.28), channel_id=1, source_target_pairs={{0,1},{1,0},{2,3},{3,2},{4,5},{5,4},{6,7},{7,6},{8,9},{9,8},{10,11... | collective-permute-start | bytes 602120 | tf_op jit(solution)/shard_map/ppermute | solution.py:286
  4.1 15.1 %collective-permute-start.1 = (bf16[784,128]{1,0:T(8,128)(2,1)}, bf16[784,128]{1,0:T(8,128)(2,1)S(1)}, u32[]{:S(2)}, u32[]{:S(2)}) collective-permute-start(bf16[784,128]{1,0:T(8,128)(2,1)} %get-tuple-element.29), channel_id=1, source_target_pairs={{0,2},{1,3},{2,0},{3,1},{4,6},{5,7},{6,4},{7,5},{8,10},{9,11},{10,... | collective-permute-start | bytes 602120 | tf_op jit(solution)/shard_map/ppermute | solution.py:286
  6.7 12.5 %collective-permute-start.2 = (bf16[784,128]{1,0:T(8,128)(2,1)}, bf16[784,128]{1,0:T(8,128)(2,1)S(1)}, u32[]{:S(2)}, u32[]{:S(2)}) collective-permute-start(bf16[784,128]{1,0:T(8,128)(2,1)} %get-tuple-element.30), channel_id=1, source_target_pairs={{0,3},{1,2},{2,1},{3,0},{4,7},{5,6},{6,5},{7,4},{8,11},{9,10},{10,... | collective-permute-start | bytes 602120 | tf_op jit(solution)/shard_map/ppermute | solution.py:286
  6.7 4.9 %collective-permute-start.3 = (bf16[320,128]{1,0:T(8,128)(2,1)}, bf16[320,128]{1,0:T(8,128)(2,1)S(1)}, u32[]{:S(2)}, u32[]{:S(2)}) collective-permute-start(bf16[320,128]{1,0:T(8,128)(2,1)} %get-tuple-element.32), channel_id=1, source_target_pairs={{0,4},{1,5},{2,6},{3,7},{4,0},{5,1},{6,2},{7,3},{8,12},{9,13},{10,... | collective-permute-start | bytes 245768 | tf_op jit(solution)/shard_map/ppermute | solution.py:286
  8.5 9.8 %collective-permute-start.4 = (bf16[320,128]{1,0:T(8,128)(2,1)}, bf16[320,128]{1,0:T(8,128)(2,1)S(1)}, u32[]{:S(2)}, u32[]{:S(2)}) collective-permute-start(bf16[320,128]{1,0:T(8,128)(2,1)} %get-tuple-element.33), channel_id=1, source_target_pairs={{0,8},{1,9},{2,10},{3,11},{4,12},{5,13},{6,14},{7,15},{8,0},{9,1},... | collective-permute-start | bytes 245768 | tf_op jit(solution)/shard_map/ppermute | solution.py:286
  11.7 7.5 %collective-permute-start.5 = (bf16[320,128]{1,0:T(8,128)(2,1)}, bf16[320,128]{1,0:T(8,128)(2,1)S(1)}, u32[]{:S(2)}, u32[]{:S(2)}) collective-permute-start(bf16[320,128]{1,0:T(8,128)(2,1)} %get-tuple-element.34), channel_id=1, source_target_pairs={{0,12},{1,13},{2,14},{3,15},{4,8},{5,9},{6,10},{7,11},{8,4},{9,5},... | collective-permute-start | bytes 245768 | tf_op jit(solution)/shard_map/ppermute | solution.py:286
  16.5 0.9 %copy-start.4 = (bf16[784,128]{1,0:T(8,128)(2,1)S(1)}, bf16[784,128]{1,0:T(8,128)(2,1)}, u32[]{:S(2)}) copy-start(bf16[784,128]{1,0:T(8,128)(2,1)} %get-tuple-element.25.own_low) | copy-start | bytes 602116
  17.4 0.9 %copy-start.6 = (bf16[320,128]{1,0:T(8,128)(2,1)S(1)}, bf16[320,128]{1,0:T(8,128)(2,1)}, u32[]{:S(2)}) copy-start(bf16[320,128]{1,0:T(8,128)(2,1)} %get-tuple-element.26.own_high) | copy-start | bytes 245764
  18.3 12.4 %copy-start.5 = (bf16[1,12,64,64]{3,2,1,0:T(8,128)(2,1)S(1)}, bf16[1,12,64,64]{3,2,1,0:T(8,128)(2,1)}, u32[]{:S(2)}) copy-start(bf16[1,12,64,64]{3,2,1,0:T(8,128)(2,1)} %couplings_ref.1) | copy-start | bytes 294916
  18.3 12.4 %copy-start.7 = (s32[1,12]{1,0:T(1,128)S(1)}, s32[1,12]{1,0:T(1,128)}, u32[]{:S(2)}) copy-start(s32[1,12]{1,0:T(1,128)} %partner_ref.1) | copy-start | bytes 148
  20.4 6.0 %collective-permute-start.6 = (bf16[272,128]{1,0:T(8,128)(2,1)S(1)}, bf16[272,128]{1,0:T(8,128)(2,1)S(1)}, u32[]{:S(2)}, u32[]{:S(2)}) collective-permute-start(bf16[272,128]{1,0:T(8,128)(2,1)S(1)} %get-tuple-element.38), channel_id=1, source_target_pairs={{0,1},{1,0},{2,3},{3,2},{4,5},{5,4},{6,7},{7,6},{8,9},{9,8},{10,11... | collective-permute-start | bytes 208904 | tf_op jit(solution)/shard_map/ppermute | solution.py:286
  20.5 11.7 %collective-permute-start.9 = (bf16[384,128]{1,0:T(8,128)(2,1)S(1)}, bf16[384,128]{1,0:T(8,128)(2,1)S(1)}, u32[]{:S(2)}, u32[]{:S(2)}) collective-permute-start(bf16[384,128]{1,0:T(8,128)(2,1)S(1)} %get-tuple-element.42), channel_id=1, source_target_pairs={{0,4},{1,5},{2,6},{3,7},{4,0},{5,1},{6,2},{7,3},{8,12},{9,13},{10,... | collective-permute-start | bytes 294920 | tf_op jit(solution)/shard_map/ppermute | solution.py:286
  21.3 11.3 %collective-permute-start.10 = (bf16[384,128]{1,0:T(8,128)(2,1)S(1)}, bf16[384,128]{1,0:T(8,128)(2,1)S(1)}, u32[]{:S(2)}, u32[]{:S(2)}) collective-permute-start(bf16[384,128]{1,0:T(8,128)(2,1)S(1)} %get-tuple-element.43), channel_id=1, source_target_pairs={{0,8},{1,9},{2,10},{3,11},{4,12},{5,13},{6,14},{7,15},{8,0},{9,1},... | collective-permute-start | bytes 294920 | tf_op jit(solution)/shard_map/ppermute | solution.py:286
  24.9 7.8 %collective-permute-start.11 = (bf16[384,128]{1,0:T(8,128)(2,1)S(1)}, bf16[384,128]{1,0:T(8,128)(2,1)S(1)}, u32[]{:S(2)}, u32[]{:S(2)}) collective-permute-start(bf16[384,128]{1,0:T(8,128)(2,1)S(1)} %get-tuple-element.44), channel_id=1, source_target_pairs={{0,12},{1,13},{2,14},{3,15},{4,8},{5,9},{6,10},{7,11},{8,4},{9,5},... | collective-permute-start | bytes 294920 | tf_op jit(solution)/shard_map/ppermute | solution.py:286
  25.0 4.3 %collective-permute-start.7 = (bf16[272,128]{1,0:T(8,128)(2,1)S(1)}, bf16[272,128]{1,0:T(8,128)(2,1)S(1)}, u32[]{:S(2)}, u32[]{:S(2)}) collective-permute-start(bf16[272,128]{1,0:T(8,128)(2,1)S(1)} %get-tuple-element.39), channel_id=1, source_target_pairs={{0,2},{1,3},{2,0},{3,1},{4,6},{5,7},{6,4},{7,5},{8,10},{9,11},{10,... | collective-permute-start | bytes 208904 | tf_op jit(solution)/shard_map/ppermute | solution.py:286
  26.4 4.3 %collective-permute-start.8 = (bf16[272,128]{1,0:T(8,128)(2,1)S(1)}, bf16[272,128]{1,0:T(8,128)(2,1)S(1)}, u32[]{:S(2)}, u32[]{:S(2)}) collective-permute-start(bf16[272,128]{1,0:T(8,128)(2,1)S(1)} %get-tuple-element.40), channel_id=1, source_target_pairs={{0,3},{1,2},{2,1},{3,0},{4,7},{5,6},{6,5},{7,4},{8,11},{9,10},{10,... | collective-permute-start | bytes 208904 | tf_op jit(solution)/shard_map/ppermute | solution.py:286

commit v11 on v8

v11 whole, which is shorter than its diff:
```python
import functools

import jax
import jax.numpy as jnp
from jax import lax
from jax.experimental import pallas as pl
from jax.experimental.pallas import tpu as pltpu
from jax.sharding import PartitionSpec as P

CAP = 4
TILE = 16
FIRST_FAR = 2
F32 = jnp.float32
BF16 = jnp.bfloat16
I32 = jnp.int32

ANY = pl.BlockSpec(memory_space=pl.ANY)
VMEM = pl.BlockSpec(memory_space=pltpu.VMEM)
SMEM = pl.BlockSpec(memory_space=pltpu.SMEM)


def dot_t(lhs, rhs):
    return lax.dot_general(lhs, rhs, (((1,), (1,)), ((), ())), preferred_element_type=F32)


def dot(lhs, rhs):
    return lax.dot_general(lhs, rhs, (((1,), (0,)), ((), ())), preferred_element_type=F32)


class Copies:
    def __init__(self, sems):
        self.sems, self.used = sems, 0

    def start(self, src, dst):
        copy = pltpu.make_async_copy(src, dst, self.sems.at[self.used])
        self.used += 1
        copy.start()
        return copy


def grid_of(devices):
    low = 1 << (devices.bit_length() // 2)
    return devices // low, low


def up(rows):
    return -(-rows // TILE) * TILE


class Message:
    def __init__(self, fan, box, main):
        self.fan, self.slots, self.main, self.half = fan, fan * CAP, main, main // 2
        self.tile = self.slots * main
        self.leaf, self.last = self.slots, self.slots + 1
        self.box = self.tile + up(self.slots + 2)
        self.depth = self.box + (self.half if box else 0)


class Dense:
    def __init__(self, leaves, boxes, main):
        self.leaves, self.main, self.half = leaves, main, main // 2
        self.tile = leaves * main
        self.box = self.tile + up(leaves + boxes)
        self.depth = self.box + boxes * self.half


class Plan:
    def __init__(self, devices, main, leaves):
        self.high, self.low = grid_of(devices)
        self.far = range(FIRST_FAR, self.high)
        self.plane = Message(len(self.far), False, main)
        self.near = Message(self.low, True, main)
        self.along = Dense(leaves, 0, main)
        self.within = Dense(leaves, self.high, main)
        self.parts = self.low + FIRST_FAR


def products_kernel(plan, *refs):
    dest_hbm, leaf_hbm, probes_hbm, basis_hbm, transfer_hbm, blocks_hbm = refs[:6]
    outs = refs[6:-11]
    (
        dest_ref, leaf_ref, probes_ref, basis_ref, transfer_ref, blocks_ref, send_ref, box_ref, tails, count, sems,
    ) = refs[-11:]
    low, plane, near = plan.low, plan.plane, plan.near
    me = lax.axis_index("leaf")
    main, half = plane.main, plane.half
    leaves, per_leaf, size = blocks_ref.shape[:3]
    columns, rank = probes_ref.shape[0], basis_ref.shape[1]
    copies = Copies(sems)
    early = [
        copies.start(probes_hbm, probes_ref),
        copies.start(basis_hbm, basis_ref),
        copies.start(transfer_hbm, transfer_ref),
        copies.start(dest_hbm, dest_ref),
        copies.start(leaf_hbm, leaf_ref),
    ]
    chunk = leaves // 2
    arrivals = [
        copies.start(blocks_hbm.at[pl.ds(j, chunk)], blocks_ref.at[pl.ds(j, chunk)])
        for j in range(0, leaves, chunk)
    ]

    @pl.loop(0, count.shape[0])
    def _(i):
        count[i] = 0

    kinds = [plane] * low + [near] * FIRST_FAR
    starts = [sum(kind.depth for kind in kinds[:i]) for i in range(len(kinds))]
    tails[...] = jnp.zeros(tails.shape, F32)
    for i, kind in enumerate(kinds):
        tails[i, kind.leaf : kind.leaf + 1, :] = jnp.full((1, size), leaves, F32)
    for copy in early:
        copy.wait()
    box = jnp.zeros((columns, rank), F32)
    for j in range(leaves):
        coef = dot_t(probes_ref[:, j * size : (j + 1) * size], basis_ref[j]).astype(BF16)
        box += dot_t(coef, transfer_ref[j])
    packed = jnp.concatenate([box[:half], box[half:main]], axis=1).astype(BF16)
    last = jnp.concatenate([box[main:], jnp.zeros_like(box[main:])], axis=1)

    lane = lax.broadcasted_iota(I32, (1, size), 1)
    for j in range(leaves):
        if j % chunk == 0:
            arrivals[j // chunk].wait()
        x = probes_ref[:, j * size : (j + 1) * size]
        for first in range(0, per_leaf, 4):
            many = min(4, per_leaf - first)
            rhs = blocks_ref[j, first : first + many].reshape(many * size, size)
            product = dot_t(x, rhs)
            for b in range(many):
                target = jnp.bitwise_xor(dest_ref[first + b, j], me)
                slot = count[target]
                count[target] = slot + 1
                to_high, to_low = target // low, target % low
                is_near = to_high < FIRST_FAR
                part = jnp.where(is_near, low + to_high, to_low)
                at = jnp.where(is_near, to_low, to_high - FIRST_FAR) * CAP + slot
                start = jnp.where(is_near, low * plane.depth + to_high * near.depth, to_low * plane.depth)
                rows = pl.ds(pl.multiple_of(start + at * main, TILE), main)
                block = product[:, b * size : (b + 1) * size]
                send_ref[rows, :] = block[:main].astype(BF16)
                tails[part, pl.ds(at, 1), :] = block[main:]
                row = pl.ds(jnp.where(is_near, near.leaf, plane.leaf), 1)
                number = leaf_ref[first + b, j].astype(F32)
                tails[part, row, :] = jnp.where(lane == at, number, tails[part, row, :])

    leaving = []
    for i, kind in enumerate(kinds):
        tails[i, kind.last : kind.last + 1, :] = last
        start = starts[i]
        send_ref[start + kind.tile : start + kind.box, :] = tails[i, : kind.box - kind.tile, :].astype(BF16)
        if kind.depth > kind.box:
            send_ref[start + kind.box : start + kind.depth, :] = packed
        leaving.append(copies.start(send_ref.at[pl.ds(start, kind.depth)], outs[i]))
    box_ref[:half, :] = packed
    box_ref[half:, :] = jnp.broadcast_to(last, (TILE, size)).astype(BF16)
    leaving.append(copies.start(box_ref, outs[-1]))
    for copy in leaving:
        copy.wait()


def read_leaves(kind, came, meta, leaf_ref, late, meanwhile):
    for i, ref in enumerate(came):
        tile = ref[kind.tile : kind.box, :].astype(F32)
        meta[i : i + 1, :] = tile[kind.leaf : kind.leaf + 1].astype(I32)
    numbers = pltpu.make_async_copy(meta, leaf_ref, late)
    numbers.start()
    for ref in meanwhile:
        ref[...] = jnp.zeros(ref.shape, F32)
    numbers.wait()


def add_slots(kind, came, leaf_ref, total, tails):
    main = kind.main
    for i, ref in enumerate(came):
        tile = ref[kind.tile : kind.box, :].astype(F32)
        for k in range(kind.fan):
            for at in range(k * CAP, (k + 1) * CAP):
                leaf = leaf_ref[i, at]
                rows = pl.ds(pl.multiple_of(leaf * main, TILE), main)
                total[k, rows, :] += ref[at * main : (at + 1) * main, :].astype(F32)
                tails[k, pl.ds(leaf, 1), :] += tile[at : at + 1]


def far_sum_kernel(plan, *refs):
    came, outs = refs[: plan.low], refs[plan.low : -5]
    meta, leaf_ref, total, tails, late = refs[-5:]
    to = plan.along
    read_leaves(plan.plane, came, meta, leaf_ref, late, (total, tails))
    add_slots(plan.plane, came, leaf_ref, total, tails)
    for k, out in enumerate(outs):
        out[: to.tile, :] = total[k, : to.tile, :].astype(BF16)
        out[to.tile : to.box, :] = tails[k, : to.box - to.tile, :].astype(BF16)


def near_sum_kernel(plan, *refs):
    came, boxes = refs[:FIRST_FAR], refs[FIRST_FAR : plan.high]
    outs = refs[plan.high : -5]
    meta, leaf_ref, total, tails, late = refs[-5:]
    kind, to = plan.near, plan.within
    read_leaves(kind, came, meta, leaf_ref, late, (total, tails))
    add_slots(kind, came, leaf_ref, total, tails)
    lasts = [ref[kind.tile : kind.box, :].astype(F32)[kind.last : kind.last + 1] for ref in came]
    lasts += [ref[kind.half :, :].astype(F32)[:1] for ref in boxes]
    packed = [ref[kind.box :, :] for ref in came] + [ref[: kind.half, :] for ref in boxes]
    for p, out in enumerate(outs):
        out[: to.tile, :] = total[p, : to.tile, :].astype(BF16)
        for k, last in enumerate(lasts):
            tails[p, to.leaves + k : to.leaves + k + 1, :] = last
        out[to.tile : to.box, :] = tails[p, : to.box - to.tile, :].astype(BF16)
        for k, rows in enumerate(packed):
            out[to.box + k * to.half : to.box + (k + 1) * to.half, :] = rows


def keep_kernel(*refs):
    for came, kept in zip(refs[: len(refs) // 2], refs[len(refs) // 2 :]):
        kept[...] = came[...]


def local_kernel(probes_ref, local_ref, out_ref):
    leaves, size = local_ref.shape[0], local_ref.shape[2]
    for i in range(leaves):
        total = dot_t(probes_ref[:, :size], local_ref[i, 0])
        for c in range(1, leaves):
            total += dot_t(probes_ref[:, c * size : (c + 1) * size], local_ref[i, c])
        out_ref[:, i * size : (i + 1) * size] = total


def far_kernel(plan, partner_ref, base_ref, couplings_ref, transfer_ref, basis_ref, *refs):
    high, low, came_as = plan.high, plan.low, plan.within
    came, out_ref, boxes = refs[:low], refs[low], refs[low + 1]
    columns = out_ref.shape[0]
    leaves, rank, size = basis_ref.shape
    me = lax.axis_index("leaf")
    for p in range(low):
        tile = came[p][came_as.tile : came_as.box, :].astype(F32)
        for k in range(high):
            start = came_as.box + k * came_as.half
            packed = came[p][start : start + came_as.half, :]
            last = tile[leaves + k : leaves + k + 1, :rank]
            boxes[k * low + p] = jnp.concatenate(
                [packed[:, :rank].astype(F32), packed[:, rank:].astype(F32), last], axis=0
            ).astype(BF16)
    far = jnp.zeros((columns, rank), F32)
    for f in range(couplings_ref.shape[1]):
        source = jnp.bitwise_xor(partner_ref[0, f], me)
        far += dot_t(boxes[source], couplings_ref[0, f])
    far = far.astype(BF16)
    down = [dot(far, transfer_ref[j]).astype(BF16) for j in range(leaves)]
    for j in range(leaves):
        cols = slice(j * size, (j + 1) * size)
        out_ref[:, cols] = base_ref[:, cols] + dot(down[j], basis_ref[j])


def last_kernel(leaves, main, base_ref, *refs):
    came, out_ref = refs[:-1], refs[-1]
    size = base_ref.shape[1] // leaves
    tile = leaves * main
    tails = sum(ref[tile : tile + TILE, :].astype(F32) for ref in came)
    for j in range(leaves):
        cols = slice(j * size, (j + 1) * size)
        rows = slice(j * main, (j + 1) * main)
        out_ref[:main, cols] = base_ref[:main, cols] + sum(ref[rows, :].astype(F32) for ref in came)
        out_ref[main:, cols] = base_ref[main:, cols] + tails[j : j + 1]


def call(kernel, out_shape, specs, operands, scratch, flops, room=None):
    outs = jax.tree.leaves(out_shape)
    nbytes = sum(a.size * a.dtype.itemsize for a in (*operands, *outs))
    limit = None if room is None else nbytes + room + 2**21
    return pl.pallas_call(
        kernel,
        out_shape=out_shape,
        in_specs=specs[0],
        out_specs=specs[1],
        scratch_shapes=scratch,
        compiler_params=pltpu.CompilerParams(vmem_limit_bytes=limit),
        cost_estimate=pl.CostEstimate(flops=flops, bytes_accessed=nbytes, transcendentals=0),
    )(*operands)


def per_device(
    probes, basis, transfer, local_blocks, remote_blocks, near_dest, near_leaf, couplings, far_list
):
    columns, points = probes.shape
    leaves, rank, size = basis.shape
    devices = lax.axis_size("leaf")
    main = columns // TILE * TILE
    plan = Plan(devices, main, leaves)
    high, low = plan.high, plan.low
    blocks = remote_blocks.shape[0] * remote_blocks.shape[1]
    unit = 2 * columns * size * size
    array = lambda rows, dtype=BF16: jax.ShapeDtypeStruct((*rows, size), dtype)
    like = lambda *arrays: [pltpu.VMEM(a.shape, a.dtype) for a in arrays]
    numbers = lambda *arrays: [pltpu.SMEM(a.shape, a.dtype) for a in arrays]
    sems = lambda count: [pltpu.SemaphoreType.DMA((count,))]
    relative = lambda x, way: lax.ppermute(x, "leaf", [(i, i ^ way) for i in range(devices)])

    dest, leaf = near_dest.T, near_leaf.T
    sizes = [plan.plane.depth] * low + [plan.near.depth] * FIRST_FAR + [main // 2 + TILE]
    sent = call(
        functools.partial(products_kernel, plan),
        [array((rows,)) for rows in sizes],
        ([ANY] * 6, [ANY] * len(sizes)),
        (dest, leaf, probes, basis, transfer, remote_blocks),
        numbers(dest, leaf)
        + like(probes, basis, transfer, remote_blocks)
        + like(array((sum(sizes[:-1]),)), array(sizes[-1:]))
        + [
            pltpu.VMEM((plan.parts, max(k.box - k.tile for k in (plan.plane, plan.near)), size), F32),
            pltpu.SMEM((devices,), I32),
        ]
        + sems(7 + len(sizes)),
        blocks * unit,
    )
    plane, near, box = list(sent[:low]), list(sent[low:-1]), sent[-1]
    for p in range(1, low):
        plane[p] = relative(plane[p], p)
    for k in range(1, FIRST_FAR):
        near[k] = relative(near[k], k * low)
    boxes = [relative(box, k * low) for k in plan.far]
    plane[0], near[0] = call(
        keep_kernel, (array(sizes[:1]), array(sizes[low : low + 1])), ([VMEM] * 2, (VMEM,) * 2), (plane[0], near[0]), [], 0, 0
    )

    def summed(kernel, kind, dense, came, others):
        count = kind.fan
        total = array((count, (leaves + 1) * main), F32)
        tails = array((count, max(TILE, dense.box - dense.tile)), F32)
        return call(
            functools.partial(kernel, plan),
            [array((dense.depth,))] * count,
            ([VMEM] * (len(came) + len(others)), [VMEM] * count),
            (*came, *others),
            [pltpu.VMEM((len(came), size), I32), pltpu.SMEM((len(came), size), I32)]
            + like(total, tails)
            + [pltpu.SemaphoreType.DMA(())],
            len(came) * kind.slots * columns * size,
            4 * (total.size + tails.size),
        )

    along = summed(far_sum_kernel, plan.plane, plan.along, plane, [])
    near[0], *along = lax.optimization_barrier((near[0], *along))
    along = [relative(x, k * low) for k, x in zip(plan.far, along)]
    within = list(summed(near_sum_kernel, plan.near, plan.within, near, boxes))
    probes_then, within[0] = lax.optimization_barrier((probes, within[0]))
    for p in range(1, low):
        within[p] = relative(within[p], p)

    base_shape = jax.ShapeDtypeStruct((columns, points), F32)
    base = call(
        local_kernel, base_shape, ([VMEM] * 2, VMEM), (probes_then, local_blocks), [], leaves * leaves * unit, 0
    )
    every = jax.ShapeDtypeStruct((devices, columns, rank), BF16)
    base = call(
        functools.partial(far_kernel, plan),
        base_shape,
        ([SMEM] + [VMEM] * (4 + low), VMEM),
        (far_list, base, couplings, transfer, basis, *within),
        like(every),
        4 * leaves * unit,
        4 * every.size,
    )
    came = (*within, *along)
    return call(
        functools.partial(last_kernel, leaves, main),
        base_shape,
        ([VMEM] * (1 + len(came)), VMEM),
        (base, *came),
        [],
        devices * columns * size,
        0,
    )


def solution(mesh):
    placed = (
        P(None, ("grp", "leaf")),
        P(("grp", "leaf"), None, None),
        P(("grp", "leaf"), None, None),
        P(("grp", "leaf"), None, None, None),
        P(("grp", "leaf"), None, None, None),
        P(("grp", "leaf"), None),
        P(("grp", "leaf"), None),
        P(("grp", "leaf"), None, None, None),
        P(("grp", "leaf"), None),
    )
    return jax.shard_map(
        per_device, mesh=mesh, in_specs=placed, out_specs=P(None, ("grp", "leaf")), check_vma=False
    )
```

time: 34 us -> 33.4 us (0.982)
  the two profiles are of different devices: /device:TPU:0 before, /device:TPU:15 now
where the time goes in v11:
time: 33.4 us; the launch traced here: 33.3 us
  starting transfers between devices  11.2 us (34%)
  waiting for transfers between devices  10.9 us (33%)
  Pallas kernels  9.1 us (27%)
  local copies, waits for them, and re-layouts  1.89 us (6%)
    ppermute x11, starting transfers between devices, per_device(): lax.ppermute(x, 'leaf', [(i, i ^ way) for i in range(devices)])  11.2 us
    ppermute x11, waiting for transfers between devices, per_device(): lax.ppermute(x, 'leaf', [(i, i ^ way) for i in range(devices)])  10.9 us
    pallas_call x7, Pallas kernels, call(): pl.pallas_call(kernel, out_shape=out_shape, in_specs=specs[0], out_specs=...  9.1 us
    unnamed x16, local copies, waits for them, and re-layouts  1.89 us
  transfers between devices with their start and end apart: 11, of which 4 were waited for; matrix products, arithmetic and copies ran while one was open for 0% of the time, Pallas kernels for 11%

profile of v11, /device:TPU:15, one launch (start us, length us, event | category | flops | bytes accessed | tf_op | source)
XLA Modules:
  0.0 33.3 jit_solution(3974901459030092262)
XLA Ops:
  0.0 3.5 %shard_map.91 = (bf16[528,128]{1,0:T(8,128)(2,1)}, bf16[528,128]{1,0:T(8,128)(2,1)}, bf16[528,128]{1,0:T(8,128)(2,1)}, bf16[528,128]{1,0:T(8,128)(2,1)}, bf16[10...) custom-call(s32[4,8]{1,0:T(4,128)} %bitcast.2, s32[4,8]{1,0:T(4,128)} %bitcast.3, ...), custom_call_target="tpu_custom_call" | custom-call | flops 68157440 | bytes 2488576 | tf_op jit(solution)/shard_map/pallas_call | solution.py:271
  3.5 0.0 copy-start.2
  3.6 0.2 collective-permute-start.3
  3.8 0.9 %collective-permute-start = (bf16[528,128]{1,0:T(8,128)(2,1)}, bf16[528,128]{1,0:T(8,128)(2,1)S(1)}, u32[]{:S(2)}, u32[]{:S(2)}) collective-permute-start(bf16[528,128]{1,0:T(8,128)(2,1)} %get-tuple-element.29), channel_id=1, source_target_pairs={{0,1},{1,0},{2,3},{3,2},{4,5},{5,4},{6,7},{7,6},{8,9},{9,8},{10,11... | collective-permute-start | bytes 405512 | tf_op jit(solution)/shard_map/ppermute | solution.py:297
  4.8 0.2 collective-permute-start.1
  5.0 1.4 %collective-permute-start.2 = (bf16[528,128]{1,0:T(8,128)(2,1)}, bf16[528,128]{1,0:T(8,128)(2,1)S(1)}, u32[]{:S(2)}, u32[]{:S(2)}) collective-permute-start(bf16[528,128]{1,0:T(8,128)(2,1)} %get-tuple-element.31), channel_id=1, source_target_pairs={{0,3},{1,2},{2,1},{3,0},{4,7},{5,6},{6,5},{7,4},{8,11},{9,10},{10,... | collective-permute-start | bytes 405512 | tf_op jit(solution)/shard_map/ppermute | solution.py:297
  6.4 2.4 %collective-permute-start.5 = (bf16[48,128]{1,0:T(8,128)(2,1)}, bf16[48,128]{1,0:T(8,128)(2,1)S(1)}, u32[]{:S(2)}, u32[]{:S(2)}) collective-permute-start(bf16[48,128]{1,0:T(8,128)(2,1)} %get-tuple-element.36), channel_id=1, source_target_pairs={{0,12},{1,13},{2,14},{3,15},{4,8},{5,9},{6,10},{7,11},{8,4},{9,5},... | collective-permute-start | bytes 36872 | tf_op jit(solution)/shard_map/ppermute | solution.py:297
  8.8 0.9 %collective-permute-start.4 = (bf16[48,128]{1,0:T(8,128)(2,1)}, bf16[48,128]{1,0:T(8,128)(2,1)S(1)}, u32[]{:S(2)}, u32[]{:S(2)}) collective-permute-start(bf16[48,128]{1,0:T(8,128)(2,1)} %get-tuple-element.36), channel_id=1, source_target_pairs={{0,8},{1,9},{2,10},{3,11},{4,12},{5,13},{6,14},{7,15},{8,0},{9,1},... | collective-permute-start | bytes 36872 | tf_op jit(solution)/shard_map/ppermute | solution.py:297
  9.8 1.0 %copy-done.4 = bf16[1088,128]{1,0:T(8,128)(2,1)S(1)} copy-done((bf16[1088,128]{1,0:T(8,128)(2,1)S(1)}, bf16[1088,128]{1,0:T(8,128)(2,1)}, u32[]{:S(2)}) %copy-start.4) | copy-done | bytes 278552
  10.7 0.9 %copy-done.6 = bf16[528,128]{1,0:T(8,128)(2,1)S(1)} copy-done((bf16[528,128]{1,0:T(8,128)(2,1)S(1)}, bf16[528,128]{1,0:T(8,128)(2,1)}, u32[]{:S(2)}) %copy-start.6) | copy-done | bytes 135192
  11.7 1.5 %collective-permute-done.2.refs_3_ = bf16[528,128]{1,0:T(8,128)(2,1)S(1)} collective-permute-done((bf16[528,128]{1,0:T(8,128)(2,1)}, bf16[528,128]{1,0:T(8,128)(2,1)S(1)}, u32[]{:S(2)}, u32[]{:S(2)}) %collective-permute-start.2) | collective-permute-done | bytes 135200 | tf_op jit(solution)/shard_map/ppermute | solution.py:297
  13.2 0.9 %shard_map.93 = (bf16[528,128]{1,0:T(8,128)(2,1)S(1)}, bf16[528,128]{1,0:T(8,128)(2,1)S(1)}) custom-call(bf16[528,128]{1,0:T(8,128)(2,1)S(1)} %get-tuple-element.28.refs_0_, bf16[528,128]{1,0:T(8,128)(2,1)S(1)} %collective-permute-done.refs_1_, bf16[528,128]{1,0:T(8,128)(2,1)S(1)} %collective-permute-done.1.refs_2_, ...), custom_call_target="tpu_custom_call" | custom-call | flops 266240 | bytes 811008 | tf_op jit(solution)/shard_map/pallas_call | solution.py:271
  14.1 0.9 %shard_map.94 = (bf16[656,128]{1,0:T(8,128)(2,1)S(1)}, bf16[656,128]{1,0:T(8,128)(2,1)S(1)}, bf16[656,128]{1,0:T(8,128)(2,1)S(1)}, bf16[656,128]{1,0:T(8,128)(2,1)S(1)}) custom-call(bf16[1088,128]{1,0:T(8,128)(2,1)S(1)} %get-tuple-element.34.refs_0_, bf16[1088,128]{1,0:T(8,128)(2,1)S(1)} %collective-permute-done.3.refs_1_, ...), custom_call_target="tpu_custom_call" | custom-call | flops 266240 | bytes 1253376 | tf_op jit(solution)/shard_map/pallas_call | solution.py:271
  15.0 0.5 %collective-permute-start.6 = (bf16[656,128]{1,0:T(8,128)(2,1)S(1)}, bf16[656,128]{1,0:T(8,128)(2,1)S(1)}, u32[]{:S(2)}, u32[]{:S(2)}) collective-permute-start(bf16[656,128]{1,0:T(8,128)(2,1)S(1)} %get-tuple-element.40), channel_id=1, source_target_pairs={{0,1},{1,0},{2,3},{3,2},{4,5},{5,4},{6,7},{7,6},{8,9},{9,8},{10,11... | collective-permute-start | bytes 503816 | tf_op jit(solution)/shard_map/ppermute | solution.py:297
  15.4 0.2 collective-permute-start.7
  15.7 1.6 %collective-permute-start.8 = (bf16[656,128]{1,0:T(8,128)(2,1)S(1)}, bf16[656,128]{1,0:T(8,128)(2,1)S(1)}, u32[]{:S(2)}, u32[]{:S(2)}) collective-permute-start(bf16[656,128]{1,0:T(8,128)(2,1)S(1)} %get-tuple-element.42), channel_id=1, source_target_pairs={{0,3},{1,2},{2,1},{3,0},{4,7},{5,6},{6,5},{7,4},{8,11},{9,10},{10,... | collective-permute-start | bytes 503816 | tf_op jit(solution)/shard_map/ppermute | solution.py:297
  17.2 2.3 %collective-permute-start.9 = (bf16[528,128]{1,0:T(8,128)(2,1)S(1)}, bf16[528,128]{1,0:T(8,128)(2,1)S(1)}, u32[]{:S(2)}, u32[]{:S(2)}) collective-permute-start(bf16[528,128]{1,0:T(8,128)(2,1)S(1)} %get-tuple-element.43), channel_id=1, source_target_pairs={{0,8},{1,9},{2,10},{3,11},{4,12},{5,13},{6,14},{7,15},{8,0},{9,1},... | collective-permute-start | bytes 405512 | tf_op jit(solution)/shard_map/ppermute | solution.py:297
  19.5 0.5 %collective-permute-start.10 = (bf16[528,128]{1,0:T(8,128)(2,1)S(1)}, bf16[528,128]{1,0:T(8,128)(2,1)S(1)}, u32[]{:S(2)}, u32[]{:S(2)}) collective-permute-start(bf16[528,128]{1,0:T(8,128)(2,1)S(1)} %get-tuple-element.44), channel_id=1, source_target_pairs={{0,12},{1,13},{2,14},{3,15},{4,8},{5,9},{6,10},{7,11},{8,4},{9,5},... | collective-permute-start | bytes 405512 | tf_op jit(solution)/shard_map/ppermute | solution.py:297
  20.0 1.5 %shard_map.95.base_ref = f32[65,1024]{1,0:T(8,128)S(1)} custom-call(bf16[65,1024]{1,0:T(8,128)(2,1)S(1)} %copy-done.1, bf16[8,8,128,128]{3,2,1,0:T(8,128)(2,1)S(1)} %copy-done), custom_call_target="tpu_custom_call" | custom-call | flops 136314880 | bytes 2496512 | tf_op jit(solution)/shard_map/pallas_call | solution.py:271
  21.5 3.5 %collective-permute-done.8.refs_3_ = bf16[656,128]{1,0:T(8,128)(2,1)S(1)} collective-permute-done((bf16[656,128]{1,0:T(8,128)(2,1)S(1)}, bf16[656,128]{1,0:T(8,128)(2,1)S(1)}, u32[]{:S(2)}, u32[]{:S(2)}) %collective-permute-start.8) | collective-permute-done | bytes 167968 | tf_op jit(solution)/shard_map/ppermute | solution.py:297
  25.1 1.4 %shard_map.96.base_ref = f32[65,1024]{1,0:T(8,128)S(1)} custom-call(s32[1,12]{1,0:T(1,128)S(1)} %copy-done.7, f32[65,1024]{1,0:T(8,128)S(1)} %shard_map.95.base_ref, bf16[1,12,64,64]{3,2,1,0:T(8,128)(2,1)S(1)} %copy-done.5, bf16[8,64,64]{2,1,0:T(8,128)(2,1)S(1)} %copy-done.2, bf16[8,64,128]{2,1,0:T(8,128)(2,1)S(1)} %copy-done.3, ...), custom_call_target="tpu_custom_call" | custom-call | flops 68157440 | bytes 1499184 | tf_op jit(solution)/shard_map/pallas_call | solution.py:271
  26.5 1.8 %collective-permute-done.9.refs_4_ = bf16[528,128]{1,0:T(8,128)(2,1)S(1)} collective-permute-done((bf16[528,128]{1,0:T(8,128)(2,1)S(1)}, bf16[528,128]{1,0:T(8,128)(2,1)S(1)}, u32[]{:S(2)}, u32[]{:S(2)}) %collective-permute-start.9) | collective-permute-done | bytes 135200 | tf_op jit(solution)/shard_map/ppermute | solution.py:297
  28.3 4.1 %collective-permute-done.10.refs_5_ = bf16[528,128]{1,0:T(8,128)(2,1)S(1)} collective-permute-done((bf16[528,128]{1,0:T(8,128)(2,1)S(1)}, bf16[528,128]{1,0:T(8,128)(2,1)S(1)}, u32[]{:S(2)}, u32[]{:S(2)}) %collective-permute-start.10) | collective-permute-done | bytes 135200 | tf_op jit(solution)/shard_map/ppermute | solution.py:297
  32.4 0.8 %shard_map.97 = f32[65,1024]{1,0:T(8,128)} custom-call(f32[65,1024]{1,0:T(8,128)S(1)} %shard_map.96.base_ref, bf16[656,128]{1,0:T(8,128)(2,1)S(1)} %get-tuple-element.39.refs_0_, bf16[656,128]{1,0:T(8,128)(2,1)S(1)} %collective-permute-done.6.refs_1_, bf16[656,128]{1,0:T(8,128)(2,1)S(1)} %collective-permute-done.7.refs_2_, ...), custom_call_target="tpu_custom_call" | custom-call | flops 133120 | bytes 1474560 | tf_op jit(solution)/shard_map/pallas_call | solution.py:271
  (21 shorter events, 0.1 us)
Async XLA Ops:
  0.0 20.0 %copy-start.1 = (bf16[65,1024]{1,0:T(8,128)(2,1)S(1)}, bf16[65,1024]{1,0:T(8,128)(2,1)}, u32[]{:S(2)}) copy-start(bf16[65,1024]{1,0:T(8,128)(2,1)} %probes_ref) | copy-start | bytes 399364
  0.0 20.0 %copy-start = (bf16[8,8,128,128]{3,2,1,0:T(8,128)(2,1)S(1)}, bf16[8,8,128,128]{3,2,1,0:T(8,128)(2,1)}, u32[]{:S(2)}) copy-start(bf16[8,8,128,128]{3,2,1,0:T(8,128)(2,1)} %local_ref.1) | copy-start | bytes 6291460
  3.5 21.5 %copy-start.2 = (bf16[8,64,64]{2,1,0:T(8,128)(2,1)S(1)}, bf16[8,64,64]{2,1,0:T(8,128)(2,1)}, u32[]{:S(2)}) copy-start(bf16[8,64,64]{2,1,0:T(8,128)(2,1)} %transfer_ref.1) | copy-start | bytes 196612
  3.6 21.5 %copy-start.3 = (bf16[8,64,128]{2,1,0:T(8,128)(2,1)S(1)}, bf16[8,64,128]{2,1,0:T(8,128)(2,1)}, u32[]{:S(2)}) copy-start(bf16[8,64,128]{2,1,0:T(8,128)(2,1)} %basis_ref.1) | copy-start | bytes 393220
  3.6 10.5 %collective-permute-start.3 = (bf16[1088,128]{1,0:T(8,128)(2,1)}, bf16[1088,128]{1,0:T(8,128)(2,1)S(1)}, u32[]{:S(2)}, u32[]{:S(2)}) collective-permute-start(bf16[1088,128]{1,0:T(8,128)(2,1)} %get-tuple-element.35), channel_id=1, source_target_pairs={{0,4},{1,5},{2,6},{3,7},{4,0},{5,1},{6,2},{7,3},{8,12},{9,13},{10,... | collective-permute-start | bytes 835592 | tf_op jit(solution)/shard_map/ppermute | solution.py:297
  3.8 5.0 %collective-permute-start = (bf16[528,128]{1,0:T(8,128)(2,1)}, bf16[528,128]{1,0:T(8,128)(2,1)S(1)}, u32[]{:S(2)}, u32[]{:S(2)}) collective-permute-start(bf16[528,128]{1,0:T(8,128)(2,1)} %get-tuple-element.29), channel_id=1, source_target_pairs={{0,1},{1,0},{2,3},{3,2},{4,5},{5,4},{6,7},{7,6},{8,9},{9,8},{10,11... | collective-permute-start | bytes 405512 | tf_op jit(solution)/shard_map/ppermute | solution.py:297
  4.8 6.9 %collective-permute-start.1 = (bf16[528,128]{1,0:T(8,128)(2,1)}, bf16[528,128]{1,0:T(8,128)(2,1)S(1)}, u32[]{:S(2)}, u32[]{:S(2)}) collective-permute-start(bf16[528,128]{1,0:T(8,128)(2,1)} %get-tuple-element.30), channel_id=1, source_target_pairs={{0,2},{1,3},{2,0},{3,1},{4,6},{5,7},{6,4},{7,5},{8,10},{9,11},{10,... | collective-permute-start | bytes 405512 | tf_op jit(solution)/shard_map/ppermute | solution.py:297
  5.0 8.2 %collective-permute-start.2 = (bf16[528,128]{1,0:T(8,128)(2,1)}, bf16[528,128]{1,0:T(8,128)(2,1)S(1)}, u32[]{:S(2)}, u32[]{:S(2)}) collective-permute-start(bf16[528,128]{1,0:T(8,128)(2,1)} %get-tuple-element.31), channel_id=1, source_target_pairs={{0,3},{1,2},{2,1},{3,0},{4,7},{5,6},{6,5},{7,4},{8,11},{9,10},{10,... | collective-permute-start | bytes 405512 | tf_op jit(solution)/shard_map/ppermute | solution.py:297
  6.4 7.7 %collective-permute-start.5 = (bf16[48,128]{1,0:T(8,128)(2,1)}, bf16[48,128]{1,0:T(8,128)(2,1)S(1)}, u32[]{:S(2)}, u32[]{:S(2)}) collective-permute-start(bf16[48,128]{1,0:T(8,128)(2,1)} %get-tuple-element.36), channel_id=1, source_target_pairs={{0,12},{1,13},{2,14},{3,15},{4,8},{5,9},{6,10},{7,11},{8,4},{9,5},... | collective-permute-start | bytes 36872 | tf_op jit(solution)/shard_map/ppermute | solution.py:297
  8.8 5.2 %collective-permute-start.4 = (bf16[48,128]{1,0:T(8,128)(2,1)}, bf16[48,128]{1,0:T(8,128)(2,1)S(1)}, u32[]{:S(2)}, u32[]{:S(2)}) collective-permute-start(bf16[48,128]{1,0:T(8,128)(2,1)} %get-tuple-element.36), channel_id=1, source_target_pairs={{0,8},{1,9},{2,10},{3,11},{4,12},{5,13},{6,14},{7,15},{8,0},{9,1},... | collective-permute-start | bytes 36872 | tf_op jit(solution)/shard_map/ppermute | solution.py:297
  9.8 1.0 %copy-start.4 = (bf16[1088,128]{1,0:T(8,128)(2,1)S(1)}, bf16[1088,128]{1,0:T(8,128)(2,1)}, u32[]{:S(2)}) copy-start(bf16[1088,128]{1,0:T(8,128)(2,1)} %get-tuple-element.26.refs_1_) | copy-start | bytes 835588
  10.7 0.9 %copy-start.6 = (bf16[528,128]{1,0:T(8,128)(2,1)S(1)}, bf16[528,128]{1,0:T(8,128)(2,1)}, u32[]{:S(2)}) copy-start(bf16[528,128]{1,0:T(8,128)(2,1)} %get-tuple-element.25.refs_0_) | copy-start | bytes 405508
  11.6 13.4 %copy-start.5 = (bf16[1,12,64,64]{3,2,1,0:T(8,128)(2,1)S(1)}, bf16[1,12,64,64]{3,2,1,0:T(8,128)(2,1)}, u32[]{:S(2)}) copy-start(bf16[1,12,64,64]{3,2,1,0:T(8,128)(2,1)} %couplings_ref.1) | copy-start | bytes 294916
  11.6 13.4 %copy-start.7 = (s32[1,12]{1,0:T(1,128)S(1)}, s32[1,12]{1,0:T(1,128)}, u32[]{:S(2)}) copy-start(s32[1,12]{1,0:T(1,128)} %partner_ref.1) | copy-start | bytes 148
  15.0 6.5 %collective-permute-start.6 = (bf16[656,128]{1,0:T(8,128)(2,1)S(1)}, bf16[656,128]{1,0:T(8,128)(2,1)S(1)}, u32[]{:S(2)}, u32[]{:S(2)}) collective-permute-start(bf16[656,128]{1,0:T(8,128)(2,1)S(1)} %get-tuple-element.40), channel_id=1, source_target_pairs={{0,1},{1,0},{2,3},{3,2},{4,5},{5,4},{6,7},{7,6},{8,9},{9,8},{10,11... | collective-permute-start | bytes 503816 | tf_op jit(solution)/shard_map/ppermute | solution.py:297
  15.4 6.1 %collective-permute-start.7 = (bf16[656,128]{1,0:T(8,128)(2,1)S(1)}, bf16[656,128]{1,0:T(8,128)(2,1)S(1)}, u32[]{:S(2)}, u32[]{:S(2)}) collective-permute-start(bf16[656,128]{1,0:T(8,128)(2,1)S(1)} %get-tuple-element.41), channel_id=1, source_target_pairs={{0,2},{1,3},{2,0},{3,1},{4,6},{5,7},{6,4},{7,5},{8,10},{9,11},{10,... | collective-permute-start | bytes 503816 | tf_op jit(solution)/shard_map/ppermute | solution.py:297
  15.7 9.4 %collective-permute-start.8 = (bf16[656,128]{1,0:T(8,128)(2,1)S(1)}, bf16[656,128]{1,0:T(8,128)(2,1)S(1)}, u32[]{:S(2)}, u32[]{:S(2)}) collective-permute-start(bf16[656,128]{1,0:T(8,128)(2,1)S(1)} %get-tuple-element.42), channel_id=1, source_target_pairs={{0,3},{1,2},{2,1},{3,0},{4,7},{5,6},{6,5},{7,4},{8,11},{9,10},{10,... | collective-permute-start | bytes 503816 | tf_op jit(solution)/shard_map/ppermute | solution.py:297
  17.2 11.0 %collective-permute-start.9 = (bf16[528,128]{1,0:T(8,128)(2,1)S(1)}, bf16[528,128]{1,0:T(8,128)(2,1)S(1)}, u32[]{:S(2)}, u32[]{:S(2)}) collective-permute-start(bf16[528,128]{1,0:T(8,128)(2,1)S(1)} %get-tuple-element.43), channel_id=1, source_target_pairs={{0,8},{1,9},{2,10},{3,11},{4,12},{5,13},{6,14},{7,15},{8,0},{9,1},... | collective-permute-start | bytes 405512 | tf_op jit(solution)/shard_map/ppermute | solution.py:297
  19.5 12.9 %collective-permute-start.10 = (bf16[528,128]{1,0:T(8,128)(2,1)S(1)}, bf16[528,128]{1,0:T(8,128)(2,1)S(1)}, u32[]{:S(2)}, u32[]{:S(2)}) collective-permute-start(bf16[528,128]{1,0:T(8,128)(2,1)S(1)} %get-tuple-element.44), channel_id=1, source_target_pairs={{0,12},{1,13},{2,14},{3,15},{4,8},{5,9},{6,10},{7,11},{8,4},{9,5},... | collective-permute-start | bytes 405512 | tf_op jit(solution)/shard_map/ppermute | solution.py:297

commit v12 on v11

--- a/solution.py
+++ b/solution.py
@@ -182,15 +182,27 @@
                 tails[k, pl.ds(leaf, 1), :] += tile[at : at + 1]
 
 
+def split(keys, bit):
+    return [k for k in keys if k & bit], [k for k in keys if not k & bit]
+
+
 def far_sum_kernel(plan, *refs):
     came, outs = refs[: plan.low], refs[plan.low : -5]
     meta, leaf_ref, total, tails, late = refs[-5:]
     to = plan.along
     read_leaves(plan.plane, came, meta, leaf_ref, late, (total, tails))
     add_slots(plan.plane, came, leaf_ref, total, tails)
-    for k, out in enumerate(outs):
-        out[: to.tile, :] = total[k, : to.tile, :].astype(BF16)
-        out[to.tile : to.box, :] = tails[k, : to.box - to.tile, :].astype(BF16)
+    for out, keys in zip(outs, split(plan.far, 1)):
+        for i, k in enumerate(keys):
+            out[i, : to.tile, :] = total[k - FIRST_FAR, : to.tile, :].astype(BF16)
+            out[i, to.tile :, :] = tails[k - FIRST_FAR, : to.box - to.tile, :].astype(BF16)
+
+
+def fold_kernel(terms, *refs):
+    inputs, outs = refs[: -len(terms)], refs[-len(terms) :]
+    for out, entries in zip(outs, terms):
+        for i, entry in enumerate(entries):
+            out[i] = sum(inputs[n][at].astype(F32) for n, at in entry).astype(BF16)
 
 
 def near_sum_kernel(plan, *refs):
@@ -252,8 +264,9 @@
         out_ref[:, cols] = base_ref[:, cols] + dot(down[j], basis_ref[j])
 
 
-def last_kernel(leaves, main, base_ref, *refs):
-    came, out_ref = refs[:-1], refs[-1]
+def last_kernel(leaves, main, picks, base_ref, *refs):
+    out_ref = refs[-1]
+    came = [ref if at is None else ref.at[at] for ref, at in zip(refs, picks)]
     size = base_ref.shape[1] // leaves
     tile = leaves * main
     tails = sum(ref[tile : tile + TILE, :].astype(F32) for ref in came)
@@ -323,14 +336,13 @@
         keep_kernel, (array(sizes[:1]), array(sizes[low : low + 1])), ([VMEM] * 2, (VMEM,) * 2), (plane[0], near[0]), [], 0, 0
     )
 
-    def summed(kernel, kind, dense, came, others):
-        count = kind.fan
-        total = array((count, (leaves + 1) * main), F32)
-        tails = array((count, max(TILE, dense.box - dense.tile)), F32)
+    def summed(kernel, kind, dense, outs, came, others):
+        total = array((kind.fan, (leaves + 1) * main), F32)
+        tails = array((kind.fan, max(TILE, dense.box - dense.tile)), F32)
         return call(
             functools.partial(kernel, plan),
-            [array((dense.depth,))] * count,
-            ([VMEM] * (len(came) + len(others)), [VMEM] * count),
+            outs,
+            ([VMEM] * (len(came) + len(others)), [VMEM] * len(outs)),
             (*came, *others),
             [pltpu.VMEM((len(came), size), I32), pltpu.SMEM((len(came), size), I32)]
             + like(total, tails)
@@ -339,10 +351,34 @@
             4 * (total.size + tails.size),
         )
 
-    along = summed(far_sum_kernel, plan.plane, plan.along, plane, [])
-    near[0], *along = lax.optimization_barrier((near[0], *along))
-    along = [relative(x, k * low) for k, x in zip(plan.far, along)]
-    within = list(summed(near_sum_kernel, plan.near, plan.within, near, boxes))
+    plane[0], *boxes = lax.optimization_barrier((plane[0], *boxes))
+    stack = lambda keys: array((len(keys), plan.along.depth))
+    leaving, staying = split(plan.far, 1)
+    going, kept = summed(far_sum_kernel, plan.plane, plan.along, [stack(leaving), stack(staying)], plane, [])
+    near[0], kept = lax.optimization_barrier((near[0], kept))
+    finals, bit = [], 1
+    while True:
+        came = relative(going, bit * low)
+        arrived = [k ^ bit for k in leaving]
+        finals += [(came, arrived.index(0))] if 0 in arrived else []
+        bit *= 2
+        if bit >= high:
+            break
+        leaving, staying_next = split(staying, bit)
+        entry = lambda k: [(0, staying.index(k))] + ([(1, arrived.index(k))] if k in arrived else [])
+        keys = [group for group in (leaving, staying_next) if group]
+        going, *rest = call(
+            functools.partial(fold_kernel, [[entry(k) for k in group] for group in keys]),
+            [stack(group) for group in keys],
+            ([VMEM] * 2, [VMEM] * len(keys)),
+            (kept, came),
+            [],
+            going.size,
+            0,
+        )
+        kept, staying = (rest[0] if rest else None), staying_next
+
+    within = list(summed(near_sum_kernel, plan.near, plan.within, [array((plan.within.depth,))] * low, near, boxes))
     probes_then, within[0] = lax.optimization_barrier((probes, within[0]))
     for p in range(1, low):
         within[p] = relative(within[p], p)
@@ -361,9 +397,10 @@
         4 * leaves * unit,
         4 * every.size,
     )
-    came = (*within, *along)
+    came = (*within, *(ref for ref, _ in finals))
+    picks = [None] * low + [at for _, at in finals]
     return call(
-        functools.partial(last_kernel, leaves, main),
+        functools.partial(last_kernel, leaves, main, picks),
         base_shape,
         ([VMEM] * (1 + len(came)), VMEM),
         (base, *came),

time: 33.4 us -> 35.3 us (1.057)
  the two profiles are of different devices: /device:TPU:15 before, /device:TPU:0 now
where the time goes in v12:
time: 35.3 us; the launch traced here: 35.1 us
  waiting for transfers between devices  14.4 us (41%)
  starting transfers between devices  9.57 us (27%)
  Pallas kernels  9.11 us (26%)
  local copies, waits for them, and re-layouts  1.89 us (5%)
    ppermute x11, waiting for transfers between devices, per_device(): lax.ppermute(x, 'leaf', [(i, i ^ way) for i in range(devices)])  14.4 us
    ppermute x11, starting transfers between devices, per_device(): lax.ppermute(x, 'leaf', [(i, i ^ way) for i in range(devices)])  9.57 us
    pallas_call x8, Pallas kernels, call(): pl.pallas_call(kernel, out_shape=out_shape, in_specs=specs[0], out_specs=...  9.11 us
    unnamed x16, local copies, waits for them, and re-layouts  1.89 us
  transfers between devices with their start and end apart: 11, of which 6 were waited for; matrix products, arithmetic and copies ran while one was open for 0% of the time, Pallas kernels for 14%

profile of v12, /device:TPU:0, one launch (start us, length us, event | category | flops | bytes accessed | tf_op | source)
XLA Modules:
  0.0 35.1 jit_solution(10865363733545026869)
XLA Ops:
  0.0 3.5 %shard_map.91 = (bf16[528,128]{1,0:T(8,128)(2,1)}, bf16[528,128]{1,0:T(8,128)(2,1)}, bf16[528,128]{1,0:T(8,128)(2,1)}, bf16[528,128]{1,0:T(8,128)(2,1)}, bf16[10...) custom-call(s32[4,8]{1,0:T(4,128)} %bitcast.2, s32[4,8]{1,0:T(4,128)} %bitcast.3, ...), custom_call_target="tpu_custom_call" | custom-call | flops 68157440 | bytes 2488576 | tf_op jit(solution)/shard_map/pallas_call | solution.py:284
  3.5 3.1 %collective-permute-start.5 = (bf16[1088,128]{1,0:T(8,128)(2,1)}, bf16[1088,128]{1,0:T(8,128)(2,1)S(1)}, u32[]{:S(2)}, u32[]{:S(2)}) collective-permute-start(bf16[1088,128]{1,0:T(8,128)(2,1)} %get-tuple-element.38), channel_id=1, source_target_pairs={{0,4},{1,5},{2,6},{3,7},{4,0},{5,1},{6,2},{7,3},{8,12},{9,13},{10,... | collective-permute-start | bytes 835592 | tf_op jit(solution)/shard_map/ppermute | solution.py:310
  6.6 1.5 %collective-permute-start.3 = (bf16[528,128]{1,0:T(8,128)(2,1)}, bf16[528,128]{1,0:T(8,128)(2,1)S(1)}, u32[]{:S(2)}, u32[]{:S(2)}) collective-permute-start(bf16[528,128]{1,0:T(8,128)(2,1)} %get-tuple-element.34), channel_id=1, source_target_pairs={{0,2},{1,3},{2,0},{3,1},{4,6},{5,7},{6,4},{7,5},{8,10},{9,11},{10,... | collective-permute-start | bytes 405512 | tf_op jit(solution)/shard_map/ppermute | solution.py:310
  8.2 0.3 collective-permute-start.4
  8.5 2.5 %collective-permute-start.1 = (bf16[48,128]{1,0:T(8,128)(2,1)}, bf16[48,128]{1,0:T(8,128)(2,1)S(1)}, u32[]{:S(2)}, u32[]{:S(2)}) collective-permute-start(bf16[48,128]{1,0:T(8,128)(2,1)} %get-tuple-element.31), channel_id=1, source_target_pairs={{0,12},{1,13},{2,14},{3,15},{4,8},{5,9},{6,10},{7,11},{8,4},{9,5},... | collective-permute-start | bytes 36872 | tf_op jit(solution)/shard_map/ppermute | solution.py:310
  11.0 5.0 %collective-permute-done.1.refs_3_ = bf16[48,128]{1,0:T(8,128)(2,1)S(1)} collective-permute-done((bf16[48,128]{1,0:T(8,128)(2,1)}, bf16[48,128]{1,0:T(8,128)(2,1)S(1)}, u32[]{:S(2)}, u32[]{:S(2)}) %collective-permute-start.1) | collective-permute-done | bytes 12320 | tf_op jit(solution)/shard_map/ppermute | solution.py:310
  16.0 1.0 %copy-done.4 = bf16[1088,128]{1,0:T(8,128)(2,1)S(1)} copy-done((bf16[1088,128]{1,0:T(8,128)(2,1)S(1)}, bf16[1088,128]{1,0:T(8,128)(2,1)}, u32[]{:S(2)}) %copy-start.4) | copy-done | bytes 278552
  16.9 0.9 %copy-done.6 = bf16[528,128]{1,0:T(8,128)(2,1)S(1)} copy-done((bf16[528,128]{1,0:T(8,128)(2,1)S(1)}, bf16[528,128]{1,0:T(8,128)(2,1)}, u32[]{:S(2)}) %copy-start.6) | copy-done | bytes 135192
  17.9 0.0 copy-start.5
  17.9 2.9 %collective-permute-done.refs_2_ = bf16[48,128]{1,0:T(8,128)(2,1)S(1)} collective-permute-done((bf16[48,128]{1,0:T(8,128)(2,1)}, bf16[48,128]{1,0:T(8,128)(2,1)S(1)}, u32[]{:S(2)}, u32[]{:S(2)}) %collective-permute-start) | collective-permute-done | bytes 12320 | tf_op jit(solution)/shard_map/ppermute | solution.py:310
  20.8 0.9 %shard_map.93 = (bf16[1,528,128]{2,1,0:T(8,128)(2,1)S(1)}, bf16[1,528,128]{2,1,0:T(8,128)(2,1)S(1)}) custom-call(bf16[528,128]{1,0:T(8,128)(2,1)S(1)} %get-tuple-element.32.refs_0_, bf16[528,128]{1,0:T(8,128)(2,1)S(1)} %collective-permute-done.2.refs_1_, bf16[528,128]{1,0:T(8,128)(2,1)S(1)} %collective-permute-done.3.refs_2_, ...), custom_call_target="tpu_custom_call" | custom-call | flops 266240 | bytes 811008 | tf_op jit(solution)/shard_map/pallas_call | solution.py:284
  21.6 0.1 collective-permute-start.9
  21.7 0.9 %shard_map.94 = (bf16[656,128]{1,0:T(8,128)(2,1)S(1)}, bf16[656,128]{1,0:T(8,128)(2,1)S(1)}, bf16[656,128]{1,0:T(8,128)(2,1)S(1)}, bf16[656,128]{1,0:T(8,128)(2,1)S(1)}) custom-call(bf16[1088,128]{1,0:T(8,128)(2,1)S(1)} %get-tuple-element.37.refs_0_, bf16[1088,128]{1,0:T(8,128)(2,1)S(1)} %collective-permute-done.5.refs_1_, ...), custom_call_target="tpu_custom_call" | custom-call | flops 266240 | bytes 1253376 | tf_op jit(solution)/shard_map/pallas_call | solution.py:284
  22.6 0.1 collective-permute-start.6
  22.7 1.6 %collective-permute-start.7 = (bf16[656,128]{1,0:T(8,128)(2,1)S(1)}, bf16[656,128]{1,0:T(8,128)(2,1)S(1)}, u32[]{:S(2)}, u32[]{:S(2)}) collective-permute-start(bf16[656,128]{1,0:T(8,128)(2,1)S(1)} %get-tuple-element.45), channel_id=1, source_target_pairs={{0,2},{1,3},{2,0},{3,1},{4,6},{5,7},{6,4},{7,5},{8,10},{9,11},{10,... | collective-permute-start | bytes 503816 | tf_op jit(solution)/shard_map/ppermute | solution.py:310
  24.3 0.3 collective-permute-start.8
  24.6 2.1 %collective-permute-done.9.refs_1_ = bf16[1,528,128]{2,1,0:T(8,128)(2,1)S(1)} collective-permute-done((bf16[1,528,128]{2,1,0:T(8,128)(2,1)S(1)}, bf16[1,528,128]{2,1,0:T(8,128)(2,1)S(1)}, u32[]{:S(2)}, u32[]{:S(2)}) %collective-permute-start.9) | collective-permute-done | bytes 135200 | tf_op jit(solution)/shard_map/ppermute | solution.py:310
  26.7 0.1 collective-permute-start.10
  26.9 1.5 %shard_map.95.base_ref = f32[65,1024]{1,0:T(8,128)S(1)} custom-call(bf16[65,1024]{1,0:T(8,128)(2,1)S(1)} %copy-done.1, bf16[8,8,128,128]{3,2,1,0:T(8,128)(2,1)S(1)} %copy-done), custom_call_target="tpu_custom_call" | custom-call | flops 136314880 | bytes 2496512 | tf_op jit(solution)/shard_map/pallas_call | solution.py:284
  28.4 1.4 %collective-permute-done.7.refs_2_ = bf16[656,128]{1,0:T(8,128)(2,1)S(1)} collective-permute-done((bf16[656,128]{1,0:T(8,128)(2,1)S(1)}, bf16[656,128]{1,0:T(8,128)(2,1)S(1)}, u32[]{:S(2)}, u32[]{:S(2)}) %collective-permute-start.7) | collective-permute-done | bytes 167968 | tf_op jit(solution)/shard_map/ppermute | solution.py:310
  29.9 2.7 %collective-permute-done.8.refs_3_ = bf16[656,128]{1,0:T(8,128)(2,1)S(1)} collective-permute-done((bf16[656,128]{1,0:T(8,128)(2,1)S(1)}, bf16[656,128]{1,0:T(8,128)(2,1)S(1)}, u32[]{:S(2)}, u32[]{:S(2)}) %collective-permute-start.8) | collective-permute-done | bytes 167968 | tf_op jit(solution)/shard_map/ppermute | solution.py:310
  32.6 1.4 %shard_map.96.base_ref = f32[65,1024]{1,0:T(8,128)S(1)} custom-call(s32[1,12]{1,0:T(1,128)S(1)} %copy-done.7, f32[65,1024]{1,0:T(8,128)S(1)} %shard_map.95.base_ref, bf16[1,12,64,64]{3,2,1,0:T(8,128)(2,1)S(1)} %copy-done.5, bf16[8,64,64]{2,1,0:T(8,128)(2,1)S(1)} %copy-done.2, bf16[8,64,128]{2,1,0:T(8,128)(2,1)S(1)} %copy-done.3, ...), custom_call_target="tpu_custom_call" | custom-call | flops 68157440 | bytes 1499184 | tf_op jit(solution)/shard_map/pallas_call | solution.py:284
  34.0 0.3 collective-permute-done.10.refs_4_
  34.3 0.8 %shard_map.98 = f32[65,1024]{1,0:T(8,128)} custom-call(f32[65,1024]{1,0:T(8,128)S(1)} %shard_map.96.base_ref, bf16[656,128]{1,0:T(8,128)(2,1)S(1)} %get-tuple-element.43.refs_0_, bf16[656,128]{1,0:T(8,128)(2,1)S(1)} %collective-permute-done.6.refs_1_, bf16[656,128]{1,0:T(8,128)(2,1)S(1)} %collective-permute-done.7.refs_2_, ...), custom_call_target="tpu_custom_call" | custom-call | flops 133120 | bytes 1339392 | tf_op jit(solution)/shard_map/pallas_call | solution.py:284
  (22 shorter events, 0.1 us)
Async XLA Ops:
  0.0 26.9 %copy-start.1 = (bf16[65,1024]{1,0:T(8,128)(2,1)S(1)}, bf16[65,1024]{1,0:T(8,128)(2,1)}, u32[]{:S(2)}) copy-start(bf16[65,1024]{1,0:T(8,128)(2,1)} %probes_ref) | copy-start | bytes 399364
  0.0 26.9 %copy-start = (bf16[8,8,128,128]{3,2,1,0:T(8,128)(2,1)S(1)}, bf16[8,8,128,128]{3,2,1,0:T(8,128)(2,1)}, u32[]{:S(2)}) copy-start(bf16[8,8,128,128]{3,2,1,0:T(8,128)(2,1)} %local_ref.1) | copy-start | bytes 6291460
  3.5 18.2 %collective-permute-start.5 = (bf16[1088,128]{1,0:T(8,128)(2,1)}, bf16[1088,128]{1,0:T(8,128)(2,1)S(1)}, u32[]{:S(2)}, u32[]{:S(2)}) collective-permute-start(bf16[1088,128]{1,0:T(8,128)(2,1)} %get-tuple-element.38), channel_id=1, source_target_pairs={{0,4},{1,5},{2,6},{3,7},{4,0},{5,1},{6,2},{7,3},{8,12},{9,13},{10,... | collective-permute-start | bytes 835592 | tf_op jit(solution)/shard_map/ppermute | solution.py:310
  6.6 14.1 %collective-permute-start.2 = (bf16[528,128]{1,0:T(8,128)(2,1)}, bf16[528,128]{1,0:T(8,128)(2,1)S(1)}, u32[]{:S(2)}, u32[]{:S(2)}) collective-permute-start(bf16[528,128]{1,0:T(8,128)(2,1)} %get-tuple-element.33), channel_id=1, source_target_pairs={{0,1},{1,0},{2,3},{3,2},{4,5},{5,4},{6,7},{7,6},{8,9},{9,8},{10,11... | collective-permute-start | bytes 405512 | tf_op jit(solution)/shard_map/ppermute | solution.py:310
  6.6 14.1 %collective-permute-start.3 = (bf16[528,128]{1,0:T(8,128)(2,1)}, bf16[528,128]{1,0:T(8,128)(2,1)S(1)}, u32[]{:S(2)}, u32[]{:S(2)}) collective-permute-start(bf16[528,128]{1,0:T(8,128)(2,1)} %get-tuple-element.34), channel_id=1, source_target_pairs={{0,2},{1,3},{2,0},{3,1},{4,6},{5,7},{6,4},{7,5},{8,10},{9,11},{10,... | collective-permute-start | bytes 405512 | tf_op jit(solution)/shard_map/ppermute | solution.py:310
  8.2 12.6 %collective-permute-start.4 = (bf16[528,128]{1,0:T(8,128)(2,1)}, bf16[528,128]{1,0:T(8,128)(2,1)S(1)}, u32[]{:S(2)}, u32[]{:S(2)}) collective-permute-start(bf16[528,128]{1,0:T(8,128)(2,1)} %get-tuple-element.35), channel_id=1, source_target_pairs={{0,3},{1,2},{2,1},{3,0},{4,7},{5,6},{6,5},{7,4},{8,11},{9,10},{10,... | collective-permute-start | bytes 405512 | tf_op jit(solution)/shard_map/ppermute | solution.py:310
  8.5 7.5 %collective-permute-start.1 = (bf16[48,128]{1,0:T(8,128)(2,1)}, bf16[48,128]{1,0:T(8,128)(2,1)S(1)}, u32[]{:S(2)}, u32[]{:S(2)}) collective-permute-start(bf16[48,128]{1,0:T(8,128)(2,1)} %get-tuple-element.31), channel_id=1, source_target_pairs={{0,12},{1,13},{2,14},{3,15},{4,8},{5,9},{6,10},{7,11},{8,4},{9,5},... | collective-permute-start | bytes 36872 | tf_op jit(solution)/shard_map/ppermute | solution.py:310
  16.0 4.8 %collective-permute-start = (bf16[48,128]{1,0:T(8,128)(2,1)}, bf16[48,128]{1,0:T(8,128)(2,1)S(1)}, u32[]{:S(2)}, u32[]{:S(2)}) collective-permute-start(bf16[48,128]{1,0:T(8,128)(2,1)} %get-tuple-element.31), channel_id=1, source_target_pairs={{0,8},{1,9},{2,10},{3,11},{4,12},{5,13},{6,14},{7,15},{8,0},{9,1},... | collective-permute-start | bytes 36872 | tf_op jit(solution)/shard_map/ppermute | solution.py:310
  16.0 1.0 %copy-start.4 = (bf16[1088,128]{1,0:T(8,128)(2,1)S(1)}, bf16[1088,128]{1,0:T(8,128)(2,1)}, u32[]{:S(2)}) copy-start(bf16[1088,128]{1,0:T(8,128)(2,1)} %get-tuple-element.28.refs_1_) | copy-start | bytes 835588
  16.9 0.9 %copy-start.6 = (bf16[528,128]{1,0:T(8,128)(2,1)S(1)}, bf16[528,128]{1,0:T(8,128)(2,1)}, u32[]{:S(2)}) copy-start(bf16[528,128]{1,0:T(8,128)(2,1)} %get-tuple-element.27.refs_0_) | copy-start | bytes 405508
  17.9 14.7 %copy-start.2 = (bf16[8,64,64]{2,1,0:T(8,128)(2,1)S(1)}, bf16[8,64,64]{2,1,0:T(8,128)(2,1)}, u32[]{:S(2)}) copy-start(bf16[8,64,64]{2,1,0:T(8,128)(2,1)} %transfer_ref.1) | copy-start | bytes 196612
  17.9 14.7 %copy-start.3 = (bf16[8,64,128]{2,1,0:T(8,128)(2,1)S(1)}, bf16[8,64,128]{2,1,0:T(8,128)(2,1)}, u32[]{:S(2)}) copy-start(bf16[8,64,128]{2,1,0:T(8,128)(2,1)} %basis_ref.1) | copy-start | bytes 393220
  17.9 14.7 %copy-start.5 = (bf16[1,12,64,64]{3,2,1,0:T(8,128)(2,1)S(1)}, bf16[1,12,64,64]{3,2,1,0:T(8,128)(2,1)}, u32[]{:S(2)}) copy-start(bf16[1,12,64,64]{3,2,1,0:T(8,128)(2,1)} %couplings_ref.1) | copy-start | bytes 294916
  17.9 14.7 %copy-start.7 = (s32[1,12]{1,0:T(1,128)S(1)}, s32[1,12]{1,0:T(1,128)}, u32[]{:S(2)}) copy-start(s32[1,12]{1,0:T(1,128)} %partner_ref.1) | copy-start | bytes 148
  21.6 5.1 %collective-permute-start.9 = (bf16[1,528,128]{2,1,0:T(8,128)(2,1)S(1)}, bf16[1,528,128]{2,1,0:T(8,128)(2,1)S(1)}, u32[]{:S(2)}, u32[]{:S(2)}) collective-permute-start(bf16[1,528,128]{2,1,0:T(8,128)(2,1)S(1)} %get-tuple-element.48), channel_id=1, source_target_pairs={{0,4},{1,5},{2,6},{3,7},{4,0},{5,1},{6,2},{7,3},{8,12},{9,13},{10,... | collective-permute-start | bytes 405512 | tf_op jit(solution)/shard_map/ppermute | solution.py:310
  22.6 5.8 %collective-permute-start.6 = (bf16[656,128]{1,0:T(8,128)(2,1)S(1)}, bf16[656,128]{1,0:T(8,128)(2,1)S(1)}, u32[]{:S(2)}, u32[]{:S(2)}) collective-permute-start(bf16[656,128]{1,0:T(8,128)(2,1)S(1)} %get-tuple-element.44), channel_id=1, source_target_pairs={{0,1},{1,0},{2,3},{3,2},{4,5},{5,4},{6,7},{7,6},{8,9},{9,8},{10,11... | collective-permute-start | bytes 503816 | tf_op jit(solution)/shard_map/ppermute | solution.py:310
  22.7 7.2 %collective-permute-start.7 = (bf16[656,128]{1,0:T(8,128)(2,1)S(1)}, bf16[656,128]{1,0:T(8,128)(2,1)S(1)}, u32[]{:S(2)}, u32[]{:S(2)}) collective-permute-start(bf16[656,128]{1,0:T(8,128)(2,1)S(1)} %get-tuple-element.45), channel_id=1, source_target_pairs={{0,2},{1,3},{2,0},{3,1},{4,6},{5,7},{6,4},{7,5},{8,10},{9,11},{10,... | collective-permute-start | bytes 503816 | tf_op jit(solution)/shard_map/ppermute | solution.py:310
  24.3 8.2 %collective-permute-start.8 = (bf16[656,128]{1,0:T(8,128)(2,1)S(1)}, bf16[656,128]{1,0:T(8,128)(2,1)S(1)}, u32[]{:S(2)}, u32[]{:S(2)}) collective-permute-start(bf16[656,128]{1,0:T(8,128)(2,1)S(1)} %get-tuple-element.46), channel_id=1, source_target_pairs={{0,3},{1,2},{2,1},{3,0},{4,7},{5,6},{6,5},{7,4},{8,11},{9,10},{10,... | collective-permute-start | bytes 503816 | tf_op jit(solution)/shard_map/ppermute | solution.py:310
  26.7 7.6 %collective-permute-start.10 = (bf16[1,528,128]{2,1,0:T(8,128)(2,1)S(1)}, bf16[1,528,128]{2,1,0:T(8,128)(2,1)S(1)}, u32[]{:S(2)}, u32[]{:S(2)}) collective-permute-start(bf16[1,528,128]{2,1,0:T(8,128)(2,1)S(1)} %shard_map.97), channel_id=1, source_target_pairs={{0,8},{1,9},{2,10},{3,11},{4,12},{5,13},{6,14},{7,15},{8,0},{9,1},... | collective-permute-start | bytes 405512 | tf_op jit(solution)/shard_map/ppermute | solution.py:310

commit v13 on v8

--- a/solution.py
+++ b/solution.py
@@ -9,7 +9,8 @@
 
 CAP = 4
 TILE = 16
-LANES = 128
+HEAVY = 4 * 10**9
+
 F32 = jnp.float32
 BF16 = jnp.bfloat16
 I32 = jnp.int32
@@ -156,9 +157,14 @@
         copy.wait()
 
 
-def sum_kernel(route, ways, *refs):
-    came, outs = refs[:ways], refs[ways : ways + route.fan]
-    meta, leaf_ref, total, tails, late = refs[ways + route.fan :]
+def split(keys, bit):
+    return [k for k in keys if k & bit], [k for k in keys if not k & bit]
+
+
+def sum_kernel(route, ways, places, *refs):
+    came, given = refs[:ways], refs[ways:-5]
+    meta, leaf_ref, total, tails, late = refs[-5:]
+    outs = [given[n] if at is None else given[n].at[at] for n, at in places]
     leaves, half = route.leaves, route.half
     lasts = []
     for i in range(ways):
@@ -190,6 +196,18 @@
                 start = route.dense_box + i * half
                 outs[k][start : start + half, :] = came[i][route.box :, :]
             outs[k][route.dense_tails : route.dense_box, :] = tails[k].astype(BF16)
+
+
+def fold_kernel(terms, *refs):
+    inputs, outs = refs[: -len(terms)], refs[-len(terms) :]
+    for out, entries in zip(outs, terms):
+        for i, entry in enumerate(entries):
+            out[i] = sum(inputs[n][at].astype(F32) for n, at in entry).astype(BF16)
+
+
+def keep_kernel(own_low, own_high, kept_low, kept_high):
+    kept_low[...] = own_low[...]
+    kept_high[...] = own_high[...]
 
 
 def local_kernel(probes_ref, local_ref, out_ref):
@@ -227,16 +245,17 @@
         out_ref[:, cols] = base_ref[:, cols] + dot(down[j], basis_ref[j])
 
 
-def last_kernel(routes, devices, base_ref, *refs):
+def last_kernel(routes, devices, picks, base_ref, *refs):
     by_low, by_high = routes
-    high, low = grid_of(devices)
-    came_high, came_low, out_ref = refs[:high], refs[high : high + low], refs[high + low]
+    low = grid_of(devices)[1]
+    came_low, out_ref = refs[:low], refs[-1]
+    came_high = [refs[low + n].at[at] for n, at in enumerate(picks)]
     leaves, split, main = by_low.leaves, by_low.rows, by_low.main
     size = base_ref.shape[1] // leaves
     tails = sum(came_low[k][by_high.dense_tails : by_high.dense_box, :].astype(F32) for k in range(low))
     for j in range(leaves):
         cols = slice(j * size, (j + 1) * size)
-        upper = sum(came_high[k][j * by_low.rows : (j + 1) * by_low.rows, :].astype(F32) for k in range(high))
+        upper = sum(ref[j * by_low.rows : (j + 1) * by_low.rows, :].astype(F32) for ref in came_high)
         lower = sum(came_low[k][j * by_high.rows : (j + 1) * by_high.rows, :].astype(F32) for k in range(low))
         out_ref[:split, cols] = base_ref[:split, cols] + upper
         out_ref[split:main, cols] = base_ref[split:main, cols] + lower
@@ -279,18 +298,18 @@
     def stacked(count, like_this):
         return pltpu.VMEM((count, *like_this.shape), like_this.dtype)
 
-    def summed(route, ways, came):
+    def summed(route, ways, came, outs, places):
         total = jax.ShapeDtypeStruct((route.fan, (leaves + 1) * route.rows, size), F32)
         tails = jax.ShapeDtypeStruct((route.fan, max(TILE, route.dense_box - route.dense_tails), size), F32)
         return call(
-            functools.partial(sum_kernel, route, ways),
-            [dense(route)] * route.fan,
-            ([VMEM] * ways, [VMEM] * route.fan),
+            functools.partial(sum_kernel, route, ways, places),
+            outs,
+            ([VMEM] * ways, [VMEM] * len(outs)),
             came,
             [pltpu.VMEM((ways, size), I32), pltpu.SMEM((ways, size), I32)]
             + like(total, tails)
             + [pltpu.SemaphoreType.DMA(())],
-            devices * CAP * route.rows * size,
+            HEAVY,
             4 * (total.size + tails.size),
         )
 
@@ -321,19 +340,54 @@
         came_low[k] = relative(came_low[k], k)
     came_high[1] = relative(came_high[1], low)
 
-    probes_then, came_low[0] = lax.optimization_barrier((probes, came_low[0]))
     base_shape = jax.ShapeDtypeStruct((columns, points), F32)
+    came_low[0], came_high[0] = call(
+        keep_kernel,
+        (message(by_low), message(by_high)),
+        ([VMEM] * 2, (VMEM,) * 2),
+        (came_low[0], came_high[0]),
+        [],
+        0,
+        0,
+    )
+
+    stack = lambda keys: jax.ShapeDtypeStruct((len(keys), by_low.dense_depth, size), BF16)
+    leaving, staying = split(range(high), 1)
+    places = [(0, leaving.index(k)) if k in leaving else (1, staying.index(k)) for k in range(high)]
+    going, kept = summed(by_low, low, came_low, [stack(leaving), stack(staying)], places)
+    came_high[0], kept = lax.optimization_barrier((came_high[0], kept))
+    finals, bit = [(kept, staying.index(0))], 1
+    while True:
+        came = relative(going, bit * low)
+        arrived = [k ^ bit for k in leaving]
+        finals += [(came, arrived.index(0))]
+        bit *= 2
+        if bit >= high:
+            break
+        leaving, staying_next = split([k for k in staying if k], bit)
+        entry = lambda k: [(0, staying.index(k)), (1, arrived.index(k))]
+        groups = [group for group in (leaving, staying_next) if group]
+        outs = [stack(group) for group in groups]
+        going, *rest = call(
+            functools.partial(fold_kernel, [[entry(k) for k in group] for group in groups]),
+            outs,
+            ([VMEM] * 2, [VMEM] * len(outs)),
+            (kept, came),
+            [],
+            going.size,
+            0,
+        )
+        kept, staying = (rest[0] if rest else None), staying_next
+
+    to_low = list(
+        summed(by_high, high, came_high, [dense(by_high)] * low, [(p, None) for p in range(low)])
+    )
+    probes_then, to_low[0] = lax.optimization_barrier((probes, to_low[0]))
+    for k in range(1, low):
+        to_low[k] = relative(to_low[k], k)
     base = call(
         local_kernel, base_shape, ([VMEM] * 2, VMEM), (probes_then, local_blocks), [], leaves * leaves * unit, 0
     )
-
-    to_high = list(summed(by_low, low, came_low))
-    for k in range(high - 1, 0, -1):
-        to_high[k] = relative(to_high[k], k * low)
-    came_high[0], to_high[0] = lax.optimization_barrier((came_high[0], to_high[0]))
-    to_low = list(summed(by_high, high, came_high))
-    for k in range(low - 1, 0, -1):
-        to_low[k] = relative(to_low[k], k)
 
     boxes = jax.ShapeDtypeStruct((devices, columns, rank), BF16)
     base = call(
@@ -342,14 +396,14 @@
         ([SMEM] + [VMEM] * (4 + low), VMEM),
         (far_list, base, couplings, transfer, basis, *to_low),
         like(boxes),
-        4 * leaves * unit,
+        HEAVY,
         4 * boxes.size,
     )
     return call(
-        functools.partial(last_kernel, routes, devices),
+        functools.partial(last_kernel, routes, devices, [at for _, at in finals]),
         base_shape,
-        ([VMEM] * (1 + high + low), VMEM),
-        (base, *to_high, *to_low),
+        ([VMEM] * (1 + low + len(finals)), VMEM),
+        (base, *to_low, *(ref for ref, _ in finals)),
         [],
         devices * columns * size,
         0,

time: 34 us -> 33.4 us (0.982)
    ppermute x12 -> x11, waiting for transfers between devices: 8.51 us -> 8.19 us  [per_device(): lax.ppermute(x, 'leaf', [(i, i ^ way) for i in range(devices)])]
    ppermute x12 -> x11, starting transfers between devices: 14.2 us -> 13.9 us  [per_device(): lax.ppermute(x, 'leaf', [(i, i ^ way) for i in range(devices)])]
    pallas_call x6 -> x8, Pallas kernels: 9.22 us -> 9.08 us  [call(): pl.pallas_call(kernel, out_shape=out_shape, in_specs=specs[0], out_specs=...]
  transfers between devices with their start and end apart: 12 -> 11, of which waited for: 5 -> 4; matrix products, arithmetic and copies ran while one was open for 0% -> 0% of each run, Pallas kernels for 12% -> 15%
where the time goes in v13:
time: 33.4 us; the launch traced here: 33.2 us
  starting transfers between devices  13.9 us (42%)
  Pallas kernels  9.08 us (27%)
  waiting for transfers between devices  8.19 us (25%)
  local copies, waits for them, and re-layouts  1.85 us (6%)
    ppermute x11, starting transfers between devices, per_device(): lax.ppermute(x, 'leaf', [(i, i ^ way) for i in range(devices)])  13.9 us
    pallas_call x8, Pallas kernels, call(): pl.pallas_call(kernel, out_shape=out_shape, in_specs=specs[0], out_specs=...  9.08 us
    ppermute x11, waiting for transfers between devices, per_device(): lax.ppermute(x, 'leaf', [(i, i ^ way) for i in range(devices)])  8.19 us
    unnamed x16, local copies, waits for them, and re-layouts  1.85 us
  transfers between devices with their start and end apart: 11, of which 4 were waited for; matrix products, arithmetic and copies ran while one was open for 0% of the time, Pallas kernels for 15%

profile of v13, /device:TPU:0, one launch (start us, length us, event | category | flops | bytes accessed | tf_op | source)
XLA Modules:
  0.0 33.2 jit_solution(16717425044066466017)
XLA Ops:
  0.0 3.4 %shard_map.91 = (bf16[784,128]{1,0:T(8,128)(2,1)}, bf16[784,128]{1,0:T(8,128)(2,1)}, bf16[784,128]{1,0:T(8,128)(2,1)}, bf16[784,128]{1,0:T(8,128)(2,1)}, bf16[32...) custom-call(s32[4,8]{1,0:T(4,128)} %bitcast.2, ...), custom_call_target="tpu_custom_call" | custom-call | flops 68157440 | bytes 2509056 | tf_op jit(solution)/shard_map/pallas_call | solution.py:269
  3.4 0.5 %collective-permute-start = (bf16[784,128]{1,0:T(8,128)(2,1)}, bf16[784,128]{1,0:T(8,128)(2,1)S(1)}, u32[]{:S(2)}, u32[]{:S(2)}) collective-permute-start(bf16[784,128]{1,0:T(8,128)(2,1)} %get-tuple-element.29), channel_id=1, source_target_pairs={{0,1},{1,0},{2,3},{3,2},{4,5},{5,4},{6,7},{7,6},{8,9},{9,8},{10,11... | collective-permute-start | bytes 602120 | tf_op jit(solution)/shard_map/ppermute | solution.py:294
  3.9 2.6 %collective-permute-start.1 = (bf16[784,128]{1,0:T(8,128)(2,1)}, bf16[784,128]{1,0:T(8,128)(2,1)S(1)}, u32[]{:S(2)}, u32[]{:S(2)}) collective-permute-start(bf16[784,128]{1,0:T(8,128)(2,1)} %get-tuple-element.30), channel_id=1, source_target_pairs={{0,2},{1,3},{2,0},{3,1},{4,6},{5,7},{6,4},{7,5},{8,10},{9,11},{10,... | collective-permute-start | bytes 602120 | tf_op jit(solution)/shard_map/ppermute | solution.py:294
  6.5 0.1 collective-permute-start.2
  6.6 1.8 %collective-permute-start.3 = (bf16[320,128]{1,0:T(8,128)(2,1)}, bf16[320,128]{1,0:T(8,128)(2,1)S(1)}, u32[]{:S(2)}, u32[]{:S(2)}) collective-permute-start(bf16[320,128]{1,0:T(8,128)(2,1)} %get-tuple-element.34), channel_id=1, source_target_pairs={{0,4},{1,5},{2,6},{3,7},{4,0},{5,1},{6,2},{7,3},{8,12},{9,13},{10,... | collective-permute-start | bytes 245768 | tf_op jit(solution)/shard_map/ppermute | solution.py:294
  8.4 2.6 %collective-permute-start.4 = (bf16[320,128]{1,0:T(8,128)(2,1)}, bf16[320,128]{1,0:T(8,128)(2,1)S(1)}, u32[]{:S(2)}, u32[]{:S(2)}) collective-permute-start(bf16[320,128]{1,0:T(8,128)(2,1)} %get-tuple-element.35), channel_id=1, source_target_pairs={{0,8},{1,9},{2,10},{3,11},{4,12},{5,13},{6,14},{7,15},{8,0},{9,1},... | collective-permute-start | bytes 245768 | tf_op jit(solution)/shard_map/ppermute | solution.py:294
  10.9 0.9 %copy-done.2 = bf16[784,128]{1,0:T(8,128)(2,1)S(1)} copy-done((bf16[784,128]{1,0:T(8,128)(2,1)S(1)}, bf16[784,128]{1,0:T(8,128)(2,1)}, u32[]{:S(2)}) %copy-start.2) | copy-done | bytes 200728
  11.9 0.9 %copy-done.5 = bf16[320,128]{1,0:T(8,128)(2,1)S(1)} copy-done((bf16[320,128]{1,0:T(8,128)(2,1)S(1)}, bf16[320,128]{1,0:T(8,128)(2,1)}, u32[]{:S(2)}) %copy-start.5) | copy-done | bytes 81944
  12.8 0.1 collective-permute-start.5
  12.9 3.5 %collective-permute-done.2.refs_3_ = bf16[784,128]{1,0:T(8,128)(2,1)S(1)} collective-permute-done((bf16[784,128]{1,0:T(8,128)(2,1)}, bf16[784,128]{1,0:T(8,128)(2,1)S(1)}, u32[]{:S(2)}, u32[]{:S(2)}) %collective-permute-start.2) | collective-permute-done | bytes 200736 | tf_op jit(solution)/shard_map/ppermute | solution.py:294
  16.3 1.0 %shard_map.93 = (bf16[2,384,128]{2,1,0:T(8,128)(2,1)S(1)}, bf16[2,384,128]{2,1,0:T(8,128)(2,1)S(1)}) custom-call(bf16[784,128]{1,0:T(8,128)(2,1)S(1)} %get-tuple-element.28.refs_0_, bf16[784,128]{1,0:T(8,128)(2,1)S(1)} %collective-permute-done.refs_1_, bf16[784,128]{1,0:T(8,128)(2,1)S(1)} %collective-permute-done.1.refs_2_, ...), custom_call_target="tpu_custom_call" | custom-call | flops 4000000000 | bytes 1196032 | tf_op jit(solution)/shard_map/pallas_call | solution.py:269
  17.4 0.0 copy-start.1
  17.4 1.7 %collective-permute-start.9 = (bf16[2,384,128]{2,1,0:T(8,128)(2,1)S(1)}, bf16[2,384,128]{2,1,0:T(8,128)(2,1)S(1)}, u32[]{:S(2)}, u32[]{:S(2)}) collective-permute-start(bf16[2,384,128]{2,1,0:T(8,128)(2,1)S(1)} %get-tuple-element.44), channel_id=1, source_target_pairs={{0,4},{1,5},{2,6},{3,7},{4,0},{5,1},{6,2},{7,3},{8,12},{9,13},{10,... | collective-permute-start | bytes 589832 | tf_op jit(solution)/shard_map/ppermute | solution.py:294
  19.1 0.2 collective-permute-done.5.refs_3_
  19.3 0.9 %shard_map.94 = (bf16[272,128]{1,0:T(8,128)(2,1)S(1)}, bf16[272,128]{1,0:T(8,128)(2,1)S(1)}, bf16[272,128]{1,0:T(8,128)(2,1)S(1)}, bf16[272,128]{1,0:T(8,128)(2,1)S(1)}) custom-call(bf16[320,128]{1,0:T(8,128)(2,1)S(1)} %get-tuple-element.33.refs_0_, bf16[320,128]{1,0:T(8,128)(2,1)S(1)} %collective-permute-done.3.refs_1_, ...), custom_call_target="tpu_custom_call" | custom-call | flops 4000000000 | bytes 606208 | tf_op jit(solution)/shard_map/pallas_call | solution.py:269
  20.3 0.1 collective-permute-start.6
  20.4 1.6 %collective-permute-start.7 = (bf16[272,128]{1,0:T(8,128)(2,1)S(1)}, bf16[272,128]{1,0:T(8,128)(2,1)S(1)}, u32[]{:S(2)}, u32[]{:S(2)}) collective-permute-start(bf16[272,128]{1,0:T(8,128)(2,1)S(1)} %get-tuple-element.41), channel_id=1, source_target_pairs={{0,2},{1,3},{2,0},{3,1},{4,6},{5,7},{6,4},{7,5},{8,10},{9,11},{10,... | collective-permute-start | bytes 208904 | tf_op jit(solution)/shard_map/ppermute | solution.py:294
  22.0 0.3 collective-permute-start.8
  22.2 1.5 %shard_map.95.base_ref = f32[65,1024]{1,0:T(8,128)S(1)} custom-call(bf16[65,1024]{1,0:T(8,128)(2,1)S(1)} %copy-done.1, bf16[8,8,128,128]{3,2,1,0:T(8,128)(2,1)S(1)} %copy-done), custom_call_target="tpu_custom_call" | custom-call | flops 136314880 | bytes 2496512 | tf_op jit(solution)/shard_map/pallas_call | solution.py:269
  23.8 0.9 %collective-permute-done.9.refs_1_.refs_5_ = bf16[2,384,128]{2,1,0:T(8,128)(2,1)S(1)} collective-permute-done((bf16[2,384,128]{2,1,0:T(8,128)(2,1)S(1)}, bf16[2,384,128]{2,1,0:T(8,128)(2,1)S(1)}, u32[]{:S(2)}, u32[]{:S(2)}) %collective-permute-start.9) | collective-permute-done | bytes 196640 | tf_op jit(solution)/shard_map/ppermute | solution.py:294
  24.7 2.7 %collective-permute-start.10 = (bf16[1,384,128]{2,1,0:T(8,128)(2,1)S(1)}, bf16[1,384,128]{2,1,0:T(8,128)(2,1)S(1)}, u32[]{:S(2)}, u32[]{:S(2)}) collective-permute-start(bf16[1,384,128]{2,1,0:T(8,128)(2,1)S(1)} %shard_map.97), channel_id=1, source_target_pairs={{0,8},{1,9},{2,10},{3,11},{4,12},{5,13},{6,14},{7,15},{8,0},{9,1},... | collective-permute-start | bytes 294920 | tf_op jit(solution)/shard_map/ppermute | solution.py:294
  27.5 1.4 %shard_map.96.base_ref = f32[65,1024]{1,0:T(8,128)S(1)} custom-call(s32[1,12]{1,0:T(1,128)S(1)} %copy-done.7, f32[65,1024]{1,0:T(8,128)S(1)} %shard_map.95.base_ref, bf16[1,12,64,64]{3,2,1,0:T(8,128)(2,1)S(1)} %copy-done.6, bf16[8,64,64]{2,1,0:T(8,128)(2,1)S(1)} %copy-done.3, bf16[8,64,128]{2,1,0:T(8,128)(2,1)S(1)} %copy-done.4, ...), custom_call_target="tpu_custom_call" | custom-call | flops 4000000000 | bytes 1105968 | tf_op jit(solution)/shard_map/pallas_call | solution.py:269
  28.9 3.5 %collective-permute-done.10.refs_6_ = bf16[1,384,128]{2,1,0:T(8,128)(2,1)S(1)} collective-permute-done((bf16[1,384,128]{2,1,0:T(8,128)(2,1)S(1)}, bf16[1,384,128]{2,1,0:T(8,128)(2,1)S(1)}, u32[]{:S(2)}, u32[]{:S(2)}) %collective-permute-start.10) | collective-permute-done | bytes 98336 | tf_op jit(solution)/shard_map/ppermute | solution.py:294
  32.4 0.8 %shard_map.98 = f32[65,1024]{1,0:T(8,128)} custom-call(f32[65,1024]{1,0:T(8,128)S(1)} %shard_map.96.base_ref, bf16[272,128]{1,0:T(8,128)(2,1)S(1)} %get-tuple-element.39.refs_0_, bf16[272,128]{1,0:T(8,128)(2,1)S(1)} %collective-permute-done.6.refs_1_, bf16[272,128]{1,0:T(8,128)(2,1)S(1)} %collective-permute-done.7.refs_2_, ...), custom_call_target="tpu_custom_call" | custom-call | flops 133120 | bytes 1302528 | tf_op jit(solution)/shard_map/pallas_call | solution.py:269
  (22 shorter events, 0.1 us)
Async XLA Ops:
  3.4 9.4 %collective-permute-start = (bf16[784,128]{1,0:T(8,128)(2,1)}, bf16[784,128]{1,0:T(8,128)(2,1)S(1)}, u32[]{:S(2)}, u32[]{:S(2)}) collective-permute-start(bf16[784,128]{1,0:T(8,128)(2,1)} %get-tuple-element.29), channel_id=1, source_target_pairs={{0,1},{1,0},{2,3},{3,2},{4,5},{5,4},{6,7},{7,6},{8,9},{9,8},{10,11... | collective-permute-start | bytes 602120 | tf_op jit(solution)/shard_map/ppermute | solution.py:294
  3.9 9.0 %collective-permute-start.1 = (bf16[784,128]{1,0:T(8,128)(2,1)}, bf16[784,128]{1,0:T(8,128)(2,1)S(1)}, u32[]{:S(2)}, u32[]{:S(2)}) collective-permute-start(bf16[784,128]{1,0:T(8,128)(2,1)} %get-tuple-element.30), channel_id=1, source_target_pairs={{0,2},{1,3},{2,0},{3,1},{4,6},{5,7},{6,4},{7,5},{8,10},{9,11},{10,... | collective-permute-start | bytes 602120 | tf_op jit(solution)/shard_map/ppermute | solution.py:294
  6.5 9.8 %collective-permute-start.2 = (bf16[784,128]{1,0:T(8,128)(2,1)}, bf16[784,128]{1,0:T(8,128)(2,1)S(1)}, u32[]{:S(2)}, u32[]{:S(2)}) collective-permute-start(bf16[784,128]{1,0:T(8,128)(2,1)} %get-tuple-element.31), channel_id=1, source_target_pairs={{0,3},{1,2},{2,1},{3,0},{4,7},{5,6},{6,5},{7,4},{8,11},{9,10},{10,... | collective-permute-start | bytes 602120 | tf_op jit(solution)/shard_map/ppermute | solution.py:294
  6.6 12.5 %collective-permute-start.3 = (bf16[320,128]{1,0:T(8,128)(2,1)}, bf16[320,128]{1,0:T(8,128)(2,1)S(1)}, u32[]{:S(2)}, u32[]{:S(2)}) collective-permute-start(bf16[320,128]{1,0:T(8,128)(2,1)} %get-tuple-element.34), channel_id=1, source_target_pairs={{0,4},{1,5},{2,6},{3,7},{4,0},{5,1},{6,2},{7,3},{8,12},{9,13},{10,... | collective-permute-start | bytes 245768 | tf_op jit(solution)/shard_map/ppermute | solution.py:294
  8.4 10.7 %collective-permute-start.4 = (bf16[320,128]{1,0:T(8,128)(2,1)}, bf16[320,128]{1,0:T(8,128)(2,1)S(1)}, u32[]{:S(2)}, u32[]{:S(2)}) collective-permute-start(bf16[320,128]{1,0:T(8,128)(2,1)} %get-tuple-element.35), channel_id=1, source_target_pairs={{0,8},{1,9},{2,10},{3,11},{4,12},{5,13},{6,14},{7,15},{8,0},{9,1},... | collective-permute-start | bytes 245768 | tf_op jit(solution)/shard_map/ppermute | solution.py:294
  10.9 0.9 %copy-start.2 = (bf16[784,128]{1,0:T(8,128)(2,1)S(1)}, bf16[784,128]{1,0:T(8,128)(2,1)}, u32[]{:S(2)}) copy-start(bf16[784,128]{1,0:T(8,128)(2,1)} %get-tuple-element.25.own_low) | copy-start | bytes 602116
  11.9 0.9 %copy-start.5 = (bf16[320,128]{1,0:T(8,128)(2,1)S(1)}, bf16[320,128]{1,0:T(8,128)(2,1)}, u32[]{:S(2)}) copy-start(bf16[320,128]{1,0:T(8,128)(2,1)} %get-tuple-element.26.own_high) | copy-start | bytes 245764
  12.8 6.5 %collective-permute-start.5 = (bf16[320,128]{1,0:T(8,128)(2,1)}, bf16[320,128]{1,0:T(8,128)(2,1)S(1)}, u32[]{:S(2)}, u32[]{:S(2)}) collective-permute-start(bf16[320,128]{1,0:T(8,128)(2,1)} %get-tuple-element.36), channel_id=1, source_target_pairs={{0,12},{1,13},{2,14},{3,15},{4,8},{5,9},{6,10},{7,11},{8,4},{9,5},... | collective-permute-start | bytes 245768 | tf_op jit(solution)/shard_map/ppermute | solution.py:294
  17.3 4.9 %copy-start = (bf16[8,8,128,128]{3,2,1,0:T(8,128)(2,1)S(1)}, bf16[8,8,128,128]{3,2,1,0:T(8,128)(2,1)}, u32[]{:S(2)}) copy-start(bf16[8,8,128,128]{3,2,1,0:T(8,128)(2,1)} %local_ref.1) | copy-start | bytes 6291460
  17.4 4.9 %copy-start.1 = (bf16[65,1024]{1,0:T(8,128)(2,1)S(1)}, bf16[65,1024]{1,0:T(8,128)(2,1)}, u32[]{:S(2)}) copy-start(bf16[65,1024]{1,0:T(8,128)(2,1)} %probes_ref) | copy-start | bytes 399364
  17.4 7.3 %collective-permute-start.9 = (bf16[2,384,128]{2,1,0:T(8,128)(2,1)S(1)}, bf16[2,384,128]{2,1,0:T(8,128)(2,1)S(1)}, u32[]{:S(2)}, u32[]{:S(2)}) collective-permute-start(bf16[2,384,128]{2,1,0:T(8,128)(2,1)S(1)} %get-tuple-element.44), channel_id=1, source_target_pairs={{0,4},{1,5},{2,6},{3,7},{4,0},{5,1},{6,2},{7,3},{8,12},{9,13},{10,... | collective-permute-start | bytes 589832 | tf_op jit(solution)/shard_map/ppermute | solution.py:294
  20.3 7.2 %copy-start.3 = (bf16[8,64,64]{2,1,0:T(8,128)(2,1)S(1)}, bf16[8,64,64]{2,1,0:T(8,128)(2,1)}, u32[]{:S(2)}) copy-start(bf16[8,64,64]{2,1,0:T(8,128)(2,1)} %transfer_ref.1) | copy-start | bytes 196612
  20.3 7.2 %copy-start.4 = (bf16[8,64,128]{2,1,0:T(8,128)(2,1)S(1)}, bf16[8,64,128]{2,1,0:T(8,128)(2,1)}, u32[]{:S(2)}) copy-start(bf16[8,64,128]{2,1,0:T(8,128)(2,1)} %basis_ref.1) | copy-start | bytes 393220
  20.3 7.2 %copy-start.6 = (bf16[1,12,64,64]{3,2,1,0:T(8,128)(2,1)S(1)}, bf16[1,12,64,64]{3,2,1,0:T(8,128)(2,1)}, u32[]{:S(2)}) copy-start(bf16[1,12,64,64]{3,2,1,0:T(8,128)(2,1)} %couplings_ref.1) | copy-start | bytes 294916
  20.3 7.2 %copy-start.7 = (s32[1,12]{1,0:T(1,128)S(1)}, s32[1,12]{1,0:T(1,128)}, u32[]{:S(2)}) copy-start(s32[1,12]{1,0:T(1,128)} %partner_ref.1) | copy-start | bytes 148
  20.3 7.1 %collective-permute-start.6 = (bf16[272,128]{1,0:T(8,128)(2,1)S(1)}, bf16[272,128]{1,0:T(8,128)(2,1)S(1)}, u32[]{:S(2)}, u32[]{:S(2)}) collective-permute-start(bf16[272,128]{1,0:T(8,128)(2,1)S(1)} %get-tuple-element.40), channel_id=1, source_target_pairs={{0,1},{1,0},{2,3},{3,2},{4,5},{5,4},{6,7},{7,6},{8,9},{9,8},{10,11... | collective-permute-start | bytes 208904 | tf_op jit(solution)/shard_map/ppermute | solution.py:294
  20.4 7.0 %collective-permute-start.7 = (bf16[272,128]{1,0:T(8,128)(2,1)S(1)}, bf16[272,128]{1,0:T(8,128)(2,1)S(1)}, u32[]{:S(2)}, u32[]{:S(2)}) collective-permute-start(bf16[272,128]{1,0:T(8,128)(2,1)S(1)} %get-tuple-element.41), channel_id=1, source_target_pairs={{0,2},{1,3},{2,0},{3,1},{4,6},{5,7},{6,4},{7,5},{8,10},{9,11},{10,... | collective-permute-start | bytes 208904 | tf_op jit(solution)/shard_map/ppermute | solution.py:294
  22.0 5.5 %collective-permute-start.8 = (bf16[272,128]{1,0:T(8,128)(2,1)S(1)}, bf16[272,128]{1,0:T(8,128)(2,1)S(1)}, u32[]{:S(2)}, u32[]{:S(2)}) collective-permute-start(bf16[272,128]{1,0:T(8,128)(2,1)S(1)} %get-tuple-element.42), channel_id=1, source_target_pairs={{0,3},{1,2},{2,1},{3,0},{4,7},{5,6},{6,5},{7,4},{8,11},{9,10},{10,... | collective-permute-start | bytes 208904 | tf_op jit(solution)/shard_map/ppermute | solution.py:294
  24.7 7.7 %collective-permute-start.10 = (bf16[1,384,128]{2,1,0:T(8,128)(2,1)S(1)}, bf16[1,384,128]{2,1,0:T(8,128)(2,1)S(1)}, u32[]{:S(2)}, u32[]{:S(2)}) collective-permute-start(bf16[1,384,128]{2,1,0:T(8,128)(2,1)S(1)} %shard_map.97), channel_id=1, source_target_pairs={{0,8},{1,9},{2,10},{3,11},{4,12},{5,13},{6,14},{7,15},{8,0},{9,1},... | collective-permute-start | bytes 294920 | tf_op jit(solution)/shard_map/ppermute | solution.py:294

commit v14 on v10

--- a/solution.py
+++ b/solution.py
@@ -9,7 +9,6 @@
 
 CAP = 4
 TILE = 16
-LANES = 128
 F32 = jnp.float32
 BF16 = jnp.bfloat16
 I32 = jnp.int32
@@ -72,11 +71,11 @@
 
 def products_kernel(routes, devices, *refs):
     dest_hbm, leaf_hbm, probes_hbm, basis_hbm, transfer_hbm, blocks_hbm = refs[:6]
-    outs = refs[6:-13]
+    outs = refs[6:-11]
     (
         dest_ref, leaf_ref, probes_ref, basis_ref, transfer_ref, blocks_ref,
-        send_low, send_high, tails, meta_low, meta_high, count, sems,
-    ) = refs[-13:]
+        send_low, send_high, tails, count, sems,
+    ) = refs[-11:]
     by_low, by_high = routes
     high, low = grid_of(devices)
     me = lax.axis_index("leaf")
@@ -102,8 +101,6 @@
         count[i] = 0
 
     tails[...] = jnp.zeros(tails.shape, F32)
-    meta_low[...] = jnp.full(meta_low.shape, leaves, F32)
-    meta_high[...] = jnp.full(meta_high.shape, leaves, F32)
     for copy in early:
         copy.wait()
     box = jnp.zeros((columns, rank), F32)
@@ -114,7 +111,9 @@
     packed = jnp.concatenate([box[:half], box[half:main]], axis=1).astype(BF16)
     last = jnp.concatenate([box[main:], jnp.zeros_like(box[main:])], axis=1)
 
-    lane = lax.broadcasted_iota(I32, (1, size), 1)
+    numbers = jnp.full((-(-(low + high) // 8) * 8, size), leaves, I32)
+    row = lax.broadcasted_iota(I32, numbers.shape, 0)
+    lane = lax.broadcasted_iota(I32, numbers.shape, 1)
     for j in range(leaves):
         if j % chunk == 0:
             arrivals[j // chunk].wait()
@@ -127,28 +126,32 @@
                 target = jnp.bitwise_xor(dest_ref[first + b, j], me)
                 slot = count[target]
                 count[target] = slot + 1
-                to_high, to_low = target // low, target % low
+                to_high = lax.shift_right_logical(target, low.bit_length() - 1)
+                to_low = jnp.bitwise_and(target, low - 1)
                 block = product[:, b * size : (b + 1) * size]
                 piece = block[:main].astype(BF16)
-                number = leaf_ref[first + b, j].astype(F32)
+                number = leaf_ref[first + b, j]
 
                 at = to_high * CAP + slot
                 rows = pl.ds(pl.multiple_of(at * by_low.rows, TILE), by_low.rows)
                 send_low[to_low, rows, :] = piece[: by_low.rows]
-                meta_low[to_low, 0:1, :] = jnp.where(lane == at, number, meta_low[to_low, 0:1, :])
+                numbers = jnp.where((row == to_low) & (lane == at), number, numbers)
 
                 at = to_low * CAP + slot
                 rows = pl.ds(pl.multiple_of(at * by_high.rows, TILE), by_high.rows)
                 send_high[to_high, rows, :] = piece[by_low.rows :]
                 tails[to_high, pl.ds(at, 1), :] = block[main:]
-                meta_high[to_high, 0:1, :] = jnp.where(lane == at, number, meta_high[to_high, 0:1, :])
-
+                numbers = jnp.where((row == low + to_high) & (lane == at), number, numbers)
+
+    numbers = numbers.astype(F32)
+    blank = jnp.zeros((TILE - 2, size), F32)
     for i in range(low):
-        send_low[i, by_low.meta : by_low.box, :] = meta_low[i].astype(BF16)
+        tile = jnp.concatenate([numbers[i : i + 1], last, blank], axis=0)
+        send_low[i, by_low.meta : by_low.box, :] = tile.astype(BF16)
     for i in range(high):
-        meta_high[i, 1:2, :] = last
+        tile = jnp.concatenate([numbers[low + i : low + i + 1], last, blank], axis=0)
         send_high[i, by_high.tails : by_high.meta, :] = tails[i].astype(BF16)
-        send_high[i, by_high.meta : by_high.box, :] = meta_high[i].astype(BF16)
+        send_high[i, by_high.meta : by_high.box, :] = tile.astype(BF16)
         send_high[i, by_high.box :, :] = packed
     leaving = [copies.start(send_low.at[i], outs[i]) for i in range(low)]
     leaving += [copies.start(send_high.at[i], outs[low + i]) for i in range(high)]
@@ -198,9 +201,10 @@
     sum_route(by_high, came[low:], outs[high:], low, leaf_ref, total_high, tails)
 
 
-def keep_kernel(own_low, own_high, kept_low, kept_high):
-    kept_low[...] = own_low[...]
-    kept_high[...] = own_high[...]
+def keep_kernel(*refs):
+    half = len(refs) // 2
+    for came, kept in zip(refs[:half], refs[half:]):
+        kept[...] = came[...]
 
 
 def local_kernel(probes_ref, local_ref, out_ref):
@@ -302,25 +306,21 @@
             stacked(low, message(by_low)),
             stacked(high, message(by_high)),
             pltpu.VMEM((high, by_high.meta - by_high.tails, size), F32),
-            pltpu.VMEM((low, TILE, size), F32),
-            pltpu.VMEM((high, TILE, size), F32),
             pltpu.SMEM((devices,), I32),
         ]
         + sems(7 + low + high),
         blocks * unit,
     )
     came_low, came_high = list(sent[:low]), list(sent[low:])
-    came_low[1] = relative(came_low[1], 1)
-    for k in range(max(low, high) - 1, 0, -1):
-        if 1 < k < low:
-            came_low[k] = relative(came_low[k], k)
-        if k < high:
-            came_high[k] = relative(came_high[k], k * low)
-    came_low[0], came_high[0] = call(
+    for k in range(low - 1, 0, -1):
+        came_low[k] = relative(came_low[k], k)
+    for k in range(high - 1, 0, -1):
+        came_high[k] = relative(came_high[k], k * low)
+    came_low[0], came_low[1], came_high[0] = call(
         keep_kernel,
-        (message(by_low), message(by_high)),
-        ([VMEM] * 2, (VMEM,) * 2),
-        (came_low[0], came_high[0]),
+        (message(by_low), message(by_low), message(by_high)),
+        ([VMEM] * 3, (VMEM,) * 3),
+        (came_low[0], came_low[1], came_high[0]),
         [],
         0,
         0,

time: 33.6 us -> 32.9 us (0.979)
  starting transfers between devices: 18.4 us -> 13.6 us
  waiting for transfers between devices: 4.64 us -> 8.8 us
    ppermute x12, starting transfers between devices: 18.4 us -> 13.6 us  [per_device(): lax.ppermute(x, 'leaf', [(i, i ^ way) for i in range(devices)])]
    ppermute x12, waiting for transfers between devices: 4.64 us -> 8.8 us  [per_device(): lax.ppermute(x, 'leaf', [(i, i ^ way) for i in range(devices)])]
  transfers between devices with their start and end apart: 12 -> 12, of which waited for: 5 -> 4; matrix products, arithmetic and copies ran while one was open for 0% -> 0% of each run, Pallas kernels for 9% -> 9%
where the time goes in v14:
time: 32.9 us; the launch traced here: 32.7 us
  starting transfers between devices  13.6 us (41%)
  waiting for transfers between devices  8.8 us (27%)
  Pallas kernels  8.4 us (26%)
  local copies, waits for them, and re-layouts  1.84 us (6%)
    ppermute x12, starting transfers between devices, per_device(): lax.ppermute(x, 'leaf', [(i, i ^ way) for i in range(devices)])  13.6 us
    ppermute x12, waiting for transfers between devices, per_device(): lax.ppermute(x, 'leaf', [(i, i ^ way) for i in range(devices)])  8.8 us
    pallas_call x6, Pallas kernels, call(): pl.pallas_call(kernel, out_shape=out_shape, in_specs=specs[0], out_specs=...  8.4 us
    unnamed x16, local copies, waits for them, and re-layouts  1.84 us
  transfers between devices with their start and end apart: 12, of which 4 were waited for; matrix products, arithmetic and copies ran while one was open for 0% of the time, Pallas kernels for 9%

profile of v14, /device:TPU:0, one launch (start us, length us, event | category | flops | bytes accessed | tf_op | source)
XLA Modules:
  0.0 32.7 jit_solution(11786808345876136762)
XLA Ops:
  0.0 3.4 %shard_map.91 = (bf16[784,128]{1,0:T(8,128)(2,1)}, bf16[784,128]{1,0:T(8,128)(2,1)}, bf16[784,128]{1,0:T(8,128)(2,1)}, bf16[784,128]{1,0:T(8,128)(2,1)}, bf16[32...) custom-call(s32[4,8]{1,0:T(4,128)} %bitcast.2, ...), custom_call_target="tpu_custom_call" | custom-call | flops 68157440 | bytes 2509056 | tf_op jit(solution)/shard_map/pallas_call | solution.py:265
  3.5 0.0 copy-start.2
  3.5 0.0 copy-start.3
  3.5 0.5 %collective-permute-start = (bf16[784,128]{1,0:T(8,128)(2,1)}, bf16[784,128]{1,0:T(8,128)(2,1)S(1)}, u32[]{:S(2)}, u32[]{:S(2)}) collective-permute-start(bf16[784,128]{1,0:T(8,128)(2,1)} %get-tuple-element.27), channel_id=1, source_target_pairs={{0,1},{1,0},{2,3},{3,2},{4,5},{5,4},{6,7},{7,6},{8,9},{9,8},{10,11... | collective-permute-start | bytes 602120 | tf_op jit(solution)/shard_map/ppermute | solution.py:290
  4.0 2.6 %collective-permute-start.1 = (bf16[784,128]{1,0:T(8,128)(2,1)}, bf16[784,128]{1,0:T(8,128)(2,1)S(1)}, u32[]{:S(2)}, u32[]{:S(2)}) collective-permute-start(bf16[784,128]{1,0:T(8,128)(2,1)} %get-tuple-element.31), channel_id=1, source_target_pairs={{0,2},{1,3},{2,0},{3,1},{4,6},{5,7},{6,4},{7,5},{8,10},{9,11},{10,... | collective-permute-start | bytes 602120 | tf_op jit(solution)/shard_map/ppermute | solution.py:290
  6.6 0.1 collective-permute-start.2
  6.7 1.8 %collective-permute-start.3 = (bf16[320,128]{1,0:T(8,128)(2,1)}, bf16[320,128]{1,0:T(8,128)(2,1)S(1)}, u32[]{:S(2)}, u32[]{:S(2)}) collective-permute-start(bf16[320,128]{1,0:T(8,128)(2,1)} %get-tuple-element.34), channel_id=1, source_target_pairs={{0,4},{1,5},{2,6},{3,7},{4,0},{5,1},{6,2},{7,3},{8,12},{9,13},{10,... | collective-permute-start | bytes 245768 | tf_op jit(solution)/shard_map/ppermute | solution.py:290
  8.4 2.6 %collective-permute-start.4 = (bf16[320,128]{1,0:T(8,128)(2,1)}, bf16[320,128]{1,0:T(8,128)(2,1)S(1)}, u32[]{:S(2)}, u32[]{:S(2)}) collective-permute-start(bf16[320,128]{1,0:T(8,128)(2,1)} %get-tuple-element.35), channel_id=1, source_target_pairs={{0,8},{1,9},{2,10},{3,11},{4,12},{5,13},{6,14},{7,15},{8,0},{9,1},... | collective-permute-start | bytes 245768 | tf_op jit(solution)/shard_map/ppermute | solution.py:290
  11.0 0.0 collective-permute-start.5
  11.1 0.9 %copy-done.4 = bf16[784,128]{1,0:T(8,128)(2,1)S(1)} copy-done((bf16[784,128]{1,0:T(8,128)(2,1)S(1)}, bf16[784,128]{1,0:T(8,128)(2,1)}, u32[]{:S(2)}) %copy-start.4) | copy-done | bytes 200728
  12.0 0.9 %copy-done.6 = bf16[320,128]{1,0:T(8,128)(2,1)S(1)} copy-done((bf16[320,128]{1,0:T(8,128)(2,1)S(1)}, bf16[320,128]{1,0:T(8,128)(2,1)}, u32[]{:S(2)}) %copy-start.6) | copy-done | bytes 81944
  12.9 5.2 %collective-permute-done.4.refs_6_ = bf16[320,128]{1,0:T(8,128)(2,1)S(1)} collective-permute-done((bf16[320,128]{1,0:T(8,128)(2,1)}, bf16[320,128]{1,0:T(8,128)(2,1)S(1)}, u32[]{:S(2)}, u32[]{:S(2)}) %collective-permute-start.4) | collective-permute-done | bytes 81952 | tf_op jit(solution)/shard_map/ppermute | solution.py:290
  18.1 1.2 %shard_map.93 = (bf16[384,128]{1,0:T(8,128)(2,1)S(1)}, bf16[384,128]{1,0:T(8,128)(2,1)S(1)}, bf16[384,128]{1,0:T(8,128)(2,1)S(1)}, bf16[384,128]{1,0:T(8,128)(2,...) custom-call(bf16[784,128]{1,0:T(8,128)(2,1)S(1)} %get-tuple-element., ...), custom_call_target="tpu_custom_call" | custom-call | flops 532480 | bytes 1802240 | tf_op jit(solution)/shard_map/pallas_call | solution.py:265
  19.3 0.1 collective-permute-start.6
  19.4 1.7 %collective-permute-start.9 = (bf16[384,128]{1,0:T(8,128)(2,1)S(1)}, bf16[384,128]{1,0:T(8,128)(2,1)S(1)}, u32[]{:S(2)}, u32[]{:S(2)}) collective-permute-start(bf16[384,128]{1,0:T(8,128)(2,1)S(1)} %get-tuple-element.44), channel_id=1, source_target_pairs={{0,4},{1,5},{2,6},{3,7},{4,0},{5,1},{6,2},{7,3},{8,12},{9,13},{10,... | collective-permute-start | bytes 294920 | tf_op jit(solution)/shard_map/ppermute | solution.py:290
  21.2 1.6 %collective-permute-start.10 = (bf16[384,128]{1,0:T(8,128)(2,1)S(1)}, bf16[384,128]{1,0:T(8,128)(2,1)S(1)}, u32[]{:S(2)}, u32[]{:S(2)}) collective-permute-start(bf16[384,128]{1,0:T(8,128)(2,1)S(1)} %get-tuple-element.45), channel_id=1, source_target_pairs={{0,8},{1,9},{2,10},{3,11},{4,12},{5,13},{6,14},{7,15},{8,0},{9,1},... | collective-permute-start | bytes 294920 | tf_op jit(solution)/shard_map/ppermute | solution.py:290
  22.8 1.1 %collective-permute-start.11 = (bf16[384,128]{1,0:T(8,128)(2,1)S(1)}, bf16[384,128]{1,0:T(8,128)(2,1)S(1)}, u32[]{:S(2)}, u32[]{:S(2)}) collective-permute-start(bf16[384,128]{1,0:T(8,128)(2,1)S(1)} %get-tuple-element.46), channel_id=1, source_target_pairs={{0,12},{1,13},{2,14},{3,15},{4,8},{5,9},{6,10},{7,11},{8,4},{9,5},... | collective-permute-start | bytes 294920 | tf_op jit(solution)/shard_map/ppermute | solution.py:290
  23.9 1.5 %collective-permute-start.7 = (bf16[272,128]{1,0:T(8,128)(2,1)S(1)}, bf16[272,128]{1,0:T(8,128)(2,1)S(1)}, u32[]{:S(2)}, u32[]{:S(2)}) collective-permute-start(bf16[272,128]{1,0:T(8,128)(2,1)S(1)} %get-tuple-element.41), channel_id=1, source_target_pairs={{0,2},{1,3},{2,0},{3,1},{4,6},{5,7},{6,4},{7,5},{8,10},{9,11},{10,... | collective-permute-start | bytes 208904 | tf_op jit(solution)/shard_map/ppermute | solution.py:290
  25.4 1.5 %shard_map.94.base_ref = f32[65,1024]{1,0:T(8,128)S(1)} custom-call(bf16[65,1024]{1,0:T(8,128)(2,1)S(1)} %copy-done.1, bf16[8,8,128,128]{3,2,1,0:T(8,128)(2,1)S(1)} %copy-done), custom_call_target="tpu_custom_call" | custom-call | flops 136314880 | bytes 2496512 | tf_op jit(solution)/shard_map/pallas_call | solution.py:265
  26.9 1.3 %collective-permute-done.7.refs_2_.refs_6_ = bf16[272,128]{1,0:T(8,128)(2,1)S(1)} collective-permute-done((bf16[272,128]{1,0:T(8,128)(2,1)S(1)}, bf16[272,128]{1,0:T(8,128)(2,1)S(1)}, u32[]{:S(2)}, u32[]{:S(2)}) %collective-permute-start.7) | collective-permute-done | bytes 69664 | tf_op jit(solution)/shard_map/ppermute | solution.py:290
  28.2 1.5 %collective-permute-done.8.refs_3_.refs_7_ = bf16[272,128]{1,0:T(8,128)(2,1)S(1)} collective-permute-done((bf16[272,128]{1,0:T(8,128)(2,1)S(1)}, bf16[272,128]{1,0:T(8,128)(2,1)S(1)}, u32[]{:S(2)}, u32[]{:S(2)}) %collective-permute-start.8) | collective-permute-done | bytes 69664 | tf_op jit(solution)/shard_map/ppermute | solution.py:290
  29.7 1.4 %shard_map.95.base_ref = f32[65,1024]{1,0:T(8,128)S(1)} custom-call(s32[1,12]{1,0:T(1,128)S(1)} %copy-done.7, f32[65,1024]{1,0:T(8,128)S(1)} %shard_map.94.base_ref, bf16[1,12,64,64]{3,2,1,0:T(8,128)(2,1)S(1)} %copy-done.5, bf16[8,64,64]{2,1,0:T(8,128)(2,1)S(1)} %copy-done.2, bf16[8,64,128]{2,1,0:T(8,128)(2,1)S(1)} %copy-done.3, ...), custom_call_target="tpu_custom_call" | custom-call | flops 68157440 | bytes 1105968 | tf_op jit(solution)/shard_map/pallas_call | solution.py:265
  31.1 0.8 %collective-permute-done.10.refs_2_ = bf16[384,128]{1,0:T(8,128)(2,1)S(1)} collective-permute-done((bf16[384,128]{1,0:T(8,128)(2,1)S(1)}, bf16[384,128]{1,0:T(8,128)(2,1)S(1)}, u32[]{:S(2)}, u32[]{:S(2)}) %collective-permute-start.10) | collective-permute-done | bytes 98336 | tf_op jit(solution)/shard_map/ppermute | solution.py:290
  31.9 0.8 %shard_map.96 = f32[65,1024]{1,0:T(8,128)} custom-call(f32[65,1024]{1,0:T(8,128)S(1)} %shard_map.95.base_ref, bf16[384,128]{1,0:T(8,128)(2,1)S(1)} %get-tuple-element.43.refs_0_, bf16[384,128]{1,0:T(8,128)(2,1)S(1)} %collective-permute-done.9.refs_1_, bf16[384,128]{1,0:T(8,128)(2,1)S(1)} %collective-permute-done.10.refs_2_, ...), custom_call_target="tpu_custom_call" | custom-call | flops 133120 | bytes 1204224 | tf_op jit(solution)/shard_map/pallas_call | solution.py:265
  (22 shorter events, 0.1 us)
Async XLA Ops:
  0.0 25.4 %copy-start.1 = (bf16[65,1024]{1,0:T(8,128)(2,1)S(1)}, bf16[65,1024]{1,0:T(8,128)(2,1)}, u32[]{:S(2)}) copy-start(bf16[65,1024]{1,0:T(8,128)(2,1)} %probes_ref) | copy-start | bytes 399364
  0.0 25.4 %copy-start = (bf16[8,8,128,128]{3,2,1,0:T(8,128)(2,1)S(1)}, bf16[8,8,128,128]{3,2,1,0:T(8,128)(2,1)}, u32[]{:S(2)}) copy-start(bf16[8,8,128,128]{3,2,1,0:T(8,128)(2,1)} %local_ref.1) | copy-start | bytes 6291460
  3.5 26.2 %copy-start.2 = (bf16[8,64,64]{2,1,0:T(8,128)(2,1)S(1)}, bf16[8,64,64]{2,1,0:T(8,128)(2,1)}, u32[]{:S(2)}) copy-start(bf16[8,64,64]{2,1,0:T(8,128)(2,1)} %transfer_ref.1) | copy-start | bytes 196612
  3.5 26.2 %copy-start.3 = (bf16[8,64,128]{2,1,0:T(8,128)(2,1)S(1)}, bf16[8,64,128]{2,1,0:T(8,128)(2,1)}, u32[]{:S(2)}) copy-start(bf16[8,64,128]{2,1,0:T(8,128)(2,1)} %basis_ref.1) | copy-start | bytes 393220
  3.5 7.6 %collective-permute-start = (bf16[784,128]{1,0:T(8,128)(2,1)}, bf16[784,128]{1,0:T(8,128)(2,1)S(1)}, u32[]{:S(2)}, u32[]{:S(2)}) collective-permute-start(bf16[784,128]{1,0:T(8,128)(2,1)} %get-tuple-element.27), channel_id=1, source_target_pairs={{0,1},{1,0},{2,3},{3,2},{4,5},{5,4},{6,7},{7,6},{8,9},{9,8},{10,11... | collective-permute-start | bytes 602120 | tf_op jit(solution)/shard_map/ppermute | solution.py:290
  4.0 14.1 %collective-permute-start.1 = (bf16[784,128]{1,0:T(8,128)(2,1)}, bf16[784,128]{1,0:T(8,128)(2,1)S(1)}, u32[]{:S(2)}, u32[]{:S(2)}) collective-permute-start(bf16[784,128]{1,0:T(8,128)(2,1)} %get-tuple-element.31), channel_id=1, source_target_pairs={{0,2},{1,3},{2,0},{3,1},{4,6},{5,7},{6,4},{7,5},{8,10},{9,11},{10,... | collective-permute-start | bytes 602120 | tf_op jit(solution)/shard_map/ppermute | solution.py:290
  6.6 11.6 %collective-permute-start.2 = (bf16[784,128]{1,0:T(8,128)(2,1)}, bf16[784,128]{1,0:T(8,128)(2,1)S(1)}, u32[]{:S(2)}, u32[]{:S(2)}) collective-permute-start(bf16[784,128]{1,0:T(8,128)(2,1)} %get-tuple-element.32), channel_id=1, source_target_pairs={{0,3},{1,2},{2,1},{3,0},{4,7},{5,6},{6,5},{7,4},{8,11},{9,10},{10,... | collective-permute-start | bytes 602120 | tf_op jit(solution)/shard_map/ppermute | solution.py:290
  6.7 6.3 %collective-permute-start.3 = (bf16[320,128]{1,0:T(8,128)(2,1)}, bf16[320,128]{1,0:T(8,128)(2,1)S(1)}, u32[]{:S(2)}, u32[]{:S(2)}) collective-permute-start(bf16[320,128]{1,0:T(8,128)(2,1)} %get-tuple-element.34), channel_id=1, source_target_pairs={{0,4},{1,5},{2,6},{3,7},{4,0},{5,1},{6,2},{7,3},{8,12},{9,13},{10,... | collective-permute-start | bytes 245768 | tf_op jit(solution)/shard_map/ppermute | solution.py:290
  8.4 9.7 %collective-permute-start.4 = (bf16[320,128]{1,0:T(8,128)(2,1)}, bf16[320,128]{1,0:T(8,128)(2,1)S(1)}, u32[]{:S(2)}, u32[]{:S(2)}) collective-permute-start(bf16[320,128]{1,0:T(8,128)(2,1)} %get-tuple-element.35), channel_id=1, source_target_pairs={{0,8},{1,9},{2,10},{3,11},{4,12},{5,13},{6,14},{7,15},{8,0},{9,1},... | collective-permute-start | bytes 245768 | tf_op jit(solution)/shard_map/ppermute | solution.py:290
  11.0 7.1 %collective-permute-start.5 = (bf16[320,128]{1,0:T(8,128)(2,1)}, bf16[320,128]{1,0:T(8,128)(2,1)S(1)}, u32[]{:S(2)}, u32[]{:S(2)}) collective-permute-start(bf16[320,128]{1,0:T(8,128)(2,1)} %get-tuple-element.36), channel_id=1, source_target_pairs={{0,12},{1,13},{2,14},{3,15},{4,8},{5,9},{6,10},{7,11},{8,4},{9,5},... | collective-permute-start | bytes 245768 | tf_op jit(solution)/shard_map/ppermute | solution.py:290
  11.0 0.9 %copy-start.4 = (bf16[784,128]{1,0:T(8,128)(2,1)S(1)}, bf16[784,128]{1,0:T(8,128)(2,1)}, u32[]{:S(2)}) copy-start(bf16[784,128]{1,0:T(8,128)(2,1)} %get-tuple-element.26.refs_0_) | copy-start | bytes 602116
  12.0 0.9 %copy-start.6 = (bf16[320,128]{1,0:T(8,128)(2,1)S(1)}, bf16[320,128]{1,0:T(8,128)(2,1)}, u32[]{:S(2)}) copy-start(bf16[320,128]{1,0:T(8,128)(2,1)} %get-tuple-element.28.refs_2_) | copy-start | bytes 245764
  12.9 16.8 %copy-start.5 = (bf16[1,12,64,64]{3,2,1,0:T(8,128)(2,1)S(1)}, bf16[1,12,64,64]{3,2,1,0:T(8,128)(2,1)}, u32[]{:S(2)}) copy-start(bf16[1,12,64,64]{3,2,1,0:T(8,128)(2,1)} %couplings_ref.1) | copy-start | bytes 294916
  12.9 16.8 %copy-start.7 = (s32[1,12]{1,0:T(1,128)S(1)}, s32[1,12]{1,0:T(1,128)}, u32[]{:S(2)}) copy-start(s32[1,12]{1,0:T(1,128)} %partner_ref.1) | copy-start | bytes 148
  19.3 6.0 %collective-permute-start.6 = (bf16[272,128]{1,0:T(8,128)(2,1)S(1)}, bf16[272,128]{1,0:T(8,128)(2,1)S(1)}, u32[]{:S(2)}, u32[]{:S(2)}) collective-permute-start(bf16[272,128]{1,0:T(8,128)(2,1)S(1)} %get-tuple-element.40), channel_id=1, source_target_pairs={{0,1},{1,0},{2,3},{3,2},{4,5},{5,4},{6,7},{7,6},{8,9},{9,8},{10,11... | collective-permute-start | bytes 208904 | tf_op jit(solution)/shard_map/ppermute | solution.py:290
  19.4 11.7 %collective-permute-start.9 = (bf16[384,128]{1,0:T(8,128)(2,1)S(1)}, bf16[384,128]{1,0:T(8,128)(2,1)S(1)}, u32[]{:S(2)}, u32[]{:S(2)}) collective-permute-start(bf16[384,128]{1,0:T(8,128)(2,1)S(1)} %get-tuple-element.44), channel_id=1, source_target_pairs={{0,4},{1,5},{2,6},{3,7},{4,0},{5,1},{6,2},{7,3},{8,12},{9,13},{10,... | collective-permute-start | bytes 294920 | tf_op jit(solution)/shard_map/ppermute | solution.py:290
  21.2 10.8 %collective-permute-start.10 = (bf16[384,128]{1,0:T(8,128)(2,1)S(1)}, bf16[384,128]{1,0:T(8,128)(2,1)S(1)}, u32[]{:S(2)}, u32[]{:S(2)}) collective-permute-start(bf16[384,128]{1,0:T(8,128)(2,1)S(1)} %get-tuple-element.45), channel_id=1, source_target_pairs={{0,8},{1,9},{2,10},{3,11},{4,12},{5,13},{6,14},{7,15},{8,0},{9,1},... | collective-permute-start | bytes 294920 | tf_op jit(solution)/shard_map/ppermute | solution.py:290
  22.8 9.2 %collective-permute-start.11 = (bf16[384,128]{1,0:T(8,128)(2,1)S(1)}, bf16[384,128]{1,0:T(8,128)(2,1)S(1)}, u32[]{:S(2)}, u32[]{:S(2)}) collective-permute-start(bf16[384,128]{1,0:T(8,128)(2,1)S(1)} %get-tuple-element.46), channel_id=1, source_target_pairs={{0,12},{1,13},{2,14},{3,15},{4,8},{5,9},{6,10},{7,11},{8,4},{9,5},... | collective-permute-start | bytes 294920 | tf_op jit(solution)/shard_map/ppermute | solution.py:290
  23.9 4.3 %collective-permute-start.7 = (bf16[272,128]{1,0:T(8,128)(2,1)S(1)}, bf16[272,128]{1,0:T(8,128)(2,1)S(1)}, u32[]{:S(2)}, u32[]{:S(2)}) collective-permute-start(bf16[272,128]{1,0:T(8,128)(2,1)S(1)} %get-tuple-element.41), channel_id=1, source_target_pairs={{0,2},{1,3},{2,0},{3,1},{4,6},{5,7},{6,4},{7,5},{8,10},{9,11},{10,... | collective-permute-start | bytes 208904 | tf_op jit(solution)/shard_map/ppermute | solution.py:290
  25.4 4.3 %collective-permute-start.8 = (bf16[272,128]{1,0:T(8,128)(2,1)S(1)}, bf16[272,128]{1,0:T(8,128)(2,1)S(1)}, u32[]{:S(2)}, u32[]{:S(2)}) collective-permute-start(bf16[272,128]{1,0:T(8,128)(2,1)S(1)} %get-tuple-element.42), channel_id=1, source_target_pairs={{0,3},{1,2},{2,1},{3,0},{4,7},{5,6},{6,5},{7,4},{8,11},{9,10},{10,... | collective-permute-start | bytes 208904 | tf_op jit(solution)/shard_map/ppermute | solution.py:290

commit v15 on v14

--- a/solution.py
+++ b/solution.py
@@ -312,9 +312,11 @@
         blocks * unit,
     )
     came_low, came_high = list(sent[:low]), list(sent[low:])
-    for k in range(low - 1, 0, -1):
+    ways_low = range(low - 1, 0, -1)
+    ways_high = [high - 1, *range(1, 2), *range(high - 2, 1, -1)]
+    for k in ways_low:
         came_low[k] = relative(came_low[k], k)
-    for k in range(high - 1, 0, -1):
+    for k in ways_high:
         came_high[k] = relative(came_high[k], k * low)
     came_low[0], came_low[1], came_high[0] = call(
         keep_kernel,
@@ -341,11 +343,10 @@
     )
     to_high, to_low = list(sums[:high]), list(sums[high:])
     probes_then, to_low[0] = lax.optimization_barrier((probes, to_low[0]))
-    for k in range(max(low, high) - 1, 0, -1):
-        if k < high:
-            to_high[k] = relative(to_high[k], k * low)
-        if k < low:
-            to_low[k] = relative(to_low[k], k)
+    for k in ways_high:
+        to_high[k] = relative(to_high[k], k * low)
+    for k in ways_low:
+        to_low[k] = relative(to_low[k], k)
 
     base_shape = jax.ShapeDtypeStruct((columns, points), F32)
     base = call(

time: 32.9 us -> 32.9 us (level)
  no operation moved by 1% of the time
where the time goes in v15:
time: 32.9 us; the launch traced here: 32.7 us
  starting transfers between devices  13.6 us (41%)
  waiting for transfers between devices  8.74 us (27%)
  Pallas kernels  8.4 us (26%)
  local copies, waits for them, and re-layouts  1.84 us (6%)
    ppermute x12, starting transfers between devices, per_device(): lax.ppermute(x, 'leaf', [(i, i ^ way) for i in range(devices)])  13.6 us
    ppermute x12, waiting for transfers between devices, per_device(): lax.ppermute(x, 'leaf', [(i, i ^ way) for i in range(devices)])  8.74 us
    pallas_call x6, Pallas kernels, call(): pl.pallas_call(kernel, out_shape=out_shape, in_specs=specs[0], out_specs=...  8.4 us
    unnamed x16, local copies, waits for them, and re-layouts  1.84 us
  transfers between devices with their start and end apart: 12, of which 4 were waited for; matrix products, arithmetic and copies ran while one was open for 0% of the time, Pallas kernels for 9%

profile of v15, /device:TPU:0, one launch (start us, length us, event | category | flops | bytes accessed | tf_op | source)
XLA Modules:
  0.0 32.7 jit_solution(11786808345876136762)
XLA Ops:
  0.0 3.4 %shard_map.91 = (bf16[784,128]{1,0:T(8,128)(2,1)}, bf16[784,128]{1,0:T(8,128)(2,1)}, bf16[784,128]{1,0:T(8,128)(2,1)}, bf16[784,128]{1,0:T(8,128)(2,1)}, bf16[32...) custom-call(s32[4,8]{1,0:T(4,128)} %bitcast.2, ...), custom_call_target="tpu_custom_call" | custom-call | flops 68157440 | bytes 2509056 | tf_op jit(solution)/shard_map/pallas_call | solution.py:265
  3.5 0.0 copy-start.2
  3.5 0.0 copy-start.3
  3.5 0.5 %collective-permute-start = (bf16[784,128]{1,0:T(8,128)(2,1)}, bf16[784,128]{1,0:T(8,128)(2,1)S(1)}, u32[]{:S(2)}, u32[]{:S(2)}) collective-permute-start(bf16[784,128]{1,0:T(8,128)(2,1)} %get-tuple-element.27), channel_id=1, source_target_pairs={{0,1},{1,0},{2,3},{3,2},{4,5},{5,4},{6,7},{7,6},{8,9},{9,8},{10,11... | collective-permute-start | bytes 602120 | tf_op jit(solution)/shard_map/ppermute | solution.py:290
  4.0 2.6 %collective-permute-start.1 = (bf16[784,128]{1,0:T(8,128)(2,1)}, bf16[784,128]{1,0:T(8,128)(2,1)S(1)}, u32[]{:S(2)}, u32[]{:S(2)}) collective-permute-start(bf16[784,128]{1,0:T(8,128)(2,1)} %get-tuple-element.31), channel_id=1, source_target_pairs={{0,2},{1,3},{2,0},{3,1},{4,6},{5,7},{6,4},{7,5},{8,10},{9,11},{10,... | collective-permute-start | bytes 602120 | tf_op jit(solution)/shard_map/ppermute | solution.py:290
  6.6 0.1 collective-permute-start.2
  6.7 1.8 %collective-permute-start.3 = (bf16[320,128]{1,0:T(8,128)(2,1)}, bf16[320,128]{1,0:T(8,128)(2,1)S(1)}, u32[]{:S(2)}, u32[]{:S(2)}) collective-permute-start(bf16[320,128]{1,0:T(8,128)(2,1)} %get-tuple-element.34), channel_id=1, source_target_pairs={{0,4},{1,5},{2,6},{3,7},{4,0},{5,1},{6,2},{7,3},{8,12},{9,13},{10,... | collective-permute-start | bytes 245768 | tf_op jit(solution)/shard_map/ppermute | solution.py:290
  8.4 2.6 %collective-permute-start.4 = (bf16[320,128]{1,0:T(8,128)(2,1)}, bf16[320,128]{1,0:T(8,128)(2,1)S(1)}, u32[]{:S(2)}, u32[]{:S(2)}) collective-permute-start(bf16[320,128]{1,0:T(8,128)(2,1)} %get-tuple-element.35), channel_id=1, source_target_pairs={{0,8},{1,9},{2,10},{3,11},{4,12},{5,13},{6,14},{7,15},{8,0},{9,1},... | collective-permute-start | bytes 245768 | tf_op jit(solution)/shard_map/ppermute | solution.py:290
  11.0 0.0 collective-permute-start.5
  11.1 0.9 %copy-done.4 = bf16[784,128]{1,0:T(8,128)(2,1)S(1)} copy-done((bf16[784,128]{1,0:T(8,128)(2,1)S(1)}, bf16[784,128]{1,0:T(8,128)(2,1)}, u32[]{:S(2)}) %copy-start.4) | copy-done | bytes 200728
  12.0 0.9 %copy-done.6 = bf16[320,128]{1,0:T(8,128)(2,1)S(1)} copy-done((bf16[320,128]{1,0:T(8,128)(2,1)S(1)}, bf16[320,128]{1,0:T(8,128)(2,1)}, u32[]{:S(2)}) %copy-start.6) | copy-done | bytes 81944
  12.9 5.2 %collective-permute-done.4.refs_6_ = bf16[320,128]{1,0:T(8,128)(2,1)S(1)} collective-permute-done((bf16[320,128]{1,0:T(8,128)(2,1)}, bf16[320,128]{1,0:T(8,128)(2,1)S(1)}, u32[]{:S(2)}, u32[]{:S(2)}) %collective-permute-start.4) | collective-permute-done | bytes 81952 | tf_op jit(solution)/shard_map/ppermute | solution.py:290
  18.1 1.2 %shard_map.93 = (bf16[384,128]{1,0:T(8,128)(2,1)S(1)}, bf16[384,128]{1,0:T(8,128)(2,1)S(1)}, bf16[384,128]{1,0:T(8,128)(2,1)S(1)}, bf16[384,128]{1,0:T(8,128)(2,...) custom-call(bf16[784,128]{1,0:T(8,128)(2,1)S(1)} %get-tuple-element., ...), custom_call_target="tpu_custom_call" | custom-call | flops 532480 | bytes 1802240 | tf_op jit(solution)/shard_map/pallas_call | solution.py:265
  19.3 0.1 collective-permute-start.6
  19.4 1.7 %collective-permute-start.9 = (bf16[384,128]{1,0:T(8,128)(2,1)S(1)}, bf16[384,128]{1,0:T(8,128)(2,1)S(1)}, u32[]{:S(2)}, u32[]{:S(2)}) collective-permute-start(bf16[384,128]{1,0:T(8,128)(2,1)S(1)} %get-tuple-element.44), channel_id=1, source_target_pairs={{0,4},{1,5},{2,6},{3,7},{4,0},{5,1},{6,2},{7,3},{8,12},{9,13},{10,... | collective-permute-start | bytes 294920 | tf_op jit(solution)/shard_map/ppermute | solution.py:290
  21.2 1.6 %collective-permute-start.10 = (bf16[384,128]{1,0:T(8,128)(2,1)S(1)}, bf16[384,128]{1,0:T(8,128)(2,1)S(1)}, u32[]{:S(2)}, u32[]{:S(2)}) collective-permute-start(bf16[384,128]{1,0:T(8,128)(2,1)S(1)} %get-tuple-element.45), channel_id=1, source_target_pairs={{0,8},{1,9},{2,10},{3,11},{4,12},{5,13},{6,14},{7,15},{8,0},{9,1},... | collective-permute-start | bytes 294920 | tf_op jit(solution)/shard_map/ppermute | solution.py:290
  22.8 1.1 %collective-permute-start.11 = (bf16[384,128]{1,0:T(8,128)(2,1)S(1)}, bf16[384,128]{1,0:T(8,128)(2,1)S(1)}, u32[]{:S(2)}, u32[]{:S(2)}) collective-permute-start(bf16[384,128]{1,0:T(8,128)(2,1)S(1)} %get-tuple-element.46), channel_id=1, source_target_pairs={{0,12},{1,13},{2,14},{3,15},{4,8},{5,9},{6,10},{7,11},{8,4},{9,5},... | collective-permute-start | bytes 294920 | tf_op jit(solution)/shard_map/ppermute | solution.py:290
  23.9 1.5 %collective-permute-start.7 = (bf16[272,128]{1,0:T(8,128)(2,1)S(1)}, bf16[272,128]{1,0:T(8,128)(2,1)S(1)}, u32[]{:S(2)}, u32[]{:S(2)}) collective-permute-start(bf16[272,128]{1,0:T(8,128)(2,1)S(1)} %get-tuple-element.41), channel_id=1, source_target_pairs={{0,2},{1,3},{2,0},{3,1},{4,6},{5,7},{6,4},{7,5},{8,10},{9,11},{10,... | collective-permute-start | bytes 208904 | tf_op jit(solution)/shard_map/ppermute | solution.py:290
  25.4 1.5 %shard_map.94.base_ref = f32[65,1024]{1,0:T(8,128)S(1)} custom-call(bf16[65,1024]{1,0:T(8,128)(2,1)S(1)} %copy-done.1, bf16[8,8,128,128]{3,2,1,0:T(8,128)(2,1)S(1)} %copy-done), custom_call_target="tpu_custom_call" | custom-call | flops 136314880 | bytes 2496512 | tf_op jit(solution)/shard_map/pallas_call | solution.py:265
  26.9 1.2 %collective-permute-done.7.refs_2_.refs_6_ = bf16[272,128]{1,0:T(8,128)(2,1)S(1)} collective-permute-done((bf16[272,128]{1,0:T(8,128)(2,1)S(1)}, bf16[272,128]{1,0:T(8,128)(2,1)S(1)}, u32[]{:S(2)}, u32[]{:S(2)}) %collective-permute-start.7) | collective-permute-done | bytes 69664 | tf_op jit(solution)/shard_map/ppermute | solution.py:290
  28.2 1.5 %collective-permute-done.8.refs_3_.refs_7_ = bf16[272,128]{1,0:T(8,128)(2,1)S(1)} collective-permute-done((bf16[272,128]{1,0:T(8,128)(2,1)S(1)}, bf16[272,128]{1,0:T(8,128)(2,1)S(1)}, u32[]{:S(2)}, u32[]{:S(2)}) %collective-permute-start.8) | collective-permute-done | bytes 69664 | tf_op jit(solution)/shard_map/ppermute | solution.py:290
  29.7 1.4 %shard_map.95.base_ref = f32[65,1024]{1,0:T(8,128)S(1)} custom-call(s32[1,12]{1,0:T(1,128)S(1)} %copy-done.7, f32[65,1024]{1,0:T(8,128)S(1)} %shard_map.94.base_ref, bf16[1,12,64,64]{3,2,1,0:T(8,128)(2,1)S(1)} %copy-done.5, bf16[8,64,64]{2,1,0:T(8,128)(2,1)S(1)} %copy-done.2, bf16[8,64,128]{2,1,0:T(8,128)(2,1)S(1)} %copy-done.3, ...), custom_call_target="tpu_custom_call" | custom-call | flops 68157440 | bytes 1105968 | tf_op jit(solution)/shard_map/pallas_call | solution.py:265
  31.1 0.8 %collective-permute-done.10.refs_2_ = bf16[384,128]{1,0:T(8,128)(2,1)S(1)} collective-permute-done((bf16[384,128]{1,0:T(8,128)(2,1)S(1)}, bf16[384,128]{1,0:T(8,128)(2,1)S(1)}, u32[]{:S(2)}, u32[]{:S(2)}) %collective-permute-start.10) | collective-permute-done | bytes 98336 | tf_op jit(solution)/shard_map/ppermute | solution.py:290
  31.9 0.8 %shard_map.96 = f32[65,1024]{1,0:T(8,128)} custom-call(f32[65,1024]{1,0:T(8,128)S(1)} %shard_map.95.base_ref, bf16[384,128]{1,0:T(8,128)(2,1)S(1)} %get-tuple-element.43.refs_0_, bf16[384,128]{1,0:T(8,128)(2,1)S(1)} %collective-permute-done.9.refs_1_, bf16[384,128]{1,0:T(8,128)(2,1)S(1)} %collective-permute-done.10.refs_2_, ...), custom_call_target="tpu_custom_call" | custom-call | flops 133120 | bytes 1204224 | tf_op jit(solution)/shard_map/pallas_call | solution.py:265
  (22 shorter events, 0.1 us)
Async XLA Ops:
  0.0 25.4 %copy-start.1 = (bf16[65,1024]{1,0:T(8,128)(2,1)S(1)}, bf16[65,1024]{1,0:T(8,128)(2,1)}, u32[]{:S(2)}) copy-start(bf16[65,1024]{1,0:T(8,128)(2,1)} %probes_ref) | copy-start | bytes 399364
  0.0 25.4 %copy-start = (bf16[8,8,128,128]{3,2,1,0:T(8,128)(2,1)S(1)}, bf16[8,8,128,128]{3,2,1,0:T(8,128)(2,1)}, u32[]{:S(2)}) copy-start(bf16[8,8,128,128]{3,2,1,0:T(8,128)(2,1)} %local_ref.1) | copy-start | bytes 6291460
  3.5 26.2 %copy-start.2 = (bf16[8,64,64]{2,1,0:T(8,128)(2,1)S(1)}, bf16[8,64,64]{2,1,0:T(8,128)(2,1)}, u32[]{:S(2)}) copy-start(bf16[8,64,64]{2,1,0:T(8,128)(2,1)} %transfer_ref.1) | copy-start | bytes 196612
  3.5 26.2 %copy-start.3 = (bf16[8,64,128]{2,1,0:T(8,128)(2,1)S(1)}, bf16[8,64,128]{2,1,0:T(8,128)(2,1)}, u32[]{:S(2)}) copy-start(bf16[8,64,128]{2,1,0:T(8,128)(2,1)} %basis_ref.1) | copy-start | bytes 393220
  3.5 7.6 %collective-permute-start = (bf16[784,128]{1,0:T(8,128)(2,1)}, bf16[784,128]{1,0:T(8,128)(2,1)S(1)}, u32[]{:S(2)}, u32[]{:S(2)}) collective-permute-start(bf16[784,128]{1,0:T(8,128)(2,1)} %get-tuple-element.27), channel_id=1, source_target_pairs={{0,1},{1,0},{2,3},{3,2},{4,5},{5,4},{6,7},{7,6},{8,9},{9,8},{10,11... | collective-permute-start | bytes 602120 | tf_op jit(solution)/shard_map/ppermute | solution.py:290
  4.0 14.1 %collective-permute-start.1 = (bf16[784,128]{1,0:T(8,128)(2,1)}, bf16[784,128]{1,0:T(8,128)(2,1)S(1)}, u32[]{:S(2)}, u32[]{:S(2)}) collective-permute-start(bf16[784,128]{1,0:T(8,128)(2,1)} %get-tuple-element.31), channel_id=1, source_target_pairs={{0,2},{1,3},{2,0},{3,1},{4,6},{5,7},{6,4},{7,5},{8,10},{9,11},{10,... | collective-permute-start | bytes 602120 | tf_op jit(solution)/shard_map/ppermute | solution.py:290
  6.6 11.6 %collective-permute-start.2 = (bf16[784,128]{1,0:T(8,128)(2,1)}, bf16[784,128]{1,0:T(8,128)(2,1)S(1)}, u32[]{:S(2)}, u32[]{:S(2)}) collective-permute-start(bf16[784,128]{1,0:T(8,128)(2,1)} %get-tuple-element.32), channel_id=1, source_target_pairs={{0,3},{1,2},{2,1},{3,0},{4,7},{5,6},{6,5},{7,4},{8,11},{9,10},{10,... | collective-permute-start | bytes 602120 | tf_op jit(solution)/shard_map/ppermute | solution.py:290
  6.7 6.3 %collective-permute-start.3 = (bf16[320,128]{1,0:T(8,128)(2,1)}, bf16[320,128]{1,0:T(8,128)(2,1)S(1)}, u32[]{:S(2)}, u32[]{:S(2)}) collective-permute-start(bf16[320,128]{1,0:T(8,128)(2,1)} %get-tuple-element.34), channel_id=1, source_target_pairs={{0,4},{1,5},{2,6},{3,7},{4,0},{5,1},{6,2},{7,3},{8,12},{9,13},{10,... | collective-permute-start | bytes 245768 | tf_op jit(solution)/shard_map/ppermute | solution.py:290
  8.4 9.7 %collective-permute-start.4 = (bf16[320,128]{1,0:T(8,128)(2,1)}, bf16[320,128]{1,0:T(8,128)(2,1)S(1)}, u32[]{:S(2)}, u32[]{:S(2)}) collective-permute-start(bf16[320,128]{1,0:T(8,128)(2,1)} %get-tuple-element.35), channel_id=1, source_target_pairs={{0,8},{1,9},{2,10},{3,11},{4,12},{5,13},{6,14},{7,15},{8,0},{9,1},... | collective-permute-start | bytes 245768 | tf_op jit(solution)/shard_map/ppermute | solution.py:290
  11.0 7.1 %collective-permute-start.5 = (bf16[320,128]{1,0:T(8,128)(2,1)}, bf16[320,128]{1,0:T(8,128)(2,1)S(1)}, u32[]{:S(2)}, u32[]{:S(2)}) collective-permute-start(bf16[320,128]{1,0:T(8,128)(2,1)} %get-tuple-element.36), channel_id=1, source_target_pairs={{0,12},{1,13},{2,14},{3,15},{4,8},{5,9},{6,10},{7,11},{8,4},{9,5},... | collective-permute-start | bytes 245768 | tf_op jit(solution)/shard_map/ppermute | solution.py:290
  11.0 0.9 %copy-start.4 = (bf16[784,128]{1,0:T(8,128)(2,1)S(1)}, bf16[784,128]{1,0:T(8,128)(2,1)}, u32[]{:S(2)}) copy-start(bf16[784,128]{1,0:T(8,128)(2,1)} %get-tuple-element.26.refs_0_) | copy-start | bytes 602116
  12.0 0.9 %copy-start.6 = (bf16[320,128]{1,0:T(8,128)(2,1)S(1)}, bf16[320,128]{1,0:T(8,128)(2,1)}, u32[]{:S(2)}) copy-start(bf16[320,128]{1,0:T(8,128)(2,1)} %get-tuple-element.28.refs_2_) | copy-start | bytes 245764
  12.9 16.8 %copy-start.5 = (bf16[1,12,64,64]{3,2,1,0:T(8,128)(2,1)S(1)}, bf16[1,12,64,64]{3,2,1,0:T(8,128)(2,1)}, u32[]{:S(2)}) copy-start(bf16[1,12,64,64]{3,2,1,0:T(8,128)(2,1)} %couplings_ref.1) | copy-start | bytes 294916
  12.9 16.8 %copy-start.7 = (s32[1,12]{1,0:T(1,128)S(1)}, s32[1,12]{1,0:T(1,128)}, u32[]{:S(2)}) copy-start(s32[1,12]{1,0:T(1,128)} %partner_ref.1) | copy-start | bytes 148
  19.3 6.1 %collective-permute-start.6 = (bf16[272,128]{1,0:T(8,128)(2,1)S(1)}, bf16[272,128]{1,0:T(8,128)(2,1)S(1)}, u32[]{:S(2)}, u32[]{:S(2)}) collective-permute-start(bf16[272,128]{1,0:T(8,128)(2,1)S(1)} %get-tuple-element.40), channel_id=1, source_target_pairs={{0,1},{1,0},{2,3},{3,2},{4,5},{5,4},{6,7},{7,6},{8,9},{9,8},{10,11... | collective-permute-start | bytes 208904 | tf_op jit(solution)/shard_map/ppermute | solution.py:290
  19.4 11.7 %collective-permute-start.9 = (bf16[384,128]{1,0:T(8,128)(2,1)S(1)}, bf16[384,128]{1,0:T(8,128)(2,1)S(1)}, u32[]{:S(2)}, u32[]{:S(2)}) collective-permute-start(bf16[384,128]{1,0:T(8,128)(2,1)S(1)} %get-tuple-element.44), channel_id=1, source_target_pairs={{0,4},{1,5},{2,6},{3,7},{4,0},{5,1},{6,2},{7,3},{8,12},{9,13},{10,... | collective-permute-start | bytes 294920 | tf_op jit(solution)/shard_map/ppermute | solution.py:290
  21.2 10.8 %collective-permute-start.10 = (bf16[384,128]{1,0:T(8,128)(2,1)S(1)}, bf16[384,128]{1,0:T(8,128)(2,1)S(1)}, u32[]{:S(2)}, u32[]{:S(2)}) collective-permute-start(bf16[384,128]{1,0:T(8,128)(2,1)S(1)} %get-tuple-element.45), channel_id=1, source_target_pairs={{0,8},{1,9},{2,10},{3,11},{4,12},{5,13},{6,14},{7,15},{8,0},{9,1},... | collective-permute-start | bytes 294920 | tf_op jit(solution)/shard_map/ppermute | solution.py:290
  22.8 9.1 %collective-permute-start.11 = (bf16[384,128]{1,0:T(8,128)(2,1)S(1)}, bf16[384,128]{1,0:T(8,128)(2,1)S(1)}, u32[]{:S(2)}, u32[]{:S(2)}) collective-permute-start(bf16[384,128]{1,0:T(8,128)(2,1)S(1)} %get-tuple-element.46), channel_id=1, source_target_pairs={{0,12},{1,13},{2,14},{3,15},{4,8},{5,9},{6,10},{7,11},{8,4},{9,5},... | collective-permute-start | bytes 294920 | tf_op jit(solution)/shard_map/ppermute | solution.py:290
  23.9 4.3 %collective-permute-start.7 = (bf16[272,128]{1,0:T(8,128)(2,1)S(1)}, bf16[272,128]{1,0:T(8,128)(2,1)S(1)}, u32[]{:S(2)}, u32[]{:S(2)}) collective-permute-start(bf16[272,128]{1,0:T(8,128)(2,1)S(1)} %get-tuple-element.41), channel_id=1, source_target_pairs={{0,2},{1,3},{2,0},{3,1},{4,6},{5,7},{6,4},{7,5},{8,10},{9,11},{10,... | collective-permute-start | bytes 208904 | tf_op jit(solution)/shard_map/ppermute | solution.py:290
  25.4 4.3 %collective-permute-start.8 = (bf16[272,128]{1,0:T(8,128)(2,1)S(1)}, bf16[272,128]{1,0:T(8,128)(2,1)S(1)}, u32[]{:S(2)}, u32[]{:S(2)}) collective-permute-start(bf16[272,128]{1,0:T(8,128)(2,1)S(1)} %get-tuple-element.42), channel_id=1, source_target_pairs={{0,3},{1,2},{2,1},{3,0},{4,7},{5,6},{6,5},{7,4},{8,11},{9,10},{10,... | collective-permute-start | bytes 208904 | tf_op jit(solution)/shard_map/ppermute | solution.py:290

commit v16 on v15

--- a/solution.py
+++ b/solution.py
@@ -159,7 +159,7 @@
         copy.wait()
 
 
-def sum_route(route, came, outs, base, leaf_ref, total, tails):
+def sum_route(route, came, planes, outs, base, leaf_ref, total, tails):
     leaves, half, ways = route.leaves, route.half, len(came)
     for i in range(ways):
         if route.extra:
@@ -178,10 +178,15 @@
         if route.extra:
             for i in range(ways):
                 last = came[i][route.meta : route.box, :].astype(F32)[1:2]
-                tails[k, leaves + i : leaves + i + 1, :] = last
-                start = route.dense_box + i * half
+                at = planes[i]
+                tails[k, leaves + at : leaves + at + 1, :] = last
+                start = route.dense_box + at * half
                 outs[k][start : start + half, :] = came[i][route.box :, :]
             outs[k][route.dense_tails : route.dense_box, :] = tails[k].astype(BF16)
+
+
+def across_first(high):
+    return [0, *range(2, high), 1]
 
 
 def sum_kernel(routes, devices, *refs):
@@ -197,8 +202,8 @@
     for ref in (total_low, total_high, tails):
         ref[...] = jnp.zeros(ref.shape, F32)
     numbers.wait()
-    sum_route(by_low, came[:low], outs[:high], 0, leaf_ref, total_low, None)
-    sum_route(by_high, came[low:], outs[high:], low, leaf_ref, total_high, tails)
+    sum_route(by_low, came[:low], None, outs[:high], 0, leaf_ref, total_low, None)
+    sum_route(by_high, came[low:], across_first(high), outs[high:], low, leaf_ref, total_high, tails)
 
 
 def keep_kernel(*refs):
@@ -312,11 +317,10 @@
         blocks * unit,
     )
     came_low, came_high = list(sent[:low]), list(sent[low:])
-    ways_low = range(low - 1, 0, -1)
-    ways_high = [high - 1, *range(1, 2), *range(high - 2, 1, -1)]
-    for k in ways_low:
+    planes = across_first(high)
+    for k in range(1, low):
         came_low[k] = relative(came_low[k], k)
-    for k in ways_high:
+    for k in planes[1:]:
         came_high[k] = relative(came_high[k], k * low)
     came_low[0], came_low[1], came_high[0] = call(
         keep_kernel,
@@ -334,7 +338,7 @@
         functools.partial(sum_kernel, routes, devices),
         [dense(by_low)] * high + [dense(by_high)] * low,
         ([VMEM] * (low + high), [VMEM] * (low + high)),
-        (*came_low, *came_high),
+        (*came_low, *(came_high[k] for k in planes)),
         [pltpu.VMEM((low + high, size), I32), pltpu.SMEM((low + high, size), I32)]
         + like(total(by_low), total(by_high), tails)
         + [pltpu.SemaphoreType.DMA(())],
@@ -343,9 +347,9 @@
     )
     to_high, to_low = list(sums[:high]), list(sums[high:])
     probes_then, to_low[0] = lax.optimization_barrier((probes, to_low[0]))
-    for k in ways_high:
+    for k in planes[1:]:
         to_high[k] = relative(to_high[k], k * low)
-    for k in ways_low:
+    for k in range(1, low):
         to_low[k] = relative(to_low[k], k)
 
     base_shape = jax.ShapeDtypeStruct((columns, points), F32)
@@ -366,7 +370,7 @@
         functools.partial(last_kernel, routes, devices),
         base_shape,
         ([VMEM] * (1 + high + low), VMEM),
-        (base, *to_high, *to_low),
+        (base, *(to_high[k] for k in planes), *to_low),
         [],
         devices * columns * size,
         0,

time: 32.9 us -> 31.8 us (0.967)
  waiting for transfers between devices: 8.74 us -> 8.09 us
    ppermute x12, waiting for transfers between devices: 8.74 us -> 8.09 us  [per_device(): lax.ppermute(x, 'leaf', [(i, i ^ way) for i in range(devices)])]
    ppermute x12, starting transfers between devices: 13.6 us -> 13.3 us  [per_device(): lax.ppermute(x, 'leaf', [(i, i ^ way) for i in range(devices)])]
  transfers between devices with their start and end apart: 12 -> 12, of which waited for: 4 -> 6; matrix products, arithmetic and copies ran while one was open for 0% -> 0% of each run, Pallas kernels for 9% -> 9%
where the time goes in v16:
time: 31.8 us; the launch traced here: 31.7 us
  starting transfers between devices  13.3 us (42%)
  Pallas kernels  8.37 us (26%)
  waiting for transfers between devices  8.09 us (25%)
  local copies, waits for them, and re-layouts  1.84 us (6%)
    ppermute x12, starting transfers between devices, per_device(): lax.ppermute(x, 'leaf', [(i, i ^ way) for i in range(devices)])  13.3 us
    pallas_call x6, Pallas kernels, call(): pl.pallas_call(kernel, out_shape=out_shape, in_specs=specs[0], out_specs=...  8.37 us
    ppermute x12, waiting for transfers between devices, per_device(): lax.ppermute(x, 'leaf', [(i, i ^ way) for i in range(devices)])  8.09 us
    unnamed x16, local copies, waits for them, and re-layouts  1.84 us
  transfers between devices with their start and end apart: 12, of which 6 were waited for; matrix products, arithmetic and copies ran while one was open for 0% of the time, Pallas kernels for 9%

profile of v16, /device:TPU:0, one launch (start us, length us, event | category | flops | bytes accessed | tf_op | source)
XLA Modules:
  0.0 31.7 jit_solution(7081225356924037328)
XLA Ops:
  0.0 3.4 %shard_map.91 = (bf16[784,128]{1,0:T(8,128)(2,1)}, bf16[784,128]{1,0:T(8,128)(2,1)}, bf16[784,128]{1,0:T(8,128)(2,1)}, bf16[784,128]{1,0:T(8,128)(2,1)}, bf16[32...) custom-call(s32[4,8]{1,0:T(4,128)} %bitcast.2, ...), custom_call_target="tpu_custom_call" | custom-call | flops 68157440 | bytes 2509056 | tf_op jit(solution)/shard_map/pallas_call | solution.py:270
  3.5 0.5 %collective-permute-start = (bf16[784,128]{1,0:T(8,128)(2,1)}, bf16[784,128]{1,0:T(8,128)(2,1)S(1)}, u32[]{:S(2)}, u32[]{:S(2)}) collective-permute-start(bf16[784,128]{1,0:T(8,128)(2,1)} %get-tuple-element.27), channel_id=1, source_target_pairs={{0,1},{1,0},{2,3},{3,2},{4,5},{5,4},{6,7},{7,6},{8,9},{9,8},{10,11... | collective-permute-start | bytes 602120 | tf_op jit(solution)/shard_map/ppermute | solution.py:295
  4.0 2.6 %collective-permute-start.1 = (bf16[784,128]{1,0:T(8,128)(2,1)}, bf16[784,128]{1,0:T(8,128)(2,1)S(1)}, u32[]{:S(2)}, u32[]{:S(2)}) collective-permute-start(bf16[784,128]{1,0:T(8,128)(2,1)} %get-tuple-element.31), channel_id=1, source_target_pairs={{0,2},{1,3},{2,0},{3,1},{4,6},{5,7},{6,4},{7,5},{8,10},{9,11},{10,... | collective-permute-start | bytes 602120 | tf_op jit(solution)/shard_map/ppermute | solution.py:295
  6.6 0.1 collective-permute-start.2
  6.7 2.8 %collective-permute-start.3 = (bf16[320,128]{1,0:T(8,128)(2,1)}, bf16[320,128]{1,0:T(8,128)(2,1)S(1)}, u32[]{:S(2)}, u32[]{:S(2)}) collective-permute-start(bf16[320,128]{1,0:T(8,128)(2,1)} %get-tuple-element.34), channel_id=1, source_target_pairs={{0,8},{1,9},{2,10},{3,11},{4,12},{5,13},{6,14},{7,15},{8,0},{9,1},... | collective-permute-start | bytes 245768 | tf_op jit(solution)/shard_map/ppermute | solution.py:295
  9.5 1.3 %collective-permute-start.4 = (bf16[320,128]{1,0:T(8,128)(2,1)}, bf16[320,128]{1,0:T(8,128)(2,1)S(1)}, u32[]{:S(2)}, u32[]{:S(2)}) collective-permute-start(bf16[320,128]{1,0:T(8,128)(2,1)} %get-tuple-element.35), channel_id=1, source_target_pairs={{0,12},{1,13},{2,14},{3,15},{4,8},{5,9},{6,10},{7,11},{8,4},{9,5},... | collective-permute-start | bytes 245768 | tf_op jit(solution)/shard_map/ppermute | solution.py:295
  10.8 0.2 collective-permute-start.5
  11.0 0.9 %copy-done.4 = bf16[784,128]{1,0:T(8,128)(2,1)S(1)} copy-done((bf16[784,128]{1,0:T(8,128)(2,1)S(1)}, bf16[784,128]{1,0:T(8,128)(2,1)}, u32[]{:S(2)}) %copy-start.4) | copy-done | bytes 200728
  12.0 0.9 %copy-done.6 = bf16[320,128]{1,0:T(8,128)(2,1)S(1)} copy-done((bf16[320,128]{1,0:T(8,128)(2,1)S(1)}, bf16[320,128]{1,0:T(8,128)(2,1)}, u32[]{:S(2)}) %copy-start.6) | copy-done | bytes 81944
  12.9 3.4 %collective-permute-done.3.refs_5_ = bf16[320,128]{1,0:T(8,128)(2,1)S(1)} collective-permute-done((bf16[320,128]{1,0:T(8,128)(2,1)}, bf16[320,128]{1,0:T(8,128)(2,1)S(1)}, u32[]{:S(2)}, u32[]{:S(2)}) %collective-permute-start.3) | collective-permute-done | bytes 81952 | tf_op jit(solution)/shard_map/ppermute | solution.py:295
  16.3 0.5 %collective-permute-done.4.refs_6_ = bf16[320,128]{1,0:T(8,128)(2,1)S(1)} collective-permute-done((bf16[320,128]{1,0:T(8,128)(2,1)}, bf16[320,128]{1,0:T(8,128)(2,1)S(1)}, u32[]{:S(2)}, u32[]{:S(2)}) %collective-permute-start.4) | collective-permute-done | bytes 81952 | tf_op jit(solution)/shard_map/ppermute | solution.py:295
  16.8 0.7 %collective-permute-done.5.refs_7_ = bf16[320,128]{1,0:T(8,128)(2,1)S(1)} collective-permute-done((bf16[320,128]{1,0:T(8,128)(2,1)}, bf16[320,128]{1,0:T(8,128)(2,1)S(1)}, u32[]{:S(2)}, u32[]{:S(2)}) %collective-permute-start.5) | collective-permute-done | bytes 81952 | tf_op jit(solution)/shard_map/ppermute | solution.py:295
  17.5 1.2 %shard_map.93 = (bf16[384,128]{1,0:T(8,128)(2,1)S(1)}, bf16[384,128]{1,0:T(8,128)(2,1)S(1)}, bf16[384,128]{1,0:T(8,128)(2,1)S(1)}, bf16[384,128]{1,0:T(8,128)(2,...) custom-call(bf16[784,128]{1,0:T(8,128)(2,1)S(1)} %get-tuple-element., ...), custom_call_target="tpu_custom_call" | custom-call | flops 532480 | bytes 1802240 | tf_op jit(solution)/shard_map/pallas_call | solution.py:270
  18.7 0.1 collective-permute-start.6
  18.8 3.1 %collective-permute-start.9 = (bf16[384,128]{1,0:T(8,128)(2,1)S(1)}, bf16[384,128]{1,0:T(8,128)(2,1)S(1)}, u32[]{:S(2)}, u32[]{:S(2)}) collective-permute-start(bf16[384,128]{1,0:T(8,128)(2,1)S(1)} %get-tuple-element.44), channel_id=1, source_target_pairs={{0,8},{1,9},{2,10},{3,11},{4,12},{5,13},{6,14},{7,15},{8,0},{9,1},... | collective-permute-start | bytes 294920 | tf_op jit(solution)/shard_map/ppermute | solution.py:295
  21.9 0.5 %collective-permute-start.10 = (bf16[384,128]{1,0:T(8,128)(2,1)S(1)}, bf16[384,128]{1,0:T(8,128)(2,1)S(1)}, u32[]{:S(2)}, u32[]{:S(2)}) collective-permute-start(bf16[384,128]{1,0:T(8,128)(2,1)S(1)} %get-tuple-element.45), channel_id=1, source_target_pairs={{0,12},{1,13},{2,14},{3,15},{4,8},{5,9},{6,10},{7,11},{8,4},{9,5},... | collective-permute-start | bytes 294920 | tf_op jit(solution)/shard_map/ppermute | solution.py:295
  22.4 0.4 %collective-permute-start.11 = (bf16[384,128]{1,0:T(8,128)(2,1)S(1)}, bf16[384,128]{1,0:T(8,128)(2,1)S(1)}, u32[]{:S(2)}, u32[]{:S(2)}) collective-permute-start(bf16[384,128]{1,0:T(8,128)(2,1)S(1)} %get-tuple-element.46), channel_id=1, source_target_pairs={{0,4},{1,5},{2,6},{3,7},{4,0},{5,1},{6,2},{7,3},{8,12},{9,13},{10,... | collective-permute-start | bytes 294920 | tf_op jit(solution)/shard_map/ppermute | solution.py:295
  22.9 1.5 %collective-permute-start.7 = (bf16[272,128]{1,0:T(8,128)(2,1)S(1)}, bf16[272,128]{1,0:T(8,128)(2,1)S(1)}, u32[]{:S(2)}, u32[]{:S(2)}) collective-permute-start(bf16[272,128]{1,0:T(8,128)(2,1)S(1)} %get-tuple-element.41), channel_id=1, source_target_pairs={{0,2},{1,3},{2,0},{3,1},{4,6},{5,7},{6,4},{7,5},{8,10},{9,11},{10,... | collective-permute-start | bytes 208904 | tf_op jit(solution)/shard_map/ppermute | solution.py:295
  24.4 1.5 %shard_map.94.base_ref = f32[65,1024]{1,0:T(8,128)S(1)} custom-call(bf16[65,1024]{1,0:T(8,128)(2,1)S(1)} %copy-done.1, bf16[8,8,128,128]{3,2,1,0:T(8,128)(2,1)S(1)} %copy-done), custom_call_target="tpu_custom_call" | custom-call | flops 136314880 | bytes 2496512 | tf_op jit(solution)/shard_map/pallas_call | solution.py:270
  25.9 1.2 %collective-permute-done.7.refs_2_.refs_6_ = bf16[272,128]{1,0:T(8,128)(2,1)S(1)} collective-permute-done((bf16[272,128]{1,0:T(8,128)(2,1)S(1)}, bf16[272,128]{1,0:T(8,128)(2,1)S(1)}, u32[]{:S(2)}, u32[]{:S(2)}) %collective-permute-start.7) | collective-permute-done | bytes 69664 | tf_op jit(solution)/shard_map/ppermute | solution.py:295
  27.2 1.5 %collective-permute-done.8.refs_3_.refs_7_ = bf16[272,128]{1,0:T(8,128)(2,1)S(1)} collective-permute-done((bf16[272,128]{1,0:T(8,128)(2,1)S(1)}, bf16[272,128]{1,0:T(8,128)(2,1)S(1)}, u32[]{:S(2)}, u32[]{:S(2)}) %collective-permute-start.8) | collective-permute-done | bytes 69664 | tf_op jit(solution)/shard_map/ppermute | solution.py:295
  28.7 1.4 %shard_map.95.base_ref = f32[65,1024]{1,0:T(8,128)S(1)} custom-call(s32[1,12]{1,0:T(1,128)S(1)} %copy-done.7, f32[65,1024]{1,0:T(8,128)S(1)} %shard_map.94.base_ref, bf16[1,12,64,64]{3,2,1,0:T(8,128)(2,1)S(1)} %copy-done.5, bf16[8,64,64]{2,1,0:T(8,128)(2,1)S(1)} %copy-done.2, bf16[8,64,128]{2,1,0:T(8,128)(2,1)S(1)} %copy-done.3, ...), custom_call_target="tpu_custom_call" | custom-call | flops 68157440 | bytes 1105968 | tf_op jit(solution)/shard_map/pallas_call | solution.py:270
  30.1 0.7 %collective-permute-done.11.refs_3_ = bf16[384,128]{1,0:T(8,128)(2,1)S(1)} collective-permute-done((bf16[384,128]{1,0:T(8,128)(2,1)S(1)}, bf16[384,128]{1,0:T(8,128)(2,1)S(1)}, u32[]{:S(2)}, u32[]{:S(2)}) %collective-permute-start.11) | collective-permute-done | bytes 98336 | tf_op jit(solution)/shard_map/ppermute | solution.py:295
  30.9 0.8 %shard_map.96 = f32[65,1024]{1,0:T(8,128)} custom-call(f32[65,1024]{1,0:T(8,128)S(1)} %shard_map.95.base_ref, bf16[384,128]{1,0:T(8,128)(2,1)S(1)} %get-tuple-element.43.refs_0_, bf16[384,128]{1,0:T(8,128)(2,1)S(1)} %collective-permute-done.9.refs_1_, bf16[384,128]{1,0:T(8,128)(2,1)S(1)} %collective-permute-done.10.refs_2_, ...), custom_call_target="tpu_custom_call" | custom-call | flops 133120 | bytes 1204224 | tf_op jit(solution)/shard_map/pallas_call | solution.py:270
  (22 shorter events, 0.1 us)
Async XLA Ops:
  0.0 24.4 %copy-start.1 = (bf16[65,1024]{1,0:T(8,128)(2,1)S(1)}, bf16[65,1024]{1,0:T(8,128)(2,1)}, u32[]{:S(2)}) copy-start(bf16[65,1024]{1,0:T(8,128)(2,1)} %probes_ref) | copy-start | bytes 399364
  0.0 24.4 %copy-start = (bf16[8,8,128,128]{3,2,1,0:T(8,128)(2,1)S(1)}, bf16[8,8,128,128]{3,2,1,0:T(8,128)(2,1)}, u32[]{:S(2)}) copy-start(bf16[8,8,128,128]{3,2,1,0:T(8,128)(2,1)} %local_ref.1) | copy-start | bytes 6291460
  3.5 25.2 %copy-start.2 = (bf16[8,64,64]{2,1,0:T(8,128)(2,1)S(1)}, bf16[8,64,64]{2,1,0:T(8,128)(2,1)}, u32[]{:S(2)}) copy-start(bf16[8,64,64]{2,1,0:T(8,128)(2,1)} %transfer_ref.1) | copy-start | bytes 196612
  3.5 25.2 %copy-start.3 = (bf16[8,64,128]{2,1,0:T(8,128)(2,1)S(1)}, bf16[8,64,128]{2,1,0:T(8,128)(2,1)}, u32[]{:S(2)}) copy-start(bf16[8,64,128]{2,1,0:T(8,128)(2,1)} %basis_ref.1) | copy-start | bytes 393220
  3.5 7.3 %collective-permute-start = (bf16[784,128]{1,0:T(8,128)(2,1)}, bf16[784,128]{1,0:T(8,128)(2,1)S(1)}, u32[]{:S(2)}, u32[]{:S(2)}) collective-permute-start(bf16[784,128]{1,0:T(8,128)(2,1)} %get-tuple-element.27), channel_id=1, source_target_pairs={{0,1},{1,0},{2,3},{3,2},{4,5},{5,4},{6,7},{7,6},{8,9},{9,8},{10,11... | collective-permute-start | bytes 602120 | tf_op jit(solution)/shard_map/ppermute | solution.py:295
  4.0 13.5 %collective-permute-start.1 = (bf16[784,128]{1,0:T(8,128)(2,1)}, bf16[784,128]{1,0:T(8,128)(2,1)S(1)}, u32[]{:S(2)}, u32[]{:S(2)}) collective-permute-start(bf16[784,128]{1,0:T(8,128)(2,1)} %get-tuple-element.31), channel_id=1, source_target_pairs={{0,2},{1,3},{2,0},{3,1},{4,6},{5,7},{6,4},{7,5},{8,10},{9,11},{10,... | collective-permute-start | bytes 602120 | tf_op jit(solution)/shard_map/ppermute | solution.py:295
  6.6 10.9 %collective-permute-start.2 = (bf16[784,128]{1,0:T(8,128)(2,1)}, bf16[784,128]{1,0:T(8,128)(2,1)S(1)}, u32[]{:S(2)}, u32[]{:S(2)}) collective-permute-start(bf16[784,128]{1,0:T(8,128)(2,1)} %get-tuple-element.32), channel_id=1, source_target_pairs={{0,3},{1,2},{2,1},{3,0},{4,7},{5,6},{6,5},{7,4},{8,11},{9,10},{10,... | collective-permute-start | bytes 602120 | tf_op jit(solution)/shard_map/ppermute | solution.py:295
  6.7 9.6 %collective-permute-start.3 = (bf16[320,128]{1,0:T(8,128)(2,1)}, bf16[320,128]{1,0:T(8,128)(2,1)S(1)}, u32[]{:S(2)}, u32[]{:S(2)}) collective-permute-start(bf16[320,128]{1,0:T(8,128)(2,1)} %get-tuple-element.34), channel_id=1, source_target_pairs={{0,8},{1,9},{2,10},{3,11},{4,12},{5,13},{6,14},{7,15},{8,0},{9,1},... | collective-permute-start | bytes 245768 | tf_op jit(solution)/shard_map/ppermute | solution.py:295
  9.5 7.3 %collective-permute-start.4 = (bf16[320,128]{1,0:T(8,128)(2,1)}, bf16[320,128]{1,0:T(8,128)(2,1)S(1)}, u32[]{:S(2)}, u32[]{:S(2)}) collective-permute-start(bf16[320,128]{1,0:T(8,128)(2,1)} %get-tuple-element.35), channel_id=1, source_target_pairs={{0,12},{1,13},{2,14},{3,15},{4,8},{5,9},{6,10},{7,11},{8,4},{9,5},... | collective-permute-start | bytes 245768 | tf_op jit(solution)/shard_map/ppermute | solution.py:295
  10.8 6.7 %collective-permute-start.5 = (bf16[320,128]{1,0:T(8,128)(2,1)}, bf16[320,128]{1,0:T(8,128)(2,1)S(1)}, u32[]{:S(2)}, u32[]{:S(2)}) collective-permute-start(bf16[320,128]{1,0:T(8,128)(2,1)} %get-tuple-element.36), channel_id=1, source_target_pairs={{0,4},{1,5},{2,6},{3,7},{4,0},{5,1},{6,2},{7,3},{8,12},{9,13},{10,... | collective-permute-start | bytes 245768 | tf_op jit(solution)/shard_map/ppermute | solution.py:295
  11.0 0.9 %copy-start.4 = (bf16[784,128]{1,0:T(8,128)(2,1)S(1)}, bf16[784,128]{1,0:T(8,128)(2,1)}, u32[]{:S(2)}) copy-start(bf16[784,128]{1,0:T(8,128)(2,1)} %get-tuple-element.26.refs_0_) | copy-start | bytes 602116
  12.0 0.9 %copy-start.6 = (bf16[320,128]{1,0:T(8,128)(2,1)S(1)}, bf16[320,128]{1,0:T(8,128)(2,1)}, u32[]{:S(2)}) copy-start(bf16[320,128]{1,0:T(8,128)(2,1)} %get-tuple-element.28.refs_2_) | copy-start | bytes 245764
  12.9 15.8 %copy-start.5 = (bf16[1,12,64,64]{3,2,1,0:T(8,128)(2,1)S(1)}, bf16[1,12,64,64]{3,2,1,0:T(8,128)(2,1)}, u32[]{:S(2)}) copy-start(bf16[1,12,64,64]{3,2,1,0:T(8,128)(2,1)} %couplings_ref.1) | copy-start | bytes 294916
  12.9 15.8 %copy-start.7 = (s32[1,12]{1,0:T(1,128)S(1)}, s32[1,12]{1,0:T(1,128)}, u32[]{:S(2)}) copy-start(s32[1,12]{1,0:T(1,128)} %partner_ref.1) | copy-start | bytes 148
  18.7 5.7 %collective-permute-start.6 = (bf16[272,128]{1,0:T(8,128)(2,1)S(1)}, bf16[272,128]{1,0:T(8,128)(2,1)S(1)}, u32[]{:S(2)}, u32[]{:S(2)}) collective-permute-start(bf16[272,128]{1,0:T(8,128)(2,1)S(1)} %get-tuple-element.40), channel_id=1, source_target_pairs={{0,1},{1,0},{2,3},{3,2},{4,5},{5,4},{6,7},{7,6},{8,9},{9,8},{10,11... | collective-permute-start | bytes 208904 | tf_op jit(solution)/shard_map/ppermute | solution.py:295
  18.8 11.4 %collective-permute-start.9 = (bf16[384,128]{1,0:T(8,128)(2,1)S(1)}, bf16[384,128]{1,0:T(8,128)(2,1)S(1)}, u32[]{:S(2)}, u32[]{:S(2)}) collective-permute-start(bf16[384,128]{1,0:T(8,128)(2,1)S(1)} %get-tuple-element.44), channel_id=1, source_target_pairs={{0,8},{1,9},{2,10},{3,11},{4,12},{5,13},{6,14},{7,15},{8,0},{9,1},... | collective-permute-start | bytes 294920 | tf_op jit(solution)/shard_map/ppermute | solution.py:295
  21.9 8.2 %collective-permute-start.10 = (bf16[384,128]{1,0:T(8,128)(2,1)S(1)}, bf16[384,128]{1,0:T(8,128)(2,1)S(1)}, u32[]{:S(2)}, u32[]{:S(2)}) collective-permute-start(bf16[384,128]{1,0:T(8,128)(2,1)S(1)} %get-tuple-element.45), channel_id=1, source_target_pairs={{0,12},{1,13},{2,14},{3,15},{4,8},{5,9},{6,10},{7,11},{8,4},{9,5},... | collective-permute-start | bytes 294920 | tf_op jit(solution)/shard_map/ppermute | solution.py:295
  22.4 8.4 %collective-permute-start.11 = (bf16[384,128]{1,0:T(8,128)(2,1)S(1)}, bf16[384,128]{1,0:T(8,128)(2,1)S(1)}, u32[]{:S(2)}, u32[]{:S(2)}) collective-permute-start(bf16[384,128]{1,0:T(8,128)(2,1)S(1)} %get-tuple-element.46), channel_id=1, source_target_pairs={{0,4},{1,5},{2,6},{3,7},{4,0},{5,1},{6,2},{7,3},{8,12},{9,13},{10,... | collective-permute-start | bytes 294920 | tf_op jit(solution)/shard_map/ppermute | solution.py:295
  22.9 4.3 %collective-permute-start.7 = (bf16[272,128]{1,0:T(8,128)(2,1)S(1)}, bf16[272,128]{1,0:T(8,128)(2,1)S(1)}, u32[]{:S(2)}, u32[]{:S(2)}) collective-permute-start(bf16[272,128]{1,0:T(8,128)(2,1)S(1)} %get-tuple-element.41), channel_id=1, source_target_pairs={{0,2},{1,3},{2,0},{3,1},{4,6},{5,7},{6,4},{7,5},{8,10},{9,11},{10,... | collective-permute-start | bytes 208904 | tf_op jit(solution)/shard_map/ppermute | solution.py:295
  24.4 4.3 %collective-permute-start.8 = (bf16[272,128]{1,0:T(8,128)(2,1)S(1)}, bf16[272,128]{1,0:T(8,128)(2,1)S(1)}, u32[]{:S(2)}, u32[]{:S(2)}) collective-permute-start(bf16[272,128]{1,0:T(8,128)(2,1)S(1)} %get-tuple-element.42), channel_id=1, source_target_pairs={{0,3},{1,2},{2,1},{3,0},{4,7},{5,6},{6,5},{7,4},{8,11},{9,10},{10,... | collective-permute-start | bytes 208904 | tf_op jit(solution)/shard_map/ppermute | solution.py:295

commit v17 on v16

--- a/solution.py
+++ b/solution.py
@@ -83,18 +83,17 @@
     leaves, per_leaf, size = blocks_ref.shape[:3]
     columns, rank = probes_ref.shape[0], basis_ref.shape[1]
     copies = Copies(sems)
+    chunk = leaves // 2
+    arrivals = []
     early = [
         copies.start(probes_hbm, probes_ref),
-        copies.start(basis_hbm, basis_ref),
-        copies.start(transfer_hbm, transfer_ref),
         copies.start(dest_hbm, dest_ref),
         copies.start(leaf_hbm, leaf_ref),
     ]
-    chunk = leaves // 2
-    arrivals = [
-        copies.start(blocks_hbm.at[pl.ds(j, chunk)], blocks_ref.at[pl.ds(j, chunk)])
-        for j in range(0, leaves, chunk)
-    ]
+    for j in range(0, leaves, chunk):
+        arrivals.append(copies.start(blocks_hbm.at[pl.ds(j, chunk)], blocks_ref.at[pl.ds(j, chunk)]))
+        if j == 0:
+            early += [copies.start(basis_hbm, basis_ref), copies.start(transfer_hbm, transfer_ref)]
 
     @pl.loop(0, devices)
     def _(i):
@@ -104,12 +103,6 @@
     for copy in early:
         copy.wait()
     box = jnp.zeros((columns, rank), F32)
-    for j in range(leaves):
-        coef = dot_t(probes_ref[:, j * size : (j + 1) * size], basis_ref[j]).astype(BF16)
-        box += dot_t(coef, transfer_ref[j])
-    half = by_high.half
-    packed = jnp.concatenate([box[:half], box[half:main]], axis=1).astype(BF16)
-    last = jnp.concatenate([box[main:], jnp.zeros_like(box[main:])], axis=1)
 
     numbers = jnp.full((-(-(low + high) // 8) * 8, size), leaves, I32)
     row = lax.broadcasted_iota(I32, numbers.shape, 0)
@@ -118,6 +111,7 @@
         if j % chunk == 0:
             arrivals[j // chunk].wait()
         x = probes_ref[:, j * size : (j + 1) * size]
+        box += dot_t(dot_t(x, basis_ref[j]).astype(BF16), transfer_ref[j])
         for first in range(0, per_leaf, 4):
             many = min(4, per_leaf - first)
             rhs = blocks_ref[j, first : first + many].reshape(many * size, size)
@@ -143,6 +137,9 @@
                 tails[to_high, pl.ds(at, 1), :] = block[main:]
                 numbers = jnp.where((row == low + to_high) & (lane == at), number, numbers)
 
+    half = by_high.half
+    packed = jnp.concatenate([box[:half], box[half:main]], axis=1).astype(BF16)
+    last = jnp.concatenate([box[main:], jnp.zeros_like(box[main:])], axis=1)
     numbers = numbers.astype(F32)
     blank = jnp.zeros((TILE - 2, size), F32)
     for i in range(low):

time: 31.8 us -> 31.9 us (level)
  no operation moved by 1% of the time
where the time goes in v17:
time: 31.9 us; the launch traced here: 31.7 us
  starting transfers between devices  13.2 us (41%)
  Pallas kernels  8.43 us (26%)
  waiting for transfers between devices  8.13 us (25%)
  local copies, waits for them, and re-layouts  1.84 us (6%)
    ppermute x12, starting transfers between devices, per_device(): lax.ppermute(x, 'leaf', [(i, i ^ way) for i in range(devices)])  13.2 us
    pallas_call x6, Pallas kernels, call(): pl.pallas_call(kernel, out_shape=out_shape, in_specs=specs[0], out_specs=...  8.43 us
    ppermute x12, waiting for transfers between devices, per_device(): lax.ppermute(x, 'leaf', [(i, i ^ way) for i in range(devices)])  8.13 us
    unnamed x16, local copies, waits for them, and re-layouts  1.84 us
  transfers between devices with their start and end apart: 12, of which 6 were waited for; matrix products, arithmetic and copies ran while one was open for 0% of the time, Pallas kernels for 9%

profile of v17, /device:TPU:0, one launch (start us, length us, event | category | flops | bytes accessed | tf_op | source)
XLA Modules:
  0.0 31.7 jit_solution(6033922186310660046)
XLA Ops:
  0.0 3.5 %shard_map.91 = (bf16[784,128]{1,0:T(8,128)(2,1)}, bf16[784,128]{1,0:T(8,128)(2,1)}, bf16[784,128]{1,0:T(8,128)(2,1)}, bf16[784,128]{1,0:T(8,128)(2,1)}, bf16[32...) custom-call(s32[4,8]{1,0:T(4,128)} %bitcast.2, ...), custom_call_target="tpu_custom_call" | custom-call | flops 68157440 | bytes 2509056 | tf_op jit(solution)/shard_map/pallas_call | solution.py:267
  3.5 0.5 %collective-permute-start = (bf16[784,128]{1,0:T(8,128)(2,1)}, bf16[784,128]{1,0:T(8,128)(2,1)S(1)}, u32[]{:S(2)}, u32[]{:S(2)}) collective-permute-start(bf16[784,128]{1,0:T(8,128)(2,1)} %get-tuple-element.27), channel_id=1, source_target_pairs={{0,1},{1,0},{2,3},{3,2},{4,5},{5,4},{6,7},{7,6},{8,9},{9,8},{10,11... | collective-permute-start | bytes 602120 | tf_op jit(solution)/shard_map/ppermute | solution.py:292
  4.0 2.6 %collective-permute-start.1 = (bf16[784,128]{1,0:T(8,128)(2,1)}, bf16[784,128]{1,0:T(8,128)(2,1)S(1)}, u32[]{:S(2)}, u32[]{:S(2)}) collective-permute-start(bf16[784,128]{1,0:T(8,128)(2,1)} %get-tuple-element.31), channel_id=1, source_target_pairs={{0,2},{1,3},{2,0},{3,1},{4,6},{5,7},{6,4},{7,5},{8,10},{9,11},{10,... | collective-permute-start | bytes 602120 | tf_op jit(solution)/shard_map/ppermute | solution.py:292
  6.6 0.1 collective-permute-start.2
  6.7 2.8 %collective-permute-start.3 = (bf16[320,128]{1,0:T(8,128)(2,1)}, bf16[320,128]{1,0:T(8,128)(2,1)S(1)}, u32[]{:S(2)}, u32[]{:S(2)}) collective-permute-start(bf16[320,128]{1,0:T(8,128)(2,1)} %get-tuple-element.34), channel_id=1, source_target_pairs={{0,8},{1,9},{2,10},{3,11},{4,12},{5,13},{6,14},{7,15},{8,0},{9,1},... | collective-permute-start | bytes 245768 | tf_op jit(solution)/shard_map/ppermute | solution.py:292
  9.5 1.3 %collective-permute-start.4 = (bf16[320,128]{1,0:T(8,128)(2,1)}, bf16[320,128]{1,0:T(8,128)(2,1)S(1)}, u32[]{:S(2)}, u32[]{:S(2)}) collective-permute-start(bf16[320,128]{1,0:T(8,128)(2,1)} %get-tuple-element.35), channel_id=1, source_target_pairs={{0,12},{1,13},{2,14},{3,15},{4,8},{5,9},{6,10},{7,11},{8,4},{9,5},... | collective-permute-start | bytes 245768 | tf_op jit(solution)/shard_map/ppermute | solution.py:292
  10.8 0.2 collective-permute-start.5
  11.1 0.9 %copy-done.4 = bf16[784,128]{1,0:T(8,128)(2,1)S(1)} copy-done((bf16[784,128]{1,0:T(8,128)(2,1)S(1)}, bf16[784,128]{1,0:T(8,128)(2,1)}, u32[]{:S(2)}) %copy-start.4) | copy-done | bytes 200728
  12.0 0.9 %copy-done.6 = bf16[320,128]{1,0:T(8,128)(2,1)S(1)} copy-done((bf16[320,128]{1,0:T(8,128)(2,1)S(1)}, bf16[320,128]{1,0:T(8,128)(2,1)}, u32[]{:S(2)}) %copy-start.6) | copy-done | bytes 81944
  12.9 3.4 %collective-permute-done.3.refs_5_ = bf16[320,128]{1,0:T(8,128)(2,1)S(1)} collective-permute-done((bf16[320,128]{1,0:T(8,128)(2,1)}, bf16[320,128]{1,0:T(8,128)(2,1)S(1)}, u32[]{:S(2)}, u32[]{:S(2)}) %collective-permute-start.3) | collective-permute-done | bytes 81952 | tf_op jit(solution)/shard_map/ppermute | solution.py:292
  16.3 0.5 %collective-permute-done.4.refs_6_ = bf16[320,128]{1,0:T(8,128)(2,1)S(1)} collective-permute-done((bf16[320,128]{1,0:T(8,128)(2,1)}, bf16[320,128]{1,0:T(8,128)(2,1)S(1)}, u32[]{:S(2)}, u32[]{:S(2)}) %collective-permute-start.4) | collective-permute-done | bytes 81952 | tf_op jit(solution)/shard_map/ppermute | solution.py:292
  16.8 0.7 %collective-permute-done.5.refs_7_ = bf16[320,128]{1,0:T(8,128)(2,1)S(1)} collective-permute-done((bf16[320,128]{1,0:T(8,128)(2,1)}, bf16[320,128]{1,0:T(8,128)(2,1)S(1)}, u32[]{:S(2)}, u32[]{:S(2)}) %collective-permute-start.5) | collective-permute-done | bytes 81952 | tf_op jit(solution)/shard_map/ppermute | solution.py:292
  17.5 1.2 %shard_map.93 = (bf16[384,128]{1,0:T(8,128)(2,1)S(1)}, bf16[384,128]{1,0:T(8,128)(2,1)S(1)}, bf16[384,128]{1,0:T(8,128)(2,1)S(1)}, bf16[384,128]{1,0:T(8,128)(2,...) custom-call(bf16[784,128]{1,0:T(8,128)(2,1)S(1)} %get-tuple-element., ...), custom_call_target="tpu_custom_call" | custom-call | flops 532480 | bytes 1802240 | tf_op jit(solution)/shard_map/pallas_call | solution.py:267
  18.7 0.1 collective-permute-start.6
  18.8 3.1 %collective-permute-start.9 = (bf16[384,128]{1,0:T(8,128)(2,1)S(1)}, bf16[384,128]{1,0:T(8,128)(2,1)S(1)}, u32[]{:S(2)}, u32[]{:S(2)}) collective-permute-start(bf16[384,128]{1,0:T(8,128)(2,1)S(1)} %get-tuple-element.44), channel_id=1, source_target_pairs={{0,8},{1,9},{2,10},{3,11},{4,12},{5,13},{6,14},{7,15},{8,0},{9,1},... | collective-permute-start | bytes 294920 | tf_op jit(solution)/shard_map/ppermute | solution.py:292
  21.9 0.6 %collective-permute-start.10 = (bf16[384,128]{1,0:T(8,128)(2,1)S(1)}, bf16[384,128]{1,0:T(8,128)(2,1)S(1)}, u32[]{:S(2)}, u32[]{:S(2)}) collective-permute-start(bf16[384,128]{1,0:T(8,128)(2,1)S(1)} %get-tuple-element.45), channel_id=1, source_target_pairs={{0,12},{1,13},{2,14},{3,15},{4,8},{5,9},{6,10},{7,11},{8,4},{9,5},... | collective-permute-start | bytes 294920 | tf_op jit(solution)/shard_map/ppermute | solution.py:292
  22.5 0.4 %collective-permute-start.11 = (bf16[384,128]{1,0:T(8,128)(2,1)S(1)}, bf16[384,128]{1,0:T(8,128)(2,1)S(1)}, u32[]{:S(2)}, u32[]{:S(2)}) collective-permute-start(bf16[384,128]{1,0:T(8,128)(2,1)S(1)} %get-tuple-element.46), channel_id=1, source_target_pairs={{0,4},{1,5},{2,6},{3,7},{4,0},{5,1},{6,2},{7,3},{8,12},{9,13},{10,... | collective-permute-start | bytes 294920 | tf_op jit(solution)/shard_map/ppermute | solution.py:292
  22.9 1.5 %collective-permute-start.7 = (bf16[272,128]{1,0:T(8,128)(2,1)S(1)}, bf16[272,128]{1,0:T(8,128)(2,1)S(1)}, u32[]{:S(2)}, u32[]{:S(2)}) collective-permute-start(bf16[272,128]{1,0:T(8,128)(2,1)S(1)} %get-tuple-element.41), channel_id=1, source_target_pairs={{0,2},{1,3},{2,0},{3,1},{4,6},{5,7},{6,4},{7,5},{8,10},{9,11},{10,... | collective-permute-start | bytes 208904 | tf_op jit(solution)/shard_map/ppermute | solution.py:292
  24.4 1.5 %shard_map.94.base_ref = f32[65,1024]{1,0:T(8,128)S(1)} custom-call(bf16[65,1024]{1,0:T(8,128)(2,1)S(1)} %copy-done.1, bf16[8,8,128,128]{3,2,1,0:T(8,128)(2,1)S(1)} %copy-done), custom_call_target="tpu_custom_call" | custom-call | flops 136314880 | bytes 2496512 | tf_op jit(solution)/shard_map/pallas_call | solution.py:267
  25.9 1.3 %collective-permute-done.7.refs_2_.refs_6_ = bf16[272,128]{1,0:T(8,128)(2,1)S(1)} collective-permute-done((bf16[272,128]{1,0:T(8,128)(2,1)S(1)}, bf16[272,128]{1,0:T(8,128)(2,1)S(1)}, u32[]{:S(2)}, u32[]{:S(2)}) %collective-permute-start.7) | collective-permute-done | bytes 69664 | tf_op jit(solution)/shard_map/ppermute | solution.py:292
  27.2 1.5 %collective-permute-done.8.refs_3_.refs_7_ = bf16[272,128]{1,0:T(8,128)(2,1)S(1)} collective-permute-done((bf16[272,128]{1,0:T(8,128)(2,1)S(1)}, bf16[272,128]{1,0:T(8,128)(2,1)S(1)}, u32[]{:S(2)}, u32[]{:S(2)}) %collective-permute-start.8) | collective-permute-done | bytes 69664 | tf_op jit(solution)/shard_map/ppermute | solution.py:292
  28.7 1.4 %shard_map.95.base_ref = f32[65,1024]{1,0:T(8,128)S(1)} custom-call(s32[1,12]{1,0:T(1,128)S(1)} %copy-done.7, f32[65,1024]{1,0:T(8,128)S(1)} %shard_map.94.base_ref, bf16[1,12,64,64]{3,2,1,0:T(8,128)(2,1)S(1)} %copy-done.5, bf16[8,64,64]{2,1,0:T(8,128)(2,1)S(1)} %copy-done.2, bf16[8,64,128]{2,1,0:T(8,128)(2,1)S(1)} %copy-done.3, ...), custom_call_target="tpu_custom_call" | custom-call | flops 68157440 | bytes 1105968 | tf_op jit(solution)/shard_map/pallas_call | solution.py:267
  30.2 0.8 %collective-permute-done.11.refs_3_ = bf16[384,128]{1,0:T(8,128)(2,1)S(1)} collective-permute-done((bf16[384,128]{1,0:T(8,128)(2,1)S(1)}, bf16[384,128]{1,0:T(8,128)(2,1)S(1)}, u32[]{:S(2)}, u32[]{:S(2)}) %collective-permute-start.11) | collective-permute-done | bytes 98336 | tf_op jit(solution)/shard_map/ppermute | solution.py:292
  30.9 0.8 %shard_map.96 = f32[65,1024]{1,0:T(8,128)} custom-call(f32[65,1024]{1,0:T(8,128)S(1)} %shard_map.95.base_ref, bf16[384,128]{1,0:T(8,128)(2,1)S(1)} %get-tuple-element.43.refs_0_, bf16[384,128]{1,0:T(8,128)(2,1)S(1)} %collective-permute-done.9.refs_1_, bf16[384,128]{1,0:T(8,128)(2,1)S(1)} %collective-permute-done.10.refs_2_, ...), custom_call_target="tpu_custom_call" | custom-call | flops 133120 | bytes 1204224 | tf_op jit(solution)/shard_map/pallas_call | solution.py:267
  (22 shorter events, 0.1 us)
Async XLA Ops:
  0.0 24.4 %copy-start.1 = (bf16[65,1024]{1,0:T(8,128)(2,1)S(1)}, bf16[65,1024]{1,0:T(8,128)(2,1)}, u32[]{:S(2)}) copy-start(bf16[65,1024]{1,0:T(8,128)(2,1)} %probes_ref) | copy-start | bytes 399364
  0.0 24.4 %copy-start = (bf16[8,8,128,128]{3,2,1,0:T(8,128)(2,1)S(1)}, bf16[8,8,128,128]{3,2,1,0:T(8,128)(2,1)}, u32[]{:S(2)}) copy-start(bf16[8,8,128,128]{3,2,1,0:T(8,128)(2,1)} %local_ref.1) | copy-start | bytes 6291460
  3.5 25.2 %copy-start.2 = (bf16[8,64,64]{2,1,0:T(8,128)(2,1)S(1)}, bf16[8,64,64]{2,1,0:T(8,128)(2,1)}, u32[]{:S(2)}) copy-start(bf16[8,64,64]{2,1,0:T(8,128)(2,1)} %transfer_ref.1) | copy-start | bytes 196612
  3.5 25.2 %copy-start.3 = (bf16[8,64,128]{2,1,0:T(8,128)(2,1)S(1)}, bf16[8,64,128]{2,1,0:T(8,128)(2,1)}, u32[]{:S(2)}) copy-start(bf16[8,64,128]{2,1,0:T(8,128)(2,1)} %basis_ref.1) | copy-start | bytes 393220
  3.5 7.3 %collective-permute-start = (bf16[784,128]{1,0:T(8,128)(2,1)}, bf16[784,128]{1,0:T(8,128)(2,1)S(1)}, u32[]{:S(2)}, u32[]{:S(2)}) collective-permute-start(bf16[784,128]{1,0:T(8,128)(2,1)} %get-tuple-element.27), channel_id=1, source_target_pairs={{0,1},{1,0},{2,3},{3,2},{4,5},{5,4},{6,7},{7,6},{8,9},{9,8},{10,11... | collective-permute-start | bytes 602120 | tf_op jit(solution)/shard_map/ppermute | solution.py:292
  4.0 13.5 %collective-permute-start.1 = (bf16[784,128]{1,0:T(8,128)(2,1)}, bf16[784,128]{1,0:T(8,128)(2,1)S(1)}, u32[]{:S(2)}, u32[]{:S(2)}) collective-permute-start(bf16[784,128]{1,0:T(8,128)(2,1)} %get-tuple-element.31), channel_id=1, source_target_pairs={{0,2},{1,3},{2,0},{3,1},{4,6},{5,7},{6,4},{7,5},{8,10},{9,11},{10,... | collective-permute-start | bytes 602120 | tf_op jit(solution)/shard_map/ppermute | solution.py:292
  6.6 10.9 %collective-permute-start.2 = (bf16[784,128]{1,0:T(8,128)(2,1)}, bf16[784,128]{1,0:T(8,128)(2,1)S(1)}, u32[]{:S(2)}, u32[]{:S(2)}) collective-permute-start(bf16[784,128]{1,0:T(8,128)(2,1)} %get-tuple-element.32), channel_id=1, source_target_pairs={{0,3},{1,2},{2,1},{3,0},{4,7},{5,6},{6,5},{7,4},{8,11},{9,10},{10,... | collective-permute-start | bytes 602120 | tf_op jit(solution)/shard_map/ppermute | solution.py:292
  6.7 9.6 %collective-permute-start.3 = (bf16[320,128]{1,0:T(8,128)(2,1)}, bf16[320,128]{1,0:T(8,128)(2,1)S(1)}, u32[]{:S(2)}, u32[]{:S(2)}) collective-permute-start(bf16[320,128]{1,0:T(8,128)(2,1)} %get-tuple-element.34), channel_id=1, source_target_pairs={{0,8},{1,9},{2,10},{3,11},{4,12},{5,13},{6,14},{7,15},{8,0},{9,1},... | collective-permute-start | bytes 245768 | tf_op jit(solution)/shard_map/ppermute | solution.py:292
  9.5 7.3 %collective-permute-start.4 = (bf16[320,128]{1,0:T(8,128)(2,1)}, bf16[320,128]{1,0:T(8,128)(2,1)S(1)}, u32[]{:S(2)}, u32[]{:S(2)}) collective-permute-start(bf16[320,128]{1,0:T(8,128)(2,1)} %get-tuple-element.35), channel_id=1, source_target_pairs={{0,12},{1,13},{2,14},{3,15},{4,8},{5,9},{6,10},{7,11},{8,4},{9,5},... | collective-permute-start | bytes 245768 | tf_op jit(solution)/shard_map/ppermute | solution.py:292
  10.8 6.7 %collective-permute-start.5 = (bf16[320,128]{1,0:T(8,128)(2,1)}, bf16[320,128]{1,0:T(8,128)(2,1)S(1)}, u32[]{:S(2)}, u32[]{:S(2)}) collective-permute-start(bf16[320,128]{1,0:T(8,128)(2,1)} %get-tuple-element.36), channel_id=1, source_target_pairs={{0,4},{1,5},{2,6},{3,7},{4,0},{5,1},{6,2},{7,3},{8,12},{9,13},{10,... | collective-permute-start | bytes 245768 | tf_op jit(solution)/shard_map/ppermute | solution.py:292
  11.1 0.9 %copy-start.4 = (bf16[784,128]{1,0:T(8,128)(2,1)S(1)}, bf16[784,128]{1,0:T(8,128)(2,1)}, u32[]{:S(2)}) copy-start(bf16[784,128]{1,0:T(8,128)(2,1)} %get-tuple-element.26.refs_0_) | copy-start | bytes 602116
  12.0 0.9 %copy-start.6 = (bf16[320,128]{1,0:T(8,128)(2,1)S(1)}, bf16[320,128]{1,0:T(8,128)(2,1)}, u32[]{:S(2)}) copy-start(bf16[320,128]{1,0:T(8,128)(2,1)} %get-tuple-element.28.refs_2_) | copy-start | bytes 245764
  12.9 15.8 %copy-start.5 = (bf16[1,12,64,64]{3,2,1,0:T(8,128)(2,1)S(1)}, bf16[1,12,64,64]{3,2,1,0:T(8,128)(2,1)}, u32[]{:S(2)}) copy-start(bf16[1,12,64,64]{3,2,1,0:T(8,128)(2,1)} %couplings_ref.1) | copy-start | bytes 294916
  12.9 15.8 %copy-start.7 = (s32[1,12]{1,0:T(1,128)S(1)}, s32[1,12]{1,0:T(1,128)}, u32[]{:S(2)}) copy-start(s32[1,12]{1,0:T(1,128)} %partner_ref.1) | copy-start | bytes 148
  18.7 5.7 %collective-permute-start.6 = (bf16[272,128]{1,0:T(8,128)(2,1)S(1)}, bf16[272,128]{1,0:T(8,128)(2,1)S(1)}, u32[]{:S(2)}, u32[]{:S(2)}) collective-permute-start(bf16[272,128]{1,0:T(8,128)(2,1)S(1)} %get-tuple-element.40), channel_id=1, source_target_pairs={{0,1},{1,0},{2,3},{3,2},{4,5},{5,4},{6,7},{7,6},{8,9},{9,8},{10,11... | collective-permute-start | bytes 208904 | tf_op jit(solution)/shard_map/ppermute | solution.py:292
  18.8 11.3 %collective-permute-start.9 = (bf16[384,128]{1,0:T(8,128)(2,1)S(1)}, bf16[384,128]{1,0:T(8,128)(2,1)S(1)}, u32[]{:S(2)}, u32[]{:S(2)}) collective-permute-start(bf16[384,128]{1,0:T(8,128)(2,1)S(1)} %get-tuple-element.44), channel_id=1, source_target_pairs={{0,8},{1,9},{2,10},{3,11},{4,12},{5,13},{6,14},{7,15},{8,0},{9,1},... | collective-permute-start | bytes 294920 | tf_op jit(solution)/shard_map/ppermute | solution.py:292
  21.9 8.2 %collective-permute-start.10 = (bf16[384,128]{1,0:T(8,128)(2,1)S(1)}, bf16[384,128]{1,0:T(8,128)(2,1)S(1)}, u32[]{:S(2)}, u32[]{:S(2)}) collective-permute-start(bf16[384,128]{1,0:T(8,128)(2,1)S(1)} %get-tuple-element.45), channel_id=1, source_target_pairs={{0,12},{1,13},{2,14},{3,15},{4,8},{5,9},{6,10},{7,11},{8,4},{9,5},... | collective-permute-start | bytes 294920 | tf_op jit(solution)/shard_map/ppermute | solution.py:292
  22.5 8.4 %collective-permute-start.11 = (bf16[384,128]{1,0:T(8,128)(2,1)S(1)}, bf16[384,128]{1,0:T(8,128)(2,1)S(1)}, u32[]{:S(2)}, u32[]{:S(2)}) collective-permute-start(bf16[384,128]{1,0:T(8,128)(2,1)S(1)} %get-tuple-element.46), channel_id=1, source_target_pairs={{0,4},{1,5},{2,6},{3,7},{4,0},{5,1},{6,2},{7,3},{8,12},{9,13},{10,... | collective-permute-start | bytes 294920 | tf_op jit(solution)/shard_map/ppermute | solution.py:292
  22.9 4.3 %collective-permute-start.7 = (bf16[272,128]{1,0:T(8,128)(2,1)S(1)}, bf16[272,128]{1,0:T(8,128)(2,1)S(1)}, u32[]{:S(2)}, u32[]{:S(2)}) collective-permute-start(bf16[272,128]{1,0:T(8,128)(2,1)S(1)} %get-tuple-element.41), channel_id=1, source_target_pairs={{0,2},{1,3},{2,0},{3,1},{4,6},{5,7},{6,4},{7,5},{8,10},{9,11},{10,... | collective-permute-start | bytes 208904 | tf_op jit(solution)/shard_map/ppermute | solution.py:292
  24.4 4.3 %collective-permute-start.8 = (bf16[272,128]{1,0:T(8,128)(2,1)S(1)}, bf16[272,128]{1,0:T(8,128)(2,1)S(1)}, u32[]{:S(2)}, u32[]{:S(2)}) collective-permute-start(bf16[272,128]{1,0:T(8,128)(2,1)S(1)} %get-tuple-element.42), channel_id=1, source_target_pairs={{0,3},{1,2},{2,1},{3,0},{4,7},{5,6},{6,5},{7,4},{8,11},{9,10},{10,... | collective-permute-start | bytes 208904 | tf_op jit(solution)/shard_map/ppermute | solution.py:292

commit v18 on v17

--- a/solution.py
+++ b/solution.py
@@ -9,6 +9,8 @@
 
 CAP = 4
 TILE = 16
+HEAVY = 4 * 10**9
+
 F32 = jnp.float32
 BF16 = jnp.bfloat16
 I32 = jnp.int32
@@ -186,21 +188,17 @@
     return [0, *range(2, high), 1]
 
 
-def sum_kernel(routes, devices, *refs):
-    by_low, by_high = routes
-    high, low = grid_of(devices)
-    ways = low + high
-    came, outs, scratch = refs[:ways], refs[ways : 2 * ways], refs[2 * ways :]
-    meta, leaf_ref, total_low, total_high, tails, late = scratch
-    for i, route in enumerate([by_low] * low + [by_high] * high):
-        meta[i : i + 1, :] = came[i][route.meta : route.box, :].astype(F32)[:1].astype(I32)
+def sum_kernel(route, planes, ways, *refs):
+    came, outs = refs[:ways], refs[ways:-5]
+    meta, leaf_ref, total, tails, late = refs[-5:]
+    for i, ref in enumerate(came):
+        meta[i : i + 1, :] = ref[route.meta : route.box, :].astype(F32)[:1].astype(I32)
     numbers = pltpu.make_async_copy(meta, leaf_ref, late)
     numbers.start()
-    for ref in (total_low, total_high, tails):
+    for ref in (total, tails):
         ref[...] = jnp.zeros(ref.shape, F32)
     numbers.wait()
-    sum_route(by_low, came[:low], None, outs[:high], 0, leaf_ref, total_low, None)
-    sum_route(by_high, came[low:], across_first(high), outs[high:], low, leaf_ref, total_high, tails)
+    sum_route(route, came, planes, outs, 0, leaf_ref, total, tails)
 
 
 def keep_kernel(*refs):
@@ -244,16 +242,21 @@
         out_ref[:, cols] = base_ref[:, cols] + dot(down[j], basis_ref[j])
 
 
+def across_kernel(came_own, *refs):
+    out_ref = refs[-1]
+    out_ref[...] = sum(ref[...].astype(F32) for ref in (came_own, *refs[:-1]))
+
+
 def last_kernel(routes, devices, base_ref, *refs):
     by_low, by_high = routes
     high, low = grid_of(devices)
-    came_high, came_low, out_ref = refs[:high], refs[high : high + low], refs[high + low]
+    came_high, came_low, out_ref = refs[: -low - 1], refs[-low - 1 : -1], refs[-1]
     leaves, split, main = by_low.leaves, by_low.rows, by_low.main
     size = base_ref.shape[1] // leaves
     tails = sum(came_low[k][by_high.dense_tails : by_high.dense_box, :].astype(F32) for k in range(low))
     for j in range(leaves):
         cols = slice(j * size, (j + 1) * size)
-        upper = sum(came_high[k][j * by_low.rows : (j + 1) * by_low.rows, :].astype(F32) for k in range(high))
+        upper = sum(ref[j * by_low.rows : (j + 1) * by_low.rows, :].astype(F32) for ref in came_high)
         lower = sum(came_low[k][j * by_high.rows : (j + 1) * by_high.rows, :].astype(F32) for k in range(low))
         out_ref[:split, cols] = base_ref[:split, cols] + upper
         out_ref[split:main, cols] = base_ref[split:main, cols] + lower
@@ -329,30 +332,37 @@
         0,
     )
 
-    total = lambda route: jax.ShapeDtypeStruct((route.fan, (leaves + 1) * route.rows, size), F32)
-    tails = jax.ShapeDtypeStruct((low, by_high.dense_box - by_high.dense_tails, size), F32)
-    sums = call(
-        functools.partial(sum_kernel, routes, devices),
-        [dense(by_low)] * high + [dense(by_high)] * low,
-        ([VMEM] * (low + high), [VMEM] * (low + high)),
-        (*came_low, *(came_high[k] for k in planes)),
-        [pltpu.VMEM((low + high, size), I32), pltpu.SMEM((low + high, size), I32)]
-        + like(total(by_low), total(by_high), tails)
-        + [pltpu.SemaphoreType.DMA(())],
-        devices * CAP * columns * size,
-        4 * (total(by_low).size + total(by_high).size + tails.size),
-    )
-    to_high, to_low = list(sums[:high]), list(sums[high:])
+    def summed(route, planes, came):
+        total = jax.ShapeDtypeStruct((route.fan, (leaves + 1) * route.rows, size), F32)
+        tails = jax.ShapeDtypeStruct((route.fan, max(TILE, route.dense_box - route.dense_tails), size), F32)
+        ways = len(came)
+        return list(
+            call(
+                functools.partial(sum_kernel, route, planes, ways),
+                [dense(route)] * route.fan,
+                ([VMEM] * ways, [VMEM] * route.fan),
+                came,
+                [pltpu.VMEM((ways, size), I32), pltpu.SMEM((ways, size), I32)]
+                + like(total, tails)
+                + [pltpu.SemaphoreType.DMA(())],
+                devices * CAP * route.rows * size,
+                4 * (total.size + tails.size),
+            )
+        )
+
+    to_high = summed(by_low, None, came_low)
+    came_high[0], to_high[0] = lax.optimization_barrier((came_high[0], to_high[0]))
+    to_low = summed(by_high, planes, [came_high[k] for k in planes])
+    base_shape = jax.ShapeDtypeStruct((columns, points), F32)
     probes_then, to_low[0] = lax.optimization_barrier((probes, to_low[0]))
+    base = call(
+        local_kernel, base_shape, ([VMEM] * 2, VMEM), (probes_then, local_blocks), [], leaves * leaves * unit, 0
+    )
     for k in planes[1:]:
         to_high[k] = relative(to_high[k], k * low)
     for k in range(1, low):
         to_low[k] = relative(to_low[k], k)
 
-    base_shape = jax.ShapeDtypeStruct((columns, points), F32)
-    base = call(
-        local_kernel, base_shape, ([VMEM] * 2, VMEM), (probes_then, local_blocks), [], leaves * leaves * unit, 0
-    )
     boxes = jax.ShapeDtypeStruct((devices, columns, rank), BF16)
     base = call(
         functools.partial(far_kernel, by_high, low),
@@ -363,11 +373,20 @@
         4 * leaves * unit,
         4 * boxes.size,
     )
+    across = call(
+        across_kernel,
+        jax.ShapeDtypeStruct((by_low.dense_depth, size), F32),
+        ([VMEM] * (high - 1), VMEM),
+        [to_high[k] for k in planes[:-1]],
+        [],
+        HEAVY,
+        0,
+    )
     return call(
         functools.partial(last_kernel, routes, devices),
         base_shape,
-        ([VMEM] * (1 + high + low), VMEM),
-        (base, *(to_high[k] for k in planes), *to_low),
+        ([VMEM] * (3 + low), VMEM),
+        (base, across, to_high[1], *to_low),
         [],
         devices * columns * size,
         0,

time: 31.9 us -> 32 us (level)
  waiting for transfers between devices: 8.13 us -> 6.81 us
  Pallas kernels: 8.43 us -> 9.22 us
  starting transfers between devices: 13.2 us -> 13.8 us
    ppermute x12, waiting for transfers between devices: 8.13 us -> 6.81 us  [per_device(): lax.ppermute(x, 'leaf', [(i, i ^ way) for i in range(devices)])]
    pallas_call x6 -> x8, Pallas kernels: 8.43 us -> 9.22 us  [call(): pl.pallas_call(kernel, out_shape=out_shape, in_specs=specs[0], out_specs=...]
    ppermute x12, starting transfers between devices: 13.2 us -> 13.8 us  [per_device(): lax.ppermute(x, 'leaf', [(i, i ^ way) for i in range(devices)])]
  transfers between devices with their start and end apart: 12 -> 12, of which waited for: 6 -> 4; matrix products, arithmetic and copies ran while one was open for 0% -> 0% of each run, Pallas kernels for 9% -> 16%
where the time goes in v18:
time: 32 us; the launch traced here: 31.8 us
  starting transfers between devices  13.8 us (43%)
  Pallas kernels  9.22 us (29%)
  waiting for transfers between devices  6.81 us (21%)
  local copies, waits for them, and re-layouts  1.84 us (6%)
    ppermute x12, starting transfers between devices, per_device(): lax.ppermute(x, 'leaf', [(i, i ^ way) for i in range(devices)])  13.8 us
    pallas_call x8, Pallas kernels, call(): pl.pallas_call(kernel, out_shape=out_shape, in_specs=specs[0], out_specs=...  9.22 us
    ppermute x12, waiting for transfers between devices, per_device(): lax.ppermute(x, 'leaf', [(i, i ^ way) for i in range(devices)])  6.81 us
    unnamed x16, local copies, waits for them, and re-layouts  1.84 us
  transfers between devices with their start and end apart: 12, of which 4 were waited for; matrix products, arithmetic and copies ran while one was open for 0% of the time, Pallas kernels for 16%

profile of v18, /device:TPU:0, one launch (start us, length us, event | category | flops | bytes accessed | tf_op | source)
XLA Modules:
  0.0 31.8 jit_solution(17596089065430850007)
XLA Ops:
  0.0 3.5 %shard_map.91 = (bf16[784,128]{1,0:T(8,128)(2,1)}, bf16[784,128]{1,0:T(8,128)(2,1)}, bf16[784,128]{1,0:T(8,128)(2,1)}, bf16[784,128]{1,0:T(8,128)(2,1)}, bf16[32...) custom-call(s32[4,8]{1,0:T(4,128)} %bitcast.2, ...), custom_call_target="tpu_custom_call" | custom-call | flops 68157440 | bytes 2509056 | tf_op jit(solution)/shard_map/pallas_call | solution.py:270
  3.5 0.5 %collective-permute-start = (bf16[784,128]{1,0:T(8,128)(2,1)}, bf16[784,128]{1,0:T(8,128)(2,1)S(1)}, u32[]{:S(2)}, u32[]{:S(2)}) collective-permute-start(bf16[784,128]{1,0:T(8,128)(2,1)} %get-tuple-element.29), channel_id=1, source_target_pairs={{0,1},{1,0},{2,3},{3,2},{4,5},{5,4},{6,7},{7,6},{8,9},{9,8},{10,11... | collective-permute-start | bytes 602120 | tf_op jit(solution)/shard_map/ppermute | solution.py:295
  4.0 2.6 %collective-permute-start.1 = (bf16[784,128]{1,0:T(8,128)(2,1)}, bf16[784,128]{1,0:T(8,128)(2,1)S(1)}, u32[]{:S(2)}, u32[]{:S(2)}) collective-permute-start(bf16[784,128]{1,0:T(8,128)(2,1)} %get-tuple-element.34), channel_id=1, source_target_pairs={{0,2},{1,3},{2,0},{3,1},{4,6},{5,7},{6,4},{7,5},{8,10},{9,11},{10,... | collective-permute-start | bytes 602120 | tf_op jit(solution)/shard_map/ppermute | solution.py:295
  6.6 0.1 collective-permute-start.2
  6.7 2.8 %collective-permute-start.3 = (bf16[320,128]{1,0:T(8,128)(2,1)}, bf16[320,128]{1,0:T(8,128)(2,1)S(1)}, u32[]{:S(2)}, u32[]{:S(2)}) collective-permute-start(bf16[320,128]{1,0:T(8,128)(2,1)} %get-tuple-element.38), channel_id=1, source_target_pairs={{0,8},{1,9},{2,10},{3,11},{4,12},{5,13},{6,14},{7,15},{8,0},{9,1},... | collective-permute-start | bytes 245768 | tf_op jit(solution)/shard_map/ppermute | solution.py:295
  9.5 1.3 %collective-permute-start.4 = (bf16[320,128]{1,0:T(8,128)(2,1)}, bf16[320,128]{1,0:T(8,128)(2,1)S(1)}, u32[]{:S(2)}, u32[]{:S(2)}) collective-permute-start(bf16[320,128]{1,0:T(8,128)(2,1)} %get-tuple-element.39), channel_id=1, source_target_pairs={{0,12},{1,13},{2,14},{3,15},{4,8},{5,9},{6,10},{7,11},{8,4},{9,5},... | collective-permute-start | bytes 245768 | tf_op jit(solution)/shard_map/ppermute | solution.py:295
  10.8 0.2 collective-permute-start.5
  11.1 0.9 %copy-done.4 = bf16[784,128]{1,0:T(8,128)(2,1)S(1)} copy-done((bf16[784,128]{1,0:T(8,128)(2,1)S(1)}, bf16[784,128]{1,0:T(8,128)(2,1)}, u32[]{:S(2)}) %copy-start.4) | copy-done | bytes 200728
  12.0 0.9 %copy-done.6 = bf16[320,128]{1,0:T(8,128)(2,1)S(1)} copy-done((bf16[320,128]{1,0:T(8,128)(2,1)S(1)}, bf16[320,128]{1,0:T(8,128)(2,1)}, u32[]{:S(2)}) %copy-start.6) | copy-done | bytes 81944
  13.0 3.5 %collective-permute-done.2.refs_3_ = bf16[784,128]{1,0:T(8,128)(2,1)S(1)} collective-permute-done((bf16[784,128]{1,0:T(8,128)(2,1)}, bf16[784,128]{1,0:T(8,128)(2,1)S(1)}, u32[]{:S(2)}, u32[]{:S(2)}) %collective-permute-start.2) | collective-permute-done | bytes 200736 | tf_op jit(solution)/shard_map/ppermute | solution.py:295
  16.5 1.0 %shard_map.93 = (bf16[384,128]{1,0:T(8,128)(2,1)S(1)}, bf16[384,128]{1,0:T(8,128)(2,1)S(1)}, bf16[384,128]{1,0:T(8,128)(2,1)S(1)}, bf16[384,128]{1,0:T(8,128)(2,1)S(1)}) custom-call(bf16[784,128]{1,0:T(8,128)(2,1)S(1)} %get-tuple-element.32.refs_0_, bf16[784,128]{1,0:T(8,128)(2,1)S(1)} %get-tuple-element.33.refs_1_, ...), custom_call_target="tpu_custom_call" | custom-call | flops 393216 | bytes 1196032 | tf_op jit(solution)/shard_map/pallas_call | solution.py:270
  17.5 2.7 %collective-permute-start.9 = (bf16[384,128]{1,0:T(8,128)(2,1)S(1)}, bf16[384,128]{1,0:T(8,128)(2,1)S(1)}, u32[]{:S(2)}, u32[]{:S(2)}) collective-permute-start(bf16[384,128]{1,0:T(8,128)(2,1)S(1)} %get-tuple-element.48), channel_id=1, source_target_pairs={{0,8},{1,9},{2,10},{3,11},{4,12},{5,13},{6,14},{7,15},{8,0},{9,1},... | collective-permute-start | bytes 294920 | tf_op jit(solution)/shard_map/ppermute | solution.py:295
  20.2 1.4 %collective-permute-start.10 = (bf16[384,128]{1,0:T(8,128)(2,1)S(1)}, bf16[384,128]{1,0:T(8,128)(2,1)S(1)}, u32[]{:S(2)}, u32[]{:S(2)}) collective-permute-start(bf16[384,128]{1,0:T(8,128)(2,1)S(1)} %get-tuple-element.49), channel_id=1, source_target_pairs={{0,12},{1,13},{2,14},{3,15},{4,8},{5,9},{6,10},{7,11},{8,4},{9,5},... | collective-permute-start | bytes 294920 | tf_op jit(solution)/shard_map/ppermute | solution.py:295
  21.5 0.9 %shard_map.94 = (bf16[272,128]{1,0:T(8,128)(2,1)S(1)}, bf16[272,128]{1,0:T(8,128)(2,1)S(1)}, bf16[272,128]{1,0:T(8,128)(2,1)S(1)}, bf16[272,128]{1,0:T(8,128)(2,1)S(1)}) custom-call(bf16[320,128]{1,0:T(8,128)(2,1)S(1)} %get-tuple-element.37.refs_0_, bf16[320,128]{1,0:T(8,128)(2,1)S(1)} %collective-permute-done.3.refs_1_, ...), custom_call_target="tpu_custom_call" | custom-call | flops 131072 | bytes 606208 | tf_op jit(solution)/shard_map/pallas_call | solution.py:270
  22.5 0.1 collective-permute-start.6
  22.6 1.5 %collective-permute-start.7 = (bf16[272,128]{1,0:T(8,128)(2,1)S(1)}, bf16[272,128]{1,0:T(8,128)(2,1)S(1)}, u32[]{:S(2)}, u32[]{:S(2)}) collective-permute-start(bf16[272,128]{1,0:T(8,128)(2,1)S(1)} %get-tuple-element.45), channel_id=1, source_target_pairs={{0,2},{1,3},{2,0},{3,1},{4,6},{5,7},{6,4},{7,5},{8,10},{9,11},{10,... | collective-permute-start | bytes 208904 | tf_op jit(solution)/shard_map/ppermute | solution.py:295
  24.2 0.3 collective-permute-start.8
  24.4 1.5 %shard_map.95.base_ref = f32[65,1024]{1,0:T(8,128)S(1)} custom-call(bf16[65,1024]{1,0:T(8,128)(2,1)S(1)} %copy-done.1, bf16[8,8,128,128]{3,2,1,0:T(8,128)(2,1)S(1)} %copy-done), custom_call_target="tpu_custom_call" | custom-call | flops 136314880 | bytes 2496512 | tf_op jit(solution)/shard_map/pallas_call | solution.py:270
  26.0 0.3 %collective-permute-start.11 = (bf16[384,128]{1,0:T(8,128)(2,1)S(1)}, bf16[384,128]{1,0:T(8,128)(2,1)S(1)}, u32[]{:S(2)}, u32[]{:S(2)}) collective-permute-start(bf16[384,128]{1,0:T(8,128)(2,1)S(1)} %get-tuple-element.50), channel_id=1, source_target_pairs={{0,4},{1,5},{2,6},{3,7},{4,0},{5,1},{6,2},{7,3},{8,12},{9,13},{10,... | collective-permute-start | bytes 294920 | tf_op jit(solution)/shard_map/ppermute | solution.py:295
  26.3 0.9 %collective-permute-done.7.refs_2_.refs_4_ = bf16[272,128]{1,0:T(8,128)(2,1)S(1)} collective-permute-done((bf16[272,128]{1,0:T(8,128)(2,1)S(1)}, bf16[272,128]{1,0:T(8,128)(2,1)S(1)}, u32[]{:S(2)}, u32[]{:S(2)}) %collective-permute-start.7) | collective-permute-done | bytes 69664 | tf_op jit(solution)/shard_map/ppermute | solution.py:295
  27.2 1.1 %collective-permute-done.8.refs_3_.refs_5_ = bf16[272,128]{1,0:T(8,128)(2,1)S(1)} collective-permute-done((bf16[272,128]{1,0:T(8,128)(2,1)S(1)}, bf16[272,128]{1,0:T(8,128)(2,1)S(1)}, u32[]{:S(2)}, u32[]{:S(2)}) %collective-permute-start.8) | collective-permute-done | bytes 69664 | tf_op jit(solution)/shard_map/ppermute | solution.py:295
  28.3 1.4 %shard_map.96.base_ref = f32[65,1024]{1,0:T(8,128)S(1)} custom-call(s32[1,12]{1,0:T(1,128)S(1)} %copy-done.7, f32[65,1024]{1,0:T(8,128)S(1)} %shard_map.95.base_ref, bf16[1,12,64,64]{3,2,1,0:T(8,128)(2,1)S(1)} %copy-done.5, bf16[8,64,64]{2,1,0:T(8,128)(2,1)S(1)} %copy-done.2, bf16[8,64,128]{2,1,0:T(8,128)(2,1)S(1)} %copy-done.3, ...), custom_call_target="tpu_custom_call" | custom-call | flops 68157440 | bytes 1105968 | tf_op jit(solution)/shard_map/pallas_call | solution.py:270
  29.8 1.3 %collective-permute-done.11.refs_1_ = bf16[384,128]{1,0:T(8,128)(2,1)S(1)} collective-permute-done((bf16[384,128]{1,0:T(8,128)(2,1)S(1)}, bf16[384,128]{1,0:T(8,128)(2,1)S(1)}, u32[]{:S(2)}, u32[]{:S(2)}) %collective-permute-start.11) | collective-permute-done | bytes 98336 | tf_op jit(solution)/shard_map/ppermute | solution.py:295
  31.1 0.8 %shard_map.98 = f32[65,1024]{1,0:T(8,128)} custom-call(f32[65,1024]{1,0:T(8,128)S(1)} %shard_map.96.base_ref, f32[384,128]{1,0:T(8,128)S(1)} %shard_map.97.refs_0_, bf16[384,128]{1,0:T(8,128)(2,1)S(1)} %collective-permute-done.11.refs_1_, bf16[272,128]{1,0:T(8,128)(2,1)S(1)} %get-tuple-element.43.refs_0_.refs_2_, ...), custom_call_target="tpu_custom_call" | custom-call | flops 133120 | bytes 1105920 | tf_op jit(solution)/shard_map/pallas_call | solution.py:270
  (24 shorter events, 0.1 us)
Async XLA Ops:
  0.0 24.4 %copy-start.1 = (bf16[65,1024]{1,0:T(8,128)(2,1)S(1)}, bf16[65,1024]{1,0:T(8,128)(2,1)}, u32[]{:S(2)}) copy-start(bf16[65,1024]{1,0:T(8,128)(2,1)} %probes_ref) | copy-start | bytes 399364
  0.0 24.4 %copy-start = (bf16[8,8,128,128]{3,2,1,0:T(8,128)(2,1)S(1)}, bf16[8,8,128,128]{3,2,1,0:T(8,128)(2,1)}, u32[]{:S(2)}) copy-start(bf16[8,8,128,128]{3,2,1,0:T(8,128)(2,1)} %local_ref.1) | copy-start | bytes 6291460
  3.5 24.8 %copy-start.2 = (bf16[8,64,64]{2,1,0:T(8,128)(2,1)S(1)}, bf16[8,64,64]{2,1,0:T(8,128)(2,1)}, u32[]{:S(2)}) copy-start(bf16[8,64,64]{2,1,0:T(8,128)(2,1)} %transfer_ref.1) | copy-start | bytes 196612
  3.5 24.8 %copy-start.3 = (bf16[8,64,128]{2,1,0:T(8,128)(2,1)S(1)}, bf16[8,64,128]{2,1,0:T(8,128)(2,1)}, u32[]{:S(2)}) copy-start(bf16[8,64,128]{2,1,0:T(8,128)(2,1)} %basis_ref.1) | copy-start | bytes 393220
  3.5 7.3 %collective-permute-start = (bf16[784,128]{1,0:T(8,128)(2,1)}, bf16[784,128]{1,0:T(8,128)(2,1)S(1)}, u32[]{:S(2)}, u32[]{:S(2)}) collective-permute-start(bf16[784,128]{1,0:T(8,128)(2,1)} %get-tuple-element.29), channel_id=1, source_target_pairs={{0,1},{1,0},{2,3},{3,2},{4,5},{5,4},{6,7},{7,6},{8,9},{9,8},{10,11... | collective-permute-start | bytes 602120 | tf_op jit(solution)/shard_map/ppermute | solution.py:295
  4.0 8.9 %collective-permute-start.1 = (bf16[784,128]{1,0:T(8,128)(2,1)}, bf16[784,128]{1,0:T(8,128)(2,1)S(1)}, u32[]{:S(2)}, u32[]{:S(2)}) collective-permute-start(bf16[784,128]{1,0:T(8,128)(2,1)} %get-tuple-element.34), channel_id=1, source_target_pairs={{0,2},{1,3},{2,0},{3,1},{4,6},{5,7},{6,4},{7,5},{8,10},{9,11},{10,... | collective-permute-start | bytes 602120 | tf_op jit(solution)/shard_map/ppermute | solution.py:295
  6.6 9.8 %collective-permute-start.2 = (bf16[784,128]{1,0:T(8,128)(2,1)}, bf16[784,128]{1,0:T(8,128)(2,1)S(1)}, u32[]{:S(2)}, u32[]{:S(2)}) collective-permute-start(bf16[784,128]{1,0:T(8,128)(2,1)} %get-tuple-element.35), channel_id=1, source_target_pairs={{0,3},{1,2},{2,1},{3,0},{4,7},{5,6},{6,5},{7,4},{8,11},{9,10},{10,... | collective-permute-start | bytes 602120 | tf_op jit(solution)/shard_map/ppermute | solution.py:295
  6.7 14.8 %collective-permute-start.3 = (bf16[320,128]{1,0:T(8,128)(2,1)}, bf16[320,128]{1,0:T(8,128)(2,1)S(1)}, u32[]{:S(2)}, u32[]{:S(2)}) collective-permute-start(bf16[320,128]{1,0:T(8,128)(2,1)} %get-tuple-element.38), channel_id=1, source_target_pairs={{0,8},{1,9},{2,10},{3,11},{4,12},{5,13},{6,14},{7,15},{8,0},{9,1},... | collective-permute-start | bytes 245768 | tf_op jit(solution)/shard_map/ppermute | solution.py:295
  9.5 12.0 %collective-permute-start.4 = (bf16[320,128]{1,0:T(8,128)(2,1)}, bf16[320,128]{1,0:T(8,128)(2,1)S(1)}, u32[]{:S(2)}, u32[]{:S(2)}) collective-permute-start(bf16[320,128]{1,0:T(8,128)(2,1)} %get-tuple-element.39), channel_id=1, source_target_pairs={{0,12},{1,13},{2,14},{3,15},{4,8},{5,9},{6,10},{7,11},{8,4},{9,5},... | collective-permute-start | bytes 245768 | tf_op jit(solution)/shard_map/ppermute | solution.py:295
  10.8 10.7 %collective-permute-start.5 = (bf16[320,128]{1,0:T(8,128)(2,1)}, bf16[320,128]{1,0:T(8,128)(2,1)S(1)}, u32[]{:S(2)}, u32[]{:S(2)}) collective-permute-start(bf16[320,128]{1,0:T(8,128)(2,1)} %get-tuple-element.40), channel_id=1, source_target_pairs={{0,4},{1,5},{2,6},{3,7},{4,0},{5,1},{6,2},{7,3},{8,12},{9,13},{10,... | collective-permute-start | bytes 245768 | tf_op jit(solution)/shard_map/ppermute | solution.py:295
  11.1 0.9 %copy-start.4 = (bf16[784,128]{1,0:T(8,128)(2,1)S(1)}, bf16[784,128]{1,0:T(8,128)(2,1)}, u32[]{:S(2)}) copy-start(bf16[784,128]{1,0:T(8,128)(2,1)} %get-tuple-element.28.refs_0_) | copy-start | bytes 602116
  12.0 0.9 %copy-start.6 = (bf16[320,128]{1,0:T(8,128)(2,1)S(1)}, bf16[320,128]{1,0:T(8,128)(2,1)}, u32[]{:S(2)}) copy-start(bf16[320,128]{1,0:T(8,128)(2,1)} %get-tuple-element.30.refs_2_) | copy-start | bytes 245764
  12.9 15.4 %copy-start.5 = (bf16[1,12,64,64]{3,2,1,0:T(8,128)(2,1)S(1)}, bf16[1,12,64,64]{3,2,1,0:T(8,128)(2,1)}, u32[]{:S(2)}) copy-start(bf16[1,12,64,64]{3,2,1,0:T(8,128)(2,1)} %couplings_ref.1) | copy-start | bytes 294916
  12.9 15.4 %copy-start.7 = (s32[1,12]{1,0:T(1,128)S(1)}, s32[1,12]{1,0:T(1,128)}, u32[]{:S(2)}) copy-start(s32[1,12]{1,0:T(1,128)} %partner_ref.1) | copy-start | bytes 148
  17.5 12.2 %collective-permute-start.9 = (bf16[384,128]{1,0:T(8,128)(2,1)S(1)}, bf16[384,128]{1,0:T(8,128)(2,1)S(1)}, u32[]{:S(2)}, u32[]{:S(2)}) collective-permute-start(bf16[384,128]{1,0:T(8,128)(2,1)S(1)} %get-tuple-element.48), channel_id=1, source_target_pairs={{0,8},{1,9},{2,10},{3,11},{4,12},{5,13},{6,14},{7,15},{8,0},{9,1},... | collective-permute-start | bytes 294920 | tf_op jit(solution)/shard_map/ppermute | solution.py:295
  20.2 9.6 %collective-permute-start.10 = (bf16[384,128]{1,0:T(8,128)(2,1)S(1)}, bf16[384,128]{1,0:T(8,128)(2,1)S(1)}, u32[]{:S(2)}, u32[]{:S(2)}) collective-permute-start(bf16[384,128]{1,0:T(8,128)(2,1)S(1)} %get-tuple-element.49), channel_id=1, source_target_pairs={{0,12},{1,13},{2,14},{3,15},{4,8},{5,9},{6,10},{7,11},{8,4},{9,5},... | collective-permute-start | bytes 294920 | tf_op jit(solution)/shard_map/ppermute | solution.py:295
  22.5 3.5 %collective-permute-start.6 = (bf16[272,128]{1,0:T(8,128)(2,1)S(1)}, bf16[272,128]{1,0:T(8,128)(2,1)S(1)}, u32[]{:S(2)}, u32[]{:S(2)}) collective-permute-start(bf16[272,128]{1,0:T(8,128)(2,1)S(1)} %get-tuple-element.44), channel_id=1, source_target_pairs={{0,1},{1,0},{2,3},{3,2},{4,5},{5,4},{6,7},{7,6},{8,9},{9,8},{10,11... | collective-permute-start | bytes 208904 | tf_op jit(solution)/shard_map/ppermute | solution.py:295
  22.6 4.5 %collective-permute-start.7 = (bf16[272,128]{1,0:T(8,128)(2,1)S(1)}, bf16[272,128]{1,0:T(8,128)(2,1)S(1)}, u32[]{:S(2)}, u32[]{:S(2)}) collective-permute-start(bf16[272,128]{1,0:T(8,128)(2,1)S(1)} %get-tuple-element.45), channel_id=1, source_target_pairs={{0,2},{1,3},{2,0},{3,1},{4,6},{5,7},{6,4},{7,5},{8,10},{9,11},{10,... | collective-permute-start | bytes 208904 | tf_op jit(solution)/shard_map/ppermute | solution.py:295
  24.2 4.1 %collective-permute-start.8 = (bf16[272,128]{1,0:T(8,128)(2,1)S(1)}, bf16[272,128]{1,0:T(8,128)(2,1)S(1)}, u32[]{:S(2)}, u32[]{:S(2)}) collective-permute-start(bf16[272,128]{1,0:T(8,128)(2,1)S(1)} %get-tuple-element.46), channel_id=1, source_target_pairs={{0,3},{1,2},{2,1},{3,0},{4,7},{5,6},{6,5},{7,4},{8,11},{9,10},{10,... | collective-permute-start | bytes 208904 | tf_op jit(solution)/shard_map/ppermute | solution.py:295
  26.0 5.1 %collective-permute-start.11 = (bf16[384,128]{1,0:T(8,128)(2,1)S(1)}, bf16[384,128]{1,0:T(8,128)(2,1)S(1)}, u32[]{:S(2)}, u32[]{:S(2)}) collective-permute-start(bf16[384,128]{1,0:T(8,128)(2,1)S(1)} %get-tuple-element.50), channel_id=1, source_target_pairs={{0,4},{1,5},{2,6},{3,7},{4,0},{5,1},{6,2},{7,3},{8,12},{9,13},{10,... | collective-permute-start | bytes 294920 | tf_op jit(solution)/shard_map/ppermute | solution.py:295

commit v19 on v18

--- a/solution.py
+++ b/solution.py
@@ -209,11 +209,14 @@
 
 def local_kernel(probes_ref, local_ref, out_ref):
     leaves, size = local_ref.shape[0], local_ref.shape[2]
-    for i in range(leaves):
-        total = dot_t(probes_ref[:, :size], local_ref[i, 0])
-        for c in range(1, leaves):
-            total += dot_t(probes_ref[:, c * size : (c + 1) * size], local_ref[i, c])
-        out_ref[:, i * size : (i + 1) * size] = total
+    for i in range(0, leaves, 2):
+        total = 0.0
+        for c in range(0, leaves, 2):
+            square = jnp.concatenate(
+                [jnp.concatenate([local_ref[r, c], local_ref[r, c + 1]], axis=1) for r in (i, i + 1)], axis=0
+            )
+            total += dot_t(probes_ref[:, c * size : (c + 2) * size], square)
+        out_ref[:, i * size : (i + 2) * size] = total
 
 
 def far_kernel(by_high, low, partner_ref, base_ref, couplings_ref, transfer_ref, basis_ref, *refs):
@@ -354,15 +357,15 @@
     came_high[0], to_high[0] = lax.optimization_barrier((came_high[0], to_high[0]))
     to_low = summed(by_high, planes, [came_high[k] for k in planes])
     base_shape = jax.ShapeDtypeStruct((columns, points), F32)
-    probes_then, to_low[0] = lax.optimization_barrier((probes, to_low[0]))
-    base = call(
-        local_kernel, base_shape, ([VMEM] * 2, VMEM), (probes_then, local_blocks), [], leaves * leaves * unit, 0
-    )
     for k in planes[1:]:
         to_high[k] = relative(to_high[k], k * low)
     for k in range(1, low):
         to_low[k] = relative(to_low[k], k)
 
+    probes_then, to_low[1] = lax.optimization_barrier((probes, to_low[1]))
+    base = call(
+        local_kernel, base_shape, ([VMEM] * 2, VMEM), (probes_then, local_blocks), [], leaves * leaves * unit, 0
+    )
     boxes = jax.ShapeDtypeStruct((devices, columns, rank), BF16)
     base = call(
         functools.partial(far_kernel, by_high, low),

time: 32 us -> 31 us (0.969)
  Pallas kernels: 9.22 us -> 8.46 us
    pallas_call x8, Pallas kernels: 9.22 us -> 8.46 us  [call(): pl.pallas_call(kernel, out_shape=out_shape, in_specs=specs[0], out_specs=...]
  transfers between devices with their start and end apart: 12 -> 12, of which waited for: 4 -> 4; matrix products, arithmetic and copies ran while one was open for 0% -> 0% of each run, Pallas kernels for 16% -> 14%
where the time goes in v19:
time: 31 us; the launch traced here: 30.8 us
  starting transfers between devices  13.7 us (44%)
  Pallas kernels  8.46 us (27%)
  waiting for transfers between devices  6.64 us (21%)
  local copies, waits for them, and re-layouts  1.84 us (6%)
    ppermute x12, starting transfers between devices, per_device(): lax.ppermute(x, 'leaf', [(i, i ^ way) for i in range(devices)])  13.7 us
    pallas_call x8, Pallas kernels, call(): pl.pallas_call(kernel, out_shape=out_shape, in_specs=specs[0], out_specs=...  8.46 us
    ppermute x12, waiting for transfers between devices, per_device(): lax.ppermute(x, 'leaf', [(i, i ^ way) for i in range(devices)])  6.64 us
    unnamed x16, local copies, waits for them, and re-layouts  1.84 us
  transfers between devices with their start and end apart: 12, of which 4 were waited for; matrix products, arithmetic and copies ran while one was open for 0% of the time, Pallas kernels for 14%

profile of v19, /device:TPU:0, one launch (start us, length us, event | category | flops | bytes accessed | tf_op | source)
XLA Modules:
  0.0 30.8 jit_solution(17547695563813659957)
XLA Ops:
  0.0 3.5 %shard_map.91 = (bf16[784,128]{1,0:T(8,128)(2,1)}, bf16[784,128]{1,0:T(8,128)(2,1)}, bf16[784,128]{1,0:T(8,128)(2,1)}, bf16[784,128]{1,0:T(8,128)(2,1)}, bf16[32...) custom-call(s32[4,8]{1,0:T(4,128)} %bitcast.2, ...), custom_call_target="tpu_custom_call" | custom-call | flops 68157440 | bytes 2509056 | tf_op jit(solution)/shard_map/pallas_call | solution.py:273
  3.5 0.5 %collective-permute-start = (bf16[784,128]{1,0:T(8,128)(2,1)}, bf16[784,128]{1,0:T(8,128)(2,1)S(1)}, u32[]{:S(2)}, u32[]{:S(2)}) collective-permute-start(bf16[784,128]{1,0:T(8,128)(2,1)} %get-tuple-element.29), channel_id=1, source_target_pairs={{0,1},{1,0},{2,3},{3,2},{4,5},{5,4},{6,7},{7,6},{8,9},{9,8},{10,11... | collective-permute-start | bytes 602120 | tf_op jit(solution)/shard_map/ppermute | solution.py:298
  4.0 2.6 %collective-permute-start.1 = (bf16[784,128]{1,0:T(8,128)(2,1)}, bf16[784,128]{1,0:T(8,128)(2,1)S(1)}, u32[]{:S(2)}, u32[]{:S(2)}) collective-permute-start(bf16[784,128]{1,0:T(8,128)(2,1)} %get-tuple-element.34), channel_id=1, source_target_pairs={{0,2},{1,3},{2,0},{3,1},{4,6},{5,7},{6,4},{7,5},{8,10},{9,11},{10,... | collective-permute-start | bytes 602120 | tf_op jit(solution)/shard_map/ppermute | solution.py:298
  6.6 0.1 collective-permute-start.2
  6.7 2.8 %collective-permute-start.3 = (bf16[320,128]{1,0:T(8,128)(2,1)}, bf16[320,128]{1,0:T(8,128)(2,1)S(1)}, u32[]{:S(2)}, u32[]{:S(2)}) collective-permute-start(bf16[320,128]{1,0:T(8,128)(2,1)} %get-tuple-element.38), channel_id=1, source_target_pairs={{0,8},{1,9},{2,10},{3,11},{4,12},{5,13},{6,14},{7,15},{8,0},{9,1},... | collective-permute-start | bytes 245768 | tf_op jit(solution)/shard_map/ppermute | solution.py:298
  9.5 1.3 %collective-permute-start.4 = (bf16[320,128]{1,0:T(8,128)(2,1)}, bf16[320,128]{1,0:T(8,128)(2,1)S(1)}, u32[]{:S(2)}, u32[]{:S(2)}) collective-permute-start(bf16[320,128]{1,0:T(8,128)(2,1)} %get-tuple-element.39), channel_id=1, source_target_pairs={{0,12},{1,13},{2,14},{3,15},{4,8},{5,9},{6,10},{7,11},{8,4},{9,5},... | collective-permute-start | bytes 245768 | tf_op jit(solution)/shard_map/ppermute | solution.py:298
  10.8 0.2 collective-permute-start.5
  11.1 0.9 %copy-done.4 = bf16[784,128]{1,0:T(8,128)(2,1)S(1)} copy-done((bf16[784,128]{1,0:T(8,128)(2,1)S(1)}, bf16[784,128]{1,0:T(8,128)(2,1)}, u32[]{:S(2)}) %copy-start.4) | copy-done | bytes 200728
  12.0 0.9 %copy-done.6 = bf16[320,128]{1,0:T(8,128)(2,1)S(1)} copy-done((bf16[320,128]{1,0:T(8,128)(2,1)S(1)}, bf16[320,128]{1,0:T(8,128)(2,1)}, u32[]{:S(2)}) %copy-start.6) | copy-done | bytes 81944
  13.0 3.5 %collective-permute-done.2.refs_3_ = bf16[784,128]{1,0:T(8,128)(2,1)S(1)} collective-permute-done((bf16[784,128]{1,0:T(8,128)(2,1)}, bf16[784,128]{1,0:T(8,128)(2,1)S(1)}, u32[]{:S(2)}, u32[]{:S(2)}) %collective-permute-start.2) | collective-permute-done | bytes 200736 | tf_op jit(solution)/shard_map/ppermute | solution.py:298
  16.5 1.0 %shard_map.93 = (bf16[384,128]{1,0:T(8,128)(2,1)S(1)}, bf16[384,128]{1,0:T(8,128)(2,1)S(1)}, bf16[384,128]{1,0:T(8,128)(2,1)S(1)}, bf16[384,128]{1,0:T(8,128)(2,1)S(1)}) custom-call(bf16[784,128]{1,0:T(8,128)(2,1)S(1)} %get-tuple-element.32.refs_0_, bf16[784,128]{1,0:T(8,128)(2,1)S(1)} %get-tuple-element.33.refs_1_, ...), custom_call_target="tpu_custom_call" | custom-call | flops 393216 | bytes 1196032 | tf_op jit(solution)/shard_map/pallas_call | solution.py:273
  17.5 2.7 %collective-permute-start.9 = (bf16[384,128]{1,0:T(8,128)(2,1)S(1)}, bf16[384,128]{1,0:T(8,128)(2,1)S(1)}, u32[]{:S(2)}, u32[]{:S(2)}) collective-permute-start(bf16[384,128]{1,0:T(8,128)(2,1)S(1)} %get-tuple-element.48), channel_id=1, source_target_pairs={{0,8},{1,9},{2,10},{3,11},{4,12},{5,13},{6,14},{7,15},{8,0},{9,1},... | collective-permute-start | bytes 294920 | tf_op jit(solution)/shard_map/ppermute | solution.py:298
  20.2 1.4 %collective-permute-start.10 = (bf16[384,128]{1,0:T(8,128)(2,1)S(1)}, bf16[384,128]{1,0:T(8,128)(2,1)S(1)}, u32[]{:S(2)}, u32[]{:S(2)}) collective-permute-start(bf16[384,128]{1,0:T(8,128)(2,1)S(1)} %get-tuple-element.49), channel_id=1, source_target_pairs={{0,12},{1,13},{2,14},{3,15},{4,8},{5,9},{6,10},{7,11},{8,4},{9,5},... | collective-permute-start | bytes 294920 | tf_op jit(solution)/shard_map/ppermute | solution.py:298
  21.6 0.9 %shard_map.94 = (bf16[272,128]{1,0:T(8,128)(2,1)S(1)}, bf16[272,128]{1,0:T(8,128)(2,1)S(1)}, bf16[272,128]{1,0:T(8,128)(2,1)S(1)}, bf16[272,128]{1,0:T(8,128)(2,1)S(1)}) custom-call(bf16[320,128]{1,0:T(8,128)(2,1)S(1)} %get-tuple-element.37.refs_0_, bf16[320,128]{1,0:T(8,128)(2,1)S(1)} %collective-permute-done.3.refs_1_, ...), custom_call_target="tpu_custom_call" | custom-call | flops 131072 | bytes 606208 | tf_op jit(solution)/shard_map/pallas_call | solution.py:273
  22.5 0.1 collective-permute-start.6
  22.6 1.6 %collective-permute-start.7 = (bf16[272,128]{1,0:T(8,128)(2,1)S(1)}, bf16[272,128]{1,0:T(8,128)(2,1)S(1)}, u32[]{:S(2)}, u32[]{:S(2)}) collective-permute-start(bf16[272,128]{1,0:T(8,128)(2,1)S(1)} %get-tuple-element.45), channel_id=1, source_target_pairs={{0,2},{1,3},{2,0},{3,1},{4,6},{5,7},{6,4},{7,5},{8,10},{9,11},{10,... | collective-permute-start | bytes 208904 | tf_op jit(solution)/shard_map/ppermute | solution.py:298
  24.2 0.3 collective-permute-start.8
  24.5 0.2 collective-permute-start.11
  24.7 0.7 %shard_map.95.base_ref = f32[65,1024]{1,0:T(8,128)S(1)} custom-call(bf16[65,1024]{1,0:T(8,128)(2,1)S(1)} %copy-done.1, bf16[8,8,128,128]{3,2,1,0:T(8,128)(2,1)S(1)} %copy-done), custom_call_target="tpu_custom_call" | custom-call | flops 136314880 | bytes 2496512 | tf_op jit(solution)/shard_map/pallas_call | solution.py:273
  25.4 1.8 %collective-permute-done.7.refs_2_.refs_4_ = bf16[272,128]{1,0:T(8,128)(2,1)S(1)} collective-permute-done((bf16[272,128]{1,0:T(8,128)(2,1)S(1)}, bf16[272,128]{1,0:T(8,128)(2,1)S(1)}, u32[]{:S(2)}, u32[]{:S(2)}) %collective-permute-start.7) | collective-permute-done | bytes 69664 | tf_op jit(solution)/shard_map/ppermute | solution.py:298
  27.2 1.1 %collective-permute-done.8.refs_3_.refs_5_ = bf16[272,128]{1,0:T(8,128)(2,1)S(1)} collective-permute-done((bf16[272,128]{1,0:T(8,128)(2,1)S(1)}, bf16[272,128]{1,0:T(8,128)(2,1)S(1)}, u32[]{:S(2)}, u32[]{:S(2)}) %collective-permute-start.8) | collective-permute-done | bytes 69664 | tf_op jit(solution)/shard_map/ppermute | solution.py:298
  28.4 1.4 %shard_map.96.base_ref = f32[65,1024]{1,0:T(8,128)S(1)} custom-call(s32[1,12]{1,0:T(1,128)S(1)} %copy-done.7, f32[65,1024]{1,0:T(8,128)S(1)} %shard_map.95.base_ref, bf16[1,12,64,64]{3,2,1,0:T(8,128)(2,1)S(1)} %copy-done.5, bf16[8,64,64]{2,1,0:T(8,128)(2,1)S(1)} %copy-done.2, bf16[8,64,128]{2,1,0:T(8,128)(2,1)S(1)} %copy-done.3, ...), custom_call_target="tpu_custom_call" | custom-call | flops 68157440 | bytes 1105968 | tf_op jit(solution)/shard_map/pallas_call | solution.py:273
  29.9 0.2 collective-permute-done.11.refs_1_
  30.0 0.8 %shard_map.98 = f32[65,1024]{1,0:T(8,128)} custom-call(f32[65,1024]{1,0:T(8,128)S(1)} %shard_map.96.base_ref, f32[384,128]{1,0:T(8,128)S(1)} %shard_map.97.refs_0_, bf16[384,128]{1,0:T(8,128)(2,1)S(1)} %collective-permute-done.11.refs_1_, bf16[272,128]{1,0:T(8,128)(2,1)S(1)} %get-tuple-element.43.refs_0_.refs_2_, ...), custom_call_target="tpu_custom_call" | custom-call | flops 133120 | bytes 1105920 | tf_op jit(solution)/shard_map/pallas_call | solution.py:273
  (24 shorter events, 0.1 us)
Async XLA Ops:
  0.0 24.7 %copy-start.1 = (bf16[65,1024]{1,0:T(8,128)(2,1)S(1)}, bf16[65,1024]{1,0:T(8,128)(2,1)}, u32[]{:S(2)}) copy-start(bf16[65,1024]{1,0:T(8,128)(2,1)} %probes_ref) | copy-start | bytes 399364
  0.0 24.7 %copy-start = (bf16[8,8,128,128]{3,2,1,0:T(8,128)(2,1)S(1)}, bf16[8,8,128,128]{3,2,1,0:T(8,128)(2,1)}, u32[]{:S(2)}) copy-start(bf16[8,8,128,128]{3,2,1,0:T(8,128)(2,1)} %local_ref.1) | copy-start | bytes 6291460
  3.5 24.9 %copy-start.2 = (bf16[8,64,64]{2,1,0:T(8,128)(2,1)S(1)}, bf16[8,64,64]{2,1,0:T(8,128)(2,1)}, u32[]{:S(2)}) copy-start(bf16[8,64,64]{2,1,0:T(8,128)(2,1)} %transfer_ref.1) | copy-start | bytes 196612
  3.5 24.9 %copy-start.3 = (bf16[8,64,128]{2,1,0:T(8,128)(2,1)S(1)}, bf16[8,64,128]{2,1,0:T(8,128)(2,1)}, u32[]{:S(2)}) copy-start(bf16[8,64,128]{2,1,0:T(8,128)(2,1)} %basis_ref.1) | copy-start | bytes 393220
  3.5 7.3 %collective-permute-start = (bf16[784,128]{1,0:T(8,128)(2,1)}, bf16[784,128]{1,0:T(8,128)(2,1)S(1)}, u32[]{:S(2)}, u32[]{:S(2)}) collective-permute-start(bf16[784,128]{1,0:T(8,128)(2,1)} %get-tuple-element.29), channel_id=1, source_target_pairs={{0,1},{1,0},{2,3},{3,2},{4,5},{5,4},{6,7},{7,6},{8,9},{9,8},{10,11... | collective-permute-start | bytes 602120 | tf_op jit(solution)/shard_map/ppermute | solution.py:298
  4.0 8.9 %collective-permute-start.1 = (bf16[784,128]{1,0:T(8,128)(2,1)}, bf16[784,128]{1,0:T(8,128)(2,1)S(1)}, u32[]{:S(2)}, u32[]{:S(2)}) collective-permute-start(bf16[784,128]{1,0:T(8,128)(2,1)} %get-tuple-element.34), channel_id=1, source_target_pairs={{0,2},{1,3},{2,0},{3,1},{4,6},{5,7},{6,4},{7,5},{8,10},{9,11},{10,... | collective-permute-start | bytes 602120 | tf_op jit(solution)/shard_map/ppermute | solution.py:298
  6.6 9.8 %collective-permute-start.2 = (bf16[784,128]{1,0:T(8,128)(2,1)}, bf16[784,128]{1,0:T(8,128)(2,1)S(1)}, u32[]{:S(2)}, u32[]{:S(2)}) collective-permute-start(bf16[784,128]{1,0:T(8,128)(2,1)} %get-tuple-element.35), channel_id=1, source_target_pairs={{0,3},{1,2},{2,1},{3,0},{4,7},{5,6},{6,5},{7,4},{8,11},{9,10},{10,... | collective-permute-start | bytes 602120 | tf_op jit(solution)/shard_map/ppermute | solution.py:298
  6.7 14.9 %collective-permute-start.3 = (bf16[320,128]{1,0:T(8,128)(2,1)}, bf16[320,128]{1,0:T(8,128)(2,1)S(1)}, u32[]{:S(2)}, u32[]{:S(2)}) collective-permute-start(bf16[320,128]{1,0:T(8,128)(2,1)} %get-tuple-element.38), channel_id=1, source_target_pairs={{0,8},{1,9},{2,10},{3,11},{4,12},{5,13},{6,14},{7,15},{8,0},{9,1},... | collective-permute-start | bytes 245768 | tf_op jit(solution)/shard_map/ppermute | solution.py:298
  9.5 12.1 %collective-permute-start.4 = (bf16[320,128]{1,0:T(8,128)(2,1)}, bf16[320,128]{1,0:T(8,128)(2,1)S(1)}, u32[]{:S(2)}, u32[]{:S(2)}) collective-permute-start(bf16[320,128]{1,0:T(8,128)(2,1)} %get-tuple-element.39), channel_id=1, source_target_pairs={{0,12},{1,13},{2,14},{3,15},{4,8},{5,9},{6,10},{7,11},{8,4},{9,5},... | collective-permute-start | bytes 245768 | tf_op jit(solution)/shard_map/ppermute | solution.py:298
  10.8 10.7 %collective-permute-start.5 = (bf16[320,128]{1,0:T(8,128)(2,1)}, bf16[320,128]{1,0:T(8,128)(2,1)S(1)}, u32[]{:S(2)}, u32[]{:S(2)}) collective-permute-start(bf16[320,128]{1,0:T(8,128)(2,1)} %get-tuple-element.40), channel_id=1, source_target_pairs={{0,4},{1,5},{2,6},{3,7},{4,0},{5,1},{6,2},{7,3},{8,12},{9,13},{10,... | collective-permute-start | bytes 245768 | tf_op jit(solution)/shard_map/ppermute | solution.py:298
  11.1 0.9 %copy-start.4 = (bf16[784,128]{1,0:T(8,128)(2,1)S(1)}, bf16[784,128]{1,0:T(8,128)(2,1)}, u32[]{:S(2)}) copy-start(bf16[784,128]{1,0:T(8,128)(2,1)} %get-tuple-element.28.refs_0_) | copy-start | bytes 602116
  12.0 0.9 %copy-start.6 = (bf16[320,128]{1,0:T(8,128)(2,1)S(1)}, bf16[320,128]{1,0:T(8,128)(2,1)}, u32[]{:S(2)}) copy-start(bf16[320,128]{1,0:T(8,128)(2,1)} %get-tuple-element.30.refs_2_) | copy-start | bytes 245764
  12.9 15.5 %copy-start.5 = (bf16[1,12,64,64]{3,2,1,0:T(8,128)(2,1)S(1)}, bf16[1,12,64,64]{3,2,1,0:T(8,128)(2,1)}, u32[]{:S(2)}) copy-start(bf16[1,12,64,64]{3,2,1,0:T(8,128)(2,1)} %couplings_ref.1) | copy-start | bytes 294916
  12.9 15.5 %copy-start.7 = (s32[1,12]{1,0:T(1,128)S(1)}, s32[1,12]{1,0:T(1,128)}, u32[]{:S(2)}) copy-start(s32[1,12]{1,0:T(1,128)} %partner_ref.1) | copy-start | bytes 148
  17.5 12.3 %collective-permute-start.9 = (bf16[384,128]{1,0:T(8,128)(2,1)S(1)}, bf16[384,128]{1,0:T(8,128)(2,1)S(1)}, u32[]{:S(2)}, u32[]{:S(2)}) collective-permute-start(bf16[384,128]{1,0:T(8,128)(2,1)S(1)} %get-tuple-element.48), channel_id=1, source_target_pairs={{0,8},{1,9},{2,10},{3,11},{4,12},{5,13},{6,14},{7,15},{8,0},{9,1},... | collective-permute-start | bytes 294920 | tf_op jit(solution)/shard_map/ppermute | solution.py:298
  20.2 9.6 %collective-permute-start.10 = (bf16[384,128]{1,0:T(8,128)(2,1)S(1)}, bf16[384,128]{1,0:T(8,128)(2,1)S(1)}, u32[]{:S(2)}, u32[]{:S(2)}) collective-permute-start(bf16[384,128]{1,0:T(8,128)(2,1)S(1)} %get-tuple-element.49), channel_id=1, source_target_pairs={{0,12},{1,13},{2,14},{3,15},{4,8},{5,9},{6,10},{7,11},{8,4},{9,5},... | collective-permute-start | bytes 294920 | tf_op jit(solution)/shard_map/ppermute | solution.py:298
  22.5 1.9 %collective-permute-start.6 = (bf16[272,128]{1,0:T(8,128)(2,1)S(1)}, bf16[272,128]{1,0:T(8,128)(2,1)S(1)}, u32[]{:S(2)}, u32[]{:S(2)}) collective-permute-start(bf16[272,128]{1,0:T(8,128)(2,1)S(1)} %get-tuple-element.41), channel_id=1, source_target_pairs={{0,1},{1,0},{2,3},{3,2},{4,5},{5,4},{6,7},{7,6},{8,9},{9,8},{10,11... | collective-permute-start | bytes 208904 | tf_op jit(solution)/shard_map/ppermute | solution.py:298
  22.6 4.6 %collective-permute-start.7 = (bf16[272,128]{1,0:T(8,128)(2,1)S(1)}, bf16[272,128]{1,0:T(8,128)(2,1)S(1)}, u32[]{:S(2)}, u32[]{:S(2)}) collective-permute-start(bf16[272,128]{1,0:T(8,128)(2,1)S(1)} %get-tuple-element.45), channel_id=1, source_target_pairs={{0,2},{1,3},{2,0},{3,1},{4,6},{5,7},{6,4},{7,5},{8,10},{9,11},{10,... | collective-permute-start | bytes 208904 | tf_op jit(solution)/shard_map/ppermute | solution.py:298
  24.2 4.2 %collective-permute-start.8 = (bf16[272,128]{1,0:T(8,128)(2,1)S(1)}, bf16[272,128]{1,0:T(8,128)(2,1)S(1)}, u32[]{:S(2)}, u32[]{:S(2)}) collective-permute-start(bf16[272,128]{1,0:T(8,128)(2,1)S(1)} %get-tuple-element.46), channel_id=1, source_target_pairs={{0,3},{1,2},{2,1},{3,0},{4,7},{5,6},{6,5},{7,4},{8,11},{9,10},{10,... | collective-permute-start | bytes 208904 | tf_op jit(solution)/shard_map/ppermute | solution.py:298
  24.5 5.6 %collective-permute-start.11 = (bf16[384,128]{1,0:T(8,128)(2,1)S(1)}, bf16[384,128]{1,0:T(8,128)(2,1)S(1)}, u32[]{:S(2)}, u32[]{:S(2)}) collective-permute-start(bf16[384,128]{1,0:T(8,128)(2,1)S(1)} %get-tuple-element.50), channel_id=1, source_target_pairs={{0,4},{1,5},{2,6},{3,7},{4,0},{5,1},{6,2},{7,3},{8,12},{9,13},{10,... | collective-permute-start | bytes 294920 | tf_op jit(solution)/shard_map/ppermute | solution.py:298

commit v20 on v19

--- a/solution.py
+++ b/solution.py
@@ -85,15 +85,16 @@
     leaves, per_leaf, size = blocks_ref.shape[:3]
     columns, rank = probes_ref.shape[0], basis_ref.shape[1]
     copies = Copies(sems)
-    chunk = leaves // 2
-    arrivals = []
+    cuts = (0, leaves // 4, leaves)
+    arrivals = {}
     early = [
         copies.start(probes_hbm, probes_ref),
         copies.start(dest_hbm, dest_ref),
         copies.start(leaf_hbm, leaf_ref),
     ]
-    for j in range(0, leaves, chunk):
-        arrivals.append(copies.start(blocks_hbm.at[pl.ds(j, chunk)], blocks_ref.at[pl.ds(j, chunk)]))
+    for j, after in zip(cuts, cuts[1:]):
+        part = pl.ds(j, after - j)
+        arrivals[j] = copies.start(blocks_hbm.at[part], blocks_ref.at[part])
         if j == 0:
             early += [copies.start(basis_hbm, basis_ref), copies.start(transfer_hbm, transfer_ref)]
 
@@ -110,8 +111,8 @@
     row = lax.broadcasted_iota(I32, numbers.shape, 0)
     lane = lax.broadcasted_iota(I32, numbers.shape, 1)
     for j in range(leaves):
-        if j % chunk == 0:
-            arrivals[j // chunk].wait()
+        if j in arrivals:
+            arrivals[j].wait()
         x = probes_ref[:, j * size : (j + 1) * size]
         box += dot_t(dot_t(x, basis_ref[j]).astype(BF16), transfer_ref[j])
         for first in range(0, per_leaf, 4):
@@ -323,17 +324,19 @@
     planes = across_first(high)
     for k in range(1, low):
         came_low[k] = relative(came_low[k], k)
-    for k in planes[1:]:
-        came_high[k] = relative(came_high[k], k * low)
-    came_low[0], came_low[1], came_high[0] = call(
+    came_low[0], came_high[0] = call(
         keep_kernel,
-        (message(by_low), message(by_low), message(by_high)),
-        ([VMEM] * 3, (VMEM,) * 3),
-        (came_low[0], came_low[1], came_high[0]),
+        (message(by_low), message(by_high)),
+        ([VMEM] * 2, (VMEM,) * 2),
+        (came_low[0], came_high[0]),
         [],
         0,
         0,
     )
+
+    came_high[1], came_low[0] = lax.optimization_barrier((came_high[1], came_low[0]))
+    for k in planes[1:]:
+        came_high[k] = relative(came_high[k], k * low)
 
     def summed(route, planes, came):
         total = jax.ShapeDtypeStruct((route.fan, (leaves + 1) * route.rows, size), F32)
@@ -353,7 +356,7 @@
             )
         )
 
-    to_high = summed(by_low, None, came_low)
+    to_high = summed(by_low, None, [came_low[k] for k in (0, *range(2, low), 1)])
     came_high[0], to_high[0] = lax.optimization_barrier((came_high[0], to_high[0]))
     to_low = summed(by_high, planes, [came_high[k] for k in planes])
     base_shape = jax.ShapeDtypeStruct((columns, points), F32)

time: 31 us -> 30.3 us (0.977)
  waiting for transfers between devices: 6.64 us -> 2.65 us
  starting transfers between devices: 13.7 us -> 17.4 us
    ppermute x12, waiting for transfers between devices: 6.64 us -> 2.65 us  [per_device(): lax.ppermute(x, 'leaf', [(i, i ^ way) for i in range(devices)])]
    ppermute x12, starting transfers between devices: 13.7 us -> 17.4 us  [per_device(): lax.ppermute(x, 'leaf', [(i, i ^ way) for i in range(devices)])]
  transfers between devices with their start and end apart: 12 -> 12, of which waited for: 4 -> 3; matrix products, arithmetic and copies ran while one was open for 0% -> 0% of each run, Pallas kernels for 14% -> 14%
where the time goes in v20:
time: 30.3 us; the launch traced here: 30.2 us
  starting transfers between devices  17.4 us (57%)
  Pallas kernels  8.17 us (27%)
  waiting for transfers between devices  2.65 us (9%)
  local copies, waits for them, and re-layouts  1.84 us (6%)
    ppermute x12, starting transfers between devices, per_device(): lax.ppermute(x, 'leaf', [(i, i ^ way) for i in range(devices)])  17.4 us
    pallas_call x8, Pallas kernels, call(): pl.pallas_call(kernel, out_shape=out_shape, in_specs=specs[0], out_specs=...  8.17 us
    ppermute x12, waiting for transfers between devices, per_device(): lax.ppermute(x, 'leaf', [(i, i ^ way) for i in range(devices)])  2.65 us
    unnamed x16, local copies, waits for them, and re-layouts  1.84 us
  transfers between devices with their start and end apart: 12, of which 3 were waited for; matrix products, arithmetic and copies ran while one was open for 0% of the time, Pallas kernels for 14%

profile of v20, /device:TPU:0, one launch (start us, length us, event | category | flops | bytes accessed | tf_op | source)
XLA Modules:
  0.0 30.2 jit_solution(2155477051624233169)
XLA Ops:
  0.0 3.2 %shard_map.91 = (bf16[784,128]{1,0:T(8,128)(2,1)}, bf16[784,128]{1,0:T(8,128)(2,1)}, bf16[784,128]{1,0:T(8,128)(2,1)}, bf16[784,128]{1,0:T(8,128)(2,1)}, bf16[32...) custom-call(s32[4,8]{1,0:T(4,128)} %bitcast.2, ...), custom_call_target="tpu_custom_call" | custom-call | flops 68157440 | bytes 2509056 | tf_op jit(solution)/shard_map/pallas_call | solution.py:274
  3.2 0.0 copy-start.2
  3.2 0.0 copy-start.3
  3.3 3.0 %collective-permute-start = (bf16[784,128]{1,0:T(8,128)(2,1)}, bf16[784,128]{1,0:T(8,128)(2,1)S(1)}, u32[]{:S(2)}, u32[]{:S(2)}) collective-permute-start(bf16[784,128]{1,0:T(8,128)(2,1)} %get-tuple-element.35), channel_id=1, source_target_pairs={{0,2},{1,3},{2,0},{3,1},{4,6},{5,7},{6,4},{7,5},{8,10},{9,11},{10,... | collective-permute-start | bytes 602120 | tf_op jit(solution)/shard_map/ppermute | solution.py:299
  6.3 0.2 collective-permute-start.2
  6.5 0.9 %copy-done.4 = bf16[784,128]{1,0:T(8,128)(2,1)S(1)} copy-done((bf16[784,128]{1,0:T(8,128)(2,1)S(1)}, bf16[784,128]{1,0:T(8,128)(2,1)}, u32[]{:S(2)}) %copy-start.4) | copy-done | bytes 200728
  7.4 0.9 %copy-done.6 = bf16[320,128]{1,0:T(8,128)(2,1)S(1)} copy-done((bf16[320,128]{1,0:T(8,128)(2,1)S(1)}, bf16[320,128]{1,0:T(8,128)(2,1)}, u32[]{:S(2)}) %copy-start.6) | copy-done | bytes 81944
  8.3 2.1 %collective-permute-start.5 = (bf16[320,128]{1,0:T(8,128)(2,1)}, bf16[320,128]{1,0:T(8,128)(2,1)S(1)}, u32[]{:S(2)}, u32[]{:S(2)}) collective-permute-start(bf16[320,128]{1,0:T(8,128)(2,1)} %get-tuple-element.42), channel_id=1, source_target_pairs={{0,4},{1,5},{2,6},{3,7},{4,0},{5,1},{6,2},{7,3},{8,12},{9,13},{10,... | collective-permute-start | bytes 245768 | tf_op jit(solution)/shard_map/ppermute | solution.py:299
  10.4 2.6 %collective-permute-start.3 = (bf16[320,128]{1,0:T(8,128)(2,1)}, bf16[320,128]{1,0:T(8,128)(2,1)S(1)}, u32[]{:S(2)}, u32[]{:S(2)}) collective-permute-start(bf16[320,128]{1,0:T(8,128)(2,1)} %get-tuple-element.40), channel_id=1, source_target_pairs={{0,8},{1,9},{2,10},{3,11},{4,12},{5,13},{6,14},{7,15},{8,0},{9,1},... | collective-permute-start | bytes 245768 | tf_op jit(solution)/shard_map/ppermute | solution.py:299
  13.0 0.0 collective-permute-done.refs_1_
  13.0 3.5 %collective-permute-start.4 = (bf16[320,128]{1,0:T(8,128)(2,1)}, bf16[320,128]{1,0:T(8,128)(2,1)S(1)}, u32[]{:S(2)}, u32[]{:S(2)}) collective-permute-start(bf16[320,128]{1,0:T(8,128)(2,1)} %get-tuple-element.41), channel_id=1, source_target_pairs={{0,12},{1,13},{2,14},{3,15},{4,8},{5,9},{6,10},{7,11},{8,4},{9,5},... | collective-permute-start | bytes 245768 | tf_op jit(solution)/shard_map/ppermute | solution.py:299
  16.5 1.0 %shard_map.93 = (bf16[384,128]{1,0:T(8,128)(2,1)S(1)}, bf16[384,128]{1,0:T(8,128)(2,1)S(1)}, bf16[384,128]{1,0:T(8,128)(2,1)S(1)}, bf16[384,128]{1,0:T(8,128)(2,1)S(1)}) custom-call(bf16[784,128]{1,0:T(8,128)(2,1)S(1)} %get-tuple-element.34.refs_0_, bf16[784,128]{1,0:T(8,128)(2,1)S(1)} %collective-permute-done.refs_1_, ...), custom_call_target="tpu_custom_call" | custom-call | flops 393216 | bytes 1196032 | tf_op jit(solution)/shard_map/pallas_call | solution.py:274
  17.5 1.3 %collective-permute-start.9 = (bf16[384,128]{1,0:T(8,128)(2,1)S(1)}, bf16[384,128]{1,0:T(8,128)(2,1)S(1)}, u32[]{:S(2)}, u32[]{:S(2)}) collective-permute-start(bf16[384,128]{1,0:T(8,128)(2,1)S(1)} %get-tuple-element.50), channel_id=1, source_target_pairs={{0,8},{1,9},{2,10},{3,11},{4,12},{5,13},{6,14},{7,15},{8,0},{9,1},... | collective-permute-start | bytes 294920 | tf_op jit(solution)/shard_map/ppermute | solution.py:299
  18.8 1.4 %collective-permute-start.10 = (bf16[384,128]{1,0:T(8,128)(2,1)S(1)}, bf16[384,128]{1,0:T(8,128)(2,1)S(1)}, u32[]{:S(2)}, u32[]{:S(2)}) collective-permute-start(bf16[384,128]{1,0:T(8,128)(2,1)S(1)} %get-tuple-element.51), channel_id=1, source_target_pairs={{0,12},{1,13},{2,14},{3,15},{4,8},{5,9},{6,10},{7,11},{8,4},{9,5},... | collective-permute-start | bytes 294920 | tf_op jit(solution)/shard_map/ppermute | solution.py:299
  20.2 0.9 %shard_map.94 = (bf16[272,128]{1,0:T(8,128)(2,1)S(1)}, bf16[272,128]{1,0:T(8,128)(2,1)S(1)}, bf16[272,128]{1,0:T(8,128)(2,1)S(1)}, bf16[272,128]{1,0:T(8,128)(2,1)S(1)}) custom-call(bf16[320,128]{1,0:T(8,128)(2,1)S(1)} %get-tuple-element.39.refs_0_, bf16[320,128]{1,0:T(8,128)(2,1)S(1)} %collective-permute-done.3.refs_1_, ...), custom_call_target="tpu_custom_call" | custom-call | flops 131072 | bytes 606208 | tf_op jit(solution)/shard_map/pallas_call | solution.py:274
  21.2 0.5 %collective-permute-start.6 = (bf16[272,128]{1,0:T(8,128)(2,1)S(1)}, bf16[272,128]{1,0:T(8,128)(2,1)S(1)}, u32[]{:S(2)}, u32[]{:S(2)}) collective-permute-start(bf16[272,128]{1,0:T(8,128)(2,1)S(1)} %get-tuple-element.43), channel_id=1, source_target_pairs={{0,1},{1,0},{2,3},{3,2},{4,5},{5,4},{6,7},{7,6},{8,9},{9,8},{10,11... | collective-permute-start | bytes 208904 | tf_op jit(solution)/shard_map/ppermute | solution.py:299
  21.7 1.5 %collective-permute-start.7 = (bf16[272,128]{1,0:T(8,128)(2,1)S(1)}, bf16[272,128]{1,0:T(8,128)(2,1)S(1)}, u32[]{:S(2)}, u32[]{:S(2)}) collective-permute-start(bf16[272,128]{1,0:T(8,128)(2,1)S(1)} %get-tuple-element.47), channel_id=1, source_target_pairs={{0,2},{1,3},{2,0},{3,1},{4,6},{5,7},{6,4},{7,5},{8,10},{9,11},{10,... | collective-permute-start | bytes 208904 | tf_op jit(solution)/shard_map/ppermute | solution.py:299
  23.2 1.3 %collective-permute-start.11 = (bf16[384,128]{1,0:T(8,128)(2,1)S(1)}, bf16[384,128]{1,0:T(8,128)(2,1)S(1)}, u32[]{:S(2)}, u32[]{:S(2)}) collective-permute-start(bf16[384,128]{1,0:T(8,128)(2,1)S(1)} %get-tuple-element.52), channel_id=1, source_target_pairs={{0,4},{1,5},{2,6},{3,7},{4,0},{5,1},{6,2},{7,3},{8,12},{9,13},{10,... | collective-permute-start | bytes 294920 | tf_op jit(solution)/shard_map/ppermute | solution.py:299
  24.5 0.7 %shard_map.95.base_ref = f32[65,1024]{1,0:T(8,128)S(1)} custom-call(bf16[65,1024]{1,0:T(8,128)(2,1)S(1)} %copy-done.1, bf16[8,8,128,128]{3,2,1,0:T(8,128)(2,1)S(1)} %copy-done), custom_call_target="tpu_custom_call" | custom-call | flops 136314880 | bytes 2496512 | tf_op jit(solution)/shard_map/pallas_call | solution.py:274
  25.3 0.7 %collective-permute-done.7.refs_2_.refs_4_ = bf16[272,128]{1,0:T(8,128)(2,1)S(1)} collective-permute-done((bf16[272,128]{1,0:T(8,128)(2,1)S(1)}, bf16[272,128]{1,0:T(8,128)(2,1)S(1)}, u32[]{:S(2)}, u32[]{:S(2)}) %collective-permute-start.7) | collective-permute-done | bytes 69664 | tf_op jit(solution)/shard_map/ppermute | solution.py:299
  26.0 1.7 %collective-permute-done.8.refs_3_.refs_5_ = bf16[272,128]{1,0:T(8,128)(2,1)S(1)} collective-permute-done((bf16[272,128]{1,0:T(8,128)(2,1)S(1)}, bf16[272,128]{1,0:T(8,128)(2,1)S(1)}, u32[]{:S(2)}, u32[]{:S(2)}) %collective-permute-start.8) | collective-permute-done | bytes 69664 | tf_op jit(solution)/shard_map/ppermute | solution.py:299
  27.6 1.4 %shard_map.96.base_ref = f32[65,1024]{1,0:T(8,128)S(1)} custom-call(s32[1,12]{1,0:T(1,128)S(1)} %copy-done.7, f32[65,1024]{1,0:T(8,128)S(1)} %shard_map.95.base_ref, bf16[1,12,64,64]{3,2,1,0:T(8,128)(2,1)S(1)} %copy-done.5, bf16[8,64,64]{2,1,0:T(8,128)(2,1)S(1)} %copy-done.2, bf16[8,64,128]{2,1,0:T(8,128)(2,1)S(1)} %copy-done.3, ...), custom_call_target="tpu_custom_call" | custom-call | flops 68157440 | bytes 1105968 | tf_op jit(solution)/shard_map/pallas_call | solution.py:274
  29.1 0.3 collective-permute-done.11.refs_1_
  29.4 0.8 %shard_map.98 = f32[65,1024]{1,0:T(8,128)} custom-call(f32[65,1024]{1,0:T(8,128)S(1)} %shard_map.96.base_ref, f32[384,128]{1,0:T(8,128)S(1)} %shard_map.97.refs_0_, bf16[384,128]{1,0:T(8,128)(2,1)S(1)} %collective-permute-done.11.refs_1_, bf16[272,128]{1,0:T(8,128)(2,1)S(1)} %get-tuple-element.45.refs_0_.refs_2_, ...), custom_call_target="tpu_custom_call" | custom-call | flops 133120 | bytes 1105920 | tf_op jit(solution)/shard_map/pallas_call | solution.py:274
  (24 shorter events, 0.1 us)
Async XLA Ops:
  0.0 24.5 %copy-start.1 = (bf16[65,1024]{1,0:T(8,128)(2,1)S(1)}, bf16[65,1024]{1,0:T(8,128)(2,1)}, u32[]{:S(2)}) copy-start(bf16[65,1024]{1,0:T(8,128)(2,1)} %probes_ref) | copy-start | bytes 399364
  0.0 24.5 %copy-start = (bf16[8,8,128,128]{3,2,1,0:T(8,128)(2,1)S(1)}, bf16[8,8,128,128]{3,2,1,0:T(8,128)(2,1)}, u32[]{:S(2)}) copy-start(bf16[8,8,128,128]{3,2,1,0:T(8,128)(2,1)} %local_ref.1) | copy-start | bytes 6291460
  3.2 24.4 %copy-start.2 = (bf16[8,64,64]{2,1,0:T(8,128)(2,1)S(1)}, bf16[8,64,64]{2,1,0:T(8,128)(2,1)}, u32[]{:S(2)}) copy-start(bf16[8,64,64]{2,1,0:T(8,128)(2,1)} %transfer_ref.1) | copy-start | bytes 196612
  3.2 24.4 %copy-start.3 = (bf16[8,64,128]{2,1,0:T(8,128)(2,1)S(1)}, bf16[8,64,128]{2,1,0:T(8,128)(2,1)}, u32[]{:S(2)}) copy-start(bf16[8,64,128]{2,1,0:T(8,128)(2,1)} %basis_ref.1) | copy-start | bytes 393220
  3.3 9.7 %collective-permute-start = (bf16[784,128]{1,0:T(8,128)(2,1)}, bf16[784,128]{1,0:T(8,128)(2,1)S(1)}, u32[]{:S(2)}, u32[]{:S(2)}) collective-permute-start(bf16[784,128]{1,0:T(8,128)(2,1)} %get-tuple-element.35), channel_id=1, source_target_pairs={{0,2},{1,3},{2,0},{3,1},{4,6},{5,7},{6,4},{7,5},{8,10},{9,11},{10,... | collective-permute-start | bytes 602120 | tf_op jit(solution)/shard_map/ppermute | solution.py:299
  6.3 10.2 %collective-permute-start.1 = (bf16[784,128]{1,0:T(8,128)(2,1)}, bf16[784,128]{1,0:T(8,128)(2,1)S(1)}, u32[]{:S(2)}, u32[]{:S(2)}) collective-permute-start(bf16[784,128]{1,0:T(8,128)(2,1)} %get-tuple-element.36), channel_id=1, source_target_pairs={{0,3},{1,2},{2,1},{3,0},{4,7},{5,6},{6,5},{7,4},{8,11},{9,10},{10,... | collective-permute-start | bytes 602120 | tf_op jit(solution)/shard_map/ppermute | solution.py:299
  6.3 10.2 %collective-permute-start.2 = (bf16[784,128]{1,0:T(8,128)(2,1)}, bf16[784,128]{1,0:T(8,128)(2,1)S(1)}, u32[]{:S(2)}, u32[]{:S(2)}) collective-permute-start(bf16[784,128]{1,0:T(8,128)(2,1)} %get-tuple-element.37), channel_id=1, source_target_pairs={{0,1},{1,0},{2,3},{3,2},{4,5},{5,4},{6,7},{7,6},{8,9},{9,8},{10,11... | collective-permute-start | bytes 602120 | tf_op jit(solution)/shard_map/ppermute | solution.py:299
  6.5 0.9 %copy-start.4 = (bf16[784,128]{1,0:T(8,128)(2,1)S(1)}, bf16[784,128]{1,0:T(8,128)(2,1)}, u32[]{:S(2)}) copy-start(bf16[784,128]{1,0:T(8,128)(2,1)} %get-tuple-element.29.refs_0_) | copy-start | bytes 602116
  7.4 0.9 %copy-start.6 = (bf16[320,128]{1,0:T(8,128)(2,1)S(1)}, bf16[320,128]{1,0:T(8,128)(2,1)}, u32[]{:S(2)}) copy-start(bf16[320,128]{1,0:T(8,128)(2,1)} %get-tuple-element.30.refs_1_) | copy-start | bytes 245764
  8.3 19.3 %copy-start.5 = (bf16[1,12,64,64]{3,2,1,0:T(8,128)(2,1)S(1)}, bf16[1,12,64,64]{3,2,1,0:T(8,128)(2,1)}, u32[]{:S(2)}) copy-start(bf16[1,12,64,64]{3,2,1,0:T(8,128)(2,1)} %couplings_ref.1) | copy-start | bytes 294916
  8.3 19.3 %copy-start.7 = (s32[1,12]{1,0:T(1,128)S(1)}, s32[1,12]{1,0:T(1,128)}, u32[]{:S(2)}) copy-start(s32[1,12]{1,0:T(1,128)} %partner_ref.1) | copy-start | bytes 148
  8.3 11.9 %collective-permute-start.5 = (bf16[320,128]{1,0:T(8,128)(2,1)}, bf16[320,128]{1,0:T(8,128)(2,1)S(1)}, u32[]{:S(2)}, u32[]{:S(2)}) collective-permute-start(bf16[320,128]{1,0:T(8,128)(2,1)} %get-tuple-element.42), channel_id=1, source_target_pairs={{0,4},{1,5},{2,6},{3,7},{4,0},{5,1},{6,2},{7,3},{8,12},{9,13},{10,... | collective-permute-start | bytes 245768 | tf_op jit(solution)/shard_map/ppermute | solution.py:299
  10.4 9.8 %collective-permute-start.3 = (bf16[320,128]{1,0:T(8,128)(2,1)}, bf16[320,128]{1,0:T(8,128)(2,1)S(1)}, u32[]{:S(2)}, u32[]{:S(2)}) collective-permute-start(bf16[320,128]{1,0:T(8,128)(2,1)} %get-tuple-element.40), channel_id=1, source_target_pairs={{0,8},{1,9},{2,10},{3,11},{4,12},{5,13},{6,14},{7,15},{8,0},{9,1},... | collective-permute-start | bytes 245768 | tf_op jit(solution)/shard_map/ppermute | solution.py:299
  13.0 7.2 %collective-permute-start.4 = (bf16[320,128]{1,0:T(8,128)(2,1)}, bf16[320,128]{1,0:T(8,128)(2,1)S(1)}, u32[]{:S(2)}, u32[]{:S(2)}) collective-permute-start(bf16[320,128]{1,0:T(8,128)(2,1)} %get-tuple-element.41), channel_id=1, source_target_pairs={{0,12},{1,13},{2,14},{3,15},{4,8},{5,9},{6,10},{7,11},{8,4},{9,5},... | collective-permute-start | bytes 245768 | tf_op jit(solution)/shard_map/ppermute | solution.py:299
  17.5 11.6 %collective-permute-start.9 = (bf16[384,128]{1,0:T(8,128)(2,1)S(1)}, bf16[384,128]{1,0:T(8,128)(2,1)S(1)}, u32[]{:S(2)}, u32[]{:S(2)}) collective-permute-start(bf16[384,128]{1,0:T(8,128)(2,1)S(1)} %get-tuple-element.50), channel_id=1, source_target_pairs={{0,8},{1,9},{2,10},{3,11},{4,12},{5,13},{6,14},{7,15},{8,0},{9,1},... | collective-permute-start | bytes 294920 | tf_op jit(solution)/shard_map/ppermute | solution.py:299
  18.8 10.3 %collective-permute-start.10 = (bf16[384,128]{1,0:T(8,128)(2,1)S(1)}, bf16[384,128]{1,0:T(8,128)(2,1)S(1)}, u32[]{:S(2)}, u32[]{:S(2)}) collective-permute-start(bf16[384,128]{1,0:T(8,128)(2,1)S(1)} %get-tuple-element.51), channel_id=1, source_target_pairs={{0,12},{1,13},{2,14},{3,15},{4,8},{5,9},{6,10},{7,11},{8,4},{9,5},... | collective-permute-start | bytes 294920 | tf_op jit(solution)/shard_map/ppermute | solution.py:299
  21.2 2.0 %collective-permute-start.6 = (bf16[272,128]{1,0:T(8,128)(2,1)S(1)}, bf16[272,128]{1,0:T(8,128)(2,1)S(1)}, u32[]{:S(2)}, u32[]{:S(2)}) collective-permute-start(bf16[272,128]{1,0:T(8,128)(2,1)S(1)} %get-tuple-element.43), channel_id=1, source_target_pairs={{0,1},{1,0},{2,3},{3,2},{4,5},{5,4},{6,7},{7,6},{8,9},{9,8},{10,11... | collective-permute-start | bytes 208904 | tf_op jit(solution)/shard_map/ppermute | solution.py:299
  21.7 4.3 %collective-permute-start.7 = (bf16[272,128]{1,0:T(8,128)(2,1)S(1)}, bf16[272,128]{1,0:T(8,128)(2,1)S(1)}, u32[]{:S(2)}, u32[]{:S(2)}) collective-permute-start(bf16[272,128]{1,0:T(8,128)(2,1)S(1)} %get-tuple-element.47), channel_id=1, source_target_pairs={{0,2},{1,3},{2,0},{3,1},{4,6},{5,7},{6,4},{7,5},{8,10},{9,11},{10,... | collective-permute-start | bytes 208904 | tf_op jit(solution)/shard_map/ppermute | solution.py:299
  23.2 4.5 %collective-permute-start.8 = (bf16[272,128]{1,0:T(8,128)(2,1)S(1)}, bf16[272,128]{1,0:T(8,128)(2,1)S(1)}, u32[]{:S(2)}, u32[]{:S(2)}) collective-permute-start(bf16[272,128]{1,0:T(8,128)(2,1)S(1)} %get-tuple-element.48), channel_id=1, source_target_pairs={{0,3},{1,2},{2,1},{3,0},{4,7},{5,6},{6,5},{7,4},{8,11},{9,10},{10,... | collective-permute-start | bytes 208904 | tf_op jit(solution)/shard_map/ppermute | solution.py:299
  23.2 6.2 %collective-permute-start.11 = (bf16[384,128]{1,0:T(8,128)(2,1)S(1)}, bf16[384,128]{1,0:T(8,128)(2,1)S(1)}, u32[]{:S(2)}, u32[]{:S(2)}) collective-permute-start(bf16[384,128]{1,0:T(8,128)(2,1)S(1)} %get-tuple-element.52), channel_id=1, source_target_pairs={{0,4},{1,5},{2,6},{3,7},{4,0},{5,1},{6,2},{7,3},{8,12},{9,13},{10,... | collective-permute-start | bytes 294920 | tf_op jit(solution)/shard_map/ppermute | solution.py:299

commit v21 on v20

--- a/solution.py
+++ b/solution.py
@@ -334,7 +334,6 @@
         0,
     )
 
-    came_high[1], came_low[0] = lax.optimization_barrier((came_high[1], came_low[0]))
     for k in planes[1:]:
         came_high[k] = relative(came_high[k], k * low)
 
@@ -351,7 +350,7 @@
                 [pltpu.VMEM((ways, size), I32), pltpu.SMEM((ways, size), I32)]
                 + like(total, tails)
                 + [pltpu.SemaphoreType.DMA(())],
-                devices * CAP * route.rows * size,
+                HEAVY if route is by_low else devices * CAP * route.rows * size,
                 4 * (total.size + tails.size),
             )
         )

time: 30.3 us -> 30 us (0.990)
  starting transfers between devices: 17.4 us -> 15.7 us
  waiting for transfers between devices: 2.65 us -> 4.07 us
    ppermute x12, starting transfers between devices: 17.4 us -> 15.7 us  [per_device(): lax.ppermute(x, 'leaf', [(i, i ^ way) for i in range(devices)])]
    ppermute x12, waiting for transfers between devices: 2.65 us -> 4.07 us  [per_device(): lax.ppermute(x, 'leaf', [(i, i ^ way) for i in range(devices)])]
where the time goes in v21:
time: 30 us; the launch traced here: 29.8 us
  starting transfers between devices  15.7 us (52%)
  Pallas kernels  8.03 us (27%)
  waiting for transfers between devices  4.07 us (14%)
  local copies, waits for them, and re-layouts  1.85 us (6%)
    ppermute x12, starting transfers between devices, per_device(): lax.ppermute(x, 'leaf', [(i, i ^ way) for i in range(devices)])  15.7 us
    pallas_call x8, Pallas kernels, call(): pl.pallas_call(kernel, out_shape=out_shape, in_specs=specs[0], out_specs=...  8.03 us
    ppermute x12, waiting for transfers between devices, per_device(): lax.ppermute(x, 'leaf', [(i, i ^ way) for i in range(devices)])  4.07 us
    unnamed x16, local copies, waits for them, and re-layouts  1.85 us
  transfers between devices with their start and end apart: 12, of which 3 were waited for; matrix products, arithmetic and copies ran while one was open for 0% of the time, Pallas kernels for 14%

profile of v21, /device:TPU:0, one launch (start us, length us, event | category | flops | bytes accessed | tf_op | source)
XLA Modules:
  0.0 29.8 jit_solution(10793580618082742458)
XLA Ops:
  0.0 3.1 %shard_map.91 = (bf16[784,128]{1,0:T(8,128)(2,1)}, bf16[784,128]{1,0:T(8,128)(2,1)}, bf16[784,128]{1,0:T(8,128)(2,1)}, bf16[784,128]{1,0:T(8,128)(2,1)}, bf16[32...) custom-call(s32[4,8]{1,0:T(4,128)} %bitcast.2, ...), custom_call_target="tpu_custom_call" | custom-call | flops 68157440 | bytes 2509056 | tf_op jit(solution)/shard_map/pallas_call | solution.py:274
  3.1 3.0 %collective-permute-start = (bf16[784,128]{1,0:T(8,128)(2,1)}, bf16[784,128]{1,0:T(8,128)(2,1)S(1)}, u32[]{:S(2)}, u32[]{:S(2)}) collective-permute-start(bf16[784,128]{1,0:T(8,128)(2,1)} %get-tuple-element.31), channel_id=1, source_target_pairs={{0,2},{1,3},{2,0},{3,1},{4,6},{5,7},{6,4},{7,5},{8,10},{9,11},{10,... | collective-permute-start | bytes 602120 | tf_op jit(solution)/shard_map/ppermute | solution.py:299
  6.1 0.2 collective-permute-start.2
  6.3 3.0 %collective-permute-start.3 = (bf16[320,128]{1,0:T(8,128)(2,1)}, bf16[320,128]{1,0:T(8,128)(2,1)S(1)}, u32[]{:S(2)}, u32[]{:S(2)}) collective-permute-start(bf16[320,128]{1,0:T(8,128)(2,1)} %get-tuple-element.36), channel_id=1, source_target_pairs={{0,8},{1,9},{2,10},{3,11},{4,12},{5,13},{6,14},{7,15},{8,0},{9,1},... | collective-permute-start | bytes 245768 | tf_op jit(solution)/shard_map/ppermute | solution.py:299
  9.3 1.3 %collective-permute-start.4 = (bf16[320,128]{1,0:T(8,128)(2,1)}, bf16[320,128]{1,0:T(8,128)(2,1)S(1)}, u32[]{:S(2)}, u32[]{:S(2)}) collective-permute-start(bf16[320,128]{1,0:T(8,128)(2,1)} %get-tuple-element.37), channel_id=1, source_target_pairs={{0,12},{1,13},{2,14},{3,15},{4,8},{5,9},{6,10},{7,11},{8,4},{9,5},... | collective-permute-start | bytes 245768 | tf_op jit(solution)/shard_map/ppermute | solution.py:299
  10.7 0.9 %copy-done.4 = bf16[784,128]{1,0:T(8,128)(2,1)S(1)} copy-done((bf16[784,128]{1,0:T(8,128)(2,1)S(1)}, bf16[784,128]{1,0:T(8,128)(2,1)}, u32[]{:S(2)}) %copy-start.4) | copy-done | bytes 200728
  11.6 0.9 %copy-done.6 = bf16[320,128]{1,0:T(8,128)(2,1)S(1)} copy-done((bf16[320,128]{1,0:T(8,128)(2,1)S(1)}, bf16[320,128]{1,0:T(8,128)(2,1)}, u32[]{:S(2)}) %copy-start.6) | copy-done | bytes 81944
  12.5 1.7 %collective-permute-start.5 = (bf16[320,128]{1,0:T(8,128)(2,1)}, bf16[320,128]{1,0:T(8,128)(2,1)S(1)}, u32[]{:S(2)}, u32[]{:S(2)}) collective-permute-start(bf16[320,128]{1,0:T(8,128)(2,1)} %get-tuple-element.38), channel_id=1, source_target_pairs={{0,4},{1,5},{2,6},{3,7},{4,0},{5,1},{6,2},{7,3},{8,12},{9,13},{10,... | collective-permute-start | bytes 245768 | tf_op jit(solution)/shard_map/ppermute | solution.py:299
  14.3 0.7 %collective-permute-done.1.refs_2_ = bf16[784,128]{1,0:T(8,128)(2,1)S(1)} collective-permute-done((bf16[784,128]{1,0:T(8,128)(2,1)}, bf16[784,128]{1,0:T(8,128)(2,1)S(1)}, u32[]{:S(2)}, u32[]{:S(2)}) %collective-permute-start.1) | collective-permute-done | bytes 200736 | tf_op jit(solution)/shard_map/ppermute | solution.py:299
  15.0 1.0 %shard_map.93 = (bf16[384,128]{1,0:T(8,128)(2,1)S(1)}, bf16[384,128]{1,0:T(8,128)(2,1)S(1)}, bf16[384,128]{1,0:T(8,128)(2,1)S(1)}, bf16[384,128]{1,0:T(8,128)(2,1)S(1)}) custom-call(bf16[784,128]{1,0:T(8,128)(2,1)S(1)} %get-tuple-element.30.refs_0_, bf16[784,128]{1,0:T(8,128)(2,1)S(1)} %collective-permute-done.refs_1_, ...), custom_call_target="tpu_custom_call" | custom-call | flops 4000000000 | bytes 1196032 | tf_op jit(solution)/shard_map/pallas_call | solution.py:274
  16.0 0.0 copy-start.2
  16.0 0.0 copy-start.3
  16.1 0.0 copy-start.5
  16.1 2.7 %collective-permute-start.9 = (bf16[384,128]{1,0:T(8,128)(2,1)S(1)}, bf16[384,128]{1,0:T(8,128)(2,1)S(1)}, u32[]{:S(2)}, u32[]{:S(2)}) collective-permute-start(bf16[384,128]{1,0:T(8,128)(2,1)S(1)} %get-tuple-element.46), channel_id=1, source_target_pairs={{0,8},{1,9},{2,10},{3,11},{4,12},{5,13},{6,14},{7,15},{8,0},{9,1},... | collective-permute-start | bytes 294920 | tf_op jit(solution)/shard_map/ppermute | solution.py:299
  18.7 1.4 %collective-permute-start.10 = (bf16[384,128]{1,0:T(8,128)(2,1)S(1)}, bf16[384,128]{1,0:T(8,128)(2,1)S(1)}, u32[]{:S(2)}, u32[]{:S(2)}) collective-permute-start(bf16[384,128]{1,0:T(8,128)(2,1)S(1)} %get-tuple-element.47), channel_id=1, source_target_pairs={{0,12},{1,13},{2,14},{3,15},{4,8},{5,9},{6,10},{7,11},{8,4},{9,5},... | collective-permute-start | bytes 294920 | tf_op jit(solution)/shard_map/ppermute | solution.py:299
  20.1 0.9 %shard_map.94 = (bf16[272,128]{1,0:T(8,128)(2,1)S(1)}, bf16[272,128]{1,0:T(8,128)(2,1)S(1)}, bf16[272,128]{1,0:T(8,128)(2,1)S(1)}, bf16[272,128]{1,0:T(8,128)(2,1)S(1)}) custom-call(bf16[320,128]{1,0:T(8,128)(2,1)S(1)} %get-tuple-element.35.refs_0_, bf16[320,128]{1,0:T(8,128)(2,1)S(1)} %collective-permute-done.3.refs_1_, ...), custom_call_target="tpu_custom_call" | custom-call | flops 131072 | bytes 606208 | tf_op jit(solution)/shard_map/pallas_call | solution.py:274
  21.0 0.5 %collective-permute-start.6 = (bf16[272,128]{1,0:T(8,128)(2,1)S(1)}, bf16[272,128]{1,0:T(8,128)(2,1)S(1)}, u32[]{:S(2)}, u32[]{:S(2)}) collective-permute-start(bf16[272,128]{1,0:T(8,128)(2,1)S(1)} %get-tuple-element.39), channel_id=1, source_target_pairs={{0,1},{1,0},{2,3},{3,2},{4,5},{5,4},{6,7},{7,6},{8,9},{9,8},{10,11... | collective-permute-start | bytes 208904 | tf_op jit(solution)/shard_map/ppermute | solution.py:299
  21.5 1.5 %collective-permute-start.7 = (bf16[272,128]{1,0:T(8,128)(2,1)S(1)}, bf16[272,128]{1,0:T(8,128)(2,1)S(1)}, u32[]{:S(2)}, u32[]{:S(2)}) collective-permute-start(bf16[272,128]{1,0:T(8,128)(2,1)S(1)} %get-tuple-element.43), channel_id=1, source_target_pairs={{0,2},{1,3},{2,0},{3,1},{4,6},{5,7},{6,4},{7,5},{8,10},{9,11},{10,... | collective-permute-start | bytes 208904 | tf_op jit(solution)/shard_map/ppermute | solution.py:299
  23.0 0.4 %collective-permute-start.11 = (bf16[384,128]{1,0:T(8,128)(2,1)S(1)}, bf16[384,128]{1,0:T(8,128)(2,1)S(1)}, u32[]{:S(2)}, u32[]{:S(2)}) collective-permute-start(bf16[384,128]{1,0:T(8,128)(2,1)S(1)} %get-tuple-element.48), channel_id=1, source_target_pairs={{0,4},{1,5},{2,6},{3,7},{4,0},{5,1},{6,2},{7,3},{8,12},{9,13},{10,... | collective-permute-start | bytes 294920 | tf_op jit(solution)/shard_map/ppermute | solution.py:299
  23.4 0.8 %shard_map.95.base_ref = f32[65,1024]{1,0:T(8,128)S(1)} custom-call(bf16[65,1024]{1,0:T(8,128)(2,1)S(1)} %copy-done.1, bf16[8,8,128,128]{3,2,1,0:T(8,128)(2,1)S(1)} %copy-done), custom_call_target="tpu_custom_call" | custom-call | flops 136314880 | bytes 2496512 | tf_op jit(solution)/shard_map/pallas_call | solution.py:274
  24.2 1.6 %collective-permute-done.7.refs_2_.refs_4_ = bf16[272,128]{1,0:T(8,128)(2,1)S(1)} collective-permute-done((bf16[272,128]{1,0:T(8,128)(2,1)S(1)}, bf16[272,128]{1,0:T(8,128)(2,1)S(1)}, u32[]{:S(2)}, u32[]{:S(2)}) %collective-permute-start.7) | collective-permute-done | bytes 69664 | tf_op jit(solution)/shard_map/ppermute | solution.py:299
  25.8 1.7 %collective-permute-done.8.refs_3_.refs_5_ = bf16[272,128]{1,0:T(8,128)(2,1)S(1)} collective-permute-done((bf16[272,128]{1,0:T(8,128)(2,1)S(1)}, bf16[272,128]{1,0:T(8,128)(2,1)S(1)}, u32[]{:S(2)}, u32[]{:S(2)}) %collective-permute-start.8) | collective-permute-done | bytes 69664 | tf_op jit(solution)/shard_map/ppermute | solution.py:299
  27.5 1.4 %shard_map.96.base_ref = f32[65,1024]{1,0:T(8,128)S(1)} custom-call(s32[1,12]{1,0:T(1,128)S(1)} %copy-done.7, f32[65,1024]{1,0:T(8,128)S(1)} %shard_map.95.base_ref, bf16[1,12,64,64]{3,2,1,0:T(8,128)(2,1)S(1)} %copy-done.5, bf16[8,64,64]{2,1,0:T(8,128)(2,1)S(1)} %copy-done.2, bf16[8,64,128]{2,1,0:T(8,128)(2,1)S(1)} %copy-done.3, ...), custom_call_target="tpu_custom_call" | custom-call | flops 68157440 | bytes 1105968 | tf_op jit(solution)/shard_map/pallas_call | solution.py:274
  29.0 0.8 %shard_map.98 = f32[65,1024]{1,0:T(8,128)} custom-call(f32[65,1024]{1,0:T(8,128)S(1)} %shard_map.96.base_ref, f32[384,128]{1,0:T(8,128)S(1)} %shard_map.97.refs_0_, bf16[384,128]{1,0:T(8,128)(2,1)S(1)} %collective-permute-done.11.refs_1_, bf16[272,128]{1,0:T(8,128)(2,1)S(1)} %get-tuple-element.41.refs_0_.refs_2_, ...), custom_call_target="tpu_custom_call" | custom-call | flops 133120 | bytes 1105920 | tf_op jit(solution)/shard_map/pallas_call | solution.py:274
  (24 shorter events, 0.1 us)
Async XLA Ops:
  3.1 9.4 %collective-permute-start = (bf16[784,128]{1,0:T(8,128)(2,1)}, bf16[784,128]{1,0:T(8,128)(2,1)S(1)}, u32[]{:S(2)}, u32[]{:S(2)}) collective-permute-start(bf16[784,128]{1,0:T(8,128)(2,1)} %get-tuple-element.31), channel_id=1, source_target_pairs={{0,2},{1,3},{2,0},{3,1},{4,6},{5,7},{6,4},{7,5},{8,10},{9,11},{10,... | collective-permute-start | bytes 602120 | tf_op jit(solution)/shard_map/ppermute | solution.py:299
  6.1 8.9 %collective-permute-start.1 = (bf16[784,128]{1,0:T(8,128)(2,1)}, bf16[784,128]{1,0:T(8,128)(2,1)S(1)}, u32[]{:S(2)}, u32[]{:S(2)}) collective-permute-start(bf16[784,128]{1,0:T(8,128)(2,1)} %get-tuple-element.32), channel_id=1, source_target_pairs={{0,3},{1,2},{2,1},{3,0},{4,7},{5,6},{6,5},{7,4},{8,11},{9,10},{10,... | collective-permute-start | bytes 602120 | tf_op jit(solution)/shard_map/ppermute | solution.py:299
  6.1 8.9 %collective-permute-start.2 = (bf16[784,128]{1,0:T(8,128)(2,1)}, bf16[784,128]{1,0:T(8,128)(2,1)S(1)}, u32[]{:S(2)}, u32[]{:S(2)}) collective-permute-start(bf16[784,128]{1,0:T(8,128)(2,1)} %get-tuple-element.33), channel_id=1, source_target_pairs={{0,1},{1,0},{2,3},{3,2},{4,5},{5,4},{6,7},{7,6},{8,9},{9,8},{10,11... | collective-permute-start | bytes 602120 | tf_op jit(solution)/shard_map/ppermute | solution.py:299
  6.3 13.8 %collective-permute-start.3 = (bf16[320,128]{1,0:T(8,128)(2,1)}, bf16[320,128]{1,0:T(8,128)(2,1)S(1)}, u32[]{:S(2)}, u32[]{:S(2)}) collective-permute-start(bf16[320,128]{1,0:T(8,128)(2,1)} %get-tuple-element.36), channel_id=1, source_target_pairs={{0,8},{1,9},{2,10},{3,11},{4,12},{5,13},{6,14},{7,15},{8,0},{9,1},... | collective-permute-start | bytes 245768 | tf_op jit(solution)/shard_map/ppermute | solution.py:299
  9.3 10.8 %collective-permute-start.4 = (bf16[320,128]{1,0:T(8,128)(2,1)}, bf16[320,128]{1,0:T(8,128)(2,1)S(1)}, u32[]{:S(2)}, u32[]{:S(2)}) collective-permute-start(bf16[320,128]{1,0:T(8,128)(2,1)} %get-tuple-element.37), channel_id=1, source_target_pairs={{0,12},{1,13},{2,14},{3,15},{4,8},{5,9},{6,10},{7,11},{8,4},{9,5},... | collective-permute-start | bytes 245768 | tf_op jit(solution)/shard_map/ppermute | solution.py:299
  10.7 0.9 %copy-start.4 = (bf16[784,128]{1,0:T(8,128)(2,1)S(1)}, bf16[784,128]{1,0:T(8,128)(2,1)}, u32[]{:S(2)}) copy-start(bf16[784,128]{1,0:T(8,128)(2,1)} %get-tuple-element.27.refs_0_) | copy-start | bytes 602116
  11.6 0.9 %copy-start.6 = (bf16[320,128]{1,0:T(8,128)(2,1)S(1)}, bf16[320,128]{1,0:T(8,128)(2,1)}, u32[]{:S(2)}) copy-start(bf16[320,128]{1,0:T(8,128)(2,1)} %get-tuple-element.28.refs_1_) | copy-start | bytes 245764
  12.5 7.6 %collective-permute-start.5 = (bf16[320,128]{1,0:T(8,128)(2,1)}, bf16[320,128]{1,0:T(8,128)(2,1)S(1)}, u32[]{:S(2)}, u32[]{:S(2)}) collective-permute-start(bf16[320,128]{1,0:T(8,128)(2,1)} %get-tuple-element.38), channel_id=1, source_target_pairs={{0,4},{1,5},{2,6},{3,7},{4,0},{5,1},{6,2},{7,3},{8,12},{9,13},{10,... | collective-permute-start | bytes 245768 | tf_op jit(solution)/shard_map/ppermute | solution.py:299
  15.0 8.4 %copy-start = (bf16[8,8,128,128]{3,2,1,0:T(8,128)(2,1)S(1)}, bf16[8,8,128,128]{3,2,1,0:T(8,128)(2,1)}, u32[]{:S(2)}) copy-start(bf16[8,8,128,128]{3,2,1,0:T(8,128)(2,1)} %local_ref.1) | copy-start | bytes 6291460
  15.0 8.4 %copy-start.1 = (bf16[65,1024]{1,0:T(8,128)(2,1)S(1)}, bf16[65,1024]{1,0:T(8,128)(2,1)}, u32[]{:S(2)}) copy-start(bf16[65,1024]{1,0:T(8,128)(2,1)} %probes_ref) | copy-start | bytes 399364
  16.0 11.5 %copy-start.2 = (bf16[8,64,64]{2,1,0:T(8,128)(2,1)S(1)}, bf16[8,64,64]{2,1,0:T(8,128)(2,1)}, u32[]{:S(2)}) copy-start(bf16[8,64,64]{2,1,0:T(8,128)(2,1)} %transfer_ref.1) | copy-start | bytes 196612
  16.0 11.5 %copy-start.3 = (bf16[8,64,128]{2,1,0:T(8,128)(2,1)S(1)}, bf16[8,64,128]{2,1,0:T(8,128)(2,1)}, u32[]{:S(2)}) copy-start(bf16[8,64,128]{2,1,0:T(8,128)(2,1)} %basis_ref.1) | copy-start | bytes 393220
  16.1 11.5 %copy-start.5 = (bf16[1,12,64,64]{3,2,1,0:T(8,128)(2,1)S(1)}, bf16[1,12,64,64]{3,2,1,0:T(8,128)(2,1)}, u32[]{:S(2)}) copy-start(bf16[1,12,64,64]{3,2,1,0:T(8,128)(2,1)} %couplings_ref.1) | copy-start | bytes 294916
  16.1 11.5 %copy-start.7 = (s32[1,12]{1,0:T(1,128)S(1)}, s32[1,12]{1,0:T(1,128)}, u32[]{:S(2)}) copy-start(s32[1,12]{1,0:T(1,128)} %partner_ref.1) | copy-start | bytes 148
  16.1 12.9 %collective-permute-start.9 = (bf16[384,128]{1,0:T(8,128)(2,1)S(1)}, bf16[384,128]{1,0:T(8,128)(2,1)S(1)}, u32[]{:S(2)}, u32[]{:S(2)}) collective-permute-start(bf16[384,128]{1,0:T(8,128)(2,1)S(1)} %get-tuple-element.46), channel_id=1, source_target_pairs={{0,8},{1,9},{2,10},{3,11},{4,12},{5,13},{6,14},{7,15},{8,0},{9,1},... | collective-permute-start | bytes 294920 | tf_op jit(solution)/shard_map/ppermute | solution.py:299
  18.7 10.2 %collective-permute-start.10 = (bf16[384,128]{1,0:T(8,128)(2,1)S(1)}, bf16[384,128]{1,0:T(8,128)(2,1)S(1)}, u32[]{:S(2)}, u32[]{:S(2)}) collective-permute-start(bf16[384,128]{1,0:T(8,128)(2,1)S(1)} %get-tuple-element.47), channel_id=1, source_target_pairs={{0,12},{1,13},{2,14},{3,15},{4,8},{5,9},{6,10},{7,11},{8,4},{9,5},... | collective-permute-start | bytes 294920 | tf_op jit(solution)/shard_map/ppermute | solution.py:299
  21.0 2.0 %collective-permute-start.6 = (bf16[272,128]{1,0:T(8,128)(2,1)S(1)}, bf16[272,128]{1,0:T(8,128)(2,1)S(1)}, u32[]{:S(2)}, u32[]{:S(2)}) collective-permute-start(bf16[272,128]{1,0:T(8,128)(2,1)S(1)} %get-tuple-element.39), channel_id=1, source_target_pairs={{0,1},{1,0},{2,3},{3,2},{4,5},{5,4},{6,7},{7,6},{8,9},{9,8},{10,11... | collective-permute-start | bytes 208904 | tf_op jit(solution)/shard_map/ppermute | solution.py:299
  21.5 4.3 %collective-permute-start.7 = (bf16[272,128]{1,0:T(8,128)(2,1)S(1)}, bf16[272,128]{1,0:T(8,128)(2,1)S(1)}, u32[]{:S(2)}, u32[]{:S(2)}) collective-permute-start(bf16[272,128]{1,0:T(8,128)(2,1)S(1)} %get-tuple-element.43), channel_id=1, source_target_pairs={{0,2},{1,3},{2,0},{3,1},{4,6},{5,7},{6,4},{7,5},{8,10},{9,11},{10,... | collective-permute-start | bytes 208904 | tf_op jit(solution)/shard_map/ppermute | solution.py:299
  23.0 4.5 %collective-permute-start.8 = (bf16[272,128]{1,0:T(8,128)(2,1)S(1)}, bf16[272,128]{1,0:T(8,128)(2,1)S(1)}, u32[]{:S(2)}, u32[]{:S(2)}) collective-permute-start(bf16[272,128]{1,0:T(8,128)(2,1)S(1)} %get-tuple-element.44), channel_id=1, source_target_pairs={{0,3},{1,2},{2,1},{3,0},{4,7},{5,6},{6,5},{7,4},{8,11},{9,10},{10,... | collective-permute-start | bytes 208904 | tf_op jit(solution)/shard_map/ppermute | solution.py:299
  23.0 6.0 %collective-permute-start.11 = (bf16[384,128]{1,0:T(8,128)(2,1)S(1)}, bf16[384,128]{1,0:T(8,128)(2,1)S(1)}, u32[]{:S(2)}, u32[]{:S(2)}) collective-permute-start(bf16[384,128]{1,0:T(8,128)(2,1)S(1)} %get-tuple-element.48), channel_id=1, source_target_pairs={{0,4},{1,5},{2,6},{3,7},{4,0},{5,1},{6,2},{7,3},{8,12},{9,13},{10,... | collective-permute-start | bytes 294920 | tf_op jit(solution)/shard_map/ppermute | solution.py:299

commit v22 on v21

--- a/solution.py
+++ b/solution.py
@@ -208,7 +208,20 @@
         kept[...] = came[...]
 
 
-def local_kernel(probes_ref, local_ref, out_ref):
+def local_kernel(
+    probes_ref, local_ref, couplings_ref, transfer_ref, basis_ref, out_ref, pairs_ref, across_ref, twos_ref
+):
+    rank = basis_ref.shape[1]
+    blank = jnp.zeros((rank, rank), BF16)
+    for f in range(couplings_ref.shape[1]):
+        cols = slice(2 * f * rank, 2 * (f + 1) * rank)
+        pairs_ref[:rank, cols] = jnp.concatenate([couplings_ref[0, f], blank], axis=1)
+        pairs_ref[rank:, cols] = jnp.concatenate([blank, couplings_ref[0, f]], axis=1)
+    for i in range(0, basis_ref.shape[0], 2):
+        across_ref[:, i * rank : (i + 2) * rank] = jnp.concatenate([transfer_ref[i], transfer_ref[i + 1]], axis=1)
+        none = jnp.zeros_like(basis_ref[i])
+        twos_ref[i // 2, :rank, :] = jnp.concatenate([basis_ref[i], none], axis=1)
+        twos_ref[i // 2, rank:, :] = jnp.concatenate([none, basis_ref[i + 1]], axis=1)
     leaves, size = local_ref.shape[0], local_ref.shape[2]
     for i in range(0, leaves, 2):
         total = 0.0
@@ -220,30 +233,33 @@
         out_ref[:, i * size : (i + 2) * size] = total
 
 
-def far_kernel(by_high, low, partner_ref, base_ref, couplings_ref, transfer_ref, basis_ref, *refs):
-    came, out_ref, boxes = refs[:low], refs[low], refs[low + 1]
-    columns = out_ref.shape[0]
-    leaves, rank, size = basis_ref.shape
+def far_kernel(by_high, low, partner_ref, base_ref, pairs_ref, across_ref, twos_ref, *refs):
+    came, out_ref, boxes, lasts = refs[:low], refs[low], refs[low + 1], refs[low + 2]
+    leaves, half = by_high.leaves, by_high.half
+    rank = across_ref.shape[0]
     high = boxes.shape[0] // low
     me = lax.axis_index("leaf")
     for k in range(low):
         tile = came[k][by_high.dense_tails : by_high.dense_box, :].astype(F32)
         for i in range(high):
-            start = by_high.dense_box + i * by_high.half
-            packed = came[k][start : start + by_high.half, :]
-            last = tile[leaves + i : leaves + i + 1, :rank]
-            boxes[i * low + k] = jnp.concatenate(
-                [packed[:, :rank].astype(F32), packed[:, rank:].astype(F32), last], axis=0
-            ).astype(BF16)
-    far = jnp.zeros((columns, rank), F32)
-    for f in range(couplings_ref.shape[1]):
+            start = by_high.dense_box + i * half
+            boxes[i * low + k] = came[k][start : start + half, :]
+            lasts[i * low + k : i * low + k + 1, :] = tile[leaves + i : leaves + i + 1, :]
+    chosen = []
+    for f in range(partner_ref.shape[1]):
         source = jnp.bitwise_xor(partner_ref[0, f], me)
-        far += dot_t(boxes[source], couplings_ref[0, f])
-    far = far.astype(BF16)
-    down = [dot(far, transfer_ref[j]).astype(BF16) for j in range(leaves)]
-    for j in range(leaves):
-        cols = slice(j * size, (j + 1) * size)
-        out_ref[:, cols] = base_ref[:, cols] + dot(down[j], basis_ref[j])
+        rows = jnp.concatenate([boxes[source].astype(F32), lasts[pl.ds(source, 1), :]], axis=0)
+        chosen.append(rows.astype(BF16))
+    far = 0.0
+    for f in range(0, len(chosen), 2):
+        cols = slice(2 * f * rank, 2 * (f + 2) * rank)
+        far += dot_t(jnp.concatenate(chosen[f : f + 2], axis=1), pairs_ref[:, cols])
+    far = jnp.concatenate([far[:half, :rank], far[:half, rank:], far[half:, :rank]], axis=0).astype(BF16)
+    down = dot(far, across_ref[...]).astype(BF16)
+    size = twos_ref.shape[2]
+    for i in range(leaves // 2):
+        cols = slice(i * size, (i + 1) * size)
+        out_ref[:, cols] = base_ref[:, cols] + dot(down[:, 2 * i * rank : 2 * (i + 1) * rank], twos_ref[i])
 
 
 def across_kernel(came_own, *refs):
@@ -365,16 +381,27 @@
         to_low[k] = relative(to_low[k], k)
 
     probes_then, to_low[1] = lax.optimization_barrier((probes, to_low[1]))
-    base = call(
-        local_kernel, base_shape, ([VMEM] * 2, VMEM), (probes_then, local_blocks), [], leaves * leaves * unit, 0
-    )
-    boxes = jax.ShapeDtypeStruct((devices, columns, rank), BF16)
+    base, *ready = call(
+        local_kernel,
+        (
+            base_shape,
+            jax.ShapeDtypeStruct((2 * rank, 2 * rank * couplings.shape[1]), BF16),
+            jax.ShapeDtypeStruct((rank, leaves * rank), BF16),
+            jax.ShapeDtypeStruct((leaves // 2, 2 * rank, 2 * size), BF16),
+        ),
+        ([VMEM] * 5, (VMEM,) * 4),
+        (probes_then, local_blocks, couplings, transfer, basis),
+        [],
+        leaves * leaves * unit,
+        0,
+    )
+    boxes = jax.ShapeDtypeStruct((devices, main // 2, size), BF16)
     base = call(
         functools.partial(far_kernel, by_high, low),
         base_shape,
         ([SMEM] + [VMEM] * (4 + low), VMEM),
-        (far_list, base, couplings, transfer, basis, *to_low),
-        like(boxes),
+        (far_list, base, *ready, *to_low),
+        like(boxes, jax.ShapeDtypeStruct((devices, size), F32)),
         4 * leaves * unit,
         4 * boxes.size,
     )

time: 30 us -> 29.8 us (level)
  transfers between devices with their start and end apart: 12 -> 12, of which waited for: 3 -> 4; matrix products, arithmetic and copies ran while one was open for 0% -> 0% of each run, Pallas kernels for 14% -> 13%
where the time goes in v22:
time: 29.8 us; the launch traced here: 29.6 us
  starting transfers between devices  15.7 us (53%)
  Pallas kernels  7.83 us (26%)
  waiting for transfers between devices  4.04 us (14%)
  local copies, waits for them, and re-layouts  1.84 us (6%)
    ppermute x12, starting transfers between devices, per_device(): lax.ppermute(x, 'leaf', [(i, i ^ way) for i in range(devices)])  15.7 us
    pallas_call x8, Pallas kernels, call(): pl.pallas_call(kernel, out_shape=out_shape, in_specs=specs[0], out_specs=...  7.83 us
    ppermute x12, waiting for transfers between devices, per_device(): lax.ppermute(x, 'leaf', [(i, i ^ way) for i in range(devices)])  4.04 us
    unnamed x16, local copies, waits for them, and re-layouts  1.84 us
  transfers between devices with their start and end apart: 12, of which 4 were waited for; matrix products, arithmetic and copies ran while one was open for 0% of the time, Pallas kernels for 13%

profile of v22, /device:TPU:0, one launch (start us, length us, event | category | flops | bytes accessed | tf_op | source)
XLA Modules:
  0.0 29.6 jit_solution(9702715679089093170)
XLA Ops:
  0.0 3.1 %shard_map.91 = (bf16[784,128]{1,0:T(8,128)(2,1)}, bf16[784,128]{1,0:T(8,128)(2,1)}, bf16[784,128]{1,0:T(8,128)(2,1)}, bf16[784,128]{1,0:T(8,128)(2,1)}, bf16[32...) custom-call(s32[4,8]{1,0:T(4,128)} %bitcast.2, ...), custom_call_target="tpu_custom_call" | custom-call | flops 68157440 | bytes 2509056 | tf_op jit(solution)/shard_map/pallas_call | solution.py:290
  3.1 3.0 %collective-permute-start = (bf16[784,128]{1,0:T(8,128)(2,1)}, bf16[784,128]{1,0:T(8,128)(2,1)S(1)}, u32[]{:S(2)}, u32[]{:S(2)}) collective-permute-start(bf16[784,128]{1,0:T(8,128)(2,1)} %get-tuple-element.35), channel_id=1, source_target_pairs={{0,2},{1,3},{2,0},{3,1},{4,6},{5,7},{6,4},{7,5},{8,10},{9,11},{10,... | collective-permute-start | bytes 602120 | tf_op jit(solution)/shard_map/ppermute | solution.py:315
  6.1 0.2 collective-permute-start.2
  6.3 3.0 %collective-permute-start.3 = (bf16[320,128]{1,0:T(8,128)(2,1)}, bf16[320,128]{1,0:T(8,128)(2,1)S(1)}, u32[]{:S(2)}, u32[]{:S(2)}) collective-permute-start(bf16[320,128]{1,0:T(8,128)(2,1)} %get-tuple-element.40), channel_id=1, source_target_pairs={{0,8},{1,9},{2,10},{3,11},{4,12},{5,13},{6,14},{7,15},{8,0},{9,1},... | collective-permute-start | bytes 245768 | tf_op jit(solution)/shard_map/ppermute | solution.py:315
  9.3 1.3 %collective-permute-start.4 = (bf16[320,128]{1,0:T(8,128)(2,1)}, bf16[320,128]{1,0:T(8,128)(2,1)S(1)}, u32[]{:S(2)}, u32[]{:S(2)}) collective-permute-start(bf16[320,128]{1,0:T(8,128)(2,1)} %get-tuple-element.41), channel_id=1, source_target_pairs={{0,12},{1,13},{2,14},{3,15},{4,8},{5,9},{6,10},{7,11},{8,4},{9,5},... | collective-permute-start | bytes 245768 | tf_op jit(solution)/shard_map/ppermute | solution.py:315
  10.7 0.9 %copy-done.4 = bf16[784,128]{1,0:T(8,128)(2,1)S(1)} copy-done((bf16[784,128]{1,0:T(8,128)(2,1)S(1)}, bf16[784,128]{1,0:T(8,128)(2,1)}, u32[]{:S(2)}) %copy-start.4) | copy-done | bytes 200728
  11.6 0.9 %copy-done.6 = bf16[320,128]{1,0:T(8,128)(2,1)S(1)} copy-done((bf16[320,128]{1,0:T(8,128)(2,1)S(1)}, bf16[320,128]{1,0:T(8,128)(2,1)}, u32[]{:S(2)}) %copy-start.6) | copy-done | bytes 81944
  12.5 1.7 %collective-permute-start.5 = (bf16[320,128]{1,0:T(8,128)(2,1)}, bf16[320,128]{1,0:T(8,128)(2,1)S(1)}, u32[]{:S(2)}, u32[]{:S(2)}) collective-permute-start(bf16[320,128]{1,0:T(8,128)(2,1)} %get-tuple-element.42), channel_id=1, source_target_pairs={{0,4},{1,5},{2,6},{3,7},{4,0},{5,1},{6,2},{7,3},{8,12},{9,13},{10,... | collective-permute-start | bytes 245768 | tf_op jit(solution)/shard_map/ppermute | solution.py:315
  14.2 0.7 %collective-permute-done.1.refs_2_ = bf16[784,128]{1,0:T(8,128)(2,1)S(1)} collective-permute-done((bf16[784,128]{1,0:T(8,128)(2,1)}, bf16[784,128]{1,0:T(8,128)(2,1)S(1)}, u32[]{:S(2)}, u32[]{:S(2)}) %collective-permute-start.1) | collective-permute-done | bytes 200736 | tf_op jit(solution)/shard_map/ppermute | solution.py:315
  15.0 0.0 copy-start.3
  15.0 0.0 copy-start.5
  15.0 1.0 %shard_map.93 = (bf16[384,128]{1,0:T(8,128)(2,1)S(1)}, bf16[384,128]{1,0:T(8,128)(2,1)S(1)}, bf16[384,128]{1,0:T(8,128)(2,1)S(1)}, bf16[384,128]{1,0:T(8,128)(2,1)S(1)}) custom-call(bf16[784,128]{1,0:T(8,128)(2,1)S(1)} %get-tuple-element.34.refs_0_, bf16[784,128]{1,0:T(8,128)(2,1)S(1)} %collective-permute-done.refs_1_, ...), custom_call_target="tpu_custom_call" | custom-call | flops 4000000000 | bytes 1196032 | tf_op jit(solution)/shard_map/pallas_call | solution.py:290
  16.1 2.7 %collective-permute-start.9 = (bf16[384,128]{1,0:T(8,128)(2,1)S(1)}, bf16[384,128]{1,0:T(8,128)(2,1)S(1)}, u32[]{:S(2)}, u32[]{:S(2)}) collective-permute-start(bf16[384,128]{1,0:T(8,128)(2,1)S(1)} %get-tuple-element.54), channel_id=1, source_target_pairs={{0,8},{1,9},{2,10},{3,11},{4,12},{5,13},{6,14},{7,15},{8,0},{9,1},... | collective-permute-start | bytes 294920 | tf_op jit(solution)/shard_map/ppermute | solution.py:315
  18.7 1.3 %collective-permute-start.10 = (bf16[384,128]{1,0:T(8,128)(2,1)S(1)}, bf16[384,128]{1,0:T(8,128)(2,1)S(1)}, u32[]{:S(2)}, u32[]{:S(2)}) collective-permute-start(bf16[384,128]{1,0:T(8,128)(2,1)S(1)} %get-tuple-element.55), channel_id=1, source_target_pairs={{0,12},{1,13},{2,14},{3,15},{4,8},{5,9},{6,10},{7,11},{8,4},{9,5},... | collective-permute-start | bytes 294920 | tf_op jit(solution)/shard_map/ppermute | solution.py:315
  20.1 0.9 %shard_map.94 = (bf16[272,128]{1,0:T(8,128)(2,1)S(1)}, bf16[272,128]{1,0:T(8,128)(2,1)S(1)}, bf16[272,128]{1,0:T(8,128)(2,1)S(1)}, bf16[272,128]{1,0:T(8,128)(2,1)S(1)}) custom-call(bf16[320,128]{1,0:T(8,128)(2,1)S(1)} %get-tuple-element.39.refs_0_, bf16[320,128]{1,0:T(8,128)(2,1)S(1)} %collective-permute-done.3.refs_1_, ...), custom_call_target="tpu_custom_call" | custom-call | flops 131072 | bytes 606208 | tf_op jit(solution)/shard_map/pallas_call | solution.py:290
  21.0 0.5 %collective-permute-start.6 = (bf16[272,128]{1,0:T(8,128)(2,1)S(1)}, bf16[272,128]{1,0:T(8,128)(2,1)S(1)}, u32[]{:S(2)}, u32[]{:S(2)}) collective-permute-start(bf16[272,128]{1,0:T(8,128)(2,1)S(1)} %get-tuple-element.43), channel_id=1, source_target_pairs={{0,1},{1,0},{2,3},{3,2},{4,5},{5,4},{6,7},{7,6},{8,9},{9,8},{10,11... | collective-permute-start | bytes 208904 | tf_op jit(solution)/shard_map/ppermute | solution.py:315
  21.5 1.5 %collective-permute-start.7 = (bf16[272,128]{1,0:T(8,128)(2,1)S(1)}, bf16[272,128]{1,0:T(8,128)(2,1)S(1)}, u32[]{:S(2)}, u32[]{:S(2)}) collective-permute-start(bf16[272,128]{1,0:T(8,128)(2,1)S(1)} %get-tuple-element.51), channel_id=1, source_target_pairs={{0,2},{1,3},{2,0},{3,1},{4,6},{5,7},{6,4},{7,5},{8,10},{9,11},{10,... | collective-permute-start | bytes 208904 | tf_op jit(solution)/shard_map/ppermute | solution.py:315
  23.0 0.4 %collective-permute-start.11 = (bf16[384,128]{1,0:T(8,128)(2,1)S(1)}, bf16[384,128]{1,0:T(8,128)(2,1)S(1)}, u32[]{:S(2)}, u32[]{:S(2)}) collective-permute-start(bf16[384,128]{1,0:T(8,128)(2,1)S(1)} %get-tuple-element.56), channel_id=1, source_target_pairs={{0,4},{1,5},{2,6},{3,7},{4,0},{5,1},{6,2},{7,3},{8,12},{9,13},{10,... | collective-permute-start | bytes 294920 | tf_op jit(solution)/shard_map/ppermute | solution.py:315
  23.4 0.8 %shard_map.95 = (f32[65,1024]{1,0:T(8,128)S(1)}, bf16[128,1536]{1,0:T(8,128)(2,1)S(1)}, bf16[64,512]{1,0:T(8,128)(2,1)S(1)}, bf16[4,128,256]{2,1,0:T(8,128)(2,1)S(1)}) custom-call(bf16[65,1024]{1,0:T(8,128)(2,1)S(1)} %copy-done.1, bf16[8,8,128,128]{3,2,1,0:T(8,128)(2,1)S(1)} %copy-done, bf16[1,12,64,64]{3,2,1,0:T(8,128)(2,1)S(1)} %copy-done.5, ...), custom_call_target="tpu_custom_call" | custom-call | flops 136314880 | bytes 3512320 | tf_op jit(solution)/shard_map/pallas_call | solution.py:290
  24.2 1.6 %collective-permute-done.7.refs_2_.refs_4_ = bf16[272,128]{1,0:T(8,128)(2,1)S(1)} collective-permute-done((bf16[272,128]{1,0:T(8,128)(2,1)S(1)}, bf16[272,128]{1,0:T(8,128)(2,1)S(1)}, u32[]{:S(2)}, u32[]{:S(2)}) %collective-permute-start.7) | collective-permute-done | bytes 69664 | tf_op jit(solution)/shard_map/ppermute | solution.py:315
  25.8 1.6 %collective-permute-done.8.refs_3_.refs_5_ = bf16[272,128]{1,0:T(8,128)(2,1)S(1)} collective-permute-done((bf16[272,128]{1,0:T(8,128)(2,1)S(1)}, bf16[272,128]{1,0:T(8,128)(2,1)S(1)}, u32[]{:S(2)}, u32[]{:S(2)}) %collective-permute-start.8) | collective-permute-done | bytes 69664 | tf_op jit(solution)/shard_map/ppermute | solution.py:315
  27.5 1.2 %shard_map.96.base_ref = f32[65,1024]{1,0:T(8,128)S(1)} custom-call(s32[1,12]{1,0:T(1,128)S(1)} %copy-done.7, f32[65,1024]{1,0:T(8,128)S(1)} %get-tuple-element.45.base_ref, bf16[128,1536]{1,0:T(8,128)(2,1)S(1)} %get-tuple-element.46.pairs_ref, bf16[64,512]{1,0:T(8,128)(2,1)S(1)} %get-tuple-element.47.across_ref, ...), custom_call_target="tpu_custom_call" | custom-call | flops 68157440 | bytes 1531952 | tf_op jit(solution)/shard_map/pallas_call | solution.py:290
  28.7 0.1 collective-permute-done.11.refs_1_
  28.8 0.8 %shard_map.98 = f32[65,1024]{1,0:T(8,128)} custom-call(f32[65,1024]{1,0:T(8,128)S(1)} %shard_map.96.base_ref, f32[384,128]{1,0:T(8,128)S(1)} %shard_map.97.refs_0_, bf16[384,128]{1,0:T(8,128)(2,1)S(1)} %collective-permute-done.11.refs_1_, bf16[272,128]{1,0:T(8,128)(2,1)S(1)} %get-tuple-element.49.refs_0_.refs_2_, ...), custom_call_target="tpu_custom_call" | custom-call | flops 133120 | bytes 1105920 | tf_op jit(solution)/shard_map/pallas_call | solution.py:290
  (24 shorter events, 0.1 us)
Async XLA Ops:
  3.1 9.4 %collective-permute-start = (bf16[784,128]{1,0:T(8,128)(2,1)}, bf16[784,128]{1,0:T(8,128)(2,1)S(1)}, u32[]{:S(2)}, u32[]{:S(2)}) collective-permute-start(bf16[784,128]{1,0:T(8,128)(2,1)} %get-tuple-element.35), channel_id=1, source_target_pairs={{0,2},{1,3},{2,0},{3,1},{4,6},{5,7},{6,4},{7,5},{8,10},{9,11},{10,... | collective-permute-start | bytes 602120 | tf_op jit(solution)/shard_map/ppermute | solution.py:315
  6.1 8.9 %collective-permute-start.1 = (bf16[784,128]{1,0:T(8,128)(2,1)}, bf16[784,128]{1,0:T(8,128)(2,1)S(1)}, u32[]{:S(2)}, u32[]{:S(2)}) collective-permute-start(bf16[784,128]{1,0:T(8,128)(2,1)} %get-tuple-element.36), channel_id=1, source_target_pairs={{0,3},{1,2},{2,1},{3,0},{4,7},{5,6},{6,5},{7,4},{8,11},{9,10},{10,... | collective-permute-start | bytes 602120 | tf_op jit(solution)/shard_map/ppermute | solution.py:315
  6.1 8.9 %collective-permute-start.2 = (bf16[784,128]{1,0:T(8,128)(2,1)}, bf16[784,128]{1,0:T(8,128)(2,1)S(1)}, u32[]{:S(2)}, u32[]{:S(2)}) collective-permute-start(bf16[784,128]{1,0:T(8,128)(2,1)} %get-tuple-element.37), channel_id=1, source_target_pairs={{0,1},{1,0},{2,3},{3,2},{4,5},{5,4},{6,7},{7,6},{8,9},{9,8},{10,11... | collective-permute-start | bytes 602120 | tf_op jit(solution)/shard_map/ppermute | solution.py:315
  6.3 13.8 %collective-permute-start.3 = (bf16[320,128]{1,0:T(8,128)(2,1)}, bf16[320,128]{1,0:T(8,128)(2,1)S(1)}, u32[]{:S(2)}, u32[]{:S(2)}) collective-permute-start(bf16[320,128]{1,0:T(8,128)(2,1)} %get-tuple-element.40), channel_id=1, source_target_pairs={{0,8},{1,9},{2,10},{3,11},{4,12},{5,13},{6,14},{7,15},{8,0},{9,1},... | collective-permute-start | bytes 245768 | tf_op jit(solution)/shard_map/ppermute | solution.py:315
  9.3 10.8 %collective-permute-start.4 = (bf16[320,128]{1,0:T(8,128)(2,1)}, bf16[320,128]{1,0:T(8,128)(2,1)S(1)}, u32[]{:S(2)}, u32[]{:S(2)}) collective-permute-start(bf16[320,128]{1,0:T(8,128)(2,1)} %get-tuple-element.41), channel_id=1, source_target_pairs={{0,12},{1,13},{2,14},{3,15},{4,8},{5,9},{6,10},{7,11},{8,4},{9,5},... | collective-permute-start | bytes 245768 | tf_op jit(solution)/shard_map/ppermute | solution.py:315
  10.7 0.9 %copy-start.4 = (bf16[784,128]{1,0:T(8,128)(2,1)S(1)}, bf16[784,128]{1,0:T(8,128)(2,1)}, u32[]{:S(2)}) copy-start(bf16[784,128]{1,0:T(8,128)(2,1)} %get-tuple-element.31.refs_0_) | copy-start | bytes 602116
  11.6 0.9 %copy-start.6 = (bf16[320,128]{1,0:T(8,128)(2,1)S(1)}, bf16[320,128]{1,0:T(8,128)(2,1)}, u32[]{:S(2)}) copy-start(bf16[320,128]{1,0:T(8,128)(2,1)} %get-tuple-element.32.refs_1_) | copy-start | bytes 245764
  12.5 7.6 %collective-permute-start.5 = (bf16[320,128]{1,0:T(8,128)(2,1)}, bf16[320,128]{1,0:T(8,128)(2,1)S(1)}, u32[]{:S(2)}, u32[]{:S(2)}) collective-permute-start(bf16[320,128]{1,0:T(8,128)(2,1)} %get-tuple-element.42), channel_id=1, source_target_pairs={{0,4},{1,5},{2,6},{3,7},{4,0},{5,1},{6,2},{7,3},{8,12},{9,13},{10,... | collective-permute-start | bytes 245768 | tf_op jit(solution)/shard_map/ppermute | solution.py:315
  15.0 8.4 %copy-start = (bf16[8,8,128,128]{3,2,1,0:T(8,128)(2,1)S(1)}, bf16[8,8,128,128]{3,2,1,0:T(8,128)(2,1)}, u32[]{:S(2)}) copy-start(bf16[8,8,128,128]{3,2,1,0:T(8,128)(2,1)} %local_ref.1) | copy-start | bytes 6291460
  15.0 8.4 %copy-start.1 = (bf16[65,1024]{1,0:T(8,128)(2,1)S(1)}, bf16[65,1024]{1,0:T(8,128)(2,1)}, u32[]{:S(2)}) copy-start(bf16[65,1024]{1,0:T(8,128)(2,1)} %probes_ref) | copy-start | bytes 399364
  15.0 8.4 %copy-start.2 = (bf16[8,64,64]{2,1,0:T(8,128)(2,1)S(1)}, bf16[8,64,64]{2,1,0:T(8,128)(2,1)}, u32[]{:S(2)}) copy-start(bf16[8,64,64]{2,1,0:T(8,128)(2,1)} %transfer_ref.1) | copy-start | bytes 196612
  15.0 8.4 %copy-start.3 = (bf16[8,64,128]{2,1,0:T(8,128)(2,1)S(1)}, bf16[8,64,128]{2,1,0:T(8,128)(2,1)}, u32[]{:S(2)}) copy-start(bf16[8,64,128]{2,1,0:T(8,128)(2,1)} %basis_ref.1) | copy-start | bytes 393220
  15.0 8.4 %copy-start.5 = (bf16[1,12,64,64]{3,2,1,0:T(8,128)(2,1)S(1)}, bf16[1,12,64,64]{3,2,1,0:T(8,128)(2,1)}, u32[]{:S(2)}) copy-start(bf16[1,12,64,64]{3,2,1,0:T(8,128)(2,1)} %couplings_ref.1) | copy-start | bytes 294916
  16.1 11.4 %copy-start.7 = (s32[1,12]{1,0:T(1,128)S(1)}, s32[1,12]{1,0:T(1,128)}, u32[]{:S(2)}) copy-start(s32[1,12]{1,0:T(1,128)} %partner_ref.1) | copy-start | bytes 148
  16.1 12.6 %collective-permute-start.9 = (bf16[384,128]{1,0:T(8,128)(2,1)S(1)}, bf16[384,128]{1,0:T(8,128)(2,1)S(1)}, u32[]{:S(2)}, u32[]{:S(2)}) collective-permute-start(bf16[384,128]{1,0:T(8,128)(2,1)S(1)} %get-tuple-element.54), channel_id=1, source_target_pairs={{0,8},{1,9},{2,10},{3,11},{4,12},{5,13},{6,14},{7,15},{8,0},{9,1},... | collective-permute-start | bytes 294920 | tf_op jit(solution)/shard_map/ppermute | solution.py:315
  18.7 9.9 %collective-permute-start.10 = (bf16[384,128]{1,0:T(8,128)(2,1)S(1)}, bf16[384,128]{1,0:T(8,128)(2,1)S(1)}, u32[]{:S(2)}, u32[]{:S(2)}) collective-permute-start(bf16[384,128]{1,0:T(8,128)(2,1)S(1)} %get-tuple-element.55), channel_id=1, source_target_pairs={{0,12},{1,13},{2,14},{3,15},{4,8},{5,9},{6,10},{7,11},{8,4},{9,5},... | collective-permute-start | bytes 294920 | tf_op jit(solution)/shard_map/ppermute | solution.py:315
  21.0 2.0 %collective-permute-start.6 = (bf16[272,128]{1,0:T(8,128)(2,1)S(1)}, bf16[272,128]{1,0:T(8,128)(2,1)S(1)}, u32[]{:S(2)}, u32[]{:S(2)}) collective-permute-start(bf16[272,128]{1,0:T(8,128)(2,1)S(1)} %get-tuple-element.43), channel_id=1, source_target_pairs={{0,1},{1,0},{2,3},{3,2},{4,5},{5,4},{6,7},{7,6},{8,9},{9,8},{10,11... | collective-permute-start | bytes 208904 | tf_op jit(solution)/shard_map/ppermute | solution.py:315
  21.5 4.3 %collective-permute-start.7 = (bf16[272,128]{1,0:T(8,128)(2,1)S(1)}, bf16[272,128]{1,0:T(8,128)(2,1)S(1)}, u32[]{:S(2)}, u32[]{:S(2)}) collective-permute-start(bf16[272,128]{1,0:T(8,128)(2,1)S(1)} %get-tuple-element.51), channel_id=1, source_target_pairs={{0,2},{1,3},{2,0},{3,1},{4,6},{5,7},{6,4},{7,5},{8,10},{9,11},{10,... | collective-permute-start | bytes 208904 | tf_op jit(solution)/shard_map/ppermute | solution.py:315
  23.0 4.5 %collective-permute-start.8 = (bf16[272,128]{1,0:T(8,128)(2,1)S(1)}, bf16[272,128]{1,0:T(8,128)(2,1)S(1)}, u32[]{:S(2)}, u32[]{:S(2)}) collective-permute-start(bf16[272,128]{1,0:T(8,128)(2,1)S(1)} %get-tuple-element.52), channel_id=1, source_target_pairs={{0,3},{1,2},{2,1},{3,0},{4,7},{5,6},{6,5},{7,4},{8,11},{9,10},{10,... | collective-permute-start | bytes 208904 | tf_op jit(solution)/shard_map/ppermute | solution.py:315
  23.0 5.8 %collective-permute-start.11 = (bf16[384,128]{1,0:T(8,128)(2,1)S(1)}, bf16[384,128]{1,0:T(8,128)(2,1)S(1)}, u32[]{:S(2)}, u32[]{:S(2)}) collective-permute-start(bf16[384,128]{1,0:T(8,128)(2,1)S(1)} %get-tuple-element.56), channel_id=1, source_target_pairs={{0,4},{1,5},{2,6},{3,7},{4,0},{5,1},{6,2},{7,3},{8,12},{9,13},{10,... | collective-permute-start | bytes 294920 | tf_op jit(solution)/shard_map/ppermute | solution.py:315

commit v23 on v22

--- a/solution.py
+++ b/solution.py
@@ -375,6 +375,7 @@
     came_high[0], to_high[0] = lax.optimization_barrier((came_high[0], to_high[0]))
     to_low = summed(by_high, planes, [came_high[k] for k in planes])
     base_shape = jax.ShapeDtypeStruct((columns, points), F32)
+    to_high[3], to_low[0] = lax.optimization_barrier((to_high[3], to_low[0]))
     for k in planes[1:]:
         to_high[k] = relative(to_high[k], k * low)
     for k in range(1, low):
@@ -405,15 +406,17 @@
         4 * leaves * unit,
         4 * boxes.size,
     )
-    across = call(
-        across_kernel,
-        jax.ShapeDtypeStruct((by_low.dense_depth, size), F32),
-        ([VMEM] * (high - 1), VMEM),
-        [to_high[k] for k in planes[:-1]],
-        [],
-        HEAVY,
-        0,
-    )
+    across = to_high[0]
+    for came, work in ((to_high[2:3], devices * size), (to_high[3:], HEAVY)):
+        across = call(
+            across_kernel,
+            jax.ShapeDtypeStruct((by_low.dense_depth, size), F32),
+            ([VMEM] * (1 + len(came)), VMEM),
+            (across, *came),
+            [],
+            work,
+            0,
+        )
     return call(
         functools.partial(last_kernel, routes, devices),
         base_shape,

time: 29.8 us -> 30 us (level)
  starting transfers between devices: 15.7 us -> 16.2 us
    ppermute x12, starting transfers between devices: 15.7 us -> 16.2 us  [per_device(): lax.ppermute(x, 'leaf', [(i, i ^ way) for i in range(devices)])]
    pallas_call x8 -> x9, Pallas kernels: 7.83 us -> 7.83 us  [call(): pl.pallas_call(kernel, out_shape=out_shape, in_specs=specs[0], out_specs=...]
  transfers between devices with their start and end apart: 12 -> 12, of which waited for: 4 -> 3; matrix products, arithmetic and copies ran while one was open for 0% -> 0% of each run, Pallas kernels for 13% -> 13%
where the time goes in v23:
time: 30 us; the launch traced here: 29.9 us
  starting transfers between devices  16.2 us (54%)
  Pallas kernels  7.83 us (26%)
  waiting for transfers between devices  3.84 us (13%)
  local copies, waits for them, and re-layouts  1.84 us (6%)
    ppermute x12, starting transfers between devices, per_device(): lax.ppermute(x, 'leaf', [(i, i ^ way) for i in range(devices)])  16.2 us
    pallas_call x9, Pallas kernels, call(): pl.pallas_call(kernel, out_shape=out_shape, in_specs=specs[0], out_specs=...  7.83 us
    ppermute x12, waiting for transfers between devices, per_device(): lax.ppermute(x, 'leaf', [(i, i ^ way) for i in range(devices)])  3.84 us
    unnamed x16, local copies, waits for them, and re-layouts  1.84 us
  transfers between devices with their start and end apart: 12, of which 3 were waited for; matrix products, arithmetic and copies ran while one was open for 0% of the time, Pallas kernels for 13%

profile of v23, /device:TPU:0, one launch (start us, length us, event | category | flops | bytes accessed | tf_op | source)
XLA Modules:
  0.0 29.9 jit_solution(12745379791987021272)
XLA Ops:
  0.0 3.1 %shard_map.91 = (bf16[784,128]{1,0:T(8,128)(2,1)}, bf16[784,128]{1,0:T(8,128)(2,1)}, bf16[784,128]{1,0:T(8,128)(2,1)}, bf16[784,128]{1,0:T(8,128)(2,1)}, bf16[32...) custom-call(s32[4,8]{1,0:T(4,128)} %bitcast.2, ...), custom_call_target="tpu_custom_call" | custom-call | flops 68157440 | bytes 2509056 | tf_op jit(solution)/shard_map/pallas_call | solution.py:290
  3.1 3.0 %collective-permute-start = (bf16[784,128]{1,0:T(8,128)(2,1)}, bf16[784,128]{1,0:T(8,128)(2,1)S(1)}, u32[]{:S(2)}, u32[]{:S(2)}) collective-permute-start(bf16[784,128]{1,0:T(8,128)(2,1)} %get-tuple-element.37), channel_id=1, source_target_pairs={{0,2},{1,3},{2,0},{3,1},{4,6},{5,7},{6,4},{7,5},{8,10},{9,11},{10,... | collective-permute-start | bytes 602120 | tf_op jit(solution)/shard_map/ppermute | solution.py:315
  6.1 0.0 collective-permute-start.1
  6.1 0.2 collective-permute-start.2
  6.3 3.0 %collective-permute-start.3 = (bf16[320,128]{1,0:T(8,128)(2,1)}, bf16[320,128]{1,0:T(8,128)(2,1)S(1)}, u32[]{:S(2)}, u32[]{:S(2)}) collective-permute-start(bf16[320,128]{1,0:T(8,128)(2,1)} %get-tuple-element.42), channel_id=1, source_target_pairs={{0,8},{1,9},{2,10},{3,11},{4,12},{5,13},{6,14},{7,15},{8,0},{9,1},... | collective-permute-start | bytes 245768 | tf_op jit(solution)/shard_map/ppermute | solution.py:315
  9.3 1.3 %collective-permute-start.4 = (bf16[320,128]{1,0:T(8,128)(2,1)}, bf16[320,128]{1,0:T(8,128)(2,1)S(1)}, u32[]{:S(2)}, u32[]{:S(2)}) collective-permute-start(bf16[320,128]{1,0:T(8,128)(2,1)} %get-tuple-element.43), channel_id=1, source_target_pairs={{0,12},{1,13},{2,14},{3,15},{4,8},{5,9},{6,10},{7,11},{8,4},{9,5},... | collective-permute-start | bytes 245768 | tf_op jit(solution)/shard_map/ppermute | solution.py:315
  10.7 0.9 %copy-done.4 = bf16[784,128]{1,0:T(8,128)(2,1)S(1)} copy-done((bf16[784,128]{1,0:T(8,128)(2,1)S(1)}, bf16[784,128]{1,0:T(8,128)(2,1)}, u32[]{:S(2)}) %copy-start.4) | copy-done | bytes 200728
  11.6 0.9 %copy-done.6 = bf16[320,128]{1,0:T(8,128)(2,1)S(1)} copy-done((bf16[320,128]{1,0:T(8,128)(2,1)S(1)}, bf16[320,128]{1,0:T(8,128)(2,1)}, u32[]{:S(2)}) %copy-start.6) | copy-done | bytes 81944
  12.5 1.7 %collective-permute-start.5 = (bf16[320,128]{1,0:T(8,128)(2,1)}, bf16[320,128]{1,0:T(8,128)(2,1)S(1)}, u32[]{:S(2)}, u32[]{:S(2)}) collective-permute-start(bf16[320,128]{1,0:T(8,128)(2,1)} %get-tuple-element.44), channel_id=1, source_target_pairs={{0,4},{1,5},{2,6},{3,7},{4,0},{5,1},{6,2},{7,3},{8,12},{9,13},{10,... | collective-permute-start | bytes 245768 | tf_op jit(solution)/shard_map/ppermute | solution.py:315
  14.2 0.7 %collective-permute-done.1.refs_2_ = bf16[784,128]{1,0:T(8,128)(2,1)S(1)} collective-permute-done((bf16[784,128]{1,0:T(8,128)(2,1)}, bf16[784,128]{1,0:T(8,128)(2,1)S(1)}, u32[]{:S(2)}, u32[]{:S(2)}) %collective-permute-start.1) | collective-permute-done | bytes 200736 | tf_op jit(solution)/shard_map/ppermute | solution.py:315
  15.0 0.0 copy-start.3
  15.0 0.0 copy-start.5
  15.0 1.0 %shard_map.93 = (bf16[384,128]{1,0:T(8,128)(2,1)S(1)}, bf16[384,128]{1,0:T(8,128)(2,1)S(1)}, bf16[384,128]{1,0:T(8,128)(2,1)S(1)}, bf16[384,128]{1,0:T(8,128)(2,1)S(1)}) custom-call(bf16[784,128]{1,0:T(8,128)(2,1)S(1)} %get-tuple-element.36.refs_0_, bf16[784,128]{1,0:T(8,128)(2,1)S(1)} %collective-permute-done.refs_1_, ...), custom_call_target="tpu_custom_call" | custom-call | flops 4000000000 | bytes 1196032 | tf_op jit(solution)/shard_map/pallas_call | solution.py:290
  16.0 0.0 copy-start.7
  16.0 2.7 %collective-permute-start.9 = (bf16[384,128]{1,0:T(8,128)(2,1)S(1)}, bf16[384,128]{1,0:T(8,128)(2,1)S(1)}, u32[]{:S(2)}, u32[]{:S(2)}) collective-permute-start(bf16[384,128]{1,0:T(8,128)(2,1)S(1)} %get-tuple-element.58), channel_id=1, source_target_pairs={{0,8},{1,9},{2,10},{3,11},{4,12},{5,13},{6,14},{7,15},{8,0},{9,1},... | collective-permute-start | bytes 294920 | tf_op jit(solution)/shard_map/ppermute | solution.py:315
  18.7 0.9 %shard_map.94 = (bf16[272,128]{1,0:T(8,128)(2,1)S(1)}, bf16[272,128]{1,0:T(8,128)(2,1)S(1)}, bf16[272,128]{1,0:T(8,128)(2,1)S(1)}, bf16[272,128]{1,0:T(8,128)(2,1)S(1)}) custom-call(bf16[320,128]{1,0:T(8,128)(2,1)S(1)} %get-tuple-element.41.refs_0_, bf16[320,128]{1,0:T(8,128)(2,1)S(1)} %collective-permute-done.3.refs_1_, ...), custom_call_target="tpu_custom_call" | custom-call | flops 131072 | bytes 606208 | tf_op jit(solution)/shard_map/pallas_call | solution.py:290
  19.6 2.3 %collective-permute-start.10 = (bf16[384,128]{1,0:T(8,128)(2,1)S(1)}, bf16[384,128]{1,0:T(8,128)(2,1)S(1)}, u32[]{:S(2)}, u32[]{:S(2)}) collective-permute-start(bf16[384,128]{1,0:T(8,128)(2,1)S(1)} %get-tuple-element.59), channel_id=1, source_target_pairs={{0,12},{1,13},{2,14},{3,15},{4,8},{5,9},{6,10},{7,11},{8,4},{9,5},... | collective-permute-start | bytes 294920 | tf_op jit(solution)/shard_map/ppermute | solution.py:315
  22.0 1.5 %collective-permute-start.7 = (bf16[272,128]{1,0:T(8,128)(2,1)S(1)}, bf16[272,128]{1,0:T(8,128)(2,1)S(1)}, u32[]{:S(2)}, u32[]{:S(2)}) collective-permute-start(bf16[272,128]{1,0:T(8,128)(2,1)S(1)} %get-tuple-element.55), channel_id=1, source_target_pairs={{0,2},{1,3},{2,0},{3,1},{4,6},{5,7},{6,4},{7,5},{8,10},{9,11},{10,... | collective-permute-start | bytes 208904 | tf_op jit(solution)/shard_map/ppermute | solution.py:315
  23.5 0.4 %collective-permute-start.8 = (bf16[272,128]{1,0:T(8,128)(2,1)S(1)}, bf16[272,128]{1,0:T(8,128)(2,1)S(1)}, u32[]{:S(2)}, u32[]{:S(2)}) collective-permute-start(bf16[272,128]{1,0:T(8,128)(2,1)S(1)} %get-tuple-element.56), channel_id=1, source_target_pairs={{0,3},{1,2},{2,1},{3,0},{4,7},{5,6},{6,5},{7,4},{8,11},{9,10},{10,... | collective-permute-start | bytes 208904 | tf_op jit(solution)/shard_map/ppermute | solution.py:315
  23.9 0.8 %shard_map.95 = (f32[65,1024]{1,0:T(8,128)S(1)}, bf16[128,1536]{1,0:T(8,128)(2,1)S(1)}, bf16[64,512]{1,0:T(8,128)(2,1)S(1)}, bf16[4,128,256]{2,1,0:T(8,128)(2,1)S(1)}) custom-call(bf16[65,1024]{1,0:T(8,128)(2,1)S(1)} %copy-done.1, bf16[8,8,128,128]{3,2,1,0:T(8,128)(2,1)S(1)} %copy-done, bf16[1,12,64,64]{3,2,1,0:T(8,128)(2,1)S(1)} %copy-done.5, ...), custom_call_target="tpu_custom_call" | custom-call | flops 136314880 | bytes 3512320 | tf_op jit(solution)/shard_map/pallas_call | solution.py:290
  24.7 2.0 %collective-permute-done.7.refs_2_.refs_4_ = bf16[272,128]{1,0:T(8,128)(2,1)S(1)} collective-permute-done((bf16[272,128]{1,0:T(8,128)(2,1)S(1)}, bf16[272,128]{1,0:T(8,128)(2,1)S(1)}, u32[]{:S(2)}, u32[]{:S(2)}) %collective-permute-start.7) | collective-permute-done | bytes 69664 | tf_op jit(solution)/shard_map/ppermute | solution.py:315
  26.7 1.1 %collective-permute-done.8.refs_3_.refs_5_ = bf16[272,128]{1,0:T(8,128)(2,1)S(1)} collective-permute-done((bf16[272,128]{1,0:T(8,128)(2,1)S(1)}, bf16[272,128]{1,0:T(8,128)(2,1)S(1)}, u32[]{:S(2)}, u32[]{:S(2)}) %collective-permute-start.8) | collective-permute-done | bytes 69664 | tf_op jit(solution)/shard_map/ppermute | solution.py:315
  27.8 1.2 %shard_map.96.base_ref = f32[65,1024]{1,0:T(8,128)S(1)} custom-call(s32[1,12]{1,0:T(1,128)S(1)} %copy-done.7, f32[65,1024]{1,0:T(8,128)S(1)} %get-tuple-element.47.base_ref, bf16[128,1536]{1,0:T(8,128)(2,1)S(1)} %get-tuple-element.48.pairs_ref, bf16[64,512]{1,0:T(8,128)(2,1)S(1)} %get-tuple-element.49.across_ref, ...), custom_call_target="tpu_custom_call" | custom-call | flops 68157440 | bytes 1531952 | tf_op jit(solution)/shard_map/pallas_call | solution.py:290
  29.1 0.8 %shard_map.99 = f32[65,1024]{1,0:T(8,128)} custom-call(f32[65,1024]{1,0:T(8,128)S(1)} %shard_map.96.base_ref, f32[384,128]{1,0:T(8,128)S(1)} %shard_map.98.refs_0_, bf16[384,128]{1,0:T(8,128)(2,1)S(1)} %collective-permute-done.11.refs_1_, bf16[272,128]{1,0:T(8,128)(2,1)S(1)} %get-tuple-element.53.refs_0_.refs_2_, ...), custom_call_target="tpu_custom_call" | custom-call | flops 133120 | bytes 1105920 | tf_op jit(solution)/shard_map/pallas_call | solution.py:290
  (25 shorter events, 0.1 us)
Async XLA Ops:
  3.1 9.4 %collective-permute-start = (bf16[784,128]{1,0:T(8,128)(2,1)}, bf16[784,128]{1,0:T(8,128)(2,1)S(1)}, u32[]{:S(2)}, u32[]{:S(2)}) collective-permute-start(bf16[784,128]{1,0:T(8,128)(2,1)} %get-tuple-element.37), channel_id=1, source_target_pairs={{0,2},{1,3},{2,0},{3,1},{4,6},{5,7},{6,4},{7,5},{8,10},{9,11},{10,... | collective-permute-start | bytes 602120 | tf_op jit(solution)/shard_map/ppermute | solution.py:315
  6.1 8.9 %collective-permute-start.1 = (bf16[784,128]{1,0:T(8,128)(2,1)}, bf16[784,128]{1,0:T(8,128)(2,1)S(1)}, u32[]{:S(2)}, u32[]{:S(2)}) collective-permute-start(bf16[784,128]{1,0:T(8,128)(2,1)} %get-tuple-element.38), channel_id=1, source_target_pairs={{0,3},{1,2},{2,1},{3,0},{4,7},{5,6},{6,5},{7,4},{8,11},{9,10},{10,... | collective-permute-start | bytes 602120 | tf_op jit(solution)/shard_map/ppermute | solution.py:315
  6.1 8.9 %collective-permute-start.2 = (bf16[784,128]{1,0:T(8,128)(2,1)}, bf16[784,128]{1,0:T(8,128)(2,1)S(1)}, u32[]{:S(2)}, u32[]{:S(2)}) collective-permute-start(bf16[784,128]{1,0:T(8,128)(2,1)} %get-tuple-element.39), channel_id=1, source_target_pairs={{0,1},{1,0},{2,3},{3,2},{4,5},{5,4},{6,7},{7,6},{8,9},{9,8},{10,11... | collective-permute-start | bytes 602120 | tf_op jit(solution)/shard_map/ppermute | solution.py:315
  6.3 12.4 %collective-permute-start.3 = (bf16[320,128]{1,0:T(8,128)(2,1)}, bf16[320,128]{1,0:T(8,128)(2,1)S(1)}, u32[]{:S(2)}, u32[]{:S(2)}) collective-permute-start(bf16[320,128]{1,0:T(8,128)(2,1)} %get-tuple-element.42), channel_id=1, source_target_pairs={{0,8},{1,9},{2,10},{3,11},{4,12},{5,13},{6,14},{7,15},{8,0},{9,1},... | collective-permute-start | bytes 245768 | tf_op jit(solution)/shard_map/ppermute | solution.py:315
  9.3 9.4 %collective-permute-start.4 = (bf16[320,128]{1,0:T(8,128)(2,1)}, bf16[320,128]{1,0:T(8,128)(2,1)S(1)}, u32[]{:S(2)}, u32[]{:S(2)}) collective-permute-start(bf16[320,128]{1,0:T(8,128)(2,1)} %get-tuple-element.43), channel_id=1, source_target_pairs={{0,12},{1,13},{2,14},{3,15},{4,8},{5,9},{6,10},{7,11},{8,4},{9,5},... | collective-permute-start | bytes 245768 | tf_op jit(solution)/shard_map/ppermute | solution.py:315
  10.7 0.9 %copy-start.4 = (bf16[784,128]{1,0:T(8,128)(2,1)S(1)}, bf16[784,128]{1,0:T(8,128)(2,1)}, u32[]{:S(2)}) copy-start(bf16[784,128]{1,0:T(8,128)(2,1)} %get-tuple-element.33.refs_0_) | copy-start | bytes 602116
  11.6 0.9 %copy-start.6 = (bf16[320,128]{1,0:T(8,128)(2,1)S(1)}, bf16[320,128]{1,0:T(8,128)(2,1)}, u32[]{:S(2)}) copy-start(bf16[320,128]{1,0:T(8,128)(2,1)} %get-tuple-element.34.refs_1_) | copy-start | bytes 245764
  12.5 6.2 %collective-permute-start.5 = (bf16[320,128]{1,0:T(8,128)(2,1)}, bf16[320,128]{1,0:T(8,128)(2,1)S(1)}, u32[]{:S(2)}, u32[]{:S(2)}) collective-permute-start(bf16[320,128]{1,0:T(8,128)(2,1)} %get-tuple-element.44), channel_id=1, source_target_pairs={{0,4},{1,5},{2,6},{3,7},{4,0},{5,1},{6,2},{7,3},{8,12},{9,13},{10,... | collective-permute-start | bytes 245768 | tf_op jit(solution)/shard_map/ppermute | solution.py:315
  15.0 8.9 %copy-start = (bf16[8,8,128,128]{3,2,1,0:T(8,128)(2,1)S(1)}, bf16[8,8,128,128]{3,2,1,0:T(8,128)(2,1)}, u32[]{:S(2)}) copy-start(bf16[8,8,128,128]{3,2,1,0:T(8,128)(2,1)} %local_ref.1) | copy-start | bytes 6291460
  15.0 8.9 %copy-start.1 = (bf16[65,1024]{1,0:T(8,128)(2,1)S(1)}, bf16[65,1024]{1,0:T(8,128)(2,1)}, u32[]{:S(2)}) copy-start(bf16[65,1024]{1,0:T(8,128)(2,1)} %probes_ref) | copy-start | bytes 399364
  15.0 8.9 %copy-start.2 = (bf16[8,64,64]{2,1,0:T(8,128)(2,1)S(1)}, bf16[8,64,64]{2,1,0:T(8,128)(2,1)}, u32[]{:S(2)}) copy-start(bf16[8,64,64]{2,1,0:T(8,128)(2,1)} %transfer_ref.1) | copy-start | bytes 196612
  15.0 8.9 %copy-start.3 = (bf16[8,64,128]{2,1,0:T(8,128)(2,1)S(1)}, bf16[8,64,128]{2,1,0:T(8,128)(2,1)}, u32[]{:S(2)}) copy-start(bf16[8,64,128]{2,1,0:T(8,128)(2,1)} %basis_ref.1) | copy-start | bytes 393220
  15.0 8.9 %copy-start.5 = (bf16[1,12,64,64]{3,2,1,0:T(8,128)(2,1)S(1)}, bf16[1,12,64,64]{3,2,1,0:T(8,128)(2,1)}, u32[]{:S(2)}) copy-start(bf16[1,12,64,64]{3,2,1,0:T(8,128)(2,1)} %couplings_ref.1) | copy-start | bytes 294916
  16.0 11.7 %copy-start.7 = (s32[1,12]{1,0:T(1,128)S(1)}, s32[1,12]{1,0:T(1,128)}, u32[]{:S(2)}) copy-start(s32[1,12]{1,0:T(1,128)} %partner_ref.1) | copy-start | bytes 148
  16.0 13.0 %collective-permute-start.9 = (bf16[384,128]{1,0:T(8,128)(2,1)S(1)}, bf16[384,128]{1,0:T(8,128)(2,1)S(1)}, u32[]{:S(2)}, u32[]{:S(2)}) collective-permute-start(bf16[384,128]{1,0:T(8,128)(2,1)S(1)} %get-tuple-element.58), channel_id=1, source_target_pairs={{0,8},{1,9},{2,10},{3,11},{4,12},{5,13},{6,14},{7,15},{8,0},{9,1},... | collective-permute-start | bytes 294920 | tf_op jit(solution)/shard_map/ppermute | solution.py:315
  19.6 9.4 %collective-permute-start.10 = (bf16[384,128]{1,0:T(8,128)(2,1)S(1)}, bf16[384,128]{1,0:T(8,128)(2,1)S(1)}, u32[]{:S(2)}, u32[]{:S(2)}) collective-permute-start(bf16[384,128]{1,0:T(8,128)(2,1)S(1)} %get-tuple-element.59), channel_id=1, source_target_pairs={{0,12},{1,13},{2,14},{3,15},{4,8},{5,9},{6,10},{7,11},{8,4},{9,5},... | collective-permute-start | bytes 294920 | tf_op jit(solution)/shard_map/ppermute | solution.py:315
  22.0 1.9 %collective-permute-start.6 = (bf16[272,128]{1,0:T(8,128)(2,1)S(1)}, bf16[272,128]{1,0:T(8,128)(2,1)S(1)}, u32[]{:S(2)}, u32[]{:S(2)}) collective-permute-start(bf16[272,128]{1,0:T(8,128)(2,1)S(1)} %get-tuple-element.45), channel_id=1, source_target_pairs={{0,1},{1,0},{2,3},{3,2},{4,5},{5,4},{6,7},{7,6},{8,9},{9,8},{10,11... | collective-permute-start | bytes 208904 | tf_op jit(solution)/shard_map/ppermute | solution.py:315
  22.0 4.7 %collective-permute-start.7 = (bf16[272,128]{1,0:T(8,128)(2,1)S(1)}, bf16[272,128]{1,0:T(8,128)(2,1)S(1)}, u32[]{:S(2)}, u32[]{:S(2)}) collective-permute-start(bf16[272,128]{1,0:T(8,128)(2,1)S(1)} %get-tuple-element.55), channel_id=1, source_target_pairs={{0,2},{1,3},{2,0},{3,1},{4,6},{5,7},{6,4},{7,5},{8,10},{9,11},{10,... | collective-permute-start | bytes 208904 | tf_op jit(solution)/shard_map/ppermute | solution.py:315
  23.5 4.3 %collective-permute-start.8 = (bf16[272,128]{1,0:T(8,128)(2,1)S(1)}, bf16[272,128]{1,0:T(8,128)(2,1)S(1)}, u32[]{:S(2)}, u32[]{:S(2)}) collective-permute-start(bf16[272,128]{1,0:T(8,128)(2,1)S(1)} %get-tuple-element.56), channel_id=1, source_target_pairs={{0,3},{1,2},{2,1},{3,0},{4,7},{5,6},{6,5},{7,4},{8,11},{9,10},{10,... | collective-permute-start | bytes 208904 | tf_op jit(solution)/shard_map/ppermute | solution.py:315
  23.9 5.2 %collective-permute-start.11 = (bf16[384,128]{1,0:T(8,128)(2,1)S(1)}, bf16[384,128]{1,0:T(8,128)(2,1)S(1)}, u32[]{:S(2)}, u32[]{:S(2)}) collective-permute-start(bf16[384,128]{1,0:T(8,128)(2,1)S(1)} %get-tuple-element.60), channel_id=1, source_target_pairs={{0,4},{1,5},{2,6},{3,7},{4,0},{5,1},{6,2},{7,3},{8,12},{9,13},{10,... | collective-permute-start | bytes 294920 | tf_op jit(solution)/shard_map/ppermute | solution.py:315

commit v24 on v22

--- a/solution.py
+++ b/solution.py
@@ -159,15 +159,16 @@
         copy.wait()
 
 
-def sum_route(route, came, planes, outs, base, leaf_ref, total, tails):
+def sum_route(route, came, planes, outs, total, tails):
     leaves, half, ways = route.leaves, route.half, len(came)
     for i in range(ways):
+        numbers = came[i][route.meta : route.box, :].astype(F32)[:1].astype(I32)
         if route.extra:
             tail = came[i][route.tails : route.meta, :].astype(F32)
         for k in range(route.fan):
             for slot in range(CAP):
                 at = k * CAP + slot
-                leaf = leaf_ref[base + i, at]
+                leaf = numbers[0, at]
                 rows = pl.ds(pl.multiple_of(leaf * route.rows, TILE), route.rows)
                 total[k, rows, :] += came[i][at * route.rows : (at + 1) * route.rows, :].astype(F32)
                 if route.extra:
@@ -190,16 +191,11 @@
 
 
 def sum_kernel(route, planes, ways, *refs):
-    came, outs = refs[:ways], refs[ways:-5]
-    meta, leaf_ref, total, tails, late = refs[-5:]
-    for i, ref in enumerate(came):
-        meta[i : i + 1, :] = ref[route.meta : route.box, :].astype(F32)[:1].astype(I32)
-    numbers = pltpu.make_async_copy(meta, leaf_ref, late)
-    numbers.start()
+    came, outs = refs[:ways], refs[ways:-2]
+    total, tails = refs[-2:]
     for ref in (total, tails):
         ref[...] = jnp.zeros(ref.shape, F32)
-    numbers.wait()
-    sum_route(route, came, planes, outs, 0, leaf_ref, total, tails)
+    sum_route(route, came, planes, outs, total, tails)
 
 
 def keep_kernel(*refs):
@@ -363,9 +359,7 @@
                 [dense(route)] * route.fan,
                 ([VMEM] * ways, [VMEM] * route.fan),
                 came,
-                [pltpu.VMEM((ways, size), I32), pltpu.SMEM((ways, size), I32)]
-                + like(total, tails)
-                + [pltpu.SemaphoreType.DMA(())],
+                like(total, tails),
                 HEAVY if route is by_low else devices * CAP * route.rows * size,
                 4 * (total.size + tails.size),
             )

time: 29.8 us -> 29.2 us (0.980)
  Pallas kernels: 7.83 us -> 6.8 us
  waiting for transfers between devices: 4.04 us -> 4.53 us
    pallas_call x8, Pallas kernels: 7.83 us -> 6.8 us  [call(): pl.pallas_call(kernel, out_shape=out_shape, in_specs=specs[0], out_specs=...]
    ppermute x12, waiting for transfers between devices: 4.04 us -> 4.53 us  [per_device(): lax.ppermute(x, 'leaf', [(i, i ^ way) for i in range(devices)])]
  transfers between devices with their start and end apart: 12 -> 12, of which waited for: 4 -> 4; matrix products, arithmetic and copies ran while one was open for 0% -> 0% of each run, Pallas kernels for 13% -> 10%
where the time goes in v24:
time: 29.2 us; the launch traced here: 29 us
  starting transfers between devices  15.7 us (54%)
  Pallas kernels  6.8 us (23%)
  waiting for transfers between devices  4.53 us (16%)
  local copies, waits for them, and re-layouts  1.84 us (6%)
    ppermute x12, starting transfers between devices, per_device(): lax.ppermute(x, 'leaf', [(i, i ^ way) for i in range(devices)])  15.7 us
    pallas_call x8, Pallas kernels, call(): pl.pallas_call(kernel, out_shape=out_shape, in_specs=specs[0], out_specs=...  6.8 us
    ppermute x12, waiting for transfers between devices, per_device(): lax.ppermute(x, 'leaf', [(i, i ^ way) for i in range(devices)])  4.53 us
    unnamed x16, local copies, waits for them, and re-layouts  1.84 us
  transfers between devices with their start and end apart: 12, of which 4 were waited for; matrix products, arithmetic and copies ran while one was open for 0% of the time, Pallas kernels for 10%

profile of v24, /device:TPU:0, one launch (start us, length us, event | category | flops | bytes accessed | tf_op | source)
XLA Modules:
  0.0 29.0 jit_solution(533122455567436629)
XLA Ops:
  0.0 3.1 %shard_map.91 = (bf16[784,128]{1,0:T(8,128)(2,1)}, bf16[784,128]{1,0:T(8,128)(2,1)}, bf16[784,128]{1,0:T(8,128)(2,1)}, bf16[784,128]{1,0:T(8,128)(2,1)}, bf16[32...) custom-call(s32[4,8]{1,0:T(4,128)} %bitcast.2, ...), custom_call_target="tpu_custom_call" | custom-call | flops 68157440 | bytes 2509056 | tf_op jit(solution)/shard_map/pallas_call | solution.py:286
  3.1 3.0 %collective-permute-start = (bf16[784,128]{1,0:T(8,128)(2,1)}, bf16[784,128]{1,0:T(8,128)(2,1)S(1)}, u32[]{:S(2)}, u32[]{:S(2)}) collective-permute-start(bf16[784,128]{1,0:T(8,128)(2,1)} %get-tuple-element.35), channel_id=1, source_target_pairs={{0,2},{1,3},{2,0},{3,1},{4,6},{5,7},{6,4},{7,5},{8,10},{9,11},{10,... | collective-permute-start | bytes 602120 | tf_op jit(solution)/shard_map/ppermute | solution.py:311
  6.1 0.2 collective-permute-start.2
  6.3 3.0 %collective-permute-start.3 = (bf16[320,128]{1,0:T(8,128)(2,1)}, bf16[320,128]{1,0:T(8,128)(2,1)S(1)}, u32[]{:S(2)}, u32[]{:S(2)}) collective-permute-start(bf16[320,128]{1,0:T(8,128)(2,1)} %get-tuple-element.40), channel_id=1, source_target_pairs={{0,8},{1,9},{2,10},{3,11},{4,12},{5,13},{6,14},{7,15},{8,0},{9,1},... | collective-permute-start | bytes 245768 | tf_op jit(solution)/shard_map/ppermute | solution.py:311
  9.3 1.3 %collective-permute-start.4 = (bf16[320,128]{1,0:T(8,128)(2,1)}, bf16[320,128]{1,0:T(8,128)(2,1)S(1)}, u32[]{:S(2)}, u32[]{:S(2)}) collective-permute-start(bf16[320,128]{1,0:T(8,128)(2,1)} %get-tuple-element.41), channel_id=1, source_target_pairs={{0,12},{1,13},{2,14},{3,15},{4,8},{5,9},{6,10},{7,11},{8,4},{9,5},... | collective-permute-start | bytes 245768 | tf_op jit(solution)/shard_map/ppermute | solution.py:311
  10.7 0.9 %copy-done.4 = bf16[784,128]{1,0:T(8,128)(2,1)S(1)} copy-done((bf16[784,128]{1,0:T(8,128)(2,1)S(1)}, bf16[784,128]{1,0:T(8,128)(2,1)}, u32[]{:S(2)}) %copy-start.4) | copy-done | bytes 200728
  11.6 0.9 %copy-done.6 = bf16[320,128]{1,0:T(8,128)(2,1)S(1)} copy-done((bf16[320,128]{1,0:T(8,128)(2,1)S(1)}, bf16[320,128]{1,0:T(8,128)(2,1)}, u32[]{:S(2)}) %copy-start.6) | copy-done | bytes 81944
  12.5 1.7 %collective-permute-start.5 = (bf16[320,128]{1,0:T(8,128)(2,1)}, bf16[320,128]{1,0:T(8,128)(2,1)S(1)}, u32[]{:S(2)}, u32[]{:S(2)}) collective-permute-start(bf16[320,128]{1,0:T(8,128)(2,1)} %get-tuple-element.42), channel_id=1, source_target_pairs={{0,4},{1,5},{2,6},{3,7},{4,0},{5,1},{6,2},{7,3},{8,12},{9,13},{10,... | collective-permute-start | bytes 245768 | tf_op jit(solution)/shard_map/ppermute | solution.py:311
  14.2 0.7 %collective-permute-done.1.refs_2_ = bf16[784,128]{1,0:T(8,128)(2,1)S(1)} collective-permute-done((bf16[784,128]{1,0:T(8,128)(2,1)}, bf16[784,128]{1,0:T(8,128)(2,1)S(1)}, u32[]{:S(2)}, u32[]{:S(2)}) %collective-permute-start.1) | collective-permute-done | bytes 200736 | tf_op jit(solution)/shard_map/ppermute | solution.py:311
  15.0 0.0 copy-start.3
  15.0 0.0 copy-start.5
  15.0 0.5 %shard_map.93 = (bf16[384,128]{1,0:T(8,128)(2,1)S(1)}, bf16[384,128]{1,0:T(8,128)(2,1)S(1)}, bf16[384,128]{1,0:T(8,128)(2,1)S(1)}, bf16[384,128]{1,0:T(8,128)(2,1)S(1)}) custom-call(bf16[784,128]{1,0:T(8,128)(2,1)S(1)} %get-tuple-element.34.refs_0_, bf16[784,128]{1,0:T(8,128)(2,1)S(1)} %collective-permute-done.refs_1_, ...), custom_call_target="tpu_custom_call" | custom-call | flops 4000000000 | bytes 1196032 | tf_op jit(solution)/shard_map/pallas_call | solution.py:286
  15.5 2.6 %collective-permute-start.9 = (bf16[384,128]{1,0:T(8,128)(2,1)S(1)}, bf16[384,128]{1,0:T(8,128)(2,1)S(1)}, u32[]{:S(2)}, u32[]{:S(2)}) collective-permute-start(bf16[384,128]{1,0:T(8,128)(2,1)S(1)} %get-tuple-element.54), channel_id=1, source_target_pairs={{0,8},{1,9},{2,10},{3,11},{4,12},{5,13},{6,14},{7,15},{8,0},{9,1},... | collective-permute-start | bytes 294920 | tf_op jit(solution)/shard_map/ppermute | solution.py:311
  18.2 1.3 %collective-permute-start.10 = (bf16[384,128]{1,0:T(8,128)(2,1)S(1)}, bf16[384,128]{1,0:T(8,128)(2,1)S(1)}, u32[]{:S(2)}, u32[]{:S(2)}) collective-permute-start(bf16[384,128]{1,0:T(8,128)(2,1)S(1)} %get-tuple-element.55), channel_id=1, source_target_pairs={{0,12},{1,13},{2,14},{3,15},{4,8},{5,9},{6,10},{7,11},{8,4},{9,5},... | collective-permute-start | bytes 294920 | tf_op jit(solution)/shard_map/ppermute | solution.py:311
  19.5 0.4 %shard_map.94 = (bf16[272,128]{1,0:T(8,128)(2,1)S(1)}, bf16[272,128]{1,0:T(8,128)(2,1)S(1)}, bf16[272,128]{1,0:T(8,128)(2,1)S(1)}, bf16[272,128]{1,0:T(8,128)(2,1)S(1)}) custom-call(bf16[320,128]{1,0:T(8,128)(2,1)S(1)} %get-tuple-element.39.refs_0_, bf16[320,128]{1,0:T(8,128)(2,1)S(1)} %collective-permute-done.3.refs_1_, ...), custom_call_target="tpu_custom_call" | custom-call | flops 131072 | bytes 606208 | tf_op jit(solution)/shard_map/pallas_call | solution.py:286
  19.9 0.5 %collective-permute-start.6 = (bf16[272,128]{1,0:T(8,128)(2,1)S(1)}, bf16[272,128]{1,0:T(8,128)(2,1)S(1)}, u32[]{:S(2)}, u32[]{:S(2)}) collective-permute-start(bf16[272,128]{1,0:T(8,128)(2,1)S(1)} %get-tuple-element.43), channel_id=1, source_target_pairs={{0,1},{1,0},{2,3},{3,2},{4,5},{5,4},{6,7},{7,6},{8,9},{9,8},{10,11... | collective-permute-start | bytes 208904 | tf_op jit(solution)/shard_map/ppermute | solution.py:311
  20.5 1.5 %collective-permute-start.7 = (bf16[272,128]{1,0:T(8,128)(2,1)S(1)}, bf16[272,128]{1,0:T(8,128)(2,1)S(1)}, u32[]{:S(2)}, u32[]{:S(2)}) collective-permute-start(bf16[272,128]{1,0:T(8,128)(2,1)S(1)} %get-tuple-element.51), channel_id=1, source_target_pairs={{0,2},{1,3},{2,0},{3,1},{4,6},{5,7},{6,4},{7,5},{8,10},{9,11},{10,... | collective-permute-start | bytes 208904 | tf_op jit(solution)/shard_map/ppermute | solution.py:311
  22.0 0.4 %collective-permute-start.11 = (bf16[384,128]{1,0:T(8,128)(2,1)S(1)}, bf16[384,128]{1,0:T(8,128)(2,1)S(1)}, u32[]{:S(2)}, u32[]{:S(2)}) collective-permute-start(bf16[384,128]{1,0:T(8,128)(2,1)S(1)} %get-tuple-element.56), channel_id=1, source_target_pairs={{0,4},{1,5},{2,6},{3,7},{4,0},{5,1},{6,2},{7,3},{8,12},{9,13},{10,... | collective-permute-start | bytes 294920 | tf_op jit(solution)/shard_map/ppermute | solution.py:311
  22.4 0.8 %shard_map.95 = (f32[65,1024]{1,0:T(8,128)S(1)}, bf16[128,1536]{1,0:T(8,128)(2,1)S(1)}, bf16[64,512]{1,0:T(8,128)(2,1)S(1)}, bf16[4,128,256]{2,1,0:T(8,128)(2,1)S(1)}) custom-call(bf16[65,1024]{1,0:T(8,128)(2,1)S(1)} %copy-done.1, bf16[8,8,128,128]{3,2,1,0:T(8,128)(2,1)S(1)} %copy-done, bf16[1,12,64,64]{3,2,1,0:T(8,128)(2,1)S(1)} %copy-done.5, ...), custom_call_target="tpu_custom_call" | custom-call | flops 136314880 | bytes 3512320 | tf_op jit(solution)/shard_map/pallas_call | solution.py:286
  23.2 1.6 %collective-permute-done.7.refs_2_.refs_4_ = bf16[272,128]{1,0:T(8,128)(2,1)S(1)} collective-permute-done((bf16[272,128]{1,0:T(8,128)(2,1)S(1)}, bf16[272,128]{1,0:T(8,128)(2,1)S(1)}, u32[]{:S(2)}, u32[]{:S(2)}) %collective-permute-start.7) | collective-permute-done | bytes 69664 | tf_op jit(solution)/shard_map/ppermute | solution.py:311
  24.8 1.7 %collective-permute-done.8.refs_3_.refs_5_ = bf16[272,128]{1,0:T(8,128)(2,1)S(1)} collective-permute-done((bf16[272,128]{1,0:T(8,128)(2,1)S(1)}, bf16[272,128]{1,0:T(8,128)(2,1)S(1)}, u32[]{:S(2)}, u32[]{:S(2)}) %collective-permute-start.8) | collective-permute-done | bytes 69664 | tf_op jit(solution)/shard_map/ppermute | solution.py:311
  26.4 1.2 %shard_map.96.base_ref = f32[65,1024]{1,0:T(8,128)S(1)} custom-call(s32[1,12]{1,0:T(1,128)S(1)} %copy-done.7, f32[65,1024]{1,0:T(8,128)S(1)} %get-tuple-element.45.base_ref, bf16[128,1536]{1,0:T(8,128)(2,1)S(1)} %get-tuple-element.46.pairs_ref, bf16[64,512]{1,0:T(8,128)(2,1)S(1)} %get-tuple-element.47.across_ref, ...), custom_call_target="tpu_custom_call" | custom-call | flops 68157440 | bytes 1531952 | tf_op jit(solution)/shard_map/pallas_call | solution.py:286
  27.7 0.6 %collective-permute-done.11.refs_1_ = bf16[384,128]{1,0:T(8,128)(2,1)S(1)} collective-permute-done((bf16[384,128]{1,0:T(8,128)(2,1)S(1)}, bf16[384,128]{1,0:T(8,128)(2,1)S(1)}, u32[]{:S(2)}, u32[]{:S(2)}) %collective-permute-start.11) | collective-permute-done | bytes 98336 | tf_op jit(solution)/shard_map/ppermute | solution.py:311
  28.3 0.8 %shard_map.98 = f32[65,1024]{1,0:T(8,128)} custom-call(f32[65,1024]{1,0:T(8,128)S(1)} %shard_map.96.base_ref, f32[384,128]{1,0:T(8,128)S(1)} %shard_map.97.refs_0_, bf16[384,128]{1,0:T(8,128)(2,1)S(1)} %collective-permute-done.11.refs_1_, bf16[272,128]{1,0:T(8,128)(2,1)S(1)} %get-tuple-element.49.refs_0_.refs_2_, ...), custom_call_target="tpu_custom_call" | custom-call | flops 133120 | bytes 1105920 | tf_op jit(solution)/shard_map/pallas_call | solution.py:286
  (24 shorter events, 0.1 us)
Async XLA Ops:
  3.1 9.4 %collective-permute-start = (bf16[784,128]{1,0:T(8,128)(2,1)}, bf16[784,128]{1,0:T(8,128)(2,1)S(1)}, u32[]{:S(2)}, u32[]{:S(2)}) collective-permute-start(bf16[784,128]{1,0:T(8,128)(2,1)} %get-tuple-element.35), channel_id=1, source_target_pairs={{0,2},{1,3},{2,0},{3,1},{4,6},{5,7},{6,4},{7,5},{8,10},{9,11},{10,... | collective-permute-start | bytes 602120 | tf_op jit(solution)/shard_map/ppermute | solution.py:311
  6.1 8.9 %collective-permute-start.1 = (bf16[784,128]{1,0:T(8,128)(2,1)}, bf16[784,128]{1,0:T(8,128)(2,1)S(1)}, u32[]{:S(2)}, u32[]{:S(2)}) collective-permute-start(bf16[784,128]{1,0:T(8,128)(2,1)} %get-tuple-element.36), channel_id=1, source_target_pairs={{0,3},{1,2},{2,1},{3,0},{4,7},{5,6},{6,5},{7,4},{8,11},{9,10},{10,... | collective-permute-start | bytes 602120 | tf_op jit(solution)/shard_map/ppermute | solution.py:311
  6.1 8.9 %collective-permute-start.2 = (bf16[784,128]{1,0:T(8,128)(2,1)}, bf16[784,128]{1,0:T(8,128)(2,1)S(1)}, u32[]{:S(2)}, u32[]{:S(2)}) collective-permute-start(bf16[784,128]{1,0:T(8,128)(2,1)} %get-tuple-element.37), channel_id=1, source_target_pairs={{0,1},{1,0},{2,3},{3,2},{4,5},{5,4},{6,7},{7,6},{8,9},{9,8},{10,11... | collective-permute-start | bytes 602120 | tf_op jit(solution)/shard_map/ppermute | solution.py:311
  6.3 13.2 %collective-permute-start.3 = (bf16[320,128]{1,0:T(8,128)(2,1)}, bf16[320,128]{1,0:T(8,128)(2,1)S(1)}, u32[]{:S(2)}, u32[]{:S(2)}) collective-permute-start(bf16[320,128]{1,0:T(8,128)(2,1)} %get-tuple-element.40), channel_id=1, source_target_pairs={{0,8},{1,9},{2,10},{3,11},{4,12},{5,13},{6,14},{7,15},{8,0},{9,1},... | collective-permute-start | bytes 245768 | tf_op jit(solution)/shard_map/ppermute | solution.py:311
  9.3 10.2 %collective-permute-start.4 = (bf16[320,128]{1,0:T(8,128)(2,1)}, bf16[320,128]{1,0:T(8,128)(2,1)S(1)}, u32[]{:S(2)}, u32[]{:S(2)}) collective-permute-start(bf16[320,128]{1,0:T(8,128)(2,1)} %get-tuple-element.41), channel_id=1, source_target_pairs={{0,12},{1,13},{2,14},{3,15},{4,8},{5,9},{6,10},{7,11},{8,4},{9,5},... | collective-permute-start | bytes 245768 | tf_op jit(solution)/shard_map/ppermute | solution.py:311
  10.7 0.9 %copy-start.4 = (bf16[784,128]{1,0:T(8,128)(2,1)S(1)}, bf16[784,128]{1,0:T(8,128)(2,1)}, u32[]{:S(2)}) copy-start(bf16[784,128]{1,0:T(8,128)(2,1)} %get-tuple-element.31.refs_0_) | copy-start | bytes 602116
  11.6 0.9 %copy-start.6 = (bf16[320,128]{1,0:T(8,128)(2,1)S(1)}, bf16[320,128]{1,0:T(8,128)(2,1)}, u32[]{:S(2)}) copy-start(bf16[320,128]{1,0:T(8,128)(2,1)} %get-tuple-element.32.refs_1_) | copy-start | bytes 245764
  12.5 7.0 %collective-permute-start.5 = (bf16[320,128]{1,0:T(8,128)(2,1)}, bf16[320,128]{1,0:T(8,128)(2,1)S(1)}, u32[]{:S(2)}, u32[]{:S(2)}) collective-permute-start(bf16[320,128]{1,0:T(8,128)(2,1)} %get-tuple-element.42), channel_id=1, source_target_pairs={{0,4},{1,5},{2,6},{3,7},{4,0},{5,1},{6,2},{7,3},{8,12},{9,13},{10,... | collective-permute-start | bytes 245768 | tf_op jit(solution)/shard_map/ppermute | solution.py:311
  15.0 7.4 %copy-start = (bf16[8,8,128,128]{3,2,1,0:T(8,128)(2,1)S(1)}, bf16[8,8,128,128]{3,2,1,0:T(8,128)(2,1)}, u32[]{:S(2)}) copy-start(bf16[8,8,128,128]{3,2,1,0:T(8,128)(2,1)} %local_ref.1) | copy-start | bytes 6291460
  15.0 7.4 %copy-start.1 = (bf16[65,1024]{1,0:T(8,128)(2,1)S(1)}, bf16[65,1024]{1,0:T(8,128)(2,1)}, u32[]{:S(2)}) copy-start(bf16[65,1024]{1,0:T(8,128)(2,1)} %probes_ref) | copy-start | bytes 399364
  15.0 7.4 %copy-start.2 = (bf16[8,64,64]{2,1,0:T(8,128)(2,1)S(1)}, bf16[8,64,64]{2,1,0:T(8,128)(2,1)}, u32[]{:S(2)}) copy-start(bf16[8,64,64]{2,1,0:T(8,128)(2,1)} %transfer_ref.1) | copy-start | bytes 196612
  15.0 7.4 %copy-start.3 = (bf16[8,64,128]{2,1,0:T(8,128)(2,1)S(1)}, bf16[8,64,128]{2,1,0:T(8,128)(2,1)}, u32[]{:S(2)}) copy-start(bf16[8,64,128]{2,1,0:T(8,128)(2,1)} %basis_ref.1) | copy-start | bytes 393220
  15.0 7.4 %copy-start.5 = (bf16[1,12,64,64]{3,2,1,0:T(8,128)(2,1)S(1)}, bf16[1,12,64,64]{3,2,1,0:T(8,128)(2,1)}, u32[]{:S(2)}) copy-start(bf16[1,12,64,64]{3,2,1,0:T(8,128)(2,1)} %couplings_ref.1) | copy-start | bytes 294916
  15.5 10.9 %copy-start.7 = (s32[1,12]{1,0:T(1,128)S(1)}, s32[1,12]{1,0:T(1,128)}, u32[]{:S(2)}) copy-start(s32[1,12]{1,0:T(1,128)} %partner_ref.1) | copy-start | bytes 148
  15.5 12.1 %collective-permute-start.9 = (bf16[384,128]{1,0:T(8,128)(2,1)S(1)}, bf16[384,128]{1,0:T(8,128)(2,1)S(1)}, u32[]{:S(2)}, u32[]{:S(2)}) collective-permute-start(bf16[384,128]{1,0:T(8,128)(2,1)S(1)} %get-tuple-element.54), channel_id=1, source_target_pairs={{0,8},{1,9},{2,10},{3,11},{4,12},{5,13},{6,14},{7,15},{8,0},{9,1},... | collective-permute-start | bytes 294920 | tf_op jit(solution)/shard_map/ppermute | solution.py:311
  18.2 9.5 %collective-permute-start.10 = (bf16[384,128]{1,0:T(8,128)(2,1)S(1)}, bf16[384,128]{1,0:T(8,128)(2,1)S(1)}, u32[]{:S(2)}, u32[]{:S(2)}) collective-permute-start(bf16[384,128]{1,0:T(8,128)(2,1)S(1)} %get-tuple-element.55), channel_id=1, source_target_pairs={{0,12},{1,13},{2,14},{3,15},{4,8},{5,9},{6,10},{7,11},{8,4},{9,5},... | collective-permute-start | bytes 294920 | tf_op jit(solution)/shard_map/ppermute | solution.py:311
  19.9 2.0 %collective-permute-start.6 = (bf16[272,128]{1,0:T(8,128)(2,1)S(1)}, bf16[272,128]{1,0:T(8,128)(2,1)S(1)}, u32[]{:S(2)}, u32[]{:S(2)}) collective-permute-start(bf16[272,128]{1,0:T(8,128)(2,1)S(1)} %get-tuple-element.43), channel_id=1, source_target_pairs={{0,1},{1,0},{2,3},{3,2},{4,5},{5,4},{6,7},{7,6},{8,9},{9,8},{10,11... | collective-permute-start | bytes 208904 | tf_op jit(solution)/shard_map/ppermute | solution.py:311
  20.5 4.3 %collective-permute-start.7 = (bf16[272,128]{1,0:T(8,128)(2,1)S(1)}, bf16[272,128]{1,0:T(8,128)(2,1)S(1)}, u32[]{:S(2)}, u32[]{:S(2)}) collective-permute-start(bf16[272,128]{1,0:T(8,128)(2,1)S(1)} %get-tuple-element.51), channel_id=1, source_target_pairs={{0,2},{1,3},{2,0},{3,1},{4,6},{5,7},{6,4},{7,5},{8,10},{9,11},{10,... | collective-permute-start | bytes 208904 | tf_op jit(solution)/shard_map/ppermute | solution.py:311
  22.0 4.5 %collective-permute-start.8 = (bf16[272,128]{1,0:T(8,128)(2,1)S(1)}, bf16[272,128]{1,0:T(8,128)(2,1)S(1)}, u32[]{:S(2)}, u32[]{:S(2)}) collective-permute-start(bf16[272,128]{1,0:T(8,128)(2,1)S(1)} %get-tuple-element.52), channel_id=1, source_target_pairs={{0,3},{1,2},{2,1},{3,0},{4,7},{5,6},{6,5},{7,4},{8,11},{9,10},{10,... | collective-permute-start | bytes 208904 | tf_op jit(solution)/shard_map/ppermute | solution.py:311
  22.0 6.3 %collective-permute-start.11 = (bf16[384,128]{1,0:T(8,128)(2,1)S(1)}, bf16[384,128]{1,0:T(8,128)(2,1)S(1)}, u32[]{:S(2)}, u32[]{:S(2)}) collective-permute-start(bf16[384,128]{1,0:T(8,128)(2,1)S(1)} %get-tuple-element.56), channel_id=1, source_target_pairs={{0,4},{1,5},{2,6},{3,7},{4,0},{5,1},{6,2},{7,3},{8,12},{9,13},{10,... | collective-permute-start | bytes 294920 | tf_op jit(solution)/shard_map/ppermute | solution.py:311

commit v25 on v24

--- a/solution.py
+++ b/solution.py
@@ -190,12 +190,24 @@
     return [0, *range(2, high), 1]
 
 
-def sum_kernel(route, planes, ways, *refs):
-    came, outs = refs[:ways], refs[ways:-2]
+def split(keys, bit):
+    return [k for k in keys if k & bit], [k for k in keys if not k & bit]
+
+
+def sum_kernel(route, planes, ways, places, *refs):
+    came, given = refs[:ways], refs[ways:-2]
     total, tails = refs[-2:]
+    outs = [given[n] if at is None else given[n].at[at] for n, at in places]
     for ref in (total, tails):
         ref[...] = jnp.zeros(ref.shape, F32)
     sum_route(route, came, planes, outs, total, tails)
+
+
+def fold_kernel(terms, *refs):
+    inputs, outs = refs[: -len(terms)], refs[-len(terms) :]
+    for out, entries in zip(outs, terms):
+        for i, entry in enumerate(entries):
+            out[i] = sum(inputs[n][at].astype(F32) for n, at in entry).astype(BF16)
 
 
 def keep_kernel(*refs):
@@ -258,15 +270,11 @@
         out_ref[:, cols] = base_ref[:, cols] + dot(down[:, 2 * i * rank : 2 * (i + 1) * rank], twos_ref[i])
 
 
-def across_kernel(came_own, *refs):
-    out_ref = refs[-1]
-    out_ref[...] = sum(ref[...].astype(F32) for ref in (came_own, *refs[:-1]))
-
-
-def last_kernel(routes, devices, base_ref, *refs):
+def last_kernel(routes, devices, picks, base_ref, *refs):
     by_low, by_high = routes
     high, low = grid_of(devices)
-    came_high, came_low, out_ref = refs[: -low - 1], refs[-low - 1 : -1], refs[-1]
+    came_low, out_ref = refs[:low], refs[-1]
+    came_high = [ref if at is None else ref.at[at] for ref, at in zip(refs[low:-1], picks)]
     leaves, split, main = by_low.leaves, by_low.rows, by_low.main
     size = base_ref.shape[1] // leaves
     tails = sum(came_low[k][by_high.dense_tails : by_high.dense_box, :].astype(F32) for k in range(low))
@@ -349,28 +357,64 @@
     for k in planes[1:]:
         came_high[k] = relative(came_high[k], k * low)
 
-    def summed(route, planes, came):
+    def summed(route, planes, came, outs, places):
         total = jax.ShapeDtypeStruct((route.fan, (leaves + 1) * route.rows, size), F32)
         tails = jax.ShapeDtypeStruct((route.fan, max(TILE, route.dense_box - route.dense_tails), size), F32)
         ways = len(came)
         return list(
             call(
-                functools.partial(sum_kernel, route, planes, ways),
-                [dense(route)] * route.fan,
-                ([VMEM] * ways, [VMEM] * route.fan),
+                functools.partial(sum_kernel, route, planes, ways, places),
+                outs,
+                ([VMEM] * ways, [VMEM] * len(outs)),
                 came,
                 like(total, tails),
-                HEAVY if route is by_low else devices * CAP * route.rows * size,
+                HEAVY,
                 4 * (total.size + tails.size),
             )
         )
 
-    to_high = summed(by_low, None, [came_low[k] for k in (0, *range(2, low), 1)])
-    came_high[0], to_high[0] = lax.optimization_barrier((came_high[0], to_high[0]))
-    to_low = summed(by_high, planes, [came_high[k] for k in planes])
+    stack = lambda keys: jax.ShapeDtypeStruct((len(keys), by_low.dense_depth, size), BF16)
+    leaving, staying = split(range(2, high), 1)
+    places = [(0, None), (1, None)]
+    places += [(2, leaving.index(k)) if k in leaving else (3, staying.index(k)) for k in range(2, high)]
+    own, beside, going, kept = summed(
+        by_low,
+        None,
+        [came_low[k] for k in (0, *range(2, low), 1)],
+        [dense(by_low), dense(by_low), stack(leaving), stack(staying)],
+        places,
+    )
+    came_high[0], own = lax.optimization_barrier((came_high[0], own))
+    to_low = summed(
+        by_high,
+        planes,
+        [came_high[k] for k in planes],
+        [dense(by_high)] * low,
+        [(p, None) for p in range(low)],
+    )
+    across, bit = [], 1
+    while True:
+        came = relative(going, bit * low)
+        arrived = [k ^ bit for k in leaving]
+        across += [(came, arrived.index(0))] if 0 in arrived else []
+        bit *= 2
+        if bit >= high:
+            break
+        leaving, rest = split(staying, bit)
+        entry = lambda k: [(0, staying.index(k))] + ([(1, arrived.index(k))] if k in arrived else [])
+        groups = [group for group in (leaving, rest) if group]
+        going, *kept_next = call(
+            functools.partial(fold_kernel, [[entry(k) for k in group] for group in groups]),
+            [stack(group) for group in groups],
+            ([VMEM] * 2, [VMEM] * len(groups)),
+            (kept, came),
+            [],
+            going.size,
+            0,
+        )
+        kept, staying = (kept_next[0] if kept_next else None), rest
+    beside = relative(beside, low)
     base_shape = jax.ShapeDtypeStruct((columns, points), F32)
-    for k in planes[1:]:
-        to_high[k] = relative(to_high[k], k * low)
     for k in range(1, low):
         to_low[k] = relative(to_low[k], k)
 
@@ -396,23 +440,15 @@
         ([SMEM] + [VMEM] * (4 + low), VMEM),
         (far_list, base, *ready, *to_low),
         like(boxes, jax.ShapeDtypeStruct((devices, size), F32)),
-        4 * leaves * unit,
+        HEAVY,
         4 * boxes.size,
     )
-    across = call(
-        across_kernel,
-        jax.ShapeDtypeStruct((by_low.dense_depth, size), F32),
-        ([VMEM] * (high - 1), VMEM),
-        [to_high[k] for k in planes[:-1]],
-        [],
-        HEAVY,
-        0,
-    )
+    came = [(own, None), (beside, None), *across]
     return call(
-        functools.partial(last_kernel, routes, devices),
+        functools.partial(last_kernel, routes, devices, [at for _, at in came]),
         base_shape,
-        ([VMEM] * (3 + low), VMEM),
-        (base, across, to_high[1], *to_low),
+        ([VMEM] * (1 + low + len(came)), VMEM),
+        (base, *to_low, *(ref for ref, _ in came)),
         [],
         devices * columns * size,
         0,

time: 29.2 us -> 31 us (1.062)
  starting transfers between devices: 15.7 us -> 16.8 us
  waiting for transfers between devices: 4.53 us -> 5.22 us
    ppermute x12, starting transfers between devices: 15.7 us -> 16.8 us  [per_device(): lax.ppermute(x, 'leaf', [(i, i ^ way) for i in range(devices)])]
    ppermute x12, waiting for transfers between devices: 4.53 us -> 5.22 us  [per_device(): lax.ppermute(x, 'leaf', [(i, i ^ way) for i in range(devices)])]
  transfers between devices with their start and end apart: 12 -> 12, of which waited for: 4 -> 3; matrix products, arithmetic and copies ran while one was open for 0% -> 0% of each run, Pallas kernels for 10% -> 10%
where the time goes in v25:
time: 31 us; the launch traced here: 30.8 us
  starting transfers between devices  16.8 us (54%)
  Pallas kernels  6.79 us (22%)
  waiting for transfers between devices  5.22 us (17%)
  local copies, waits for them, and re-layouts  1.85 us (6%)
    ppermute x12, starting transfers between devices, per_device(): lax.ppermute(x, 'leaf', [(i, i ^ way) for i in range(devices)])  16.8 us
    pallas_call x8, Pallas kernels, call(): pl.pallas_call(kernel, out_shape=out_shape, in_specs=specs[0], out_specs=...  6.79 us
    ppermute x12, waiting for transfers between devices, per_device(): lax.ppermute(x, 'leaf', [(i, i ^ way) for i in range(devices)])  5.22 us
    unnamed x16, local copies, waits for them, and re-layouts  1.85 us
  transfers between devices with their start and end apart: 12, of which 3 were waited for; matrix products, arithmetic and copies ran while one was open for 0% of the time, Pallas kernels for 10%

profile of v25, /device:TPU:0, one launch (start us, length us, event | category | flops | bytes accessed | tf_op | source)
XLA Modules:
  0.0 30.8 jit_solution(9818725807044101200)
XLA Ops:
  0.0 3.1 %shard_map.91 = (bf16[784,128]{1,0:T(8,128)(2,1)}, bf16[784,128]{1,0:T(8,128)(2,1)}, bf16[784,128]{1,0:T(8,128)(2,1)}, bf16[784,128]{1,0:T(8,128)(2,1)}, bf16[32...) custom-call(s32[4,8]{1,0:T(4,128)} %bitcast.2, ...), custom_call_target="tpu_custom_call" | custom-call | flops 68157440 | bytes 2509056 | tf_op jit(solution)/shard_map/pallas_call | solution.py:294
  3.1 3.0 %collective-permute-start = (bf16[784,128]{1,0:T(8,128)(2,1)}, bf16[784,128]{1,0:T(8,128)(2,1)S(1)}, u32[]{:S(2)}, u32[]{:S(2)}) collective-permute-start(bf16[784,128]{1,0:T(8,128)(2,1)} %get-tuple-element.35), channel_id=1, source_target_pairs={{0,2},{1,3},{2,0},{3,1},{4,6},{5,7},{6,4},{7,5},{8,10},{9,11},{10,... | collective-permute-start | bytes 602120 | tf_op jit(solution)/shard_map/ppermute | solution.py:319
  6.1 0.2 collective-permute-start.2
  6.3 3.0 %collective-permute-start.3 = (bf16[320,128]{1,0:T(8,128)(2,1)}, bf16[320,128]{1,0:T(8,128)(2,1)S(1)}, u32[]{:S(2)}, u32[]{:S(2)}) collective-permute-start(bf16[320,128]{1,0:T(8,128)(2,1)} %get-tuple-element.40), channel_id=1, source_target_pairs={{0,8},{1,9},{2,10},{3,11},{4,12},{5,13},{6,14},{7,15},{8,0},{9,1},... | collective-permute-start | bytes 245768 | tf_op jit(solution)/shard_map/ppermute | solution.py:319
  9.3 1.3 %collective-permute-start.4 = (bf16[320,128]{1,0:T(8,128)(2,1)}, bf16[320,128]{1,0:T(8,128)(2,1)S(1)}, u32[]{:S(2)}, u32[]{:S(2)}) collective-permute-start(bf16[320,128]{1,0:T(8,128)(2,1)} %get-tuple-element.41), channel_id=1, source_target_pairs={{0,12},{1,13},{2,14},{3,15},{4,8},{5,9},{6,10},{7,11},{8,4},{9,5},... | collective-permute-start | bytes 245768 | tf_op jit(solution)/shard_map/ppermute | solution.py:319
  10.7 0.9 %copy-done.4 = bf16[784,128]{1,0:T(8,128)(2,1)S(1)} copy-done((bf16[784,128]{1,0:T(8,128)(2,1)S(1)}, bf16[784,128]{1,0:T(8,128)(2,1)}, u32[]{:S(2)}) %copy-start.4) | copy-done | bytes 200728
  11.6 0.9 %copy-done.6 = bf16[320,128]{1,0:T(8,128)(2,1)S(1)} copy-done((bf16[320,128]{1,0:T(8,128)(2,1)S(1)}, bf16[320,128]{1,0:T(8,128)(2,1)}, u32[]{:S(2)}) %copy-start.6) | copy-done | bytes 81944
  12.5 1.7 %collective-permute-start.5 = (bf16[320,128]{1,0:T(8,128)(2,1)}, bf16[320,128]{1,0:T(8,128)(2,1)S(1)}, u32[]{:S(2)}, u32[]{:S(2)}) collective-permute-start(bf16[320,128]{1,0:T(8,128)(2,1)} %get-tuple-element.42), channel_id=1, source_target_pairs={{0,4},{1,5},{2,6},{3,7},{4,0},{5,1},{6,2},{7,3},{8,12},{9,13},{10,... | collective-permute-start | bytes 245768 | tf_op jit(solution)/shard_map/ppermute | solution.py:319
  14.2 0.7 %collective-permute-done.1.refs_2_ = bf16[784,128]{1,0:T(8,128)(2,1)S(1)} collective-permute-done((bf16[784,128]{1,0:T(8,128)(2,1)}, bf16[784,128]{1,0:T(8,128)(2,1)S(1)}, u32[]{:S(2)}, u32[]{:S(2)}) %collective-permute-start.1) | collective-permute-done | bytes 200736 | tf_op jit(solution)/shard_map/ppermute | solution.py:319
  15.0 0.5 %shard_map.93 = (bf16[384,128]{1,0:T(8,128)(2,1)S(1)}, bf16[384,128]{1,0:T(8,128)(2,1)S(1)}, bf16[1,384,128]{2,1,0:T(8,128)(2,1)S(1)}, bf16[1,384,128]{2,1,0:T(8,128)(2,1)S(1)}) custom-call(bf16[784,128]{1,0:T(8,128)(2,1)S(1)} %get-tuple-element.34.refs_0_, bf16[784,128]{1,0:T(8,128)(2,1)S(1)} %collective-permute-done.refs_1_, ...), custom_call_target="tpu_custom_call" | custom-call | flops 4000000000 | bytes 1196032 | tf_op jit(solution)/shard_map/pallas_call | solution.py:294
  15.5 0.0 copy-start.1
  15.5 0.0 copy-start.2
  15.6 1.6 %collective-permute-start.10 = (bf16[1,384,128]{2,1,0:T(8,128)(2,1)S(1)}, bf16[1,384,128]{2,1,0:T(8,128)(2,1)S(1)}, u32[]{:S(2)}, u32[]{:S(2)}) collective-permute-start(bf16[1,384,128]{2,1,0:T(8,128)(2,1)S(1)} %get-tuple-element.56), channel_id=1, source_target_pairs={{0,4},{1,5},{2,6},{3,7},{4,0},{5,1},{6,2},{7,3},{8,12},{9,13},{10,... | collective-permute-start | bytes 294920 | tf_op jit(solution)/shard_map/ppermute | solution.py:319
  17.2 0.5 %collective-permute-done.5.refs_3_ = bf16[320,128]{1,0:T(8,128)(2,1)S(1)} collective-permute-done((bf16[320,128]{1,0:T(8,128)(2,1)}, bf16[320,128]{1,0:T(8,128)(2,1)S(1)}, u32[]{:S(2)}, u32[]{:S(2)}) %collective-permute-start.5) | collective-permute-done | bytes 81952 | tf_op jit(solution)/shard_map/ppermute | solution.py:319
  17.7 0.4 %shard_map.94 = (bf16[272,128]{1,0:T(8,128)(2,1)S(1)}, bf16[272,128]{1,0:T(8,128)(2,1)S(1)}, bf16[272,128]{1,0:T(8,128)(2,1)S(1)}, bf16[272,128]{1,0:T(8,128)(2,1)S(1)}) custom-call(bf16[320,128]{1,0:T(8,128)(2,1)S(1)} %get-tuple-element.39.refs_0_, bf16[320,128]{1,0:T(8,128)(2,1)S(1)} %collective-permute-done.3.refs_1_, ...), custom_call_target="tpu_custom_call" | custom-call | flops 4000000000 | bytes 606208 | tf_op jit(solution)/shard_map/pallas_call | solution.py:294
  18.1 0.3 collective-permute-start.6
  18.4 1.6 %collective-permute-start.7 = (bf16[272,128]{1,0:T(8,128)(2,1)S(1)}, bf16[272,128]{1,0:T(8,128)(2,1)S(1)}, u32[]{:S(2)}, u32[]{:S(2)}) collective-permute-start(bf16[272,128]{1,0:T(8,128)(2,1)S(1)} %get-tuple-element.51), channel_id=1, source_target_pairs={{0,2},{1,3},{2,0},{3,1},{4,6},{5,7},{6,4},{7,5},{8,10},{9,11},{10,... | collective-permute-start | bytes 208904 | tf_op jit(solution)/shard_map/ppermute | solution.py:319
  20.0 0.1 collective-permute-start.8
  20.1 1.2 %collective-permute-start.9 = (bf16[384,128]{1,0:T(8,128)(2,1)S(1)}, bf16[384,128]{1,0:T(8,128)(2,1)S(1)}, u32[]{:S(2)}, u32[]{:S(2)}) collective-permute-start(bf16[384,128]{1,0:T(8,128)(2,1)S(1)} %get-tuple-element.54), channel_id=1, source_target_pairs={{0,4},{1,5},{2,6},{3,7},{4,0},{5,1},{6,2},{7,3},{8,12},{9,13},{10,... | collective-permute-start | bytes 294920 | tf_op jit(solution)/shard_map/ppermute | solution.py:319
  21.3 0.8 %shard_map.95 = (f32[65,1024]{1,0:T(8,128)S(1)}, bf16[128,1536]{1,0:T(8,128)(2,1)S(1)}, bf16[64,512]{1,0:T(8,128)(2,1)S(1)}, bf16[4,128,256]{2,1,0:T(8,128)(2,1)S(1)}) custom-call(bf16[65,1024]{1,0:T(8,128)(2,1)S(1)} %copy-done.1, bf16[8,8,128,128]{3,2,1,0:T(8,128)(2,1)S(1)} %copy-done, bf16[1,12,64,64]{3,2,1,0:T(8,128)(2,1)S(1)} %copy-done.5, ...), custom_call_target="tpu_custom_call" | custom-call | flops 136314880 | bytes 3512320 | tf_op jit(solution)/shard_map/pallas_call | solution.py:294
  22.2 2.7 %collective-permute-start.11 = (bf16[1,384,128]{2,1,0:T(8,128)(2,1)S(1)}, bf16[1,384,128]{2,1,0:T(8,128)(2,1)S(1)}, u32[]{:S(2)}, u32[]{:S(2)}) collective-permute-start(bf16[1,384,128]{2,1,0:T(8,128)(2,1)S(1)} %shard_map.97), channel_id=1, source_target_pairs={{0,8},{1,9},{2,10},{3,11},{4,12},{5,13},{6,14},{7,15},{8,0},{9,1},... | collective-permute-start | bytes 294920 | tf_op jit(solution)/shard_map/ppermute | solution.py:319
  24.8 1.2 %shard_map.96.base_ref = f32[65,1024]{1,0:T(8,128)S(1)} custom-call(s32[1,12]{1,0:T(1,128)S(1)} %copy-done.7, f32[65,1024]{1,0:T(8,128)S(1)} %get-tuple-element.45.base_ref, bf16[128,1536]{1,0:T(8,128)(2,1)S(1)} %get-tuple-element.46.pairs_ref, bf16[64,512]{1,0:T(8,128)(2,1)S(1)} %get-tuple-element.47.across_ref, ...), custom_call_target="tpu_custom_call" | custom-call | flops 4000000000 | bytes 1531952 | tf_op jit(solution)/shard_map/pallas_call | solution.py:294
  26.1 3.9 %collective-permute-done.11.refs_6_ = bf16[1,384,128]{2,1,0:T(8,128)(2,1)S(1)} collective-permute-done((bf16[1,384,128]{2,1,0:T(8,128)(2,1)S(1)}, bf16[1,384,128]{2,1,0:T(8,128)(2,1)S(1)}, u32[]{:S(2)}, u32[]{:S(2)}) %collective-permute-start.11) | collective-permute-done | bytes 98336 | tf_op jit(solution)/shard_map/ppermute | solution.py:319
  30.0 0.8 %shard_map.98 = f32[65,1024]{1,0:T(8,128)} custom-call(f32[65,1024]{1,0:T(8,128)S(1)} %shard_map.96.base_ref, bf16[272,128]{1,0:T(8,128)(2,1)S(1)} %get-tuple-element.49.refs_0_, bf16[272,128]{1,0:T(8,128)(2,1)S(1)} %collective-permute-done.6.refs_1_, bf16[272,128]{1,0:T(8,128)(2,1)S(1)} %collective-permute-done.7.refs_2_, ...), custom_call_target="tpu_custom_call" | custom-call | flops 133120 | bytes 1105920 | tf_op jit(solution)/shard_map/pallas_call | solution.py:294
  (24 shorter events, 0.1 us)
Async XLA Ops:
  3.1 9.4 %collective-permute-start = (bf16[784,128]{1,0:T(8,128)(2,1)}, bf16[784,128]{1,0:T(8,128)(2,1)S(1)}, u32[]{:S(2)}, u32[]{:S(2)}) collective-permute-start(bf16[784,128]{1,0:T(8,128)(2,1)} %get-tuple-element.35), channel_id=1, source_target_pairs={{0,2},{1,3},{2,0},{3,1},{4,6},{5,7},{6,4},{7,5},{8,10},{9,11},{10,... | collective-permute-start | bytes 602120 | tf_op jit(solution)/shard_map/ppermute | solution.py:319
  6.1 8.9 %collective-permute-start.1 = (bf16[784,128]{1,0:T(8,128)(2,1)}, bf16[784,128]{1,0:T(8,128)(2,1)S(1)}, u32[]{:S(2)}, u32[]{:S(2)}) collective-permute-start(bf16[784,128]{1,0:T(8,128)(2,1)} %get-tuple-element.36), channel_id=1, source_target_pairs={{0,3},{1,2},{2,1},{3,0},{4,7},{5,6},{6,5},{7,4},{8,11},{9,10},{10,... | collective-permute-start | bytes 602120 | tf_op jit(solution)/shard_map/ppermute | solution.py:319
  6.1 8.9 %collective-permute-start.2 = (bf16[784,128]{1,0:T(8,128)(2,1)}, bf16[784,128]{1,0:T(8,128)(2,1)S(1)}, u32[]{:S(2)}, u32[]{:S(2)}) collective-permute-start(bf16[784,128]{1,0:T(8,128)(2,1)} %get-tuple-element.37), channel_id=1, source_target_pairs={{0,1},{1,0},{2,3},{3,2},{4,5},{5,4},{6,7},{7,6},{8,9},{9,8},{10,11... | collective-permute-start | bytes 602120 | tf_op jit(solution)/shard_map/ppermute | solution.py:319
  6.3 10.9 %collective-permute-start.3 = (bf16[320,128]{1,0:T(8,128)(2,1)}, bf16[320,128]{1,0:T(8,128)(2,1)S(1)}, u32[]{:S(2)}, u32[]{:S(2)}) collective-permute-start(bf16[320,128]{1,0:T(8,128)(2,1)} %get-tuple-element.40), channel_id=1, source_target_pairs={{0,8},{1,9},{2,10},{3,11},{4,12},{5,13},{6,14},{7,15},{8,0},{9,1},... | collective-permute-start | bytes 245768 | tf_op jit(solution)/shard_map/ppermute | solution.py:319
  9.3 7.9 %collective-permute-start.4 = (bf16[320,128]{1,0:T(8,128)(2,1)}, bf16[320,128]{1,0:T(8,128)(2,1)S(1)}, u32[]{:S(2)}, u32[]{:S(2)}) collective-permute-start(bf16[320,128]{1,0:T(8,128)(2,1)} %get-tuple-element.41), channel_id=1, source_target_pairs={{0,12},{1,13},{2,14},{3,15},{4,8},{5,9},{6,10},{7,11},{8,4},{9,5},... | collective-permute-start | bytes 245768 | tf_op jit(solution)/shard_map/ppermute | solution.py:319
  10.7 0.9 %copy-start.4 = (bf16[784,128]{1,0:T(8,128)(2,1)S(1)}, bf16[784,128]{1,0:T(8,128)(2,1)}, u32[]{:S(2)}) copy-start(bf16[784,128]{1,0:T(8,128)(2,1)} %get-tuple-element.31.refs_0_) | copy-start | bytes 602116
  11.6 0.9 %copy-start.6 = (bf16[320,128]{1,0:T(8,128)(2,1)S(1)}, bf16[320,128]{1,0:T(8,128)(2,1)}, u32[]{:S(2)}) copy-start(bf16[320,128]{1,0:T(8,128)(2,1)} %get-tuple-element.32.refs_1_) | copy-start | bytes 245764
  12.5 5.2 %collective-permute-start.5 = (bf16[320,128]{1,0:T(8,128)(2,1)}, bf16[320,128]{1,0:T(8,128)(2,1)S(1)}, u32[]{:S(2)}, u32[]{:S(2)}) collective-permute-start(bf16[320,128]{1,0:T(8,128)(2,1)} %get-tuple-element.42), channel_id=1, source_target_pairs={{0,4},{1,5},{2,6},{3,7},{4,0},{5,1},{6,2},{7,3},{8,12},{9,13},{10,... | collective-permute-start | bytes 245768 | tf_op jit(solution)/shard_map/ppermute | solution.py:319
  15.5 5.8 %copy-start = (bf16[8,8,128,128]{3,2,1,0:T(8,128)(2,1)S(1)}, bf16[8,8,128,128]{3,2,1,0:T(8,128)(2,1)}, u32[]{:S(2)}) copy-start(bf16[8,8,128,128]{3,2,1,0:T(8,128)(2,1)} %local_ref.1) | copy-start | bytes 6291460
  15.5 5.8 %copy-start.1 = (bf16[65,1024]{1,0:T(8,128)(2,1)S(1)}, bf16[65,1024]{1,0:T(8,128)(2,1)}, u32[]{:S(2)}) copy-start(bf16[65,1024]{1,0:T(8,128)(2,1)} %probes_ref) | copy-start | bytes 399364
  15.5 5.8 %copy-start.2 = (bf16[8,64,64]{2,1,0:T(8,128)(2,1)S(1)}, bf16[8,64,64]{2,1,0:T(8,128)(2,1)}, u32[]{:S(2)}) copy-start(bf16[8,64,64]{2,1,0:T(8,128)(2,1)} %transfer_ref.1) | copy-start | bytes 196612
  15.5 5.8 %copy-start.3 = (bf16[8,64,128]{2,1,0:T(8,128)(2,1)S(1)}, bf16[8,64,128]{2,1,0:T(8,128)(2,1)}, u32[]{:S(2)}) copy-start(bf16[8,64,128]{2,1,0:T(8,128)(2,1)} %basis_ref.1) | copy-start | bytes 393220
  15.6 5.8 %copy-start.5 = (bf16[1,12,64,64]{3,2,1,0:T(8,128)(2,1)S(1)}, bf16[1,12,64,64]{3,2,1,0:T(8,128)(2,1)}, u32[]{:S(2)}) copy-start(bf16[1,12,64,64]{3,2,1,0:T(8,128)(2,1)} %couplings_ref.1) | copy-start | bytes 294916
  15.6 6.6 %collective-permute-start.10 = (bf16[1,384,128]{2,1,0:T(8,128)(2,1)S(1)}, bf16[1,384,128]{2,1,0:T(8,128)(2,1)S(1)}, u32[]{:S(2)}, u32[]{:S(2)}) collective-permute-start(bf16[1,384,128]{2,1,0:T(8,128)(2,1)S(1)} %get-tuple-element.56), channel_id=1, source_target_pairs={{0,4},{1,5},{2,6},{3,7},{4,0},{5,1},{6,2},{7,3},{8,12},{9,13},{10,... | collective-permute-start | bytes 294920 | tf_op jit(solution)/shard_map/ppermute | solution.py:319
  18.1 6.7 %copy-start.7 = (s32[1,12]{1,0:T(1,128)S(1)}, s32[1,12]{1,0:T(1,128)}, u32[]{:S(2)}) copy-start(s32[1,12]{1,0:T(1,128)} %partner_ref.1) | copy-start | bytes 148
  18.1 3.2 %collective-permute-start.6 = (bf16[272,128]{1,0:T(8,128)(2,1)S(1)}, bf16[272,128]{1,0:T(8,128)(2,1)S(1)}, u32[]{:S(2)}, u32[]{:S(2)}) collective-permute-start(bf16[272,128]{1,0:T(8,128)(2,1)S(1)} %get-tuple-element.43), channel_id=1, source_target_pairs={{0,1},{1,0},{2,3},{3,2},{4,5},{5,4},{6,7},{7,6},{8,9},{9,8},{10,11... | collective-permute-start | bytes 208904 | tf_op jit(solution)/shard_map/ppermute | solution.py:319
  18.4 6.4 %collective-permute-start.7 = (bf16[272,128]{1,0:T(8,128)(2,1)S(1)}, bf16[272,128]{1,0:T(8,128)(2,1)S(1)}, u32[]{:S(2)}, u32[]{:S(2)}) collective-permute-start(bf16[272,128]{1,0:T(8,128)(2,1)S(1)} %get-tuple-element.51), channel_id=1, source_target_pairs={{0,2},{1,3},{2,0},{3,1},{4,6},{5,7},{6,4},{7,5},{8,10},{9,11},{10,... | collective-permute-start | bytes 208904 | tf_op jit(solution)/shard_map/ppermute | solution.py:319
  20.0 4.9 %collective-permute-start.8 = (bf16[272,128]{1,0:T(8,128)(2,1)S(1)}, bf16[272,128]{1,0:T(8,128)(2,1)S(1)}, u32[]{:S(2)}, u32[]{:S(2)}) collective-permute-start(bf16[272,128]{1,0:T(8,128)(2,1)S(1)} %get-tuple-element.52), channel_id=1, source_target_pairs={{0,3},{1,2},{2,1},{3,0},{4,7},{5,6},{6,5},{7,4},{8,11},{9,10},{10,... | collective-permute-start | bytes 208904 | tf_op jit(solution)/shard_map/ppermute | solution.py:319
  20.1 6.0 %collective-permute-start.9 = (bf16[384,128]{1,0:T(8,128)(2,1)S(1)}, bf16[384,128]{1,0:T(8,128)(2,1)S(1)}, u32[]{:S(2)}, u32[]{:S(2)}) collective-permute-start(bf16[384,128]{1,0:T(8,128)(2,1)S(1)} %get-tuple-element.54), channel_id=1, source_target_pairs={{0,4},{1,5},{2,6},{3,7},{4,0},{5,1},{6,2},{7,3},{8,12},{9,13},{10,... | collective-permute-start | bytes 294920 | tf_op jit(solution)/shard_map/ppermute | solution.py:319
  22.2 7.8 %collective-permute-start.11 = (bf16[1,384,128]{2,1,0:T(8,128)(2,1)S(1)}, bf16[1,384,128]{2,1,0:T(8,128)(2,1)S(1)}, u32[]{:S(2)}, u32[]{:S(2)}) collective-permute-start(bf16[1,384,128]{2,1,0:T(8,128)(2,1)S(1)} %shard_map.97), channel_id=1, source_target_pairs={{0,8},{1,9},{2,10},{3,11},{4,12},{5,13},{6,14},{7,15},{8,0},{9,1},... | collective-permute-start | bytes 294920 | tf_op jit(solution)/shard_map/ppermute | solution.py:319

commit v26 on v25

--- a/solution.py
+++ b/solution.py
@@ -413,12 +413,12 @@
             0,
         )
         kept, staying = (kept_next[0] if kept_next else None), rest
+        beside, probes_then, going = lax.optimization_barrier((beside, probes, going))
     beside = relative(beside, low)
     base_shape = jax.ShapeDtypeStruct((columns, points), F32)
     for k in range(1, low):
         to_low[k] = relative(to_low[k], k)
 
-    probes_then, to_low[1] = lax.optimization_barrier((probes, to_low[1]))
     base, *ready = call(
         local_kernel,
         (
@@ -443,7 +443,7 @@
         HEAVY,
         4 * boxes.size,
     )
-    came = [(own, None), (beside, None), *across]
+    came = [(own, None), *across, (beside, None)]
     return call(
         functools.partial(last_kernel, routes, devices, [at for _, at in came]),
         base_shape,

time: 31 us -> 30 us (0.968)
  waiting for transfers between devices: 5.22 us -> 3.79 us
  starting transfers between devices: 16.8 us -> 17.3 us
    ppermute x12, waiting for transfers between devices: 5.22 us -> 3.79 us  [per_device(): lax.ppermute(x, 'leaf', [(i, i ^ way) for i in range(devices)])]
    ppermute x12, starting transfers between devices: 16.8 us -> 17.3 us  [per_device(): lax.ppermute(x, 'leaf', [(i, i ^ way) for i in range(devices)])]
  transfers between devices with their start and end apart: 12 -> 12, of which waited for: 3 -> 5; matrix products, arithmetic and copies ran while one was open for 0% -> 0% of each run, Pallas kernels for 10% -> 10%
where the time goes in v26:
time: 30 us; the launch traced here: 29.8 us
  starting transfers between devices  17.3 us (58%)
  Pallas kernels  6.78 us (23%)
  waiting for transfers between devices  3.79 us (13%)
  local copies, waits for them, and re-layouts  1.85 us (6%)
    ppermute x12, starting transfers between devices, per_device(): lax.ppermute(x, 'leaf', [(i, i ^ way) for i in range(devices)])  17.3 us
    pallas_call x8, Pallas kernels, call(): pl.pallas_call(kernel, out_shape=out_shape, in_specs=specs[0], out_specs=...  6.78 us
    ppermute x12, waiting for transfers between devices, per_device(): lax.ppermute(x, 'leaf', [(i, i ^ way) for i in range(devices)])  3.79 us
    unnamed x16, local copies, waits for them, and re-layouts  1.85 us
  transfers between devices with their start and end apart: 12, of which 5 were waited for; matrix products, arithmetic and copies ran while one was open for 0% of the time, Pallas kernels for 10%

profile of v26, /device:TPU:0, one launch (start us, length us, event | category | flops | bytes accessed | tf_op | source)
XLA Modules:
  0.0 29.8 jit_solution(17646969186738309386)
XLA Ops:
  0.0 3.1 %shard_map.91 = (bf16[784,128]{1,0:T(8,128)(2,1)}, bf16[784,128]{1,0:T(8,128)(2,1)}, bf16[784,128]{1,0:T(8,128)(2,1)}, bf16[784,128]{1,0:T(8,128)(2,1)}, bf16[32...) custom-call(s32[4,8]{1,0:T(4,128)} %bitcast.2, ...), custom_call_target="tpu_custom_call" | custom-call | flops 68157440 | bytes 2509056 | tf_op jit(solution)/shard_map/pallas_call | solution.py:294
  3.1 3.0 %collective-permute-start = (bf16[784,128]{1,0:T(8,128)(2,1)}, bf16[784,128]{1,0:T(8,128)(2,1)S(1)}, u32[]{:S(2)}, u32[]{:S(2)}) collective-permute-start(bf16[784,128]{1,0:T(8,128)(2,1)} %get-tuple-element.35), channel_id=1, source_target_pairs={{0,2},{1,3},{2,0},{3,1},{4,6},{5,7},{6,4},{7,5},{8,10},{9,11},{10,... | collective-permute-start | bytes 602120 | tf_op jit(solution)/shard_map/ppermute | solution.py:319
  6.1 0.2 collective-permute-start.2
  6.3 3.0 %collective-permute-start.4 = (bf16[320,128]{1,0:T(8,128)(2,1)}, bf16[320,128]{1,0:T(8,128)(2,1)S(1)}, u32[]{:S(2)}, u32[]{:S(2)}) collective-permute-start(bf16[320,128]{1,0:T(8,128)(2,1)} %get-tuple-element.49), channel_id=1, source_target_pairs={{0,8},{1,9},{2,10},{3,11},{4,12},{5,13},{6,14},{7,15},{8,0},{9,1},... | collective-permute-start | bytes 245768 | tf_op jit(solution)/shard_map/ppermute | solution.py:319
  9.3 1.3 %collective-permute-start.5 = (bf16[320,128]{1,0:T(8,128)(2,1)}, bf16[320,128]{1,0:T(8,128)(2,1)S(1)}, u32[]{:S(2)}, u32[]{:S(2)}) collective-permute-start(bf16[320,128]{1,0:T(8,128)(2,1)} %get-tuple-element.50), channel_id=1, source_target_pairs={{0,12},{1,13},{2,14},{3,15},{4,8},{5,9},{6,10},{7,11},{8,4},{9,5},... | collective-permute-start | bytes 245768 | tf_op jit(solution)/shard_map/ppermute | solution.py:319
  10.7 0.9 %copy-done.4 = bf16[784,128]{1,0:T(8,128)(2,1)S(1)} copy-done((bf16[784,128]{1,0:T(8,128)(2,1)S(1)}, bf16[784,128]{1,0:T(8,128)(2,1)}, u32[]{:S(2)}) %copy-start.4) | copy-done | bytes 200728
  11.6 0.9 %copy-done.6 = bf16[320,128]{1,0:T(8,128)(2,1)S(1)} copy-done((bf16[320,128]{1,0:T(8,128)(2,1)S(1)}, bf16[320,128]{1,0:T(8,128)(2,1)}, u32[]{:S(2)}) %copy-start.6) | copy-done | bytes 81944
  12.5 1.7 %collective-permute-start.6 = (bf16[320,128]{1,0:T(8,128)(2,1)}, bf16[320,128]{1,0:T(8,128)(2,1)S(1)}, u32[]{:S(2)}, u32[]{:S(2)}) collective-permute-start(bf16[320,128]{1,0:T(8,128)(2,1)} %get-tuple-element.51), channel_id=1, source_target_pairs={{0,4},{1,5},{2,6},{3,7},{4,0},{5,1},{6,2},{7,3},{8,12},{9,13},{10,... | collective-permute-start | bytes 245768 | tf_op jit(solution)/shard_map/ppermute | solution.py:319
  14.2 0.7 %collective-permute-done.1.refs_2_ = bf16[784,128]{1,0:T(8,128)(2,1)S(1)} collective-permute-done((bf16[784,128]{1,0:T(8,128)(2,1)}, bf16[784,128]{1,0:T(8,128)(2,1)S(1)}, u32[]{:S(2)}, u32[]{:S(2)}) %collective-permute-start.1) | collective-permute-done | bytes 200736 | tf_op jit(solution)/shard_map/ppermute | solution.py:319
  15.0 0.5 %shard_map.93 = (bf16[384,128]{1,0:T(8,128)(2,1)S(1)}, bf16[384,128]{1,0:T(8,128)(2,1)S(1)}, bf16[1,384,128]{2,1,0:T(8,128)(2,1)S(1)}, bf16[1,384,128]{2,1,0:T(8,128)(2,1)S(1)}) custom-call(bf16[784,128]{1,0:T(8,128)(2,1)S(1)} %get-tuple-element.34.refs_0_, bf16[784,128]{1,0:T(8,128)(2,1)S(1)} %collective-permute-done.refs_1_, ...), custom_call_target="tpu_custom_call" | custom-call | flops 4000000000 | bytes 1196032 | tf_op jit(solution)/shard_map/pallas_call | solution.py:294
  15.5 1.7 %collective-permute-start.3 = (bf16[1,384,128]{2,1,0:T(8,128)(2,1)S(1)}, bf16[1,384,128]{2,1,0:T(8,128)(2,1)S(1)}, u32[]{:S(2)}, u32[]{:S(2)}) collective-permute-start(bf16[1,384,128]{2,1,0:T(8,128)(2,1)S(1)} %get-tuple-element.40), channel_id=1, source_target_pairs={{0,4},{1,5},{2,6},{3,7},{4,0},{5,1},{6,2},{7,3},{8,12},{9,13},{10,... | collective-permute-start | bytes 294920 | tf_op jit(solution)/shard_map/ppermute | solution.py:319
  17.2 0.5 %collective-permute-done.6.refs_3_ = bf16[320,128]{1,0:T(8,128)(2,1)S(1)} collective-permute-done((bf16[320,128]{1,0:T(8,128)(2,1)}, bf16[320,128]{1,0:T(8,128)(2,1)S(1)}, u32[]{:S(2)}, u32[]{:S(2)}) %collective-permute-start.6) | collective-permute-done | bytes 81952 | tf_op jit(solution)/shard_map/ppermute | solution.py:319
  17.7 0.4 %shard_map.96 = (bf16[272,128]{1,0:T(8,128)(2,1)S(1)}, bf16[272,128]{1,0:T(8,128)(2,1)S(1)}, bf16[272,128]{1,0:T(8,128)(2,1)S(1)}, bf16[272,128]{1,0:T(8,128)(2,1)S(1)}) custom-call(bf16[320,128]{1,0:T(8,128)(2,1)S(1)} %get-tuple-element.48.refs_0_, bf16[320,128]{1,0:T(8,128)(2,1)S(1)} %collective-permute-done.4.refs_1_, ...), custom_call_target="tpu_custom_call" | custom-call | flops 4000000000 | bytes 606208 | tf_op jit(solution)/shard_map/pallas_call | solution.py:294
  18.2 0.2 collective-permute-start.7
  18.4 1.6 %collective-permute-start.8 = (bf16[272,128]{1,0:T(8,128)(2,1)S(1)}, bf16[272,128]{1,0:T(8,128)(2,1)S(1)}, u32[]{:S(2)}, u32[]{:S(2)}) collective-permute-start(bf16[272,128]{1,0:T(8,128)(2,1)S(1)} %get-tuple-element.54), channel_id=1, source_target_pairs={{0,2},{1,3},{2,0},{3,1},{4,6},{5,7},{6,4},{7,5},{8,10},{9,11},{10,... | collective-permute-start | bytes 208904 | tf_op jit(solution)/shard_map/ppermute | solution.py:319
  20.0 0.2 collective-permute-start.9
  20.1 1.0 %collective-permute-done.3.refs_1_ = bf16[1,384,128]{2,1,0:T(8,128)(2,1)S(1)} collective-permute-done((bf16[1,384,128]{2,1,0:T(8,128)(2,1)S(1)}, bf16[1,384,128]{2,1,0:T(8,128)(2,1)S(1)}, u32[]{:S(2)}, u32[]{:S(2)}) %collective-permute-start.3) | collective-permute-done | bytes 98336 | tf_op jit(solution)/shard_map/ppermute | solution.py:319
  21.1 2.6 %collective-permute-start.10 = (bf16[1,384,128]{2,1,0:T(8,128)(2,1)S(1)}, bf16[1,384,128]{2,1,0:T(8,128)(2,1)S(1)}, u32[]{:S(2)}, u32[]{:S(2)}) collective-permute-start(bf16[1,384,128]{2,1,0:T(8,128)(2,1)S(1)} %shard_map.94), channel_id=1, source_target_pairs={{0,8},{1,9},{2,10},{3,11},{4,12},{5,13},{6,14},{7,15},{8,0},{9,1},... | collective-permute-start | bytes 294920 | tf_op jit(solution)/shard_map/ppermute | solution.py:319
  23.7 1.7 %collective-permute-start.11 = (bf16[384,128]{1,0:T(8,128)(2,1)S(1)}, bf16[384,128]{1,0:T(8,128)(2,1)S(1)}, u32[]{:S(2)}, u32[]{:S(2)}) collective-permute-start(bf16[384,128]{1,0:T(8,128)(2,1)S(1)} %get-tuple-element.58), channel_id=1, source_target_pairs={{0,4},{1,5},{2,6},{3,7},{4,0},{5,1},{6,2},{7,3},{8,12},{9,13},{10,... | collective-permute-start | bytes 294920 | tf_op jit(solution)/shard_map/ppermute | solution.py:319
  25.4 0.8 %shard_map.95 = (f32[65,1024]{1,0:T(8,128)S(1)}, bf16[128,1536]{1,0:T(8,128)(2,1)S(1)}, bf16[64,512]{1,0:T(8,128)(2,1)S(1)}, bf16[4,128,256]{2,1,0:T(8,128)(2,1)S(1)}) custom-call(bf16[65,1024]{1,0:T(8,128)(2,1)S(1)} %copy-done.1, bf16[8,8,128,128]{3,2,1,0:T(8,128)(2,1)S(1)} %copy-done, bf16[1,12,64,64]{3,2,1,0:T(8,128)(2,1)S(1)} %copy-done.5, ...), custom_call_target="tpu_custom_call" | custom-call | flops 136314880 | bytes 3512320 | tf_op jit(solution)/shard_map/pallas_call | solution.py:294
  26.3 1.2 %shard_map.97.base_ref = f32[65,1024]{1,0:T(8,128)S(1)} custom-call(s32[1,12]{1,0:T(1,128)S(1)} %copy-done.7, f32[65,1024]{1,0:T(8,128)S(1)} %get-tuple-element.42.base_ref, bf16[128,1536]{1,0:T(8,128)(2,1)S(1)} %get-tuple-element.43.pairs_ref, bf16[64,512]{1,0:T(8,128)(2,1)S(1)} %get-tuple-element.44.across_ref, ...), custom_call_target="tpu_custom_call" | custom-call | flops 4000000000 | bytes 1531952 | tf_op jit(solution)/shard_map/pallas_call | solution.py:294
  27.5 1.3 %collective-permute-done.10.refs_5_ = bf16[1,384,128]{2,1,0:T(8,128)(2,1)S(1)} collective-permute-done((bf16[1,384,128]{2,1,0:T(8,128)(2,1)S(1)}, bf16[1,384,128]{2,1,0:T(8,128)(2,1)S(1)}, u32[]{:S(2)}, u32[]{:S(2)}) %collective-permute-start.10) | collective-permute-done | bytes 98336 | tf_op jit(solution)/shard_map/ppermute | solution.py:319
  28.8 0.2 collective-permute-done.11.refs_6_
  29.0 0.8 %shard_map.98 = f32[65,1024]{1,0:T(8,128)} custom-call(f32[65,1024]{1,0:T(8,128)S(1)} %shard_map.97.base_ref, bf16[272,128]{1,0:T(8,128)(2,1)S(1)} %get-tuple-element.52.refs_0_, bf16[272,128]{1,0:T(8,128)(2,1)S(1)} %collective-permute-done.7.refs_1_, bf16[272,128]{1,0:T(8,128)(2,1)S(1)} %collective-permute-done.8.refs_2_, ...), custom_call_target="tpu_custom_call" | custom-call | flops 133120 | bytes 1105920 | tf_op jit(solution)/shard_map/pallas_call | solution.py:294
  (24 shorter events, 0.1 us)
Async XLA Ops:
  3.1 9.4 %collective-permute-start = (bf16[784,128]{1,0:T(8,128)(2,1)}, bf16[784,128]{1,0:T(8,128)(2,1)S(1)}, u32[]{:S(2)}, u32[]{:S(2)}) collective-permute-start(bf16[784,128]{1,0:T(8,128)(2,1)} %get-tuple-element.35), channel_id=1, source_target_pairs={{0,2},{1,3},{2,0},{3,1},{4,6},{5,7},{6,4},{7,5},{8,10},{9,11},{10,... | collective-permute-start | bytes 602120 | tf_op jit(solution)/shard_map/ppermute | solution.py:319
  6.1 8.9 %collective-permute-start.1 = (bf16[784,128]{1,0:T(8,128)(2,1)}, bf16[784,128]{1,0:T(8,128)(2,1)S(1)}, u32[]{:S(2)}, u32[]{:S(2)}) collective-permute-start(bf16[784,128]{1,0:T(8,128)(2,1)} %get-tuple-element.36), channel_id=1, source_target_pairs={{0,3},{1,2},{2,1},{3,0},{4,7},{5,6},{6,5},{7,4},{8,11},{9,10},{10,... | collective-permute-start | bytes 602120 | tf_op jit(solution)/shard_map/ppermute | solution.py:319
  6.1 8.9 %collective-permute-start.2 = (bf16[784,128]{1,0:T(8,128)(2,1)}, bf16[784,128]{1,0:T(8,128)(2,1)S(1)}, u32[]{:S(2)}, u32[]{:S(2)}) collective-permute-start(bf16[784,128]{1,0:T(8,128)(2,1)} %get-tuple-element.37), channel_id=1, source_target_pairs={{0,1},{1,0},{2,3},{3,2},{4,5},{5,4},{6,7},{7,6},{8,9},{9,8},{10,11... | collective-permute-start | bytes 602120 | tf_op jit(solution)/shard_map/ppermute | solution.py:319
  6.3 10.9 %collective-permute-start.4 = (bf16[320,128]{1,0:T(8,128)(2,1)}, bf16[320,128]{1,0:T(8,128)(2,1)S(1)}, u32[]{:S(2)}, u32[]{:S(2)}) collective-permute-start(bf16[320,128]{1,0:T(8,128)(2,1)} %get-tuple-element.49), channel_id=1, source_target_pairs={{0,8},{1,9},{2,10},{3,11},{4,12},{5,13},{6,14},{7,15},{8,0},{9,1},... | collective-permute-start | bytes 245768 | tf_op jit(solution)/shard_map/ppermute | solution.py:319
  9.3 7.9 %collective-permute-start.5 = (bf16[320,128]{1,0:T(8,128)(2,1)}, bf16[320,128]{1,0:T(8,128)(2,1)S(1)}, u32[]{:S(2)}, u32[]{:S(2)}) collective-permute-start(bf16[320,128]{1,0:T(8,128)(2,1)} %get-tuple-element.50), channel_id=1, source_target_pairs={{0,12},{1,13},{2,14},{3,15},{4,8},{5,9},{6,10},{7,11},{8,4},{9,5},... | collective-permute-start | bytes 245768 | tf_op jit(solution)/shard_map/ppermute | solution.py:319
  10.7 0.9 %copy-start.4 = (bf16[784,128]{1,0:T(8,128)(2,1)S(1)}, bf16[784,128]{1,0:T(8,128)(2,1)}, u32[]{:S(2)}) copy-start(bf16[784,128]{1,0:T(8,128)(2,1)} %get-tuple-element.32.refs_0_) | copy-start | bytes 602116
  11.6 0.9 %copy-start.6 = (bf16[320,128]{1,0:T(8,128)(2,1)S(1)}, bf16[320,128]{1,0:T(8,128)(2,1)}, u32[]{:S(2)}) copy-start(bf16[320,128]{1,0:T(8,128)(2,1)} %get-tuple-element.33.refs_1_) | copy-start | bytes 245764
  12.5 5.2 %collective-permute-start.6 = (bf16[320,128]{1,0:T(8,128)(2,1)}, bf16[320,128]{1,0:T(8,128)(2,1)S(1)}, u32[]{:S(2)}, u32[]{:S(2)}) collective-permute-start(bf16[320,128]{1,0:T(8,128)(2,1)} %get-tuple-element.51), channel_id=1, source_target_pairs={{0,4},{1,5},{2,6},{3,7},{4,0},{5,1},{6,2},{7,3},{8,12},{9,13},{10,... | collective-permute-start | bytes 245768 | tf_op jit(solution)/shard_map/ppermute | solution.py:319
  15.4 10.0 %copy-start = (bf16[8,8,128,128]{3,2,1,0:T(8,128)(2,1)S(1)}, bf16[8,8,128,128]{3,2,1,0:T(8,128)(2,1)}, u32[]{:S(2)}) copy-start(bf16[8,8,128,128]{3,2,1,0:T(8,128)(2,1)} %local_ref.1) | copy-start | bytes 6291460
  15.5 10.0 %copy-start.1 = (bf16[65,1024]{1,0:T(8,128)(2,1)S(1)}, bf16[65,1024]{1,0:T(8,128)(2,1)}, u32[]{:S(2)}) copy-start(bf16[65,1024]{1,0:T(8,128)(2,1)} %probes_ref) | copy-start | bytes 399364
  15.5 10.0 %copy-start.2 = (bf16[8,64,64]{2,1,0:T(8,128)(2,1)S(1)}, bf16[8,64,64]{2,1,0:T(8,128)(2,1)}, u32[]{:S(2)}) copy-start(bf16[8,64,64]{2,1,0:T(8,128)(2,1)} %transfer_ref.1) | copy-start | bytes 196612
  15.5 9.9 %copy-start.3 = (bf16[8,64,128]{2,1,0:T(8,128)(2,1)S(1)}, bf16[8,64,128]{2,1,0:T(8,128)(2,1)}, u32[]{:S(2)}) copy-start(bf16[8,64,128]{2,1,0:T(8,128)(2,1)} %basis_ref.1) | copy-start | bytes 393220
  15.5 9.9 %copy-start.5 = (bf16[1,12,64,64]{3,2,1,0:T(8,128)(2,1)S(1)}, bf16[1,12,64,64]{3,2,1,0:T(8,128)(2,1)}, u32[]{:S(2)}) copy-start(bf16[1,12,64,64]{3,2,1,0:T(8,128)(2,1)} %couplings_ref.1) | copy-start | bytes 294916
  15.5 5.6 %collective-permute-start.3 = (bf16[1,384,128]{2,1,0:T(8,128)(2,1)S(1)}, bf16[1,384,128]{2,1,0:T(8,128)(2,1)S(1)}, u32[]{:S(2)}, u32[]{:S(2)}) collective-permute-start(bf16[1,384,128]{2,1,0:T(8,128)(2,1)S(1)} %get-tuple-element.40), channel_id=1, source_target_pairs={{0,4},{1,5},{2,6},{3,7},{4,0},{5,1},{6,2},{7,3},{8,12},{9,13},{10,... | collective-permute-start | bytes 294920 | tf_op jit(solution)/shard_map/ppermute | solution.py:319
  18.2 8.1 %copy-start.7 = (s32[1,12]{1,0:T(1,128)S(1)}, s32[1,12]{1,0:T(1,128)}, u32[]{:S(2)}) copy-start(s32[1,12]{1,0:T(1,128)} %partner_ref.1) | copy-start | bytes 148
  18.2 8.0 %collective-permute-start.7 = (bf16[272,128]{1,0:T(8,128)(2,1)S(1)}, bf16[272,128]{1,0:T(8,128)(2,1)S(1)}, u32[]{:S(2)}, u32[]{:S(2)}) collective-permute-start(bf16[272,128]{1,0:T(8,128)(2,1)S(1)} %get-tuple-element.53), channel_id=1, source_target_pairs={{0,1},{1,0},{2,3},{3,2},{4,5},{5,4},{6,7},{7,6},{8,9},{9,8},{10,11... | collective-permute-start | bytes 208904 | tf_op jit(solution)/shard_map/ppermute | solution.py:319
  18.4 7.9 %collective-permute-start.8 = (bf16[272,128]{1,0:T(8,128)(2,1)S(1)}, bf16[272,128]{1,0:T(8,128)(2,1)S(1)}, u32[]{:S(2)}, u32[]{:S(2)}) collective-permute-start(bf16[272,128]{1,0:T(8,128)(2,1)S(1)} %get-tuple-element.54), channel_id=1, source_target_pairs={{0,2},{1,3},{2,0},{3,1},{4,6},{5,7},{6,4},{7,5},{8,10},{9,11},{10,... | collective-permute-start | bytes 208904 | tf_op jit(solution)/shard_map/ppermute | solution.py:319
  20.0 6.3 %collective-permute-start.9 = (bf16[272,128]{1,0:T(8,128)(2,1)S(1)}, bf16[272,128]{1,0:T(8,128)(2,1)S(1)}, u32[]{:S(2)}, u32[]{:S(2)}) collective-permute-start(bf16[272,128]{1,0:T(8,128)(2,1)S(1)} %get-tuple-element.55), channel_id=1, source_target_pairs={{0,3},{1,2},{2,1},{3,0},{4,7},{5,6},{6,5},{7,4},{8,11},{9,10},{10,... | collective-permute-start | bytes 208904 | tf_op jit(solution)/shard_map/ppermute | solution.py:319
  21.1 7.7 %collective-permute-start.10 = (bf16[1,384,128]{2,1,0:T(8,128)(2,1)S(1)}, bf16[1,384,128]{2,1,0:T(8,128)(2,1)S(1)}, u32[]{:S(2)}, u32[]{:S(2)}) collective-permute-start(bf16[1,384,128]{2,1,0:T(8,128)(2,1)S(1)} %shard_map.94), channel_id=1, source_target_pairs={{0,8},{1,9},{2,10},{3,11},{4,12},{5,13},{6,14},{7,15},{8,0},{9,1},... | collective-permute-start | bytes 294920 | tf_op jit(solution)/shard_map/ppermute | solution.py:319
  23.7 5.3 %collective-permute-start.11 = (bf16[384,128]{1,0:T(8,128)(2,1)S(1)}, bf16[384,128]{1,0:T(8,128)(2,1)S(1)}, u32[]{:S(2)}, u32[]{:S(2)}) collective-permute-start(bf16[384,128]{1,0:T(8,128)(2,1)S(1)} %get-tuple-element.58), channel_id=1, source_target_pairs={{0,4},{1,5},{2,6},{3,7},{4,0},{5,1},{6,2},{7,3},{8,12},{9,13},{10,... | collective-permute-start | bytes 294920 | tf_op jit(solution)/shard_map/ppermute | solution.py:319

commit v27 on v24

--- a/solution.py
+++ b/solution.py
@@ -85,18 +85,15 @@
     leaves, per_leaf, size = blocks_ref.shape[:3]
     columns, rank = probes_ref.shape[0], basis_ref.shape[1]
     copies = Copies(sems)
-    cuts = (0, leaves // 4, leaves)
-    arrivals = {}
+    first_leaves = leaves // 4
     early = [
         copies.start(probes_hbm, probes_ref),
         copies.start(dest_hbm, dest_ref),
         copies.start(leaf_hbm, leaf_ref),
     ]
-    for j, after in zip(cuts, cuts[1:]):
-        part = pl.ds(j, after - j)
-        arrivals[j] = copies.start(blocks_hbm.at[part], blocks_ref.at[part])
-        if j == 0:
-            early += [copies.start(basis_hbm, basis_ref), copies.start(transfer_hbm, transfer_ref)]
+    early += [copies.start(blocks_hbm.at[j], blocks_ref.at[j]) for j in range(first_leaves)]
+    later = [copies.start(blocks_hbm.at[j], blocks_ref.at[j]) for j in range(first_leaves, leaves)]
+    later += [copies.start(basis_hbm, basis_ref), copies.start(transfer_hbm, transfer_ref)]
 
     @pl.loop(0, devices)
     def _(i):
@@ -111,10 +108,13 @@
     row = lax.broadcasted_iota(I32, numbers.shape, 0)
     lane = lax.broadcasted_iota(I32, numbers.shape, 1)
     for j in range(leaves):
-        if j in arrivals:
-            arrivals[j].wait()
+        if j == first_leaves:
+            for copy in later:
+                copy.wait()
         x = probes_ref[:, j * size : (j + 1) * size]
-        box += dot_t(dot_t(x, basis_ref[j]).astype(BF16), transfer_ref[j])
+        for i in [j - first_leaves, *([j] if j >= leaves - first_leaves else [])] if j >= first_leaves else []:
+            coef = dot_t(probes_ref[:, i * size : (i + 1) * size], basis_ref[i]).astype(BF16)
+            box += dot_t(coef, transfer_ref[i])
         for first in range(0, per_leaf, 4):
             many = min(4, per_leaf - first)
             rhs = blocks_ref[j, first : first + many].reshape(many * size, size)
@@ -329,7 +329,7 @@
             pltpu.VMEM((high, by_high.meta - by_high.tails, size), F32),
             pltpu.SMEM((devices,), I32),
         ]
-        + sems(7 + low + high),
+        + sems(5 + leaves + low + high),
         blocks * unit,
     )
     came_low, came_high = list(sent[:low]), list(sent[low:])

time: 29.2 us -> 29.4 us (level)
  no operation moved by 1% of the time
where the time goes in v27:
time: 29.4 us; the launch traced here: 29.2 us
  starting transfers between devices  15.7 us (53%)
  Pallas kernels  7.04 us (24%)
  waiting for transfers between devices  4.53 us (15%)
  local copies, waits for them, and re-layouts  1.84 us (6%)
    ppermute x12, starting transfers between devices, per_device(): lax.ppermute(x, 'leaf', [(i, i ^ way) for i in range(devices)])  15.7 us
    pallas_call x8, Pallas kernels, call(): pl.pallas_call(kernel, out_shape=out_shape, in_specs=specs[0], out_specs=...  7.04 us
    ppermute x12, waiting for transfers between devices, per_device(): lax.ppermute(x, 'leaf', [(i, i ^ way) for i in range(devices)])  4.53 us
    unnamed x16, local copies, waits for them, and re-layouts  1.84 us
  transfers between devices with their start and end apart: 12, of which 4 were waited for; matrix products, arithmetic and copies ran while one was open for 0% of the time, Pallas kernels for 10%

profile of v27, /device:TPU:0, one launch (start us, length us, event | category | flops | bytes accessed | tf_op | source)
XLA Modules:
  0.0 29.2 jit_solution(7622776600889888435)
XLA Ops:
  0.0 3.3 %shard_map.91 = (bf16[784,128]{1,0:T(8,128)(2,1)}, bf16[784,128]{1,0:T(8,128)(2,1)}, bf16[784,128]{1,0:T(8,128)(2,1)}, bf16[784,128]{1,0:T(8,128)(2,1)}, bf16[32...) custom-call(s32[4,8]{1,0:T(4,128)} %bitcast.2, ...), custom_call_target="tpu_custom_call" | custom-call | flops 68157440 | bytes 2509056 | tf_op jit(solution)/shard_map/pallas_call | solution.py:286
  3.3 3.0 %collective-permute-start = (bf16[784,128]{1,0:T(8,128)(2,1)}, bf16[784,128]{1,0:T(8,128)(2,1)S(1)}, u32[]{:S(2)}, u32[]{:S(2)}) collective-permute-start(bf16[784,128]{1,0:T(8,128)(2,1)} %get-tuple-element.35), channel_id=1, source_target_pairs={{0,2},{1,3},{2,0},{3,1},{4,6},{5,7},{6,4},{7,5},{8,10},{9,11},{10,... | collective-permute-start | bytes 602120 | tf_op jit(solution)/shard_map/ppermute | solution.py:311
  6.3 0.2 collective-permute-start.2
  6.5 3.0 %collective-permute-start.3 = (bf16[320,128]{1,0:T(8,128)(2,1)}, bf16[320,128]{1,0:T(8,128)(2,1)S(1)}, u32[]{:S(2)}, u32[]{:S(2)}) collective-permute-start(bf16[320,128]{1,0:T(8,128)(2,1)} %get-tuple-element.40), channel_id=1, source_target_pairs={{0,8},{1,9},{2,10},{3,11},{4,12},{5,13},{6,14},{7,15},{8,0},{9,1},... | collective-permute-start | bytes 245768 | tf_op jit(solution)/shard_map/ppermute | solution.py:311
  9.5 1.3 %collective-permute-start.4 = (bf16[320,128]{1,0:T(8,128)(2,1)}, bf16[320,128]{1,0:T(8,128)(2,1)S(1)}, u32[]{:S(2)}, u32[]{:S(2)}) collective-permute-start(bf16[320,128]{1,0:T(8,128)(2,1)} %get-tuple-element.41), channel_id=1, source_target_pairs={{0,12},{1,13},{2,14},{3,15},{4,8},{5,9},{6,10},{7,11},{8,4},{9,5},... | collective-permute-start | bytes 245768 | tf_op jit(solution)/shard_map/ppermute | solution.py:311
  10.9 0.9 %copy-done.4 = bf16[784,128]{1,0:T(8,128)(2,1)S(1)} copy-done((bf16[784,128]{1,0:T(8,128)(2,1)S(1)}, bf16[784,128]{1,0:T(8,128)(2,1)}, u32[]{:S(2)}) %copy-start.4) | copy-done | bytes 200728
  11.8 0.9 %copy-done.6 = bf16[320,128]{1,0:T(8,128)(2,1)S(1)} copy-done((bf16[320,128]{1,0:T(8,128)(2,1)S(1)}, bf16[320,128]{1,0:T(8,128)(2,1)}, u32[]{:S(2)}) %copy-start.6) | copy-done | bytes 81944
  12.7 1.7 %collective-permute-start.5 = (bf16[320,128]{1,0:T(8,128)(2,1)}, bf16[320,128]{1,0:T(8,128)(2,1)S(1)}, u32[]{:S(2)}, u32[]{:S(2)}) collective-permute-start(bf16[320,128]{1,0:T(8,128)(2,1)} %get-tuple-element.42), channel_id=1, source_target_pairs={{0,4},{1,5},{2,6},{3,7},{4,0},{5,1},{6,2},{7,3},{8,12},{9,13},{10,... | collective-permute-start | bytes 245768 | tf_op jit(solution)/shard_map/ppermute | solution.py:311
  14.5 0.7 %collective-permute-done.1.refs_2_ = bf16[784,128]{1,0:T(8,128)(2,1)S(1)} collective-permute-done((bf16[784,128]{1,0:T(8,128)(2,1)}, bf16[784,128]{1,0:T(8,128)(2,1)S(1)}, u32[]{:S(2)}, u32[]{:S(2)}) %collective-permute-start.1) | collective-permute-done | bytes 200736 | tf_op jit(solution)/shard_map/ppermute | solution.py:311
  15.2 0.0 copy-start.3
  15.2 0.0 copy-start.5
  15.2 0.5 %shard_map.93 = (bf16[384,128]{1,0:T(8,128)(2,1)S(1)}, bf16[384,128]{1,0:T(8,128)(2,1)S(1)}, bf16[384,128]{1,0:T(8,128)(2,1)S(1)}, bf16[384,128]{1,0:T(8,128)(2,1)S(1)}) custom-call(bf16[784,128]{1,0:T(8,128)(2,1)S(1)} %get-tuple-element.34.refs_0_, bf16[784,128]{1,0:T(8,128)(2,1)S(1)} %collective-permute-done.refs_1_, ...), custom_call_target="tpu_custom_call" | custom-call | flops 4000000000 | bytes 1196032 | tf_op jit(solution)/shard_map/pallas_call | solution.py:286
  15.7 2.6 %collective-permute-start.9 = (bf16[384,128]{1,0:T(8,128)(2,1)S(1)}, bf16[384,128]{1,0:T(8,128)(2,1)S(1)}, u32[]{:S(2)}, u32[]{:S(2)}) collective-permute-start(bf16[384,128]{1,0:T(8,128)(2,1)S(1)} %get-tuple-element.54), channel_id=1, source_target_pairs={{0,8},{1,9},{2,10},{3,11},{4,12},{5,13},{6,14},{7,15},{8,0},{9,1},... | collective-permute-start | bytes 294920 | tf_op jit(solution)/shard_map/ppermute | solution.py:311
  18.4 1.3 %collective-permute-start.10 = (bf16[384,128]{1,0:T(8,128)(2,1)S(1)}, bf16[384,128]{1,0:T(8,128)(2,1)S(1)}, u32[]{:S(2)}, u32[]{:S(2)}) collective-permute-start(bf16[384,128]{1,0:T(8,128)(2,1)S(1)} %get-tuple-element.55), channel_id=1, source_target_pairs={{0,12},{1,13},{2,14},{3,15},{4,8},{5,9},{6,10},{7,11},{8,4},{9,5},... | collective-permute-start | bytes 294920 | tf_op jit(solution)/shard_map/ppermute | solution.py:311
  19.7 0.5 %shard_map.94 = (bf16[272,128]{1,0:T(8,128)(2,1)S(1)}, bf16[272,128]{1,0:T(8,128)(2,1)S(1)}, bf16[272,128]{1,0:T(8,128)(2,1)S(1)}, bf16[272,128]{1,0:T(8,128)(2,1)S(1)}) custom-call(bf16[320,128]{1,0:T(8,128)(2,1)S(1)} %get-tuple-element.39.refs_0_, bf16[320,128]{1,0:T(8,128)(2,1)S(1)} %collective-permute-done.3.refs_1_, ...), custom_call_target="tpu_custom_call" | custom-call | flops 131072 | bytes 606208 | tf_op jit(solution)/shard_map/pallas_call | solution.py:286
  20.2 0.5 %collective-permute-start.6 = (bf16[272,128]{1,0:T(8,128)(2,1)S(1)}, bf16[272,128]{1,0:T(8,128)(2,1)S(1)}, u32[]{:S(2)}, u32[]{:S(2)}) collective-permute-start(bf16[272,128]{1,0:T(8,128)(2,1)S(1)} %get-tuple-element.43), channel_id=1, source_target_pairs={{0,1},{1,0},{2,3},{3,2},{4,5},{5,4},{6,7},{7,6},{8,9},{9,8},{10,11... | collective-permute-start | bytes 208904 | tf_op jit(solution)/shard_map/ppermute | solution.py:311
  20.7 1.5 %collective-permute-start.7 = (bf16[272,128]{1,0:T(8,128)(2,1)S(1)}, bf16[272,128]{1,0:T(8,128)(2,1)S(1)}, u32[]{:S(2)}, u32[]{:S(2)}) collective-permute-start(bf16[272,128]{1,0:T(8,128)(2,1)S(1)} %get-tuple-element.51), channel_id=1, source_target_pairs={{0,2},{1,3},{2,0},{3,1},{4,6},{5,7},{6,4},{7,5},{8,10},{9,11},{10,... | collective-permute-start | bytes 208904 | tf_op jit(solution)/shard_map/ppermute | solution.py:311
  22.2 0.4 %collective-permute-start.11 = (bf16[384,128]{1,0:T(8,128)(2,1)S(1)}, bf16[384,128]{1,0:T(8,128)(2,1)S(1)}, u32[]{:S(2)}, u32[]{:S(2)}) collective-permute-start(bf16[384,128]{1,0:T(8,128)(2,1)S(1)} %get-tuple-element.56), channel_id=1, source_target_pairs={{0,4},{1,5},{2,6},{3,7},{4,0},{5,1},{6,2},{7,3},{8,12},{9,13},{10,... | collective-permute-start | bytes 294920 | tf_op jit(solution)/shard_map/ppermute | solution.py:311
  22.6 0.8 %shard_map.95 = (f32[65,1024]{1,0:T(8,128)S(1)}, bf16[128,1536]{1,0:T(8,128)(2,1)S(1)}, bf16[64,512]{1,0:T(8,128)(2,1)S(1)}, bf16[4,128,256]{2,1,0:T(8,128)(2,1)S(1)}) custom-call(bf16[65,1024]{1,0:T(8,128)(2,1)S(1)} %copy-done.1, bf16[8,8,128,128]{3,2,1,0:T(8,128)(2,1)S(1)} %copy-done, bf16[1,12,64,64]{3,2,1,0:T(8,128)(2,1)S(1)} %copy-done.5, ...), custom_call_target="tpu_custom_call" | custom-call | flops 136314880 | bytes 3512320 | tf_op jit(solution)/shard_map/pallas_call | solution.py:286
  23.4 1.6 %collective-permute-done.7.refs_2_.refs_4_ = bf16[272,128]{1,0:T(8,128)(2,1)S(1)} collective-permute-done((bf16[272,128]{1,0:T(8,128)(2,1)S(1)}, bf16[272,128]{1,0:T(8,128)(2,1)S(1)}, u32[]{:S(2)}, u32[]{:S(2)}) %collective-permute-start.7) | collective-permute-done | bytes 69664 | tf_op jit(solution)/shard_map/ppermute | solution.py:311
  25.0 1.6 %collective-permute-done.8.refs_3_.refs_5_ = bf16[272,128]{1,0:T(8,128)(2,1)S(1)} collective-permute-done((bf16[272,128]{1,0:T(8,128)(2,1)S(1)}, bf16[272,128]{1,0:T(8,128)(2,1)S(1)}, u32[]{:S(2)}, u32[]{:S(2)}) %collective-permute-start.8) | collective-permute-done | bytes 69664 | tf_op jit(solution)/shard_map/ppermute | solution.py:311
  26.6 1.2 %shard_map.96.base_ref = f32[65,1024]{1,0:T(8,128)S(1)} custom-call(s32[1,12]{1,0:T(1,128)S(1)} %copy-done.7, f32[65,1024]{1,0:T(8,128)S(1)} %get-tuple-element.45.base_ref, bf16[128,1536]{1,0:T(8,128)(2,1)S(1)} %get-tuple-element.46.pairs_ref, bf16[64,512]{1,0:T(8,128)(2,1)S(1)} %get-tuple-element.47.across_ref, ...), custom_call_target="tpu_custom_call" | custom-call | flops 68157440 | bytes 1531952 | tf_op jit(solution)/shard_map/pallas_call | solution.py:286
  27.9 0.6 %collective-permute-done.11.refs_1_ = bf16[384,128]{1,0:T(8,128)(2,1)S(1)} collective-permute-done((bf16[384,128]{1,0:T(8,128)(2,1)S(1)}, bf16[384,128]{1,0:T(8,128)(2,1)S(1)}, u32[]{:S(2)}, u32[]{:S(2)}) %collective-permute-start.11) | collective-permute-done | bytes 98336 | tf_op jit(solution)/shard_map/ppermute | solution.py:311
  28.5 0.8 %shard_map.98 = f32[65,1024]{1,0:T(8,128)} custom-call(f32[65,1024]{1,0:T(8,128)S(1)} %shard_map.96.base_ref, f32[384,128]{1,0:T(8,128)S(1)} %shard_map.97.refs_0_, bf16[384,128]{1,0:T(8,128)(2,1)S(1)} %collective-permute-done.11.refs_1_, bf16[272,128]{1,0:T(8,128)(2,1)S(1)} %get-tuple-element.49.refs_0_.refs_2_, ...), custom_call_target="tpu_custom_call" | custom-call | flops 133120 | bytes 1105920 | tf_op jit(solution)/shard_map/pallas_call | solution.py:286
  (24 shorter events, 0.1 us)
Async XLA Ops:
  3.3 9.4 %collective-permute-start = (bf16[784,128]{1,0:T(8,128)(2,1)}, bf16[784,128]{1,0:T(8,128)(2,1)S(1)}, u32[]{:S(2)}, u32[]{:S(2)}) collective-permute-start(bf16[784,128]{1,0:T(8,128)(2,1)} %get-tuple-element.35), channel_id=1, source_target_pairs={{0,2},{1,3},{2,0},{3,1},{4,6},{5,7},{6,4},{7,5},{8,10},{9,11},{10,... | collective-permute-start | bytes 602120 | tf_op jit(solution)/shard_map/ppermute | solution.py:311
  6.3 8.9 %collective-permute-start.1 = (bf16[784,128]{1,0:T(8,128)(2,1)}, bf16[784,128]{1,0:T(8,128)(2,1)S(1)}, u32[]{:S(2)}, u32[]{:S(2)}) collective-permute-start(bf16[784,128]{1,0:T(8,128)(2,1)} %get-tuple-element.36), channel_id=1, source_target_pairs={{0,3},{1,2},{2,1},{3,0},{4,7},{5,6},{6,5},{7,4},{8,11},{9,10},{10,... | collective-permute-start | bytes 602120 | tf_op jit(solution)/shard_map/ppermute | solution.py:311
  6.3 8.9 %collective-permute-start.2 = (bf16[784,128]{1,0:T(8,128)(2,1)}, bf16[784,128]{1,0:T(8,128)(2,1)S(1)}, u32[]{:S(2)}, u32[]{:S(2)}) collective-permute-start(bf16[784,128]{1,0:T(8,128)(2,1)} %get-tuple-element.37), channel_id=1, source_target_pairs={{0,1},{1,0},{2,3},{3,2},{4,5},{5,4},{6,7},{7,6},{8,9},{9,8},{10,11... | collective-permute-start | bytes 602120 | tf_op jit(solution)/shard_map/ppermute | solution.py:311
  6.5 13.2 %collective-permute-start.3 = (bf16[320,128]{1,0:T(8,128)(2,1)}, bf16[320,128]{1,0:T(8,128)(2,1)S(1)}, u32[]{:S(2)}, u32[]{:S(2)}) collective-permute-start(bf16[320,128]{1,0:T(8,128)(2,1)} %get-tuple-element.40), channel_id=1, source_target_pairs={{0,8},{1,9},{2,10},{3,11},{4,12},{5,13},{6,14},{7,15},{8,0},{9,1},... | collective-permute-start | bytes 245768 | tf_op jit(solution)/shard_map/ppermute | solution.py:311
  9.5 10.2 %collective-permute-start.4 = (bf16[320,128]{1,0:T(8,128)(2,1)}, bf16[320,128]{1,0:T(8,128)(2,1)S(1)}, u32[]{:S(2)}, u32[]{:S(2)}) collective-permute-start(bf16[320,128]{1,0:T(8,128)(2,1)} %get-tuple-element.41), channel_id=1, source_target_pairs={{0,12},{1,13},{2,14},{3,15},{4,8},{5,9},{6,10},{7,11},{8,4},{9,5},... | collective-permute-start | bytes 245768 | tf_op jit(solution)/shard_map/ppermute | solution.py:311
  10.9 0.9 %copy-start.4 = (bf16[784,128]{1,0:T(8,128)(2,1)S(1)}, bf16[784,128]{1,0:T(8,128)(2,1)}, u32[]{:S(2)}) copy-start(bf16[784,128]{1,0:T(8,128)(2,1)} %get-tuple-element.31.refs_0_) | copy-start | bytes 602116
  11.8 0.9 %copy-start.6 = (bf16[320,128]{1,0:T(8,128)(2,1)S(1)}, bf16[320,128]{1,0:T(8,128)(2,1)}, u32[]{:S(2)}) copy-start(bf16[320,128]{1,0:T(8,128)(2,1)} %get-tuple-element.32.refs_1_) | copy-start | bytes 245764
  12.7 7.0 %collective-permute-start.5 = (bf16[320,128]{1,0:T(8,128)(2,1)}, bf16[320,128]{1,0:T(8,128)(2,1)S(1)}, u32[]{:S(2)}, u32[]{:S(2)}) collective-permute-start(bf16[320,128]{1,0:T(8,128)(2,1)} %get-tuple-element.42), channel_id=1, source_target_pairs={{0,4},{1,5},{2,6},{3,7},{4,0},{5,1},{6,2},{7,3},{8,12},{9,13},{10,... | collective-permute-start | bytes 245768 | tf_op jit(solution)/shard_map/ppermute | solution.py:311
  15.2 7.4 %copy-start = (bf16[8,8,128,128]{3,2,1,0:T(8,128)(2,1)S(1)}, bf16[8,8,128,128]{3,2,1,0:T(8,128)(2,1)}, u32[]{:S(2)}) copy-start(bf16[8,8,128,128]{3,2,1,0:T(8,128)(2,1)} %local_ref.1) | copy-start | bytes 6291460
  15.2 7.4 %copy-start.1 = (bf16[65,1024]{1,0:T(8,128)(2,1)S(1)}, bf16[65,1024]{1,0:T(8,128)(2,1)}, u32[]{:S(2)}) copy-start(bf16[65,1024]{1,0:T(8,128)(2,1)} %probes_ref) | copy-start | bytes 399364
  15.2 7.4 %copy-start.2 = (bf16[8,64,64]{2,1,0:T(8,128)(2,1)S(1)}, bf16[8,64,64]{2,1,0:T(8,128)(2,1)}, u32[]{:S(2)}) copy-start(bf16[8,64,64]{2,1,0:T(8,128)(2,1)} %transfer_ref.1) | copy-start | bytes 196612
  15.2 7.4 %copy-start.3 = (bf16[8,64,128]{2,1,0:T(8,128)(2,1)S(1)}, bf16[8,64,128]{2,1,0:T(8,128)(2,1)}, u32[]{:S(2)}) copy-start(bf16[8,64,128]{2,1,0:T(8,128)(2,1)} %basis_ref.1) | copy-start | bytes 393220
  15.2 7.4 %copy-start.5 = (bf16[1,12,64,64]{3,2,1,0:T(8,128)(2,1)S(1)}, bf16[1,12,64,64]{3,2,1,0:T(8,128)(2,1)}, u32[]{:S(2)}) copy-start(bf16[1,12,64,64]{3,2,1,0:T(8,128)(2,1)} %couplings_ref.1) | copy-start | bytes 294916
  15.7 10.9 %copy-start.7 = (s32[1,12]{1,0:T(1,128)S(1)}, s32[1,12]{1,0:T(1,128)}, u32[]{:S(2)}) copy-start(s32[1,12]{1,0:T(1,128)} %partner_ref.1) | copy-start | bytes 148
  15.7 12.1 %collective-permute-start.9 = (bf16[384,128]{1,0:T(8,128)(2,1)S(1)}, bf16[384,128]{1,0:T(8,128)(2,1)S(1)}, u32[]{:S(2)}, u32[]{:S(2)}) collective-permute-start(bf16[384,128]{1,0:T(8,128)(2,1)S(1)} %get-tuple-element.54), channel_id=1, source_target_pairs={{0,8},{1,9},{2,10},{3,11},{4,12},{5,13},{6,14},{7,15},{8,0},{9,1},... | collective-permute-start | bytes 294920 | tf_op jit(solution)/shard_map/ppermute | solution.py:311
  18.4 9.5 %collective-permute-start.10 = (bf16[384,128]{1,0:T(8,128)(2,1)S(1)}, bf16[384,128]{1,0:T(8,128)(2,1)S(1)}, u32[]{:S(2)}, u32[]{:S(2)}) collective-permute-start(bf16[384,128]{1,0:T(8,128)(2,1)S(1)} %get-tuple-element.55), channel_id=1, source_target_pairs={{0,12},{1,13},{2,14},{3,15},{4,8},{5,9},{6,10},{7,11},{8,4},{9,5},... | collective-permute-start | bytes 294920 | tf_op jit(solution)/shard_map/ppermute | solution.py:311
  20.2 2.0 %collective-permute-start.6 = (bf16[272,128]{1,0:T(8,128)(2,1)S(1)}, bf16[272,128]{1,0:T(8,128)(2,1)S(1)}, u32[]{:S(2)}, u32[]{:S(2)}) collective-permute-start(bf16[272,128]{1,0:T(8,128)(2,1)S(1)} %get-tuple-element.43), channel_id=1, source_target_pairs={{0,1},{1,0},{2,3},{3,2},{4,5},{5,4},{6,7},{7,6},{8,9},{9,8},{10,11... | collective-permute-start | bytes 208904 | tf_op jit(solution)/shard_map/ppermute | solution.py:311
  20.7 4.3 %collective-permute-start.7 = (bf16[272,128]{1,0:T(8,128)(2,1)S(1)}, bf16[272,128]{1,0:T(8,128)(2,1)S(1)}, u32[]{:S(2)}, u32[]{:S(2)}) collective-permute-start(bf16[272,128]{1,0:T(8,128)(2,1)S(1)} %get-tuple-element.51), channel_id=1, source_target_pairs={{0,2},{1,3},{2,0},{3,1},{4,6},{5,7},{6,4},{7,5},{8,10},{9,11},{10,... | collective-permute-start | bytes 208904 | tf_op jit(solution)/shard_map/ppermute | solution.py:311
  22.2 4.4 %collective-permute-start.8 = (bf16[272,128]{1,0:T(8,128)(2,1)S(1)}, bf16[272,128]{1,0:T(8,128)(2,1)S(1)}, u32[]{:S(2)}, u32[]{:S(2)}) collective-permute-start(bf16[272,128]{1,0:T(8,128)(2,1)S(1)} %get-tuple-element.52), channel_id=1, source_target_pairs={{0,3},{1,2},{2,1},{3,0},{4,7},{5,6},{6,5},{7,4},{8,11},{9,10},{10,... | collective-permute-start | bytes 208904 | tf_op jit(solution)/shard_map/ppermute | solution.py:311
  22.2 6.3 %collective-permute-start.11 = (bf16[384,128]{1,0:T(8,128)(2,1)S(1)}, bf16[384,128]{1,0:T(8,128)(2,1)S(1)}, u32[]{:S(2)}, u32[]{:S(2)}) collective-permute-start(bf16[384,128]{1,0:T(8,128)(2,1)S(1)} %get-tuple-element.56), channel_id=1, source_target_pairs={{0,4},{1,5},{2,6},{3,7},{4,0},{5,1},{6,2},{7,3},{8,12},{9,13},{10,... | collective-permute-start | bytes 294920 | tf_op jit(solution)/shard_map/ppermute | solution.py:311

commit v28 on v24

--- a/solution.py
+++ b/solution.py
@@ -140,21 +140,23 @@
                 tails[to_high, pl.ds(at, 1), :] = block[main:]
                 numbers = jnp.where((row == low + to_high) & (lane == at), number, numbers)
 
+    numbers = numbers.astype(F32)
+    leaving = []
+    blank = jnp.zeros((TILE - 1, size), F32)
+    for i in (*range(2, low), 1, 0):
+        tile = jnp.concatenate([numbers[i : i + 1], blank], axis=0)
+        send_low[i, by_low.meta : by_low.box, :] = tile.astype(BF16)
+        leaving.append(copies.start(send_low.at[i], outs[i]))
     half = by_high.half
     packed = jnp.concatenate([box[:half], box[half:main]], axis=1).astype(BF16)
     last = jnp.concatenate([box[main:], jnp.zeros_like(box[main:])], axis=1)
-    numbers = numbers.astype(F32)
     blank = jnp.zeros((TILE - 2, size), F32)
-    for i in range(low):
-        tile = jnp.concatenate([numbers[i : i + 1], last, blank], axis=0)
-        send_low[i, by_low.meta : by_low.box, :] = tile.astype(BF16)
     for i in range(high):
         tile = jnp.concatenate([numbers[low + i : low + i + 1], last, blank], axis=0)
         send_high[i, by_high.tails : by_high.meta, :] = tails[i].astype(BF16)
         send_high[i, by_high.meta : by_high.box, :] = tile.astype(BF16)
         send_high[i, by_high.box :, :] = packed
-    leaving = [copies.start(send_low.at[i], outs[i]) for i in range(low)]
-    leaving += [copies.start(send_high.at[i], outs[low + i]) for i in range(high)]
+        leaving.append(copies.start(send_high.at[i], outs[low + i]))
     for copy in leaving:
         copy.wait()
 

time: 29.2 us -> 29.2 us (level)
  no operation moved by 1% of the time
where the time goes in v28:
time: 29.2 us; the launch traced here: 29 us
  starting transfers between devices  15.7 us (54%)
  Pallas kernels  6.82 us (23%)
  waiting for transfers between devices  4.55 us (16%)
  local copies, waits for them, and re-layouts  1.84 us (6%)
    ppermute x12, starting transfers between devices, per_device(): lax.ppermute(x, 'leaf', [(i, i ^ way) for i in range(devices)])  15.7 us
    pallas_call x8, Pallas kernels, call(): pl.pallas_call(kernel, out_shape=out_shape, in_specs=specs[0], out_specs=...  6.82 us
    ppermute x12, waiting for transfers between devices, per_device(): lax.ppermute(x, 'leaf', [(i, i ^ way) for i in range(devices)])  4.55 us
    unnamed x16, local copies, waits for them, and re-layouts  1.84 us
  transfers between devices with their start and end apart: 12, of which 4 were waited for; matrix products, arithmetic and copies ran while one was open for 0% of the time, Pallas kernels for 10%

profile of v28, /device:TPU:0, one launch (start us, length us, event | category | flops | bytes accessed | tf_op | source)
XLA Modules:
  0.0 29.0 jit_solution(9807452635713977715)
XLA Ops:
  0.0 3.1 %shard_map.91 = (bf16[784,128]{1,0:T(8,128)(2,1)}, bf16[784,128]{1,0:T(8,128)(2,1)}, bf16[784,128]{1,0:T(8,128)(2,1)}, bf16[784,128]{1,0:T(8,128)(2,1)}, bf16[32...) custom-call(s32[4,8]{1,0:T(4,128)} %bitcast.2, ...), custom_call_target="tpu_custom_call" | custom-call | flops 68157440 | bytes 2509056 | tf_op jit(solution)/shard_map/pallas_call | solution.py:288
  3.1 3.0 %collective-permute-start = (bf16[784,128]{1,0:T(8,128)(2,1)}, bf16[784,128]{1,0:T(8,128)(2,1)S(1)}, u32[]{:S(2)}, u32[]{:S(2)}) collective-permute-start(bf16[784,128]{1,0:T(8,128)(2,1)} %get-tuple-element.35), channel_id=1, source_target_pairs={{0,2},{1,3},{2,0},{3,1},{4,6},{5,7},{6,4},{7,5},{8,10},{9,11},{10,... | collective-permute-start | bytes 602120 | tf_op jit(solution)/shard_map/ppermute | solution.py:313
  6.1 0.2 collective-permute-start.2
  6.3 3.0 %collective-permute-start.3 = (bf16[320,128]{1,0:T(8,128)(2,1)}, bf16[320,128]{1,0:T(8,128)(2,1)S(1)}, u32[]{:S(2)}, u32[]{:S(2)}) collective-permute-start(bf16[320,128]{1,0:T(8,128)(2,1)} %get-tuple-element.40), channel_id=1, source_target_pairs={{0,8},{1,9},{2,10},{3,11},{4,12},{5,13},{6,14},{7,15},{8,0},{9,1},... | collective-permute-start | bytes 245768 | tf_op jit(solution)/shard_map/ppermute | solution.py:313
  9.3 1.3 %collective-permute-start.4 = (bf16[320,128]{1,0:T(8,128)(2,1)}, bf16[320,128]{1,0:T(8,128)(2,1)S(1)}, u32[]{:S(2)}, u32[]{:S(2)}) collective-permute-start(bf16[320,128]{1,0:T(8,128)(2,1)} %get-tuple-element.41), channel_id=1, source_target_pairs={{0,12},{1,13},{2,14},{3,15},{4,8},{5,9},{6,10},{7,11},{8,4},{9,5},... | collective-permute-start | bytes 245768 | tf_op jit(solution)/shard_map/ppermute | solution.py:313
  10.7 0.9 %copy-done.4 = bf16[784,128]{1,0:T(8,128)(2,1)S(1)} copy-done((bf16[784,128]{1,0:T(8,128)(2,1)S(1)}, bf16[784,128]{1,0:T(8,128)(2,1)}, u32[]{:S(2)}) %copy-start.4) | copy-done | bytes 200728
  11.6 0.9 %copy-done.6 = bf16[320,128]{1,0:T(8,128)(2,1)S(1)} copy-done((bf16[320,128]{1,0:T(8,128)(2,1)S(1)}, bf16[320,128]{1,0:T(8,128)(2,1)}, u32[]{:S(2)}) %copy-start.6) | copy-done | bytes 81944
  12.5 1.7 %collective-permute-start.5 = (bf16[320,128]{1,0:T(8,128)(2,1)}, bf16[320,128]{1,0:T(8,128)(2,1)S(1)}, u32[]{:S(2)}, u32[]{:S(2)}) collective-permute-start(bf16[320,128]{1,0:T(8,128)(2,1)} %get-tuple-element.42), channel_id=1, source_target_pairs={{0,4},{1,5},{2,6},{3,7},{4,0},{5,1},{6,2},{7,3},{8,12},{9,13},{10,... | collective-permute-start | bytes 245768 | tf_op jit(solution)/shard_map/ppermute | solution.py:313
  14.2 0.7 %collective-permute-done.1.refs_2_ = bf16[784,128]{1,0:T(8,128)(2,1)S(1)} collective-permute-done((bf16[784,128]{1,0:T(8,128)(2,1)}, bf16[784,128]{1,0:T(8,128)(2,1)S(1)}, u32[]{:S(2)}, u32[]{:S(2)}) %collective-permute-start.1) | collective-permute-done | bytes 200736 | tf_op jit(solution)/shard_map/ppermute | solution.py:313
  15.0 0.0 copy-start.3
  15.0 0.0 copy-start.5
  15.0 0.5 %shard_map.93 = (bf16[384,128]{1,0:T(8,128)(2,1)S(1)}, bf16[384,128]{1,0:T(8,128)(2,1)S(1)}, bf16[384,128]{1,0:T(8,128)(2,1)S(1)}, bf16[384,128]{1,0:T(8,128)(2,1)S(1)}) custom-call(bf16[784,128]{1,0:T(8,128)(2,1)S(1)} %get-tuple-element.34.refs_0_, bf16[784,128]{1,0:T(8,128)(2,1)S(1)} %collective-permute-done.refs_1_, ...), custom_call_target="tpu_custom_call" | custom-call | flops 4000000000 | bytes 1196032 | tf_op jit(solution)/shard_map/pallas_call | solution.py:288
  15.5 2.7 %collective-permute-start.9 = (bf16[384,128]{1,0:T(8,128)(2,1)S(1)}, bf16[384,128]{1,0:T(8,128)(2,1)S(1)}, u32[]{:S(2)}, u32[]{:S(2)}) collective-permute-start(bf16[384,128]{1,0:T(8,128)(2,1)S(1)} %get-tuple-element.54), channel_id=1, source_target_pairs={{0,8},{1,9},{2,10},{3,11},{4,12},{5,13},{6,14},{7,15},{8,0},{9,1},... | collective-permute-start | bytes 294920 | tf_op jit(solution)/shard_map/ppermute | solution.py:313
  18.2 1.4 %collective-permute-start.10 = (bf16[384,128]{1,0:T(8,128)(2,1)S(1)}, bf16[384,128]{1,0:T(8,128)(2,1)S(1)}, u32[]{:S(2)}, u32[]{:S(2)}) collective-permute-start(bf16[384,128]{1,0:T(8,128)(2,1)S(1)} %get-tuple-element.55), channel_id=1, source_target_pairs={{0,12},{1,13},{2,14},{3,15},{4,8},{5,9},{6,10},{7,11},{8,4},{9,5},... | collective-permute-start | bytes 294920 | tf_op jit(solution)/shard_map/ppermute | solution.py:313
  19.6 0.4 %shard_map.94 = (bf16[272,128]{1,0:T(8,128)(2,1)S(1)}, bf16[272,128]{1,0:T(8,128)(2,1)S(1)}, bf16[272,128]{1,0:T(8,128)(2,1)S(1)}, bf16[272,128]{1,0:T(8,128)(2,1)S(1)}) custom-call(bf16[320,128]{1,0:T(8,128)(2,1)S(1)} %get-tuple-element.39.refs_0_, bf16[320,128]{1,0:T(8,128)(2,1)S(1)} %collective-permute-done.3.refs_1_, ...), custom_call_target="tpu_custom_call" | custom-call | flops 131072 | bytes 606208 | tf_op jit(solution)/shard_map/pallas_call | solution.py:288
  20.0 0.5 %collective-permute-start.6 = (bf16[272,128]{1,0:T(8,128)(2,1)S(1)}, bf16[272,128]{1,0:T(8,128)(2,1)S(1)}, u32[]{:S(2)}, u32[]{:S(2)}) collective-permute-start(bf16[272,128]{1,0:T(8,128)(2,1)S(1)} %get-tuple-element.43), channel_id=1, source_target_pairs={{0,1},{1,0},{2,3},{3,2},{4,5},{5,4},{6,7},{7,6},{8,9},{9,8},{10,11... | collective-permute-start | bytes 208904 | tf_op jit(solution)/shard_map/ppermute | solution.py:313
  20.5 1.5 %collective-permute-start.7 = (bf16[272,128]{1,0:T(8,128)(2,1)S(1)}, bf16[272,128]{1,0:T(8,128)(2,1)S(1)}, u32[]{:S(2)}, u32[]{:S(2)}) collective-permute-start(bf16[272,128]{1,0:T(8,128)(2,1)S(1)} %get-tuple-element.51), channel_id=1, source_target_pairs={{0,2},{1,3},{2,0},{3,1},{4,6},{5,7},{6,4},{7,5},{8,10},{9,11},{10,... | collective-permute-start | bytes 208904 | tf_op jit(solution)/shard_map/ppermute | solution.py:313
  22.0 0.4 %collective-permute-start.11 = (bf16[384,128]{1,0:T(8,128)(2,1)S(1)}, bf16[384,128]{1,0:T(8,128)(2,1)S(1)}, u32[]{:S(2)}, u32[]{:S(2)}) collective-permute-start(bf16[384,128]{1,0:T(8,128)(2,1)S(1)} %get-tuple-element.56), channel_id=1, source_target_pairs={{0,4},{1,5},{2,6},{3,7},{4,0},{5,1},{6,2},{7,3},{8,12},{9,13},{10,... | collective-permute-start | bytes 294920 | tf_op jit(solution)/shard_map/ppermute | solution.py:313
  22.4 0.8 %shard_map.95 = (f32[65,1024]{1,0:T(8,128)S(1)}, bf16[128,1536]{1,0:T(8,128)(2,1)S(1)}, bf16[64,512]{1,0:T(8,128)(2,1)S(1)}, bf16[4,128,256]{2,1,0:T(8,128)(2,1)S(1)}) custom-call(bf16[65,1024]{1,0:T(8,128)(2,1)S(1)} %copy-done.1, bf16[8,8,128,128]{3,2,1,0:T(8,128)(2,1)S(1)} %copy-done, bf16[1,12,64,64]{3,2,1,0:T(8,128)(2,1)S(1)} %copy-done.5, ...), custom_call_target="tpu_custom_call" | custom-call | flops 136314880 | bytes 3512320 | tf_op jit(solution)/shard_map/pallas_call | solution.py:288
  23.2 1.6 %collective-permute-done.7.refs_2_.refs_4_ = bf16[272,128]{1,0:T(8,128)(2,1)S(1)} collective-permute-done((bf16[272,128]{1,0:T(8,128)(2,1)S(1)}, bf16[272,128]{1,0:T(8,128)(2,1)S(1)}, u32[]{:S(2)}, u32[]{:S(2)}) %collective-permute-start.7) | collective-permute-done | bytes 69664 | tf_op jit(solution)/shard_map/ppermute | solution.py:313
  24.8 1.6 %collective-permute-done.8.refs_3_.refs_5_ = bf16[272,128]{1,0:T(8,128)(2,1)S(1)} collective-permute-done((bf16[272,128]{1,0:T(8,128)(2,1)S(1)}, bf16[272,128]{1,0:T(8,128)(2,1)S(1)}, u32[]{:S(2)}, u32[]{:S(2)}) %collective-permute-start.8) | collective-permute-done | bytes 69664 | tf_op jit(solution)/shard_map/ppermute | solution.py:313
  26.4 1.2 %shard_map.96.base_ref = f32[65,1024]{1,0:T(8,128)S(1)} custom-call(s32[1,12]{1,0:T(1,128)S(1)} %copy-done.7, f32[65,1024]{1,0:T(8,128)S(1)} %get-tuple-element.45.base_ref, bf16[128,1536]{1,0:T(8,128)(2,1)S(1)} %get-tuple-element.46.pairs_ref, bf16[64,512]{1,0:T(8,128)(2,1)S(1)} %get-tuple-element.47.across_ref, ...), custom_call_target="tpu_custom_call" | custom-call | flops 68157440 | bytes 1531952 | tf_op jit(solution)/shard_map/pallas_call | solution.py:288
  27.7 0.6 %collective-permute-done.11.refs_1_ = bf16[384,128]{1,0:T(8,128)(2,1)S(1)} collective-permute-done((bf16[384,128]{1,0:T(8,128)(2,1)S(1)}, bf16[384,128]{1,0:T(8,128)(2,1)S(1)}, u32[]{:S(2)}, u32[]{:S(2)}) %collective-permute-start.11) | collective-permute-done | bytes 98336 | tf_op jit(solution)/shard_map/ppermute | solution.py:313
  28.3 0.8 %shard_map.98 = f32[65,1024]{1,0:T(8,128)} custom-call(f32[65,1024]{1,0:T(8,128)S(1)} %shard_map.96.base_ref, f32[384,128]{1,0:T(8,128)S(1)} %shard_map.97.refs_0_, bf16[384,128]{1,0:T(8,128)(2,1)S(1)} %collective-permute-done.11.refs_1_, bf16[272,128]{1,0:T(8,128)(2,1)S(1)} %get-tuple-element.49.refs_0_.refs_2_, ...), custom_call_target="tpu_custom_call" | custom-call | flops 133120 | bytes 1105920 | tf_op jit(solution)/shard_map/pallas_call | solution.py:288
  (24 shorter events, 0.1 us)
Async XLA Ops:
  3.1 9.4 %collective-permute-start = (bf16[784,128]{1,0:T(8,128)(2,1)}, bf16[784,128]{1,0:T(8,128)(2,1)S(1)}, u32[]{:S(2)}, u32[]{:S(2)}) collective-permute-start(bf16[784,128]{1,0:T(8,128)(2,1)} %get-tuple-element.35), channel_id=1, source_target_pairs={{0,2},{1,3},{2,0},{3,1},{4,6},{5,7},{6,4},{7,5},{8,10},{9,11},{10,... | collective-permute-start | bytes 602120 | tf_op jit(solution)/shard_map/ppermute | solution.py:313
  6.1 8.9 %collective-permute-start.1 = (bf16[784,128]{1,0:T(8,128)(2,1)}, bf16[784,128]{1,0:T(8,128)(2,1)S(1)}, u32[]{:S(2)}, u32[]{:S(2)}) collective-permute-start(bf16[784,128]{1,0:T(8,128)(2,1)} %get-tuple-element.36), channel_id=1, source_target_pairs={{0,3},{1,2},{2,1},{3,0},{4,7},{5,6},{6,5},{7,4},{8,11},{9,10},{10,... | collective-permute-start | bytes 602120 | tf_op jit(solution)/shard_map/ppermute | solution.py:313
  6.1 8.9 %collective-permute-start.2 = (bf16[784,128]{1,0:T(8,128)(2,1)}, bf16[784,128]{1,0:T(8,128)(2,1)S(1)}, u32[]{:S(2)}, u32[]{:S(2)}) collective-permute-start(bf16[784,128]{1,0:T(8,128)(2,1)} %get-tuple-element.37), channel_id=1, source_target_pairs={{0,1},{1,0},{2,3},{3,2},{4,5},{5,4},{6,7},{7,6},{8,9},{9,8},{10,11... | collective-permute-start | bytes 602120 | tf_op jit(solution)/shard_map/ppermute | solution.py:313
  6.3 13.2 %collective-permute-start.3 = (bf16[320,128]{1,0:T(8,128)(2,1)}, bf16[320,128]{1,0:T(8,128)(2,1)S(1)}, u32[]{:S(2)}, u32[]{:S(2)}) collective-permute-start(bf16[320,128]{1,0:T(8,128)(2,1)} %get-tuple-element.40), channel_id=1, source_target_pairs={{0,8},{1,9},{2,10},{3,11},{4,12},{5,13},{6,14},{7,15},{8,0},{9,1},... | collective-permute-start | bytes 245768 | tf_op jit(solution)/shard_map/ppermute | solution.py:313
  9.3 10.2 %collective-permute-start.4 = (bf16[320,128]{1,0:T(8,128)(2,1)}, bf16[320,128]{1,0:T(8,128)(2,1)S(1)}, u32[]{:S(2)}, u32[]{:S(2)}) collective-permute-start(bf16[320,128]{1,0:T(8,128)(2,1)} %get-tuple-element.41), channel_id=1, source_target_pairs={{0,12},{1,13},{2,14},{3,15},{4,8},{5,9},{6,10},{7,11},{8,4},{9,5},... | collective-permute-start | bytes 245768 | tf_op jit(solution)/shard_map/ppermute | solution.py:313
  10.7 0.9 %copy-start.4 = (bf16[784,128]{1,0:T(8,128)(2,1)S(1)}, bf16[784,128]{1,0:T(8,128)(2,1)}, u32[]{:S(2)}) copy-start(bf16[784,128]{1,0:T(8,128)(2,1)} %get-tuple-element.31.refs_0_) | copy-start | bytes 602116
  11.6 0.9 %copy-start.6 = (bf16[320,128]{1,0:T(8,128)(2,1)S(1)}, bf16[320,128]{1,0:T(8,128)(2,1)}, u32[]{:S(2)}) copy-start(bf16[320,128]{1,0:T(8,128)(2,1)} %get-tuple-element.32.refs_1_) | copy-start | bytes 245764
  12.5 7.0 %collective-permute-start.5 = (bf16[320,128]{1,0:T(8,128)(2,1)}, bf16[320,128]{1,0:T(8,128)(2,1)S(1)}, u32[]{:S(2)}, u32[]{:S(2)}) collective-permute-start(bf16[320,128]{1,0:T(8,128)(2,1)} %get-tuple-element.42), channel_id=1, source_target_pairs={{0,4},{1,5},{2,6},{3,7},{4,0},{5,1},{6,2},{7,3},{8,12},{9,13},{10,... | collective-permute-start | bytes 245768 | tf_op jit(solution)/shard_map/ppermute | solution.py:313
  15.0 7.4 %copy-start = (bf16[8,8,128,128]{3,2,1,0:T(8,128)(2,1)S(1)}, bf16[8,8,128,128]{3,2,1,0:T(8,128)(2,1)}, u32[]{:S(2)}) copy-start(bf16[8,8,128,128]{3,2,1,0:T(8,128)(2,1)} %local_ref.1) | copy-start | bytes 6291460
  15.0 7.4 %copy-start.1 = (bf16[65,1024]{1,0:T(8,128)(2,1)S(1)}, bf16[65,1024]{1,0:T(8,128)(2,1)}, u32[]{:S(2)}) copy-start(bf16[65,1024]{1,0:T(8,128)(2,1)} %probes_ref) | copy-start | bytes 399364
  15.0 7.4 %copy-start.2 = (bf16[8,64,64]{2,1,0:T(8,128)(2,1)S(1)}, bf16[8,64,64]{2,1,0:T(8,128)(2,1)}, u32[]{:S(2)}) copy-start(bf16[8,64,64]{2,1,0:T(8,128)(2,1)} %transfer_ref.1) | copy-start | bytes 196612
  15.0 7.4 %copy-start.3 = (bf16[8,64,128]{2,1,0:T(8,128)(2,1)S(1)}, bf16[8,64,128]{2,1,0:T(8,128)(2,1)}, u32[]{:S(2)}) copy-start(bf16[8,64,128]{2,1,0:T(8,128)(2,1)} %basis_ref.1) | copy-start | bytes 393220
  15.0 7.4 %copy-start.5 = (bf16[1,12,64,64]{3,2,1,0:T(8,128)(2,1)S(1)}, bf16[1,12,64,64]{3,2,1,0:T(8,128)(2,1)}, u32[]{:S(2)}) copy-start(bf16[1,12,64,64]{3,2,1,0:T(8,128)(2,1)} %couplings_ref.1) | copy-start | bytes 294916
  15.5 10.9 %copy-start.7 = (s32[1,12]{1,0:T(1,128)S(1)}, s32[1,12]{1,0:T(1,128)}, u32[]{:S(2)}) copy-start(s32[1,12]{1,0:T(1,128)} %partner_ref.1) | copy-start | bytes 148
  15.5 12.1 %collective-permute-start.9 = (bf16[384,128]{1,0:T(8,128)(2,1)S(1)}, bf16[384,128]{1,0:T(8,128)(2,1)S(1)}, u32[]{:S(2)}, u32[]{:S(2)}) collective-permute-start(bf16[384,128]{1,0:T(8,128)(2,1)S(1)} %get-tuple-element.54), channel_id=1, source_target_pairs={{0,8},{1,9},{2,10},{3,11},{4,12},{5,13},{6,14},{7,15},{8,0},{9,1},... | collective-permute-start | bytes 294920 | tf_op jit(solution)/shard_map/ppermute | solution.py:313
  18.2 9.4 %collective-permute-start.10 = (bf16[384,128]{1,0:T(8,128)(2,1)S(1)}, bf16[384,128]{1,0:T(8,128)(2,1)S(1)}, u32[]{:S(2)}, u32[]{:S(2)}) collective-permute-start(bf16[384,128]{1,0:T(8,128)(2,1)S(1)} %get-tuple-element.55), channel_id=1, source_target_pairs={{0,12},{1,13},{2,14},{3,15},{4,8},{5,9},{6,10},{7,11},{8,4},{9,5},... | collective-permute-start | bytes 294920 | tf_op jit(solution)/shard_map/ppermute | solution.py:313
  20.0 2.0 %collective-permute-start.6 = (bf16[272,128]{1,0:T(8,128)(2,1)S(1)}, bf16[272,128]{1,0:T(8,128)(2,1)S(1)}, u32[]{:S(2)}, u32[]{:S(2)}) collective-permute-start(bf16[272,128]{1,0:T(8,128)(2,1)S(1)} %get-tuple-element.43), channel_id=1, source_target_pairs={{0,1},{1,0},{2,3},{3,2},{4,5},{5,4},{6,7},{7,6},{8,9},{9,8},{10,11... | collective-permute-start | bytes 208904 | tf_op jit(solution)/shard_map/ppermute | solution.py:313
  20.5 4.3 %collective-permute-start.7 = (bf16[272,128]{1,0:T(8,128)(2,1)S(1)}, bf16[272,128]{1,0:T(8,128)(2,1)S(1)}, u32[]{:S(2)}, u32[]{:S(2)}) collective-permute-start(bf16[272,128]{1,0:T(8,128)(2,1)S(1)} %get-tuple-element.51), channel_id=1, source_target_pairs={{0,2},{1,3},{2,0},{3,1},{4,6},{5,7},{6,4},{7,5},{8,10},{9,11},{10,... | collective-permute-start | bytes 208904 | tf_op jit(solution)/shard_map/ppermute | solution.py:313
  22.0 4.4 %collective-permute-start.8 = (bf16[272,128]{1,0:T(8,128)(2,1)S(1)}, bf16[272,128]{1,0:T(8,128)(2,1)S(1)}, u32[]{:S(2)}, u32[]{:S(2)}) collective-permute-start(bf16[272,128]{1,0:T(8,128)(2,1)S(1)} %get-tuple-element.52), channel_id=1, source_target_pairs={{0,3},{1,2},{2,1},{3,0},{4,7},{5,6},{6,5},{7,4},{8,11},{9,10},{10,... | collective-permute-start | bytes 208904 | tf_op jit(solution)/shard_map/ppermute | solution.py:313
  22.0 6.3 %collective-permute-start.11 = (bf16[384,128]{1,0:T(8,128)(2,1)S(1)}, bf16[384,128]{1,0:T(8,128)(2,1)S(1)}, u32[]{:S(2)}, u32[]{:S(2)}) collective-permute-start(bf16[384,128]{1,0:T(8,128)(2,1)S(1)} %get-tuple-element.56), channel_id=1, source_target_pairs={{0,4},{1,5},{2,6},{3,7},{4,0},{5,1},{6,2},{7,3},{8,12},{9,13},{10,... | collective-permute-start | bytes 294920 | tf_op jit(solution)/shard_map/ppermute | solution.py:313

commit v29 on v28

--- a/solution.py
+++ b/solution.py
@@ -405,7 +405,7 @@
         across_kernel,
         jax.ShapeDtypeStruct((by_low.dense_depth, size), F32),
         ([VMEM] * (high - 1), VMEM),
-        [to_high[k] for k in planes[:-1]],
+        [to_high[k] for k in (0, *range(2, high - 1), 1)],
         [],
         HEAVY,
         0,
@@ -414,7 +414,7 @@
         functools.partial(last_kernel, routes, devices),
         base_shape,
         ([VMEM] * (3 + low), VMEM),
-        (base, across, to_high[1], *to_low),
+        (base, across, to_high[high - 1], *to_low),
         [],
         devices * columns * size,
         0,

time: 29.2 us -> 30.2 us (1.034)
  starting transfers between devices: 15.7 us -> 16.7 us
    ppermute x12, starting transfers between devices: 15.7 us -> 16.7 us  [per_device(): lax.ppermute(x, 'leaf', [(i, i ^ way) for i in range(devices)])]
where the time goes in v29:
time: 30.2 us; the launch traced here: 30 us
  starting transfers between devices  16.7 us (55%)
  Pallas kernels  6.81 us (23%)
  waiting for transfers between devices  4.59 us (15%)
  local copies, waits for them, and re-layouts  1.84 us (6%)
    ppermute x12, starting transfers between devices, per_device(): lax.ppermute(x, 'leaf', [(i, i ^ way) for i in range(devices)])  16.7 us
    pallas_call x8, Pallas kernels, call(): pl.pallas_call(kernel, out_shape=out_shape, in_specs=specs[0], out_specs=...  6.81 us
    ppermute x12, waiting for transfers between devices, per_device(): lax.ppermute(x, 'leaf', [(i, i ^ way) for i in range(devices)])  4.59 us
    unnamed x16, local copies, waits for them, and re-layouts  1.84 us
  transfers between devices with their start and end apart: 12, of which 4 were waited for; matrix products, arithmetic and copies ran while one was open for 0% of the time, Pallas kernels for 10%

profile of v29, /device:TPU:0, one launch (start us, length us, event | category | flops | bytes accessed | tf_op | source)
XLA Modules:
  0.0 30.0 jit_solution(3246078597395252827)
XLA Ops:
  0.0 3.1 %shard_map.91 = (bf16[784,128]{1,0:T(8,128)(2,1)}, bf16[784,128]{1,0:T(8,128)(2,1)}, bf16[784,128]{1,0:T(8,128)(2,1)}, bf16[784,128]{1,0:T(8,128)(2,1)}, bf16[32...) custom-call(s32[4,8]{1,0:T(4,128)} %bitcast.2, ...), custom_call_target="tpu_custom_call" | custom-call | flops 68157440 | bytes 2509056 | tf_op jit(solution)/shard_map/pallas_call | solution.py:288
  3.1 3.0 %collective-permute-start = (bf16[784,128]{1,0:T(8,128)(2,1)}, bf16[784,128]{1,0:T(8,128)(2,1)S(1)}, u32[]{:S(2)}, u32[]{:S(2)}) collective-permute-start(bf16[784,128]{1,0:T(8,128)(2,1)} %get-tuple-element.35), channel_id=1, source_target_pairs={{0,2},{1,3},{2,0},{3,1},{4,6},{5,7},{6,4},{7,5},{8,10},{9,11},{10,... | collective-permute-start | bytes 602120 | tf_op jit(solution)/shard_map/ppermute | solution.py:313
  6.1 0.2 collective-permute-start.2
  6.3 3.0 %collective-permute-start.3 = (bf16[320,128]{1,0:T(8,128)(2,1)}, bf16[320,128]{1,0:T(8,128)(2,1)S(1)}, u32[]{:S(2)}, u32[]{:S(2)}) collective-permute-start(bf16[320,128]{1,0:T(8,128)(2,1)} %get-tuple-element.40), channel_id=1, source_target_pairs={{0,8},{1,9},{2,10},{3,11},{4,12},{5,13},{6,14},{7,15},{8,0},{9,1},... | collective-permute-start | bytes 245768 | tf_op jit(solution)/shard_map/ppermute | solution.py:313
  9.3 1.3 %collective-permute-start.4 = (bf16[320,128]{1,0:T(8,128)(2,1)}, bf16[320,128]{1,0:T(8,128)(2,1)S(1)}, u32[]{:S(2)}, u32[]{:S(2)}) collective-permute-start(bf16[320,128]{1,0:T(8,128)(2,1)} %get-tuple-element.41), channel_id=1, source_target_pairs={{0,12},{1,13},{2,14},{3,15},{4,8},{5,9},{6,10},{7,11},{8,4},{9,5},... | collective-permute-start | bytes 245768 | tf_op jit(solution)/shard_map/ppermute | solution.py:313
  10.7 0.9 %copy-done.4 = bf16[784,128]{1,0:T(8,128)(2,1)S(1)} copy-done((bf16[784,128]{1,0:T(8,128)(2,1)S(1)}, bf16[784,128]{1,0:T(8,128)(2,1)}, u32[]{:S(2)}) %copy-start.4) | copy-done | bytes 200728
  11.6 0.9 %copy-done.6 = bf16[320,128]{1,0:T(8,128)(2,1)S(1)} copy-done((bf16[320,128]{1,0:T(8,128)(2,1)S(1)}, bf16[320,128]{1,0:T(8,128)(2,1)}, u32[]{:S(2)}) %copy-start.6) | copy-done | bytes 81944
  12.5 1.7 %collective-permute-start.5 = (bf16[320,128]{1,0:T(8,128)(2,1)}, bf16[320,128]{1,0:T(8,128)(2,1)S(1)}, u32[]{:S(2)}, u32[]{:S(2)}) collective-permute-start(bf16[320,128]{1,0:T(8,128)(2,1)} %get-tuple-element.42), channel_id=1, source_target_pairs={{0,4},{1,5},{2,6},{3,7},{4,0},{5,1},{6,2},{7,3},{8,12},{9,13},{10,... | collective-permute-start | bytes 245768 | tf_op jit(solution)/shard_map/ppermute | solution.py:313
  14.2 0.7 %collective-permute-done.1.refs_2_ = bf16[784,128]{1,0:T(8,128)(2,1)S(1)} collective-permute-done((bf16[784,128]{1,0:T(8,128)(2,1)}, bf16[784,128]{1,0:T(8,128)(2,1)S(1)}, u32[]{:S(2)}, u32[]{:S(2)}) %collective-permute-start.1) | collective-permute-done | bytes 200736 | tf_op jit(solution)/shard_map/ppermute | solution.py:313
  15.0 0.5 %shard_map.93 = (bf16[384,128]{1,0:T(8,128)(2,1)S(1)}, bf16[384,128]{1,0:T(8,128)(2,1)S(1)}, bf16[384,128]{1,0:T(8,128)(2,1)S(1)}, bf16[384,128]{1,0:T(8,128)(2,1)S(1)}) custom-call(bf16[784,128]{1,0:T(8,128)(2,1)S(1)} %get-tuple-element.34.refs_0_, bf16[784,128]{1,0:T(8,128)(2,1)S(1)} %collective-permute-done.refs_1_, ...), custom_call_target="tpu_custom_call" | custom-call | flops 4000000000 | bytes 1196032 | tf_op jit(solution)/shard_map/pallas_call | solution.py:288
  15.5 0.0 copy-start.7
  15.5 2.6 %collective-permute-start.9 = (bf16[384,128]{1,0:T(8,128)(2,1)S(1)}, bf16[384,128]{1,0:T(8,128)(2,1)S(1)}, u32[]{:S(2)}, u32[]{:S(2)}) collective-permute-start(bf16[384,128]{1,0:T(8,128)(2,1)S(1)} %get-tuple-element.54), channel_id=1, source_target_pairs={{0,8},{1,9},{2,10},{3,11},{4,12},{5,13},{6,14},{7,15},{8,0},{9,1},... | collective-permute-start | bytes 294920 | tf_op jit(solution)/shard_map/ppermute | solution.py:313
  18.2 1.6 %collective-permute-start.10 = (bf16[384,128]{1,0:T(8,128)(2,1)S(1)}, bf16[384,128]{1,0:T(8,128)(2,1)S(1)}, u32[]{:S(2)}, u32[]{:S(2)}) collective-permute-start(bf16[384,128]{1,0:T(8,128)(2,1)S(1)} %get-tuple-element.55), channel_id=1, source_target_pairs={{0,4},{1,5},{2,6},{3,7},{4,0},{5,1},{6,2},{7,3},{8,12},{9,13},{10,... | collective-permute-start | bytes 294920 | tf_op jit(solution)/shard_map/ppermute | solution.py:313
  19.8 0.4 %shard_map.94 = (bf16[272,128]{1,0:T(8,128)(2,1)S(1)}, bf16[272,128]{1,0:T(8,128)(2,1)S(1)}, bf16[272,128]{1,0:T(8,128)(2,1)S(1)}, bf16[272,128]{1,0:T(8,128)(2,1)S(1)}) custom-call(bf16[320,128]{1,0:T(8,128)(2,1)S(1)} %get-tuple-element.39.refs_0_, bf16[320,128]{1,0:T(8,128)(2,1)S(1)} %collective-permute-done.3.refs_1_, ...), custom_call_target="tpu_custom_call" | custom-call | flops 131072 | bytes 606208 | tf_op jit(solution)/shard_map/pallas_call | solution.py:288
  20.2 0.3 %collective-permute-start.6 = (bf16[272,128]{1,0:T(8,128)(2,1)S(1)}, bf16[272,128]{1,0:T(8,128)(2,1)S(1)}, u32[]{:S(2)}, u32[]{:S(2)}) collective-permute-start(bf16[272,128]{1,0:T(8,128)(2,1)S(1)} %get-tuple-element.43), channel_id=1, source_target_pairs={{0,1},{1,0},{2,3},{3,2},{4,5},{5,4},{6,7},{7,6},{8,9},{9,8},{10,11... | collective-permute-start | bytes 208904 | tf_op jit(solution)/shard_map/ppermute | solution.py:313
  20.5 1.5 %collective-permute-start.7 = (bf16[272,128]{1,0:T(8,128)(2,1)S(1)}, bf16[272,128]{1,0:T(8,128)(2,1)S(1)}, u32[]{:S(2)}, u32[]{:S(2)}) collective-permute-start(bf16[272,128]{1,0:T(8,128)(2,1)S(1)} %get-tuple-element.51), channel_id=1, source_target_pairs={{0,2},{1,3},{2,0},{3,1},{4,6},{5,7},{6,4},{7,5},{8,10},{9,11},{10,... | collective-permute-start | bytes 208904 | tf_op jit(solution)/shard_map/ppermute | solution.py:313
  22.1 0.1 collective-permute-start.8
  22.1 1.2 %collective-permute-start.11 = (bf16[384,128]{1,0:T(8,128)(2,1)S(1)}, bf16[384,128]{1,0:T(8,128)(2,1)S(1)}, u32[]{:S(2)}, u32[]{:S(2)}) collective-permute-start(bf16[384,128]{1,0:T(8,128)(2,1)S(1)} %get-tuple-element.56), channel_id=1, source_target_pairs={{0,12},{1,13},{2,14},{3,15},{4,8},{5,9},{6,10},{7,11},{8,4},{9,5},... | collective-permute-start | bytes 294920 | tf_op jit(solution)/shard_map/ppermute | solution.py:313
  23.4 0.8 %shard_map.95 = (f32[65,1024]{1,0:T(8,128)S(1)}, bf16[128,1536]{1,0:T(8,128)(2,1)S(1)}, bf16[64,512]{1,0:T(8,128)(2,1)S(1)}, bf16[4,128,256]{2,1,0:T(8,128)(2,1)S(1)}) custom-call(bf16[65,1024]{1,0:T(8,128)(2,1)S(1)} %copy-done.1, bf16[8,8,128,128]{3,2,1,0:T(8,128)(2,1)S(1)} %copy-done, bf16[1,12,64,64]{3,2,1,0:T(8,128)(2,1)S(1)} %copy-done.5, ...), custom_call_target="tpu_custom_call" | custom-call | flops 136314880 | bytes 3512320 | tf_op jit(solution)/shard_map/pallas_call | solution.py:288
  24.1 0.7 %collective-permute-done.7.refs_2_.refs_4_ = bf16[272,128]{1,0:T(8,128)(2,1)S(1)} collective-permute-done((bf16[272,128]{1,0:T(8,128)(2,1)S(1)}, bf16[272,128]{1,0:T(8,128)(2,1)S(1)}, u32[]{:S(2)}, u32[]{:S(2)}) %collective-permute-start.7) | collective-permute-done | bytes 69664 | tf_op jit(solution)/shard_map/ppermute | solution.py:313
  24.9 1.7 %collective-permute-done.8.refs_3_.refs_5_ = bf16[272,128]{1,0:T(8,128)(2,1)S(1)} collective-permute-done((bf16[272,128]{1,0:T(8,128)(2,1)S(1)}, bf16[272,128]{1,0:T(8,128)(2,1)S(1)}, u32[]{:S(2)}, u32[]{:S(2)}) %collective-permute-start.8) | collective-permute-done | bytes 69664 | tf_op jit(solution)/shard_map/ppermute | solution.py:313
  26.5 1.2 %shard_map.96.base_ref = f32[65,1024]{1,0:T(8,128)S(1)} custom-call(s32[1,12]{1,0:T(1,128)S(1)} %copy-done.7, f32[65,1024]{1,0:T(8,128)S(1)} %get-tuple-element.45.base_ref, bf16[128,1536]{1,0:T(8,128)(2,1)S(1)} %get-tuple-element.46.pairs_ref, bf16[64,512]{1,0:T(8,128)(2,1)S(1)} %get-tuple-element.47.across_ref, ...), custom_call_target="tpu_custom_call" | custom-call | flops 68157440 | bytes 1531952 | tf_op jit(solution)/shard_map/pallas_call | solution.py:288
  27.8 1.4 %collective-permute-done.11.refs_1_ = bf16[384,128]{1,0:T(8,128)(2,1)S(1)} collective-permute-done((bf16[384,128]{1,0:T(8,128)(2,1)S(1)}, bf16[384,128]{1,0:T(8,128)(2,1)S(1)}, u32[]{:S(2)}, u32[]{:S(2)}) %collective-permute-start.11) | collective-permute-done | bytes 98336 | tf_op jit(solution)/shard_map/ppermute | solution.py:313
  29.3 0.8 %shard_map.98 = f32[65,1024]{1,0:T(8,128)} custom-call(f32[65,1024]{1,0:T(8,128)S(1)} %shard_map.96.base_ref, f32[384,128]{1,0:T(8,128)S(1)} %shard_map.97.refs_0_, bf16[384,128]{1,0:T(8,128)(2,1)S(1)} %collective-permute-done.11.refs_1_, bf16[272,128]{1,0:T(8,128)(2,1)S(1)} %get-tuple-element.49.refs_0_.refs_2_, ...), custom_call_target="tpu_custom_call" | custom-call | flops 133120 | bytes 1105920 | tf_op jit(solution)/shard_map/pallas_call | solution.py:288
  (24 shorter events, 0.1 us)
Async XLA Ops:
  3.1 9.4 %collective-permute-start = (bf16[784,128]{1,0:T(8,128)(2,1)}, bf16[784,128]{1,0:T(8,128)(2,1)S(1)}, u32[]{:S(2)}, u32[]{:S(2)}) collective-permute-start(bf16[784,128]{1,0:T(8,128)(2,1)} %get-tuple-element.35), channel_id=1, source_target_pairs={{0,2},{1,3},{2,0},{3,1},{4,6},{5,7},{6,4},{7,5},{8,10},{9,11},{10,... | collective-permute-start | bytes 602120 | tf_op jit(solution)/shard_map/ppermute | solution.py:313
  6.1 8.9 %collective-permute-start.1 = (bf16[784,128]{1,0:T(8,128)(2,1)}, bf16[784,128]{1,0:T(8,128)(2,1)S(1)}, u32[]{:S(2)}, u32[]{:S(2)}) collective-permute-start(bf16[784,128]{1,0:T(8,128)(2,1)} %get-tuple-element.36), channel_id=1, source_target_pairs={{0,3},{1,2},{2,1},{3,0},{4,7},{5,6},{6,5},{7,4},{8,11},{9,10},{10,... | collective-permute-start | bytes 602120 | tf_op jit(solution)/shard_map/ppermute | solution.py:313
  6.1 8.9 %collective-permute-start.2 = (bf16[784,128]{1,0:T(8,128)(2,1)}, bf16[784,128]{1,0:T(8,128)(2,1)S(1)}, u32[]{:S(2)}, u32[]{:S(2)}) collective-permute-start(bf16[784,128]{1,0:T(8,128)(2,1)} %get-tuple-element.37), channel_id=1, source_target_pairs={{0,1},{1,0},{2,3},{3,2},{4,5},{5,4},{6,7},{7,6},{8,9},{9,8},{10,11... | collective-permute-start | bytes 602120 | tf_op jit(solution)/shard_map/ppermute | solution.py:313
  6.3 13.5 %collective-permute-start.3 = (bf16[320,128]{1,0:T(8,128)(2,1)}, bf16[320,128]{1,0:T(8,128)(2,1)S(1)}, u32[]{:S(2)}, u32[]{:S(2)}) collective-permute-start(bf16[320,128]{1,0:T(8,128)(2,1)} %get-tuple-element.40), channel_id=1, source_target_pairs={{0,8},{1,9},{2,10},{3,11},{4,12},{5,13},{6,14},{7,15},{8,0},{9,1},... | collective-permute-start | bytes 245768 | tf_op jit(solution)/shard_map/ppermute | solution.py:313
  9.3 10.5 %collective-permute-start.4 = (bf16[320,128]{1,0:T(8,128)(2,1)}, bf16[320,128]{1,0:T(8,128)(2,1)S(1)}, u32[]{:S(2)}, u32[]{:S(2)}) collective-permute-start(bf16[320,128]{1,0:T(8,128)(2,1)} %get-tuple-element.41), channel_id=1, source_target_pairs={{0,12},{1,13},{2,14},{3,15},{4,8},{5,9},{6,10},{7,11},{8,4},{9,5},... | collective-permute-start | bytes 245768 | tf_op jit(solution)/shard_map/ppermute | solution.py:313
  10.7 0.9 %copy-start.4 = (bf16[784,128]{1,0:T(8,128)(2,1)S(1)}, bf16[784,128]{1,0:T(8,128)(2,1)}, u32[]{:S(2)}) copy-start(bf16[784,128]{1,0:T(8,128)(2,1)} %get-tuple-element.31.refs_0_) | copy-start | bytes 602116
  11.6 0.9 %copy-start.6 = (bf16[320,128]{1,0:T(8,128)(2,1)S(1)}, bf16[320,128]{1,0:T(8,128)(2,1)}, u32[]{:S(2)}) copy-start(bf16[320,128]{1,0:T(8,128)(2,1)} %get-tuple-element.32.refs_1_) | copy-start | bytes 245764
  12.5 7.3 %collective-permute-start.5 = (bf16[320,128]{1,0:T(8,128)(2,1)}, bf16[320,128]{1,0:T(8,128)(2,1)S(1)}, u32[]{:S(2)}, u32[]{:S(2)}) collective-permute-start(bf16[320,128]{1,0:T(8,128)(2,1)} %get-tuple-element.42), channel_id=1, source_target_pairs={{0,4},{1,5},{2,6},{3,7},{4,0},{5,1},{6,2},{7,3},{8,12},{9,13},{10,... | collective-permute-start | bytes 245768 | tf_op jit(solution)/shard_map/ppermute | solution.py:313
  15.0 8.4 %copy-start = (bf16[8,8,128,128]{3,2,1,0:T(8,128)(2,1)S(1)}, bf16[8,8,128,128]{3,2,1,0:T(8,128)(2,1)}, u32[]{:S(2)}) copy-start(bf16[8,8,128,128]{3,2,1,0:T(8,128)(2,1)} %local_ref.1) | copy-start | bytes 6291460
  15.0 8.4 %copy-start.1 = (bf16[65,1024]{1,0:T(8,128)(2,1)S(1)}, bf16[65,1024]{1,0:T(8,128)(2,1)}, u32[]{:S(2)}) copy-start(bf16[65,1024]{1,0:T(8,128)(2,1)} %probes_ref) | copy-start | bytes 399364
  15.0 8.4 %copy-start.2 = (bf16[8,64,64]{2,1,0:T(8,128)(2,1)S(1)}, bf16[8,64,64]{2,1,0:T(8,128)(2,1)}, u32[]{:S(2)}) copy-start(bf16[8,64,64]{2,1,0:T(8,128)(2,1)} %transfer_ref.1) | copy-start | bytes 196612
  15.0 8.4 %copy-start.3 = (bf16[8,64,128]{2,1,0:T(8,128)(2,1)S(1)}, bf16[8,64,128]{2,1,0:T(8,128)(2,1)}, u32[]{:S(2)}) copy-start(bf16[8,64,128]{2,1,0:T(8,128)(2,1)} %basis_ref.1) | copy-start | bytes 393220
  15.0 8.4 %copy-start.5 = (bf16[1,12,64,64]{3,2,1,0:T(8,128)(2,1)S(1)}, bf16[1,12,64,64]{3,2,1,0:T(8,128)(2,1)}, u32[]{:S(2)}) copy-start(bf16[1,12,64,64]{3,2,1,0:T(8,128)(2,1)} %couplings_ref.1) | copy-start | bytes 294916
  15.5 11.0 %copy-start.7 = (s32[1,12]{1,0:T(1,128)S(1)}, s32[1,12]{1,0:T(1,128)}, u32[]{:S(2)}) copy-start(s32[1,12]{1,0:T(1,128)} %partner_ref.1) | copy-start | bytes 148
  15.5 12.2 %collective-permute-start.9 = (bf16[384,128]{1,0:T(8,128)(2,1)S(1)}, bf16[384,128]{1,0:T(8,128)(2,1)S(1)}, u32[]{:S(2)}, u32[]{:S(2)}) collective-permute-start(bf16[384,128]{1,0:T(8,128)(2,1)S(1)} %get-tuple-element.54), channel_id=1, source_target_pairs={{0,8},{1,9},{2,10},{3,11},{4,12},{5,13},{6,14},{7,15},{8,0},{9,1},... | collective-permute-start | bytes 294920 | tf_op jit(solution)/shard_map/ppermute | solution.py:313
  18.2 9.6 %collective-permute-start.10 = (bf16[384,128]{1,0:T(8,128)(2,1)S(1)}, bf16[384,128]{1,0:T(8,128)(2,1)S(1)}, u32[]{:S(2)}, u32[]{:S(2)}) collective-permute-start(bf16[384,128]{1,0:T(8,128)(2,1)S(1)} %get-tuple-element.55), channel_id=1, source_target_pairs={{0,4},{1,5},{2,6},{3,7},{4,0},{5,1},{6,2},{7,3},{8,12},{9,13},{10,... | collective-permute-start | bytes 294920 | tf_op jit(solution)/shard_map/ppermute | solution.py:313
  20.2 1.9 %collective-permute-start.6 = (bf16[272,128]{1,0:T(8,128)(2,1)S(1)}, bf16[272,128]{1,0:T(8,128)(2,1)S(1)}, u32[]{:S(2)}, u32[]{:S(2)}) collective-permute-start(bf16[272,128]{1,0:T(8,128)(2,1)S(1)} %get-tuple-element.43), channel_id=1, source_target_pairs={{0,1},{1,0},{2,3},{3,2},{4,5},{5,4},{6,7},{7,6},{8,9},{9,8},{10,11... | collective-permute-start | bytes 208904 | tf_op jit(solution)/shard_map/ppermute | solution.py:313
  20.5 4.3 %collective-permute-start.7 = (bf16[272,128]{1,0:T(8,128)(2,1)S(1)}, bf16[272,128]{1,0:T(8,128)(2,1)S(1)}, u32[]{:S(2)}, u32[]{:S(2)}) collective-permute-start(bf16[272,128]{1,0:T(8,128)(2,1)S(1)} %get-tuple-element.51), channel_id=1, source_target_pairs={{0,2},{1,3},{2,0},{3,1},{4,6},{5,7},{6,4},{7,5},{8,10},{9,11},{10,... | collective-permute-start | bytes 208904 | tf_op jit(solution)/shard_map/ppermute | solution.py:313
  22.1 4.5 %collective-permute-start.8 = (bf16[272,128]{1,0:T(8,128)(2,1)S(1)}, bf16[272,128]{1,0:T(8,128)(2,1)S(1)}, u32[]{:S(2)}, u32[]{:S(2)}) collective-permute-start(bf16[272,128]{1,0:T(8,128)(2,1)S(1)} %get-tuple-element.52), channel_id=1, source_target_pairs={{0,3},{1,2},{2,1},{3,0},{4,7},{5,6},{6,5},{7,4},{8,11},{9,10},{10,... | collective-permute-start | bytes 208904 | tf_op jit(solution)/shard_map/ppermute | solution.py:313
  22.1 7.1 %collective-permute-start.11 = (bf16[384,128]{1,0:T(8,128)(2,1)S(1)}, bf16[384,128]{1,0:T(8,128)(2,1)S(1)}, u32[]{:S(2)}, u32[]{:S(2)}) collective-permute-start(bf16[384,128]{1,0:T(8,128)(2,1)S(1)} %get-tuple-element.56), channel_id=1, source_target_pairs={{0,12},{1,13},{2,14},{3,15},{4,8},{5,9},{6,10},{7,11},{8,4},{9,5},... | collective-permute-start | bytes 294920 | tf_op jit(solution)/shard_map/ppermute | solution.py:313

commit v30 on v28

--- a/solution.py
+++ b/solution.py
@@ -405,7 +405,7 @@
         across_kernel,
         jax.ShapeDtypeStruct((by_low.dense_depth, size), F32),
         ([VMEM] * (high - 1), VMEM),
-        [to_high[k] for k in planes[:-1]],
+        [to_high[k] for k in (0, *range(high - 1, 1, -1))],
         [],
         HEAVY,
         0,

time: 29.2 us -> 30.2 us (1.034)
  waiting for transfers between devices: 4.55 us -> 5.52 us
    ppermute x12, waiting for transfers between devices: 4.55 us -> 5.52 us  [per_device(): lax.ppermute(x, 'leaf', [(i, i ^ way) for i in range(devices)])]
  transfers between devices with their start and end apart: 12 -> 12, of which waited for: 4 -> 5; matrix products, arithmetic and copies ran while one was open for 0% -> 0% of each run, Pallas kernels for 10% -> 10%
where the time goes in v30:
time: 30.2 us; the launch traced here: 30 us
  starting transfers between devices  15.8 us (52%)
  Pallas kernels  6.77 us (22%)
  waiting for transfers between devices  5.52 us (18%)
  local copies, waits for them, and re-layouts  1.84 us (6%)
    ppermute x12, starting transfers between devices, per_device(): lax.ppermute(x, 'leaf', [(i, i ^ way) for i in range(devices)])  15.8 us
    pallas_call x8, Pallas kernels, call(): pl.pallas_call(kernel, out_shape=out_shape, in_specs=specs[0], out_specs=...  6.77 us
    ppermute x12, waiting for transfers between devices, per_device(): lax.ppermute(x, 'leaf', [(i, i ^ way) for i in range(devices)])  5.52 us
    unnamed x16, local copies, waits for them, and re-layouts  1.84 us
  transfers between devices with their start and end apart: 12, of which 5 were waited for; matrix products, arithmetic and copies ran while one was open for 0% of the time, Pallas kernels for 10%

profile of v30, /device:TPU:0, one launch (start us, length us, event | category | flops | bytes accessed | tf_op | source)
XLA Modules:
  0.0 30.0 jit_solution(12773801083570977920)
XLA Ops:
  0.0 3.1 %shard_map.91 = (bf16[784,128]{1,0:T(8,128)(2,1)}, bf16[784,128]{1,0:T(8,128)(2,1)}, bf16[784,128]{1,0:T(8,128)(2,1)}, bf16[784,128]{1,0:T(8,128)(2,1)}, bf16[32...) custom-call(s32[4,8]{1,0:T(4,128)} %bitcast.2, ...), custom_call_target="tpu_custom_call" | custom-call | flops 68157440 | bytes 2509056 | tf_op jit(solution)/shard_map/pallas_call | solution.py:288
  3.1 3.0 %collective-permute-start = (bf16[784,128]{1,0:T(8,128)(2,1)}, bf16[784,128]{1,0:T(8,128)(2,1)S(1)}, u32[]{:S(2)}, u32[]{:S(2)}) collective-permute-start(bf16[784,128]{1,0:T(8,128)(2,1)} %get-tuple-element.35), channel_id=1, source_target_pairs={{0,2},{1,3},{2,0},{3,1},{4,6},{5,7},{6,4},{7,5},{8,10},{9,11},{10,... | collective-permute-start | bytes 602120 | tf_op jit(solution)/shard_map/ppermute | solution.py:313
  6.1 0.2 collective-permute-start.2
  6.3 3.0 %collective-permute-start.3 = (bf16[320,128]{1,0:T(8,128)(2,1)}, bf16[320,128]{1,0:T(8,128)(2,1)S(1)}, u32[]{:S(2)}, u32[]{:S(2)}) collective-permute-start(bf16[320,128]{1,0:T(8,128)(2,1)} %get-tuple-element.40), channel_id=1, source_target_pairs={{0,8},{1,9},{2,10},{3,11},{4,12},{5,13},{6,14},{7,15},{8,0},{9,1},... | collective-permute-start | bytes 245768 | tf_op jit(solution)/shard_map/ppermute | solution.py:313
  9.3 1.3 %collective-permute-start.4 = (bf16[320,128]{1,0:T(8,128)(2,1)}, bf16[320,128]{1,0:T(8,128)(2,1)S(1)}, u32[]{:S(2)}, u32[]{:S(2)}) collective-permute-start(bf16[320,128]{1,0:T(8,128)(2,1)} %get-tuple-element.41), channel_id=1, source_target_pairs={{0,12},{1,13},{2,14},{3,15},{4,8},{5,9},{6,10},{7,11},{8,4},{9,5},... | collective-permute-start | bytes 245768 | tf_op jit(solution)/shard_map/ppermute | solution.py:313
  10.7 0.9 %copy-done.4 = bf16[784,128]{1,0:T(8,128)(2,1)S(1)} copy-done((bf16[784,128]{1,0:T(8,128)(2,1)S(1)}, bf16[784,128]{1,0:T(8,128)(2,1)}, u32[]{:S(2)}) %copy-start.4) | copy-done | bytes 200728
  11.6 0.9 %copy-done.6 = bf16[320,128]{1,0:T(8,128)(2,1)S(1)} copy-done((bf16[320,128]{1,0:T(8,128)(2,1)S(1)}, bf16[320,128]{1,0:T(8,128)(2,1)}, u32[]{:S(2)}) %copy-start.6) | copy-done | bytes 81944
  12.5 1.7 %collective-permute-start.5 = (bf16[320,128]{1,0:T(8,128)(2,1)}, bf16[320,128]{1,0:T(8,128)(2,1)S(1)}, u32[]{:S(2)}, u32[]{:S(2)}) collective-permute-start(bf16[320,128]{1,0:T(8,128)(2,1)} %get-tuple-element.42), channel_id=1, source_target_pairs={{0,4},{1,5},{2,6},{3,7},{4,0},{5,1},{6,2},{7,3},{8,12},{9,13},{10,... | collective-permute-start | bytes 245768 | tf_op jit(solution)/shard_map/ppermute | solution.py:313
  14.2 0.7 %collective-permute-done.1.refs_2_ = bf16[784,128]{1,0:T(8,128)(2,1)S(1)} collective-permute-done((bf16[784,128]{1,0:T(8,128)(2,1)}, bf16[784,128]{1,0:T(8,128)(2,1)S(1)}, u32[]{:S(2)}, u32[]{:S(2)}) %collective-permute-start.1) | collective-permute-done | bytes 200736 | tf_op jit(solution)/shard_map/ppermute | solution.py:313
  15.0 0.0 copy-start.3
  15.0 0.0 copy-start.5
  15.0 0.5 %shard_map.93 = (bf16[384,128]{1,0:T(8,128)(2,1)S(1)}, bf16[384,128]{1,0:T(8,128)(2,1)S(1)}, bf16[384,128]{1,0:T(8,128)(2,1)S(1)}, bf16[384,128]{1,0:T(8,128)(2,1)S(1)}) custom-call(bf16[784,128]{1,0:T(8,128)(2,1)S(1)} %get-tuple-element.34.refs_0_, bf16[784,128]{1,0:T(8,128)(2,1)S(1)} %collective-permute-done.refs_1_, ...), custom_call_target="tpu_custom_call" | custom-call | flops 4000000000 | bytes 1196032 | tf_op jit(solution)/shard_map/pallas_call | solution.py:288
  15.5 3.7 %collective-permute-start.9 = (bf16[384,128]{1,0:T(8,128)(2,1)S(1)}, bf16[384,128]{1,0:T(8,128)(2,1)S(1)}, u32[]{:S(2)}, u32[]{:S(2)}) collective-permute-start(bf16[384,128]{1,0:T(8,128)(2,1)S(1)} %get-tuple-element.54), channel_id=1, source_target_pairs={{0,12},{1,13},{2,14},{3,15},{4,8},{5,9},{6,10},{7,11},{8,4},{9,5},... | collective-permute-start | bytes 294920 | tf_op jit(solution)/shard_map/ppermute | solution.py:313
  19.2 0.4 %shard_map.94 = (bf16[272,128]{1,0:T(8,128)(2,1)S(1)}, bf16[272,128]{1,0:T(8,128)(2,1)S(1)}, bf16[272,128]{1,0:T(8,128)(2,1)S(1)}, bf16[272,128]{1,0:T(8,128)(2,1)S(1)}) custom-call(bf16[320,128]{1,0:T(8,128)(2,1)S(1)} %get-tuple-element.39.refs_0_, bf16[320,128]{1,0:T(8,128)(2,1)S(1)} %collective-permute-done.3.refs_1_, ...), custom_call_target="tpu_custom_call" | custom-call | flops 131072 | bytes 606208 | tf_op jit(solution)/shard_map/pallas_call | solution.py:288
  19.6 0.7 %collective-permute-start.6 = (bf16[272,128]{1,0:T(8,128)(2,1)S(1)}, bf16[272,128]{1,0:T(8,128)(2,1)S(1)}, u32[]{:S(2)}, u32[]{:S(2)}) collective-permute-start(bf16[272,128]{1,0:T(8,128)(2,1)S(1)} %get-tuple-element.43), channel_id=1, source_target_pairs={{0,1},{1,0},{2,3},{3,2},{4,5},{5,4},{6,7},{7,6},{8,9},{9,8},{10,11... | collective-permute-start | bytes 208904 | tf_op jit(solution)/shard_map/ppermute | solution.py:313
  20.3 1.5 %collective-permute-start.7 = (bf16[272,128]{1,0:T(8,128)(2,1)S(1)}, bf16[272,128]{1,0:T(8,128)(2,1)S(1)}, u32[]{:S(2)}, u32[]{:S(2)}) collective-permute-start(bf16[272,128]{1,0:T(8,128)(2,1)S(1)} %get-tuple-element.51), channel_id=1, source_target_pairs={{0,2},{1,3},{2,0},{3,1},{4,6},{5,7},{6,4},{7,5},{8,10},{9,11},{10,... | collective-permute-start | bytes 208904 | tf_op jit(solution)/shard_map/ppermute | solution.py:313
  21.8 0.6 %collective-permute-start.11 = (bf16[384,128]{1,0:T(8,128)(2,1)S(1)}, bf16[384,128]{1,0:T(8,128)(2,1)S(1)}, u32[]{:S(2)}, u32[]{:S(2)}) collective-permute-start(bf16[384,128]{1,0:T(8,128)(2,1)S(1)} %get-tuple-element.56), channel_id=1, source_target_pairs={{0,4},{1,5},{2,6},{3,7},{4,0},{5,1},{6,2},{7,3},{8,12},{9,13},{10,... | collective-permute-start | bytes 294920 | tf_op jit(solution)/shard_map/ppermute | solution.py:313
  22.5 0.8 %shard_map.95 = (f32[65,1024]{1,0:T(8,128)S(1)}, bf16[128,1536]{1,0:T(8,128)(2,1)S(1)}, bf16[64,512]{1,0:T(8,128)(2,1)S(1)}, bf16[4,128,256]{2,1,0:T(8,128)(2,1)S(1)}) custom-call(bf16[65,1024]{1,0:T(8,128)(2,1)S(1)} %copy-done.1, bf16[8,8,128,128]{3,2,1,0:T(8,128)(2,1)S(1)} %copy-done, bf16[1,12,64,64]{3,2,1,0:T(8,128)(2,1)S(1)} %copy-done.5, ...), custom_call_target="tpu_custom_call" | custom-call | flops 136314880 | bytes 3512320 | tf_op jit(solution)/shard_map/pallas_call | solution.py:288
  23.2 1.4 %collective-permute-done.7.refs_2_.refs_4_ = bf16[272,128]{1,0:T(8,128)(2,1)S(1)} collective-permute-done((bf16[272,128]{1,0:T(8,128)(2,1)S(1)}, bf16[272,128]{1,0:T(8,128)(2,1)S(1)}, u32[]{:S(2)}, u32[]{:S(2)}) %collective-permute-start.7) | collective-permute-done | bytes 69664 | tf_op jit(solution)/shard_map/ppermute | solution.py:313
  24.6 1.6 %collective-permute-done.8.refs_3_.refs_5_ = bf16[272,128]{1,0:T(8,128)(2,1)S(1)} collective-permute-done((bf16[272,128]{1,0:T(8,128)(2,1)S(1)}, bf16[272,128]{1,0:T(8,128)(2,1)S(1)}, u32[]{:S(2)}, u32[]{:S(2)}) %collective-permute-start.8) | collective-permute-done | bytes 69664 | tf_op jit(solution)/shard_map/ppermute | solution.py:313
  26.3 1.2 %shard_map.96.base_ref = f32[65,1024]{1,0:T(8,128)S(1)} custom-call(s32[1,12]{1,0:T(1,128)S(1)} %copy-done.7, f32[65,1024]{1,0:T(8,128)S(1)} %get-tuple-element.45.base_ref, bf16[128,1536]{1,0:T(8,128)(2,1)S(1)} %get-tuple-element.46.pairs_ref, bf16[64,512]{1,0:T(8,128)(2,1)S(1)} %get-tuple-element.47.across_ref, ...), custom_call_target="tpu_custom_call" | custom-call | flops 68157440 | bytes 1531952 | tf_op jit(solution)/shard_map/pallas_call | solution.py:288
  27.5 1.2 %collective-permute-done.10.refs_1_ = bf16[384,128]{1,0:T(8,128)(2,1)S(1)} collective-permute-done((bf16[384,128]{1,0:T(8,128)(2,1)S(1)}, bf16[384,128]{1,0:T(8,128)(2,1)S(1)}, u32[]{:S(2)}, u32[]{:S(2)}) %collective-permute-start.10) | collective-permute-done | bytes 98336 | tf_op jit(solution)/shard_map/ppermute | solution.py:313
  28.7 0.6 %collective-permute-done.11.refs_1_ = bf16[384,128]{1,0:T(8,128)(2,1)S(1)} collective-permute-done((bf16[384,128]{1,0:T(8,128)(2,1)S(1)}, bf16[384,128]{1,0:T(8,128)(2,1)S(1)}, u32[]{:S(2)}, u32[]{:S(2)}) %collective-permute-start.11) | collective-permute-done | bytes 98336 | tf_op jit(solution)/shard_map/ppermute | solution.py:313
  29.3 0.8 %shard_map.98 = f32[65,1024]{1,0:T(8,128)} custom-call(f32[65,1024]{1,0:T(8,128)S(1)} %shard_map.96.base_ref, f32[384,128]{1,0:T(8,128)S(1)} %shard_map.97.refs_0_, bf16[384,128]{1,0:T(8,128)(2,1)S(1)} %collective-permute-done.11.refs_1_, bf16[272,128]{1,0:T(8,128)(2,1)S(1)} %get-tuple-element.49.refs_0_.refs_2_, ...), custom_call_target="tpu_custom_call" | custom-call | flops 133120 | bytes 1105920 | tf_op jit(solution)/shard_map/pallas_call | solution.py:288
  (24 shorter events, 0.1 us)
Async XLA Ops:
  3.1 9.4 %collective-permute-start = (bf16[784,128]{1,0:T(8,128)(2,1)}, bf16[784,128]{1,0:T(8,128)(2,1)S(1)}, u32[]{:S(2)}, u32[]{:S(2)}) collective-permute-start(bf16[784,128]{1,0:T(8,128)(2,1)} %get-tuple-element.35), channel_id=1, source_target_pairs={{0,2},{1,3},{2,0},{3,1},{4,6},{5,7},{6,4},{7,5},{8,10},{9,11},{10,... | collective-permute-start | bytes 602120 | tf_op jit(solution)/shard_map/ppermute | solution.py:313
  6.1 8.9 %collective-permute-start.1 = (bf16[784,128]{1,0:T(8,128)(2,1)}, bf16[784,128]{1,0:T(8,128)(2,1)S(1)}, u32[]{:S(2)}, u32[]{:S(2)}) collective-permute-start(bf16[784,128]{1,0:T(8,128)(2,1)} %get-tuple-element.36), channel_id=1, source_target_pairs={{0,3},{1,2},{2,1},{3,0},{4,7},{5,6},{6,5},{7,4},{8,11},{9,10},{10,... | collective-permute-start | bytes 602120 | tf_op jit(solution)/shard_map/ppermute | solution.py:313
  6.1 8.9 %collective-permute-start.2 = (bf16[784,128]{1,0:T(8,128)(2,1)}, bf16[784,128]{1,0:T(8,128)(2,1)S(1)}, u32[]{:S(2)}, u32[]{:S(2)}) collective-permute-start(bf16[784,128]{1,0:T(8,128)(2,1)} %get-tuple-element.37), channel_id=1, source_target_pairs={{0,1},{1,0},{2,3},{3,2},{4,5},{5,4},{6,7},{7,6},{8,9},{9,8},{10,11... | collective-permute-start | bytes 602120 | tf_op jit(solution)/shard_map/ppermute | solution.py:313
  6.3 12.9 %collective-permute-start.3 = (bf16[320,128]{1,0:T(8,128)(2,1)}, bf16[320,128]{1,0:T(8,128)(2,1)S(1)}, u32[]{:S(2)}, u32[]{:S(2)}) collective-permute-start(bf16[320,128]{1,0:T(8,128)(2,1)} %get-tuple-element.40), channel_id=1, source_target_pairs={{0,8},{1,9},{2,10},{3,11},{4,12},{5,13},{6,14},{7,15},{8,0},{9,1},... | collective-permute-start | bytes 245768 | tf_op jit(solution)/shard_map/ppermute | solution.py:313
  9.3 9.9 %collective-permute-start.4 = (bf16[320,128]{1,0:T(8,128)(2,1)}, bf16[320,128]{1,0:T(8,128)(2,1)S(1)}, u32[]{:S(2)}, u32[]{:S(2)}) collective-permute-start(bf16[320,128]{1,0:T(8,128)(2,1)} %get-tuple-element.41), channel_id=1, source_target_pairs={{0,12},{1,13},{2,14},{3,15},{4,8},{5,9},{6,10},{7,11},{8,4},{9,5},... | collective-permute-start | bytes 245768 | tf_op jit(solution)/shard_map/ppermute | solution.py:313
  10.7 0.9 %copy-start.4 = (bf16[784,128]{1,0:T(8,128)(2,1)S(1)}, bf16[784,128]{1,0:T(8,128)(2,1)}, u32[]{:S(2)}) copy-start(bf16[784,128]{1,0:T(8,128)(2,1)} %get-tuple-element.31.refs_0_) | copy-start | bytes 602116
  11.6 0.9 %copy-start.6 = (bf16[320,128]{1,0:T(8,128)(2,1)S(1)}, bf16[320,128]{1,0:T(8,128)(2,1)}, u32[]{:S(2)}) copy-start(bf16[320,128]{1,0:T(8,128)(2,1)} %get-tuple-element.32.refs_1_) | copy-start | bytes 245764
  12.5 6.7 %collective-permute-start.5 = (bf16[320,128]{1,0:T(8,128)(2,1)}, bf16[320,128]{1,0:T(8,128)(2,1)S(1)}, u32[]{:S(2)}, u32[]{:S(2)}) collective-permute-start(bf16[320,128]{1,0:T(8,128)(2,1)} %get-tuple-element.42), channel_id=1, source_target_pairs={{0,4},{1,5},{2,6},{3,7},{4,0},{5,1},{6,2},{7,3},{8,12},{9,13},{10,... | collective-permute-start | bytes 245768 | tf_op jit(solution)/shard_map/ppermute | solution.py:313
  15.0 7.5 %copy-start = (bf16[8,8,128,128]{3,2,1,0:T(8,128)(2,1)S(1)}, bf16[8,8,128,128]{3,2,1,0:T(8,128)(2,1)}, u32[]{:S(2)}) copy-start(bf16[8,8,128,128]{3,2,1,0:T(8,128)(2,1)} %local_ref.1) | copy-start | bytes 6291460
  15.0 7.5 %copy-start.1 = (bf16[65,1024]{1,0:T(8,128)(2,1)S(1)}, bf16[65,1024]{1,0:T(8,128)(2,1)}, u32[]{:S(2)}) copy-start(bf16[65,1024]{1,0:T(8,128)(2,1)} %probes_ref) | copy-start | bytes 399364
  15.0 7.5 %copy-start.2 = (bf16[8,64,64]{2,1,0:T(8,128)(2,1)S(1)}, bf16[8,64,64]{2,1,0:T(8,128)(2,1)}, u32[]{:S(2)}) copy-start(bf16[8,64,64]{2,1,0:T(8,128)(2,1)} %transfer_ref.1) | copy-start | bytes 196612
  15.0 7.5 %copy-start.3 = (bf16[8,64,128]{2,1,0:T(8,128)(2,1)S(1)}, bf16[8,64,128]{2,1,0:T(8,128)(2,1)}, u32[]{:S(2)}) copy-start(bf16[8,64,128]{2,1,0:T(8,128)(2,1)} %basis_ref.1) | copy-start | bytes 393220
  15.0 7.5 %copy-start.5 = (bf16[1,12,64,64]{3,2,1,0:T(8,128)(2,1)S(1)}, bf16[1,12,64,64]{3,2,1,0:T(8,128)(2,1)}, u32[]{:S(2)}) copy-start(bf16[1,12,64,64]{3,2,1,0:T(8,128)(2,1)} %couplings_ref.1) | copy-start | bytes 294916
  15.5 10.8 %copy-start.7 = (s32[1,12]{1,0:T(1,128)S(1)}, s32[1,12]{1,0:T(1,128)}, u32[]{:S(2)}) copy-start(s32[1,12]{1,0:T(1,128)} %partner_ref.1) | copy-start | bytes 148
  15.5 12.0 %collective-permute-start.9 = (bf16[384,128]{1,0:T(8,128)(2,1)S(1)}, bf16[384,128]{1,0:T(8,128)(2,1)S(1)}, u32[]{:S(2)}, u32[]{:S(2)}) collective-permute-start(bf16[384,128]{1,0:T(8,128)(2,1)S(1)} %get-tuple-element.54), channel_id=1, source_target_pairs={{0,12},{1,13},{2,14},{3,15},{4,8},{5,9},{6,10},{7,11},{8,4},{9,5},... | collective-permute-start | bytes 294920 | tf_op jit(solution)/shard_map/ppermute | solution.py:313
  19.2 9.5 %collective-permute-start.10 = (bf16[384,128]{1,0:T(8,128)(2,1)S(1)}, bf16[384,128]{1,0:T(8,128)(2,1)S(1)}, u32[]{:S(2)}, u32[]{:S(2)}) collective-permute-start(bf16[384,128]{1,0:T(8,128)(2,1)S(1)} %get-tuple-element.55), channel_id=1, source_target_pairs={{0,8},{1,9},{2,10},{3,11},{4,12},{5,13},{6,14},{7,15},{8,0},{9,1},... | collective-permute-start | bytes 294920 | tf_op jit(solution)/shard_map/ppermute | solution.py:313
  19.6 2.2 %collective-permute-start.6 = (bf16[272,128]{1,0:T(8,128)(2,1)S(1)}, bf16[272,128]{1,0:T(8,128)(2,1)S(1)}, u32[]{:S(2)}, u32[]{:S(2)}) collective-permute-start(bf16[272,128]{1,0:T(8,128)(2,1)S(1)} %get-tuple-element.43), channel_id=1, source_target_pairs={{0,1},{1,0},{2,3},{3,2},{4,5},{5,4},{6,7},{7,6},{8,9},{9,8},{10,11... | collective-permute-start | bytes 208904 | tf_op jit(solution)/shard_map/ppermute | solution.py:313
  20.3 4.3 %collective-permute-start.7 = (bf16[272,128]{1,0:T(8,128)(2,1)S(1)}, bf16[272,128]{1,0:T(8,128)(2,1)S(1)}, u32[]{:S(2)}, u32[]{:S(2)}) collective-permute-start(bf16[272,128]{1,0:T(8,128)(2,1)S(1)} %get-tuple-element.51), channel_id=1, source_target_pairs={{0,2},{1,3},{2,0},{3,1},{4,6},{5,7},{6,4},{7,5},{8,10},{9,11},{10,... | collective-permute-start | bytes 208904 | tf_op jit(solution)/shard_map/ppermute | solution.py:313
  21.8 4.5 %collective-permute-start.8 = (bf16[272,128]{1,0:T(8,128)(2,1)S(1)}, bf16[272,128]{1,0:T(8,128)(2,1)S(1)}, u32[]{:S(2)}, u32[]{:S(2)}) collective-permute-start(bf16[272,128]{1,0:T(8,128)(2,1)S(1)} %get-tuple-element.52), channel_id=1, source_target_pairs={{0,3},{1,2},{2,1},{3,0},{4,7},{5,6},{6,5},{7,4},{8,11},{9,10},{10,... | collective-permute-start | bytes 208904 | tf_op jit(solution)/shard_map/ppermute | solution.py:313
  21.8 7.5 %collective-permute-start.11 = (bf16[384,128]{1,0:T(8,128)(2,1)S(1)}, bf16[384,128]{1,0:T(8,128)(2,1)S(1)}, u32[]{:S(2)}, u32[]{:S(2)}) collective-permute-start(bf16[384,128]{1,0:T(8,128)(2,1)S(1)} %get-tuple-element.56), channel_id=1, source_target_pairs={{0,4},{1,5},{2,6},{3,7},{4,0},{5,1},{6,2},{7,3},{8,12},{9,13},{10,... | collective-permute-start | bytes 294920 | tf_op jit(solution)/shard_map/ppermute | solution.py:313

commit v31 on v28

--- a/solution.py
+++ b/solution.py
@@ -86,17 +86,17 @@
     columns, rank = probes_ref.shape[0], basis_ref.shape[1]
     copies = Copies(sems)
     cuts = (0, leaves // 4, leaves)
+    early = [copies.start(probes_hbm, probes_ref)]
     arrivals = {}
-    early = [
-        copies.start(probes_hbm, probes_ref),
+    for j, after in zip(cuts, cuts[1:]):
+        part = pl.ds(j, after - j)
+        arrivals[j] = copies.start(blocks_hbm.at[part], blocks_ref.at[part])
+    early += [
+        copies.start(basis_hbm, basis_ref),
+        copies.start(transfer_hbm, transfer_ref),
         copies.start(dest_hbm, dest_ref),
         copies.start(leaf_hbm, leaf_ref),
     ]
-    for j, after in zip(cuts, cuts[1:]):
-        part = pl.ds(j, after - j)
-        arrivals[j] = copies.start(blocks_hbm.at[part], blocks_ref.at[part])
-        if j == 0:
-            early += [copies.start(basis_hbm, basis_ref), copies.start(transfer_hbm, transfer_ref)]
 
     @pl.loop(0, devices)
     def _(i):

time: 29.2 us -> 29.5 us (1.010)
  no operation moved by 1% of the time
where the time goes in v31:
time: 29.5 us; the launch traced here: 29.3 us
  starting transfers between devices  15.7 us (53%)
  Pallas kernels  7.01 us (24%)
  waiting for transfers between devices  4.54 us (15%)
  local copies, waits for them, and re-layouts  1.84 us (6%)
    ppermute x12, starting transfers between devices, per_device(): lax.ppermute(x, 'leaf', [(i, i ^ way) for i in range(devices)])  15.7 us
    pallas_call x8, Pallas kernels, call(): pl.pallas_call(kernel, out_shape=out_shape, in_specs=specs[0], out_specs=...  7.01 us
    ppermute x12, waiting for transfers between devices, per_device(): lax.ppermute(x, 'leaf', [(i, i ^ way) for i in range(devices)])  4.54 us
    unnamed x16, local copies, waits for them, and re-layouts  1.84 us
  transfers between devices with their start and end apart: 12, of which 4 were waited for; matrix products, arithmetic and copies ran while one was open for 0% of the time, Pallas kernels for 10%

profile of v31, /device:TPU:0, one launch (start us, length us, event | category | flops | bytes accessed | tf_op | source)
XLA Modules:
  0.0 29.3 jit_solution(4341311420293318263)
XLA Ops:
  0.0 3.3 %shard_map.91 = (bf16[784,128]{1,0:T(8,128)(2,1)}, bf16[784,128]{1,0:T(8,128)(2,1)}, bf16[784,128]{1,0:T(8,128)(2,1)}, bf16[784,128]{1,0:T(8,128)(2,1)}, bf16[32...) custom-call(s32[4,8]{1,0:T(4,128)} %bitcast.2, ...), custom_call_target="tpu_custom_call" | custom-call | flops 68157440 | bytes 2509056 | tf_op jit(solution)/shard_map/pallas_call | solution.py:288
  3.3 3.0 %collective-permute-start = (bf16[784,128]{1,0:T(8,128)(2,1)}, bf16[784,128]{1,0:T(8,128)(2,1)S(1)}, u32[]{:S(2)}, u32[]{:S(2)}) collective-permute-start(bf16[784,128]{1,0:T(8,128)(2,1)} %get-tuple-element.35), channel_id=1, source_target_pairs={{0,2},{1,3},{2,0},{3,1},{4,6},{5,7},{6,4},{7,5},{8,10},{9,11},{10,... | collective-permute-start | bytes 602120 | tf_op jit(solution)/shard_map/ppermute | solution.py:313
  6.3 0.2 collective-permute-start.2
  6.5 3.0 %collective-permute-start.3 = (bf16[320,128]{1,0:T(8,128)(2,1)}, bf16[320,128]{1,0:T(8,128)(2,1)S(1)}, u32[]{:S(2)}, u32[]{:S(2)}) collective-permute-start(bf16[320,128]{1,0:T(8,128)(2,1)} %get-tuple-element.40), channel_id=1, source_target_pairs={{0,8},{1,9},{2,10},{3,11},{4,12},{5,13},{6,14},{7,15},{8,0},{9,1},... | collective-permute-start | bytes 245768 | tf_op jit(solution)/shard_map/ppermute | solution.py:313
  9.5 1.3 %collective-permute-start.4 = (bf16[320,128]{1,0:T(8,128)(2,1)}, bf16[320,128]{1,0:T(8,128)(2,1)S(1)}, u32[]{:S(2)}, u32[]{:S(2)}) collective-permute-start(bf16[320,128]{1,0:T(8,128)(2,1)} %get-tuple-element.41), channel_id=1, source_target_pairs={{0,12},{1,13},{2,14},{3,15},{4,8},{5,9},{6,10},{7,11},{8,4},{9,5},... | collective-permute-start | bytes 245768 | tf_op jit(solution)/shard_map/ppermute | solution.py:313
  10.9 0.9 %copy-done.4 = bf16[784,128]{1,0:T(8,128)(2,1)S(1)} copy-done((bf16[784,128]{1,0:T(8,128)(2,1)S(1)}, bf16[784,128]{1,0:T(8,128)(2,1)}, u32[]{:S(2)}) %copy-start.4) | copy-done | bytes 200728
  11.8 0.9 %copy-done.6 = bf16[320,128]{1,0:T(8,128)(2,1)S(1)} copy-done((bf16[320,128]{1,0:T(8,128)(2,1)S(1)}, bf16[320,128]{1,0:T(8,128)(2,1)}, u32[]{:S(2)}) %copy-start.6) | copy-done | bytes 81944
  12.7 1.7 %collective-permute-start.5 = (bf16[320,128]{1,0:T(8,128)(2,1)}, bf16[320,128]{1,0:T(8,128)(2,1)S(1)}, u32[]{:S(2)}, u32[]{:S(2)}) collective-permute-start(bf16[320,128]{1,0:T(8,128)(2,1)} %get-tuple-element.42), channel_id=1, source_target_pairs={{0,4},{1,5},{2,6},{3,7},{4,0},{5,1},{6,2},{7,3},{8,12},{9,13},{10,... | collective-permute-start | bytes 245768 | tf_op jit(solution)/shard_map/ppermute | solution.py:313
  14.5 0.7 %collective-permute-done.1.refs_2_ = bf16[784,128]{1,0:T(8,128)(2,1)S(1)} collective-permute-done((bf16[784,128]{1,0:T(8,128)(2,1)}, bf16[784,128]{1,0:T(8,128)(2,1)S(1)}, u32[]{:S(2)}, u32[]{:S(2)}) %collective-permute-start.1) | collective-permute-done | bytes 200736 | tf_op jit(solution)/shard_map/ppermute | solution.py:313
  15.2 0.0 copy-start.3
  15.2 0.0 copy-start.5
  15.2 0.5 %shard_map.93 = (bf16[384,128]{1,0:T(8,128)(2,1)S(1)}, bf16[384,128]{1,0:T(8,128)(2,1)S(1)}, bf16[384,128]{1,0:T(8,128)(2,1)S(1)}, bf16[384,128]{1,0:T(8,128)(2,1)S(1)}) custom-call(bf16[784,128]{1,0:T(8,128)(2,1)S(1)} %get-tuple-element.34.refs_0_, bf16[784,128]{1,0:T(8,128)(2,1)S(1)} %collective-permute-done.refs_1_, ...), custom_call_target="tpu_custom_call" | custom-call | flops 4000000000 | bytes 1196032 | tf_op jit(solution)/shard_map/pallas_call | solution.py:288
  15.8 2.6 %collective-permute-start.9 = (bf16[384,128]{1,0:T(8,128)(2,1)S(1)}, bf16[384,128]{1,0:T(8,128)(2,1)S(1)}, u32[]{:S(2)}, u32[]{:S(2)}) collective-permute-start(bf16[384,128]{1,0:T(8,128)(2,1)S(1)} %get-tuple-element.54), channel_id=1, source_target_pairs={{0,8},{1,9},{2,10},{3,11},{4,12},{5,13},{6,14},{7,15},{8,0},{9,1},... | collective-permute-start | bytes 294920 | tf_op jit(solution)/shard_map/ppermute | solution.py:313
  18.4 1.3 %collective-permute-start.10 = (bf16[384,128]{1,0:T(8,128)(2,1)S(1)}, bf16[384,128]{1,0:T(8,128)(2,1)S(1)}, u32[]{:S(2)}, u32[]{:S(2)}) collective-permute-start(bf16[384,128]{1,0:T(8,128)(2,1)S(1)} %get-tuple-element.55), channel_id=1, source_target_pairs={{0,12},{1,13},{2,14},{3,15},{4,8},{5,9},{6,10},{7,11},{8,4},{9,5},... | collective-permute-start | bytes 294920 | tf_op jit(solution)/shard_map/ppermute | solution.py:313
  19.8 0.4 %shard_map.94 = (bf16[272,128]{1,0:T(8,128)(2,1)S(1)}, bf16[272,128]{1,0:T(8,128)(2,1)S(1)}, bf16[272,128]{1,0:T(8,128)(2,1)S(1)}, bf16[272,128]{1,0:T(8,128)(2,1)S(1)}) custom-call(bf16[320,128]{1,0:T(8,128)(2,1)S(1)} %get-tuple-element.39.refs_0_, bf16[320,128]{1,0:T(8,128)(2,1)S(1)} %collective-permute-done.3.refs_1_, ...), custom_call_target="tpu_custom_call" | custom-call | flops 131072 | bytes 606208 | tf_op jit(solution)/shard_map/pallas_call | solution.py:288
  20.2 0.5 %collective-permute-start.6 = (bf16[272,128]{1,0:T(8,128)(2,1)S(1)}, bf16[272,128]{1,0:T(8,128)(2,1)S(1)}, u32[]{:S(2)}, u32[]{:S(2)}) collective-permute-start(bf16[272,128]{1,0:T(8,128)(2,1)S(1)} %get-tuple-element.43), channel_id=1, source_target_pairs={{0,1},{1,0},{2,3},{3,2},{4,5},{5,4},{6,7},{7,6},{8,9},{9,8},{10,11... | collective-permute-start | bytes 208904 | tf_op jit(solution)/shard_map/ppermute | solution.py:313
  20.7 1.5 %collective-permute-start.7 = (bf16[272,128]{1,0:T(8,128)(2,1)S(1)}, bf16[272,128]{1,0:T(8,128)(2,1)S(1)}, u32[]{:S(2)}, u32[]{:S(2)}) collective-permute-start(bf16[272,128]{1,0:T(8,128)(2,1)S(1)} %get-tuple-element.51), channel_id=1, source_target_pairs={{0,2},{1,3},{2,0},{3,1},{4,6},{5,7},{6,4},{7,5},{8,10},{9,11},{10,... | collective-permute-start | bytes 208904 | tf_op jit(solution)/shard_map/ppermute | solution.py:313
  22.2 0.4 %collective-permute-start.11 = (bf16[384,128]{1,0:T(8,128)(2,1)S(1)}, bf16[384,128]{1,0:T(8,128)(2,1)S(1)}, u32[]{:S(2)}, u32[]{:S(2)}) collective-permute-start(bf16[384,128]{1,0:T(8,128)(2,1)S(1)} %get-tuple-element.56), channel_id=1, source_target_pairs={{0,4},{1,5},{2,6},{3,7},{4,0},{5,1},{6,2},{7,3},{8,12},{9,13},{10,... | collective-permute-start | bytes 294920 | tf_op jit(solution)/shard_map/ppermute | solution.py:313
  22.6 0.8 %shard_map.95 = (f32[65,1024]{1,0:T(8,128)S(1)}, bf16[128,1536]{1,0:T(8,128)(2,1)S(1)}, bf16[64,512]{1,0:T(8,128)(2,1)S(1)}, bf16[4,128,256]{2,1,0:T(8,128)(2,1)S(1)}) custom-call(bf16[65,1024]{1,0:T(8,128)(2,1)S(1)} %copy-done.1, bf16[8,8,128,128]{3,2,1,0:T(8,128)(2,1)S(1)} %copy-done, bf16[1,12,64,64]{3,2,1,0:T(8,128)(2,1)S(1)} %copy-done.5, ...), custom_call_target="tpu_custom_call" | custom-call | flops 136314880 | bytes 3512320 | tf_op jit(solution)/shard_map/pallas_call | solution.py:288
  23.4 1.6 %collective-permute-done.7.refs_2_.refs_4_ = bf16[272,128]{1,0:T(8,128)(2,1)S(1)} collective-permute-done((bf16[272,128]{1,0:T(8,128)(2,1)S(1)}, bf16[272,128]{1,0:T(8,128)(2,1)S(1)}, u32[]{:S(2)}, u32[]{:S(2)}) %collective-permute-start.7) | collective-permute-done | bytes 69664 | tf_op jit(solution)/shard_map/ppermute | solution.py:313
  25.0 1.7 %collective-permute-done.8.refs_3_.refs_5_ = bf16[272,128]{1,0:T(8,128)(2,1)S(1)} collective-permute-done((bf16[272,128]{1,0:T(8,128)(2,1)S(1)}, bf16[272,128]{1,0:T(8,128)(2,1)S(1)}, u32[]{:S(2)}, u32[]{:S(2)}) %collective-permute-start.8) | collective-permute-done | bytes 69664 | tf_op jit(solution)/shard_map/ppermute | solution.py:313
  26.6 1.2 %shard_map.96.base_ref = f32[65,1024]{1,0:T(8,128)S(1)} custom-call(s32[1,12]{1,0:T(1,128)S(1)} %copy-done.7, f32[65,1024]{1,0:T(8,128)S(1)} %get-tuple-element.45.base_ref, bf16[128,1536]{1,0:T(8,128)(2,1)S(1)} %get-tuple-element.46.pairs_ref, bf16[64,512]{1,0:T(8,128)(2,1)S(1)} %get-tuple-element.47.across_ref, ...), custom_call_target="tpu_custom_call" | custom-call | flops 68157440 | bytes 1531952 | tf_op jit(solution)/shard_map/pallas_call | solution.py:288
  27.9 0.6 %collective-permute-done.11.refs_1_ = bf16[384,128]{1,0:T(8,128)(2,1)S(1)} collective-permute-done((bf16[384,128]{1,0:T(8,128)(2,1)S(1)}, bf16[384,128]{1,0:T(8,128)(2,1)S(1)}, u32[]{:S(2)}, u32[]{:S(2)}) %collective-permute-start.11) | collective-permute-done | bytes 98336 | tf_op jit(solution)/shard_map/ppermute | solution.py:313
  28.5 0.8 %shard_map.98 = f32[65,1024]{1,0:T(8,128)} custom-call(f32[65,1024]{1,0:T(8,128)S(1)} %shard_map.96.base_ref, f32[384,128]{1,0:T(8,128)S(1)} %shard_map.97.refs_0_, bf16[384,128]{1,0:T(8,128)(2,1)S(1)} %collective-permute-done.11.refs_1_, bf16[272,128]{1,0:T(8,128)(2,1)S(1)} %get-tuple-element.49.refs_0_.refs_2_, ...), custom_call_target="tpu_custom_call" | custom-call | flops 133120 | bytes 1105920 | tf_op jit(solution)/shard_map/pallas_call | solution.py:288
  (24 shorter events, 0.1 us)
Async XLA Ops:
  3.3 9.4 %collective-permute-start = (bf16[784,128]{1,0:T(8,128)(2,1)}, bf16[784,128]{1,0:T(8,128)(2,1)S(1)}, u32[]{:S(2)}, u32[]{:S(2)}) collective-permute-start(bf16[784,128]{1,0:T(8,128)(2,1)} %get-tuple-element.35), channel_id=1, source_target_pairs={{0,2},{1,3},{2,0},{3,1},{4,6},{5,7},{6,4},{7,5},{8,10},{9,11},{10,... | collective-permute-start | bytes 602120 | tf_op jit(solution)/shard_map/ppermute | solution.py:313
  6.3 8.9 %collective-permute-start.1 = (bf16[784,128]{1,0:T(8,128)(2,1)}, bf16[784,128]{1,0:T(8,128)(2,1)S(1)}, u32[]{:S(2)}, u32[]{:S(2)}) collective-permute-start(bf16[784,128]{1,0:T(8,128)(2,1)} %get-tuple-element.36), channel_id=1, source_target_pairs={{0,3},{1,2},{2,1},{3,0},{4,7},{5,6},{6,5},{7,4},{8,11},{9,10},{10,... | collective-permute-start | bytes 602120 | tf_op jit(solution)/shard_map/ppermute | solution.py:313
  6.3 8.9 %collective-permute-start.2 = (bf16[784,128]{1,0:T(8,128)(2,1)}, bf16[784,128]{1,0:T(8,128)(2,1)S(1)}, u32[]{:S(2)}, u32[]{:S(2)}) collective-permute-start(bf16[784,128]{1,0:T(8,128)(2,1)} %get-tuple-element.37), channel_id=1, source_target_pairs={{0,1},{1,0},{2,3},{3,2},{4,5},{5,4},{6,7},{7,6},{8,9},{9,8},{10,11... | collective-permute-start | bytes 602120 | tf_op jit(solution)/shard_map/ppermute | solution.py:313
  6.5 13.2 %collective-permute-start.3 = (bf16[320,128]{1,0:T(8,128)(2,1)}, bf16[320,128]{1,0:T(8,128)(2,1)S(1)}, u32[]{:S(2)}, u32[]{:S(2)}) collective-permute-start(bf16[320,128]{1,0:T(8,128)(2,1)} %get-tuple-element.40), channel_id=1, source_target_pairs={{0,8},{1,9},{2,10},{3,11},{4,12},{5,13},{6,14},{7,15},{8,0},{9,1},... | collective-permute-start | bytes 245768 | tf_op jit(solution)/shard_map/ppermute | solution.py:313
  9.5 10.2 %collective-permute-start.4 = (bf16[320,128]{1,0:T(8,128)(2,1)}, bf16[320,128]{1,0:T(8,128)(2,1)S(1)}, u32[]{:S(2)}, u32[]{:S(2)}) collective-permute-start(bf16[320,128]{1,0:T(8,128)(2,1)} %get-tuple-element.41), channel_id=1, source_target_pairs={{0,12},{1,13},{2,14},{3,15},{4,8},{5,9},{6,10},{7,11},{8,4},{9,5},... | collective-permute-start | bytes 245768 | tf_op jit(solution)/shard_map/ppermute | solution.py:313
  10.9 0.9 %copy-start.4 = (bf16[784,128]{1,0:T(8,128)(2,1)S(1)}, bf16[784,128]{1,0:T(8,128)(2,1)}, u32[]{:S(2)}) copy-start(bf16[784,128]{1,0:T(8,128)(2,1)} %get-tuple-element.31.refs_0_) | copy-start | bytes 602116
  11.8 0.9 %copy-start.6 = (bf16[320,128]{1,0:T(8,128)(2,1)S(1)}, bf16[320,128]{1,0:T(8,128)(2,1)}, u32[]{:S(2)}) copy-start(bf16[320,128]{1,0:T(8,128)(2,1)} %get-tuple-element.32.refs_1_) | copy-start | bytes 245764
  12.7 7.0 %collective-permute-start.5 = (bf16[320,128]{1,0:T(8,128)(2,1)}, bf16[320,128]{1,0:T(8,128)(2,1)S(1)}, u32[]{:S(2)}, u32[]{:S(2)}) collective-permute-start(bf16[320,128]{1,0:T(8,128)(2,1)} %get-tuple-element.42), channel_id=1, source_target_pairs={{0,4},{1,5},{2,6},{3,7},{4,0},{5,1},{6,2},{7,3},{8,12},{9,13},{10,... | collective-permute-start | bytes 245768 | tf_op jit(solution)/shard_map/ppermute | solution.py:313
  15.2 7.4 %copy-start = (bf16[8,8,128,128]{3,2,1,0:T(8,128)(2,1)S(1)}, bf16[8,8,128,128]{3,2,1,0:T(8,128)(2,1)}, u32[]{:S(2)}) copy-start(bf16[8,8,128,128]{3,2,1,0:T(8,128)(2,1)} %local_ref.1) | copy-start | bytes 6291460
  15.2 7.4 %copy-start.1 = (bf16[65,1024]{1,0:T(8,128)(2,1)S(1)}, bf16[65,1024]{1,0:T(8,128)(2,1)}, u32[]{:S(2)}) copy-start(bf16[65,1024]{1,0:T(8,128)(2,1)} %probes_ref) | copy-start | bytes 399364
  15.2 7.4 %copy-start.2 = (bf16[8,64,64]{2,1,0:T(8,128)(2,1)S(1)}, bf16[8,64,64]{2,1,0:T(8,128)(2,1)}, u32[]{:S(2)}) copy-start(bf16[8,64,64]{2,1,0:T(8,128)(2,1)} %transfer_ref.1) | copy-start | bytes 196612
  15.2 7.4 %copy-start.3 = (bf16[8,64,128]{2,1,0:T(8,128)(2,1)S(1)}, bf16[8,64,128]{2,1,0:T(8,128)(2,1)}, u32[]{:S(2)}) copy-start(bf16[8,64,128]{2,1,0:T(8,128)(2,1)} %basis_ref.1) | copy-start | bytes 393220
  15.2 7.4 %copy-start.5 = (bf16[1,12,64,64]{3,2,1,0:T(8,128)(2,1)S(1)}, bf16[1,12,64,64]{3,2,1,0:T(8,128)(2,1)}, u32[]{:S(2)}) copy-start(bf16[1,12,64,64]{3,2,1,0:T(8,128)(2,1)} %couplings_ref.1) | copy-start | bytes 294916
  15.8 10.9 %copy-start.7 = (s32[1,12]{1,0:T(1,128)S(1)}, s32[1,12]{1,0:T(1,128)}, u32[]{:S(2)}) copy-start(s32[1,12]{1,0:T(1,128)} %partner_ref.1) | copy-start | bytes 148
  15.8 12.1 %collective-permute-start.9 = (bf16[384,128]{1,0:T(8,128)(2,1)S(1)}, bf16[384,128]{1,0:T(8,128)(2,1)S(1)}, u32[]{:S(2)}, u32[]{:S(2)}) collective-permute-start(bf16[384,128]{1,0:T(8,128)(2,1)S(1)} %get-tuple-element.54), channel_id=1, source_target_pairs={{0,8},{1,9},{2,10},{3,11},{4,12},{5,13},{6,14},{7,15},{8,0},{9,1},... | collective-permute-start | bytes 294920 | tf_op jit(solution)/shard_map/ppermute | solution.py:313
  18.4 9.4 %collective-permute-start.10 = (bf16[384,128]{1,0:T(8,128)(2,1)S(1)}, bf16[384,128]{1,0:T(8,128)(2,1)S(1)}, u32[]{:S(2)}, u32[]{:S(2)}) collective-permute-start(bf16[384,128]{1,0:T(8,128)(2,1)S(1)} %get-tuple-element.55), channel_id=1, source_target_pairs={{0,12},{1,13},{2,14},{3,15},{4,8},{5,9},{6,10},{7,11},{8,4},{9,5},... | collective-permute-start | bytes 294920 | tf_op jit(solution)/shard_map/ppermute | solution.py:313
  20.2 2.0 %collective-permute-start.6 = (bf16[272,128]{1,0:T(8,128)(2,1)S(1)}, bf16[272,128]{1,0:T(8,128)(2,1)S(1)}, u32[]{:S(2)}, u32[]{:S(2)}) collective-permute-start(bf16[272,128]{1,0:T(8,128)(2,1)S(1)} %get-tuple-element.43), channel_id=1, source_target_pairs={{0,1},{1,0},{2,3},{3,2},{4,5},{5,4},{6,7},{7,6},{8,9},{9,8},{10,11... | collective-permute-start | bytes 208904 | tf_op jit(solution)/shard_map/ppermute | solution.py:313
  20.7 4.3 %collective-permute-start.7 = (bf16[272,128]{1,0:T(8,128)(2,1)S(1)}, bf16[272,128]{1,0:T(8,128)(2,1)S(1)}, u32[]{:S(2)}, u32[]{:S(2)}) collective-permute-start(bf16[272,128]{1,0:T(8,128)(2,1)S(1)} %get-tuple-element.51), channel_id=1, source_target_pairs={{0,2},{1,3},{2,0},{3,1},{4,6},{5,7},{6,4},{7,5},{8,10},{9,11},{10,... | collective-permute-start | bytes 208904 | tf_op jit(solution)/shard_map/ppermute | solution.py:313
  22.2 4.5 %collective-permute-start.8 = (bf16[272,128]{1,0:T(8,128)(2,1)S(1)}, bf16[272,128]{1,0:T(8,128)(2,1)S(1)}, u32[]{:S(2)}, u32[]{:S(2)}) collective-permute-start(bf16[272,128]{1,0:T(8,128)(2,1)S(1)} %get-tuple-element.52), channel_id=1, source_target_pairs={{0,3},{1,2},{2,1},{3,0},{4,7},{5,6},{6,5},{7,4},{8,11},{9,10},{10,... | collective-permute-start | bytes 208904 | tf_op jit(solution)/shard_map/ppermute | solution.py:313
  22.2 6.3 %collective-permute-start.11 = (bf16[384,128]{1,0:T(8,128)(2,1)S(1)}, bf16[384,128]{1,0:T(8,128)(2,1)S(1)}, u32[]{:S(2)}, u32[]{:S(2)}) collective-permute-start(bf16[384,128]{1,0:T(8,128)(2,1)S(1)} %get-tuple-element.56), channel_id=1, source_target_pairs={{0,4},{1,5},{2,6},{3,7},{4,0},{5,1},{6,2},{7,3},{8,12},{9,13},{10,... | collective-permute-start | bytes 294920 | tf_op jit(solution)/shard_map/ppermute | solution.py:313
